TPU v7x, 32 devices: a whole 2x2x4 slice. The times are simulated.
32 devices in a mesh: dp: 4 (over y, x), ctx: 8 (over z, core).
Axes of the slice: x: 2, y: 2, z: 4, core: 2. Of those that a mesh axis runs over, the one named last changes fastest.
Arguments:
- projected: bfloat16 [4, 1024, 3, 8192], P('dp', 'ctx'), may hold values from -6 to 6
- short_filter: float32 [3, 7, 8192], replicated, may hold values from -2.4 to 2.4
- residues: float32 [512, 16], replicated, may hold values from -0.06 to 0.06
- decay_rates: float32 [512, 16], replicated, may hold values from 9.765625e-05 to 0.03125
- skip_gain: float32 [8192], replicated, may hold values from 0.5 to 1.5
- cotangent: bfloat16 [4, 1024, 8192], P('dp', 'ctx'), may hold values from -6 to 6
Outputs:
- output: bfloat16 [4, 1024, 8192], P('dp', 'ctx')
- grad_projected: bfloat16 [4, 1024, 3, 8192], P('dp', 'ctx')
- grad_short: float32 [3, 7, 8192], replicated
- grad_skip: float32 [8192], replicated
All inputs are finite; a program needn't handle non-finite values.
Results may differ from a plain program's by a relative error of at most 0.001.
Values may be sent and summed in bfloat16 or wider, within the bound.
No kernel may reach another device: no remote copies, remote signals or barrier semaphores. Data moves between devices by JAX's collectives and lax.ppermute only.
A program may use at most 320 MiB of HBM per device.

v0:
```python
import jax
import jax.numpy as jnp
from jax import lax
from jax.sharding import PartitionSpec as P

BLK = 64


HIGHEST = lax.Precision.HIGHEST


def passed_along(value, axis, steps):
    count = lax.axis_size(axis)
    first, last = (max(0, -steps), min(count, count - steps))
    return lax.ppermute(value, axis, [(source, source + steps) for source in range(first, last)])


def edge_tables(residues, decay_rates, span):
    offsets = jnp.arange(span).astype(jnp.float32)
    carry_fwd = residues[:, None, :] * jnp.exp(
        -decay_rates[:, None, :] * (offsets[None, :, None] + 1.0)
    )
    carry_bwd = residues[:, None, :] * jnp.exp(
        -decay_rates[:, None, :] * (span - offsets)[None, :, None]
    )
    decay_factor = jnp.exp(-decay_rates * span)
    return (carry_fwd, carry_bwd, decay_factor)


def block_tables(residues, decay_rates, block_rows):
    offsets = jnp.arange(block_rows).astype(jnp.float32)
    powers = jnp.exp(-decay_rates[:, :, None] * offsets[None, None, :])
    lag_filter = jnp.sum(residues[:, :, None] * powers, axis=1)
    lag_index = jnp.arange(block_rows)[:, None] - jnp.arange(block_rows)[None, :]
    toeplitz = jnp.where(lag_index >= 0, lag_filter[:, jnp.maximum(lag_index, 0)], 0.0)
    carry_fwd, carry_bwd, decay_factor = edge_tables(residues, decay_rates, block_rows)
    return (toeplitz, powers[:, :, ::-1], powers, carry_fwd, carry_bwd, decay_factor)


def forward_local(inputs, tables):
    toeplitz, end_weights, start_weights, carry_fwd, carry_bwd, decay_factor = tables
    local_out = jnp.einsum("gts,bkswg->bktwg", toeplitz, inputs, precision=HIGHEST)
    block_ends = jnp.einsum("gns,bkswg->bknwg", end_weights, inputs, precision=HIGHEST)
    factor = decay_factor.T[:, None, :]

    def forward_advance(carried, block_term):
        return (factor * carried + block_term, carried)

    final_state, entering = lax.scan(
        forward_advance, jnp.zeros_like(block_ends[:, 0]), jnp.moveaxis(block_ends, 1, 0)
    )
    entering = jnp.moveaxis(entering, 0, 1)
    local_out = local_out + jnp.einsum("gjn,bknwg->bkjwg", carry_fwd, entering, precision=HIGHEST)
    return (local_out, final_state)


def backward_local(grads, tables):
    toeplitz, end_weights, start_weights, carry_fwd, carry_bwd, decay_factor = tables
    local_grad = jnp.einsum("gts,bktwg->bkswg", toeplitz, grads, precision=HIGHEST)
    block_starts = jnp.einsum("gnt,bktwg->bknwg", start_weights, grads, precision=HIGHEST)
    factor = decay_factor.T[:, None, :]

    def backward_advance(carried, block_term):
        return (factor * carried + block_term, carried)

    final_adjoint, following = lax.scan(
        backward_advance,
        jnp.zeros_like(block_starts[:, 0]),
        jnp.moveaxis(block_starts, 1, 0),
        reverse=True,
    )
    following = jnp.moveaxis(following, 0, 1)
    local_grad = local_grad + jnp.einsum(
        "gsn,bknwg->bkswg", carry_bwd, following, precision=HIGHEST
    )
    return (local_grad, final_adjoint)


def short_conv(padded, short_filter, count):
    tap_count = short_filter.shape[1]
    total = jnp.zeros((padded.shape[0], count) + padded.shape[2:], jnp.float32)
    for offset in range(tap_count):
        begin = tap_count - 1 - offset
        total = total + short_filter[:, offset, :] * padded[:, begin : begin + count].astype(
            jnp.float32
        )
    return total


def short_conv_grad(ahead, short_filter, count):
    tap_count = short_filter.shape[1]
    total = jnp.zeros((ahead.shape[0], count) + ahead.shape[2:], jnp.float32)
    for offset in range(tap_count):
        total = total + short_filter[:, offset, :] * ahead[:, offset : offset + count]
    return total


def filter_grad(grad_mixed, padded, tap_count, count):
    products = jnp.stack(
        [
            grad_mixed
            * padded[:, tap_count - 1 - offset : tap_count - 1 - offset + count].astype(jnp.float32)
            for offset in range(tap_count)
        ],
        axis=3,
    )
    return jnp.sum(products, axis=(0, 1))


def chains(local_end, local_adjoint, factor):
    wide_factor = factor[:, None, :]

    def forward_turn(turn_index, incoming):
        return passed_along(wide_factor * incoming + local_end, "ctx", 1)

    def backward_turn(turn_index, incoming):
        return passed_along(wide_factor * incoming + local_adjoint, "ctx", -1)

    entering = lax.fori_loop(0, lax.axis_size("ctx") - 1, forward_turn, jnp.zeros_like(local_end))
    arriving = lax.fori_loop(
        0, lax.axis_size("ctx") - 1, backward_turn, jnp.zeros_like(local_adjoint)
    )
    return (entering, arriving)


def local(projected, short_filter, residues, decay_rates, skip_gain, cotangent):
    batch_size = projected.shape[0]
    local_rows = projected.shape[1]
    channels = projected.shape[3]
    tap_count = short_filter.shape[1]
    filter_groups = residues.shape[0]
    group_width = channels // filter_groups
    previous = passed_along(projected[:, local_rows - (tap_count - 1) :], "ctx", 1)
    padded = jnp.concatenate([previous, projected], axis=1)
    mixed = short_conv(padded, short_filter, local_rows)
    query_part = mixed[:, :, 0]
    key_part = mixed[:, :, 1]
    value_part = mixed[:, :, 2]
    gated = key_part * value_part
    tables = block_tables(residues, decay_rates, BLK)
    carry_fwd, carry_bwd, decay_device = edge_tables(residues, decay_rates, local_rows)
    device_factor = decay_device.T
    block_shape = (batch_size, local_rows // BLK, BLK, group_width, filter_groups)
    conv_out, local_end = forward_local(gated.reshape(block_shape), tables)
    upstream = cotangent.astype(jnp.float32)
    grad_filtered = upstream * query_part
    conv_grad, local_adjoint = backward_local(grad_filtered.reshape(block_shape), tables)
    entering, arriving = chains(local_end, local_adjoint, device_factor)
    carried = jnp.einsum("gtn,bnwg->btwg", carry_fwd, entering, precision=HIGHEST)
    filtered = conv_out.reshape(gated.shape) + carried.reshape(gated.shape) + skip_gain * gated
    output = (query_part * filtered).astype(jnp.bfloat16)
    grad_query = upstream * filtered
    returned = jnp.einsum("gsn,bnwg->bswg", carry_bwd, arriving, precision=HIGHEST)
    grad_gated = (
        conv_grad.reshape(gated.shape) + returned.reshape(gated.shape) + skip_gain * grad_filtered
    )
    grad_mixed = jnp.stack([grad_query, grad_gated * value_part, grad_gated * key_part], axis=2)
    following = passed_along(grad_mixed[:, : tap_count - 1], "ctx", -1)
    ahead = jnp.concatenate([grad_mixed, following], axis=1)
    grad_projected = short_conv_grad(ahead, short_filter, local_rows).astype(jnp.bfloat16)
    short_local = filter_grad(grad_mixed, padded, tap_count, local_rows)
    skip_local = jnp.sum(grad_filtered * gated, axis=(0, 1))
    grad_short, grad_skip = lax.psum((short_local, skip_local), ("dp", "ctx"))
    return (output, grad_projected, grad_short, grad_skip)


def solution(mesh):
    placed = (P("dp", "ctx", None, None), P(), P(), P(), P(), P("dp", "ctx", None))
    return jax.shard_map(
        local,
        mesh=mesh,
        in_specs=placed,
        out_specs=(P("dp", "ctx", None), P("dp", "ctx", None, None), P(), P()),
        check_vma=False,
    )
```

profile of v0, /device:TPU:0, one launch (start us, length us, event | category | flops | bytes accessed | tf_op | source)
XLA Modules:
  0.0 766.1 jit_solution(5029338715192167112)
XLA Ops:
  10.8 4.2 fusion.99
  16.9 6.9 multiply_exponential_fusion
  23.8 7.2 rev.3
  31.2 16.8 %gather_fusion = f32[4096,512]{1,0:T(8,128)} fusion(f32[512,64]{0,1:T(8,128)S(1)} %copy.52, s32[4096]{0:T(1024)S(1)} %broadcast_clamp_fusion), kind=kCustom, calls=%fused_computation | custom fusion | bytes 16793600 | tf_op jit(solution)/shard_map/gather | solution.py:35
  48.0 16.2 %copy.53 = f32[64,64,512]{1,0,2:T(8,128)} copy(f32[64,64,512]{2,1,0:T(8,128)} %bitcast.190) | data formatting | bytes 16777216 | tf_op jit(solution)/shard_map/gather | solution.py:35
  64.8 18.8 %fusion.11 = f32[1,128,3,8192]{3,1,2,0:T(8,128)S(1)} fusion(bf16[1,128,3,8192]{3,1,2,0:T(8,128)(2,1)} %param.14, bf16[1,6,3,8192]{3,1,2,0:T(8,128)(2,1)S(1)} %collective-permute-done.2, f32[3,8192]{1,0:T(4,128)S(1)} %get-tuple-element.314, f32[3,8192]{1,0:T(4,128)S(1)} %get-tuple-element.315, f32[3,8192]{1,0:T(4,128)S(1)} %get-tuple-element.316, ...), kind=kLoop, calls=%fused_computation.38 | loop fusion | flops 119537664 | bytes 19857408 | tf_op jit(solution)/shard_map/add | solution.py:84
  84.2 5.6 copy.89
  89.9 9.1 %copy.54 = f32[2,64,16,512]{1,2,0,3:T(8,128)} copy(f32[2,64,16,512]{3,2,1,0:T(8,128)} %bitcast.194) | data formatting | bytes 8388608 | tf_op jit(solution)/shard_map/mul | solution.py:139
  99.0 12.9 %fusion.67 = f32[2,1,16,16,512]{2,3,0,4,1:T(8,128)} fusion(f32[2,64,16,512]{1,2,0,3:T(8,128)} %copy.54, f32[512,16,64]{2,1,0:T(8,128)} %rev.3), kind=kOutput, calls=%fused_computation.117 | convolution fusion | flops 201326592 | bytes 7340032 | tf_op jit(solution)/shard_map/gns,bkswg->bknwg/dot_general | solution.py:43
  111.8 5.4 copy.56
  118.0 7.5 copy.59
  125.5 29.5 %fusion.2 = f32[512,2,16,64]{3,2,1,0:T(8,128)S(1)} fusion(f32[2,64,16,512]{1,2,0,3:T(8,128)} %copy.54, f32[64,64,512]{1,0,2:T(8,128)} %copy.53, pred[64,64]{1,0:T(8,128)(4,1)S(1)} %subtract_compare_fusion), kind=kOutput, calls=%fused_computation.9 | convolution fusion | flops 807403520 | bytes 16781312 | tf_op jit(solution)/shard_map/gts,bkswg->bktwg/dot_general | solution.py:42
  154.9 11.6 %add_bitcast_fusion.1 = f32[1,2,64,16,512]{2,3,1,4,0:T(8,128)} fusion(f32[512,2,16,64]{3,2,1,0:T(8,128)S(1)} %fusion.2, f32[2,16,16,512]{1,2,0,3:T(8,128)S(1)} %copy-done.7, f32[64]{0:T(128)S(1)} %broadcast_add_fusion, f32[512,16]{1,0:T(8,128)S(1)} %copy.51, f32[512,16]{1,0:T(8,128)S(1)} %copy.50), kind=kOutput, calls=%fused_computation.70 | convolution fusion | flops 203423744 | bytes 9502976 | tf_op jit(solution)/shard_map/gjn,bknwg->bkjwg/dot_general | solution.py:53
  166.5 7.6 copy.60
  174.1 5.0 reshape.346
  179.2 67.5 %while.50 = (s32[]{:T(128)}, f32[1,16,16,512]{3,2,1,0:T(8,128)S(1)}, f32[16,512]{1,0:T(8,128)S(1)}, f32[1,16,16,512]{3,2,1,0:T(8,128)S(1)}, s32[]{:T(128)}) while((s32[]{:T(128)}, f32[1,16,16,512]{3,2,1,0:T(8,128)S(1)}, f32[16,512]{1,0:T(8,128)S(1)}, f32[1,16,16,512]{3,2,1,0:T(8,128)S(1)}, s32[]{:T(128)}) %tuple.113), condition=%wide.region_4.5_spmd, body=%wide.region_3.4_spmd.sunk | while | flops 262146 | bytes 3702885 | solution.py:119
  179.3 4.6 collective-permute-start
  185.5 6.5 collective-permute-start
  193.6 9.0 %collective-permute-start = (f32[1,16,16,512]{3,2,1,0:T(8,128)S(1)}, f32[1,16,16,512]{3,2,1,0:T(8,128)S(1)}, u32[]{:S(2)}, u32[]{:S(2)}) collective-permute-start(f32[1,16,16,512]{3,2,1,0:T(8,128)S(1)} %multiply_add_fusion.8), channel_id=1, source_target_pairs={{0,1},{1,2},{2,3},{3,4},{4,5},{5,6},{6,7},{8,9},{9,10},{10,11},{11... | collective-permute-start | bytes 1572872 | tf_op jit(solution)/shard_map/while/body/eval_jaxpr/ppermute | solution.py:15
  204.3 9.0 %collective-permute-start = (f32[1,16,16,512]{3,2,1,0:T(8,128)S(1)}, f32[1,16,16,512]{3,2,1,0:T(8,128)S(1)}, u32[]{:S(2)}, u32[]{:S(2)}) collective-permute-start(f32[1,16,16,512]{3,2,1,0:T(8,128)S(1)} %multiply_add_fusion.8), channel_id=1, source_target_pairs={{0,1},{1,2},{2,3},{3,4},{4,5},{5,6},{6,7},{8,9},{9,10},{10,11},{11... | collective-permute-start | bytes 1572872 | tf_op jit(solution)/shard_map/while/body/eval_jaxpr/ppermute | solution.py:15
  214.9 9.0 %collective-permute-start = (f32[1,16,16,512]{3,2,1,0:T(8,128)S(1)}, f32[1,16,16,512]{3,2,1,0:T(8,128)S(1)}, u32[]{:S(2)}, u32[]{:S(2)}) collective-permute-start(f32[1,16,16,512]{3,2,1,0:T(8,128)S(1)} %multiply_add_fusion.8), channel_id=1, source_target_pairs={{0,1},{1,2},{2,3},{3,4},{4,5},{5,6},{6,7},{8,9},{9,10},{10,11},{11... | collective-permute-start | bytes 1572872 | tf_op jit(solution)/shard_map/while/body/eval_jaxpr/ppermute | solution.py:15
  225.5 9.0 %collective-permute-start = (f32[1,16,16,512]{3,2,1,0:T(8,128)S(1)}, f32[1,16,16,512]{3,2,1,0:T(8,128)S(1)}, u32[]{:S(2)}, u32[]{:S(2)}) collective-permute-start(f32[1,16,16,512]{3,2,1,0:T(8,128)S(1)} %multiply_add_fusion.8), channel_id=1, source_target_pairs={{0,1},{1,2},{2,3},{3,4},{4,5},{5,6},{6,7},{8,9},{9,10},{10,11},{11... | collective-permute-start | bytes 1572872 | tf_op jit(solution)/shard_map/while/body/eval_jaxpr/ppermute | solution.py:15
  236.1 9.0 %collective-permute-start = (f32[1,16,16,512]{3,2,1,0:T(8,128)S(1)}, f32[1,16,16,512]{3,2,1,0:T(8,128)S(1)}, u32[]{:S(2)}, u32[]{:S(2)}) collective-permute-start(f32[1,16,16,512]{3,2,1,0:T(8,128)S(1)} %multiply_add_fusion.8), channel_id=1, source_target_pairs={{0,1},{1,2},{2,3},{3,4},{4,5},{5,6},{6,7},{8,9},{9,10},{10,11},{11... | collective-permute-start | bytes 1572872 | tf_op jit(solution)/shard_map/while/body/eval_jaxpr/ppermute | solution.py:15
  246.6 3.7 copy.63
  250.3 7.5 fusion.77
  257.9 3.3 copy.64
  261.2 5.7 copy.65
  266.8 13.5 %multiply_reduce_fusion = (f32[8192]{0:T(1024)}, f32[1,128,8192]{2,1,0:T(8,128)S(1)}, f32[1,128,1,8192]{3,1,2,0:T(8,128)}, f32[1,128,8192]{2,1,0:T(8,128)}) fusion(f32[1,128,3,8192]{3,1,2,0:T(8,128)} %copy-done.3, bf16[1,128,8192]{2,1,0:T(8,128)(2,1)} %param.19, f32[8192]{0:T(1024)S(1)} %copy-done.24, f32[1,128,8192]{2,1,0:T(8,128)} %reshape.346, ...), kind=kLoop, calls=%fused_computation.96 | loop fusion | flops 9428992 | bytes 35717120 | tf_op jit(solution)/shard_map/reduce_sum | solution.py:162
  282.3 5.2 copy.90
  287.5 9.1 %copy.66 = f32[2,64,16,512]{1,2,0,3:T(8,128)} copy(f32[2,64,16,512]{3,2,1,0:T(8,128)} %bitcast.196) | data formatting | bytes 8388608 | tf_op jit(solution)/shard_map/reshape.31
  296.6 12.2 %fusion.72 = f32[2,1,16,16,512]{2,3,0,4,1:T(8,128)} fusion(f32[2,64,16,512]{1,2,0,3:T(8,128)} %copy.66, f32[64]{0:T(128)S(1)} %iota_convert_fusion, f32[512,16]{1,0:T(8,128)S(1)} %copy.51), kind=kOutput, calls=%fused_computation.118 | convolution fusion | flops 201850880 | bytes 5275904 | tf_op jit(solution)/shard_map/gnt,bktwg->bknwg/dot_general | solution.py:60
  308.9 19.1 %fusion = f32[512,2,16,64]{3,2,1,0:T(8,128)} fusion(f32[2,64,16,512]{1,2,0,3:T(8,128)S(1)} %copy-done.5, f32[64,64,512]{1,0,2:T(8,128)} %copy.53, pred[64,64]{1,0:T(8,128)(4,1)S(1)} %subtract_compare_fusion), kind=kOutput, calls=%fused_computation.7 | convolution fusion | flops 807403520 | bytes 16781312 | tf_op jit(solution)/shard_map/gts,bktwg->bkswg/dot_general | solution.py:59
  328.0 5.6 copy.68
  334.3 7.5 copy.69
  341.8 13.7 %add_bitcast_fusion = f32[1,2,64,16,512]{2,3,1,4,0:T(8,128)} fusion(f32[512,2,16,64]{3,2,1,0:T(8,128)} %fusion, f32[2,16,16,512]{1,2,0,3:T(8,128)} %copy.69, f32[64]{0:T(128)S(1)} %broadcast_subtract_fusion, f32[512,16]{1,0:T(8,128)S(1)} %copy.51, f32[512,16]{1,0:T(8,128)S(1)} %copy.50), kind=kOutput, calls=%fused_computation.69 | convolution fusion | flops 203423744 | bytes 9502976 | tf_op jit(solution)/shard_map/gsn,bknwg->bkswg/dot_general | solution.py:73
  355.6 7.7 %copy.70 = f32[1,2,64,16,512]{4,3,2,1,0:T(8,128)} copy(f32[1,2,64,16,512]{2,3,1,4,0:T(8,128)} %add_bitcast_fusion) | data formatting | bytes 8388608 | tf_op jit(solution)/shard_map/add | solution.py:73
  363.2 5.0 reshape.351
  368.2 75.0 %while.51 = (s32[]{:T(128)}, f32[1,16,16,512]{3,2,1,0:T(8,128)S(1)}, f32[16,512]{1,0:T(8,128)S(1)}, f32[1,16,16,512]{3,2,1,0:T(8,128)S(1)}, s32[]{:T(128)}) while((s32[]{:T(128)}, f32[1,16,16,512]{3,2,1,0:T(8,128)S(1)}, f32[16,512]{1,0:T(8,128)S(1)}, f32[1,16,16,512]{3,2,1,0:T(8,128)S(1)}, s32[]{:T(128)}) %tuple.125), condition=%wide.region_8.9_spmd, body=%wide.region_7.8_spmd.sunk | while | flops 262146 | bytes 3702885 | solution.py:120
  369.7 9.1 %collective-permute-done.1 = f32[1,16,16,512]{3,2,1,0:T(8,128)S(1)} collective-permute-done((f32[1,16,16,512]{3,2,1,0:T(8,128)S(1)}, f32[1,16,16,512]{3,2,1,0:T(8,128)S(1)}, u32[]{:S(2)}, u32[]{:S(2)}) %collective-permute-start.1) | collective-permute-done | bytes 524320 | tf_op jit(solution)/shard_map/while/body/eval_jaxpr/ppermute | solution.py:15
  380.2 9.9 %collective-permute-done.1 = f32[1,16,16,512]{3,2,1,0:T(8,128)S(1)} collective-permute-done((f32[1,16,16,512]{3,2,1,0:T(8,128)S(1)}, f32[1,16,16,512]{3,2,1,0:T(8,128)S(1)}, u32[]{:S(2)}, u32[]{:S(2)}) %collective-permute-start.1) | collective-permute-done | bytes 524320 | tf_op jit(solution)/shard_map/while/body/eval_jaxpr/ppermute | solution.py:15
  391.5 9.2 %collective-permute-done.1 = f32[1,16,16,512]{3,2,1,0:T(8,128)S(1)} collective-permute-done((f32[1,16,16,512]{3,2,1,0:T(8,128)S(1)}, f32[1,16,16,512]{3,2,1,0:T(8,128)S(1)}, u32[]{:S(2)}, u32[]{:S(2)}) %collective-permute-start.1) | collective-permute-done | bytes 524320 | tf_op jit(solution)/shard_map/while/body/eval_jaxpr/ppermute | solution.py:15
  402.2 9.2 %collective-permute-done.1 = f32[1,16,16,512]{3,2,1,0:T(8,128)S(1)} collective-permute-done((f32[1,16,16,512]{3,2,1,0:T(8,128)S(1)}, f32[1,16,16,512]{3,2,1,0:T(8,128)S(1)}, u32[]{:S(2)}, u32[]{:S(2)}) %collective-permute-start.1) | collective-permute-done | bytes 524320 | tf_op jit(solution)/shard_map/while/body/eval_jaxpr/ppermute | solution.py:15
  412.8 9.2 %collective-permute-done.1 = f32[1,16,16,512]{3,2,1,0:T(8,128)S(1)} collective-permute-done((f32[1,16,16,512]{3,2,1,0:T(8,128)S(1)}, f32[1,16,16,512]{3,2,1,0:T(8,128)S(1)}, u32[]{:S(2)}, u32[]{:S(2)}) %collective-permute-start.1) | collective-permute-done | bytes 524320 | tf_op jit(solution)/shard_map/while/body/eval_jaxpr/ppermute | solution.py:15
  423.4 9.2 %collective-permute-done.1 = f32[1,16,16,512]{3,2,1,0:T(8,128)S(1)} collective-permute-done((f32[1,16,16,512]{3,2,1,0:T(8,128)S(1)}, f32[1,16,16,512]{3,2,1,0:T(8,128)S(1)}, u32[]{:S(2)}, u32[]{:S(2)}) %collective-permute-start.1) | collective-permute-done | bytes 524320 | tf_op jit(solution)/shard_map/while/body/eval_jaxpr/ppermute | solution.py:15
  434.0 9.2 %collective-permute-done.1 = f32[1,16,16,512]{3,2,1,0:T(8,128)S(1)} collective-permute-done((f32[1,16,16,512]{3,2,1,0:T(8,128)S(1)}, f32[1,16,16,512]{3,2,1,0:T(8,128)S(1)}, u32[]{:S(2)}, u32[]{:S(2)}) %collective-permute-start.1) | collective-permute-done | bytes 524320 | tf_op jit(solution)/shard_map/while/body/eval_jaxpr/ppermute | solution.py:15
  443.2 3.8 copy.71
  447.0 7.5 fusion.80
  454.5 3.3 copy.72
  457.8 5.9 copy.73
  463.7 10.8 %fusion.51 = (f32[1,128,1,8192]{3,1,2,0:T(8,128)}, f32[1,128,8192]{2,1,0:T(8,128)}) fusion(f32[1,128,3,8192]{3,1,2,0:T(8,128)} %copy-done.3, f32[1,128,8192]{2,1,0:T(8,128)} %copy-done.6, f32[8192]{0:T(1024)S(1)} %copy-done.24, f32[1,128,8192]{2,1,0:T(8,128)} %reshape.351, f32[1,128,8192]{2,1,0:T(8,128)} %copy.73), kind=kLoop, calls=%fused_computation.93 | loop fusion | flops 4194304 | bytes 25198592 | tf_op jit(solution)/shard_map/stack | solution.py:157
  474.5 9.8 %fusion.52 = (f32[1,128,1,8192]{3,1,2,0:T(8,128)}, bf16[1,128,8192]{2,1,0:T(8,128)(2,1)}) fusion(f32[1,128,8192]{2,1,0:T(8,128)} %get-tuple-element.297, f32[1,128,3,8192]{3,1,2,0:T(8,128)} %copy-done.3, f32[1,128,8192]{2,1,0:T(8,128)} %get-tuple-element.299), kind=kLoop, calls=%fused_computation.95 | loop fusion | flops 3145728 | bytes 23068672 | tf_op jit(solution)/shard_map/stack | solution.py:157
  484.3 10.9 %fusion.13 = f32[1,128,3,7,8192]{4,1,2,3,0:T(8,128)} fusion(bf16[1,128,3,8192]{3,1,2,0:T(8,128)(2,1)} %param.14, f32[1,128,1,8192]{3,1,2,0:T(8,128)} %get-tuple-element.300, f32[1,128,1,8192]{3,1,2,0:T(8,128)} %get-tuple-element.296, f32[1,128,1,8192]{3,1,2,0:T(8,128)S(1)} %copy-done), kind=kLoop, calls=%fused_computation.40 | loop fusion | flops 12582911 | bytes 31457280
  495.2 9.3 %pad_maximum_fusion.1 = f32[1,128,3,8192]{3,1,2,0:T(8,128)} fusion(f32[1,128,1,8192]{3,1,2,0:T(8,128)} %get-tuple-element.300, f32[1,128,1,8192]{3,1,2,0:T(8,128)} %get-tuple-element.296, f32[1,128,1,8192]{3,1,2,0:T(8,128)S(1)} %copy-done), kind=kLoop, calls=%fused_computation.66 | loop fusion | flops 6291456 | bytes 25165824 | tf_op jit(solution)/shard_map/stack | solution.py:157
  508.0 11.8 %fusion.15 = f32[1,128,3,7,8192]{4,1,2,3,0:T(8,128)} fusion(f32[1,128,3,7,8192]{4,1,2,3,0:T(8,128)} %fusion.13, bf16[1,128,3,8192]{3,1,2,0:T(8,128)(2,1)} %param.14, bf16[1,6,3,8192]{3,1,2,0:T(8,128)(2,1)S(1)} %copy-done.9, f32[1,128,1,8192]{3,1,2,0:T(8,128)} %get-tuple-element.300, f32[1,128,1,8192]{3,1,2,0:T(8,128)} %get-tuple-element.296, ...), kind=kLoop, calls=%fused_computation.42 | loop fusion | flops 22020096 | bytes 31752192
  519.8 5.4 fusion.17
  525.2 5.3 fusion.19
  530.6 5.5 fusion.21
  536.0 5.3 fusion.23
  541.4 5.4 fusion.25
  546.8 27.9 %reduce_sum.28 = f32[3,7,8192]{2,0,1:T(4,128)} reduce(f32[1,128,3,7,8192]{4,1,2,3,0:T(8,128)} %fusion.25, f32[]{:T(128)} %constant.65.clone.1), dimensions={0,1}, to_apply=%region_9.10 | reduce | flops 21848064 | bytes 88768512 | tf_op jit(solution)/shard_map/reduce_sum | solution.py:107
  574.8 48.0 %psum.15 = f32[8192]{0:T(1024)} all-reduce(f32[8192]{0:T(1024)S(1)} %copy-done.25), channel_id=1, replica_groups=mesh['dp'=4,'ctx'=8] {'dp','ctx'}, use_global_device_ids=true, to_apply=%region_12.13 | all-reduce | flops 8192 | bytes 65536 | tf_op jit(solution)/shard_map/psum | solution.py:163
  622.8 89.6 %all-reduce.2.cloned.1.call-done = f32[3,7,8192]{2,0,1:T(4,128)} async-done(((f32[3,7,8192]{2,0,1:T(4,128)}), f32[3,7,8192]{2,0,1:T(4,128)}) %all-reduce.2.cloned.1.call-update) | async-done | bytes 688144 | tf_op jit(solution)/shard_map/psum | solution.py:163
  715.4 9.8 %pad_maximum_fusion = f32[1,134,3,8192]{3,1,2,0:T(8,128)} fusion(f32[1,6,3,8192]{3,1,2,0:T(8,128)S(1)} %copy.75, f32[1,128,1,8192]{3,1,2,0:T(8,128)} %get-tuple-element.300, f32[1,128,1,8192]{3,1,2,0:T(8,128)} %get-tuple-element.296, f32[1,128,1,8192]{3,1,2,0:T(8,128)} %get-tuple-element.298), kind=kLoop, calls=%fused_computation.32 | loop fusion | flops 9879552 | bytes 26345472 | tf_op jit(solution)/shard_map/concatenate | solution.py:159
  725.2 33.6 %fusion.27 = bf16[1,128,3,8192]{3,1,2,0:T(8,128)(2,1)} fusion(f32[1,134,3,8192]{3,1,2,0:T(8,128)} %pad_maximum_fusion, f32[3,8192]{1,0:T(4,128)S(1)} %copy-done.13, f32[3,8192]{1,0:T(4,128)S(1)} %copy-done.15, f32[3,8192]{1,0:T(4,128)S(1)} %copy-done.17, f32[3,8192]{1,0:T(4,128)S(1)} %copy-done.19, f32[3,8192]{1,0:T(4,128)S(1)} %copy-done.21, ...), kind=kLoop, calls=%fused_computation.55 | loop fusion | flops 50331648 | bytes 95059968 | tf_op jit(solution)/shard_map/convert_element_type | solution.py:160
  (130 shorter events, 38.4 us)
Async XLA Ops:
  7.2 705.3 %all-reduce.2.cloned.1.call-start = ((), (), s32[]{:S(2)}) async-start(), calls=%async_computation | async-start | bytes 1835008 | tf_op jit(solution)/shard_map/psum | solution.py:163
  8.3 56.5 %collective-permute-start.2 = (bf16[1,6,3,8192]{3,1,2,0:T(8,128)(2,1)S(1)}, bf16[1,6,3,8192]{3,1,2,0:T(8,128)(2,1)S(1)}, u32[]{:S(2)}, u32[]{:S(2)}) collective-permute-start(bf16[1,6,3,8192]{3,1,2,0:T(8,128)(2,1)S(1)} %slice.87), channel_id=1, source_target_pairs={{0,1},{1,2},{2,3},{3,4},{4,5},{5,6},{6,7},{8,9},{9,10},{10,11},{11... | collective-permute-start | bytes 884744 | tf_op jit(solution)/shard_map/ppermute | solution.py:15
  15.0 49.8 %copy-start.10 = (f32[3,1,8192]{2,0,1:T(4,128)}, f32[3,1,8192]{2,0,1:T(4,128)S(1)}, u32[]{:S(2)}) copy-start(f32[3,1,8192]{2,0,1:T(4,128)S(1)} %copy.98) | copy-start | bytes 294916
  64.4 19.2 %copy-start.12 = (f32[3,8192]{1,0:T(4,128)}, f32[3,8192]{1,0:T(4,128)S(1)}, u32[]{:S(2)}) copy-start(f32[3,8192]{1,0:T(4,128)S(1)} %get-tuple-element.314) | copy-start | bytes 294916
  64.4 19.2 %copy-start.14 = (f32[3,8192]{1,0:T(4,128)}, f32[3,8192]{1,0:T(4,128)S(1)}, u32[]{:S(2)}) copy-start(f32[3,8192]{1,0:T(4,128)S(1)} %get-tuple-element.315) | copy-start | bytes 294916
  64.6 19.1 %copy-start.16 = (f32[3,8192]{1,0:T(4,128)}, f32[3,8192]{1,0:T(4,128)S(1)}, u32[]{:S(2)}) copy-start(f32[3,8192]{1,0:T(4,128)S(1)} %get-tuple-element.316) | copy-start | bytes 294916
  64.6 19.1 %copy-start.18 = (f32[3,8192]{1,0:T(4,128)}, f32[3,8192]{1,0:T(4,128)S(1)}, u32[]{:S(2)}) copy-start(f32[3,8192]{1,0:T(4,128)S(1)} %get-tuple-element.317) | copy-start | bytes 294916
  64.7 19.0 %copy-start.20 = (f32[3,8192]{1,0:T(4,128)}, f32[3,8192]{1,0:T(4,128)S(1)}, u32[]{:S(2)}) copy-start(f32[3,8192]{1,0:T(4,128)S(1)} %get-tuple-element.318) | copy-start | bytes 294916
  64.7 19.0 %copy-start.22 = (f32[3,8192]{1,0:T(4,128)}, f32[3,8192]{1,0:T(4,128)S(1)}, u32[]{:S(2)}) copy-start(f32[3,8192]{1,0:T(4,128)S(1)} %get-tuple-element.319) | copy-start | bytes 294916
  64.8 18.9 %copy-start.8 = (bf16[1,6,3,8192]{3,1,2,0:T(8,128)(2,1)}, bf16[1,6,3,8192]{3,1,2,0:T(8,128)(2,1)S(1)}, u32[]{:S(2)}) copy-start(bf16[1,6,3,8192]{3,1,2,0:T(8,128)(2,1)S(1)} %collective-permute-done.2) | copy-start | bytes 884740
  83.7 6.2 copy-start.3
  125.5 29.5 %copy-start.7 = (f32[2,16,16,512]{1,2,0,3:T(8,128)S(1)}, f32[2,16,16,512]{1,2,0,3:T(8,128)}, u32[]{:S(2)}) copy-start(f32[2,16,16,512]{1,2,0,3:T(8,128)} %copy.59) | copy-start | bytes 3145732
  179.3 6.1 collective-permute-start
  185.5 8.0 %collective-permute-start = (f32[1,16,16,512]{3,2,1,0:T(8,128)S(1)}, f32[1,16,16,512]{3,2,1,0:T(8,128)S(1)}, u32[]{:S(2)}, u32[]{:S(2)}) collective-permute-start(f32[1,16,16,512]{3,2,1,0:T(8,128)S(1)} %multiply_add_fusion.8), channel_id=1, source_target_pairs={{0,1},{1,2},{2,3},{3,4},{4,5},{5,6},{6,7},{8,9},{9,10},{10,11},{11... | collective-permute-start | bytes 1572872 | tf_op jit(solution)/shard_map/while/body/eval_jaxpr/ppermute | solution.py:15
  193.6 10.5 %collective-permute-start = (f32[1,16,16,512]{3,2,1,0:T(8,128)S(1)}, f32[1,16,16,512]{3,2,1,0:T(8,128)S(1)}, u32[]{:S(2)}, u32[]{:S(2)}) collective-permute-start(f32[1,16,16,512]{3,2,1,0:T(8,128)S(1)} %multiply_add_fusion.8), channel_id=1, source_target_pairs={{0,1},{1,2},{2,3},{3,4},{4,5},{5,6},{6,7},{8,9},{9,10},{10,11},{11... | collective-permute-start | bytes 1572872 | tf_op jit(solution)/shard_map/while/body/eval_jaxpr/ppermute | solution.py:15
  204.3 10.5 %collective-permute-start = (f32[1,16,16,512]{3,2,1,0:T(8,128)S(1)}, f32[1,16,16,512]{3,2,1,0:T(8,128)S(1)}, u32[]{:S(2)}, u32[]{:S(2)}) collective-permute-start(f32[1,16,16,512]{3,2,1,0:T(8,128)S(1)} %multiply_add_fusion.8), channel_id=1, source_target_pairs={{0,1},{1,2},{2,3},{3,4},{4,5},{5,6},{6,7},{8,9},{9,10},{10,11},{11... | collective-permute-start | bytes 1572872 | tf_op jit(solution)/shard_map/while/body/eval_jaxpr/ppermute | solution.py:15
  214.9 10.5 %collective-permute-start = (f32[1,16,16,512]{3,2,1,0:T(8,128)S(1)}, f32[1,16,16,512]{3,2,1,0:T(8,128)S(1)}, u32[]{:S(2)}, u32[]{:S(2)}) collective-permute-start(f32[1,16,16,512]{3,2,1,0:T(8,128)S(1)} %multiply_add_fusion.8), channel_id=1, source_target_pairs={{0,1},{1,2},{2,3},{3,4},{4,5},{5,6},{6,7},{8,9},{9,10},{10,11},{11... | collective-permute-start | bytes 1572872 | tf_op jit(solution)/shard_map/while/body/eval_jaxpr/ppermute | solution.py:15
  225.5 10.5 %collective-permute-start = (f32[1,16,16,512]{3,2,1,0:T(8,128)S(1)}, f32[1,16,16,512]{3,2,1,0:T(8,128)S(1)}, u32[]{:S(2)}, u32[]{:S(2)}) collective-permute-start(f32[1,16,16,512]{3,2,1,0:T(8,128)S(1)} %multiply_add_fusion.8), channel_id=1, source_target_pairs={{0,1},{1,2},{2,3},{3,4},{4,5},{5,6},{6,7},{8,9},{9,10},{10,11},{11... | collective-permute-start | bytes 1572872 | tf_op jit(solution)/shard_map/while/body/eval_jaxpr/ppermute | solution.py:15
  236.1 10.5 %collective-permute-start = (f32[1,16,16,512]{3,2,1,0:T(8,128)S(1)}, f32[1,16,16,512]{3,2,1,0:T(8,128)S(1)}, u32[]{:S(2)}, u32[]{:S(2)}) collective-permute-start(f32[1,16,16,512]{3,2,1,0:T(8,128)S(1)} %multiply_add_fusion.8), channel_id=1, source_target_pairs={{0,1},{1,2},{2,3},{3,4},{4,5},{5,6},{6,7},{8,9},{9,10},{10,11},{11... | collective-permute-start | bytes 1572872 | tf_op jit(solution)/shard_map/while/body/eval_jaxpr/ppermute | solution.py:15
  257.9 9.0 %copy-start.24 = (f32[8192]{0:T(1024)S(1)}, f32[8192]{0:T(1024)}, u32[]{:S(2)}) copy-start(f32[8192]{0:T(1024)} %param.18) | copy-start | bytes 98308
  280.3 2.0 copy-start.6
  296.6 12.2 %copy-start.5 = (f32[2,64,16,512]{1,2,0,3:T(8,128)S(1)}, f32[2,64,16,512]{1,2,0,3:T(8,128)}, u32[]{:S(2)}) copy-start(f32[2,64,16,512]{1,2,0,3:T(8,128)} %copy.66) | copy-start | bytes 12582916
  328.0 5.7 copy-start.4
  368.4 10.4 %collective-permute-start.1 = (f32[1,16,16,512]{3,2,1,0:T(8,128)S(1)}, f32[1,16,16,512]{3,2,1,0:T(8,128)S(1)}, u32[]{:S(2)}, u32[]{:S(2)}) collective-permute-start(f32[1,16,16,512]{3,2,1,0:T(8,128)S(1)} %multiply_add_fusion.9), channel_id=1, source_target_pairs={{1,0},{2,1},{3,2},{4,3},{5,4},{6,5},{7,6},{9,8},{10,9},{11,10},{12... | collective-permute-start | bytes 1572872 | tf_op jit(solution)/shard_map/while/body/eval_jaxpr/ppermute | solution.py:15
  378.9 11.2 %collective-permute-start.1 = (f32[1,16,16,512]{3,2,1,0:T(8,128)S(1)}, f32[1,16,16,512]{3,2,1,0:T(8,128)S(1)}, u32[]{:S(2)}, u32[]{:S(2)}) collective-permute-start(f32[1,16,16,512]{3,2,1,0:T(8,128)S(1)} %multiply_add_fusion.9), channel_id=1, source_target_pairs={{1,0},{2,1},{3,2},{4,3},{5,4},{6,5},{7,6},{9,8},{10,9},{11,10},{12... | collective-permute-start | bytes 1572872 | tf_op jit(solution)/shard_map/while/body/eval_jaxpr/ppermute | solution.py:15
  390.2 10.5 %collective-permute-start.1 = (f32[1,16,16,512]{3,2,1,0:T(8,128)S(1)}, f32[1,16,16,512]{3,2,1,0:T(8,128)S(1)}, u32[]{:S(2)}, u32[]{:S(2)}) collective-permute-start(f32[1,16,16,512]{3,2,1,0:T(8,128)S(1)} %multiply_add_fusion.9), channel_id=1, source_target_pairs={{1,0},{2,1},{3,2},{4,3},{5,4},{6,5},{7,6},{9,8},{10,9},{11,10},{12... | collective-permute-start | bytes 1572872 | tf_op jit(solution)/shard_map/while/body/eval_jaxpr/ppermute | solution.py:15
  400.9 10.5 %collective-permute-start.1 = (f32[1,16,16,512]{3,2,1,0:T(8,128)S(1)}, f32[1,16,16,512]{3,2,1,0:T(8,128)S(1)}, u32[]{:S(2)}, u32[]{:S(2)}) collective-permute-start(f32[1,16,16,512]{3,2,1,0:T(8,128)S(1)} %multiply_add_fusion.9), channel_id=1, source_target_pairs={{1,0},{2,1},{3,2},{4,3},{5,4},{6,5},{7,6},{9,8},{10,9},{11,10},{12... | collective-permute-start | bytes 1572872 | tf_op jit(solution)/shard_map/while/body/eval_jaxpr/ppermute | solution.py:15
  411.5 10.5 %collective-permute-start.1 = (f32[1,16,16,512]{3,2,1,0:T(8,128)S(1)}, f32[1,16,16,512]{3,2,1,0:T(8,128)S(1)}, u32[]{:S(2)}, u32[]{:S(2)}) collective-permute-start(f32[1,16,16,512]{3,2,1,0:T(8,128)S(1)} %multiply_add_fusion.9), channel_id=1, source_target_pairs={{1,0},{2,1},{3,2},{4,3},{5,4},{6,5},{7,6},{9,8},{10,9},{11,10},{12... | collective-permute-start | bytes 1572872 | tf_op jit(solution)/shard_map/while/body/eval_jaxpr/ppermute | solution.py:15
  422.1 10.5 %collective-permute-start.1 = (f32[1,16,16,512]{3,2,1,0:T(8,128)S(1)}, f32[1,16,16,512]{3,2,1,0:T(8,128)S(1)}, u32[]{:S(2)}, u32[]{:S(2)}) collective-permute-start(f32[1,16,16,512]{3,2,1,0:T(8,128)S(1)} %multiply_add_fusion.9), channel_id=1, source_target_pairs={{1,0},{2,1},{3,2},{4,3},{5,4},{6,5},{7,6},{9,8},{10,9},{11,10},{12... | collective-permute-start | bytes 1572872 | tf_op jit(solution)/shard_map/while/body/eval_jaxpr/ppermute | solution.py:15
  432.7 10.5 %collective-permute-start.1 = (f32[1,16,16,512]{3,2,1,0:T(8,128)S(1)}, f32[1,16,16,512]{3,2,1,0:T(8,128)S(1)}, u32[]{:S(2)}, u32[]{:S(2)}) collective-permute-start(f32[1,16,16,512]{3,2,1,0:T(8,128)S(1)} %multiply_add_fusion.9), channel_id=1, source_target_pairs={{1,0},{2,1},{3,2},{4,3},{5,4},{6,5},{7,6},{9,8},{10,9},{11,10},{12... | collective-permute-start | bytes 1572872 | tf_op jit(solution)/shard_map/while/body/eval_jaxpr/ppermute | solution.py:15
  474.5 9.8 %copy-start = (f32[1,128,1,8192]{3,1,2,0:T(8,128)S(1)}, f32[1,128,1,8192]{3,1,2,0:T(8,128)}, u32[]{:S(2)}) copy-start(f32[1,128,1,8192]{3,1,2,0:T(8,128)} %get-tuple-element.298) | copy-start | bytes 12582916
  495.2 12.7 %copy-start.9 = (bf16[1,6,3,8192]{3,1,2,0:T(8,128)(2,1)S(1)}, bf16[1,6,3,8192]{3,1,2,0:T(8,128)(2,1)}, u32[]{:S(2)}) copy-start(bf16[1,6,3,8192]{3,1,2,0:T(8,128)(2,1)} %copy-done.8) | copy-start | bytes 884740
  505.7 14.1 %slice-start = ((s8[6291456]{0:T(1024)(128)(4,1)}), s8[4194304]{0:T(1024)(128)(4,1)S(1)}, s32[]{:S(2)}) async-start(s8[6291456]{0:T(1024)(128)(4,1)} %bitcast.188), calls=%async_computation.1 | async-start | bytes 8388608
  506.4 13.4 %copy-start.1 = (f32[1,128,1,8192]{3,1,2,0:T(8,128)S(1)}, f32[1,128,1,8192]{3,1,2,0:T(8,128)}, u32[]{:S(2)}) copy-start(f32[1,128,1,8192]{3,1,2,0:T(8,128)} %get-tuple-element.296) | copy-start | bytes 12582916
  506.4 13.4 %copy-start.2 = (f32[1,128,1,8192]{3,1,2,0:T(8,128)S(1)}, f32[1,128,1,8192]{3,1,2,0:T(8,128)}, u32[]{:S(2)}) copy-start(f32[1,128,1,8192]{3,1,2,0:T(8,128)} %get-tuple-element.300) | copy-start | bytes 12582916
  506.4 13.4 %slice-start.1 = ((s8[6291456]{0:T(1024)(128)(4,1)}), s8[2097152]{0:T(1024)(128)(4,1)S(1)}, s32[]{:S(2)}) async-start(s8[6291456]{0:T(1024)(128)(4,1)} %bitcast.188), calls=%async_computation.2 | async-start | bytes 4194304
  506.4 208.6 %collective-permute-start.3 = (f32[1,6,3,8192]{3,0,2,1:T(1,128)S(1)}, f32[1,6,3,8192]{3,0,2,1:T(1,128)S(1)}, u32[]{:S(2)}, u32[]{:S(2)}) collective-permute-start(f32[1,6,3,8192]{3,0,2,1:T(1,128)S(1)} %copy.74), channel_id=1, source_target_pairs={{1,0},{2,1},{3,2},{4,3},{5,4},{6,5},{7,6},{9,8},{10,9},{11,10},{12... | collective-permute-start | bytes 1769480 | tf_op jit(solution)/shard_map/ppermute | solution.py:15
  546.8 28.0 %copy-start.25 = (f32[8192]{0:T(1024)S(1)}, f32[8192]{0:T(1024)}, u32[]{:S(2)}) copy-start(f32[8192]{0:T(1024)} %get-tuple-element.292) | copy-start | bytes 98308
  715.3 9.9 %copy-start.11 = (f32[3,1,8192]{2,0,1:T(4,128)S(1)}, f32[3,1,8192]{2,0,1:T(4,128)}, u32[]{:S(2)}) copy-start(f32[3,1,8192]{2,0,1:T(4,128)} %copy-done.10) | copy-start | bytes 294916
  715.3 9.9 %copy-start.13 = (f32[3,8192]{1,0:T(4,128)S(1)}, f32[3,8192]{1,0:T(4,128)}, u32[]{:S(2)}) copy-start(f32[3,8192]{1,0:T(4,128)} %copy-done.12) | copy-start | bytes 294916
  715.3 9.9 %copy-start.15 = (f32[3,8192]{1,0:T(4,128)S(1)}, f32[3,8192]{1,0:T(4,128)}, u32[]{:S(2)}) copy-start(f32[3,8192]{1,0:T(4,128)} %copy-done.14) | copy-start | bytes 294916
  715.3 9.9 %copy-start.17 = (f32[3,8192]{1,0:T(4,128)S(1)}, f32[3,8192]{1,0:T(4,128)}, u32[]{:S(2)}) copy-start(f32[3,8192]{1,0:T(4,128)} %copy-done.16) | copy-start | bytes 294916
  715.3 9.9 %copy-start.19 = (f32[3,8192]{1,0:T(4,128)S(1)}, f32[3,8192]{1,0:T(4,128)}, u32[]{:S(2)}) copy-start(f32[3,8192]{1,0:T(4,128)} %copy-done.18) | copy-start | bytes 294916
  715.4 9.9 %copy-start.21 = (f32[3,8192]{1,0:T(4,128)S(1)}, f32[3,8192]{1,0:T(4,128)}, u32[]{:S(2)}) copy-start(f32[3,8192]{1,0:T(4,128)} %copy-done.20) | copy-start | bytes 294916
  715.4 9.9 %copy-start.23 = (f32[3,8192]{1,0:T(4,128)S(1)}, f32[3,8192]{1,0:T(4,128)}, u32[]{:S(2)}) copy-start(f32[3,8192]{1,0:T(4,128)} %copy-done.22) | copy-start | bytes 294916
Sparse Core Ops, SparseCore 0:
  574.9 137.5 all-reduce.1
where the time goes:
time: 777 us; the launch traced here: 766 us
  other arithmetic  194 us (25%)
  waiting for transfers between devices  165 us (21%)
  local copies, waits for them, and re-layouts  160 us (21%)
  matrix products  114 us (15%)
  starting transfers between devices  69.2 us (9%)
  blocking collectives  48 us (6%)
  between operations  15.1 us (2%)
    psum x1, waiting for transfers between devices, local(): grad_short, grad_skip = lax.psum((short_local, skip_local), ('dp', 'ctx'))  89.6 us
    ppermute x16, waiting for transfers between devices, passed_along(): lax.ppermute(value, axis, [(source, source + steps) for source in range(f...  75.4 us
    ppermute x16, starting transfers between devices, passed_along(): lax.ppermute(value, axis, [(source, source + steps) for source in range(f...  69.2 us
    psum x1, blocking collectives, local(): grad_short, grad_skip = lax.psum((short_local, skip_local), ('dp', 'ctx'))  48 us
    unnamed x9, other arithmetic  44.3 us
    convert_element_type x1, other arithmetic, local(): short_conv_grad(ahead, short_filter, local_rows).astype(jnp.bfloat16)  33.6 us
    gather x2, local copies, waits for them, and re-layouts, block_tables(): lag_filter[:, jnp.maximum(lag_index, 0)]  33.1 us
    another operation x9, local copies, waits for them, and re-layouts  32 us
  transfers between devices with their start and end apart: 17, of which 15 were waited for; matrix products, arithmetic and copies ran while one was open for 16% of the time, Pallas kernels for 0%

commit v1 on v0

v1 whole, which is shorter than its diff:
```python
import functools

import jax
import jax.numpy as jnp
import numpy as np
from jax import lax
from jax.experimental import pallas as pl
from jax.experimental.pallas import tpu as pltpu
from jax.sharding import PartitionSpec as P

LANES = 128
SUB = 8
F32 = jnp.float32
BF16 = jnp.bfloat16


def split(value):
    high = value.astype(BF16)
    return high, (value - high.astype(F32)).astype(BF16)


def fourier(rows):
    run = rows // SUB
    row = np.arange(rows)
    time = run * (row % SUB) + row // SUB
    angle = 2.0 * np.pi * (np.arange(rows)[:, None] + 0.5) * time[None, :] / (2 * rows)
    ahead = np.concatenate([np.cos(angle), -np.sin(angle)], axis=0)
    back = ahead.T / rows
    return ahead.astype(np.float32), back.astype(np.float32)


def states_kernel(p, hb, ha, u, filt, f1, we, wb, qkvg, e_out, a_out, xs):
    rows = p.shape[1]
    run = rows // SUB
    taps = filt.shape[1]
    poles = f1.shape[0]

    def tile(lt, carry):
        lanes = pl.ds(pl.multiple_of(lt * LANES, LANES), LANES)
        for j in range(3):
            xs[j, 0:SUB] = hb[j, :, lanes].astype(F32)
            xs[j, SUB : SUB + rows] = p[j, :, lanes].astype(F32)
            xs[j, SUB + rows :] = ha[j, :, lanes].astype(F32)
        xs[3, SUB : SUB + rows] = u[:, lanes].astype(F32)
        xs[3, SUB + rows :] = ha[3, :, lanes].astype(F32)
        for j in range(3):
            tap = [filt[j, i : i + 1, lanes] for i in range(taps)]
            view = [xs[j, pl.ds(SUB + a, SUB, stride=run), :] for a in range(1 - taps, run)]
            for a in range(run):
                total = tap[0] * view[a + taps - 1]
                for i in range(1, taps):
                    total = total + tap[i] * view[a + taps - 1 - i]
                qkvg[j, SUB * a : SUB * a + SUB, lanes] = total
            total = tap[0] * xs[j, SUB + rows : 2 * SUB + rows]
            for i in range(1, taps):
                total = total + tap[i] * xs[j, SUB + rows - i : 2 * SUB + rows - i]
            qkvg[j, rows : rows + SUB, lanes] = total
        for a in range(run):
            at = slice(SUB * a, SUB * a + SUB)
            qkvg[3, at, lanes] = xs[3, pl.ds(SUB + a, SUB, stride=run), :] * qkvg[0, at, lanes]
        at = slice(rows, rows + SUB)
        qkvg[3, at, lanes] = xs[3, SUB + rows :] * qkvg[0, at, lanes]
        decay = [jnp.broadcast_to(f1[n : n + 1, lanes], (SUB, LANES)) for n in range(poles)]
        for order, weight, out in ((range(run), we, e_out), (range(run - 1, -1, -1), wb, a_out)):
            state = None
            for a in order:
                at = slice(SUB * a, SUB * a + SUB)
                if out is e_out:
                    value = qkvg[1, at, lanes] * qkvg[2, at, lanes]
                else:
                    value = qkvg[3, at, lanes]
                if state is None:
                    state = [value] * poles
                else:
                    state = [decay[n] * state[n] + value for n in range(poles)]
            for n in range(poles):
                out[0, n : n + 1, lanes] = jnp.sum(
                    state[n] * weight[n, :, lanes], axis=0, keepdims=True
                )
        return carry

    lax.fori_loop(0, p.shape[2] // LANES, tile, 0)


def long_kernel(qkvg, lag, fwd, fwd_hi, inv_hi, inv_lo, conv, convg, spectrum):
    rows = conv.shape[0]

    def transform(value):
        high, low = split(value)
        both = jnp.concatenate([high, high], axis=0)
        return jnp.dot(fwd[...], both, preferred_element_type=F32) + jnp.dot(
            fwd_hi[...], low, preferred_element_type=F32
        )

    def inverse(real, imag):
        high, low = split(jnp.concatenate([real, imag], axis=0))
        return (
            jnp.dot(inv_hi[...], high, preferred_element_type=F32)
            + jnp.dot(inv_lo[...], high, preferred_element_type=F32)
            + jnp.dot(inv_hi[...], low, preferred_element_type=F32)
        )

    @pl.when(pl.program_id(0) == 0)
    def _():
        spectrum[...] = transform(lag[...])

    h_re = spectrum[0:rows]
    h_im = spectrum[rows:]
    x = transform(qkvg[1, 0:rows] * qkvg[2, 0:rows])
    x_re, x_im = x[0:rows], x[rows:]
    conv[...] = inverse(h_re * x_re - h_im * x_im, h_re * x_im + h_im * x_re)
    x = transform(qkvg[3, 0:rows])
    x_re, x_im = x[0:rows], x[rows:]
    convg[...] = inverse(h_re * x_re + h_im * x_im, h_re * x_im - h_im * x_re)


def final_kernel(
    p, hb, u, ha, qkvg, conv, convg, enter, arrive, ends, filt, skip, f1, f_all, cz, cy, ce, cb,
    near, output, grad_p, sums, ps, us, gs, os, es
):
    rows = p.shape[1]
    run = rows // SUB
    taps = filt.shape[1]
    poles = f1.shape[0]
    main = slice(0, rows)
    beyond = slice(rows, rows + SUB)

    def tile(lt, carry):
        lanes = pl.ds(pl.multiple_of(lt * LANES, LANES), LANES)
        for j in range(3):
            ps[j, 0:SUB] = hb[j, :, lanes].astype(F32)
            ps[j, SUB : SUB + rows] = p[j, :, lanes].astype(F32)
        us[...] = u[:, lanes].astype(F32)
        gain = skip[0:1, lanes]
        decay = [jnp.broadcast_to(f1[n : n + 1, lanes], (SUB, LANES)) for n in range(poles)]

        state = [cz[n, :, lanes] * enter[0, n : n + 1, lanes] for n in range(poles)]
        skip_sum = jnp.zeros((SUB, LANES), F32)
        for a in range(run):
            at = slice(SUB * a, SUB * a + SUB)
            gated = qkvg[1, at, lanes] * qkvg[2, at, lanes]
            skip_sum = skip_sum + gated * qkvg[3, at, lanes]
            filtered = conv[at, lanes] + gain * gated
            terms = list(state)
            while len(terms) > 1:
                terms = [sum(terms[k : k + 2][1:], terms[k]) for k in range(0, len(terms), 2)]
            filtered = filtered + terms[0]
            spread = pl.ds(a, SUB, stride=run)
            os[spread, :] = qkvg[0, at, lanes] * filtered
            gs[0, spread, :] = us[spread, :] * filtered
            if a + 1 < run:
                state = [state[n] * decay[n] for n in range(poles)]
        output[:, lanes] = os[...].astype(BF16)
        es[0:SUB] = jnp.zeros((SUB, LANES), F32)
        es[SUB:] = qkvg[1, beyond, lanes] * qkvg[2, beyond, lanes]
        total = (near[taps : taps + 1, lanes] + gain) * es[SUB:]
        for m in range(1, taps - 1):
            total = total + near[taps + m : taps + m + 1, lanes] * es[SUB - m : 2 * SUB - m]
        for n in range(poles):
            at_end = ends[0, n : n + 1, lanes] + f_all[n : n + 1, lanes] * enter[0, n : n + 1, lanes]
            total = total + ce[n, :, lanes] * at_end
        gs[0, beyond] = ha[3, :, lanes].astype(F32) * total

        state = [cy[n, :, lanes] * arrive[0, n : n + 1, lanes] for n in range(poles)]
        for a in range(run - 1, -1, -1):
            at = slice(SUB * a, SUB * a + SUB)
            terms = list(state)
            while len(terms) > 1:
                terms = [sum(terms[k : k + 2][1:], terms[k]) for k in range(0, len(terms), 2)]
            grad = convg[at, lanes] + gain * qkvg[3, at, lanes] + terms[0]
            spread = pl.ds(a, SUB, stride=run)
            gs[1, spread, :] = grad * qkvg[2, at, lanes]
            gs[2, spread, :] = grad * qkvg[1, at, lanes]
            if a:
                state = [state[n] * decay[n] for n in range(poles)]
        es[SUB:] = qkvg[3, beyond, lanes]
        total = gain * es[SUB:]
        for m in range(1, taps - 1):
            total = total - near[taps - m : taps - m + 1, lanes] * es[SUB - m : 2 * SUB - m]
        for n in range(poles):
            total = total + cb[n, :, lanes] * arrive[0, n : n + 1, lanes]
        gs[1, beyond] = total * qkvg[2, beyond, lanes]
        gs[2, beyond] = total * qkvg[1, beyond, lanes]

        for j in range(3):
            tap = [filt[j, i : i + 1, lanes] for i in range(taps)]
            grads = [gs[j, pl.ds(a, SUB, stride=run), :] for a in range(run + taps - 1)]
            views = [ps[j, pl.ds(SUB + a, SUB, stride=run), :] for a in range(1 - taps, run)]
            sums_of = [None] * taps
            for a in range(run):
                total = tap[0] * grads[a]
                for i in range(1, taps):
                    total = total + tap[i] * grads[a + i]
                os[pl.ds(a, SUB, stride=run), :] = total
                for i in range(taps):
                    term = grads[a] * views[a + taps - 1 - i]
                    sums_of[i] = term if a == 0 else sums_of[i] + term
            grad_p[j, :, lanes] = os[...].astype(BF16)
            for i in range(taps):
                at = j * taps + i
                sums[0, at : at + 1, lanes] = jnp.sum(sums_of[i], axis=0, keepdims=True)
        at = 3 * taps
        sums[0, at : at + 1, lanes] = jnp.sum(skip_sum, axis=0, keepdims=True)
        return carry

    lax.fori_loop(0, p.shape[2] // LANES, tile, 0)


def shifted(value, axis, steps):
    count = lax.axis_size(axis)
    first, last = (max(0, -steps), min(count, count - steps))
    return lax.ppermute(value, axis, [(source, source + steps) for source in range(first, last)])


def rotated(value, axis, steps):
    count = lax.axis_size(axis)
    return lax.ppermute(value, axis, [(s, (s + steps) % count) for s in range(count)])


def swapped(value):
    count = lax.axis_size("ctx")
    return lax.ppermute(value, "ctx", [(s, s ^ 1) for s in range(count)])


def exchange(ends, adjoints, f_all):
    chips = lax.axis_size("ctx") // 2
    core = lax.rem(lax.axis_index("ctx"), 2)
    half = ends.shape[0] // 2
    other_ends, other_adjoints = swapped(ends), swapped(adjoints)
    mine = lambda value: lax.dynamic_slice_in_dim(value, core * half, half, 0)
    first = core == 0
    my_e, my_a = mine(ends), mine(adjoints)
    their_e, their_a = mine(other_ends), mine(other_adjoints)
    chip_e = jnp.where(first, f_all * my_e + their_e, f_all * their_e + my_e)
    chip_a = jnp.where(first, my_a + f_all * their_a, their_a + f_all * my_a)
    f_chip = f_all * f_all
    before = after = None
    for hop in range(chips - 1):
        before = shifted(chip_e if hop == 0 else f_chip * before + chip_e, "ctx", 2)
        after = shifted(chip_a if hop == 0 else f_chip * after + chip_a, "ctx", -2)
    other_before, other_after = swapped(before), swapped(after)
    whole = lambda own, other: jnp.concatenate(
        [jnp.where(first, own, other), jnp.where(first, other, own)], axis=0
    )
    before, after = whole(before, other_before), whole(after, other_after)
    enter = jnp.where(first, before, f_all * before + other_ends)
    arrive = jnp.where(first, other_adjoints + f_all * after, after)
    return enter, arrive


def summed(value):
    index = lax.axis_index("ctx")
    core = lax.rem(index, 2)
    chip = index // 2
    chips = lax.axis_size("ctx") // 2
    dp = lax.axis_index("dp")
    parts = lax.axis_size("dp")
    half = value.shape[0] // 2
    keep = lax.dynamic_slice_in_dim(value, core * half, half, 0)
    give = lax.dynamic_slice_in_dim(value, (1 - core) * half, half, 0)
    value = keep + swapped(give)
    size = half // parts
    piece = lambda k: lax.dynamic_slice_in_dim(value, lax.rem(dp + k, parts) * size, size, 0)
    total = piece(0)
    for k in range(1, parts):
        total = total + rotated(piece(k), "dp", k)
    gathered = jnp.zeros((chips,) + total.shape, F32)
    put = lambda into, at, what: lax.dynamic_update_slice_in_dim(into, what[None], at, 0)
    gathered = put(gathered, chip, total)
    for k in range(1, chips):
        gathered = put(gathered, lax.rem(chip + chips - k, chips), rotated(total, "ctx", 2 * k))
    total = gathered[0]
    for k in range(1, chips):
        total = total + gathered[k]
    gathered = jnp.zeros((parts,) + total.shape, F32)
    gathered = put(gathered, dp, total)
    for k in range(1, parts):
        gathered = put(gathered, lax.rem(dp + parts - k, parts), rotated(total, "dp", k))
    mine = gathered.reshape((half,) + total.shape[1:])
    other = swapped(mine)
    first = core == 0
    return jnp.concatenate([jnp.where(first, mine, other), jnp.where(first, other, mine)], axis=0)


def local(projected, short_filter, residues, decay_rates, skip_gain, cotangent):
    rows = projected.shape[1]
    channels = projected.shape[3]
    taps = short_filter.shape[1]
    groups, poles = residues.shape
    width = channels // groups
    run = rows // SUB
    p = projected[0].transpose(1, 0, 2)
    u = cotangent[0]
    hb = shifted(p[:, rows - SUB :], "ctx", 1)
    ha = shifted(jnp.concatenate([p[:, :SUB], u[None, :SUB]], axis=0), "ctx", -1)

    rate = decay_rates.T
    weight = residues.T
    sub = np.arange(SUB)
    powers = np.stack(
        [run * (7 - sub), run * sub, 1 + run * sub, 1 + run * (7 - sub), 1 + sub, -sub]
    ).astype(np.float32)
    table = jnp.exp(-rate[None, :, None, :] * powers[:, None, :, None])
    we, wb = table[0], table[1]
    cz, cy, ce, cb = [weight[:, None, :] * table[k] for k in range(2, 6)]
    f1 = jnp.exp(-rate)
    f_all = jnp.exp(-rate * rows)
    row = np.arange(rows)
    lags = (run * (row % SUB) + row // SUB).astype(np.float32)
    lag = jnp.sum(weight[:, None, :] * jnp.exp(-rate[:, None, :] * lags[None, :, None]), axis=0)
    close = np.arange(-taps, 16 - taps).astype(np.float32)
    near = jnp.sum(weight[:, None, :] * jnp.exp(-rate[:, None, :] * close[None, :, None]), axis=0)
    ahead, back = fourier(rows)
    fwd_hi, fwd_lo = split(jnp.asarray(ahead))
    fwd = jnp.concatenate([fwd_hi, fwd_lo], axis=1)
    inv_hi, inv_lo = split(jnp.asarray(back))

    def by_w(*shape):
        axis = len(shape) - 1
        return pl.BlockSpec(shape, lambda w: (0,) * axis + (w,))

    def per_w(*shape):
        return pl.BlockSpec((1,) + shape, lambda w: (w,) + (0,) * len(shape))

    def fixed(value):
        return pl.BlockSpec(value.shape, lambda w: (0,) * value.ndim)

    params = pltpu.CompilerParams(vmem_limit_bytes=48 * 1024 * 1024)
    shape_of = jax.ShapeDtypeStruct
    qkvg, ends, adjoints = pl.pallas_call(
        states_kernel,
        grid=(width,),
        in_specs=[
            by_w(3, rows, groups), by_w(3, SUB, groups), by_w(4, SUB, groups), by_w(rows, groups),
            by_w(3, taps, groups), fixed(f1), fixed(we), fixed(wb),
        ],
        out_specs=[by_w(4, rows + SUB, groups), per_w(poles, groups), per_w(poles, groups)],
        out_shape=[
            shape_of((4, rows + SUB, channels), F32),
            shape_of((width, poles, groups), F32),
            shape_of((width, poles, groups), F32),
        ],
        scratch_shapes=[pltpu.VMEM((4, rows + 2 * SUB, LANES), F32)],
        compiler_params=params,
        name="states",
    )(p, hb, ha, u, short_filter, f1, we, wb)

    enter, arrive = exchange(ends, adjoints, f_all)

    conv, convg = pl.pallas_call(
        long_kernel,
        grid=(width,),
        in_specs=[
            by_w(4, rows + SUB, groups), fixed(lag), fixed(fwd), fixed(fwd_hi), fixed(inv_hi),
            fixed(inv_lo),
        ],
        out_specs=[by_w(rows, groups)] * 2,
        out_shape=[shape_of((rows, channels), F32)] * 2,
        scratch_shapes=[pltpu.VMEM((2 * rows, groups), F32)],
        compiler_params=params,
        cost_estimate=pl.CostEstimate(
            flops=2 * 2 * 6 * 256 * rows * channels, bytes_accessed=26 * 2**20, transcendentals=0
        ),
        name="long",
    )(qkvg, lag, fwd, fwd_hi, inv_hi, inv_lo)

    count = 3 * taps + 3
    output, grad_p, sums = pl.pallas_call(
        final_kernel,
        grid=(width,),
        in_specs=[
            by_w(3, rows, groups), by_w(3, SUB, groups), by_w(rows, groups), by_w(4, SUB, groups),
            by_w(4, rows + SUB, groups), by_w(rows, groups), by_w(rows, groups),
            per_w(poles, groups), per_w(poles, groups), per_w(poles, groups),
            by_w(3, taps, groups), by_w(1, groups), fixed(f1), fixed(f_all),
            fixed(cz), fixed(cy), fixed(ce), fixed(cb), fixed(near),
        ],
        out_specs=[by_w(rows, groups), by_w(3, rows, groups), per_w(count, groups)],
        out_shape=[
            shape_of((rows, channels), BF16),
            shape_of((3, rows, channels), BF16),
            shape_of((width, count, groups), F32),
        ],
        scratch_shapes=[
            pltpu.VMEM((3, rows + SUB, LANES), F32),
            pltpu.VMEM((rows, LANES), F32),
            pltpu.VMEM((3, rows + SUB, LANES), F32),
            pltpu.VMEM((rows, LANES), F32),
            pltpu.VMEM((2 * SUB, LANES), F32),
        ],
        compiler_params=params,
        name="final",
    )(
        p, hb, u, ha, qkvg, conv, convg, enter, arrive, ends, short_filter, skip_gain[None],
        f1, f_all, cz, cy, ce, cb, near,
    )

    total = summed(sums).transpose(1, 0, 2).reshape(count, channels)
    grad_short = total[: 3 * taps].reshape(3, taps, channels)
    grad_skip = total[3 * taps]
    return output[None], grad_p.transpose(1, 0, 2)[None], grad_short, grad_skip


def solution(mesh):
    placed = (P("dp", "ctx", None, None), P(), P(), P(), P(), P("dp", "ctx", None))
    return jax.shard_map(
        local,
        mesh=mesh,
        in_specs=placed,
        out_specs=(P("dp", "ctx", None), P("dp", "ctx", None, None), P(), P()),
        check_vma=False,
    )
```

time: 777 us -> 186 us (0.24); the launches traced: 766 us -> 185 us
  other arithmetic: 194 us -> 8.79 us
  local copies, waits for them, and re-layouts: 160 us -> 7.74 us
  waiting for transfers between devices: 165 us -> 39.3 us
  matrix products: 114 us -> 0 us
  Pallas kernels: 0 us -> 89.6 us
  blocking collectives: 48 us -> 0 us
  starting transfers between devices: 69.2 us -> 38.8 us
  between operations: 15.1 us -> 1.15 us
    dot_general x8 -> x0, matrix products: 114 us -> none  [the longest x1 29.5 us: forward_local(): jnp.einsum('gts,bkswg->bktwg', toeplitz, inputs, precision=HIGHEST)]
    psum x1 -> x0, waiting for transfers between devices: 89.6 us -> none  [local(): grad_short, grad_skip = lax.psum((short_local, skip_local), ('dp', 'ctx'))]
    pallas_call x0 -> x3, Pallas kernels: none -> 89.6 us  [the longest x1 43.3 us: local(): pl.pallas_call(final_kernel, grid=(width,), in_specs=[by_w(3, rows, group...]
    psum x1 -> x0, blocking collectives: 48 us -> none  [local(): grad_short, grad_skip = lax.psum((short_local, skip_local), ('dp', 'ctx'))]
    unnamed x9 -> x0, other arithmetic: 44.3 us -> none
    reduce_sum x2, other arithmetic: 41.4 us -> 0.91 us  [the longest x1 0.74 us: local(): jnp.sum(weight[:, None, :] * jnp.exp(-rate[:, None, :] * lags[None, :, No...]
    ppermute x16 -> x23, waiting for transfers between devices: 75.4 us -> 39.3 us  [the longest x8 21 us: shifted(): lax.ppermute(value, axis, [(source, source + steps) for source in range(f...]
    another operation x4 -> x0, other arithmetic: 35.4 us -> none  [the longest x3 30 us: local(): jnp.stack([grad_query, grad_gated * value_part, grad_gated * key_part], a...]
  transfers between devices with their start and end apart: 17 -> 23, of which waited for: 15 -> 18; matrix products, arithmetic and copies ran while one was open for 16% -> 3% of each run, Pallas kernels for 0% -> 12%
where the time goes in v1:
time: 186 us; the launch traced here: 185 us
  Pallas kernels  89.6 us (48%)
  waiting for transfers between devices  39.3 us (21%)
  starting transfers between devices  38.8 us (21%)
  other arithmetic  8.79 us (5%)
  local copies, waits for them, and re-layouts  7.74 us (4%)
    pallas_call x1, Pallas kernels, local(): pl.pallas_call(final_kernel, grid=(width,), in_specs=[by_w(3, rows, group...  43.3 us
    pallas_call x1, Pallas kernels, local(): pl.pallas_call(states_kernel, grid=(width,), in_specs=[by_w(3, rows, grou...  24.8 us
    pallas_call x1, Pallas kernels, local(): pl.pallas_call(long_kernel, grid=(width,), in_specs=[by_w(4, rows + SUB,...  21.5 us
    ppermute x8, waiting for transfers between devices, shifted(): lax.ppermute(value, axis, [(source, source + steps) for source in range(f...  21 us
    ppermute x8, starting transfers between devices, shifted(): lax.ppermute(value, axis, [(source, source + steps) for source in range(f...  20.6 us
    ppermute x9, starting transfers between devices, rotated(): lax.ppermute(value, axis, [(s, (s + steps) % count) for s in range(count)])  12.8 us
    ppermute x9, waiting for transfers between devices, rotated(): lax.ppermute(value, axis, [(s, (s + steps) % count) for s in range(count)])  12.8 us
    ppermute x6, waiting for transfers between devices, swapped(): return lax.ppermute(value, 'ctx', [(s, s ^ 1) for s in range(count)])  5.48 us
  transfers between devices with their start and end apart: 23, of which 18 were waited for; matrix products, arithmetic and copies ran while one was open for 3% of the time, Pallas kernels for 12%

profile of v1, /device:TPU:0, one launch (start us, length us, event | category | flops | bytes accessed | tf_op | source)
XLA Modules:
  0.0 185.4 jit_solution(469752987488588029)
XLA Ops:
  0.7 1.3 fusion.6
  2.0 0.9 slice.50
  3.0 1.3 collective-permute-start.1
  4.3 3.1 %collective-permute-start = (bf16[3,8,8192]{2,1,0:T(8,128)(2,1)S(1)}, bf16[3,8,8192]{2,1,0:T(8,128)(2,1)S(1)}, u32[]{:S(2)}, u32[]{:S(2)}) collective-permute-start(bf16[3,8,8192]{2,1,0:T(8,128)(2,1)S(1)} %get-tuple-element.25), channel_id=1, source_target_pairs={{0,1},{1,2},{2,3},{3,4},{4,5},{5,6},{6,7},{8,9},{9,10},{10,11},{11... | collective-permute-start | bytes 1179656 | tf_op jit(solution)/shard_map/ppermute | solution.py:212
  7.3 0.8 negate_bitcast_fusion
  8.1 1.0 multiply_exponential_fusion
  9.2 1.0 copy-done.10
  10.2 24.8 %states.1 = (f32[4,136,8192]{2,1,0:T(8,128)}, f32[16,16,512]{2,1,0:T(8,128)}, f32[16,16,512]{2,1,0:T(8,128)}) custom-call(bf16[3,128,8192]{2,1,0:T(8,128)(2,1)} %bitcast.63, bf16[3,8,8192]{2,1,0:T(8,128)(2,1)S(1)} %collective-permute-done.hb, bf16[4,8,8192]{2,1,0:T(8,128)(2,1)S(1)} %collective-permute-done.1.ha, bf16[128,8192]{1,0:T(8,128)(2,1)S(1)} %bitcast.60, ...), custom_call_target="tpu_custom_call" | custom-call | tf_op jit(solution)/shard_map/states/pallas_call | solution.py:330
  35.0 4.7 %collective-permute-start.2 = (f32[16,16,512]{2,1,0:T(8,128)}, f32[16,16,512]{2,1,0:T(8,128)S(1)}, u32[]{:S(2)}, u32[]{:S(2)}) collective-permute-start(f32[16,16,512]{2,1,0:T(8,128)} %get-tuple-element.15.ends), channel_id=1, source_target_pairs={{0,1},{1,0},{2,3},{3,2},{4,5},{5,4},{6,7},{7,6},{8,9},{9,8},{10,11... | collective-permute-start | bytes 1572872 | tf_op jit(solution)/shard_map/ppermute | solution.py:222
  39.8 0.1 collective-permute-start.7
  39.9 1.7 collective-permute-done.2
  41.5 0.7 collective-permute-done.7
  42.3 1.1 add_select_fusion.2
  43.5 4.7 %collective-permute-start.3 = (f32[8,16,512]{2,1,0:T(8,128)S(1)}, f32[8,16,512]{2,1,0:T(8,128)S(1)}, u32[]{:S(2)}, u32[]{:S(2)}) collective-permute-start(f32[8,16,512]{2,1,0:T(8,128)S(1)} %get-tuple-element.48), channel_id=1, source_target_pairs={{0,2},{1,3},{2,4},{3,5},{4,6},{5,7},{8,10},{9,11},{10,12},{11,13},... | collective-permute-start | bytes 786440 | tf_op jit(solution)/shard_map/ppermute | solution.py:212
  48.2 1.3 collective-permute-start.8
  49.5 4.5 %collective-permute-done.3 = f32[8,16,512]{2,1,0:T(8,128)S(1)} collective-permute-done((f32[8,16,512]{2,1,0:T(8,128)S(1)}, f32[8,16,512]{2,1,0:T(8,128)S(1)}, u32[]{:S(2)}, u32[]{:S(2)}) %collective-permute-start.3) | collective-permute-done | bytes 262176 | tf_op jit(solution)/shard_map/ppermute | solution.py:212
  54.0 4.1 %collective-permute-done.8 = f32[8,16,512]{2,1,0:T(8,128)S(1)} collective-permute-done((f32[8,16,512]{2,1,0:T(8,128)S(1)}, f32[8,16,512]{2,1,0:T(8,128)S(1)}, u32[]{:S(2)}, u32[]{:S(2)}) %collective-permute-start.8) | collective-permute-done | bytes 262176 | tf_op jit(solution)/shard_map/ppermute | solution.py:212
  58.2 0.1 multiply_add_fusion.1
  58.3 3.5 %collective-permute-start.4 = (f32[8,16,512]{2,1,0:T(8,128)S(1)}, f32[8,16,512]{2,1,0:T(8,128)S(1)}, u32[]{:S(2)}, u32[]{:S(2)}) collective-permute-start(f32[8,16,512]{2,1,0:T(8,128)S(1)} %get-tuple-element.46), channel_id=1, source_target_pairs={{0,2},{1,3},{2,4},{3,5},{4,6},{5,7},{8,10},{9,11},{10,12},{11,13},... | collective-permute-start | bytes 786440 | tf_op jit(solution)/shard_map/ppermute | solution.py:212
  61.8 1.3 collective-permute-start.9
  63.1 0.7 multiply_reduce_fusion.lag
  63.8 2.6 %collective-permute-done.4 = f32[8,16,512]{2,1,0:T(8,128)S(1)} collective-permute-done((f32[8,16,512]{2,1,0:T(8,128)S(1)}, f32[8,16,512]{2,1,0:T(8,128)S(1)}, u32[]{:S(2)}, u32[]{:S(2)}) %collective-permute-start.4) | collective-permute-done | bytes 262176 | tf_op jit(solution)/shard_map/ppermute | solution.py:212
  66.4 4.1 %collective-permute-done.9 = f32[8,16,512]{2,1,0:T(8,128)S(1)} collective-permute-done((f32[8,16,512]{2,1,0:T(8,128)S(1)}, f32[8,16,512]{2,1,0:T(8,128)S(1)}, u32[]{:S(2)}, u32[]{:S(2)}) %collective-permute-start.9) | collective-permute-done | bytes 262176 | tf_op jit(solution)/shard_map/ppermute | solution.py:212
  70.6 0.8 multiply_add_fusion
  71.4 4.2 %collective-permute-start.5 = (f32[8,16,512]{2,1,0:T(8,128)}, f32[8,16,512]{2,1,0:T(8,128)}, u32[]{:S(2)}, u32[]{:S(2)}) collective-permute-start(f32[8,16,512]{2,1,0:T(8,128)} %get-tuple-element.44), channel_id=1, source_target_pairs={{0,2},{1,3},{2,4},{3,5},{4,6},{5,7},{8,10},{9,11},{10,12},{11,13},... | collective-permute-start | bytes 786440 | tf_op jit(solution)/shard_map/ppermute | solution.py:212
  75.5 1.3 collective-permute-start.10
  76.8 0.2 multiply_reduce_fusion.1.near
  77.0 1.3 fusion
  78.3 0.7 collective-permute-done.5
  79.0 4.9 %collective-permute-done.10 = f32[8,16,512]{2,1,0:T(8,128)} collective-permute-done((f32[8,16,512]{2,1,0:T(8,128)S(1)}, f32[8,16,512]{2,1,0:T(8,128)}, u32[]{:S(2)}, u32[]{:S(2)}) %collective-permute-start.10) | collective-permute-done | bytes 262176 | tf_op jit(solution)/shard_map/ppermute | solution.py:212
  83.9 21.5 %long.1 = (f32[128,8192]{1,0:T(8,128)S(1)}, f32[128,8192]{1,0:T(8,128)}) custom-call(f32[4,136,8192]{2,1,0:T(8,128)} %get-tuple-element.12.qkvg, f32[128,512]{1,0:T(8,128)S(1)} %multiply_reduce_fusion.lag, bf16[256,256]{1,0:T(8,128)(2,1)S(1)} %copy-done.6, bf16[256,128]{1,0:T(8,128)(2,1)S(1)} %copy-done.7, bf16[128,256]{1,0:T(8,128)(2,1)S(1)} %copy-done.8, ...), custom_call_target="tpu_custom_call" | custom-call | flops 6442450944 | bytes 27262976 | tf_op jit(solution)/shard_map/long/pallas_call | solution.py:350
  105.4 2.0 %copy-done.1 = f32[128,8192]{1,0:T(8,128)} copy-done((f32[128,8192]{1,0:T(8,128)}, f32[128,8192]{1,0:T(8,128)S(1)}, u32[]{:S(2)}) %copy-start.1) | copy-done | bytes 4194328
  107.4 1.0 broadcast_select_fusion.5
  108.5 1.0 broadcast_select_fusion.3
  109.5 0.3 add_select_fusion
  109.8 43.3 %final.1 = (bf16[128,8192]{1,0:T(8,128)(2,1)}, bf16[3,128,8192]{2,1,0:T(8,128)(2,1)}, f32[16,24,512]{2,1,0:T(8,128)S(1)}) custom-call(bf16[3,128,8192]{2,1,0:T(8,128)(2,1)} %bitcast.64, bf16[3,8,8192]{2,1,0:T(8,128)(2,1)S(1)} %copy-done.4, bf16[128,8192]{1,0:T(8,128)(2,1)} %bitcast.59, bf16[4,8,8192]{2,1,0:T(8,128)(2,1)S(1)} %collective-permute-done.1.ha, ...), custom_call_target="tpu_custom_call" | custom-call | tf_op jit(solution)/shard_map/final/pallas_call | solution.py:368
  153.1 0.6 collective-permute-start.12
  153.7 1.3 collective-permute-done.12
  155.0 0.1 dynamic-slice_add_fusion
  155.1 1.6 collective-permute-start.13
  156.7 1.5 collective-permute-start.14
  158.2 1.4 collective-permute-start.15
  159.6 2.1 %collective-permute-done.13 = f32[2,24,512]{2,1,0:T(8,128)S(1)} collective-permute-done((f32[2,24,512]{2,1,0:T(8,128)S(1)}, f32[2,24,512]{2,1,0:T(8,128)S(1)}, u32[]{:S(2)}, u32[]{:S(2)}) %collective-permute-start.13) | collective-permute-done | bytes 98336 | tf_op jit(solution)/shard_map/ppermute | solution.py:217
  161.7 1.6 collective-permute-done.14
  163.3 0.1 collective-permute-done.15
  163.4 0.1 collective-permute-start.16
  163.5 0.1 collective-permute-start.17
  163.6 3.7 %collective-permute-start.18 = (f32[2,24,512]{2,1,0:T(8,128)S(1)}, f32[2,24,512]{2,1,0:T(8,128)S(1)}, u32[]{:S(2)}, u32[]{:S(2)}) collective-permute-start(f32[2,24,512]{2,1,0:T(8,128)S(1)} %get-tuple-element.23), channel_id=1, source_target_pairs={{0,6},{1,7},{2,0},{3,1},{4,2},{5,3},{6,4},{7,5},{8,14},{9,15},{10,... | collective-permute-start | bytes 294920 | tf_op jit(solution)/shard_map/ppermute | solution.py:217
  167.3 3.7 %collective-permute-done.16 = f32[2,24,512]{2,1,0:T(8,128)S(1)} collective-permute-done((f32[2,24,512]{2,1,0:T(8,128)S(1)}, f32[2,24,512]{2,1,0:T(8,128)S(1)}, u32[]{:S(2)}, u32[]{:S(2)}) %collective-permute-start.16) | collective-permute-done | bytes 98336 | tf_op jit(solution)/shard_map/ppermute | solution.py:217
  171.0 3.2 %collective-permute-done.17 = f32[2,24,512]{2,1,0:T(8,128)S(1)} collective-permute-done((f32[2,24,512]{2,1,0:T(8,128)S(1)}, f32[2,24,512]{2,1,0:T(8,128)S(1)}, u32[]{:S(2)}, u32[]{:S(2)}) %collective-permute-start.17) | collective-permute-done | bytes 98336 | tf_op jit(solution)/shard_map/ppermute | solution.py:217
  174.4 1.2 collective-permute-start.19
  175.6 0.4 collective-permute-start.20
  176.0 2.8 %collective-permute-start.21 = (f32[2,24,512]{2,1,0:T(8,128)S(1)}, f32[2,24,512]{2,1,0:T(8,128)S(1)}, u32[]{:S(2)}, u32[]{:S(2)}) collective-permute-start(f32[2,24,512]{2,1,0:T(8,128)S(1)} %bitcast.69), channel_id=1, source_target_pairs={{0,24},{8,0},{16,8},{24,16},{1,25},{9,1},{17,9},{25,17},{2,26},{10... | collective-permute-start | bytes 294920 | tf_op jit(solution)/shard_map/ppermute | solution.py:217
  178.9 1.2 collective-permute-done.19
  180.0 1.0 collective-permute-done.20
  181.0 0.1 collective-permute-done.21
  181.1 0.2 copy.19
  181.3 0.1 collective-permute-start.22
  181.4 1.7 collective-permute-done.22
  183.1 0.3 broadcast_select_fusion.1
  183.4 0.1 maximum_bitcast_fusion
  183.5 0.1 slice.75
  183.5 1.2 reshape.32
  184.8 0.6 copy.21
  (51 shorter events, 0.5 us)
Async XLA Ops:
  0.6 9.6 %copy-start = (bf16[1,128,8192]{2,1,0:T(8,128)(2,1)S(1)}, bf16[1,128,8192]{2,1,0:T(8,128)(2,1)}, u32[]{:S(2)}) copy-start(bf16[1,128,8192]{2,1,0:T(8,128)(2,1)} %param.16) | copy-start | bytes 6291460
  0.6 8.4 %copy-start.11 = (f32[512,16]{0,1:T(8,128)S(1)}, f32[512,16]{0,1:T(8,128)}, u32[]{:S(2)}) copy-start(f32[512,16]{0,1:T(8,128)} %param.14) | copy-start | bytes 98308
  0.7 9.6 %copy-start.2 = (f32[3,7,8192]{2,1,0:T(8,128)S(1)}, f32[3,7,8192]{2,1,0:T(8,128)}, u32[]{:S(2)}) copy-start(f32[3,7,8192]{2,1,0:T(8,128)} %filt.3) | copy-start | bytes 2064388
  3.0 6.2 %collective-permute-start.1 = (bf16[4,8,8192]{2,1,0:T(8,128)(2,1)S(1)}, bf16[4,8,8192]{2,1,0:T(8,128)(2,1)S(1)}, u32[]{:S(2)}, u32[]{:S(2)}) collective-permute-start(bf16[4,8,8192]{2,1,0:T(8,128)(2,1)S(1)} %pad_maximum_fusion), channel_id=1, source_target_pairs={{1,0},{2,1},{3,2},{4,3},{5,4},{6,5},{7,6},{9,8},{10,9},{11,10},{12... | collective-permute-start | bytes 1572872 | tf_op jit(solution)/shard_map/ppermute | solution.py:212
  4.3 4.9 %collective-permute-start = (bf16[3,8,8192]{2,1,0:T(8,128)(2,1)S(1)}, bf16[3,8,8192]{2,1,0:T(8,128)(2,1)S(1)}, u32[]{:S(2)}, u32[]{:S(2)}) collective-permute-start(bf16[3,8,8192]{2,1,0:T(8,128)(2,1)S(1)} %get-tuple-element.25), channel_id=1, source_target_pairs={{0,1},{1,2},{2,3},{3,4},{4,5},{5,6},{6,7},{8,9},{9,10},{10,11},{11... | collective-permute-start | bytes 1179656 | tf_op jit(solution)/shard_map/ppermute | solution.py:212
  9.1 1.1 copy-start.10
  9.2 25.9 %copy-start.3 = (bf16[3,8,8192]{2,1,0:T(8,128)(2,1)}, bf16[3,8,8192]{2,1,0:T(8,128)(2,1)S(1)}, u32[]{:S(2)}) copy-start(bf16[3,8,8192]{2,1,0:T(8,128)(2,1)S(1)} %collective-permute-done.hb) | copy-start | bytes 1179652
  10.2 52.8 %copy-start.12 = (f32[512,16]{0,1:T(8,128)S(1)}, f32[512,16]{0,1:T(8,128)}, u32[]{:S(2)}) copy-start(f32[512,16]{0,1:T(8,128)} %param.13) | copy-start | bytes 98308
  10.2 52.8 %copy-start.14 = (f32[128]{0:T(128)S(1)}, f32[128]{0:T(128)}, u32[]{:S(2)}) copy-start(f32[128]{0:T(128)} %constant.88) | copy-start | bytes 1540
  35.0 41.8 %copy-start.13 = (f32[16]{0:T(128)S(1)}, f32[16]{0:T(128)}, u32[]{:S(2)}) copy-start(f32[16]{0:T(128)} %constant.98) | copy-start | bytes 196
  35.0 6.5 %collective-permute-start.2 = (f32[16,16,512]{2,1,0:T(8,128)}, f32[16,16,512]{2,1,0:T(8,128)S(1)}, u32[]{:S(2)}, u32[]{:S(2)}) collective-permute-start(f32[16,16,512]{2,1,0:T(8,128)} %get-tuple-element.15.ends), channel_id=1, source_target_pairs={{0,1},{1,0},{2,3},{3,2},{4,5},{5,4},{6,7},{7,6},{8,9},{9,8},{10,11... | collective-permute-start | bytes 1572872 | tf_op jit(solution)/shard_map/ppermute | solution.py:222
  39.8 2.5 %collective-permute-start.7 = (f32[16,16,512]{2,1,0:T(8,128)}, f32[16,16,512]{2,1,0:T(8,128)S(1)}, u32[]{:S(2)}, u32[]{:S(2)}) collective-permute-start(f32[16,16,512]{2,1,0:T(8,128)} %get-tuple-element.16), channel_id=1, source_target_pairs={{0,1},{1,0},{2,3},{3,2},{4,5},{5,4},{6,7},{7,6},{8,9},{9,8},{10,11... | collective-permute-start | bytes 1572872 | tf_op jit(solution)/shard_map/ppermute | solution.py:222
  43.4 40.5 %copy-start.6 = (bf16[256,256]{1,0:T(8,128)(2,1)S(1)}, bf16[256,256]{1,0:T(8,128)(2,1)}, u32[]{:S(2)}) copy-start(bf16[256,256]{1,0:T(8,128)(2,1)} %constant.93.fwd) | copy-start | bytes 393220
  43.4 40.5 %copy-start.7 = (bf16[256,128]{1,0:T(8,128)(2,1)S(1)}, bf16[256,128]{1,0:T(8,128)(2,1)}, u32[]{:S(2)}) copy-start(bf16[256,128]{1,0:T(8,128)(2,1)} %constant.89.fwd_hi) | copy-start | bytes 196612
  43.5 40.5 %copy-start.8 = (bf16[128,256]{1,0:T(8,128)(2,1)S(1)}, bf16[128,256]{1,0:T(8,128)(2,1)}, u32[]{:S(2)}) copy-start(bf16[128,256]{1,0:T(8,128)(2,1)} %constant.94.inv_hi) | copy-start | bytes 196612
  43.5 40.5 %copy-start.9 = (bf16[128,256]{1,0:T(8,128)(2,1)S(1)}, bf16[128,256]{1,0:T(8,128)(2,1)}, u32[]{:S(2)}) copy-start(bf16[128,256]{1,0:T(8,128)(2,1)} %constant.97.inv_lo) | copy-start | bytes 196612
  43.5 10.5 %collective-permute-start.3 = (f32[8,16,512]{2,1,0:T(8,128)S(1)}, f32[8,16,512]{2,1,0:T(8,128)S(1)}, u32[]{:S(2)}, u32[]{:S(2)}) collective-permute-start(f32[8,16,512]{2,1,0:T(8,128)S(1)} %get-tuple-element.48), channel_id=1, source_target_pairs={{0,2},{1,3},{2,4},{3,5},{4,6},{5,7},{8,10},{9,11},{10,12},{11,13},... | collective-permute-start | bytes 786440 | tf_op jit(solution)/shard_map/ppermute | solution.py:212
  48.2 10.0 %collective-permute-start.8 = (f32[8,16,512]{2,1,0:T(8,128)S(1)}, f32[8,16,512]{2,1,0:T(8,128)S(1)}, u32[]{:S(2)}, u32[]{:S(2)}) collective-permute-start(f32[8,16,512]{2,1,0:T(8,128)S(1)} %get-tuple-element.47), channel_id=1, source_target_pairs={{2,0},{3,1},{4,2},{5,3},{6,4},{7,5},{10,8},{11,9},{12,10},{13,11},... | collective-permute-start | bytes 786440 | tf_op jit(solution)/shard_map/ppermute | solution.py:212
  58.3 8.2 %collective-permute-start.4 = (f32[8,16,512]{2,1,0:T(8,128)S(1)}, f32[8,16,512]{2,1,0:T(8,128)S(1)}, u32[]{:S(2)}, u32[]{:S(2)}) collective-permute-start(f32[8,16,512]{2,1,0:T(8,128)S(1)} %get-tuple-element.46), channel_id=1, source_target_pairs={{0,2},{1,3},{2,4},{3,5},{4,6},{5,7},{8,10},{9,11},{10,12},{11,13},... | collective-permute-start | bytes 786440 | tf_op jit(solution)/shard_map/ppermute | solution.py:212
  61.8 8.8 %collective-permute-start.9 = (f32[8,16,512]{2,1,0:T(8,128)S(1)}, f32[8,16,512]{2,1,0:T(8,128)S(1)}, u32[]{:S(2)}, u32[]{:S(2)}) collective-permute-start(f32[8,16,512]{2,1,0:T(8,128)S(1)} %get-tuple-element.45), channel_id=1, source_target_pairs={{2,0},{3,1},{4,2},{5,3},{6,4},{7,5},{10,8},{11,9},{12,10},{13,11},... | collective-permute-start | bytes 786440 | tf_op jit(solution)/shard_map/ppermute | solution.py:212
  71.4 7.7 %collective-permute-start.5 = (f32[8,16,512]{2,1,0:T(8,128)}, f32[8,16,512]{2,1,0:T(8,128)}, u32[]{:S(2)}, u32[]{:S(2)}) collective-permute-start(f32[8,16,512]{2,1,0:T(8,128)} %get-tuple-element.44), channel_id=1, source_target_pairs={{0,2},{1,3},{2,4},{3,5},{4,6},{5,7},{8,10},{9,11},{10,12},{11,13},... | collective-permute-start | bytes 786440 | tf_op jit(solution)/shard_map/ppermute | solution.py:212
  75.5 8.4 %collective-permute-start.10 = (f32[8,16,512]{2,1,0:T(8,128)S(1)}, f32[8,16,512]{2,1,0:T(8,128)}, u32[]{:S(2)}, u32[]{:S(2)}) collective-permute-start(f32[8,16,512]{2,1,0:T(8,128)S(1)} %get-tuple-element.43), channel_id=1, source_target_pairs={{2,0},{3,1},{4,2},{5,3},{6,4},{7,5},{10,8},{11,9},{12,10},{13,11},... | collective-permute-start | bytes 786440 | tf_op jit(solution)/shard_map/ppermute | solution.py:212
  79.0 28.4 %collective-permute-start.6 = (f32[8,16,512]{2,1,0:T(8,128)}, f32[8,16,512]{2,1,0:T(8,128)S(1)}, u32[]{:S(2)}, u32[]{:S(2)}) collective-permute-start(f32[8,16,512]{2,1,0:T(8,128)} %collective-permute-done.5), channel_id=1, source_target_pairs={{0,1},{1,0},{2,3},{3,2},{4,5},{5,4},{6,7},{7,6},{8,9},{9,8},{10,11... | collective-permute-start | bytes 786440 | tf_op jit(solution)/shard_map/ppermute | solution.py:222
  83.9 24.6 %collective-permute-start.11 = (f32[8,16,512]{2,1,0:T(8,128)}, f32[8,16,512]{2,1,0:T(8,128)S(1)}, u32[]{:S(2)}, u32[]{:S(2)}) collective-permute-start(f32[8,16,512]{2,1,0:T(8,128)} %collective-permute-done.10), channel_id=1, source_target_pairs={{0,1},{1,0},{2,3},{3,2},{4,5},{5,4},{6,7},{7,6},{8,9},{9,8},{10,11... | collective-permute-start | bytes 786440 | tf_op jit(solution)/shard_map/ppermute | solution.py:222
  105.4 2.0 %copy-start.1 = (f32[128,8192]{1,0:T(8,128)}, f32[128,8192]{1,0:T(8,128)S(1)}, u32[]{:S(2)}) copy-start(f32[128,8192]{1,0:T(8,128)S(1)} %get-tuple-element.13.conv) | copy-start | bytes 12582916
  107.4 2.3 %copy-start.4 = (bf16[3,8,8192]{2,1,0:T(8,128)(2,1)S(1)}, bf16[3,8,8192]{2,1,0:T(8,128)(2,1)}, u32[]{:S(2)}) copy-start(bf16[3,8,8192]{2,1,0:T(8,128)(2,1)} %copy-done.3) | copy-start | bytes 1179652
  107.4 2.3 %copy-start.5 = (f32[8192]{0:T(1024)S(1)}, f32[8192]{0:T(1024)}, u32[]{:S(2)}) copy-start(f32[8192]{0:T(1024)} %param.15) | copy-start | bytes 98308
  153.1 1.9 %collective-permute-start.12 = (f32[8,24,512]{2,1,0:T(8,128)S(1)}, f32[8,24,512]{2,1,0:T(8,128)S(1)}, u32[]{:S(2)}, u32[]{:S(2)}) collective-permute-start(f32[8,24,512]{2,1,0:T(8,128)S(1)} %constant_dynamic-slice_fusion.3), channel_id=1, source_target_pairs={{0,1},{1,0},{2,3},{3,2},{4,5},{5,4},{6,7},{7,6},{8,9},{9,8},{10,11... | collective-permute-start | bytes 1179656 | tf_op jit(solution)/shard_map/ppermute | solution.py:222
  155.1 6.6 %collective-permute-start.13 = (f32[2,24,512]{2,1,0:T(8,128)S(1)}, f32[2,24,512]{2,1,0:T(8,128)S(1)}, u32[]{:S(2)}, u32[]{:S(2)}) collective-permute-start(f32[2,24,512]{2,1,0:T(8,128)S(1)} %get-tuple-element.38), channel_id=1, source_target_pairs={{0,8},{8,16},{16,24},{24,0},{1,9},{9,17},{17,25},{25,1},{2,10},{10... | collective-permute-start | bytes 294920 | tf_op jit(solution)/shard_map/ppermute | solution.py:217
  156.7 6.6 %collective-permute-start.14 = (f32[2,24,512]{2,1,0:T(8,128)S(1)}, f32[2,24,512]{2,1,0:T(8,128)S(1)}, u32[]{:S(2)}, u32[]{:S(2)}) collective-permute-start(f32[2,24,512]{2,1,0:T(8,128)S(1)} %get-tuple-element.40), channel_id=1, source_target_pairs={{0,16},{8,24},{16,0},{24,8},{1,17},{9,25},{17,1},{25,9},{2,18},{10... | collective-permute-start | bytes 294920 | tf_op jit(solution)/shard_map/ppermute | solution.py:217
  158.2 5.1 %collective-permute-start.15 = (f32[2,24,512]{2,1,0:T(8,128)S(1)}, f32[2,24,512]{2,1,0:T(8,128)S(1)}, u32[]{:S(2)}, u32[]{:S(2)}) collective-permute-start(f32[2,24,512]{2,1,0:T(8,128)S(1)} %get-tuple-element.39), channel_id=1, source_target_pairs={{0,24},{8,0},{16,8},{24,16},{1,25},{9,1},{17,9},{25,17},{2,26},{10... | collective-permute-start | bytes 294920 | tf_op jit(solution)/shard_map/ppermute | solution.py:217
  163.4 7.6 %collective-permute-start.16 = (f32[2,24,512]{2,1,0:T(8,128)S(1)}, f32[2,24,512]{2,1,0:T(8,128)S(1)}, u32[]{:S(2)}, u32[]{:S(2)}) collective-permute-start(f32[2,24,512]{2,1,0:T(8,128)S(1)} %get-tuple-element.23), channel_id=1, source_target_pairs={{0,2},{1,3},{2,4},{3,5},{4,6},{5,7},{6,0},{7,1},{8,10},{9,11},{10,... | collective-permute-start | bytes 294920 | tf_op jit(solution)/shard_map/ppermute | solution.py:217
  163.5 10.7 %collective-permute-start.17 = (f32[2,24,512]{2,1,0:T(8,128)S(1)}, f32[2,24,512]{2,1,0:T(8,128)S(1)}, u32[]{:S(2)}, u32[]{:S(2)}) collective-permute-start(f32[2,24,512]{2,1,0:T(8,128)S(1)} %get-tuple-element.23), channel_id=1, source_target_pairs={{0,4},{1,5},{2,6},{3,7},{4,0},{5,1},{6,2},{7,3},{8,12},{9,13},{10,... | collective-permute-start | bytes 294920 | tf_op jit(solution)/shard_map/ppermute | solution.py:217
  163.6 10.7 %collective-permute-start.18 = (f32[2,24,512]{2,1,0:T(8,128)S(1)}, f32[2,24,512]{2,1,0:T(8,128)S(1)}, u32[]{:S(2)}, u32[]{:S(2)}) collective-permute-start(f32[2,24,512]{2,1,0:T(8,128)S(1)} %get-tuple-element.23), channel_id=1, source_target_pairs={{0,6},{1,7},{2,0},{3,1},{4,2},{5,3},{6,4},{7,5},{8,14},{9,15},{10,... | collective-permute-start | bytes 294920 | tf_op jit(solution)/shard_map/ppermute | solution.py:217
  174.4 5.7 %collective-permute-start.19 = (f32[2,24,512]{2,1,0:T(8,128)S(1)}, f32[2,24,512]{2,1,0:T(8,128)S(1)}, u32[]{:S(2)}, u32[]{:S(2)}) collective-permute-start(f32[2,24,512]{2,1,0:T(8,128)S(1)} %bitcast.67), channel_id=1, source_target_pairs={{0,8},{8,16},{16,24},{24,0},{1,9},{9,17},{17,25},{25,1},{2,10},{10... | collective-permute-start | bytes 294920 | tf_op jit(solution)/shard_map/ppermute | solution.py:217
  175.6 5.4 %collective-permute-start.20 = (f32[2,24,512]{2,1,0:T(8,128)S(1)}, f32[2,24,512]{2,1,0:T(8,128)S(1)}, u32[]{:S(2)}, u32[]{:S(2)}) collective-permute-start(f32[2,24,512]{2,1,0:T(8,128)S(1)} %bitcast.68), channel_id=1, source_target_pairs={{0,16},{8,24},{16,0},{24,8},{1,17},{9,25},{17,1},{25,9},{2,18},{10... | collective-permute-start | bytes 294920 | tf_op jit(solution)/shard_map/ppermute | solution.py:217
  176.0 5.1 %collective-permute-start.21 = (f32[2,24,512]{2,1,0:T(8,128)S(1)}, f32[2,24,512]{2,1,0:T(8,128)S(1)}, u32[]{:S(2)}, u32[]{:S(2)}) collective-permute-start(f32[2,24,512]{2,1,0:T(8,128)S(1)} %bitcast.69), channel_id=1, source_target_pairs={{0,24},{8,0},{16,8},{24,16},{1,25},{9,1},{17,9},{25,17},{2,26},{10... | collective-permute-start | bytes 294920 | tf_op jit(solution)/shard_map/ppermute | solution.py:217
  181.3 1.8 collective-permute-start.22

commit v2 on v1

v2 whole, which is shorter than its diff:
```python
import functools

import jax
import jax.numpy as jnp
import numpy as np
from jax import lax
from jax.experimental import pallas as pl
from jax.experimental.pallas import tpu as pltpu
from jax.sharding import PartitionSpec as P

LANES = 128
SUB = 8
F32 = jnp.float32
BF16 = jnp.bfloat16


def spread(row):
    return jnp.broadcast_to(row, (SUB, LANES))


def added(terms):
    while len(terms) > 1:
        pairs = [terms[k] + terms[k + 1] for k in range(0, len(terms) - 1, 2)]
        terms = pairs + terms[len(terms) - len(terms) % 2 :]
    return terms[0]


def states_kernel(p, hb, ha, u, filt, f1, we, wb, qkvg, blocks_e, blocks_a, ends, xs):
    rows = p.shape[1]
    run = (rows + SUB) // SUB
    taps = filt.shape[1]
    poles = f1.shape[0]
    own = rows - run * (SUB - 1)

    def tile(lt, carry):
        lanes = pl.ds(pl.multiple_of(lt * LANES, LANES), LANES)
        inside = lax.broadcasted_iota(jnp.int32, (SUB, LANES), 0) < SUB - 1
        for j in range(3):
            xs[j, 0:SUB] = hb[j, :, lanes].astype(F32)
            xs[j, SUB : SUB + rows] = p[j, :, lanes].astype(F32)
            xs[j, SUB + rows :] = ha[j, :, lanes].astype(F32)
        xs[3, SUB : SUB + rows] = u[:, lanes].astype(F32)
        xs[3, SUB + rows :] = ha[3, :, lanes].astype(F32)
        for j in range(3):
            tap = [spread(filt[j, i : i + 1, lanes]) for i in range(taps)]
            view = [xs[j, pl.ds(SUB + a, SUB, stride=run), :] for a in range(1 - taps, run)]
            for a in range(run):
                total = added([tap[i] * view[a + taps - 1 - i] for i in range(taps)])
                qkvg[j, SUB * a : SUB * a + SUB, lanes] = total
        decay = [spread(f1[n : n + 1, lanes]) for n in range(poles)]
        state = None
        for a in range(run):
            at = slice(SUB * a, SUB * a + SUB)
            value = qkvg[1, at, lanes] * qkvg[2, at, lanes]
            if a >= own:
                value = jnp.where(inside, value, 0.0)
            state = [value] * poles if a == 0 else [decay[n] * state[n] + value for n in range(poles)]
        for n in range(poles):
            blocks_e[n, :, lanes] = state[n]
            ends[0, 0, n : n + 1, lanes] = jnp.sum(state[n] * we[n, :, lanes], axis=0, keepdims=True)
        state = None
        for a in range(run - 1, -1, -1):
            at = slice(SUB * a, SUB * a + SUB)
            value = xs[3, pl.ds(SUB + a, SUB, stride=run), :] * qkvg[0, at, lanes]
            qkvg[3, at, lanes] = value
            if a >= own:
                value = jnp.where(inside, value, 0.0)
            state = [value] * poles if a == run - 1 else [decay[n] * state[n] + value for n in range(poles)]
        for n in range(poles):
            blocks_a[n, :, lanes] = state[n]
            ends[1, 0, n : n + 1, lanes] = jnp.sum(state[n] * wb[n, :, lanes], axis=0, keepdims=True)
        return carry

    lax.fori_loop(0, p.shape[2] // LANES, tile, 0)


def blocks_kernel(kvg, blocks_e, blocks_a, near, skip, join_e, join_a, conv, convg, from_e, from_a):
    run = conv.shape[0] // SUB
    rows = conv.shape[0] - SUB
    taps = near.shape[0] - run
    poles = blocks_e.shape[0]
    own = rows - run * (SUB - 1)

    def tile(lt, carry):
        lanes = pl.ds(pl.multiple_of(lt * LANES, LANES), LANES)
        inside = lax.broadcasted_iota(jnp.int32, (SUB, LANES), 0) < SUB - 1
        gain = spread(skip[0:1, lanes])
        lag = [spread(near[taps + m : taps + m + 1, lanes]) for m in range(run)]
        lag[0] = lag[0] + gain
        x = [
            kvg[1, SUB * a : SUB * a + SUB, lanes] * kvg[2, SUB * a : SUB * a + SUB, lanes]
            for a in range(run)
        ]
        for a in range(run):
            conv[SUB * a : SUB * a + SUB, lanes] = added([lag[m] * x[a - m] for m in range(a + 1)])
        x = [kvg[3, SUB * a : SUB * a + SUB, lanes] for a in range(run)]
        masked = [x[a] if a < own else jnp.where(inside, x[a], 0.0) for a in range(run)]
        past = [jnp.where(inside, 0.0, gain)] + [
            jnp.where(inside, 0.0, -spread(near[taps - m : taps - m + 1, lanes]))
            for m in range(1, taps - 1)
        ]
        for a in range(run):
            terms = [lag[m] * masked[a + m] for m in range(run - a)]
            if own <= a < own + taps - 1:
                terms = terms + [past[m] * x[a - m] for m in range(a - own + 1)]
            convg[SUB * a : SUB * a + SUB, lanes] = added(terms)
        for n in range(poles):
            value = pltpu.roll(blocks_e[n, :, lanes], 1, 0) * join_e[0, n, :, lanes]
            for k, step in ((1, 1), (2, 2), (3, 4)):
                value = value + pltpu.roll(value, step, 0) * join_e[k, n, :, lanes]
            from_e[n, :, lanes] = value
            value = pltpu.roll(blocks_a[n, :, lanes], SUB - 1, 0) * join_a[0, n, :, lanes]
            for k, step in ((1, 1), (2, 2), (3, 4)):
                value = value + pltpu.roll(value, SUB - step, 0) * join_a[k, n, :, lanes]
            from_a[n, :, lanes] = value
        return carry

    lax.fori_loop(0, conv.shape[1] // LANES, tile, 0)


def final_kernel(
    p, hb, u, ha, qkvg, conv, convg, from_e, from_a, enter, arrive, filt, f1, cz, cy,
    output, grad_p, sums, ps, us, gs, os,
):
    rows = p.shape[1]
    run = (rows + SUB) // SUB
    taps = filt.shape[1]
    poles = f1.shape[0]
    own = rows - run * (SUB - 1)

    def tile(lt, carry):
        lanes = pl.ds(pl.multiple_of(lt * LANES, LANES), LANES)
        inside = lax.broadcasted_iota(jnp.int32, (SUB, LANES), 0) < SUB - 1
        for j in range(3):
            ps[j, 0:SUB] = hb[j, :, lanes].astype(F32)
            ps[j, SUB : SUB + rows] = p[j, :, lanes].astype(F32)
            ps[j, SUB + rows :] = ha[j, :, lanes].astype(F32)
        us[0:rows] = u[:, lanes].astype(F32)
        us[rows:] = ha[3, :, lanes].astype(F32)
        decay = [spread(f1[n : n + 1, lanes]) for n in range(poles)]

        state = [
            from_e[n, :, lanes] + cz[n, :, lanes] * spread(enter[0, n : n + 1, lanes])
            for n in range(poles)
        ]
        skip_sum = None
        for a in range(run):
            at = slice(SUB * a, SUB * a + SUB)
            term = qkvg[1, at, lanes] * qkvg[2, at, lanes] * qkvg[3, at, lanes]
            if a >= own:
                term = jnp.where(inside, term, 0.0)
            skip_sum = term if a == 0 else skip_sum + term
            filtered = conv[at, lanes] + added(list(state))
            os[pl.ds(a, SUB, stride=run), :] = qkvg[0, at, lanes] * filtered
            gs[0, pl.ds(a, SUB, stride=run), :] = us[pl.ds(a, SUB, stride=run), :] * filtered
            if a + 1 < run:
                state = [state[n] * decay[n] for n in range(poles)]
        output[:, lanes] = os[0:rows].astype(BF16)

        state = [
            from_a[n, :, lanes] + cy[n, :, lanes] * spread(arrive[0, n : n + 1, lanes])
            for n in range(poles)
        ]
        for a in range(run - 1, -1, -1):
            at = slice(SUB * a, SUB * a + SUB)
            grad = convg[at, lanes] + added(list(state))
            gs[1, pl.ds(a, SUB, stride=run), :] = grad * qkvg[2, at, lanes]
            gs[2, pl.ds(a, SUB, stride=run), :] = grad * qkvg[1, at, lanes]
            if a:
                state = [state[n] * decay[n] for n in range(poles)]

        for j in range(3):
            tap = [spread(filt[j, i : i + 1, lanes]) for i in range(taps)]
            grads = [gs[j, pl.ds(a, SUB, stride=run), :] for a in range(run + taps - 1)]
            views = [ps[j, pl.ds(SUB + a, SUB, stride=run), :] for a in range(1 - taps, run)]
            sums_of = [None] * taps
            for a in range(run):
                total = added([tap[i] * grads[a + i] for i in range(taps)])
                os[pl.ds(a, SUB, stride=run), :] = total
                grad = grads[a] if a < own else jnp.where(inside, grads[a], 0.0)
                for i in range(taps):
                    term = grad * views[a + taps - 1 - i]
                    sums_of[i] = term if a == 0 else sums_of[i] + term
            grad_p[j, :, lanes] = os[0:rows].astype(BF16)
            for i in range(taps):
                at = j * taps + i
                sums[0, at : at + 1, lanes] = jnp.sum(sums_of[i], axis=0, keepdims=True)
        at = 3 * taps
        sums[0, at : at + 1, lanes] = jnp.sum(skip_sum, axis=0, keepdims=True)
        return carry

    lax.fori_loop(0, p.shape[2] // LANES, tile, 0)


def shifted(value, axis, steps):
    count = lax.axis_size(axis)
    first, last = (max(0, -steps), min(count, count - steps))
    return lax.ppermute(value, axis, [(source, source + steps) for source in range(first, last)])


def rotated(value, axis, steps):
    count = lax.axis_size(axis)
    return lax.ppermute(value, axis, [(s, (s + steps) % count) for s in range(count)])


def swapped(value):
    count = lax.axis_size("ctx")
    return lax.ppermute(value, "ctx", [(s, s ^ 1) for s in range(count)])


def outward(ends, f_all):
    chips = lax.axis_size("ctx") // 2
    core = lax.rem(lax.axis_index("ctx"), 2)
    half = ends.shape[1] // 2
    other = swapped(ends)
    first = core == 0
    mine = lax.dynamic_slice_in_dim(ends, core * half, half, 1)
    theirs = lax.dynamic_slice_in_dim(other, core * half, half, 1)
    one, two = jnp.where(first, mine, theirs), jnp.where(first, theirs, mine)
    chip_e = f_all * one[0] + two[0]
    chip_a = one[1] + f_all * two[1]
    f_chip = f_all * f_all
    if chips <= 4:
        hops = range(1, chips)
        found = [(shifted(chip_e, "ctx", 2 * k), shifted(chip_a, "ctx", -2 * k)) for k in hops]
    else:
        before, after = shifted(chip_e, "ctx", 2), shifted(chip_a, "ctx", -2)
        for hop in range(2, chips):
            before = shifted(f_chip * before + chip_e, "ctx", 2)
            after = shifted(f_chip * after + chip_a, "ctx", -2)
        found = [(before, after)]
    return other, found, chip_e


def inward(other, found, f_all):
    first = lax.rem(lax.axis_index("ctx"), 2) == 0
    f_chip = f_all * f_all
    factor = f_chip
    before, after = found[0]
    for early, late in found[1:]:
        before = before + factor * early
        after = after + factor * late
        factor = factor * f_chip
    both = jnp.stack([before, after])
    found = swapped(both)
    both = jnp.concatenate([jnp.where(first, both, found), jnp.where(first, found, both)], axis=1)
    enter = jnp.where(first, both[0], f_all * both[0] + other[0])
    arrive = jnp.where(first, other[1] + f_all * both[1], both[1])
    return enter, arrive


def summed(value):
    index = lax.axis_index("ctx")
    core = lax.rem(index, 2)
    chip = index // 2
    chips = lax.axis_size("ctx") // 2
    dp = lax.axis_index("dp")
    parts = lax.axis_size("dp")
    half = value.shape[0] // 2
    keep = lax.dynamic_slice_in_dim(value, core * half, half, 0)
    give = lax.dynamic_slice_in_dim(value, (1 - core) * half, half, 0)
    value = keep + swapped(give)
    size = half // parts
    piece = lambda k: lax.dynamic_slice_in_dim(value, lax.rem(dp + k, parts) * size, size, 0)
    total = piece(0)
    for k in range(1, parts):
        total = total + rotated(piece(k), "dp", k)
    gathered = jnp.zeros((chips,) + total.shape, F32)
    put = lambda into, at, what: lax.dynamic_update_slice_in_dim(into, what[None], at, 0)
    gathered = put(gathered, chip, total)
    for k in range(1, chips):
        gathered = put(gathered, lax.rem(chip + chips - k, chips), rotated(total, "ctx", 2 * k))
    total = gathered[0]
    for k in range(1, chips):
        total = total + gathered[k]
    gathered = jnp.zeros((parts,) + total.shape, F32)
    gathered = put(gathered, dp, total)
    for k in range(1, parts):
        gathered = put(gathered, lax.rem(dp + parts - k, parts), rotated(total, "dp", k))
    mine = gathered.reshape((half,) + total.shape[1:])
    other = swapped(mine)
    first = core == 0
    return jnp.concatenate([jnp.where(first, mine, other), jnp.where(first, other, mine)], axis=0)


def local(projected, short_filter, residues, decay_rates, skip_gain, cotangent):
    rows = projected.shape[1]
    channels = projected.shape[3]
    taps = short_filter.shape[1]
    groups, poles = residues.shape
    width = channels // groups
    run = (rows + SUB) // SUB
    held = rows + SUB
    p = projected[0].transpose(1, 0, 2)
    u = cotangent[0]
    hb = shifted(p[:, rows - SUB :], "ctx", 1)
    ha = shifted(jnp.concatenate([p[:, :SUB], u[None, :SUB]], axis=0), "ctx", -1)

    rate = decay_rates.T
    weight = residues.T
    sub = np.arange(SUB)
    powers = np.stack([run * (7 - sub) - SUB, run * sub, 1 + run * sub, rows - run * (sub + 1) + 1])
    table = jnp.exp(-rate[None, :, None, :] * powers.astype(np.float32)[:, None, :, None])
    we, wb = table[0], table[1]
    cz, cy = weight[:, None, :] * table[2], weight[:, None, :] * table[3]
    f1 = jnp.exp(-rate)
    f_all = jnp.exp(-rate * rows)
    steps = np.array([1, run, 2 * run, 4 * run], np.float32)
    factor = jnp.exp(-rate[None] * steps[:, None, None])
    factor = jnp.concatenate([weight[None] * factor[:1], factor[1:]], axis=0)
    reach = np.array([1, 1, 2, 4])[:, None]
    down, up = sub[None] >= reach, sub[None] < SUB - reach
    join_e = jnp.where(down[:, None, :, None], factor[:, :, None, :], 0.0)
    join_a = jnp.where(up[:, None, :, None], factor[:, :, None, :], 0.0)
    close = np.arange(-taps, run).astype(np.float32)
    near = jnp.sum(weight[:, None, :] * jnp.exp(-rate[:, None, :] * close[None, :, None]), axis=0)

    def by_w(*shape):
        axis = len(shape) - 1
        return pl.BlockSpec(shape, lambda w: (0,) * axis + (w,))

    def per_w(*shape):
        return pl.BlockSpec((1,) + shape, lambda w: (w,) + (0,) * len(shape))

    def fixed(value):
        return pl.BlockSpec(value.shape, lambda w: (0,) * value.ndim)

    params = pltpu.CompilerParams(vmem_limit_bytes=48 * 1024 * 1024)
    shape_of = jax.ShapeDtypeStruct
    state_shape = shape_of((poles, SUB, channels), F32)
    qkvg, blocks_e, blocks_a, ends = pl.pallas_call(
        states_kernel,
        grid=(width,),
        in_specs=[
            by_w(3, rows, groups), by_w(3, SUB, groups), by_w(4, SUB, groups), by_w(rows, groups),
            by_w(3, taps, groups), fixed(f1), fixed(we), fixed(wb),
        ],
        out_specs=[
            by_w(4, held, groups), by_w(poles, SUB, groups), by_w(poles, SUB, groups),
            pl.BlockSpec((2, 1, poles, groups), lambda w: (0, w, 0, 0)),
        ],
        out_shape=[
            shape_of((4, held, channels), F32), state_shape, state_shape,
            shape_of((2, width, poles, groups), F32),
        ],
        scratch_shapes=[pltpu.VMEM((4, held + SUB, LANES), F32)],
        compiler_params=params,
        name="states",
    )(p, hb, ha, u, short_filter, f1, we, wb)

    other, found, chip_e = outward(ends, f_all)
    near, _ = lax.optimization_barrier((near, chip_e))

    conv, convg, from_e, from_a = pl.pallas_call(
        blocks_kernel,
        grid=(width,),
        in_specs=[
            by_w(4, held, groups), by_w(poles, SUB, groups), by_w(poles, SUB, groups), fixed(near),
            by_w(1, groups), fixed(join_e), fixed(join_a),
        ],
        out_specs=[by_w(held, groups)] * 2 + [by_w(poles, SUB, groups)] * 2,
        out_shape=[shape_of((held, channels), F32)] * 2 + [state_shape] * 2,
        compiler_params=params,
        cost_estimate=pl.CostEstimate(
            flops=60 * rows * channels, bytes_accessed=45 * 2**20, transcendentals=0
        ),
        name="blocks",
    )(qkvg, blocks_e, blocks_a, near, skip_gain[None], join_e, join_a)

    found, conv = lax.optimization_barrier((found, conv))
    enter, arrive = inward(other, found, f_all)

    count = 3 * taps + 3
    output, grad_p, sums = pl.pallas_call(
        final_kernel,
        grid=(width,),
        in_specs=[
            by_w(3, rows, groups), by_w(3, SUB, groups), by_w(rows, groups), by_w(4, SUB, groups),
            by_w(4, held, groups), by_w(held, groups), by_w(held, groups),
            by_w(poles, SUB, groups), by_w(poles, SUB, groups),
            per_w(poles, groups), per_w(poles, groups),
            by_w(3, taps, groups), fixed(f1), fixed(cz), fixed(cy),
        ],
        out_specs=[by_w(rows, groups), by_w(3, rows, groups), per_w(count, groups)],
        out_shape=[
            shape_of((rows, channels), BF16),
            shape_of((3, rows, channels), BF16),
            shape_of((width, count, groups), F32),
        ],
        scratch_shapes=[
            pltpu.VMEM((3, held + SUB, LANES), F32),
            pltpu.VMEM((held, LANES), F32),
            pltpu.VMEM((3, held + SUB, LANES), F32),
            pltpu.VMEM((held, LANES), F32),
        ],
        compiler_params=params,
        name="final",
    )(
        p, hb, u, ha, qkvg, conv, convg, from_e, from_a, enter, arrive, short_filter, f1, cz, cy,
    )

    total = summed(sums).transpose(1, 0, 2).reshape(count, channels)
    grad_short = total[: 3 * taps].reshape(3, taps, channels)
    grad_skip = total[3 * taps]
    return output[None], grad_p.transpose(1, 0, 2)[None], grad_short, grad_skip


def solution(mesh):
    placed = (P("dp", "ctx", None, None), P(), P(), P(), P(), P("dp", "ctx", None))
    return jax.shard_map(
        local,
        mesh=mesh,
        in_specs=placed,
        out_specs=(P("dp", "ctx", None), P("dp", "ctx", None, None), P(), P()),
        check_vma=False,
    )
```

time: 186 us -> 165 us (0.89)
  waiting for transfers between devices: 39.3 us -> 20.4 us
  Pallas kernels: 89.6 us -> 78.1 us
  starting transfers between devices: 38.8 us -> 43.4 us
  other arithmetic: 8.79 us -> 13.2 us
    ppermute x8, waiting for transfers between devices: 21 us -> 0.02 us  [shifted(): lax.ppermute(value, axis, [(source, source + steps) for source in range(f...]
    pallas_call x1, Pallas kernels: 43.3 us -> 32.1 us  [local(): pl.pallas_call(final_kernel, grid=(width,), in_specs=[by_w(3, rows, group...]
    ppermute x8, starting transfers between devices: 20.6 us -> 24.8 us  [shifted(): lax.ppermute(value, axis, [(source, source + steps) for source in range(f...]
    pallas_call x1, Pallas kernels: 24.8 us -> 22.2 us  [local(): pl.pallas_call(states_kernel, grid=(width,), in_specs=[by_w(3, rows, grou...]
    pallas_call x1, Pallas kernels: 21.5 us -> 23.8 us  [local(): pl.pallas_call(blocks_kernel, grid=(width,), in_specs=[by_w(4, held, grou...]
    mul x2 -> x3, other arithmetic: 1.32 us -> 3.33 us  [the longest x1 1.44 us: inward(): f_chip = f_all * f_all]
    unnamed x32 -> x34, local copies, waits for them, and re-layouts: 3.75 us -> 2.27 us
    ppermute x6 -> x4, waiting for transfers between devices: 5.48 us -> 6.93 us  [swapped(): return lax.ppermute(value, 'ctx', [(s, s ^ 1) for s in range(count)])]
  transfers between devices with their start and end apart: 23 -> 21, of which waited for: 18 -> 12; matrix products, arithmetic and copies ran while one was open for 3% -> 4% of each run, Pallas kernels for 12% -> 15%
where the time goes in v2:
time: 165 us; the launch traced here: 163 us
  Pallas kernels  78.1 us (47%)
  starting transfers between devices  43.4 us (26%)
  waiting for transfers between devices  20.4 us (12%)
  other arithmetic  13.2 us (8%)
  local copies, waits for them, and re-layouts  6.26 us (4%)
    pallas_call x1, Pallas kernels, local(): pl.pallas_call(final_kernel, grid=(width,), in_specs=[by_w(3, rows, group...  32.1 us
    ppermute x8, starting transfers between devices, shifted(): lax.ppermute(value, axis, [(source, source + steps) for source in range(f...  24.8 us
    pallas_call x1, Pallas kernels, local(): pl.pallas_call(blocks_kernel, grid=(width,), in_specs=[by_w(4, held, grou...  23.8 us
    pallas_call x1, Pallas kernels, local(): pl.pallas_call(states_kernel, grid=(width,), in_specs=[by_w(3, rows, grou...  22.2 us
    ppermute x9, starting transfers between devices, rotated(): lax.ppermute(value, axis, [(s, (s + steps) % count) for s in range(count)])  14 us
    ppermute x9, waiting for transfers between devices, rotated(): lax.ppermute(value, axis, [(s, (s + steps) % count) for s in range(count)])  13.4 us
    ppermute x4, waiting for transfers between devices, swapped(): return lax.ppermute(value, 'ctx', [(s, s ^ 1) for s in range(count)])  6.93 us
    ppermute x4, starting transfers between devices, swapped(): return lax.ppermute(value, 'ctx', [(s, s ^ 1) for s in range(count)])  4.6 us
  transfers between devices with their start and end apart: 21, of which 12 were waited for; matrix products, arithmetic and copies ran while one was open for 4% of the time, Pallas kernels for 15%

profile of v2, /device:TPU:0, one launch (start us, length us, event | category | flops | bytes accessed | tf_op | source)
XLA Modules:
  0.0 162.6 jit_solution(4858725128115054324)
XLA Ops:
  0.6 0.0 copy-start
  0.7 1.3 fusion.15
  2.0 0.9 slice.76
  2.9 1.3 collective-permute-start.1
  4.2 3.1 %collective-permute-start = (bf16[3,8,8192]{2,1,0:T(8,128)(2,1)S(1)}, bf16[3,8,8192]{2,1,0:T(8,128)(2,1)S(1)}, u32[]{:S(2)}, u32[]{:S(2)}) collective-permute-start(bf16[3,8,8192]{2,1,0:T(8,128)(2,1)S(1)} %get-tuple-element.47), channel_id=1, source_target_pairs={{0,1},{1,2},{2,3},{3,4},{4,5},{5,6},{6,7},{8,9},{9,10},{10,11},{11... | collective-permute-start | bytes 1179656 | tf_op jit(solution)/shard_map/ppermute | solution.py:198
  7.3 0.8 negate_bitcast_fusion
  8.1 0.9 multiply_exponential_fusion
  9.0 1.4 fusion.14
  10.5 0.0 copy-start.12
  10.5 22.2 %states.1 = (f32[4,136,8192]{2,1,0:T(8,128)}, f32[16,8,8192]{2,1,0:T(8,128)}, f32[16,8,8192]{2,1,0:T(8,128)}, f32[2,16,16,512]{3,2,1,0:T(8,128)}) custom-call(bf16[3,128,8192]{2,1,0:T(8,128)(2,1)} %bitcast.104, bf16[3,8,8192]{2,1,0:T(8,128)(2,1)S(1)} %collective-permute-done.hb, bf16[4,8,8192]{2,1,0:T(8,128)(2,1)S(1)} %collective-permute-done.1.ha, ...), custom_call_target="tpu_custom_call" | custom-call | tf_op jit(solution)/shard_map/states/pallas_call | solution.py:331
  32.8 0.0 copy-start.13
  32.8 0.0 copy-start.14
  32.8 0.0 copy-start.5
  32.8 4.3 %collective-permute-start.2 = (f32[2,16,16,512]{3,2,1,0:T(8,128)}, f32[2,16,16,512]{3,2,1,0:T(8,128)}, u32[]{:S(2)}, u32[]{:S(2)}) collective-permute-start(f32[2,16,16,512]{3,2,1,0:T(8,128)} %get-tuple-element.24), channel_id=1, source_target_pairs={{0,1},{1,0},{2,3},{3,2},{4,5},{5,4},{6,7},{7,6},{8,9},{9,8},{10,11... | collective-permute-start | bytes 3145736 | tf_op jit(solution)/shard_map/ppermute | solution.py:208
  37.2 0.1 multiply_exponential_fusion.1
  37.3 2.5 %collective-permute-done.2 = f32[2,16,16,512]{3,2,1,0:T(8,128)} collective-permute-done((f32[2,16,16,512]{3,2,1,0:T(8,128)}, f32[2,16,16,512]{3,2,1,0:T(8,128)}, u32[]{:S(2)}, u32[]{:S(2)}) %collective-permute-start.2) | collective-permute-done | bytes 1048608 | tf_op jit(solution)/shard_map/ppermute | solution.py:208
  39.8 1.3 dynamic-slice_select_fusion.1
  41.1 0.1 fusion.10
  41.2 4.6 %collective-permute-start.3 = (f32[8,16,512]{2,1,0:T(8,128)S(1)}, f32[8,16,512]{2,1,0:T(8,128)S(1)}, u32[]{:S(2)}, u32[]{:S(2)}) collective-permute-start(f32[8,16,512]{2,1,0:T(8,128)S(1)} %get-tuple-element.55), channel_id=1, source_target_pairs={{0,2},{1,3},{2,4},{3,5},{4,6},{5,7},{8,10},{9,11},{10,12},{11,13},... | collective-permute-start | bytes 786440 | tf_op jit(solution)/shard_map/ppermute | solution.py:198
  45.8 0.8 slice_multiply_fusion
  46.6 1.0 multiply_reduce_fusion.near
  47.6 4.5 %collective-permute-start.5 = (f32[8,16,512]{2,1,0:T(8,128)S(1)}, f32[8,16,512]{2,1,0:T(8,128)S(1)}, u32[]{:S(2)}, u32[]{:S(2)}) collective-permute-start(f32[8,16,512]{2,1,0:T(8,128)S(1)} %get-tuple-element.55), channel_id=1, source_target_pairs={{0,4},{1,5},{2,6},{3,7},{8,12},{9,13},{10,14},{11,15},{16,20},{17,... | collective-permute-start | bytes 786440 | tf_op jit(solution)/shard_map/ppermute | solution.py:198
  52.1 1.3 collective-permute-start.4
  53.4 1.3 collective-permute-start.6
  54.7 7.6 %collective-permute-start.7 = (f32[8,16,512]{2,1,0:T(8,128)S(1)}, f32[8,16,512]{2,1,0:T(8,128)S(1)}, u32[]{:S(2)}, u32[]{:S(2)}) collective-permute-start(f32[8,16,512]{2,1,0:T(8,128)S(1)} %get-tuple-element.55), channel_id=1, source_target_pairs={{0,6},{1,7},{8,14},{9,15},{16,22},{17,23},{24,30},{25,31}} | collective-permute-start | bytes 786440 | tf_op jit(solution)/shard_map/ppermute | solution.py:198
  62.3 1.3 collective-permute-start.8
  63.6 0.3 broadcast_select_fusion
  64.0 23.8 %blocks.1 = (f32[136,8192]{1,0:T(8,128)}, f32[136,8192]{1,0:T(8,128)}, f32[16,8,8192]{2,1,0:T(8,128)}, f32[16,8,8192]{2,1,0:T(8,128)}) custom-call(f32[4,136,8192]{2,1,0:T(8,128)} %get-tuple-element.23.kvg.qkvg, f32[16,8,8192]{2,1,0:T(8,128)} %get-tuple-element.25.blocks_e, f32[16,8,8192]{2,1,0:T(8,128)} %get-tuple-element.26.blocks_a, ...), custom_call_target="tpu_custom_call" | custom-call | flops 62914560 | bytes 47185920 | tf_op jit(solution)/shard_map/blocks/pallas_call | solution.py:354
  87.8 0.2 add_bitcast_fusion.1
  88.0 0.7 copy-done.7
  88.7 0.8 pad_maximum_fusion.2
  89.6 1.1 fusion.7
  90.7 1.1 collective-permute-done.9
  91.8 1.3 broadcast_select_fusion.3
  93.2 1.5 fusion.4
  94.7 32.1 %final.1 = (bf16[128,8192]{1,0:T(8,128)(2,1)}, bf16[3,128,8192]{2,1,0:T(8,128)(2,1)}, f32[16,24,512]{2,1,0:T(8,128)S(1)}) custom-call(bf16[3,128,8192]{2,1,0:T(8,128)(2,1)} %bitcast.105, bf16[3,8,8192]{2,1,0:T(8,128)(2,1)S(1)} %copy-done.3, bf16[128,8192]{1,0:T(8,128)(2,1)S(1)} %bitcast.101, bf16[4,8,8192]{2,1,0:T(8,128)(2,1)S(1)} %collective-permute-done.1.ha, ...), custom_call_target="tpu_custom_call" | custom-call | tf_op jit(solution)/shard_map/final/pallas_call | solution.py:374
  126.8 0.9 copy-done.4
  127.7 0.2 collective-permute-start.10
  127.9 1.6 collective-permute-done.10
  129.5 1.1 dynamic-slice_add_fusion
  130.6 1.5 collective-permute-start.11
  132.1 1.5 collective-permute-start.12
  133.6 1.4 collective-permute-start.13
  135.1 1.9 %collective-permute-done.11 = f32[2,24,512]{2,1,0:T(8,128)S(1)} collective-permute-done((f32[2,24,512]{2,1,0:T(8,128)S(1)}, f32[2,24,512]{2,1,0:T(8,128)S(1)}, u32[]{:S(2)}, u32[]{:S(2)}) %collective-permute-start.11) | collective-permute-done | bytes 98336 | tf_op jit(solution)/shard_map/ppermute | solution.py:203
  137.0 1.4 collective-permute-done.12
  138.4 0.1 collective-permute-done.13
  138.6 0.1 collective-permute-start.14
  138.7 5.0 %collective-permute-start.15 = (f32[2,24,512]{2,1,0:T(8,128)S(1)}, f32[2,24,512]{2,1,0:T(8,128)S(1)}, u32[]{:S(2)}, u32[]{:S(2)}) collective-permute-start(f32[2,24,512]{2,1,0:T(8,128)S(1)} %get-tuple-element.45), channel_id=1, source_target_pairs={{0,4},{1,5},{2,6},{3,7},{4,0},{5,1},{6,2},{7,3},{8,12},{9,13},{10,... | collective-permute-start | bytes 294920 | tf_op jit(solution)/shard_map/ppermute | solution.py:203
  143.7 3.1 %collective-permute-done.14 = f32[2,24,512]{2,1,0:T(8,128)S(1)} collective-permute-done((f32[2,24,512]{2,1,0:T(8,128)S(1)}, f32[2,24,512]{2,1,0:T(8,128)S(1)}, u32[]{:S(2)}, u32[]{:S(2)}) %collective-permute-start.14) | collective-permute-done | bytes 98336 | tf_op jit(solution)/shard_map/ppermute | solution.py:203
  146.8 3.5 %collective-permute-done.15 = f32[2,24,512]{2,1,0:T(8,128)S(1)} collective-permute-done((f32[2,24,512]{2,1,0:T(8,128)S(1)}, f32[2,24,512]{2,1,0:T(8,128)S(1)}, u32[]{:S(2)}, u32[]{:S(2)}) %collective-permute-start.15) | collective-permute-done | bytes 98336 | tf_op jit(solution)/shard_map/ppermute | solution.py:203
  150.5 1.4 collective-permute-start.17
  151.9 0.3 collective-permute-start.18
  152.1 2.8 %collective-permute-start.19 = (f32[2,24,512]{2,1,0:T(8,128)S(1)}, f32[2,24,512]{2,1,0:T(8,128)S(1)}, u32[]{:S(2)}, u32[]{:S(2)}) collective-permute-start(f32[2,24,512]{2,1,0:T(8,128)S(1)} %bitcast.112), channel_id=1, source_target_pairs={{0,24},{8,0},{16,8},{24,16},{1,25},{9,1},{17,9},{25,17},{2,26},{10... | collective-permute-start | bytes 294920 | tf_op jit(solution)/shard_map/ppermute | solution.py:203
  155.0 2.1 %collective-permute-done.17 = f32[2,24,512]{2,1,0:T(8,128)S(1)} collective-permute-done((f32[2,24,512]{2,1,0:T(8,128)S(1)}, f32[2,24,512]{2,1,0:T(8,128)S(1)}, u32[]{:S(2)}, u32[]{:S(2)}) %collective-permute-start.17) | collective-permute-done | bytes 98336 | tf_op jit(solution)/shard_map/ppermute | solution.py:203
  157.0 0.9 collective-permute-done.18
  157.9 0.3 collective-permute-done.19
  158.3 0.2 copy.19
  158.5 0.1 collective-permute-start.20
  158.6 1.7 %collective-permute-done.20 = f32[8,24,512]{2,0,1:T(8,128)S(1)} collective-permute-done((f32[8,24,512]{2,0,1:T(8,128)S(1)}, f32[8,24,512]{2,0,1:T(8,128)S(1)}, u32[]{:S(2)}, u32[]{:S(2)}) %collective-permute-start.20) | collective-permute-done | bytes 393248 | tf_op jit(solution)/shard_map/ppermute | solution.py:208
  160.3 0.3 broadcast_select_fusion.5
  160.6 0.1 maximum_bitcast_fusion
  160.6 0.1 slice.117
  160.7 1.2 reshape.36
  162.0 0.6 copy.21
  (53 shorter events, 0.5 us)
Async XLA Ops:
  0.6 9.9 %copy-start = (bf16[1,128,8192]{2,1,0:T(8,128)(2,1)S(1)}, bf16[1,128,8192]{2,1,0:T(8,128)(2,1)}, u32[]{:S(2)}) copy-start(bf16[1,128,8192]{2,1,0:T(8,128)(2,1)} %param.16) | copy-start | bytes 6291460
  0.6 9.9 %copy-start.1 = (f32[3,7,8192]{2,1,0:T(8,128)S(1)}, f32[3,7,8192]{2,1,0:T(8,128)}, u32[]{:S(2)}) copy-start(f32[3,7,8192]{2,1,0:T(8,128)} %filt.3) | copy-start | bytes 2064388
  2.9 7.5 %collective-permute-start.1 = (bf16[4,8,8192]{2,1,0:T(8,128)(2,1)S(1)}, bf16[4,8,8192]{2,1,0:T(8,128)(2,1)S(1)}, u32[]{:S(2)}, u32[]{:S(2)}) collective-permute-start(bf16[4,8,8192]{2,1,0:T(8,128)(2,1)S(1)} %pad_maximum_fusion.1), channel_id=1, source_target_pairs={{1,0},{2,1},{3,2},{4,3},{5,4},{6,5},{7,6},{9,8},{10,9},{11,10},{12... | collective-permute-start | bytes 1572872 | tf_op jit(solution)/shard_map/ppermute | solution.py:198
  4.2 6.2 %collective-permute-start = (bf16[3,8,8192]{2,1,0:T(8,128)(2,1)S(1)}, bf16[3,8,8192]{2,1,0:T(8,128)(2,1)S(1)}, u32[]{:S(2)}, u32[]{:S(2)}) collective-permute-start(bf16[3,8,8192]{2,1,0:T(8,128)(2,1)S(1)} %get-tuple-element.47), channel_id=1, source_target_pairs={{0,1},{1,2},{2,3},{3,4},{4,5},{5,6},{6,7},{8,9},{9,10},{10,11},{11... | collective-permute-start | bytes 1179656 | tf_op jit(solution)/shard_map/ppermute | solution.py:198
  9.0 1.5 copy-start.6
  10.5 22.3 %copy-start.2 = (bf16[3,8,8192]{2,1,0:T(8,128)(2,1)}, bf16[3,8,8192]{2,1,0:T(8,128)(2,1)S(1)}, u32[]{:S(2)}) copy-start(bf16[3,8,8192]{2,1,0:T(8,128)(2,1)S(1)} %collective-permute-done.hb) | copy-start | bytes 1179652
  10.5 26.6 %copy-start.12 = (f32[4]{0:T(128)S(1)}, f32[4]{0:T(128)}, u32[]{:S(2)}) copy-start(f32[4]{0:T(128)} %constant.90) | copy-start | bytes 52
  32.8 13.8 %copy-start.15 = (f32[24]{0:T(128)S(1)}, f32[24]{0:T(128)}, u32[]{:S(2)}) copy-start(f32[24]{0:T(128)} %constant.88) | copy-start | bytes 292
  32.8 30.8 %copy-start.13 = (pred[4,8]{1,0:T(4,128)(4,1)S(1)}, pred[4,8]{1,0:T(4,128)(4,1)}, u32[]{:S(2)}) copy-start(pred[4,8]{1,0:T(4,128)(4,1)} %constant.89) | copy-start | bytes 100
  32.8 30.8 %copy-start.14 = (pred[4,8]{1,0:T(4,128)(4,1)S(1)}, pred[4,8]{1,0:T(4,128)(4,1)}, u32[]{:S(2)}) copy-start(pred[4,8]{1,0:T(4,128)(4,1)} %constant.91) | copy-start | bytes 100
  32.8 31.1 %copy-start.5 = (f32[8192]{0:T(1024)S(1)}, f32[8192]{0:T(1024)}, u32[]{:S(2)}) copy-start(f32[8192]{0:T(1024)} %param.15) | copy-start | bytes 98308
  32.8 7.0 %collective-permute-start.2 = (f32[2,16,16,512]{3,2,1,0:T(8,128)}, f32[2,16,16,512]{3,2,1,0:T(8,128)}, u32[]{:S(2)}, u32[]{:S(2)}) collective-permute-start(f32[2,16,16,512]{3,2,1,0:T(8,128)} %get-tuple-element.24), channel_id=1, source_target_pairs={{0,1},{1,0},{2,3},{3,2},{4,5},{5,4},{6,7},{7,6},{8,9},{9,8},{10,11... | collective-permute-start | bytes 3145736 | tf_op jit(solution)/shard_map/ppermute | solution.py:208
  41.2 21.0 %collective-permute-start.3 = (f32[8,16,512]{2,1,0:T(8,128)S(1)}, f32[8,16,512]{2,1,0:T(8,128)S(1)}, u32[]{:S(2)}, u32[]{:S(2)}) collective-permute-start(f32[8,16,512]{2,1,0:T(8,128)S(1)} %get-tuple-element.55), channel_id=1, source_target_pairs={{0,2},{1,3},{2,4},{3,5},{4,6},{5,7},{8,10},{9,11},{10,12},{11,13},... | collective-permute-start | bytes 786440 | tf_op jit(solution)/shard_map/ppermute | solution.py:198
  47.6 40.2 %collective-permute-start.5 = (f32[8,16,512]{2,1,0:T(8,128)S(1)}, f32[8,16,512]{2,1,0:T(8,128)S(1)}, u32[]{:S(2)}, u32[]{:S(2)}) collective-permute-start(f32[8,16,512]{2,1,0:T(8,128)S(1)} %get-tuple-element.55), channel_id=1, source_target_pairs={{0,4},{1,5},{2,6},{3,7},{8,12},{9,13},{10,14},{11,15},{16,20},{17,... | collective-permute-start | bytes 786440 | tf_op jit(solution)/shard_map/ppermute | solution.py:198
  52.1 35.7 %collective-permute-start.4 = (f32[8,16,512]{2,1,0:T(8,128)S(1)}, f32[8,16,512]{2,1,0:T(8,128)S(1)}, u32[]{:S(2)}, u32[]{:S(2)}) collective-permute-start(f32[8,16,512]{2,1,0:T(8,128)S(1)} %get-tuple-element.54), channel_id=1, source_target_pairs={{2,0},{3,1},{4,2},{5,3},{6,4},{7,5},{10,8},{11,9},{12,10},{13,11},... | collective-permute-start | bytes 786440 | tf_op jit(solution)/shard_map/ppermute | solution.py:198
  53.4 34.4 %collective-permute-start.6 = (f32[8,16,512]{2,1,0:T(8,128)S(1)}, f32[8,16,512]{2,1,0:T(8,128)S(1)}, u32[]{:S(2)}, u32[]{:S(2)}) collective-permute-start(f32[8,16,512]{2,1,0:T(8,128)S(1)} %get-tuple-element.54), channel_id=1, source_target_pairs={{4,0},{5,1},{6,2},{7,3},{12,8},{13,9},{14,10},{15,11},{20,16},{21,... | collective-permute-start | bytes 786440 | tf_op jit(solution)/shard_map/ppermute | solution.py:198
  54.7 33.1 %collective-permute-start.7 = (f32[8,16,512]{2,1,0:T(8,128)S(1)}, f32[8,16,512]{2,1,0:T(8,128)S(1)}, u32[]{:S(2)}, u32[]{:S(2)}) collective-permute-start(f32[8,16,512]{2,1,0:T(8,128)S(1)} %get-tuple-element.55), channel_id=1, source_target_pairs={{0,6},{1,7},{8,14},{9,15},{16,22},{17,23},{24,30},{25,31}} | collective-permute-start | bytes 786440 | tf_op jit(solution)/shard_map/ppermute | solution.py:198
  62.3 25.5 %collective-permute-start.8 = (f32[8,16,512]{2,1,0:T(8,128)S(1)}, f32[8,16,512]{2,1,0:T(8,128)S(1)}, u32[]{:S(2)}, u32[]{:S(2)}) collective-permute-start(f32[8,16,512]{2,1,0:T(8,128)S(1)} %get-tuple-element.54), channel_id=1, source_target_pairs={{6,0},{7,1},{14,8},{15,9},{22,16},{23,17},{30,24},{31,25}} | collective-permute-start | bytes 786440 | tf_op jit(solution)/shard_map/ppermute | solution.py:198
  63.9 23.9 %copy-start.9 = (f32[16,512]{1,0:T(8,128)S(1)}, f32[16,512]{1,0:T(8,128)}, u32[]{:S(2)}) copy-start(f32[16,512]{1,0:T(8,128)} %get-tuple-element.69) | copy-start | bytes 98308
  63.9 23.9 %copy-start.10 = (f32[16,512]{1,0:T(8,128)S(1)}, f32[16,512]{1,0:T(8,128)}, u32[]{:S(2)}) copy-start(f32[16,512]{1,0:T(8,128)} %get-tuple-element.70) | copy-start | bytes 98308
  64.0 25.6 %copy-start.11 = (f32[512,16]{0,1:T(8,128)S(1)}, f32[512,16]{0,1:T(8,128)}, u32[]{:S(2)}) copy-start(f32[512,16]{0,1:T(8,128)} %param.13) | copy-start | bytes 98308
  88.0 0.7 copy-start.7
  88.0 1.5 copy-start.8
  89.6 2.3 %collective-permute-start.9 = (f32[2,8,16,512]{3,2,1,0:T(8,128)}, f32[2,8,16,512]{3,2,1,0:T(8,128)}, u32[]{:S(2)}, u32[]{:S(2)}) collective-permute-start(f32[2,8,16,512]{3,2,1,0:T(8,128)} %pad_maximum_fusion.2), channel_id=1, source_target_pairs={{0,1},{1,0},{2,3},{3,2},{4,5},{5,4},{6,7},{7,6},{8,9},{9,8},{10,11... | collective-permute-start | bytes 1572872 | tf_op jit(solution)/shard_map/ppermute | solution.py:208
  89.6 5.1 %copy-start.3 = (bf16[3,8,8192]{2,1,0:T(8,128)(2,1)S(1)}, bf16[3,8,8192]{2,1,0:T(8,128)(2,1)}, u32[]{:S(2)}) copy-start(bf16[3,8,8192]{2,1,0:T(8,128)(2,1)} %copy-done.2) | copy-start | bytes 1179652
  126.8 0.9 copy-start.4
  127.7 1.8 %collective-permute-start.10 = (f32[8,24,512]{2,1,0:T(8,128)S(1)}, f32[8,24,512]{2,1,0:T(8,128)S(1)}, u32[]{:S(2)}, u32[]{:S(2)}) collective-permute-start(f32[8,24,512]{2,1,0:T(8,128)S(1)} %constant_dynamic-slice_fusion.3), channel_id=1, source_target_pairs={{0,1},{1,0},{2,3},{3,2},{4,5},{5,4},{6,7},{7,6},{8,9},{9,8},{10,11... | collective-permute-start | bytes 1179656 | tf_op jit(solution)/shard_map/ppermute | solution.py:208
  130.6 6.4 %collective-permute-start.11 = (f32[2,24,512]{2,1,0:T(8,128)S(1)}, f32[2,24,512]{2,1,0:T(8,128)S(1)}, u32[]{:S(2)}, u32[]{:S(2)}) collective-permute-start(f32[2,24,512]{2,1,0:T(8,128)S(1)} %get-tuple-element.62), channel_id=1, source_target_pairs={{0,8},{8,16},{16,24},{24,0},{1,9},{9,17},{17,25},{25,1},{2,10},{10... | collective-permute-start | bytes 294920 | tf_op jit(solution)/shard_map/ppermute | solution.py:203
  132.1 6.4 %collective-permute-start.12 = (f32[2,24,512]{2,1,0:T(8,128)S(1)}, f32[2,24,512]{2,1,0:T(8,128)S(1)}, u32[]{:S(2)}, u32[]{:S(2)}) collective-permute-start(f32[2,24,512]{2,1,0:T(8,128)S(1)} %get-tuple-element.64), channel_id=1, source_target_pairs={{0,16},{8,24},{16,0},{24,8},{1,17},{9,25},{17,1},{25,9},{2,18},{10... | collective-permute-start | bytes 294920 | tf_op jit(solution)/shard_map/ppermute | solution.py:203
  133.6 4.9 %collective-permute-start.13 = (f32[2,24,512]{2,1,0:T(8,128)S(1)}, f32[2,24,512]{2,1,0:T(8,128)S(1)}, u32[]{:S(2)}, u32[]{:S(2)}) collective-permute-start(f32[2,24,512]{2,1,0:T(8,128)S(1)} %get-tuple-element.63), channel_id=1, source_target_pairs={{0,24},{8,0},{16,8},{24,16},{1,25},{9,1},{17,9},{25,17},{2,26},{10... | collective-permute-start | bytes 294920 | tf_op jit(solution)/shard_map/ppermute | solution.py:203
  138.6 8.2 %collective-permute-start.14 = (f32[2,24,512]{2,1,0:T(8,128)S(1)}, f32[2,24,512]{2,1,0:T(8,128)S(1)}, u32[]{:S(2)}, u32[]{:S(2)}) collective-permute-start(f32[2,24,512]{2,1,0:T(8,128)S(1)} %get-tuple-element.45), channel_id=1, source_target_pairs={{0,2},{1,3},{2,4},{3,5},{4,6},{5,7},{6,0},{7,1},{8,10},{9,11},{10,... | collective-permute-start | bytes 294920 | tf_op jit(solution)/shard_map/ppermute | solution.py:203
  138.7 11.7 %collective-permute-start.15 = (f32[2,24,512]{2,1,0:T(8,128)S(1)}, f32[2,24,512]{2,1,0:T(8,128)S(1)}, u32[]{:S(2)}, u32[]{:S(2)}) collective-permute-start(f32[2,24,512]{2,1,0:T(8,128)S(1)} %get-tuple-element.45), channel_id=1, source_target_pairs={{0,4},{1,5},{2,6},{3,7},{4,0},{5,1},{6,2},{7,3},{8,12},{9,13},{10,... | collective-permute-start | bytes 294920 | tf_op jit(solution)/shard_map/ppermute | solution.py:203
  143.7 6.7 %collective-permute-start.16 = (f32[2,24,512]{2,1,0:T(8,128)S(1)}, f32[2,24,512]{2,1,0:T(8,128)S(1)}, u32[]{:S(2)}, u32[]{:S(2)}) collective-permute-start(f32[2,24,512]{2,1,0:T(8,128)S(1)} %get-tuple-element.45), channel_id=1, source_target_pairs={{0,6},{1,7},{2,0},{3,1},{4,2},{5,3},{6,4},{7,5},{8,14},{9,15},{10,... | collective-permute-start | bytes 294920 | tf_op jit(solution)/shard_map/ppermute | solution.py:203
  150.5 6.5 %collective-permute-start.17 = (f32[2,24,512]{2,1,0:T(8,128)S(1)}, f32[2,24,512]{2,1,0:T(8,128)S(1)}, u32[]{:S(2)}, u32[]{:S(2)}) collective-permute-start(f32[2,24,512]{2,1,0:T(8,128)S(1)} %bitcast.110), channel_id=1, source_target_pairs={{0,8},{8,16},{16,24},{24,0},{1,9},{9,17},{17,25},{25,1},{2,10},{10... | collective-permute-start | bytes 294920 | tf_op jit(solution)/shard_map/ppermute | solution.py:203
  151.9 6.0 %collective-permute-start.18 = (f32[2,24,512]{2,1,0:T(8,128)S(1)}, f32[2,24,512]{2,1,0:T(8,128)S(1)}, u32[]{:S(2)}, u32[]{:S(2)}) collective-permute-start(f32[2,24,512]{2,1,0:T(8,128)S(1)} %bitcast.111), channel_id=1, source_target_pairs={{0,16},{8,24},{16,0},{24,8},{1,17},{9,25},{17,1},{25,9},{2,18},{10... | collective-permute-start | bytes 294920 | tf_op jit(solution)/shard_map/ppermute | solution.py:203
  152.1 6.1 %collective-permute-start.19 = (f32[2,24,512]{2,1,0:T(8,128)S(1)}, f32[2,24,512]{2,1,0:T(8,128)S(1)}, u32[]{:S(2)}, u32[]{:S(2)}) collective-permute-start(f32[2,24,512]{2,1,0:T(8,128)S(1)} %bitcast.112), channel_id=1, source_target_pairs={{0,24},{8,0},{16,8},{24,16},{1,25},{9,1},{17,9},{25,17},{2,26},{10... | collective-permute-start | bytes 294920 | tf_op jit(solution)/shard_map/ppermute | solution.py:203
  158.5 1.8 %collective-permute-start.20 = (f32[8,24,512]{2,0,1:T(8,128)S(1)}, f32[8,24,512]{2,0,1:T(8,128)S(1)}, u32[]{:S(2)}, u32[]{:S(2)}) collective-permute-start(f32[8,24,512]{2,0,1:T(8,128)S(1)} %copy.19), channel_id=1, source_target_pairs={{0,1},{1,0},{2,3},{3,2},{4,5},{5,4},{6,7},{7,6},{8,9},{9,8},{10,11... | collective-permute-start | bytes 1179656 | tf_op jit(solution)/shard_map/ppermute | solution.py:208

commit v3 on v2

v3 whole, which is shorter than its diff:
```python
import functools

import jax
import jax.numpy as jnp
import numpy as np
from jax import lax
from jax.experimental import pallas as pl
from jax.experimental.pallas import tpu as pltpu
from jax.sharding import PartitionSpec as P

LANES = 128
SUB = 8
F32 = jnp.float32
BF16 = jnp.bfloat16


def spread(row):
    return jnp.broadcast_to(row, (SUB, LANES))


def added(terms):
    while len(terms) > 1:
        pairs = [terms[k] + terms[k + 1] for k in range(0, len(terms) - 1, 2)]
        terms = pairs + terms[len(terms) - len(terms) % 2 :]
    return terms[0]


def states_kernel(p, hb, ha, u, filt, f1, we, wb, xg, blocks_e, blocks_a, ends, xs):
    rows = p.shape[1]
    run = (rows + SUB) // SUB
    taps = filt.shape[1]
    poles, groups = f1.shape
    own = rows - run * (SUB - 1)
    tiles = groups // LANES

    def tile(lt, carry):
        lanes = pl.ds(pl.multiple_of(lt * LANES, LANES), LANES)
        part = pl.ds(pl.multiple_of(lax.rem(lt, tiles) * LANES, LANES), LANES)
        which = lt // tiles
        inside = lax.broadcasted_iota(jnp.int32, (SUB, LANES), 0) < SUB - 1
        for j in range(3):
            xs[j, 0:SUB] = hb[j, :, lanes].astype(F32)
            xs[j, SUB : SUB + rows] = p[j, :, lanes].astype(F32)
            xs[j, SUB + rows :] = ha[j, :, lanes].astype(F32)
        xs[3, SUB : SUB + rows] = u[:, lanes].astype(F32)
        xs[3, SUB + rows :] = ha[3, :, lanes].astype(F32)

        def mixed(j):
            tap = [spread(filt[j, i : i + 1, lanes]) for i in range(taps)]
            view = [xs[j, pl.ds(SUB + a, SUB, stride=run), :] for a in range(1 - taps, run)]
            return [
                added([tap[i] * view[a + taps - 1 - i] for i in range(taps)]) for a in range(run)
            ]

        decay = [spread(f1[n : n + 1, part]) for n in range(poles)]
        key, value = mixed(1), mixed(2)
        state = None
        for a in range(run):
            x = key[a] * value[a]
            xg[0, SUB * a : SUB * a + SUB, lanes] = x
            if a >= own:
                x = jnp.where(inside, x, 0.0)
            state = [x] * poles if a == 0 else [decay[n] * state[n] + x for n in range(poles)]
        for n in range(poles):
            blocks_e[n, :, lanes] = state[n]
            ends[0, which, n : n + 1, part] = jnp.sum(state[n] * we[n, :, part], axis=0, keepdims=True)
        query = mixed(0)
        state = None
        for a in range(run - 1, -1, -1):
            x = xs[3, pl.ds(SUB + a, SUB, stride=run), :] * query[a]
            xg[1, SUB * a : SUB * a + SUB, lanes] = x
            if a >= own:
                x = jnp.where(inside, x, 0.0)
            state = [x] * poles if a == run - 1 else [decay[n] * state[n] + x for n in range(poles)]
        for n in range(poles):
            blocks_a[n, :, lanes] = state[n]
            ends[1, which, n : n + 1, part] = jnp.sum(state[n] * wb[n, :, part], axis=0, keepdims=True)
        return carry

    lax.fori_loop(0, p.shape[2] // LANES, tile, 0)


def blocks_kernel(xg, blocks_e, blocks_a, near, skip, join_e, join_a, conv, from_e, from_a):
    run = xg.shape[1] // SUB
    rows = xg.shape[1] - SUB
    taps = near.shape[0] - run
    poles, groups = blocks_e.shape[0], near.shape[1]
    own = rows - run * (SUB - 1)
    tiles = groups // LANES

    def tile(lt, carry):
        lanes = pl.ds(pl.multiple_of(lt * LANES, LANES), LANES)
        part = pl.ds(pl.multiple_of(lax.rem(lt, tiles) * LANES, LANES), LANES)
        inside = lax.broadcasted_iota(jnp.int32, (SUB, LANES), 0) < SUB - 1
        gain = spread(skip[0:1, lanes])
        lag = [spread(near[taps + m : taps + m + 1, part]) for m in range(run)]
        lag[0] = lag[0] + gain
        x = [xg[0, SUB * a : SUB * a + SUB, lanes] for a in range(run)]
        for a in range(run):
            conv[0, SUB * a : SUB * a + SUB, lanes] = added([lag[m] * x[a - m] for m in range(a + 1)])
        x = [xg[1, SUB * a : SUB * a + SUB, lanes] for a in range(run)]
        masked = [x[a] if a < own else jnp.where(inside, x[a], 0.0) for a in range(run)]
        past = [jnp.where(inside, 0.0, gain)] + [
            jnp.where(inside, 0.0, -spread(near[taps - m : taps - m + 1, part]))
            for m in range(1, taps - 1)
        ]
        for a in range(run):
            terms = [lag[m] * masked[a + m] for m in range(run - a)]
            if own <= a < own + taps - 1:
                terms = terms + [past[m] * x[a - m] for m in range(a - own + 1)]
            conv[1, SUB * a : SUB * a + SUB, lanes] = added(terms)
        for n in range(poles):
            value = pltpu.roll(blocks_e[n, :, lanes], 1, 0) * join_e[0, n, :, part]
            for k, step in ((1, 1), (2, 2), (3, 4)):
                value = value + pltpu.roll(value, step, 0) * join_e[k, n, :, part]
            from_e[n, :, lanes] = value
            value = pltpu.roll(blocks_a[n, :, lanes], SUB - 1, 0) * join_a[0, n, :, part]
            for k, step in ((1, 1), (2, 2), (3, 4)):
                value = value + pltpu.roll(value, SUB - step, 0) * join_a[k, n, :, part]
            from_a[n, :, lanes] = value
        return carry

    lax.fori_loop(0, xg.shape[2] // LANES, tile, 0)


def final_kernel(
    p, hb, u, ha, conv, from_e, from_a, enter, arrive, filt, f1, cz, cy,
    output, grad_p, sums, ps, us, qs, gs, os,
):
    rows = p.shape[1]
    run = (rows + SUB) // SUB
    taps = filt.shape[1]
    poles, groups = f1.shape
    own = rows - run * (SUB - 1)
    tiles = groups // LANES

    def tile(lt, carry):
        lanes = pl.ds(pl.multiple_of(lt * LANES, LANES), LANES)
        part = pl.ds(pl.multiple_of(lax.rem(lt, tiles) * LANES, LANES), LANES)
        which = lt // tiles
        inside = lax.broadcasted_iota(jnp.int32, (SUB, LANES), 0) < SUB - 1
        for j in range(3):
            ps[j, 0:SUB] = hb[j, :, lanes].astype(F32)
            ps[j, SUB : SUB + rows] = p[j, :, lanes].astype(F32)
            ps[j, SUB + rows :] = ha[j, :, lanes].astype(F32)
        us[0:rows] = u[:, lanes].astype(F32)
        us[rows:] = ha[3, :, lanes].astype(F32)
        for j in range(3):
            tap = [spread(filt[j, i : i + 1, lanes]) for i in range(taps)]
            view = [ps[j, pl.ds(SUB + a, SUB, stride=run), :] for a in range(1 - taps, run)]
            for a in range(run):
                qs[j, SUB * a : SUB * a + SUB] = added(
                    [tap[i] * view[a + taps - 1 - i] for i in range(taps)]
                )
        decay = [spread(f1[n : n + 1, part]) for n in range(poles)]

        state = [
            from_e[n, :, lanes] + cz[n, :, part] * spread(enter[which, n : n + 1, part])
            for n in range(poles)
        ]
        skip_sum = None
        for a in range(run):
            at = slice(SUB * a, SUB * a + SUB)
            query, upstream = qs[0, at], us[pl.ds(a, SUB, stride=run), :]
            term = (qs[1, at] * qs[2, at]) * (query * upstream)
            if a >= own:
                term = jnp.where(inside, term, 0.0)
            skip_sum = term if a == 0 else skip_sum + term
            filtered = conv[0, at, lanes] + added(list(state))
            os[pl.ds(a, SUB, stride=run), :] = query * filtered
            gs[0, pl.ds(a, SUB, stride=run), :] = upstream * filtered
            if a + 1 < run:
                state = [state[n] * decay[n] for n in range(poles)]
        output[:, lanes] = os[0:rows].astype(BF16)

        state = [
            from_a[n, :, lanes] + cy[n, :, part] * spread(arrive[which, n : n + 1, part])
            for n in range(poles)
        ]
        for a in range(run - 1, -1, -1):
            at = slice(SUB * a, SUB * a + SUB)
            grad = conv[1, at, lanes] + added(list(state))
            gs[1, pl.ds(a, SUB, stride=run), :] = grad * qs[2, at]
            gs[2, pl.ds(a, SUB, stride=run), :] = grad * qs[1, at]
            if a:
                state = [state[n] * decay[n] for n in range(poles)]

        for j in range(3):
            tap = [spread(filt[j, i : i + 1, lanes]) for i in range(taps)]
            grads = [gs[j, pl.ds(a, SUB, stride=run), :] for a in range(run + taps - 1)]
            views = [ps[j, pl.ds(SUB + a, SUB, stride=run), :] for a in range(1 - taps, run)]
            sums_of = [None] * taps
            for a in range(run):
                total = added([tap[i] * grads[a + i] for i in range(taps)])
                os[pl.ds(a, SUB, stride=run), :] = total
                grad = grads[a] if a < own else jnp.where(inside, grads[a], 0.0)
                for i in range(taps):
                    term = grad * views[a + taps - 1 - i]
                    sums_of[i] = term if a == 0 else sums_of[i] + term
            grad_p[j, :, lanes] = os[0:rows].astype(BF16)
            for i in range(taps):
                at = j * taps + i
                sums[which, at : at + 1, part] = jnp.sum(sums_of[i], axis=0, keepdims=True)
        at = 3 * taps
        sums[which, at : at + 1, part] = jnp.sum(skip_sum, axis=0, keepdims=True)
        return carry

    lax.fori_loop(0, p.shape[2] // LANES, tile, 0)


def shifted(value, axis, steps):
    count = lax.axis_size(axis)
    first, last = (max(0, -steps), min(count, count - steps))
    return lax.ppermute(value, axis, [(source, source + steps) for source in range(first, last)])


def rotated(value, axis, steps):
    count = lax.axis_size(axis)
    return lax.ppermute(value, axis, [(s, (s + steps) % count) for s in range(count)])


def swapped(value):
    count = lax.axis_size("ctx")
    return lax.ppermute(value, "ctx", [(s, s ^ 1) for s in range(count)])


def joined(ends, f_all):
    core = lax.rem(lax.axis_index("ctx"), 2)
    half = ends.shape[1] // 2
    other = swapped(ends)
    first = core == 0
    mine = lax.dynamic_slice_in_dim(ends, core * half, half, 1)
    theirs = lax.dynamic_slice_in_dim(other, core * half, half, 1)
    one, two = jnp.where(first, mine, theirs), jnp.where(first, theirs, mine)
    return other, f_all * one[0] + two[0], one[1] + f_all * two[1]


def scanned(chip_e, chip_a, f_all, beside):
    chips = lax.axis_size("ctx") // 2
    f_chip = f_all * f_all
    before = after = None
    reach = 1
    kept = None
    while reach < chips:
        early, late = shifted(chip_e, "ctx", 2 * reach), shifted(chip_a, "ctx", -2 * reach)
        if 2 * reach >= chips:
            kept = beside(chip_e)
            (early, late), kept = lax.optimization_barrier(((early, late), kept))
        if before is None:
            before, after = early, late
        else:
            factor = f_chip ** (reach - 1)
            before, after = before + factor * early, after + factor * late
        factor = f_chip**reach
        chip_e, chip_a = chip_e + factor * early, chip_a + factor * late
        reach = 2 * reach
    return before, after, kept


def inward(other, before, after, f_all):
    first = lax.rem(lax.axis_index("ctx"), 2) == 0
    both = jnp.stack([before, after])
    found = swapped(both)
    both = jnp.concatenate([jnp.where(first, both, found), jnp.where(first, found, both)], axis=1)
    enter = jnp.where(first, both[0], f_all * both[0] + other[0])
    arrive = jnp.where(first, other[1] + f_all * both[1], both[1])
    return enter, arrive


def summed(value):
    index = lax.axis_index("ctx")
    core = lax.rem(index, 2)
    chip = index // 2
    chips = lax.axis_size("ctx") // 2
    dp = lax.axis_index("dp")
    parts = lax.axis_size("dp")
    half = value.shape[0] // 2
    keep = lax.dynamic_slice_in_dim(value, core * half, half, 0)
    give = lax.dynamic_slice_in_dim(value, (1 - core) * half, half, 0)
    value = keep + swapped(give)
    size = half // parts
    piece = lambda k: lax.dynamic_slice_in_dim(value, lax.rem(dp + k, parts) * size, size, 0)
    total = piece(0)
    for k in range(1, parts):
        total = total + rotated(piece(k), "dp", k)
    gathered = jnp.zeros((chips,) + total.shape, F32)
    put = lambda into, at, what: lax.dynamic_update_slice_in_dim(into, what[None], at, 0)
    gathered = put(gathered, chip, total)
    for k in range(1, chips):
        gathered = put(gathered, lax.rem(chip + chips - k, chips), rotated(total, "ctx", 2 * k))
    total = gathered[0]
    for k in range(1, chips):
        total = total + gathered[k]
    gathered = jnp.zeros((parts,) + total.shape, F32)
    gathered = put(gathered, dp, total)
    for k in range(1, parts):
        gathered = put(gathered, lax.rem(dp + parts - k, parts), rotated(total, "dp", k))
    mine = gathered.reshape((half,) + total.shape[1:])
    other = swapped(mine)
    first = core == 0
    return jnp.concatenate([jnp.where(first, mine, other), jnp.where(first, other, mine)], axis=0)


def local(projected, short_filter, residues, decay_rates, skip_gain, cotangent):
    rows = projected.shape[1]
    channels = projected.shape[3]
    taps = short_filter.shape[1]
    groups, poles = residues.shape
    width = channels // groups
    run = (rows + SUB) // SUB
    held = rows + SUB
    p = projected[0].transpose(1, 0, 2)
    u = cotangent[0]
    hb = shifted(p[:, rows - SUB :], "ctx", 1)
    ha = shifted(jnp.concatenate([p[:, :SUB], u[None, :SUB]], axis=0), "ctx", -1)

    rate = decay_rates.T
    weight = residues.T
    sub = np.arange(SUB)
    powers = np.stack([run * (7 - sub) - SUB, run * sub, 1 + run * sub, rows - run * (sub + 1) + 1])
    table = jnp.exp(-rate[None, :, None, :] * powers.astype(np.float32)[:, None, :, None])
    we, wb = table[0], table[1]
    cz, cy = weight[:, None, :] * table[2], weight[:, None, :] * table[3]
    f1 = jnp.exp(-rate)
    f_all = jnp.exp(-rate * rows)
    steps = np.array([1, run, 2 * run, 4 * run], np.float32)
    factor = jnp.exp(-rate[None] * steps[:, None, None])
    factor = jnp.concatenate([weight[None] * factor[:1], factor[1:]], axis=0)
    reach = np.array([1, 1, 2, 4])[:, None]
    down, up = sub[None] >= reach, sub[None] < SUB - reach
    join_e = jnp.where(down[:, None, :, None], factor[:, :, None, :], 0.0)
    join_a = jnp.where(up[:, None, :, None], factor[:, :, None, :], 0.0)
    close = np.arange(-taps, run).astype(np.float32)
    near = jnp.sum(weight[:, None, :] * jnp.exp(-rate[:, None, :] * close[None, :, None]), axis=0)

    each = 2 if width % 2 == 0 else 1

    def by_w(*shape):
        axis = len(shape)
        return pl.BlockSpec(shape + (each * groups,), lambda w: (0,) * axis + (w,))

    def per_w(*shape):
        return pl.BlockSpec((each,) + shape, lambda w: (w,) + (0,) * len(shape))

    def fixed(value):
        return pl.BlockSpec(
            value.shape, lambda w: (0,) * value.ndim, pipeline_mode=pl.Buffered(1)
        )

    params = pltpu.CompilerParams(vmem_limit_bytes=20 * 1024 * 1024)
    shape_of = jax.ShapeDtypeStruct
    state_shape = shape_of((poles, SUB, channels), F32)
    xg, blocks_e, blocks_a, ends = pl.pallas_call(
        states_kernel,
        grid=(width // each,),
        in_specs=[
            by_w(3, rows), by_w(3, SUB), by_w(4, SUB), by_w(rows), by_w(3, taps),
            fixed(f1), fixed(we), fixed(wb),
        ],
        out_specs=[
            by_w(2, held), by_w(poles, SUB), by_w(poles, SUB),
            pl.BlockSpec((2, each, poles, groups), lambda w: (0, w, 0, 0)),
        ],
        out_shape=[
            shape_of((2, held, channels), F32), state_shape, state_shape,
            shape_of((2, width, poles, groups), F32),
        ],
        scratch_shapes=[pltpu.VMEM((4, held + SUB, LANES), F32)],
        compiler_params=params,
        name="states",
    )(p, hb, ha, u, short_filter, f1, we, wb)

    def blocks(chip_e):
        close, _ = lax.optimization_barrier((near, chip_e))
        return pl.pallas_call(
            blocks_kernel,
            grid=(width // each,),
            in_specs=[
                by_w(2, held), by_w(poles, SUB), by_w(poles, SUB), fixed(near), by_w(1),
                fixed(join_e), fixed(join_a),
            ],
            out_specs=[by_w(2, held), by_w(poles, SUB), by_w(poles, SUB)],
            out_shape=[shape_of((2, held, channels), F32), state_shape, state_shape],
            input_output_aliases={0: 0, 1: 1, 2: 2},
            compiler_params=params,
            cost_estimate=pl.CostEstimate(
                flops=60 * rows * channels, bytes_accessed=35 * 2**20, transcendentals=0
            ),
            name="blocks",
        )(xg, blocks_e, blocks_a, close, skip_gain[None], join_e, join_a)

    other, chip_e, chip_a = joined(ends, f_all)
    before, after, (conv, from_e, from_a) = scanned(chip_e, chip_a, f_all, blocks)
    enter, arrive = inward(other, before, after, f_all)

    count = 3 * taps + 3
    scratch = [
        pltpu.VMEM((3, held + SUB, LANES), F32),
        pltpu.VMEM((held, LANES), F32),
        pltpu.VMEM((3, held, LANES), F32),
        pltpu.VMEM((3, held + SUB, LANES), F32),
        pltpu.VMEM((held, LANES), F32),
    ]
    output, grad_p, sums = pl.pallas_call(
        final_kernel,
        grid=(width // each,),
        in_specs=[
            by_w(3, rows), by_w(3, SUB), by_w(rows), by_w(4, SUB), by_w(2, held),
            by_w(poles, SUB), by_w(poles, SUB), per_w(poles, groups), per_w(poles, groups),
            by_w(3, taps), fixed(f1), fixed(cz), fixed(cy),
        ],
        out_specs=[by_w(rows), by_w(3, rows), per_w(count, groups)],
        out_shape=[
            shape_of((rows, channels), BF16),
            shape_of((3, rows, channels), BF16),
            shape_of((width, count, groups), F32),
        ],
        scratch_shapes=scratch,
        compiler_params=params,
        name="final",
    )(p, hb, u, ha, conv, from_e, from_a, enter, arrive, short_filter, f1, cz, cy)

    total = summed(sums).transpose(1, 0, 2).reshape(count, channels)
    grad_short = total[: 3 * taps].reshape(3, taps, channels)
    grad_skip = total[3 * taps]
    return output[None], grad_p.transpose(1, 0, 2)[None], grad_short, grad_skip


def solution(mesh):
    placed = (P("dp", "ctx", None, None), P(), P(), P(), P(), P("dp", "ctx", None))
    return jax.shard_map(
        local,
        mesh=mesh,
        in_specs=placed,
        out_specs=(P("dp", "ctx", None), P("dp", "ctx", None, None), P(), P()),
        check_vma=False,
    )
```

time: 165 us -> 189 us (1.15)
  local copies, waits for them, and re-layouts: 6.26 us -> 36.2 us
  waiting for transfers between devices: 20.4 us -> 26.3 us
  starting transfers between devices: 43.4 us -> 37.6 us
  Pallas kernels: 78.1 us -> 74.8 us
    unnamed x34 -> x60, local copies, waits for them, and re-layouts: 2.27 us -> 32.2 us
    ppermute x8 -> x6, starting transfers between devices: 24.8 us -> 16.2 us  [shifted(): lax.ppermute(value, axis, [(source, source + steps) for source in range(f...]
    ppermute x8 -> x6, waiting for transfers between devices: 0.02 us -> 6.89 us  [shifted(): lax.ppermute(value, axis, [(source, source + steps) for source in range(f...]
    pallas_call x3, Pallas kernels: 78.1 us -> 74.8 us  [the longest x1 38.4 us: local(): pl.pallas_call(final_kernel, grid=(width // each,), in_specs=[by_w(3, row...]
    ppermute x4, starting transfers between devices: 4.6 us -> 7.47 us  [swapped(): return lax.ppermute(value, 'ctx', [(s, s ^ 1) for s in range(count)])]
  transfers between devices with their start and end apart: 21 -> 19, of which waited for: 12 -> 13; matrix products, arithmetic and copies ran while one was open for 4% -> 3% of each run, Pallas kernels for 15% -> 7%
where the time goes in v3:
time: 189 us; the launch traced here: 188 us
  Pallas kernels  74.8 us (40%)
  starting transfers between devices  37.6 us (20%)
  local copies, waits for them, and re-layouts  36.2 us (19%)
  waiting for transfers between devices  26.3 us (14%)
  other arithmetic  11.8 us (6%)
    pallas_call x1, Pallas kernels, local(): pl.pallas_call(final_kernel, grid=(width // each,), in_specs=[by_w(3, row...  38.4 us
    unnamed x60, local copies, waits for them, and re-layouts  32.2 us
    pallas_call x1, Pallas kernels, local(): pl.pallas_call(states_kernel, grid=(width // each,), in_specs=[by_w(3, ro...  23 us
    ppermute x6, starting transfers between devices, shifted(): lax.ppermute(value, axis, [(source, source + steps) for source in range(f...  16.2 us
    ppermute x9, starting transfers between devices, rotated(): lax.ppermute(value, axis, [(s, (s + steps) % count) for s in range(count)])  13.9 us
    pallas_call x1, Pallas kernels, blocks(): pl.pallas_call(blocks_kernel, grid=(width // each,), in_specs=[by_w(2, he...  13.4 us
    ppermute x9, waiting for transfers between devices, rotated(): lax.ppermute(value, axis, [(s, (s + steps) % count) for s in range(count)])  12.6 us
    ppermute x4, starting transfers between devices, swapped(): return lax.ppermute(value, 'ctx', [(s, s ^ 1) for s in range(count)])  7.47 us
  transfers between devices with their start and end apart: 19, of which 13 were waited for; matrix products, arithmetic and copies ran while one was open for 3% of the time, Pallas kernels for 7%

profile of v3, /device:TPU:0, one launch (start us, length us, event | category | flops | bytes accessed | tf_op | source)
XLA Modules:
  0.0 187.9 jit_solution(15251892427581349239)
XLA Ops:
  0.7 1.3 fusion.15
  2.0 2.4 %collective-permute-start = (bf16[3,8,8192]{2,1,0:T(8,128)(2,1)S(1)}, bf16[3,8,8192]{2,1,0:T(8,128)(2,1)S(1)}, u32[]{:S(2)}, u32[]{:S(2)}) collective-permute-start(bf16[3,8,8192]{2,1,0:T(8,128)(2,1)S(1)} %get-tuple-element.41), channel_id=1, source_target_pairs={{0,1},{1,2},{2,3},{3,4},{4,5},{5,6},{6,7},{8,9},{9,10},{10,11},{11... | collective-permute-start | bytes 1179656 | tf_op jit(solution)/shard_map/ppermute | solution.py:214
  4.4 0.9 slice.76
  5.3 1.3 collective-permute-start.1
  6.6 0.8 negate_bitcast_fusion
  7.4 0.9 multiply_exponential_fusion
  8.3 0.8 fusion.14
  9.2 2.1 %collective-permute-done.1.ha = bf16[4,8,8192]{2,1,0:T(8,128)(2,1)S(1)} collective-permute-done((bf16[4,8,8192]{2,1,0:T(8,128)(2,1)S(1)}, bf16[4,8,8192]{2,1,0:T(8,128)(2,1)S(1)}, u32[]{:S(2)}, u32[]{:S(2)}) %collective-permute-start.1) | collective-permute-done | bytes 524320 | tf_op jit(solution)/shard_map/ppermute | solution.py:214
  11.3 2.8 %copy-done.4 = bf16[1,128,3,8192]{3,1,2,0:T(8,128)(2,1)S(1)} copy-done((bf16[1,128,3,8192]{3,1,2,0:T(8,128)(2,1)S(1)}, bf16[1,128,3,8192]{3,1,2,0:T(8,128)(2,1)}, u32[]{:S(2)}) %copy-start.4) | copy-done | bytes 6291480
  14.1 23.0 %states.1 = (f32[2,136,8192]{2,1,0:T(8,128)S(1)}, f32[16,8,8192]{2,1,0:T(8,128)S(1)}, f32[16,8,8192]{2,1,0:T(8,128)S(1)}, f32[2,16,16,512]{3,2,1,0:T(8,128)}) custom-call(bf16[3,128,8192]{2,1,0:T(8,128)(2,1)S(1)} %bitcast.99, bf16[3,8,8192]{2,1,0:T(8,128)(2,1)S(1)} %collective-permute-done.hb, bf16[4,8,8192]{2,1,0:T(8,128)(2,1)S(1)} %collective-permute-done.1.ha, ...), custom_call_target="tpu_custom_call" | custom-call | tf_op jit(solution)/shard_map/states/pallas_call | solution.py:353
  37.1 3.5 %copy-done = f32[2,136,8192]{2,1,0:T(8,128)} copy-done((f32[2,136,8192]{2,1,0:T(8,128)}, f32[2,136,8192]{2,1,0:T(8,128)S(1)}, u32[]{:S(2)}) %copy-start) | copy-done | bytes 8912920
  40.6 2.0 %copy-done.6 = f32[16,8,8192]{2,1,0:T(8,128)} copy-done((f32[16,8,8192]{2,1,0:T(8,128)}, f32[16,8,8192]{2,1,0:T(8,128)S(1)}, u32[]{:S(2)}) %copy-start.6) | copy-done | bytes 4194328
  42.6 2.1 %copy-done.10 = f32[16,8,8192]{2,1,0:T(8,128)} copy-done((f32[16,8,8192]{2,1,0:T(8,128)}, f32[16,8,8192]{2,1,0:T(8,128)S(1)}, u32[]{:S(2)}) %copy-start.10) | copy-done | bytes 4194328
  44.7 7.2 %collective-permute-start.2 = (f32[2,16,16,512]{3,2,1,0:T(8,128)}, f32[2,16,16,512]{3,2,1,0:T(8,128)}, u32[]{:S(2)}, u32[]{:S(2)}) collective-permute-start(f32[2,16,16,512]{3,2,1,0:T(8,128)} %get-tuple-element.20), channel_id=1, source_target_pairs={{0,1},{1,0},{2,3},{3,2},{4,5},{5,4},{6,7},{7,6},{8,9},{9,8},{10,11... | collective-permute-start | bytes 3145736 | tf_op jit(solution)/shard_map/ppermute | solution.py:224
  52.1 2.5 %collective-permute-done.2 = f32[2,16,16,512]{3,2,1,0:T(8,128)} collective-permute-done((f32[2,16,16,512]{3,2,1,0:T(8,128)}, f32[2,16,16,512]{3,2,1,0:T(8,128)}, u32[]{:S(2)}, u32[]{:S(2)}) %collective-permute-start.2) | collective-permute-done | bytes 1048608 | tf_op jit(solution)/shard_map/ppermute | solution.py:224
  54.5 1.3 dynamic-slice_select_fusion.1
  56.0 1.3 collective-permute-start.5
  57.3 4.6 %collective-permute-start.3 = (f32[8,16,512]{2,1,0:T(8,128)S(1)}, f32[8,16,512]{2,1,0:T(8,128)S(1)}, u32[]{:S(2)}, u32[]{:S(2)}) collective-permute-start(f32[8,16,512]{2,1,0:T(8,128)S(1)} %get-tuple-element.49), channel_id=1, source_target_pairs={{0,2},{1,3},{2,4},{3,5},{4,6},{5,7},{8,10},{9,11},{10,12},{11,13},... | collective-permute-start | bytes 786440 | tf_op jit(solution)/shard_map/ppermute | solution.py:214
  61.9 0.8 slice_multiply_fusion
  62.7 0.2 multiply_reduce_fusion.near
  62.9 3.6 %collective-permute-done.5 = f32[8,16,512]{2,1,0:T(8,128)S(1)} collective-permute-done((f32[8,16,512]{2,1,0:T(8,128)S(1)}, f32[8,16,512]{2,1,0:T(8,128)S(1)}, u32[]{:S(2)}, u32[]{:S(2)}) %collective-permute-start.5) | collective-permute-done | bytes 262176 | tf_op jit(solution)/shard_map/ppermute | solution.py:214
  66.5 1.2 collective-permute-done.3
  67.8 5.4 %collective-permute-start.4 = (f32[8,16,512]{2,1,0:T(8,128)S(1)}, f32[8,16,512]{2,1,0:T(8,128)S(1)}, u32[]{:S(2)}, u32[]{:S(2)}) collective-permute-start(f32[8,16,512]{2,1,0:T(8,128)S(1)} %get-tuple-element.64), channel_id=1, source_target_pairs={{0,4},{1,5},{2,6},{3,7},{8,12},{9,13},{10,14},{11,15},{16,20},{17,... | collective-permute-start | bytes 786440 | tf_op jit(solution)/shard_map/ppermute | solution.py:214
  73.2 1.3 collective-permute-start.6
  74.5 0.3 broadcast_select_fusion
  74.9 3.5 %copy-done.1 = f32[2,136,8192]{2,1,0:T(8,128)S(1)} copy-done((f32[2,136,8192]{2,1,0:T(8,128)S(1)}, f32[2,136,8192]{2,1,0:T(8,128)}, u32[]{:S(2)}) %copy-start.1) | copy-done | bytes 8912920
  78.4 13.4 %blocks.1 = (f32[2,136,8192]{2,1,0:T(8,128)S(1)}, f32[16,8,8192]{2,1,0:T(8,128)S(1)}, f32[16,8,8192]{2,1,0:T(8,128)S(1)}) custom-call(f32[2,136,8192]{2,1,0:T(8,128)S(1)} %copy-done.1, f32[16,8,8192]{2,1,0:T(8,128)S(1)} %copy-done.7, f32[16,8,8192]{2,1,0:T(8,128)S(1)} %copy-done.11, ...), custom_call_target="tpu_custom_call", output_to_operand_aliasing={{0}: (0, {}), {1}: (1, {}), {2}: (2, {})} | custom-call | flops 62914560 | bytes 36700160 | tf_op jit(solution)/shard_map/blocks/pallas_call | solution.py:375
  91.8 3.5 %copy-done.2 = f32[2,136,8192]{2,1,0:T(8,128)} copy-done((f32[2,136,8192]{2,1,0:T(8,128)}, f32[2,136,8192]{2,1,0:T(8,128)S(1)}, u32[]{:S(2)}) %copy-start.2) | copy-done | bytes 8912920
  95.3 2.0 %copy-done.8 = f32[16,8,8192]{2,1,0:T(8,128)} copy-done((f32[16,8,8192]{2,1,0:T(8,128)}, f32[16,8,8192]{2,1,0:T(8,128)S(1)}, u32[]{:S(2)}) %copy-start.8) | copy-done | bytes 4194328
  97.3 2.1 %copy-done.12 = f32[16,8,8192]{2,1,0:T(8,128)} copy-done((f32[16,8,8192]{2,1,0:T(8,128)}, f32[16,8,8192]{2,1,0:T(8,128)S(1)}, u32[]{:S(2)}) %copy-start.12) | copy-done | bytes 4194328
  99.5 0.7 copy-done.21
  100.2 0.8 pad_maximum_fusion.2
  101.1 1.2 fusion.7
  102.3 1.0 collective-permute-done.7
  103.3 1.3 broadcast_select_fusion.3
  104.6 1.5 fusion.4
  106.1 3.5 %copy-done.3 = f32[2,136,8192]{2,1,0:T(8,128)S(1)} copy-done((f32[2,136,8192]{2,1,0:T(8,128)S(1)}, f32[2,136,8192]{2,1,0:T(8,128)}, u32[]{:S(2)}) %copy-start.3) | copy-done | bytes 8912920
  109.6 2.8 %copy-done.5 = bf16[1,128,3,8192]{3,1,2,0:T(8,128)(2,1)S(1)} copy-done((bf16[1,128,3,8192]{3,1,2,0:T(8,128)(2,1)S(1)}, bf16[1,128,3,8192]{3,1,2,0:T(8,128)(2,1)}, u32[]{:S(2)}) %copy-start.5) | copy-done | bytes 6291480
  112.4 2.2 %copy-done.13 = f32[16,8,8192]{2,1,0:T(8,128)S(1)} copy-done((f32[16,8,8192]{2,1,0:T(8,128)S(1)}, f32[16,8,8192]{2,1,0:T(8,128)}, u32[]{:S(2)}) %copy-start.13) | copy-done | bytes 4194328
  114.6 38.4 %final.1 = (bf16[128,8192]{1,0:T(8,128)(2,1)}, bf16[3,128,8192]{2,1,0:T(8,128)(2,1)}, f32[16,24,512]{2,1,0:T(8,128)S(1)}) custom-call(bf16[3,128,8192]{2,1,0:T(8,128)(2,1)S(1)} %bitcast.100, bf16[3,8,8192]{2,1,0:T(8,128)(2,1)S(1)} %copy-done.17, bf16[128,8192]{1,0:T(8,128)(2,1)S(1)} %bitcast.102, bf16[4,8,8192]{2,1,0:T(8,128)(2,1)S(1)} %collective-permute-done.1.ha, ...), custom_call_target="tpu_custom_call" | custom-call | tf_op jit(solution)/shard_map/final/pallas_call | solution.py:404
  153.0 0.9 copy-done.18
  153.9 0.2 collective-permute-start.8
  154.1 1.6 collective-permute-done.8
  155.7 1.1 dynamic-slice_add_fusion
  156.8 2.5 %collective-permute-start.11 = (f32[2,24,512]{2,1,0:T(8,128)S(1)}, f32[2,24,512]{2,1,0:T(8,128)S(1)}, u32[]{:S(2)}, u32[]{:S(2)}) collective-permute-start(f32[2,24,512]{2,1,0:T(8,128)S(1)} %get-tuple-element.57), channel_id=1, source_target_pairs={{0,24},{8,0},{16,8},{24,16},{1,25},{9,1},{17,9},{25,17},{2,26},{10... | collective-permute-start | bytes 294920 | tf_op jit(solution)/shard_map/ppermute | solution.py:219
  159.3 0.5 collective-permute-start.10
  159.8 0.6 collective-permute-start.9
  160.4 2.1 %collective-permute-done.11 = f32[2,24,512]{2,1,0:T(8,128)S(1)} collective-permute-done((f32[2,24,512]{2,1,0:T(8,128)S(1)}, f32[2,24,512]{2,1,0:T(8,128)S(1)}, u32[]{:S(2)}, u32[]{:S(2)}) %collective-permute-start.11) | collective-permute-done | bytes 98336 | tf_op jit(solution)/shard_map/ppermute | solution.py:219
  162.5 3.5 %collective-permute-done.10 = f32[2,24,512]{2,1,0:T(8,128)S(1)} collective-permute-done((f32[2,24,512]{2,1,0:T(8,128)S(1)}, f32[2,24,512]{2,1,0:T(8,128)S(1)}, u32[]{:S(2)}, u32[]{:S(2)}) %collective-permute-start.10) | collective-permute-done | bytes 98336 | tf_op jit(solution)/shard_map/ppermute | solution.py:219
  166.1 1.6 collective-permute-start.12
  167.7 3.6 %collective-permute-start.13 = (f32[2,24,512]{2,1,0:T(8,128)S(1)}, f32[2,24,512]{2,1,0:T(8,128)S(1)}, u32[]{:S(2)}, u32[]{:S(2)}) collective-permute-start(f32[2,24,512]{2,1,0:T(8,128)S(1)} %get-tuple-element.39), channel_id=1, source_target_pairs={{0,4},{1,5},{2,6},{3,7},{4,0},{5,1},{6,2},{7,3},{8,12},{9,13},{10,... | collective-permute-start | bytes 294920 | tf_op jit(solution)/shard_map/ppermute | solution.py:219
  171.3 1.3 collective-permute-start.14
  172.6 1.3 collective-permute-done.12
  174.0 2.8 %collective-permute-done.13 = f32[2,24,512]{2,1,0:T(8,128)S(1)} collective-permute-done((f32[2,24,512]{2,1,0:T(8,128)S(1)}, f32[2,24,512]{2,1,0:T(8,128)S(1)}, u32[]{:S(2)}, u32[]{:S(2)}) %collective-permute-start.13) | collective-permute-done | bytes 98336 | tf_op jit(solution)/shard_map/ppermute | solution.py:219
  176.9 1.0 collective-permute-start.15
  177.9 0.7 collective-permute-start.16
  178.6 2.1 %collective-permute-start.17 = (f32[2,24,512]{2,1,0:T(8,128)S(1)}, f32[2,24,512]{2,1,0:T(8,128)S(1)}, u32[]{:S(2)}, u32[]{:S(2)}) collective-permute-start(f32[2,24,512]{2,1,0:T(8,128)S(1)} %bitcast.110), channel_id=1, source_target_pairs={{0,24},{8,0},{16,8},{24,16},{1,25},{9,1},{17,9},{25,17},{2,26},{10... | collective-permute-start | bytes 294920 | tf_op jit(solution)/shard_map/ppermute | solution.py:219
  180.7 2.4 %collective-permute-done.15 = f32[2,24,512]{2,1,0:T(8,128)S(1)} collective-permute-done((f32[2,24,512]{2,1,0:T(8,128)S(1)}, f32[2,24,512]{2,1,0:T(8,128)S(1)}, u32[]{:S(2)}, u32[]{:S(2)}) %collective-permute-start.15) | collective-permute-done | bytes 98336 | tf_op jit(solution)/shard_map/ppermute | solution.py:219
  183.1 0.4 collective-permute-done.16
  183.6 0.2 copy.22
  183.9 1.7 collective-permute-done.18
  185.6 0.3 broadcast_select_fusion.5
  186.0 1.2 reshape.35
  187.3 0.6 copy.24
  (76 shorter events, 1.1 us)
Async XLA Ops:
  0.6 10.7 %copy-start.14 = (bf16[1,128,8192]{2,1,0:T(8,128)(2,1)S(1)}, bf16[1,128,8192]{2,1,0:T(8,128)(2,1)}, u32[]{:S(2)}) copy-start(bf16[1,128,8192]{2,1,0:T(8,128)(2,1)} %param.16) | copy-start | bytes 6291460
  0.6 10.7 %copy-start.15 = (f32[3,7,8192]{2,1,0:T(8,128)S(1)}, f32[3,7,8192]{2,1,0:T(8,128)}, u32[]{:S(2)}) copy-start(f32[3,7,8192]{2,1,0:T(8,128)} %filt.3) | copy-start | bytes 2064388
  2.0 7.2 %collective-permute-start = (bf16[3,8,8192]{2,1,0:T(8,128)(2,1)S(1)}, bf16[3,8,8192]{2,1,0:T(8,128)(2,1)S(1)}, u32[]{:S(2)}, u32[]{:S(2)}) collective-permute-start(bf16[3,8,8192]{2,1,0:T(8,128)(2,1)S(1)} %get-tuple-element.41), channel_id=1, source_target_pairs={{0,1},{1,2},{2,3},{3,4},{4,5},{5,6},{6,7},{8,9},{9,10},{10,11},{11... | collective-permute-start | bytes 1179656 | tf_op jit(solution)/shard_map/ppermute | solution.py:214
  5.3 6.0 %collective-permute-start.1 = (bf16[4,8,8192]{2,1,0:T(8,128)(2,1)S(1)}, bf16[4,8,8192]{2,1,0:T(8,128)(2,1)S(1)}, u32[]{:S(2)}, u32[]{:S(2)}) collective-permute-start(bf16[4,8,8192]{2,1,0:T(8,128)(2,1)S(1)} %pad_maximum_fusion.1), channel_id=1, source_target_pairs={{1,0},{2,1},{3,2},{4,3},{5,4},{6,5},{7,6},{9,8},{10,9},{11,10},{12... | collective-permute-start | bytes 1572872 | tf_op jit(solution)/shard_map/ppermute | solution.py:214
  8.3 3.0 %copy-start.20 = (f32[4,16,8,512]{3,2,1,0:T(8,128)}, f32[4,16,8,512]{3,2,1,0:T(8,128)S(1)}, u32[]{:S(2)}) copy-start(f32[4,16,8,512]{3,2,1,0:T(8,128)S(1)} %multiply_exponential_fusion) | copy-start | bytes 3145732
  9.2 28.0 %copy-start.16 = (bf16[3,8,8192]{2,1,0:T(8,128)(2,1)}, bf16[3,8,8192]{2,1,0:T(8,128)(2,1)S(1)}, u32[]{:S(2)}) copy-start(bf16[3,8,8192]{2,1,0:T(8,128)(2,1)S(1)} %collective-permute-done.hb) | copy-start | bytes 1179652
  11.3 2.8 %copy-start.4 = (bf16[1,128,3,8192]{3,1,2,0:T(8,128)(2,1)S(1)}, bf16[1,128,3,8192]{3,1,2,0:T(8,128)(2,1)}, u32[]{:S(2)}) copy-start(bf16[1,128,3,8192]{3,1,2,0:T(8,128)(2,1)} %param.11) | copy-start | bytes 18874372
  14.1 37.8 %copy-start.25 = (f32[4]{0:T(128)S(1)}, f32[4]{0:T(128)}, u32[]{:S(2)}) copy-start(f32[4]{0:T(128)} %constant.90) | copy-start | bytes 52
  37.1 3.5 %copy-start = (f32[2,136,8192]{2,1,0:T(8,128)}, f32[2,136,8192]{2,1,0:T(8,128)S(1)}, u32[]{:S(2)}) copy-start(f32[2,136,8192]{2,1,0:T(8,128)S(1)} %get-tuple-element.21.xg) | copy-start | bytes 26738692
  40.6 2.0 %copy-start.6 = (f32[16,8,8192]{2,1,0:T(8,128)}, f32[16,8,8192]{2,1,0:T(8,128)S(1)}, u32[]{:S(2)}) copy-start(f32[16,8,8192]{2,1,0:T(8,128)S(1)} %get-tuple-element.22.blocks_e) | copy-start | bytes 12582916
  42.6 2.1 %copy-start.10 = (f32[16,8,8192]{2,1,0:T(8,128)}, f32[16,8,8192]{2,1,0:T(8,128)S(1)}, u32[]{:S(2)}) copy-start(f32[16,8,8192]{2,1,0:T(8,128)S(1)} %get-tuple-element.23.blocks_a) | copy-start | bytes 12582916
  44.7 18.0 %copy-start.28 = (f32[24]{0:T(128)S(1)}, f32[24]{0:T(128)}, u32[]{:S(2)}) copy-start(f32[24]{0:T(128)} %constant.88) | copy-start | bytes 292
  44.7 29.8 %copy-start.26 = (pred[4,8]{1,0:T(4,128)(4,1)S(1)}, pred[4,8]{1,0:T(4,128)(4,1)}, u32[]{:S(2)}) copy-start(pred[4,8]{1,0:T(4,128)(4,1)} %constant.91) | copy-start | bytes 100
  44.7 29.8 %copy-start.27 = (pred[4,8]{1,0:T(4,128)(4,1)S(1)}, pred[4,8]{1,0:T(4,128)(4,1)}, u32[]{:S(2)}) copy-start(pred[4,8]{1,0:T(4,128)(4,1)} %constant.89) | copy-start | bytes 100
  44.7 9.8 %collective-permute-start.2 = (f32[2,16,16,512]{3,2,1,0:T(8,128)}, f32[2,16,16,512]{3,2,1,0:T(8,128)}, u32[]{:S(2)}, u32[]{:S(2)}) collective-permute-start(f32[2,16,16,512]{3,2,1,0:T(8,128)} %get-tuple-element.20), channel_id=1, source_target_pairs={{0,1},{1,0},{2,3},{3,2},{4,5},{5,4},{6,7},{7,6},{8,9},{9,8},{10,11... | collective-permute-start | bytes 3145736 | tf_op jit(solution)/shard_map/ppermute | solution.py:224
  51.9 10.8 %copy-start.23 = (f32[512,16]{0,1:T(8,128)S(1)}, f32[512,16]{0,1:T(8,128)}, u32[]{:S(2)}) copy-start(f32[512,16]{0,1:T(8,128)} %param.13) | copy-start | bytes 98308
  52.0 22.8 %copy-start.7 = (f32[16,8,8192]{2,1,0:T(8,128)S(1)}, f32[16,8,8192]{2,1,0:T(8,128)}, u32[]{:S(2)}) copy-start(f32[16,8,8192]{2,1,0:T(8,128)} %copy-done.6) | copy-start | bytes 12582916
  52.0 22.8 %copy-start.11 = (f32[16,8,8192]{2,1,0:T(8,128)S(1)}, f32[16,8,8192]{2,1,0:T(8,128)}, u32[]{:S(2)}) copy-start(f32[16,8,8192]{2,1,0:T(8,128)} %copy-done.10) | copy-start | bytes 12582916
  52.0 22.8 %copy-start.19 = (f32[8192]{0:T(1024)S(1)}, f32[8192]{0:T(1024)}, u32[]{:S(2)}) copy-start(f32[8192]{0:T(1024)} %param.15) | copy-start | bytes 98308
  56.0 10.5 %collective-permute-start.5 = (f32[8,16,512]{2,1,0:T(8,128)S(1)}, f32[8,16,512]{2,1,0:T(8,128)S(1)}, u32[]{:S(2)}, u32[]{:S(2)}) collective-permute-start(f32[8,16,512]{2,1,0:T(8,128)S(1)} %get-tuple-element.48), channel_id=1, source_target_pairs={{2,0},{3,1},{4,2},{5,3},{6,4},{7,5},{10,8},{11,9},{12,10},{13,11},... | collective-permute-start | bytes 786440 | tf_op jit(solution)/shard_map/ppermute | solution.py:214
  57.3 10.4 %collective-permute-start.3 = (f32[8,16,512]{2,1,0:T(8,128)S(1)}, f32[8,16,512]{2,1,0:T(8,128)S(1)}, u32[]{:S(2)}, u32[]{:S(2)}) collective-permute-start(f32[8,16,512]{2,1,0:T(8,128)S(1)} %get-tuple-element.49), channel_id=1, source_target_pairs={{0,2},{1,3},{2,4},{3,5},{4,6},{5,7},{8,10},{9,11},{10,12},{11,13},... | collective-permute-start | bytes 786440 | tf_op jit(solution)/shard_map/ppermute | solution.py:214
  67.8 31.6 %collective-permute-start.4 = (f32[8,16,512]{2,1,0:T(8,128)S(1)}, f32[8,16,512]{2,1,0:T(8,128)S(1)}, u32[]{:S(2)}, u32[]{:S(2)}) collective-permute-start(f32[8,16,512]{2,1,0:T(8,128)S(1)} %get-tuple-element.64), channel_id=1, source_target_pairs={{0,4},{1,5},{2,6},{3,7},{8,12},{9,13},{10,14},{11,15},{16,20},{17,... | collective-permute-start | bytes 786440 | tf_op jit(solution)/shard_map/ppermute | solution.py:214
  73.2 26.2 %collective-permute-start.6 = (f32[8,16,512]{2,1,0:T(8,128)S(1)}, f32[8,16,512]{2,1,0:T(8,128)S(1)}, u32[]{:S(2)}, u32[]{:S(2)}) collective-permute-start(f32[8,16,512]{2,1,0:T(8,128)S(1)} %get-tuple-element.63), channel_id=1, source_target_pairs={{4,0},{5,1},{6,2},{7,3},{12,8},{13,9},{14,10},{15,11},{20,16},{21,... | collective-permute-start | bytes 786440 | tf_op jit(solution)/shard_map/ppermute | solution.py:214
  74.9 3.5 %copy-start.1 = (f32[2,136,8192]{2,1,0:T(8,128)S(1)}, f32[2,136,8192]{2,1,0:T(8,128)}, u32[]{:S(2)}) copy-start(f32[2,136,8192]{2,1,0:T(8,128)} %copy-done) | copy-start | bytes 26738692
  78.4 22.7 %copy-start.24 = (f32[512,16]{0,1:T(8,128)S(1)}, f32[512,16]{0,1:T(8,128)}, u32[]{:S(2)}) copy-start(f32[512,16]{0,1:T(8,128)} %param.13) | copy-start | bytes 98308
  91.8 3.5 %copy-start.2 = (f32[2,136,8192]{2,1,0:T(8,128)}, f32[2,136,8192]{2,1,0:T(8,128)S(1)}, u32[]{:S(2)}) copy-start(f32[2,136,8192]{2,1,0:T(8,128)S(1)} %get-tuple-element.28.conv) | copy-start | bytes 26738692
  95.3 2.0 %copy-start.8 = (f32[16,8,8192]{2,1,0:T(8,128)}, f32[16,8,8192]{2,1,0:T(8,128)S(1)}, u32[]{:S(2)}) copy-start(f32[16,8,8192]{2,1,0:T(8,128)S(1)} %get-tuple-element.29.from_e) | copy-start | bytes 12582916
  97.3 2.1 %copy-start.12 = (f32[16,8,8192]{2,1,0:T(8,128)}, f32[16,8,8192]{2,1,0:T(8,128)S(1)}, u32[]{:S(2)}) copy-start(f32[16,8,8192]{2,1,0:T(8,128)S(1)} %get-tuple-element.30.from_a) | copy-start | bytes 12582916
  99.5 0.7 copy-start.21
  99.5 1.5 copy-start.22
  101.1 2.3 %collective-permute-start.7 = (f32[2,8,16,512]{3,2,1,0:T(8,128)}, f32[2,8,16,512]{3,2,1,0:T(8,128)}, u32[]{:S(2)}, u32[]{:S(2)}) collective-permute-start(f32[2,8,16,512]{3,2,1,0:T(8,128)} %pad_maximum_fusion.2), channel_id=1, source_target_pairs={{0,1},{1,0},{2,3},{3,2},{4,5},{5,4},{6,7},{7,6},{8,9},{9,8},{10,11... | collective-permute-start | bytes 1572872 | tf_op jit(solution)/shard_map/ppermute | solution.py:224
  101.1 5.0 %copy-start.9 = (f32[16,8,8192]{2,1,0:T(8,128)S(1)}, f32[16,8,8192]{2,1,0:T(8,128)}, u32[]{:S(2)}) copy-start(f32[16,8,8192]{2,1,0:T(8,128)} %copy-done.8) | copy-start | bytes 12582916
  101.1 5.0 %copy-start.17 = (bf16[3,8,8192]{2,1,0:T(8,128)(2,1)S(1)}, bf16[3,8,8192]{2,1,0:T(8,128)(2,1)}, u32[]{:S(2)}) copy-start(bf16[3,8,8192]{2,1,0:T(8,128)(2,1)} %copy-done.16) | copy-start | bytes 1179652
  106.1 3.5 %copy-start.3 = (f32[2,136,8192]{2,1,0:T(8,128)S(1)}, f32[2,136,8192]{2,1,0:T(8,128)}, u32[]{:S(2)}) copy-start(f32[2,136,8192]{2,1,0:T(8,128)} %copy-done.2) | copy-start | bytes 26738692
  109.6 2.8 %copy-start.5 = (bf16[1,128,3,8192]{3,1,2,0:T(8,128)(2,1)S(1)}, bf16[1,128,3,8192]{3,1,2,0:T(8,128)(2,1)}, u32[]{:S(2)}) copy-start(bf16[1,128,3,8192]{3,1,2,0:T(8,128)(2,1)} %param.11) | copy-start | bytes 18874372
  112.4 2.2 %copy-start.13 = (f32[16,8,8192]{2,1,0:T(8,128)S(1)}, f32[16,8,8192]{2,1,0:T(8,128)}, u32[]{:S(2)}) copy-start(f32[16,8,8192]{2,1,0:T(8,128)} %copy-done.12) | copy-start | bytes 12582916
  153.0 0.9 copy-start.18
  153.9 1.8 collective-permute-start.8
  156.8 5.7 %collective-permute-start.11 = (f32[2,24,512]{2,1,0:T(8,128)S(1)}, f32[2,24,512]{2,1,0:T(8,128)S(1)}, u32[]{:S(2)}, u32[]{:S(2)}) collective-permute-start(f32[2,24,512]{2,1,0:T(8,128)S(1)} %get-tuple-element.57), channel_id=1, source_target_pairs={{0,24},{8,0},{16,8},{24,16},{1,25},{9,1},{17,9},{25,17},{2,26},{10... | collective-permute-start | bytes 294920 | tf_op jit(solution)/shard_map/ppermute | solution.py:219
  159.3 6.7 %collective-permute-start.10 = (f32[2,24,512]{2,1,0:T(8,128)S(1)}, f32[2,24,512]{2,1,0:T(8,128)S(1)}, u32[]{:S(2)}, u32[]{:S(2)}) collective-permute-start(f32[2,24,512]{2,1,0:T(8,128)S(1)} %get-tuple-element.58), channel_id=1, source_target_pairs={{0,16},{8,24},{16,0},{24,8},{1,17},{9,25},{17,1},{25,9},{2,18},{10... | collective-permute-start | bytes 294920 | tf_op jit(solution)/shard_map/ppermute | solution.py:219
  159.8 6.2 %collective-permute-start.9 = (f32[2,24,512]{2,1,0:T(8,128)S(1)}, f32[2,24,512]{2,1,0:T(8,128)S(1)}, u32[]{:S(2)}, u32[]{:S(2)}) collective-permute-start(f32[2,24,512]{2,1,0:T(8,128)S(1)} %get-tuple-element.56), channel_id=1, source_target_pairs={{0,8},{8,16},{16,24},{24,0},{1,9},{9,17},{17,25},{25,1},{2,10},{10... | collective-permute-start | bytes 294920 | tf_op jit(solution)/shard_map/ppermute | solution.py:219
  166.1 7.9 %collective-permute-start.12 = (f32[2,24,512]{2,1,0:T(8,128)S(1)}, f32[2,24,512]{2,1,0:T(8,128)S(1)}, u32[]{:S(2)}, u32[]{:S(2)}) collective-permute-start(f32[2,24,512]{2,1,0:T(8,128)S(1)} %get-tuple-element.39), channel_id=1, source_target_pairs={{0,2},{1,3},{2,4},{3,5},{4,6},{5,7},{6,0},{7,1},{8,10},{9,11},{10,... | collective-permute-start | bytes 294920 | tf_op jit(solution)/shard_map/ppermute | solution.py:219
  167.7 9.1 %collective-permute-start.13 = (f32[2,24,512]{2,1,0:T(8,128)S(1)}, f32[2,24,512]{2,1,0:T(8,128)S(1)}, u32[]{:S(2)}, u32[]{:S(2)}) collective-permute-start(f32[2,24,512]{2,1,0:T(8,128)S(1)} %get-tuple-element.39), channel_id=1, source_target_pairs={{0,4},{1,5},{2,6},{3,7},{4,0},{5,1},{6,2},{7,3},{8,12},{9,13},{10,... | collective-permute-start | bytes 294920 | tf_op jit(solution)/shard_map/ppermute | solution.py:219
  171.3 5.6 %collective-permute-start.14 = (f32[2,24,512]{2,1,0:T(8,128)S(1)}, f32[2,24,512]{2,1,0:T(8,128)S(1)}, u32[]{:S(2)}, u32[]{:S(2)}) collective-permute-start(f32[2,24,512]{2,1,0:T(8,128)S(1)} %get-tuple-element.39), channel_id=1, source_target_pairs={{0,6},{1,7},{2,0},{3,1},{4,2},{5,3},{6,4},{7,5},{8,14},{9,15},{10,... | collective-permute-start | bytes 294920 | tf_op jit(solution)/shard_map/ppermute | solution.py:219
  176.9 6.2 %collective-permute-start.15 = (f32[2,24,512]{2,1,0:T(8,128)S(1)}, f32[2,24,512]{2,1,0:T(8,128)S(1)}, u32[]{:S(2)}, u32[]{:S(2)}) collective-permute-start(f32[2,24,512]{2,1,0:T(8,128)S(1)} %bitcast.108), channel_id=1, source_target_pairs={{0,8},{8,16},{16,24},{24,0},{1,9},{9,17},{17,25},{25,1},{2,10},{10... | collective-permute-start | bytes 294920 | tf_op jit(solution)/shard_map/ppermute | solution.py:219
  177.9 5.6 %collective-permute-start.16 = (f32[2,24,512]{2,1,0:T(8,128)S(1)}, f32[2,24,512]{2,1,0:T(8,128)S(1)}, u32[]{:S(2)}, u32[]{:S(2)}) collective-permute-start(f32[2,24,512]{2,1,0:T(8,128)S(1)} %bitcast.109), channel_id=1, source_target_pairs={{0,16},{8,24},{16,0},{24,8},{1,17},{9,25},{17,1},{25,9},{2,18},{10... | collective-permute-start | bytes 294920 | tf_op jit(solution)/shard_map/ppermute | solution.py:219
  178.6 5.0 %collective-permute-start.17 = (f32[2,24,512]{2,1,0:T(8,128)S(1)}, f32[2,24,512]{2,1,0:T(8,128)S(1)}, u32[]{:S(2)}, u32[]{:S(2)}) collective-permute-start(f32[2,24,512]{2,1,0:T(8,128)S(1)} %bitcast.110), channel_id=1, source_target_pairs={{0,24},{8,0},{16,8},{24,16},{1,25},{9,1},{17,9},{25,17},{2,26},{10... | collective-permute-start | bytes 294920 | tf_op jit(solution)/shard_map/ppermute | solution.py:219
  183.8 1.8 collective-permute-start.18

commit v4 on v3

--- a/solution.py
+++ b/solution.py
@@ -25,7 +25,28 @@
     return terms[0]
 
 
-def states_kernel(p, hb, ha, u, filt, f1, we, wb, xg, blocks_e, blocks_a, ends, xs):
+def folded(values):
+    row = lax.broadcasted_iota(jnp.int32, (SUB, LANES), 0)
+    upper = row < 4
+    values = [
+        jnp.where(upper, values[n], values[n + 4])
+        + pltpu.roll(jnp.where(upper, values[n + 4], values[n]), 4, 0)
+        for n in range(4)
+    ]
+    for step in (2, 1):
+        even = (row // step) % 2 == 0
+        values = [
+            jnp.where(
+                even,
+                values[n] + pltpu.roll(values[n], SUB - step, 0),
+                values[n + step] + pltpu.roll(values[n + step], step, 0),
+            )
+            for n in range(step)
+        ]
+    return values[0]
+
+
+def states_kernel(p, hb, ha, u, filt, f1, we, wb, qkv, xg, blocks_e, blocks_a, ends, xs):
     rows = p.shape[1]
     run = (rows + SUB) // SUB
     taps = filt.shape[1]
@@ -53,28 +74,29 @@
             ]
 
         decay = [spread(f1[n : n + 1, part]) for n in range(poles)]
-        key, value = mixed(1), mixed(2)
-        state = None
-        for a in range(run):
-            x = key[a] * value[a]
-            xg[0, SUB * a : SUB * a + SUB, lanes] = x
-            if a >= own:
-                x = jnp.where(inside, x, 0.0)
-            state = [x] * poles if a == 0 else [decay[n] * state[n] + x for n in range(poles)]
-        for n in range(poles):
-            blocks_e[n, :, lanes] = state[n]
-            ends[0, which, n : n + 1, part] = jnp.sum(state[n] * we[n, :, part], axis=0, keepdims=True)
-        query = mixed(0)
-        state = None
-        for a in range(run - 1, -1, -1):
-            x = xs[3, pl.ds(SUB + a, SUB, stride=run), :] * query[a]
-            xg[1, SUB * a : SUB * a + SUB, lanes] = x
-            if a >= own:
-                x = jnp.where(inside, x, 0.0)
-            state = [x] * poles if a == run - 1 else [decay[n] * state[n] + x for n in range(poles)]
-        for n in range(poles):
-            blocks_a[n, :, lanes] = state[n]
-            ends[1, which, n : n + 1, part] = jnp.sum(state[n] * wb[n, :, part], axis=0, keepdims=True)
+        for j in (1, 2, 0):
+            for a, total in enumerate(mixed(j)):
+                at = slice(SUB * a, SUB * a + SUB)
+                qkv[j, at, lanes] = total
+                if j == 2:
+                    xg[0, at, lanes] = qkv[1, at, lanes] * total
+                if j == 0:
+                    xg[1, at, lanes] = xs[3, pl.ds(SUB + a, SUB, stride=run), :] * total
+        for side, order, weight, blocks in (
+            (0, range(run), we, blocks_e),
+            (1, range(run - 1, -1, -1), wb, blocks_a),
+        ):
+            state = None
+            for a in order:
+                x = xg[side, SUB * a : SUB * a + SUB, lanes]
+                if a >= own:
+                    x = jnp.where(inside, x, 0.0)
+                state = [x] * poles if state is None else [decay[n] * state[n] + x for n in range(poles)]
+            for n in range(poles):
+                blocks[n, :, lanes] = state[n]
+            state = [state[n] * weight[n, :, part] for n in range(poles)]
+            for n in range(0, poles, SUB):
+                ends[side, which, n : n + SUB, part] = folded(state[n : n + SUB])
         return carry
 
     lax.fori_loop(0, p.shape[2] // LANES, tile, 0)
@@ -124,8 +146,8 @@
 
 
 def final_kernel(
-    p, hb, u, ha, conv, from_e, from_a, enter, arrive, filt, f1, cz, cy,
-    output, grad_p, sums, ps, us, qs, gs, os,
+    p, hb, u, ha, qkv, conv, from_e, from_a, enter, arrive, filt, f1, cz, cy,
+    output, grad_p, sums, ps, us, gs, os,
 ):
     rows = p.shape[1]
     run = (rows + SUB) // SUB
@@ -145,13 +167,6 @@
             ps[j, SUB + rows :] = ha[j, :, lanes].astype(F32)
         us[0:rows] = u[:, lanes].astype(F32)
         us[rows:] = ha[3, :, lanes].astype(F32)
-        for j in range(3):
-            tap = [spread(filt[j, i : i + 1, lanes]) for i in range(taps)]
-            view = [ps[j, pl.ds(SUB + a, SUB, stride=run), :] for a in range(1 - taps, run)]
-            for a in range(run):
-                qs[j, SUB * a : SUB * a + SUB] = added(
-                    [tap[i] * view[a + taps - 1 - i] for i in range(taps)]
-                )
         decay = [spread(f1[n : n + 1, part]) for n in range(poles)]
 
         state = [
@@ -161,8 +176,8 @@
         skip_sum = None
         for a in range(run):
             at = slice(SUB * a, SUB * a + SUB)
-            query, upstream = qs[0, at], us[pl.ds(a, SUB, stride=run), :]
-            term = (qs[1, at] * qs[2, at]) * (query * upstream)
+            query, upstream = qkv[0, at, lanes], us[pl.ds(a, SUB, stride=run), :]
+            term = (qkv[1, at, lanes] * qkv[2, at, lanes]) * (query * upstream)
             if a >= own:
                 term = jnp.where(inside, term, 0.0)
             skip_sum = term if a == 0 else skip_sum + term
@@ -180,11 +195,12 @@
         for a in range(run - 1, -1, -1):
             at = slice(SUB * a, SUB * a + SUB)
             grad = conv[1, at, lanes] + added(list(state))
-            gs[1, pl.ds(a, SUB, stride=run), :] = grad * qs[2, at]
-            gs[2, pl.ds(a, SUB, stride=run), :] = grad * qs[1, at]
+            gs[1, pl.ds(a, SUB, stride=run), :] = grad * qkv[2, at, lanes]
+            gs[2, pl.ds(a, SUB, stride=run), :] = grad * qkv[1, at, lanes]
             if a:
                 state = [state[n] * decay[n] for n in range(poles)]
 
+        rest = []
         for j in range(3):
             tap = [spread(filt[j, i : i + 1, lanes]) for i in range(taps)]
             grads = [gs[j, pl.ds(a, SUB, stride=run), :] for a in range(run + taps - 1)]
@@ -198,11 +214,10 @@
                     term = grad * views[a + taps - 1 - i]
                     sums_of[i] = term if a == 0 else sums_of[i] + term
             grad_p[j, :, lanes] = os[0:rows].astype(BF16)
-            for i in range(taps):
-                at = j * taps + i
-                sums[which, at : at + 1, part] = jnp.sum(sums_of[i], axis=0, keepdims=True)
-        at = 3 * taps
-        sums[which, at : at + 1, part] = jnp.sum(skip_sum, axis=0, keepdims=True)
+            rest = rest + sums_of
+        rest = rest + [skip_sum] + [jnp.zeros((SUB, LANES), F32)] * (-(len(rest) + 1) % SUB)
+        for n in range(0, len(rest), SUB):
+            sums[which, n : n + SUB, part] = folded(rest[n : n + SUB])
         return carry
 
     lax.fori_loop(0, p.shape[2] // LANES, tile, 0)
@@ -212,11 +227,6 @@
     count = lax.axis_size(axis)
     first, last = (max(0, -steps), min(count, count - steps))
     return lax.ppermute(value, axis, [(source, source + steps) for source in range(first, last)])
-
-
-def rotated(value, axis, steps):
-    count = lax.axis_size(axis)
-    return lax.ppermute(value, axis, [(s, (s + steps) % count) for s in range(count)])
 
 
 def swapped(value):
@@ -235,22 +245,34 @@
     return other, f_all * one[0] + two[0], one[1] + f_all * two[1]
 
 
+def paired(value, axis, step, lines=None):
+    count = lax.axis_size(axis)
+    return lax.ppermute(value, axis, [(source, source ^ step) for source in lines or range(count)])
+
+
 def scanned(chip_e, chip_a, f_all, beside):
     chips = lax.axis_size("ctx") // 2
     f_chip = f_all * f_all
-    before = after = None
+    if chips == 4:
+        odd = lax.rem(lax.axis_index("ctx") // 2, 2) == 1
+        sent = jnp.where(odd, chip_a, chip_e)
+        first = paired(sent, "ctx", 2)
+        kept = beside[0](sent, None)
+        first, kept = lax.optimization_barrier((first, kept))
+        sent = jnp.where(odd, chip_e, chip_a) + f_chip * first
+        near = lax.ppermute(sent, "ctx", [(2, 4), (3, 5), (4, 2), (5, 3)])
+        far = lax.ppermute(sent, "ctx", [(2, 6), (3, 7), (4, 0), (5, 1)])
+        kept = beside[1](sent, kept)
+        near, far, kept = lax.optimization_barrier((near, far, kept))
+        far = first + f_chip * far
+        return jnp.where(odd, far, near), jnp.where(odd, near, far), kept
+    kept = beside[1](chip_e, beside[0](chip_e, None))
+    before, after = jnp.zeros_like(chip_e), jnp.zeros_like(chip_a)
     reach = 1
-    kept = None
     while reach < chips:
         early, late = shifted(chip_e, "ctx", 2 * reach), shifted(chip_a, "ctx", -2 * reach)
-        if 2 * reach >= chips:
-            kept = beside(chip_e)
-            (early, late), kept = lax.optimization_barrier(((early, late), kept))
-        if before is None:
-            before, after = early, late
-        else:
-            factor = f_chip ** (reach - 1)
-            before, after = before + factor * early, after + factor * late
+        factor = f_chip ** (reach - 1)
+        before, after = before + factor * early, after + factor * late
         factor = f_chip**reach
         chip_e, chip_a = chip_e + factor * early, chip_a + factor * late
         reach = 2 * reach
@@ -268,37 +290,26 @@
 
 
 def summed(value):
-    index = lax.axis_index("ctx")
-    core = lax.rem(index, 2)
-    chip = index // 2
-    chips = lax.axis_size("ctx") // 2
-    dp = lax.axis_index("dp")
-    parts = lax.axis_size("dp")
-    half = value.shape[0] // 2
-    keep = lax.dynamic_slice_in_dim(value, core * half, half, 0)
-    give = lax.dynamic_slice_in_dim(value, (1 - core) * half, half, 0)
-    value = keep + swapped(give)
-    size = half // parts
-    piece = lambda k: lax.dynamic_slice_in_dim(value, lax.rem(dp + k, parts) * size, size, 0)
-    total = piece(0)
-    for k in range(1, parts):
-        total = total + rotated(piece(k), "dp", k)
-    gathered = jnp.zeros((chips,) + total.shape, F32)
-    put = lambda into, at, what: lax.dynamic_update_slice_in_dim(into, what[None], at, 0)
-    gathered = put(gathered, chip, total)
-    for k in range(1, chips):
-        gathered = put(gathered, lax.rem(chip + chips - k, chips), rotated(total, "ctx", 2 * k))
-    total = gathered[0]
-    for k in range(1, chips):
-        total = total + gathered[k]
-    gathered = jnp.zeros((parts,) + total.shape, F32)
-    gathered = put(gathered, dp, total)
-    for k in range(1, parts):
-        gathered = put(gathered, lax.rem(dp + parts - k, parts), rotated(total, "dp", k))
-    mine = gathered.reshape((half,) + total.shape[1:])
-    other = swapped(mine)
-    first = core == 0
-    return jnp.concatenate([jnp.where(first, mine, other), jnp.where(first, other, mine)], axis=0)
+    index, dp = lax.axis_index("ctx"), lax.axis_index("dp")
+    steps = [("ctx", 1, lax.rem(index, 2))]
+    reach = 1
+    while reach < lax.axis_size("dp"):
+        steps.append(("dp", reach, lax.rem(dp // reach, 2)))
+        reach = 2 * reach
+    for axis, step, side in steps:
+        half = value.shape[0] // 2
+        keep = lax.dynamic_slice_in_dim(value, side * half, half, 0)
+        give = lax.dynamic_slice_in_dim(value, (1 - side) * half, half, 0)
+        value = keep + paired(give, axis, step)
+    reach = 2
+    while reach < lax.axis_size("ctx"):
+        value = value + paired(value, "ctx", reach)
+        reach = 2 * reach
+    for axis, step, side in reversed(steps):
+        other = paired(value, axis, step)
+        low = side == 0
+        value = jnp.concatenate([jnp.where(low, value, other), jnp.where(low, other, value)], axis=0)
+    return value
 
 
 def local(projected, short_filter, residues, decay_rates, skip_gain, cotangent):
@@ -347,10 +358,10 @@
             value.shape, lambda w: (0,) * value.ndim, pipeline_mode=pl.Buffered(1)
         )
 
-    params = pltpu.CompilerParams(vmem_limit_bytes=20 * 1024 * 1024)
+    params = pltpu.CompilerParams(vmem_limit_bytes=48 * 1024 * 1024)
     shape_of = jax.ShapeDtypeStruct
     state_shape = shape_of((poles, SUB, channels), F32)
-    xg, blocks_e, blocks_a, ends = pl.pallas_call(
+    qkv, xg, blocks_e, blocks_a, ends = pl.pallas_call(
         states_kernel,
         grid=(width // each,),
         in_specs=[
@@ -358,46 +369,56 @@
             fixed(f1), fixed(we), fixed(wb),
         ],
         out_specs=[
-            by_w(2, held), by_w(poles, SUB), by_w(poles, SUB),
+            by_w(3, held), by_w(2, held), by_w(poles, SUB), by_w(poles, SUB),
             pl.BlockSpec((2, each, poles, groups), lambda w: (0, w, 0, 0)),
         ],
         out_shape=[
-            shape_of((2, held, channels), F32), state_shape, state_shape,
-            shape_of((2, width, poles, groups), F32),
+            shape_of((3, held, channels), F32), shape_of((2, held, channels), F32),
+            state_shape, state_shape, shape_of((2, width, poles, groups), F32),
         ],
         scratch_shapes=[pltpu.VMEM((4, held + SUB, LANES), F32)],
         compiler_params=params,
         name="states",
     )(p, hb, ha, u, short_filter, f1, we, wb)
 
-    def blocks(chip_e):
-        close, _ = lax.optimization_barrier((near, chip_e))
-        return pl.pallas_call(
-            blocks_kernel,
-            grid=(width // each,),
-            in_specs=[
-                by_w(2, held), by_w(poles, SUB), by_w(poles, SUB), fixed(near), by_w(1),
-                fixed(join_e), fixed(join_a),
-            ],
-            out_specs=[by_w(2, held), by_w(poles, SUB), by_w(poles, SUB)],
-            out_shape=[shape_of((2, held, channels), F32), state_shape, state_shape],
-            input_output_aliases={0: 0, 1: 1, 2: 2},
-            compiler_params=params,
-            cost_estimate=pl.CostEstimate(
-                flops=60 * rows * channels, bytes_accessed=35 * 2**20, transcendentals=0
-            ),
-            name="blocks",
-        )(xg, blocks_e, blocks_a, close, skip_gain[None], join_e, join_a)
-
+    def blocks(first, last):
+        def at_w(*shape):
+            axis = len(shape)
+            return pl.BlockSpec(shape + (each * groups,), lambda w: (0,) * axis + (w + first,))
+
+        def call(sent, kept):
+            close, _ = lax.optimization_barrier((near, sent))
+            return pl.pallas_call(
+                blocks_kernel,
+                grid=(last - first,),
+                in_specs=[
+                    at_w(2, held), at_w(poles, SUB), at_w(poles, SUB), fixed(near), at_w(1),
+                    fixed(join_e), fixed(join_a),
+                ],
+                out_specs=[at_w(2, held), at_w(poles, SUB), at_w(poles, SUB)],
+                out_shape=[shape_of((2, held, channels), F32), state_shape, state_shape],
+                input_output_aliases={0: 0, 1: 1, 2: 2},
+                compiler_params=params,
+                cost_estimate=pl.CostEstimate(
+                    flops=60 * rows * channels, bytes_accessed=35 * 2**20, transcendentals=0
+                ),
+                name="blocks",
+            )(*(kept or (xg, blocks_e, blocks_a)), close, skip_gain[None], join_e, join_a)
+
+        return call
+
+    steps = width // each
+    cut = (steps + 1) // 3
     other, chip_e, chip_a = joined(ends, f_all)
-    before, after, (conv, from_e, from_a) = scanned(chip_e, chip_a, f_all, blocks)
+    before, after, (conv, from_e, from_a) = scanned(
+        chip_e, chip_a, f_all, (blocks(0, cut), blocks(cut, steps))
+    )
     enter, arrive = inward(other, before, after, f_all)
 
     count = 3 * taps + 3
     scratch = [
         pltpu.VMEM((3, held + SUB, LANES), F32),
         pltpu.VMEM((held, LANES), F32),
-        pltpu.VMEM((3, held, LANES), F32),
         pltpu.VMEM((3, held + SUB, LANES), F32),
         pltpu.VMEM((held, LANES), F32),
     ]
@@ -405,7 +426,7 @@
         final_kernel,
         grid=(width // each,),
         in_specs=[
-            by_w(3, rows), by_w(3, SUB), by_w(rows), by_w(4, SUB), by_w(2, held),
+            by_w(3, rows), by_w(3, SUB), by_w(rows), by_w(4, SUB), by_w(3, held), by_w(2, held),
             by_w(poles, SUB), by_w(poles, SUB), per_w(poles, groups), per_w(poles, groups),
             by_w(3, taps), fixed(f1), fixed(cz), fixed(cy),
         ],
@@ -418,7 +439,7 @@
         scratch_shapes=scratch,
         compiler_params=params,
         name="final",
-    )(p, hb, u, ha, conv, from_e, from_a, enter, arrive, short_filter, f1, cz, cy)
+    )(p, hb, u, ha, qkv, conv, from_e, from_a, enter, arrive, short_filter, f1, cz, cy)
 
     total = summed(sums).transpose(1, 0, 2).reshape(count, channels)
     grad_short = total[: 3 * taps].reshape(3, taps, channels)

time: 189 us -> 160 us (0.85)
  local copies, waits for them, and re-layouts: 36.2 us -> 7.57 us
  starting transfers between devices: 37.6 us -> 30.1 us
  Pallas kernels: 74.8 us -> 78 us
  other arithmetic: 11.8 us -> 14 us
    unnamed x60 -> x32, local copies, waits for them, and re-layouts: 32.2 us -> 2.3 us
    ppermute x9 -> x11, waiting for transfers between devices: 12.6 us -> 25.4 us  [the longest x9 25.4 us: paired(): lax.ppermute(value, axis, [(source, source ^ step) for source in lines or...]
    ppermute x6 -> x2, starting transfers between devices: 16.2 us -> 3.67 us  [shifted(): lax.ppermute(value, axis, [(source, source + steps) for source in range(f...]
    pallas_call x1 -> x2, Pallas kernels: 13.4 us -> 19.8 us  [call(): pl.pallas_call(blocks_kernel, grid=(last - first,), in_specs=[at_w(2, hel...]
    ppermute x4 -> x2, waiting for transfers between devices: 6.78 us -> 1.1 us  [swapped(): return lax.ppermute(value, 'ctx', [(s, s ^ 1) for s in range(count)])]
    ppermute x6 -> x2, waiting for transfers between devices: 6.89 us -> 1.53 us  [shifted(): lax.ppermute(value, axis, [(source, source + steps) for source in range(f...]
    ppermute x9 -> x11, starting transfers between devices: 13.9 us -> 19.2 us  [the longest x9 17.2 us: paired(): lax.ppermute(value, axis, [(source, source ^ step) for source in lines or...]
    pallas_call x1, Pallas kernels: 38.4 us -> 34.1 us  [local(): pl.pallas_call(final_kernel, grid=(width // each,), in_specs=[by_w(3, row...]
  transfers between devices with their start and end apart: 19 -> 15, of which waited for: 13 -> 10; matrix products, arithmetic and copies ran while one was open for 3% -> 6% of each run, Pallas kernels for 7% -> 13%
where the time goes in v4:
time: 160 us; the launch traced here: 159 us
  Pallas kernels  78 us (49%)
  starting transfers between devices  30.1 us (19%)
  waiting for transfers between devices  28 us (18%)
  other arithmetic  14 us (9%)
  local copies, waits for them, and re-layouts  7.57 us (5%)
    pallas_call x1, Pallas kernels, local(): pl.pallas_call(final_kernel, grid=(width // each,), in_specs=[by_w(3, row...  34.1 us
    ppermute x9, waiting for transfers between devices, paired(): lax.ppermute(value, axis, [(source, source ^ step) for source in lines or...  25.4 us
    pallas_call x1, Pallas kernels, local(): pl.pallas_call(states_kernel, grid=(width // each,), in_specs=[by_w(3, ro...  24.1 us
    pallas_call x2, Pallas kernels, call(): pl.pallas_call(blocks_kernel, grid=(last - first,), in_specs=[at_w(2, hel...  19.8 us
    ppermute x9, starting transfers between devices, paired(): lax.ppermute(value, axis, [(source, source ^ step) for source in lines or...  17.2 us
    ppermute x2, starting transfers between devices, swapped(): return lax.ppermute(value, 'ctx', [(s, s ^ 1) for s in range(count)])  7.26 us
    ppermute x2, starting transfers between devices, shifted(): lax.ppermute(value, axis, [(source, source + steps) for source in range(f...  3.67 us
  transfers between devices with their start and end apart: 15, of which 10 were waited for; matrix products, arithmetic and copies ran while one was open for 6% of the time, Pallas kernels for 13%

profile of v4, /device:TPU:0, one launch (start us, length us, event | category | flops | bytes accessed | tf_op | source)
XLA Modules:
  0.0 158.7 jit_solution(17452243967958696821)
XLA Ops:
  0.7 1.3 fusion.15
  2.0 2.4 %collective-permute-start = (bf16[3,8,8192]{2,1,0:T(8,128)(2,1)S(1)}, bf16[3,8,8192]{2,1,0:T(8,128)(2,1)S(1)}, u32[]{:S(2)}, u32[]{:S(2)}) collective-permute-start(bf16[3,8,8192]{2,1,0:T(8,128)(2,1)S(1)} %get-tuple-element.55), channel_id=1, source_target_pairs={{0,1},{1,2},{2,3},{3,4},{4,5},{5,6},{6,7},{8,9},{9,10},{10,11},{11... | collective-permute-start | bytes 1179656 | tf_op jit(solution)/shard_map/ppermute | solution.py:229
  4.4 0.9 slice.64
  5.3 1.3 collective-permute-start.1
  6.6 0.8 negate_bitcast_fusion
  7.4 0.9 multiply_exponential_fusion
  8.3 0.0 copy-start.6
  8.3 1.4 fusion.14
  9.8 1.5 collective-permute-done.1.ha
  11.3 0.0 copy-start.12
  11.3 0.0 copy-start.15
  11.3 24.1 %states.1 = (f32[3,136,8192]{2,1,0:T(8,128)}, f32[2,136,8192]{2,1,0:T(8,128)}, f32[16,8,8192]{2,1,0:T(8,128)}, f32[16,8,8192]{2,1,0:T(8,128)}, f32[2,16,16,512]{3,2,1,0:T(8,128)}) custom-call(bf16[3,128,8192]{2,1,0:T(8,128)(2,1)} %bitcast.102, bf16[3,8,8192]{2,1,0:T(8,128)(2,1)S(1)} %collective-permute-done.hb, ...), custom_call_target="tpu_custom_call" | custom-call | tf_op jit(solution)/shard_map/states/pallas_call | solution.py:364
  35.4 0.0 copy-start.14
  35.4 7.3 %collective-permute-start.2 = (f32[2,16,16,512]{3,2,1,0:T(8,128)}, f32[2,16,16,512]{3,2,1,0:T(8,128)}, u32[]{:S(2)}, u32[]{:S(2)}) collective-permute-start(f32[2,16,16,512]{3,2,1,0:T(8,128)} %get-tuple-element.30), channel_id=1, source_target_pairs={{0,1},{1,0},{2,3},{3,2},{4,5},{5,4},{6,7},{7,6},{8,9},{9,8},{10,11... | collective-permute-start | bytes 3145736 | tf_op jit(solution)/shard_map/ppermute | solution.py:234
  42.7 0.1 multiply_exponential_fusion.1
  42.8 0.0 copy-start.9
  42.8 0.6 copy-done.9
  43.5 0.7 slice.90
  44.1 0.8 slice_multiply_fusion
  44.9 0.9 pad_maximum_fusion.5
  45.8 1.0 multiply_reduce_fusion.near
  46.8 1.3 dynamic-slice_select_fusion.1
  48.1 0.1 broadcast_select_fusion.6
  48.2 1.6 %collective-permute-start.3 = (f32[8,16,512]{2,1,0:T(8,128)S(1)}, f32[8,16,512]{2,1,0:T(8,128)S(1)}, u32[]{:S(2)}, u32[]{:S(2)}) collective-permute-start(f32[8,16,512]{2,1,0:T(8,128)S(1)} %broadcast_select_fusion.6), channel_id=1, source_target_pairs={{0,2},{1,3},{2,0},{3,1},{4,6},{5,7},{6,4},{7,5},{8,10},{9,11},{10,... | collective-permute-start | bytes 786440 | tf_op jit(solution)/shard_map/ppermute | solution.py:250
  49.9 0.3 broadcast_select_fusion
  50.2 0.0 copy-start.10
  50.2 8.1 %blocks.2 = (f32[2,136,8192]{2,1,0:T(8,128)}, f32[16,8,8192]{2,1,0:T(8,128)}, f32[16,8,8192]{2,1,0:T(8,128)}) custom-call(f32[2,136,8192]{2,1,0:T(8,128)} %get-tuple-element.31.xg, f32[16,8,8192]{2,1,0:T(8,128)} %get-tuple-element.32.blocks_e, f32[16,8,8192]{2,1,0:T(8,128)} %get-tuple-element.33.blocks_a, ...), custom_call_target="tpu_custom_call", output_to_operand_aliasing={{0}: (0, {}), {1}: (1, {}), {2}: (2, {})} | custom-call | flops 62914560 | bytes 36700160 | tf_op jit(solution)/shard_map/blocks/pallas_call | solution.py:391
  58.3 0.1 multiply_add_fusion.1
  58.5 0.0 copy-start.11
  58.5 1.3 collective-permute-start.5
  59.8 0.7 collective-permute-start.4
  60.5 11.7 %blocks.3 = (f32[2,136,8192]{2,1,0:T(8,128)}, f32[16,8,8192]{2,1,0:T(8,128)}, f32[16,8,8192]{2,1,0:T(8,128)}) custom-call(f32[2,136,8192]{2,1,0:T(8,128)} %get-tuple-element.39.xg, f32[16,8,8192]{2,1,0:T(8,128)} %get-tuple-element.40.blocks_e, f32[16,8,8192]{2,1,0:T(8,128)} %get-tuple-element.41.blocks_a, ...), custom_call_target="tpu_custom_call", output_to_operand_aliasing={{0}: (0, {}), {1}: (1, {}), {2}: (2, {})} | custom-call | flops 62914560 | bytes 36700160 | tf_op jit(solution)/shard_map/blocks/pallas_call | solution.py:391
  72.2 0.1 select_bitcast_fusion.1
  72.3 0.0 copy-start.8
  72.4 0.7 copy-done.7
  73.0 0.8 pad_maximum_fusion.2
  73.9 1.1 fusion.7
  75.0 1.1 collective-permute-done.6
  76.1 1.3 broadcast_select_fusion.3
  77.5 1.5 fusion.4
  79.0 34.1 %final.1 = (bf16[128,8192]{1,0:T(8,128)(2,1)}, bf16[3,128,8192]{2,1,0:T(8,128)(2,1)}, f32[16,24,512]{2,1,0:T(8,128)S(1)}) custom-call(bf16[3,128,8192]{2,1,0:T(8,128)(2,1)} %bitcast.103, bf16[3,8,8192]{2,1,0:T(8,128)(2,1)S(1)} %copy-done.3, bf16[128,8192]{1,0:T(8,128)(2,1)S(1)} %bitcast.98, bf16[4,8,8192]{2,1,0:T(8,128)(2,1)S(1)} %collective-permute-done.1.ha, ...), custom_call_target="tpu_custom_call" | custom-call | tf_op jit(solution)/shard_map/final/pallas_call | solution.py:425
  113.1 0.9 copy-done.4
  114.0 0.2 collective-permute-start.7
  114.2 1.6 collective-permute-done.7
  115.8 1.1 dynamic-slice_add_fusion
  116.9 1.6 collective-permute-start.8
  118.4 5.5 %collective-permute-done.8 = f32[4,24,512]{2,1,0:T(8,128)S(1)} collective-permute-done((f32[4,24,512]{2,1,0:T(8,128)S(1)}, f32[4,24,512]{2,1,0:T(8,128)S(1)}, u32[]{:S(2)}, u32[]{:S(2)}) %collective-permute-start.8) | collective-permute-done | bytes 196640 | tf_op jit(solution)/shard_map/ppermute | solution.py:250
  124.0 1.6 collective-permute-start.9
  125.5 3.1 %collective-permute-done.9 = f32[2,24,512]{2,1,0:T(8,128)S(1)} collective-permute-done((f32[2,24,512]{2,1,0:T(8,128)S(1)}, f32[2,24,512]{2,1,0:T(8,128)S(1)}, u32[]{:S(2)}, u32[]{:S(2)}) %collective-permute-start.9) | collective-permute-done | bytes 98336 | tf_op jit(solution)/shard_map/ppermute | solution.py:250
  128.7 5.4 %collective-permute-start.10 = (f32[2,24,512]{2,1,0:T(8,128)S(1)}, f32[2,24,512]{2,1,0:T(8,128)S(1)}, u32[]{:S(2)}, u32[]{:S(2)}) collective-permute-start(f32[2,24,512]{2,1,0:T(8,128)S(1)} %dynamic-slice_add_fusion.2), channel_id=1, source_target_pairs={{0,2},{1,3},{2,0},{3,1},{4,6},{5,7},{6,4},{7,5},{8,10},{9,11},{10,... | collective-permute-start | bytes 294920 | tf_op jit(solution)/shard_map/ppermute | solution.py:250
  134.1 2.6 %collective-permute-done.10 = f32[2,24,512]{2,1,0:T(8,128)S(1)} collective-permute-done((f32[2,24,512]{2,1,0:T(8,128)S(1)}, f32[2,24,512]{2,1,0:T(8,128)S(1)}, u32[]{:S(2)}, u32[]{:S(2)}) %collective-permute-start.10) | collective-permute-done | bytes 98336 | tf_op jit(solution)/shard_map/ppermute | solution.py:250
  136.7 3.6 %collective-permute-start.11 = (f32[2,24,512]{2,1,0:T(8,128)S(1)}, f32[2,24,512]{2,1,0:T(8,128)S(1)}, u32[]{:S(2)}, u32[]{:S(2)}) collective-permute-start(f32[2,24,512]{2,1,0:T(8,128)S(1)} %add.71), channel_id=1, source_target_pairs={{0,4},{1,5},{2,6},{3,7},{4,0},{5,1},{6,2},{7,3},{8,12},{9,13},{10,... | collective-permute-start | bytes 294920 | tf_op jit(solution)/shard_map/ppermute | solution.py:250
  140.3 3.6 %collective-permute-done.11 = f32[2,24,512]{2,1,0:T(8,128)S(1)} collective-permute-done((f32[2,24,512]{2,1,0:T(8,128)S(1)}, f32[2,24,512]{2,1,0:T(8,128)S(1)}, u32[]{:S(2)}, u32[]{:S(2)}) %collective-permute-start.11) | collective-permute-done | bytes 98336 | tf_op jit(solution)/shard_map/ppermute | solution.py:250
  143.9 1.6 collective-permute-start.12
  145.5 3.1 %collective-permute-done.12 = f32[2,24,512]{2,1,0:T(8,128)S(1)} collective-permute-done((f32[2,24,512]{2,1,0:T(8,128)S(1)}, f32[2,24,512]{2,1,0:T(8,128)S(1)}, u32[]{:S(2)}, u32[]{:S(2)}) %collective-permute-start.12) | collective-permute-done | bytes 98336 | tf_op jit(solution)/shard_map/ppermute | solution.py:250
  148.7 1.6 collective-permute-start.13
  150.2 4.2 %collective-permute-done.13 = f32[4,24,512]{2,1,0:T(8,128)S(1)} collective-permute-done((f32[4,24,512]{2,1,0:T(8,128)S(1)}, f32[4,24,512]{2,1,0:T(8,128)S(1)}, u32[]{:S(2)}, u32[]{:S(2)}) %collective-permute-start.13) | collective-permute-done | bytes 196640 | tf_op jit(solution)/shard_map/ppermute | solution.py:250
  154.5 0.1 collective-permute-start.14
  154.5 1.7 %collective-permute-done.14 = f32[8,24,512]{2,1,0:T(8,128)S(1)} collective-permute-done((f32[8,24,512]{2,1,0:T(8,128)S(1)}, f32[8,24,512]{2,1,0:T(8,128)S(1)}, u32[]{:S(2)}, u32[]{:S(2)}) %collective-permute-start.14) | collective-permute-done | bytes 393248 | tf_op jit(solution)/shard_map/ppermute | solution.py:250
  156.3 0.1 broadcast_select_fusion.5
  156.3 0.1 maximum_bitcast_fusion
  156.4 0.6 slice.98
  157.0 0.4 copy.22
  157.4 1.2 reshape.28
  (40 shorter events, 0.4 us)
Async XLA Ops:
  0.6 10.7 %copy-start = (bf16[1,128,8192]{2,1,0:T(8,128)(2,1)S(1)}, bf16[1,128,8192]{2,1,0:T(8,128)(2,1)}, u32[]{:S(2)}) copy-start(bf16[1,128,8192]{2,1,0:T(8,128)(2,1)} %param.16) | copy-start | bytes 6291460
  0.6 10.7 %copy-start.1 = (f32[3,7,8192]{2,1,0:T(8,128)S(1)}, f32[3,7,8192]{2,1,0:T(8,128)}, u32[]{:S(2)}) copy-start(f32[3,7,8192]{2,1,0:T(8,128)} %filt.3) | copy-start | bytes 2064388
  2.0 7.8 %collective-permute-start = (bf16[3,8,8192]{2,1,0:T(8,128)(2,1)S(1)}, bf16[3,8,8192]{2,1,0:T(8,128)(2,1)S(1)}, u32[]{:S(2)}, u32[]{:S(2)}) collective-permute-start(bf16[3,8,8192]{2,1,0:T(8,128)(2,1)S(1)} %get-tuple-element.55), channel_id=1, source_target_pairs={{0,1},{1,2},{2,3},{3,4},{4,5},{5,6},{6,7},{8,9},{9,10},{10,11},{11... | collective-permute-start | bytes 1179656 | tf_op jit(solution)/shard_map/ppermute | solution.py:229
  5.3 6.0 %collective-permute-start.1 = (bf16[4,8,8192]{2,1,0:T(8,128)(2,1)S(1)}, bf16[4,8,8192]{2,1,0:T(8,128)(2,1)S(1)}, u32[]{:S(2)}, u32[]{:S(2)}) collective-permute-start(bf16[4,8,8192]{2,1,0:T(8,128)(2,1)S(1)} %pad_maximum_fusion.1), channel_id=1, source_target_pairs={{1,0},{2,1},{3,2},{4,3},{5,4},{6,5},{7,6},{9,8},{10,9},{11,10},{12... | collective-permute-start | bytes 1572872 | tf_op jit(solution)/shard_map/ppermute | solution.py:229
  8.3 3.0 %copy-start.6 = (f32[4,16,8,512]{3,2,1,0:T(8,128)}, f32[4,16,8,512]{3,2,1,0:T(8,128)S(1)}, u32[]{:S(2)}) copy-start(f32[4,16,8,512]{3,2,1,0:T(8,128)S(1)} %multiply_exponential_fusion) | copy-start | bytes 3145732
  9.8 25.6 %copy-start.2 = (bf16[3,8,8192]{2,1,0:T(8,128)(2,1)}, bf16[3,8,8192]{2,1,0:T(8,128)(2,1)S(1)}, u32[]{:S(2)}) copy-start(bf16[3,8,8192]{2,1,0:T(8,128)(2,1)S(1)} %collective-permute-done.hb) | copy-start | bytes 1179652
  11.3 31.4 %copy-start.12 = (f32[4]{0:T(128)S(1)}, f32[4]{0:T(128)}, u32[]{:S(2)}) copy-start(f32[4]{0:T(128)} %constant.76) | copy-start | bytes 52
  11.3 34.5 %copy-start.15 = (f32[24]{0:T(128)S(1)}, f32[24]{0:T(128)}, u32[]{:S(2)}) copy-start(f32[24]{0:T(128)} %constant.74) | copy-start | bytes 292
  35.4 14.5 %copy-start.13 = (pred[4,8]{1,0:T(4,128)(4,1)S(1)}, pred[4,8]{1,0:T(4,128)(4,1)}, u32[]{:S(2)}) copy-start(pred[4,8]{1,0:T(4,128)(4,1)} %constant.77) | copy-start | bytes 100
  35.4 14.5 %copy-start.14 = (pred[4,8]{1,0:T(4,128)(4,1)S(1)}, pred[4,8]{1,0:T(4,128)(4,1)}, u32[]{:S(2)}) copy-start(pred[4,8]{1,0:T(4,128)(4,1)} %constant.75) | copy-start | bytes 100
  35.4 14.8 %copy-start.5 = (f32[8192]{0:T(1024)S(1)}, f32[8192]{0:T(1024)}, u32[]{:S(2)}) copy-start(f32[8192]{0:T(1024)} %param.15) | copy-start | bytes 98308
  35.4 11.3 %collective-permute-start.2 = (f32[2,16,16,512]{3,2,1,0:T(8,128)}, f32[2,16,16,512]{3,2,1,0:T(8,128)}, u32[]{:S(2)}, u32[]{:S(2)}) collective-permute-start(f32[2,16,16,512]{3,2,1,0:T(8,128)} %get-tuple-element.30), channel_id=1, source_target_pairs={{0,1},{1,0},{2,3},{3,2},{4,5},{5,4},{6,7},{7,6},{8,9},{9,8},{10,11... | collective-permute-start | bytes 3145736 | tf_op jit(solution)/shard_map/ppermute | solution.py:234
  42.8 0.7 copy-start.9
  48.2 10.1 %collective-permute-start.3 = (f32[8,16,512]{2,1,0:T(8,128)S(1)}, f32[8,16,512]{2,1,0:T(8,128)S(1)}, u32[]{:S(2)}, u32[]{:S(2)}) collective-permute-start(f32[8,16,512]{2,1,0:T(8,128)S(1)} %broadcast_select_fusion.6), channel_id=1, source_target_pairs={{0,2},{1,3},{2,0},{3,1},{4,6},{5,7},{6,4},{7,5},{8,10},{9,11},{10,... | collective-permute-start | bytes 786440 | tf_op jit(solution)/shard_map/ppermute | solution.py:250
  50.2 8.1 %copy-start.10 = (f32[16,512]{1,0:T(8,128)S(1)}, f32[16,512]{1,0:T(8,128)}, u32[]{:S(2)}) copy-start(f32[16,512]{1,0:T(8,128)} %get-tuple-element.76) | copy-start | bytes 98308
  58.5 15.4 %copy-start.11 = (f32[512,16]{0,1:T(8,128)S(1)}, f32[512,16]{0,1:T(8,128)}, u32[]{:S(2)}) copy-start(f32[512,16]{0,1:T(8,128)} %param.13) | copy-start | bytes 98308
  58.5 13.7 %collective-permute-start.5 = (f32[8,16,512]{2,1,0:T(8,128)S(1)}, f32[8,16,512]{2,1,0:T(8,128)S(1)}, u32[]{:S(2)}, u32[]{:S(2)}) collective-permute-start(f32[8,16,512]{2,1,0:T(8,128)S(1)} %multiply_add_fusion.1), channel_id=1, source_target_pairs={{2,6},{3,7},{4,0},{5,1},{10,14},{11,15},{12,8},{13,9},{18,22},{19,... | collective-permute-start | bytes 786440 | tf_op jit(solution)/shard_map/ppermute | solution.py:264
  59.8 12.4 %collective-permute-start.4 = (f32[8,16,512]{2,1,0:T(8,128)S(1)}, f32[8,16,512]{2,1,0:T(8,128)S(1)}, u32[]{:S(2)}, u32[]{:S(2)}) collective-permute-start(f32[8,16,512]{2,1,0:T(8,128)S(1)} %multiply_add_fusion.1), channel_id=1, source_target_pairs={{2,4},{3,5},{4,2},{5,3},{10,12},{11,13},{12,10},{13,11},{18,20},{1... | collective-permute-start | bytes 786440 | tf_op jit(solution)/shard_map/ppermute | solution.py:263
  72.3 0.7 copy-start.7
  72.3 1.5 copy-start.8
  73.9 2.3 %collective-permute-start.6 = (f32[2,8,16,512]{3,2,1,0:T(8,128)}, f32[2,8,16,512]{3,2,1,0:T(8,128)}, u32[]{:S(2)}, u32[]{:S(2)}) collective-permute-start(f32[2,8,16,512]{3,2,1,0:T(8,128)} %pad_maximum_fusion.2), channel_id=1, source_target_pairs={{0,1},{1,0},{2,3},{3,2},{4,5},{5,4},{6,7},{7,6},{8,9},{9,8},{10,11... | collective-permute-start | bytes 1572872 | tf_op jit(solution)/shard_map/ppermute | solution.py:234
  73.9 5.1 %copy-start.3 = (bf16[3,8,8192]{2,1,0:T(8,128)(2,1)S(1)}, bf16[3,8,8192]{2,1,0:T(8,128)(2,1)}, u32[]{:S(2)}) copy-start(bf16[3,8,8192]{2,1,0:T(8,128)(2,1)} %copy-done.2) | copy-start | bytes 1179652
  113.1 0.9 copy-start.4
  114.0 1.8 %collective-permute-start.7 = (f32[8,24,512]{2,1,0:T(8,128)S(1)}, f32[8,24,512]{2,1,0:T(8,128)S(1)}, u32[]{:S(2)}, u32[]{:S(2)}) collective-permute-start(f32[8,24,512]{2,1,0:T(8,128)S(1)} %constant_dynamic-slice_fusion.2), channel_id=1, source_target_pairs={{0,1},{1,0},{2,3},{3,2},{4,5},{5,4},{6,7},{7,6},{8,9},{9,8},{10,11... | collective-permute-start | bytes 1179656 | tf_op jit(solution)/shard_map/ppermute | solution.py:250
  116.9 7.0 %collective-permute-start.8 = (f32[4,24,512]{2,1,0:T(8,128)S(1)}, f32[4,24,512]{2,1,0:T(8,128)S(1)}, u32[]{:S(2)}, u32[]{:S(2)}) collective-permute-start(f32[4,24,512]{2,1,0:T(8,128)S(1)} %constant_dynamic-slice_fusion.1), channel_id=1, source_target_pairs={{0,8},{8,0},{16,24},{24,16},{1,9},{9,1},{17,25},{25,17},{2,10},{10... | collective-permute-start | bytes 589832 | tf_op jit(solution)/shard_map/ppermute | solution.py:250
  124.0 4.7 %collective-permute-start.9 = (f32[2,24,512]{2,1,0:T(8,128)S(1)}, f32[2,24,512]{2,1,0:T(8,128)S(1)}, u32[]{:S(2)}, u32[]{:S(2)}) collective-permute-start(f32[2,24,512]{2,1,0:T(8,128)S(1)} %constant_dynamic-slice_fusion), channel_id=1, source_target_pairs={{0,16},{8,24},{16,0},{24,8},{1,17},{9,25},{17,1},{25,9},{2,18},{10... | collective-permute-start | bytes 294920 | tf_op jit(solution)/shard_map/ppermute | solution.py:250
  128.7 8.0 %collective-permute-start.10 = (f32[2,24,512]{2,1,0:T(8,128)S(1)}, f32[2,24,512]{2,1,0:T(8,128)S(1)}, u32[]{:S(2)}, u32[]{:S(2)}) collective-permute-start(f32[2,24,512]{2,1,0:T(8,128)S(1)} %dynamic-slice_add_fusion.2), channel_id=1, source_target_pairs={{0,2},{1,3},{2,0},{3,1},{4,6},{5,7},{6,4},{7,5},{8,10},{9,11},{10,... | collective-permute-start | bytes 294920 | tf_op jit(solution)/shard_map/ppermute | solution.py:250
  136.7 7.2 %collective-permute-start.11 = (f32[2,24,512]{2,1,0:T(8,128)S(1)}, f32[2,24,512]{2,1,0:T(8,128)S(1)}, u32[]{:S(2)}, u32[]{:S(2)}) collective-permute-start(f32[2,24,512]{2,1,0:T(8,128)S(1)} %add.71), channel_id=1, source_target_pairs={{0,4},{1,5},{2,6},{3,7},{4,0},{5,1},{6,2},{7,3},{8,12},{9,13},{10,... | collective-permute-start | bytes 294920 | tf_op jit(solution)/shard_map/ppermute | solution.py:250
  143.9 4.7 %collective-permute-start.12 = (f32[2,24,512]{2,1,0:T(8,128)S(1)}, f32[2,24,512]{2,1,0:T(8,128)S(1)}, u32[]{:S(2)}, u32[]{:S(2)}) collective-permute-start(f32[2,24,512]{2,1,0:T(8,128)S(1)} %add.72), channel_id=1, source_target_pairs={{0,16},{8,24},{16,0},{24,8},{1,17},{9,25},{17,1},{25,9},{2,18},{10... | collective-permute-start | bytes 294920 | tf_op jit(solution)/shard_map/ppermute | solution.py:250
  148.7 5.7 %collective-permute-start.13 = (f32[4,24,512]{2,1,0:T(8,128)S(1)}, f32[4,24,512]{2,1,0:T(8,128)S(1)}, u32[]{:S(2)}, u32[]{:S(2)}) collective-permute-start(f32[4,24,512]{2,1,0:T(8,128)S(1)} %pad_maximum_fusion.4), channel_id=1, source_target_pairs={{0,8},{8,0},{16,24},{24,16},{1,9},{9,1},{17,25},{25,17},{2,10},{10... | collective-permute-start | bytes 589832 | tf_op jit(solution)/shard_map/ppermute | solution.py:250
  154.5 1.8 %collective-permute-start.14 = (f32[8,24,512]{2,1,0:T(8,128)S(1)}, f32[8,24,512]{2,1,0:T(8,128)S(1)}, u32[]{:S(2)}, u32[]{:S(2)}) collective-permute-start(f32[8,24,512]{2,1,0:T(8,128)S(1)} %pad_maximum_fusion.3), channel_id=1, source_target_pairs={{0,1},{1,0},{2,3},{3,2},{4,5},{5,4},{6,7},{7,6},{8,9},{9,8},{10,11... | collective-permute-start | bytes 1179656 | tf_op jit(solution)/shard_map/ppermute | solution.py:250

commit v5 on v4

--- a/solution.py
+++ b/solution.py
@@ -146,8 +146,8 @@
 
 
 def final_kernel(
-    p, hb, u, ha, qkv, conv, from_e, from_a, enter, arrive, filt, f1, cz, cy,
-    output, grad_p, sums, ps, us, gs, os,
+    core, p, hb, u, ha, qkv, conv, from_e, from_a, both, found, other, filt, f1, f_all, cz, cy,
+    output, grad_p, sums, ps, us, gs, os, es,
 ):
     rows = p.shape[1]
     run = (rows + SUB) // SUB
@@ -155,12 +155,19 @@
     poles, groups = f1.shape
     own = rows - run * (SUB - 1)
     tiles = groups // LANES
+    first = core[0] == 0
+    halves = pl.num_programs(0) // 2
+    kept = (pl.program_id(0) < halves) == first
 
     def tile(lt, carry):
         lanes = pl.ds(pl.multiple_of(lt * LANES, LANES), LANES)
         part = pl.ds(pl.multiple_of(lax.rem(lt, tiles) * LANES, LANES), LANES)
         which = lt // tiles
         inside = lax.broadcasted_iota(jnp.int32, (SUB, LANES), 0) < SUB - 1
+        for side in range(2):
+            far = jnp.where(kept, both[side, which, :, part], found[side, which, :, part])
+            close = other[side, which, :, part] + f_all[:, part] * far
+            es[side] = jnp.where(first == (side == 0), far, close)
         for j in range(3):
             ps[j, 0:SUB] = hb[j, :, lanes].astype(F32)
             ps[j, SUB : SUB + rows] = p[j, :, lanes].astype(F32)
@@ -170,7 +177,7 @@
         decay = [spread(f1[n : n + 1, part]) for n in range(poles)]
 
         state = [
-            from_e[n, :, lanes] + cz[n, :, part] * spread(enter[which, n : n + 1, part])
+            from_e[n, :, lanes] + cz[n, :, part] * spread(es[0, n : n + 1])
             for n in range(poles)
         ]
         skip_sum = None
@@ -189,7 +196,7 @@
         output[:, lanes] = os[0:rows].astype(BF16)
 
         state = [
-            from_a[n, :, lanes] + cy[n, :, part] * spread(arrive[which, n : n + 1, part])
+            from_a[n, :, lanes] + cy[n, :, part] * spread(es[1, n : n + 1])
             for n in range(poles)
         ]
         for a in range(run - 1, -1, -1):
@@ -279,37 +286,24 @@
     return before, after, kept
 
 
-def inward(other, before, after, f_all):
-    first = lax.rem(lax.axis_index("ctx"), 2) == 0
-    both = jnp.stack([before, after])
-    found = swapped(both)
-    both = jnp.concatenate([jnp.where(first, both, found), jnp.where(first, found, both)], axis=1)
-    enter = jnp.where(first, both[0], f_all * both[0] + other[0])
-    arrive = jnp.where(first, other[1] + f_all * both[1], both[1])
-    return enter, arrive
-
-
 def summed(value):
-    index, dp = lax.axis_index("ctx"), lax.axis_index("dp")
-    steps = [("ctx", 1, lax.rem(index, 2))]
-    reach = 1
-    while reach < lax.axis_size("dp"):
-        steps.append(("dp", reach, lax.rem(dp // reach, 2)))
-        reach = 2 * reach
-    for axis, step, side in steps:
-        half = value.shape[0] // 2
-        keep = lax.dynamic_slice_in_dim(value, side * half, half, 0)
-        give = lax.dynamic_slice_in_dim(value, (1 - side) * half, half, 0)
-        value = keep + paired(give, axis, step)
+    parts = lax.axis_size("dp")
+    side = lax.rem(lax.axis_index("ctx"), 2)
+    half = value.shape[0] // 2
+    keep = lax.dynamic_slice_in_dim(value, side * half, half, 0)
+    give = lax.dynamic_slice_in_dim(value, (1 - side) * half, half, 0)
+    value = keep + swapped(give)
+    value = value.reshape((parts, half // parts) + value.shape[1:])
+    value = jnp.sum(lax.all_to_all(value, "dp", 0, 0), axis=0)
     reach = 2
     while reach < lax.axis_size("ctx"):
         value = value + paired(value, "ctx", reach)
         reach = 2 * reach
-    for axis, step, side in reversed(steps):
-        other = paired(value, axis, step)
-        low = side == 0
-        value = jnp.concatenate([jnp.where(low, value, other), jnp.where(low, other, value)], axis=0)
-    return value
+    value = lax.all_to_all(jnp.broadcast_to(value, (parts,) + value.shape), "dp", 0, 0)
+    value = value.reshape((half,) + value.shape[2:])
+    other = swapped(value)
+    low = side == 0
+    return jnp.concatenate([jnp.where(low, value, other), jnp.where(low, other, value)], axis=0)
 
 
 def local(projected, short_filter, residues, decay_rates, skip_gain, cotangent):
@@ -344,7 +338,7 @@
     close = np.arange(-taps, run).astype(np.float32)
     near = jnp.sum(weight[:, None, :] * jnp.exp(-rate[:, None, :] * close[None, :, None]), axis=0)
 
-    each = 2 if width % 2 == 0 else 1
+    each = 1
 
     def by_w(*shape):
         axis = len(shape)
@@ -360,6 +354,10 @@
 
     params = pltpu.CompilerParams(vmem_limit_bytes=48 * 1024 * 1024)
     shape_of = jax.ShapeDtypeStruct
+    ends_spec = pl.BlockSpec((2, each, poles, groups), lambda w: (0, w, 0, 0))
+    halved = pl.BlockSpec(
+        (2, each, poles, groups), lambda w: (0, lax.rem(w, width // each // 2), 0, 0)
+    )
     state_shape = shape_of((poles, SUB, channels), F32)
     qkv, xg, blocks_e, blocks_a, ends = pl.pallas_call(
         states_kernel,
@@ -370,7 +368,7 @@
         ],
         out_specs=[
             by_w(3, held), by_w(2, held), by_w(poles, SUB), by_w(poles, SUB),
-            pl.BlockSpec((2, each, poles, groups), lambda w: (0, w, 0, 0)),
+            ends_spec,
         ],
         out_shape=[
             shape_of((3, held, channels), F32), shape_of((2, held, channels), F32),
@@ -413,7 +411,9 @@
     before, after, (conv, from_e, from_a) = scanned(
         chip_e, chip_a, f_all, (blocks(0, cut), blocks(cut, steps))
     )
-    enter, arrive = inward(other, before, after, f_all)
+    both = jnp.stack([before, after])
+    found = swapped(both)
+    core = lax.rem(lax.axis_index("ctx"), 2)
 
     count = 3 * taps + 3
     scratch = [
@@ -421,14 +421,16 @@
         pltpu.VMEM((held, LANES), F32),
         pltpu.VMEM((3, held + SUB, LANES), F32),
         pltpu.VMEM((held, LANES), F32),
+        pltpu.VMEM((2, poles, LANES), F32),
     ]
     output, grad_p, sums = pl.pallas_call(
         final_kernel,
         grid=(width // each,),
         in_specs=[
+            pl.BlockSpec(memory_space=pltpu.SMEM),
             by_w(3, rows), by_w(3, SUB), by_w(rows), by_w(4, SUB), by_w(3, held), by_w(2, held),
-            by_w(poles, SUB), by_w(poles, SUB), per_w(poles, groups), per_w(poles, groups),
-            by_w(3, taps), fixed(f1), fixed(cz), fixed(cy),
+            by_w(poles, SUB), by_w(poles, SUB), halved, halved, ends_spec,
+            by_w(3, taps), fixed(f1), fixed(f_all), fixed(cz), fixed(cy),
         ],
         out_specs=[by_w(rows), by_w(3, rows), per_w(count, groups)],
         out_shape=[
@@ -439,7 +441,10 @@
         scratch_shapes=scratch,
         compiler_params=params,
         name="final",
-    )(p, hb, u, ha, qkv, conv, from_e, from_a, enter, arrive, short_filter, f1, cz, cy)
+    )(
+        core[None], p, hb, u, ha, qkv, conv, from_e, from_a, both, found, other, short_filter,
+        f1, f_all, cz, cy,
+    )
 
     total = summed(sums).transpose(1, 0, 2).reshape(count, channels)
     grad_short = total[: 3 * taps].reshape(3, taps, channels)

time: 160 us -> 148 us (0.925)
  blocking collectives: 0 us -> 19.8 us
  waiting for transfers between devices: 28 us -> 13.6 us
  other arithmetic: 14 us -> 6.01 us
  starting transfers between devices: 30.1 us -> 23.8 us
  local copies, waits for them, and re-layouts: 7.57 us -> 4.91 us
    ppermute x9 -> x3, waiting for transfers between devices: 25.4 us -> 5.2 us  [paired(): lax.ppermute(value, axis, [(source, source ^ step) for source in lines or...]
    all_to_all x0 -> x2, blocking collectives: none -> 19.8 us  [the longest x1 10.9 us: summed(): value = jnp.sum(lax.all_to_all(value, 'dp', 0, 0), axis=0)]
    ppermute x9 -> x3, starting transfers between devices: 17.2 us -> 10.3 us  [paired(): lax.ppermute(value, axis, [(source, source ^ step) for source in lines or...]
    ppermute x2 -> x4, waiting for transfers between devices: 1.1 us -> 6.29 us  [swapped(): return lax.ppermute(value, 'ctx', [(s, s ^ 1) for s in range(count)])]
    select_n x2 -> x0, other arithmetic: 2.84 us -> none  [the longest x1 1.51 us: inward(): arrive = jnp.where(first, other[1] + f_all * both[1], both[1])]
    unnamed x32 -> x22, local copies, waits for them, and re-layouts: 2.3 us -> 0.07 us
    pallas_call x2, Pallas kernels: 19.8 us -> 22 us  [call(): pl.pallas_call(blocks_kernel, grid=(last - first,), in_specs=[at_w(2, hel...]
    ppermute x2 -> x4, starting transfers between devices: 7.26 us -> 7.68 us  [swapped(): return lax.ppermute(value, 'ctx', [(s, s ^ 1) for s in range(count)])]
  transfers between devices with their start and end apart: 15 -> 11, of which waited for: 10 -> 7; matrix products, arithmetic and copies ran while one was open for 6% -> 4% of each run, Pallas kernels for 13% -> 15%
where the time goes in v5:
time: 148 us; the launch traced here: 147 us
  Pallas kernels  78.1 us (53%)
  starting transfers between devices  23.8 us (16%)
  blocking collectives  19.8 us (13%)
  waiting for transfers between devices  13.6 us (9%)
  other arithmetic  6.01 us (4%)
  local copies, waits for them, and re-layouts  4.91 us (3%)
    pallas_call x1, Pallas kernels, local(): pl.pallas_call(final_kernel, grid=(width // each,), in_specs=[pl.BlockSpe...  33.4 us
    pallas_call x1, Pallas kernels, local(): pl.pallas_call(states_kernel, grid=(width // each,), in_specs=[by_w(3, ro...  22.7 us
    pallas_call x2, Pallas kernels, call(): pl.pallas_call(blocks_kernel, grid=(last - first,), in_specs=[at_w(2, hel...  22 us
    all_to_all x1, blocking collectives, summed(): value = jnp.sum(lax.all_to_all(value, 'dp', 0, 0), axis=0)  10.9 us
    ppermute x3, starting transfers between devices, paired(): lax.ppermute(value, axis, [(source, source ^ step) for source in lines or...  10.3 us
    all_to_all x1, blocking collectives, summed(): lax.all_to_all(jnp.broadcast_to(value, (parts,) + value.shape), 'dp', 0, 0)  8.82 us
    ppermute x4, starting transfers between devices, swapped(): return lax.ppermute(value, 'ctx', [(s, s ^ 1) for s in range(count)])  7.68 us
    ppermute x4, waiting for transfers between devices, swapped(): return lax.ppermute(value, 'ctx', [(s, s ^ 1) for s in range(count)])  6.29 us
  transfers between devices with their start and end apart: 11, of which 7 were waited for; matrix products, arithmetic and copies ran while one was open for 4% of the time, Pallas kernels for 15%

profile of v5, /device:TPU:0, one launch (start us, length us, event | category | flops | bytes accessed | tf_op | source)
XLA Modules:
  0.0 147.1 jit_solution(7442973552629982096)
XLA Ops:
  0.6 0.0 copy-start
  0.6 0.0 copy-start.1
  0.7 1.3 fusion.8
  2.0 2.4 %collective-permute-start = (bf16[3,8,8192]{2,1,0:T(8,128)(2,1)S(1)}, bf16[3,8,8192]{2,1,0:T(8,128)(2,1)S(1)}, u32[]{:S(2)}, u32[]{:S(2)}) collective-permute-start(bf16[3,8,8192]{2,1,0:T(8,128)(2,1)S(1)} %get-tuple-element.55), channel_id=1, source_target_pairs={{0,1},{1,2},{2,3},{3,4},{4,5},{5,6},{6,7},{8,9},{9,10},{10,11},{11... | collective-permute-start | bytes 1179656 | tf_op jit(solution)/shard_map/ppermute | solution.py:236
  4.4 0.9 slice.50
  5.3 1.3 collective-permute-start.1
  6.6 0.8 negate_bitcast_fusion
  7.4 0.9 multiply_exponential_fusion
  8.3 0.0 copy-start.5
  8.3 0.8 fusion.7
  9.2 0.0 collective-permute-done.hb
  9.2 0.0 copy-start.2
  9.2 2.1 %collective-permute-done.1.ha = bf16[4,8,8192]{2,1,0:T(8,128)(2,1)S(1)} collective-permute-done((bf16[4,8,8192]{2,1,0:T(8,128)(2,1)S(1)}, bf16[4,8,8192]{2,1,0:T(8,128)(2,1)S(1)}, u32[]{:S(2)}, u32[]{:S(2)}) %collective-permute-start.1) | collective-permute-done | bytes 524320 | tf_op jit(solution)/shard_map/ppermute | solution.py:236
  11.3 0.0 copy-done.5
  11.3 0.0 copy-done
  11.3 0.0 copy-start.7
  11.3 0.0 copy-start.6
  11.3 0.0 copy-start.10
  11.4 22.7 %states.1 = (f32[3,136,8192]{2,1,0:T(8,128)}, f32[2,136,8192]{2,1,0:T(8,128)}, f32[16,8,8192]{2,1,0:T(8,128)}, f32[16,8,8192]{2,1,0:T(8,128)}, f32[2,16,16,512]{3,2,1,0:T(8,128)}) custom-call(bf16[3,128,8192]{2,1,0:T(8,128)(2,1)} %bitcast.87, bf16[3,8,8192]{2,1,0:T(8,128)(2,1)S(1)} %collective-permute-done.hb, ...), custom_call_target="tpu_custom_call" | custom-call | tf_op jit(solution)/shard_map/states/pallas_call | solution.py:362
  34.0 0.0 copy-start.9
  34.1 0.0 copy-start.4
  34.1 7.3 %collective-permute-start.2 = (f32[2,16,16,512]{3,2,1,0:T(8,128)}, f32[2,16,16,512]{3,2,1,0:T(8,128)S(1)}, u32[]{:S(2)}, u32[]{:S(2)}) collective-permute-start(f32[2,16,16,512]{3,2,1,0:T(8,128)} %get-tuple-element.30), channel_id=1, source_target_pairs={{0,1},{1,0},{2,3},{3,2},{4,5},{5,4},{6,7},{7,6},{8,9},{9,8},{10,11... | collective-permute-start | bytes 3145736 | tf_op jit(solution)/shard_map/ppermute | solution.py:241
  41.3 0.1 multiply_exponential_fusion.1
  41.4 0.0 copy-done.6
  41.5 0.2 multiply_reduce_fusion.near
  41.7 2.1 %collective-permute-done.2.other = f32[2,16,16,512]{3,2,1,0:T(8,128)S(1)} collective-permute-done((f32[2,16,16,512]{3,2,1,0:T(8,128)}, f32[2,16,16,512]{3,2,1,0:T(8,128)S(1)}, u32[]{:S(2)}, u32[]{:S(2)}) %collective-permute-start.2) | collective-permute-done | bytes 1048608 | tf_op jit(solution)/shard_map/ppermute | solution.py:241
  43.8 1.2 dynamic-slice_select_fusion.1
  45.0 0.1 broadcast_select_fusion.4
  45.1 1.7 %collective-permute-start.3 = (f32[8,16,512]{2,1,0:T(8,128)S(1)}, f32[8,16,512]{2,1,0:T(8,128)S(1)}, u32[]{:S(2)}, u32[]{:S(2)}) collective-permute-start(f32[8,16,512]{2,1,0:T(8,128)S(1)} %broadcast_select_fusion.4), channel_id=1, source_target_pairs={{0,2},{1,3},{2,0},{3,1},{4,6},{5,7},{6,4},{7,5},{8,10},{9,11},{10,... | collective-permute-start | bytes 786440 | tf_op jit(solution)/shard_map/ppermute | solution.py:257
  46.8 0.0 copy-done.8
  46.8 0.3 broadcast_select_fusion
  47.1 7.5 %blocks.2 = (f32[2,136,8192]{2,1,0:T(8,128)}, f32[16,8,8192]{2,1,0:T(8,128)}, f32[16,8,8192]{2,1,0:T(8,128)}) custom-call(f32[2,136,8192]{2,1,0:T(8,128)} %get-tuple-element.31.xg, f32[16,8,8192]{2,1,0:T(8,128)} %get-tuple-element.32.blocks_e, f32[16,8,8192]{2,1,0:T(8,128)} %get-tuple-element.33.blocks_a, ...), custom_call_target="tpu_custom_call", output_to_operand_aliasing={{0}: (0, {}), {1}: (1, {}), {2}: (2, {})} | custom-call | flops 62914560 | bytes 36700160 | tf_op jit(solution)/shard_map/blocks/pallas_call | solution.py:389
  54.6 0.0 collective-permute-done.3
  54.6 0.1 multiply_add_fusion.1
  54.8 0.0 copy-start.3
  54.8 1.4 collective-permute-start.5
  56.2 0.7 collective-permute-start.4
  56.9 14.5 %blocks.3 = (f32[2,136,8192]{2,1,0:T(8,128)}, f32[16,8,8192]{2,1,0:T(8,128)}, f32[16,8,8192]{2,1,0:T(8,128)}) custom-call(f32[2,136,8192]{2,1,0:T(8,128)} %get-tuple-element.39.xg, f32[16,8,8192]{2,1,0:T(8,128)} %get-tuple-element.40.blocks_e, f32[16,8,8192]{2,1,0:T(8,128)} %get-tuple-element.41.blocks_a, ...), custom_call_target="tpu_custom_call", output_to_operand_aliasing={{0}: (0, {}), {1}: (1, {}), {2}: (2, {})} | custom-call | flops 62914560 | bytes 36700160 | tf_op jit(solution)/shard_map/blocks/pallas_call | solution.py:389
  71.4 0.0 collective-permute-done.5
  71.4 0.0 collective-permute-done.4
  71.4 0.1 select_bitcast_fusion.1
  71.5 0.1 collective-permute-start.6
  71.7 1.1 fusion
  72.8 0.9 collective-permute-done.6.found
  73.7 33.4 %final.1 = (bf16[128,8192]{1,0:T(8,128)(2,1)}, bf16[3,128,8192]{2,1,0:T(8,128)(2,1)}, f32[16,24,512]{2,1,0:T(8,128)S(1)}) custom-call(s32[1]{0:T(128)} %bitcast.core, bf16[3,128,8192]{2,1,0:T(8,128)(2,1)} %bitcast.88, bf16[3,8,8192]{2,1,0:T(8,128)(2,1)S(1)} %copy-done.3, bf16[128,8192]{1,0:T(8,128)(2,1)} %bitcast.82, ...), custom_call_target="tpu_custom_call" | custom-call | tf_op jit(solution)/shard_map/final/pallas_call | solution.py:426
  107.0 0.2 collective-permute-start.7
  107.2 1.6 %collective-permute-done.7 = f32[8,24,512]{2,1,0:T(8,128)S(1)} collective-permute-done((f32[8,24,512]{2,1,0:T(8,128)S(1)}, f32[8,24,512]{2,1,0:T(8,128)S(1)}, u32[]{:S(2)}, u32[]{:S(2)}) %collective-permute-start.7) | collective-permute-done | bytes 393248 | tf_op jit(solution)/shard_map/ppermute | solution.py:241
  108.8 0.1 dynamic-slice_add_fusion
  108.9 10.9 %all_to_all.10 = f32[4,2,24,512]{3,2,1,0:T(8,128)S(1)} all-to-all(f32[4,2,24,512]{3,2,1,0:T(8,128)S(1)} %bitcast.91), channel_id=1, replica_groups=mesh['dp'=4,'ctx'=8] {'dp'}, dimensions={0} | all-to-all | bytes 786432 | tf_op jit(solution)/shard_map/all_to_all | solution.py:297
  119.9 5.4 %collective-permute-start.8 = (f32[2,24,512]{2,1,0:T(8,128)S(1)}, f32[2,24,512]{2,1,0:T(8,128)S(1)}, u32[]{:S(2)}, u32[]{:S(2)}) collective-permute-start(f32[2,24,512]{2,1,0:T(8,128)S(1)} %reduce_sum.19), channel_id=1, source_target_pairs={{0,2},{1,3},{2,0},{3,1},{4,6},{5,7},{6,4},{7,5},{8,10},{9,11},{10,... | collective-permute-start | bytes 294920 | tf_op jit(solution)/shard_map/ppermute | solution.py:257
  125.3 2.6 %collective-permute-done.8 = f32[2,24,512]{2,1,0:T(8,128)S(1)} collective-permute-done((f32[2,24,512]{2,1,0:T(8,128)S(1)}, f32[2,24,512]{2,1,0:T(8,128)S(1)}, u32[]{:S(2)}, u32[]{:S(2)}) %collective-permute-start.8) | collective-permute-done | bytes 98336 | tf_op jit(solution)/shard_map/ppermute | solution.py:257
  127.9 3.3 %collective-permute-start.9 = (f32[2,24,512]{2,1,0:T(8,128)S(1)}, f32[2,24,512]{2,1,0:T(8,128)S(1)}, u32[]{:S(2)}, u32[]{:S(2)}) collective-permute-start(f32[2,24,512]{2,1,0:T(8,128)S(1)} %add.37), channel_id=1, source_target_pairs={{0,4},{1,5},{2,6},{3,7},{4,0},{5,1},{6,2},{7,3},{8,12},{9,13},{10,... | collective-permute-start | bytes 294920 | tf_op jit(solution)/shard_map/ppermute | solution.py:257
  131.2 2.6 %collective-permute-done.9 = f32[2,24,512]{2,1,0:T(8,128)S(1)} collective-permute-done((f32[2,24,512]{2,1,0:T(8,128)S(1)}, f32[2,24,512]{2,1,0:T(8,128)S(1)}, u32[]{:S(2)}, u32[]{:S(2)}) %collective-permute-start.9) | collective-permute-done | bytes 98336 | tf_op jit(solution)/shard_map/ppermute | solution.py:257
  133.8 0.1 copy.27
  133.9 0.1 broadcast_in_dim.76
  134.0 8.8 %all_to_all.11 = f32[4,2,24,512]{3,1,2,0:T(2,128)S(1)} all-to-all(f32[4,2,24,512]{3,1,2,0:T(2,128)S(1)} %broadcast_in_dim.76), channel_id=1, replica_groups=mesh['dp'=4,'ctx'=8] {'dp'}, dimensions={0} | all-to-all | bytes 786432 | tf_op jit(solution)/shard_map/all_to_all | solution.py:302
  142.8 0.1 copy.28
  142.9 0.1 collective-permute-start.10
  143.0 1.7 %collective-permute-done.10 = f32[8,24,512]{2,1,0:T(8,128)S(1)} collective-permute-done((f32[8,24,512]{2,1,0:T(8,128)S(1)}, f32[8,24,512]{2,1,0:T(8,128)S(1)}, u32[]{:S(2)}, u32[]{:S(2)}) %collective-permute-start.10) | collective-permute-done | bytes 393248 | tf_op jit(solution)/shard_map/ppermute | solution.py:241
  144.7 0.1 broadcast_select_fusion.3
  144.8 0.1 maximum_bitcast_fusion
  144.8 0.6 slice.76
  145.5 0.4 copy.29
  145.9 1.2 reshape.36
  (18 shorter events, 0.3 us)
Async XLA Ops:
  0.6 10.7 %copy-start = (bf16[1,128,8192]{2,1,0:T(8,128)(2,1)S(1)}, bf16[1,128,8192]{2,1,0:T(8,128)(2,1)}, u32[]{:S(2)}) copy-start(bf16[1,128,8192]{2,1,0:T(8,128)(2,1)} %param.16) | copy-start | bytes 6291460
  0.6 10.7 %copy-start.1 = (f32[3,7,8192]{2,1,0:T(8,128)S(1)}, f32[3,7,8192]{2,1,0:T(8,128)}, u32[]{:S(2)}) copy-start(f32[3,7,8192]{2,1,0:T(8,128)} %filt.3) | copy-start | bytes 2064388
  2.0 7.2 %collective-permute-start = (bf16[3,8,8192]{2,1,0:T(8,128)(2,1)S(1)}, bf16[3,8,8192]{2,1,0:T(8,128)(2,1)S(1)}, u32[]{:S(2)}, u32[]{:S(2)}) collective-permute-start(bf16[3,8,8192]{2,1,0:T(8,128)(2,1)S(1)} %get-tuple-element.55), channel_id=1, source_target_pairs={{0,1},{1,2},{2,3},{3,4},{4,5},{5,6},{6,7},{8,9},{9,10},{10,11},{11... | collective-permute-start | bytes 1179656 | tf_op jit(solution)/shard_map/ppermute | solution.py:236
  5.3 6.0 %collective-permute-start.1 = (bf16[4,8,8192]{2,1,0:T(8,128)(2,1)S(1)}, bf16[4,8,8192]{2,1,0:T(8,128)(2,1)S(1)}, u32[]{:S(2)}, u32[]{:S(2)}) collective-permute-start(bf16[4,8,8192]{2,1,0:T(8,128)(2,1)S(1)} %pad_maximum_fusion), channel_id=1, source_target_pairs={{1,0},{2,1},{3,2},{4,3},{5,4},{6,5},{7,6},{9,8},{10,9},{11,10},{12... | collective-permute-start | bytes 1572872 | tf_op jit(solution)/shard_map/ppermute | solution.py:236
  8.3 3.0 %copy-start.5 = (f32[4,16,8,512]{3,2,1,0:T(8,128)}, f32[4,16,8,512]{3,2,1,0:T(8,128)S(1)}, u32[]{:S(2)}) copy-start(f32[4,16,8,512]{3,2,1,0:T(8,128)S(1)} %multiply_exponential_fusion) | copy-start | bytes 3145732
  9.2 24.9 %copy-start.2 = (bf16[3,8,8192]{2,1,0:T(8,128)(2,1)}, bf16[3,8,8192]{2,1,0:T(8,128)(2,1)S(1)}, u32[]{:S(2)}) copy-start(bf16[3,8,8192]{2,1,0:T(8,128)(2,1)S(1)} %collective-permute-done.hb) | copy-start | bytes 1179652
  11.3 30.0 %copy-start.7 = (f32[4]{0:T(128)S(1)}, f32[4]{0:T(128)}, u32[]{:S(2)}) copy-start(f32[4]{0:T(128)} %constant.50) | copy-start | bytes 52
  11.3 30.1 %copy-start.6 = (f32[512,16]{0,1:T(8,128)S(1)}, f32[512,16]{0,1:T(8,128)}, u32[]{:S(2)}) copy-start(f32[512,16]{0,1:T(8,128)} %param.13) | copy-start | bytes 98308
  11.3 30.1 %copy-start.10 = (f32[24]{0:T(128)S(1)}, f32[24]{0:T(128)}, u32[]{:S(2)}) copy-start(f32[24]{0:T(128)} %constant.48) | copy-start | bytes 292
  34.0 12.7 %copy-start.8 = (pred[4,8]{1,0:T(4,128)(4,1)S(1)}, pred[4,8]{1,0:T(4,128)(4,1)}, u32[]{:S(2)}) copy-start(pred[4,8]{1,0:T(4,128)(4,1)} %constant.51) | copy-start | bytes 100
  34.0 12.7 %copy-start.9 = (pred[4,8]{1,0:T(4,128)(4,1)S(1)}, pred[4,8]{1,0:T(4,128)(4,1)}, u32[]{:S(2)}) copy-start(pred[4,8]{1,0:T(4,128)(4,1)} %constant.49) | copy-start | bytes 100
  34.1 13.0 %copy-start.4 = (f32[8192]{0:T(1024)S(1)}, f32[8192]{0:T(1024)}, u32[]{:S(2)}) copy-start(f32[8192]{0:T(1024)} %param.15) | copy-start | bytes 98308
  34.1 9.8 %collective-permute-start.2 = (f32[2,16,16,512]{3,2,1,0:T(8,128)}, f32[2,16,16,512]{3,2,1,0:T(8,128)S(1)}, u32[]{:S(2)}, u32[]{:S(2)}) collective-permute-start(f32[2,16,16,512]{3,2,1,0:T(8,128)} %get-tuple-element.30), channel_id=1, source_target_pairs={{0,1},{1,0},{2,3},{3,2},{4,5},{5,4},{6,7},{7,6},{8,9},{9,8},{10,11... | collective-permute-start | bytes 3145736 | tf_op jit(solution)/shard_map/ppermute | solution.py:241
  45.1 9.5 %collective-permute-start.3 = (f32[8,16,512]{2,1,0:T(8,128)S(1)}, f32[8,16,512]{2,1,0:T(8,128)S(1)}, u32[]{:S(2)}, u32[]{:S(2)}) collective-permute-start(f32[8,16,512]{2,1,0:T(8,128)S(1)} %broadcast_select_fusion.4), channel_id=1, source_target_pairs={{0,2},{1,3},{2,0},{3,1},{4,6},{5,7},{6,4},{7,5},{8,10},{9,11},{10,... | collective-permute-start | bytes 786440 | tf_op jit(solution)/shard_map/ppermute | solution.py:257
  54.8 18.9 %copy-start.3 = (bf16[3,8,8192]{2,1,0:T(8,128)(2,1)S(1)}, bf16[3,8,8192]{2,1,0:T(8,128)(2,1)}, u32[]{:S(2)}) copy-start(bf16[3,8,8192]{2,1,0:T(8,128)(2,1)} %copy-done.2) | copy-start | bytes 1179652
  54.8 16.6 %collective-permute-start.5 = (f32[8,16,512]{2,1,0:T(8,128)S(1)}, f32[8,16,512]{2,1,0:T(8,128)S(1)}, u32[]{:S(2)}, u32[]{:S(2)}) collective-permute-start(f32[8,16,512]{2,1,0:T(8,128)S(1)} %multiply_add_fusion.1), channel_id=1, source_target_pairs={{2,6},{3,7},{4,0},{5,1},{10,14},{11,15},{12,8},{13,9},{18,22},{19,... | collective-permute-start | bytes 786440 | tf_op jit(solution)/shard_map/ppermute | solution.py:271
  56.2 15.2 %collective-permute-start.4 = (f32[8,16,512]{2,1,0:T(8,128)S(1)}, f32[8,16,512]{2,1,0:T(8,128)S(1)}, u32[]{:S(2)}, u32[]{:S(2)}) collective-permute-start(f32[8,16,512]{2,1,0:T(8,128)S(1)} %multiply_add_fusion.1), channel_id=1, source_target_pairs={{2,4},{3,5},{4,2},{5,3},{10,12},{11,13},{12,10},{13,11},{18,20},{1... | collective-permute-start | bytes 786440 | tf_op jit(solution)/shard_map/ppermute | solution.py:270
  71.5 2.1 %collective-permute-start.6 = (f32[2,8,16,512]{3,2,1,0:T(8,128)S(1)}, f32[2,8,16,512]{3,2,1,0:T(8,128)}, u32[]{:S(2)}, u32[]{:S(2)}) collective-permute-start(f32[2,8,16,512]{3,2,1,0:T(8,128)S(1)} %pad_maximum_fusion.1.both), channel_id=1, source_target_pairs={{0,1},{1,0},{2,3},{3,2},{4,5},{5,4},{6,7},{7,6},{8,9},{9,8},{10,11... | collective-permute-start | bytes 1572872 | tf_op jit(solution)/shard_map/ppermute | solution.py:241
  107.0 1.8 %collective-permute-start.7 = (f32[8,24,512]{2,1,0:T(8,128)S(1)}, f32[8,24,512]{2,1,0:T(8,128)S(1)}, u32[]{:S(2)}, u32[]{:S(2)}) collective-permute-start(f32[8,24,512]{2,1,0:T(8,128)S(1)} %constant_dynamic-slice_fusion), channel_id=1, source_target_pairs={{0,1},{1,0},{2,3},{3,2},{4,5},{5,4},{6,7},{7,6},{8,9},{9,8},{10,11... | collective-permute-start | bytes 1179656 | tf_op jit(solution)/shard_map/ppermute | solution.py:241
  119.9 8.0 %collective-permute-start.8 = (f32[2,24,512]{2,1,0:T(8,128)S(1)}, f32[2,24,512]{2,1,0:T(8,128)S(1)}, u32[]{:S(2)}, u32[]{:S(2)}) collective-permute-start(f32[2,24,512]{2,1,0:T(8,128)S(1)} %reduce_sum.19), channel_id=1, source_target_pairs={{0,2},{1,3},{2,0},{3,1},{4,6},{5,7},{6,4},{7,5},{8,10},{9,11},{10,... | collective-permute-start | bytes 294920 | tf_op jit(solution)/shard_map/ppermute | solution.py:257
  127.9 5.9 %collective-permute-start.9 = (f32[2,24,512]{2,1,0:T(8,128)S(1)}, f32[2,24,512]{2,1,0:T(8,128)S(1)}, u32[]{:S(2)}, u32[]{:S(2)}) collective-permute-start(f32[2,24,512]{2,1,0:T(8,128)S(1)} %add.37), channel_id=1, source_target_pairs={{0,4},{1,5},{2,6},{3,7},{4,0},{5,1},{6,2},{7,3},{8,12},{9,13},{10,... | collective-permute-start | bytes 294920 | tf_op jit(solution)/shard_map/ppermute | solution.py:257
  142.9 1.8 %collective-permute-start.10 = (f32[8,24,512]{2,1,0:T(8,128)S(1)}, f32[8,24,512]{2,1,0:T(8,128)S(1)}, u32[]{:S(2)}, u32[]{:S(2)}) collective-permute-start(f32[8,24,512]{2,1,0:T(8,128)S(1)} %bitcast.90), channel_id=1, source_target_pairs={{0,1},{1,0},{2,3},{3,2},{4,5},{5,4},{6,7},{7,6},{8,9},{9,8},{10,11... | collective-permute-start | bytes 1179656 | tf_op jit(solution)/shard_map/ppermute | solution.py:241

commit v6 on v5

--- a/solution.py
+++ b/solution.py
@@ -46,13 +46,14 @@
     return values[0]
 
 
-def states_kernel(p, hb, ha, u, filt, f1, we, wb, qkv, xg, blocks_e, blocks_a, ends, xs):
+def states_kernel(core, p, hx, hi, u, filt, f1, we, wb, qkv, xg, blocks_e, blocks_a, ends, xs):
     rows = p.shape[1]
     run = (rows + SUB) // SUB
     taps = filt.shape[1]
     poles, groups = f1.shape
     own = rows - run * (SUB - 1)
     tiles = groups // LANES
+    first = core[0] == 0
 
     def tile(lt, carry):
         lanes = pl.ds(pl.multiple_of(lt * LANES, LANES), LANES)
@@ -60,11 +61,13 @@
         which = lt // tiles
         inside = lax.broadcasted_iota(jnp.int32, (SUB, LANES), 0) < SUB - 1
         for j in range(3):
-            xs[j, 0:SUB] = hb[j, :, lanes].astype(F32)
+            across, within = hx[j, :, lanes].astype(F32), hi[j, :, lanes].astype(F32)
+            xs[j, 0:SUB] = jnp.where(first, across, within)
             xs[j, SUB : SUB + rows] = p[j, :, lanes].astype(F32)
-            xs[j, SUB + rows :] = ha[j, :, lanes].astype(F32)
+            xs[j, SUB + rows :] = jnp.where(first, within, across)
         xs[3, SUB : SUB + rows] = u[:, lanes].astype(F32)
-        xs[3, SUB + rows :] = ha[3, :, lanes].astype(F32)
+        across, within = hx[3, :, lanes].astype(F32), hi[3, :, lanes].astype(F32)
+        xs[3, SUB + rows :] = jnp.where(first, within, across)
 
         def mixed(j):
             tap = [spread(filt[j, i : i + 1, lanes]) for i in range(taps)]
@@ -146,7 +149,7 @@
 
 
 def final_kernel(
-    core, p, hb, u, ha, qkv, conv, from_e, from_a, both, found, other, filt, f1, f_all, cz, cy,
+    core, p, hx, hi, u, qkv, conv, from_e, from_a, both, found, other, filt, f1, f_all, cz, cy,
     output, grad_p, sums, ps, us, gs, os, es,
 ):
     rows = p.shape[1]
@@ -158,22 +161,27 @@
     first = core[0] == 0
     halves = pl.num_programs(0) // 2
     kept = (pl.program_id(0) < halves) == first
+    cut = sums.shape[2] // LANES
 
     def tile(lt, carry):
         lanes = pl.ds(pl.multiple_of(lt * LANES, LANES), LANES)
         part = pl.ds(pl.multiple_of(lax.rem(lt, tiles) * LANES, LANES), LANES)
         which = lt // tiles
+        piece = lt // cut
+        spot = pl.ds(pl.multiple_of(lax.rem(lt, cut) * LANES, LANES), LANES)
         inside = lax.broadcasted_iota(jnp.int32, (SUB, LANES), 0) < SUB - 1
         for side in range(2):
             far = jnp.where(kept, both[side, which, :, part], found[side, which, :, part])
             close = other[side, which, :, part] + f_all[:, part] * far
             es[side] = jnp.where(first == (side == 0), far, close)
         for j in range(3):
-            ps[j, 0:SUB] = hb[j, :, lanes].astype(F32)
+            across, within = hx[j, :, lanes].astype(F32), hi[j, :, lanes].astype(F32)
+            ps[j, 0:SUB] = jnp.where(first, across, within)
             ps[j, SUB : SUB + rows] = p[j, :, lanes].astype(F32)
-            ps[j, SUB + rows :] = ha[j, :, lanes].astype(F32)
+            ps[j, SUB + rows :] = jnp.where(first, within, across)
         us[0:rows] = u[:, lanes].astype(F32)
-        us[rows:] = ha[3, :, lanes].astype(F32)
+        across, within = hx[3, :, lanes].astype(F32), hi[3, :, lanes].astype(F32)
+        us[rows:] = jnp.where(first, within, across)
         decay = [spread(f1[n : n + 1, part]) for n in range(poles)]
 
         state = [
@@ -224,7 +232,7 @@
             rest = rest + sums_of
         rest = rest + [skip_sum] + [jnp.zeros((SUB, LANES), F32)] * (-(len(rest) + 1) % SUB)
         for n in range(0, len(rest), SUB):
-            sums[which, n : n + SUB, part] = folded(rest[n : n + SUB])
+            sums[piece, n : n + SUB, spot] = folded(rest[n : n + SUB])
         return carry
 
     lax.fori_loop(0, p.shape[2] // LANES, tile, 0)
@@ -287,22 +295,22 @@
 
 
 def summed(value):
-    parts = lax.axis_size("dp")
-    side = lax.rem(lax.axis_index("ctx"), 2)
+    devices = lax.axis_size("ctx")
+    total = lax.axis_size("dp") * devices
+    sides = [[k for k in range(total) if k % 2 == side] for side in range(2)]
+    parts = total // 2
+    low = lax.rem(lax.axis_index("ctx"), 2) == 0
     half = value.shape[0] // 2
-    keep = lax.dynamic_slice_in_dim(value, side * half, half, 0)
-    give = lax.dynamic_slice_in_dim(value, (1 - side) * half, half, 0)
-    value = keep + swapped(give)
-    value = value.reshape((parts, half // parts) + value.shape[1:])
-    value = jnp.sum(lax.all_to_all(value, "dp", 0, 0), axis=0)
-    reach = 2
-    while reach < lax.axis_size("ctx"):
-        value = value + paired(value, "ctx", reach)
-        reach = 2 * reach
-    value = lax.all_to_all(jnp.broadcast_to(value, (parts,) + value.shape), "dp", 0, 0)
-    value = value.reshape((half,) + value.shape[2:])
+    left, right = value[:half], value[half:]
+    value = jnp.where(low, left, right) + swapped(jnp.where(low, right, left))
+    shape = value.shape
+
+    def dealt(value):
+        return lax.all_to_all(value, ("dp", "ctx"), 0, 0, axis_index_groups=sides)
+
+    value = jnp.sum(dealt(value.reshape(parts, shape[1] * half // parts, shape[2])), axis=0)
+    value = dealt(jnp.broadcast_to(value, (parts,) + value.shape)).reshape(shape)
     other = swapped(value)
-    low = side == 0
     return jnp.concatenate([jnp.where(low, value, other), jnp.where(low, other, value)], axis=0)
 
 
@@ -316,8 +324,14 @@
     held = rows + SUB
     p = projected[0].transpose(1, 0, 2)
     u = cotangent[0]
-    hb = shifted(p[:, rows - SUB :], "ctx", 1)
-    ha = shifted(jnp.concatenate([p[:, :SUB], u[None, :SUB]], axis=0), "ctx", -1)
+    core = lax.rem(lax.axis_index("ctx"), 2)
+    head = jnp.concatenate([p[:, :SUB], u[None, :SUB]], axis=0)
+    tail = jnp.concatenate([p[:, rows - SUB :], u[None, rows - SUB :]], axis=0)
+    devices = lax.axis_size("ctx")
+    across = [(k, k + 1) for k in range(1, devices - 1, 2)]
+    across = across + [(target, source) for source, target in across]
+    hx = lax.ppermute(jnp.where(core == 0, head, tail), "ctx", across)
+    hi = swapped(jnp.where(core == 0, tail, head))
 
     rate = decay_rates.T
     weight = residues.T
@@ -344,9 +358,6 @@
         axis = len(shape)
         return pl.BlockSpec(shape + (each * groups,), lambda w: (0,) * axis + (w,))
 
-    def per_w(*shape):
-        return pl.BlockSpec((each,) + shape, lambda w: (w,) + (0,) * len(shape))
-
     def fixed(value):
         return pl.BlockSpec(
             value.shape, lambda w: (0,) * value.ndim, pipeline_mode=pl.Buffered(1)
@@ -363,7 +374,8 @@
         states_kernel,
         grid=(width // each,),
         in_specs=[
-            by_w(3, rows), by_w(3, SUB), by_w(4, SUB), by_w(rows), by_w(3, taps),
+            pl.BlockSpec(memory_space=pltpu.SMEM),
+            by_w(3, rows), by_w(4, SUB), by_w(4, SUB), by_w(rows), by_w(3, taps),
             fixed(f1), fixed(we), fixed(wb),
         ],
         out_specs=[
@@ -377,12 +389,14 @@
         scratch_shapes=[pltpu.VMEM((4, held + SUB, LANES), F32)],
         compiler_params=params,
         name="states",
-    )(p, hb, ha, u, short_filter, f1, we, wb)
+    )(core[None], p, hx, hi, u, short_filter, f1, we, wb)
+
+    many = 2 if width % 2 == 0 else 1
 
     def blocks(first, last):
         def at_w(*shape):
             axis = len(shape)
-            return pl.BlockSpec(shape + (each * groups,), lambda w: (0,) * axis + (w + first,))
+            return pl.BlockSpec(shape + (many * groups,), lambda w: (0,) * axis + (w + first,))
 
         def call(sent, kept):
             close, _ = lax.optimization_barrier((near, sent))
@@ -405,7 +419,7 @@
 
         return call
 
-    steps = width // each
+    steps = width // many
     cut = (steps + 1) // 3
     other, chip_e, chip_a = joined(ends, f_all)
     before, after, (conv, from_e, from_a) = scanned(
@@ -413,9 +427,9 @@
     )
     both = jnp.stack([before, after])
     found = swapped(both)
-    core = lax.rem(lax.axis_index("ctx"), 2)
 
     count = 3 * taps + 3
+    split = 2 if groups % (2 * LANES) == 0 else 1
     scratch = [
         pltpu.VMEM((3, held + SUB, LANES), F32),
         pltpu.VMEM((held, LANES), F32),
@@ -428,21 +442,24 @@
         grid=(width // each,),
         in_specs=[
             pl.BlockSpec(memory_space=pltpu.SMEM),
-            by_w(3, rows), by_w(3, SUB), by_w(rows), by_w(4, SUB), by_w(3, held), by_w(2, held),
+            by_w(3, rows), by_w(4, SUB), by_w(4, SUB), by_w(rows), by_w(3, held), by_w(2, held),
             by_w(poles, SUB), by_w(poles, SUB), halved, halved, ends_spec,
             by_w(3, taps), fixed(f1), fixed(f_all), fixed(cz), fixed(cy),
         ],
-        out_specs=[by_w(rows), by_w(3, rows), per_w(count, groups)],
+        out_specs=[
+            by_w(rows), by_w(3, rows),
+            pl.BlockSpec((each * split, count, groups // split), lambda w: (w, 0, 0)),
+        ],
         out_shape=[
             shape_of((rows, channels), BF16),
             shape_of((3, rows, channels), BF16),
-            shape_of((width, count, groups), F32),
+            shape_of((width * split, count, groups // split), F32),
         ],
         scratch_shapes=scratch,
         compiler_params=params,
         name="final",
     )(
-        core[None], p, hb, u, ha, qkv, conv, from_e, from_a, both, found, other, short_filter,
+        core[None], p, hx, hi, u, qkv, conv, from_e, from_a, both, found, other, short_filter,
         f1, f_all, cz, cy,
     )
 

time: 148 us -> 148 us (level)
  blocking collectives: 19.8 us -> 38.9 us
  starting transfers between devices: 23.8 us -> 15.4 us
  waiting for transfers between devices: 13.6 us -> 6.2 us
  Pallas kernels: 78.1 us -> 76 us
  other arithmetic: 6.01 us -> 4.34 us
    all_to_all x2, blocking collectives: 19.8 us -> 38.9 us  [dealt(): return lax.all_to_all(value, ('dp', 'ctx'), 0, 0, axis_index_groups=sides)]
    ppermute x3 -> x1, starting transfers between devices: 10.3 us -> 2.18 us  [paired(): lax.ppermute(value, axis, [(source, source ^ step) for source in lines or...]
    ppermute x3 -> x1, waiting for transfers between devices: 5.2 us -> 0.01 us  [paired(): lax.ppermute(value, axis, [(source, source ^ step) for source in lines or...]
    ppermute x2 -> x1, starting transfers between devices: 3.67 us -> 0.68 us  [local(): hx = lax.ppermute(jnp.where(core == 0, head, tail), 'ctx', across)]
    ppermute x4 -> x5, starting transfers between devices: 7.68 us -> 10.4 us  [swapped(): return lax.ppermute(value, 'ctx', [(s, s ^ 1) for s in range(count)])]
    pallas_call x2, Pallas kernels: 22 us -> 19.8 us  [call(): pl.pallas_call(blocks_kernel, grid=(last - first,), in_specs=[at_w(2, hel...]
    ppermute x2 -> x1, waiting for transfers between devices: 2.13 us -> 0.01 us  [local(): hx = lax.ppermute(jnp.where(core == 0, head, tail), 'ctx', across)]
    ppermute x4 -> x5, waiting for transfers between devices: 6.29 us -> 6.19 us  [swapped(): return lax.ppermute(value, 'ctx', [(s, s ^ 1) for s in range(count)])]
  transfers between devices with their start and end apart: 11 -> 9, of which waited for: 7 -> 5; matrix products, arithmetic and copies ran while one was open for 4% -> 2% of each run, Pallas kernels for 15% -> 14%
where the time goes in v6:
time: 148 us; the launch traced here: 147 us
  Pallas kernels  76 us (51%)
  blocking collectives  38.9 us (26%)
  starting transfers between devices  15.4 us (10%)
  waiting for transfers between devices  6.2 us (4%)
  local copies, waits for them, and re-layouts  4.85 us (3%)
  other arithmetic  4.34 us (3%)
    all_to_all x2, blocking collectives, dealt(): return lax.all_to_all(value, ('dp', 'ctx'), 0, 0, axis_index_groups=sides)  38.9 us
    pallas_call x1, Pallas kernels, local(): pl.pallas_call(final_kernel, grid=(width // each,), in_specs=[pl.BlockSpe...  33.3 us
    pallas_call x1, Pallas kernels, local(): pl.pallas_call(states_kernel, grid=(width // each,), in_specs=[pl.BlockSp...  22.9 us
    pallas_call x2, Pallas kernels, call(): pl.pallas_call(blocks_kernel, grid=(last - first,), in_specs=[at_w(2, hel...  19.8 us
    ppermute x5, starting transfers between devices, swapped(): return lax.ppermute(value, 'ctx', [(s, s ^ 1) for s in range(count)])  10.4 us
    ppermute x5, waiting for transfers between devices, swapped(): return lax.ppermute(value, 'ctx', [(s, s ^ 1) for s in range(count)])  6.19 us
  transfers between devices with their start and end apart: 9, of which 5 were waited for; matrix products, arithmetic and copies ran while one was open for 2% of the time, Pallas kernels for 14%

profile of v6, /device:TPU:0, one launch (start us, length us, event | category | flops | bytes accessed | tf_op | source)
XLA Modules:
  0.0 146.6 jit_solution(4472381662849752531)
XLA Ops:
  0.6 0.0 copy-start.10
  0.6 0.0 copy-start
  0.7 0.0 copy-start.8
  0.7 0.0 copy-start.1
  0.7 0.0 copy-start.9
  0.7 1.1 fusion.9
  1.8 1.2 fusion.8
  3.0 0.1 broadcast_select_fusion.2
  3.1 0.5 collective-permute-start.1
  3.6 0.7 collective-permute-start
  4.3 0.0 copy-done.8
  4.4 0.0 copy-done.9
  4.4 0.0 copy-done.10
  4.4 0.2 multiply_exponential_fusion
  4.6 0.0 copy-start.5
  4.7 0.5 collective-permute-done.1.hi
  5.2 0.0 collective-permute-done.hx
  5.2 0.4 copy-done.5
  5.6 0.0 copy-done
  5.6 0.0 copy-done.1
  5.6 0.0 copy-start.14
  5.6 22.9 %states.1 = (f32[3,136,8192]{2,1,0:T(8,128)}, f32[2,136,8192]{2,1,0:T(8,128)}, f32[16,8,8192]{2,1,0:T(8,128)}, f32[16,8,8192]{2,1,0:T(8,128)}, f32[2,16,16,512]{3,2,1,0:T(8,128)}) custom-call(s32[1]{0:T(128)} %bitcast.core, bf16[3,128,8192]{2,1,0:T(8,128)(2,1)} %bitcast.83, bf16[4,8,8192]{2,1,0:T(8,128)(2,1)S(1)} %collective-permute-done.hx, ...), custom_call_target="tpu_custom_call" | custom-call | tf_op jit(solution)/shard_map/states/pallas_call | solution.py:373
  28.5 0.0 copy-done.2
  28.5 0.0 copy-start.13
  28.5 0.0 copy-start.4
  28.6 9.6 %collective-permute-start.2 = (f32[2,16,16,512]{3,2,1,0:T(8,128)}, f32[2,16,16,512]{3,2,1,0:T(8,128)S(1)}, u32[]{:S(2)}, u32[]{:S(2)}) collective-permute-start(f32[2,16,16,512]{3,2,1,0:T(8,128)} %get-tuple-element.30), channel_id=1, source_target_pairs={{0,1},{1,0},{2,3},{3,2},{4,5},{5,4},{6,7},{7,6},{8,9},{9,8},{10,11... | collective-permute-start | bytes 3145736 | tf_op jit(solution)/shard_map/ppermute | solution.py:249
  38.1 0.1 multiply_exponential_fusion.1
  38.3 0.8 slice_multiply_fusion
  39.1 1.0 multiply_reduce_fusion.near
  40.0 0.6 collective-permute-done.2.other
  40.6 1.2 dynamic-slice_select_fusion.1
  41.8 0.1 broadcast_select_fusion.6
  41.9 2.2 %collective-permute-start.3 = (f32[8,16,512]{2,1,0:T(8,128)S(1)}, f32[8,16,512]{2,1,0:T(8,128)S(1)}, u32[]{:S(2)}, u32[]{:S(2)}) collective-permute-start(f32[8,16,512]{2,1,0:T(8,128)S(1)} %broadcast_select_fusion.6), channel_id=1, source_target_pairs={{0,2},{1,3},{2,0},{3,1},{4,6},{5,7},{6,4},{7,5},{8,10},{9,11},{10,... | collective-permute-start | bytes 786440 | tf_op jit(solution)/shard_map/ppermute | solution.py:265
  44.1 0.0 copy-done.13
  44.1 0.3 broadcast_select_fusion
  44.4 8.0 %blocks.2 = (f32[2,136,8192]{2,1,0:T(8,128)}, f32[16,8,8192]{2,1,0:T(8,128)}, f32[16,8,8192]{2,1,0:T(8,128)}) custom-call(f32[2,136,8192]{2,1,0:T(8,128)} %get-tuple-element.31.xg, f32[16,8,8192]{2,1,0:T(8,128)} %get-tuple-element.32.blocks_e, f32[16,8,8192]{2,1,0:T(8,128)} %get-tuple-element.33.blocks_a, ...), custom_call_target="tpu_custom_call", output_to_operand_aliasing={{0}: (0, {}), {1}: (1, {}), {2}: (2, {})} | custom-call | flops 62914560 | bytes 36700160 | tf_op jit(solution)/shard_map/blocks/pallas_call | solution.py:403
  52.5 0.0 collective-permute-done.3
  52.5 0.1 multiply_add_fusion.1
  52.6 0.0 copy-start.6
  52.6 0.0 copy-start.7
  52.6 0.0 copy-start.3
  52.6 1.4 collective-permute-start.5
  54.1 0.7 collective-permute-start.4
  54.8 11.8 %blocks.3 = (f32[2,136,8192]{2,1,0:T(8,128)}, f32[16,8,8192]{2,1,0:T(8,128)}, f32[16,8,8192]{2,1,0:T(8,128)}) custom-call(f32[2,136,8192]{2,1,0:T(8,128)} %get-tuple-element.39.xg, f32[16,8,8192]{2,1,0:T(8,128)} %get-tuple-element.40.blocks_e, f32[16,8,8192]{2,1,0:T(8,128)} %get-tuple-element.41.blocks_a, ...), custom_call_target="tpu_custom_call", output_to_operand_aliasing={{0}: (0, {}), {1}: (1, {}), {2}: (2, {})} | custom-call | flops 62914560 | bytes 36700160 | tf_op jit(solution)/shard_map/blocks/pallas_call | solution.py:403
  66.5 0.0 collective-permute-done.5
  66.6 0.0 collective-permute-done.4
  66.6 0.1 select_bitcast_fusion.1
  66.7 0.1 collective-permute-start.6
  66.8 0.1 fusion
  66.9 1.8 %collective-permute-done.6.found = f32[2,8,16,512]{3,2,1,0:T(8,128)S(1)} collective-permute-done((f32[2,8,16,512]{3,2,1,0:T(8,128)S(1)}, f32[2,8,16,512]{3,2,1,0:T(8,128)S(1)}, u32[]{:S(2)}, u32[]{:S(2)}) %collective-permute-start.6) | collective-permute-done | bytes 524320 | tf_op jit(solution)/shard_map/ppermute | solution.py:249
  68.7 33.3 %final.1 = (bf16[128,8192]{1,0:T(8,128)(2,1)}, bf16[3,128,8192]{2,1,0:T(8,128)(2,1)}, f32[32,24,256]{2,1,0:T(8,128)S(1)}) custom-call(s32[1]{0:T(128)} %bitcast.core, bf16[3,128,8192]{2,1,0:T(8,128)(2,1)} %bitcast.84, bf16[4,8,8192]{2,1,0:T(8,128)(2,1)S(1)} %copy-done.3, bf16[4,8,8192]{2,1,0:T(8,128)(2,1)S(1)} %collective-permute-done.1.hi, ...), custom_call_target="tpu_custom_call" | custom-call | tf_op jit(solution)/shard_map/final/pallas_call | solution.py:440
  101.9 0.1 slice_select_fusion
  102.0 0.2 collective-permute-start.7
  102.2 1.6 %collective-permute-done.7 = f32[16,24,256]{2,1,0:T(8,128)S(1)} collective-permute-done((f32[16,24,256]{2,1,0:T(8,128)S(1)}, f32[16,24,256]{2,1,0:T(8,128)S(1)}, u32[]{:S(2)}, u32[]{:S(2)}) %collective-permute-start.7) | collective-permute-done | bytes 393248 | tf_op jit(solution)/shard_map/ppermute | solution.py:249
  103.8 0.1 select_add_fusion
  103.9 23.1 %all_to_all.10 = f32[16,24,256]{2,1,0:T(8,128)S(1)} all-to-all(f32[16,24,256]{2,1,0:T(8,128)S(1)} %select_add_fusion), channel_id=1, replica_groups={{0,2,4,6,8,10,12,14,16,18,20,22,24,26,28,30},{1,3,5,7,9,11,13,15,17,19,..., dimensions={0} | all-to-all | bytes 786432 | tf_op jit(solution)/shard_map/all_to_all | solution.py:309
  127.0 15.7 %all_to_all.11 = f32[16,24,256]{2,1,0:T(8,128)S(1)} all-to-all(f32[16,24,256]{2,1,0:T(8,128)S(1)} %broadcast_in_dim.78), channel_id=1, replica_groups={{0,2,4,6,8,10,12,14,16,18,20,22,24,26,28,30},{1,3,5,7,9,11,13,15,17,19,..., dimensions={0} | all-to-all | bytes 786432 | tf_op jit(solution)/shard_map/all_to_all | solution.py:309
  142.8 0.0 collective-permute-start.8
  142.8 1.7 %collective-permute-done.8 = f32[16,24,256]{2,1,0:T(8,128)S(1)} collective-permute-done((f32[16,24,256]{2,1,0:T(8,128)S(1)}, f32[16,24,256]{2,1,0:T(8,128)S(1)}, u32[]{:S(2)}, u32[]{:S(2)}) %collective-permute-start.8) | collective-permute-done | bytes 393248 | tf_op jit(solution)/shard_map/ppermute | solution.py:249
  144.5 0.1 broadcast_select_fusion.5
  144.6 0.1 maximum_bitcast_fusion
  144.6 0.6 slice.89
  145.3 0.2 copy.22
  145.5 1.1 reshape.30
  (18 shorter events, 0.2 us)
Async XLA Ops:
  0.6 3.8 %copy-start.10 = (f32[4,8]{1,0:T(4,128)S(1)}, f32[4,8]{1,0:T(4,128)}, u32[]{:S(2)}) copy-start(f32[4,8]{1,0:T(4,128)} %constant.47) | copy-start | bytes 388
  0.6 5.0 %copy-start = (bf16[1,128,8192]{2,1,0:T(8,128)(2,1)S(1)}, bf16[1,128,8192]{2,1,0:T(8,128)(2,1)}, u32[]{:S(2)}) copy-start(bf16[1,128,8192]{2,1,0:T(8,128)(2,1)} %param.16) | copy-start | bytes 6291460
  0.7 3.7 %copy-start.8 = (f32[512,16]{0,1:T(8,128)S(1)}, f32[512,16]{0,1:T(8,128)}, u32[]{:S(2)}) copy-start(f32[512,16]{0,1:T(8,128)} %param.14) | copy-start | bytes 98308
  0.7 4.9 %copy-start.1 = (f32[3,7,8192]{2,1,0:T(8,128)S(1)}, f32[3,7,8192]{2,1,0:T(8,128)}, u32[]{:S(2)}) copy-start(f32[3,7,8192]{2,1,0:T(8,128)} %filt.3) | copy-start | bytes 2064388
  0.7 3.7 %copy-start.9 = (f32[512,16]{0,1:T(8,128)S(1)}, f32[512,16]{0,1:T(8,128)}, u32[]{:S(2)}) copy-start(f32[512,16]{0,1:T(8,128)} %param.14) | copy-start | bytes 98308
  3.1 2.1 %collective-permute-start.1 = (bf16[4,8,8192]{2,1,0:T(8,128)(2,1)S(1)}, bf16[4,8,8192]{2,1,0:T(8,128)(2,1)S(1)}, u32[]{:S(2)}, u32[]{:S(2)}) collective-permute-start(bf16[4,8,8192]{2,1,0:T(8,128)(2,1)S(1)} %get-tuple-element.64), channel_id=1, source_target_pairs={{0,1},{1,0},{2,3},{3,2},{4,5},{5,4},{6,7},{7,6},{8,9},{9,8},{10,11... | collective-permute-start | bytes 1572872 | tf_op jit(solution)/shard_map/ppermute | solution.py:249
  3.6 1.5 %collective-permute-start = (bf16[4,8,8192]{2,1,0:T(8,128)(2,1)S(1)}, bf16[4,8,8192]{2,1,0:T(8,128)(2,1)S(1)}, u32[]{:S(2)}, u32[]{:S(2)}) collective-permute-start(bf16[4,8,8192]{2,1,0:T(8,128)(2,1)S(1)} %get-tuple-element.65), channel_id=1, source_target_pairs={{1,2},{3,4},{5,6},{2,1},{4,3},{6,5},{9,10},{11,12},{13,14},{10,9},... | collective-permute-start | bytes 1572872 | tf_op jit(solution)/shard_map/ppermute | solution.py:333
  4.6 1.0 copy-start.5
  5.6 22.9 %copy-start.2 = (bf16[4,8,8192]{2,1,0:T(8,128)(2,1)}, bf16[4,8,8192]{2,1,0:T(8,128)(2,1)S(1)}, u32[]{:S(2)}) copy-start(bf16[4,8,8192]{2,1,0:T(8,128)(2,1)S(1)} %collective-permute-done.hx) | copy-start | bytes 1572868
  5.6 32.5 %copy-start.11 = (f32[4]{0:T(128)S(1)}, f32[4]{0:T(128)}, u32[]{:S(2)}) copy-start(f32[4]{0:T(128)} %constant.50) | copy-start | bytes 52
  5.6 33.4 %copy-start.14 = (f32[24]{0:T(128)S(1)}, f32[24]{0:T(128)}, u32[]{:S(2)}) copy-start(f32[24]{0:T(128)} %constant.48) | copy-start | bytes 292
  28.5 15.6 %copy-start.12 = (pred[4,8]{1,0:T(4,128)(4,1)S(1)}, pred[4,8]{1,0:T(4,128)(4,1)}, u32[]{:S(2)}) copy-start(pred[4,8]{1,0:T(4,128)(4,1)} %constant.51) | copy-start | bytes 100
  28.5 15.6 %copy-start.13 = (pred[4,8]{1,0:T(4,128)(4,1)S(1)}, pred[4,8]{1,0:T(4,128)(4,1)}, u32[]{:S(2)}) copy-start(pred[4,8]{1,0:T(4,128)(4,1)} %constant.49) | copy-start | bytes 100
  28.5 15.9 %copy-start.4 = (f32[8192]{0:T(1024)S(1)}, f32[8192]{0:T(1024)}, u32[]{:S(2)}) copy-start(f32[8192]{0:T(1024)} %param.15) | copy-start | bytes 98308
  28.6 12.1 %collective-permute-start.2 = (f32[2,16,16,512]{3,2,1,0:T(8,128)}, f32[2,16,16,512]{3,2,1,0:T(8,128)S(1)}, u32[]{:S(2)}, u32[]{:S(2)}) collective-permute-start(f32[2,16,16,512]{3,2,1,0:T(8,128)} %get-tuple-element.30), channel_id=1, source_target_pairs={{0,1},{1,0},{2,3},{3,2},{4,5},{5,4},{6,7},{7,6},{8,9},{9,8},{10,11... | collective-permute-start | bytes 3145736 | tf_op jit(solution)/shard_map/ppermute | solution.py:249
  41.9 10.6 %collective-permute-start.3 = (f32[8,16,512]{2,1,0:T(8,128)S(1)}, f32[8,16,512]{2,1,0:T(8,128)S(1)}, u32[]{:S(2)}, u32[]{:S(2)}) collective-permute-start(f32[8,16,512]{2,1,0:T(8,128)S(1)} %broadcast_select_fusion.6), channel_id=1, source_target_pairs={{0,2},{1,3},{2,0},{3,1},{4,6},{5,7},{6,4},{7,5},{8,10},{9,11},{10,... | collective-permute-start | bytes 786440 | tf_op jit(solution)/shard_map/ppermute | solution.py:265
  52.6 14.2 %copy-start.6 = (f32[4,16,8,512]{3,2,1,0:T(8,128)S(1)}, f32[4,16,8,512]{3,2,1,0:T(8,128)}, u32[]{:S(2)}) copy-start(f32[4,16,8,512]{3,2,1,0:T(8,128)} %copy-done.5) | copy-start | bytes 3145732
  52.6 14.2 %copy-start.7 = (f32[512,16]{0,1:T(8,128)S(1)}, f32[512,16]{0,1:T(8,128)}, u32[]{:S(2)}) copy-start(f32[512,16]{0,1:T(8,128)} %param.13) | copy-start | bytes 98308
  52.6 16.0 %copy-start.3 = (bf16[4,8,8192]{2,1,0:T(8,128)(2,1)S(1)}, bf16[4,8,8192]{2,1,0:T(8,128)(2,1)}, u32[]{:S(2)}) copy-start(bf16[4,8,8192]{2,1,0:T(8,128)(2,1)} %copy-done.2) | copy-start | bytes 1572868
  52.6 13.9 %collective-permute-start.5 = (f32[8,16,512]{2,1,0:T(8,128)S(1)}, f32[8,16,512]{2,1,0:T(8,128)S(1)}, u32[]{:S(2)}, u32[]{:S(2)}) collective-permute-start(f32[8,16,512]{2,1,0:T(8,128)S(1)} %multiply_add_fusion.1), channel_id=1, source_target_pairs={{2,6},{3,7},{4,0},{5,1},{10,14},{11,15},{12,8},{13,9},{18,22},{19,... | collective-permute-start | bytes 786440 | tf_op jit(solution)/shard_map/ppermute | solution.py:279
  54.1 12.5 %collective-permute-start.4 = (f32[8,16,512]{2,1,0:T(8,128)S(1)}, f32[8,16,512]{2,1,0:T(8,128)S(1)}, u32[]{:S(2)}, u32[]{:S(2)}) collective-permute-start(f32[8,16,512]{2,1,0:T(8,128)S(1)} %multiply_add_fusion.1), channel_id=1, source_target_pairs={{2,4},{3,5},{4,2},{5,3},{10,12},{11,13},{12,10},{13,11},{18,20},{1... | collective-permute-start | bytes 786440 | tf_op jit(solution)/shard_map/ppermute | solution.py:278
  66.7 2.0 %collective-permute-start.6 = (f32[2,8,16,512]{3,2,1,0:T(8,128)S(1)}, f32[2,8,16,512]{3,2,1,0:T(8,128)S(1)}, u32[]{:S(2)}, u32[]{:S(2)}) collective-permute-start(f32[2,8,16,512]{3,2,1,0:T(8,128)S(1)} %pad_maximum_fusion.2.both), channel_id=1, source_target_pairs={{0,1},{1,0},{2,3},{3,2},{4,5},{5,4},{6,7},{7,6},{8,9},{9,8},{10,11... | collective-permute-start | bytes 1572872 | tf_op jit(solution)/shard_map/ppermute | solution.py:249
  102.0 1.8 %collective-permute-start.7 = (f32[16,24,256]{2,1,0:T(8,128)S(1)}, f32[16,24,256]{2,1,0:T(8,128)S(1)}, u32[]{:S(2)}, u32[]{:S(2)}) collective-permute-start(f32[16,24,256]{2,1,0:T(8,128)S(1)} %slice_select_fusion), channel_id=1, source_target_pairs={{0,1},{1,0},{2,3},{3,2},{4,5},{5,4},{6,7},{7,6},{8,9},{9,8},{10,11... | collective-permute-start | bytes 1179656 | tf_op jit(solution)/shard_map/ppermute | solution.py:249
  142.8 1.7 %collective-permute-start.8 = (f32[16,24,256]{2,1,0:T(8,128)S(1)}, f32[16,24,256]{2,1,0:T(8,128)S(1)}, u32[]{:S(2)}, u32[]{:S(2)}) collective-permute-start(f32[16,24,256]{2,1,0:T(8,128)S(1)} %all_to_all.11), channel_id=1, source_target_pairs={{0,1},{1,0},{2,3},{3,2},{4,5},{5,4},{6,7},{7,6},{8,9},{9,8},{10,11... | collective-permute-start | bytes 1179656 | tf_op jit(solution)/shard_map/ppermute | solution.py:249

commit v7 on v6

--- a/solution.py
+++ b/solution.py
@@ -46,7 +46,7 @@
     return values[0]
 
 
-def states_kernel(core, p, hx, hi, u, filt, f1, we, wb, qkv, xg, blocks_e, blocks_a, ends, xs):
+def states_kernel(core, p, hx_low, hx_high, hi, u, filt, f1, we, wb, qkv, xg, blocks_e, blocks_a, ends, xs):
     rows = p.shape[1]
     run = (rows + SUB) // SUB
     taps = filt.shape[1]
@@ -61,20 +61,21 @@
         which = lt // tiles
         inside = lax.broadcasted_iota(jnp.int32, (SUB, LANES), 0) < SUB - 1
         for j in range(3):
-            across, within = hx[j, :, lanes].astype(F32), hi[j, :, lanes].astype(F32)
+            across = (hx_low, hx_high)[j // 2][j % 2, :, lanes].astype(F32)
+            within = hi[j, :, lanes].astype(F32)
             xs[j, 0:SUB] = jnp.where(first, across, within)
             xs[j, SUB : SUB + rows] = p[j, :, lanes].astype(F32)
             xs[j, SUB + rows :] = jnp.where(first, within, across)
         xs[3, SUB : SUB + rows] = u[:, lanes].astype(F32)
-        across, within = hx[3, :, lanes].astype(F32), hi[3, :, lanes].astype(F32)
+        across, within = hx_high[1, :, lanes].astype(F32), hi[3, :, lanes].astype(F32)
         xs[3, SUB + rows :] = jnp.where(first, within, across)
 
         def mixed(j):
             tap = [spread(filt[j, i : i + 1, lanes]) for i in range(taps)]
-            view = [xs[j, pl.ds(SUB + a, SUB, stride=run), :] for a in range(1 - taps, run)]
-            return [
-                added([tap[i] * view[a + taps - 1 - i] for i in range(taps)]) for a in range(run)
-            ]
+            view = [xs[j, pl.ds(SUB + a, SUB, stride=run), :] for a in range(1 - taps, 0)]
+            for a in range(run):
+                view = view[-(taps - 1) :] + [xs[j, pl.ds(SUB + a, SUB, stride=run), :]]
+                yield added([tap[i] * view[-1 - i] for i in range(taps)])
 
         decay = [spread(f1[n : n + 1, part]) for n in range(poles)]
         for j in (1, 2, 0):
@@ -149,7 +150,7 @@
 
 
 def final_kernel(
-    core, p, hx, hi, u, qkv, conv, from_e, from_a, both, found, other, filt, f1, f_all, cz, cy,
+    core, p, hx_low, hx_high, hi, u, qkv, conv, from_e, from_a, both, found, other, filt, f1, f_all, cz, cy,
     output, grad_p, sums, ps, us, gs, os, es,
 ):
     rows = p.shape[1]
@@ -175,12 +176,13 @@
             close = other[side, which, :, part] + f_all[:, part] * far
             es[side] = jnp.where(first == (side == 0), far, close)
         for j in range(3):
-            across, within = hx[j, :, lanes].astype(F32), hi[j, :, lanes].astype(F32)
+            across = (hx_low, hx_high)[j // 2][j % 2, :, lanes].astype(F32)
+            within = hi[j, :, lanes].astype(F32)
             ps[j, 0:SUB] = jnp.where(first, across, within)
             ps[j, SUB : SUB + rows] = p[j, :, lanes].astype(F32)
             ps[j, SUB + rows :] = jnp.where(first, within, across)
         us[0:rows] = u[:, lanes].astype(F32)
-        across, within = hx[3, :, lanes].astype(F32), hi[3, :, lanes].astype(F32)
+        across, within = hx_high[1, :, lanes].astype(F32), hi[3, :, lanes].astype(F32)
         us[rows:] = jnp.where(first, within, across)
         decay = [spread(f1[n : n + 1, part]) for n in range(poles)]
 
@@ -218,15 +220,17 @@
         rest = []
         for j in range(3):
             tap = [spread(filt[j, i : i + 1, lanes]) for i in range(taps)]
-            grads = [gs[j, pl.ds(a, SUB, stride=run), :] for a in range(run + taps - 1)]
-            views = [ps[j, pl.ds(SUB + a, SUB, stride=run), :] for a in range(1 - taps, run)]
+            grads = [gs[j, pl.ds(a, SUB, stride=run), :] for a in range(taps - 1)]
+            views = [ps[j, pl.ds(SUB + a, SUB, stride=run), :] for a in range(1 - taps, 0)]
             sums_of = [None] * taps
             for a in range(run):
-                total = added([tap[i] * grads[a + i] for i in range(taps)])
+                grads = grads[-(taps - 1) :] + [gs[j, pl.ds(a + taps - 1, SUB, stride=run), :]]
+                views = views[-(taps - 1) :] + [ps[j, pl.ds(SUB + a, SUB, stride=run), :]]
+                total = added([tap[i] * grads[i] for i in range(taps)])
                 os[pl.ds(a, SUB, stride=run), :] = total
-                grad = grads[a] if a < own else jnp.where(inside, grads[a], 0.0)
+                grad = grads[0] if a < own else jnp.where(inside, grads[0], 0.0)
                 for i in range(taps):
-                    term = grad * views[a + taps - 1 - i]
+                    term = grad * views[-1 - i]
                     sums_of[i] = term if a == 0 else sums_of[i] + term
             grad_p[j, :, lanes] = os[0:rows].astype(BF16)
             rest = rest + sums_of
@@ -294,24 +298,35 @@
     return before, after, kept
 
 
+def chain(left, right, turn):
+    index, dp = lax.axis_index("ctx"), lax.axis_index("dp")
+    reaches = []
+    while 2 ** len(reaches) < lax.axis_size("dp"):
+        reaches.append(2 ** len(reaches))
+    chips = []
+    while 2 ** (len(chips) + 1) < lax.axis_size("ctx"):
+        chips.append(2 ** (len(chips) + 1))
+    steps = [("ctx", 1, lax.rem(index, 2) == 0)]
+    steps = steps + [("dp", step, lax.rem(dp // step, 2) == 0) for step in reaches[::turn]]
+    for axis, step, low in steps:
+        value = jnp.where(low, left, right) + paired(jnp.where(low, right, left), axis, step)
+        half = value.shape[0] // 2
+        left, right = value[:half], value[half:]
+    for step in chips[::turn]:
+        value = value + paired(value, "ctx", step)
+    for axis, step, low in reversed(steps):
+        other = paired(value, axis, step)
+        left, right = jnp.where(low, value, other), jnp.where(low, other, value)
+        value = jnp.concatenate([left, right], axis=0)
+    return left, right
+
+
 def summed(value):
-    devices = lax.axis_size("ctx")
-    total = lax.axis_size("dp") * devices
-    sides = [[k for k in range(total) if k % 2 == side] for side in range(2)]
-    parts = total // 2
-    low = lax.rem(lax.axis_index("ctx"), 2) == 0
-    half = value.shape[0] // 2
-    left, right = value[:half], value[half:]
-    value = jnp.where(low, left, right) + swapped(jnp.where(low, right, left))
-    shape = value.shape
-
-    def dealt(value):
-        return lax.all_to_all(value, ("dp", "ctx"), 0, 0, axis_index_groups=sides)
-
-    value = jnp.sum(dealt(value.reshape(parts, shape[1] * half // parts, shape[2])), axis=0)
-    value = dealt(jnp.broadcast_to(value, (parts,) + value.shape)).reshape(shape)
-    other = swapped(value)
-    return jnp.concatenate([jnp.where(low, value, other), jnp.where(low, other, value)], axis=0)
+    quarter = value.shape[0] // 4
+    parts = [value[k * quarter : (k + 1) * quarter] for k in range(4)]
+    left, right = chain(parts[0], parts[2], 1)
+    other_left, other_right = chain(parts[1], parts[3], -1)
+    return jnp.concatenate([left, other_left, right, other_right], axis=0)
 
 
 def local(projected, short_filter, residues, decay_rates, skip_gain, cotangent):
@@ -330,7 +345,8 @@
     devices = lax.axis_size("ctx")
     across = [(k, k + 1) for k in range(1, devices - 1, 2)]
     across = across + [(target, source) for source, target in across]
-    hx = lax.ppermute(jnp.where(core == 0, head, tail), "ctx", across)
+    sent = jnp.where(core == 0, head, tail)
+    hx = [lax.ppermute(sent[2 * k : 2 * k + 2], "ctx", across) for k in range(2)]
     hi = swapped(jnp.where(core == 0, tail, head))
 
     rate = decay_rates.T
@@ -375,7 +391,7 @@
         grid=(width // each,),
         in_specs=[
             pl.BlockSpec(memory_space=pltpu.SMEM),
-            by_w(3, rows), by_w(4, SUB), by_w(4, SUB), by_w(rows), by_w(3, taps),
+            by_w(3, rows), by_w(2, SUB), by_w(2, SUB), by_w(4, SUB), by_w(rows), by_w(3, taps),
             fixed(f1), fixed(we), fixed(wb),
         ],
         out_specs=[
@@ -389,7 +405,7 @@
         scratch_shapes=[pltpu.VMEM((4, held + SUB, LANES), F32)],
         compiler_params=params,
         name="states",
-    )(core[None], p, hx, hi, u, short_filter, f1, we, wb)
+    )(core[None], p, *hx, hi, u, short_filter, f1, we, wb)
 
     many = 2 if width % 2 == 0 else 1
 
@@ -442,7 +458,7 @@
         grid=(width // each,),
         in_specs=[
             pl.BlockSpec(memory_space=pltpu.SMEM),
-            by_w(3, rows), by_w(4, SUB), by_w(4, SUB), by_w(rows), by_w(3, held), by_w(2, held),
+            by_w(3, rows), by_w(2, SUB), by_w(2, SUB), by_w(4, SUB), by_w(rows), by_w(3, held), by_w(2, held),
             by_w(poles, SUB), by_w(poles, SUB), halved, halved, ends_spec,
             by_w(3, taps), fixed(f1), fixed(f_all), fixed(cz), fixed(cy),
         ],
@@ -459,7 +475,7 @@
         compiler_params=params,
         name="final",
     )(
-        core[None], p, hx, hi, u, qkv, conv, from_e, from_a, both, found, other, short_filter,
+        core[None], p, *hx, hi, u, qkv, conv, from_e, from_a, both, found, other, short_filter,
         f1, f_all, cz, cy,
     )
 

time: 148 us -> 143 us (0.966)
  blocking collectives: 38.9 us -> 0 us
  starting transfers between devices: 15.4 us -> 38 us
  waiting for transfers between devices: 6.2 us -> 18 us
    all_to_all x2 -> x0, blocking collectives: 38.9 us -> none  [dealt(): return lax.all_to_all(value, ('dp', 'ctx'), 0, 0, axis_index_groups=sides)]
    ppermute x1 -> x17, starting transfers between devices: 2.18 us -> 24.4 us  [paired(): lax.ppermute(value, axis, [(source, source ^ step) for source in lines or...]
    ppermute x1 -> x17, waiting for transfers between devices: 0.01 us -> 14.5 us  [paired(): lax.ppermute(value, axis, [(source, source ^ step) for source in lines or...]
    ppermute x5 -> x3, waiting for transfers between devices: 6.19 us -> 3.55 us  [swapped(): return lax.ppermute(value, 'ctx', [(s, s ^ 1) for s in range(count)])]
    ppermute x5 -> x3, starting transfers between devices: 10.4 us -> 10.1 us  [swapped(): return lax.ppermute(value, 'ctx', [(s, s ^ 1) for s in range(count)])]
  transfers between devices with their start and end apart: 9 -> 24, of which waited for: 5 -> 14; matrix products, arithmetic and copies ran while one was open for 2% -> 2% of each run, Pallas kernels for 14% -> 14%
where the time goes in v7:
time: 143 us; the launch traced here: 142 us
  Pallas kernels  75.4 us (53%)
  starting transfers between devices  38 us (27%)
  waiting for transfers between devices  18 us (13%)
  other arithmetic  4.54 us (3%)
  local copies, waits for them, and re-layouts  4.45 us (3%)
    pallas_call x1, Pallas kernels, local(): pl.pallas_call(final_kernel, grid=(width // each,), in_specs=[pl.BlockSpe...  33.3 us
    ppermute x17, starting transfers between devices, paired(): lax.ppermute(value, axis, [(source, source ^ step) for source in lines or...  24.4 us
    pallas_call x1, Pallas kernels, local(): pl.pallas_call(states_kernel, grid=(width // each,), in_specs=[pl.BlockSp...  22.3 us
    pallas_call x2, Pallas kernels, call(): pl.pallas_call(blocks_kernel, grid=(last - first,), in_specs=[at_w(2, hel...  19.9 us
    ppermute x17, waiting for transfers between devices, paired(): lax.ppermute(value, axis, [(source, source ^ step) for source in lines or...  14.5 us
    ppermute x3, starting transfers between devices, swapped(): return lax.ppermute(value, 'ctx', [(s, s ^ 1) for s in range(count)])  10.1 us
    ppermute x3, waiting for transfers between devices, swapped(): return lax.ppermute(value, 'ctx', [(s, s ^ 1) for s in range(count)])  3.55 us
  transfers between devices with their start and end apart: 24, of which 14 were waited for; matrix products, arithmetic and copies ran while one was open for 2% of the time, Pallas kernels for 14%

profile of v7, /device:TPU:0, one launch (start us, length us, event | category | flops | bytes accessed | tf_op | source)
XLA Modules:
  0.0 141.6 jit_solution(16767117395654534598)
XLA Ops:
  0.6 0.0 copy-start.12
  0.7 1.1 fusion.9
  1.8 1.2 fusion.8
  3.0 0.1 broadcast_select_fusion.2
  3.2 0.7 collective-permute-start.1
  3.8 0.7 collective-permute-start
  4.5 5.7 %collective-permute-start.2 = (bf16[4,8,8192]{2,1,0:T(8,128)(2,1)S(1)}, bf16[4,8,8192]{2,1,0:T(8,128)(2,1)S(1)}, u32[]{:S(2)}, u32[]{:S(2)}) collective-permute-start(bf16[4,8,8192]{2,1,0:T(8,128)(2,1)S(1)} %get-tuple-element.64), channel_id=1, source_target_pairs={{0,1},{1,0},{2,3},{3,2},{4,5},{5,4},{6,7},{7,6},{8,9},{9,8},{10,11... | collective-permute-start | bytes 1572872 | tf_op jit(solution)/shard_map/ppermute | solution.py:253
  10.2 0.2 multiply_exponential_fusion
  10.6 1.2 collective-permute-done.2.hi
  11.8 0.0 copy-start.16
  11.8 22.3 %states.1 = (f32[3,136,8192]{2,1,0:T(8,128)}, f32[2,136,8192]{2,1,0:T(8,128)}, f32[16,8,8192]{2,1,0:T(8,128)}, f32[16,8,8192]{2,1,0:T(8,128)}, f32[2,16,16,512]{3,2,1,0:T(8,128)}) custom-call(s32[1]{0:T(128)} %bitcast.core, bf16[3,128,8192]{2,1,0:T(8,128)(2,1)} %bitcast.83, bf16[2,8,8192]{2,1,0:T(8,128)(2,1)S(1)} %collective-permute-done.hx_low, ...), custom_call_target="tpu_custom_call" | custom-call | tf_op jit(solution)/shard_map/states/pallas_call | solution.py:389
  34.1 4.3 %collective-permute-start.3 = (f32[2,16,16,512]{3,2,1,0:T(8,128)}, f32[2,16,16,512]{3,2,1,0:T(8,128)S(1)}, u32[]{:S(2)}, u32[]{:S(2)}) collective-permute-start(f32[2,16,16,512]{3,2,1,0:T(8,128)} %get-tuple-element.30), channel_id=1, source_target_pairs={{0,1},{1,0},{2,3},{3,2},{4,5},{5,4},{6,7},{7,6},{8,9},{9,8},{10,11... | collective-permute-start | bytes 3145736 | tf_op jit(solution)/shard_map/ppermute | solution.py:253
  38.4 0.1 multiply_exponential_fusion.1
  38.5 0.8 slice_multiply_fusion
  39.3 1.0 multiply_reduce_fusion.near
  40.3 0.6 collective-permute-done.3.other
  40.9 1.2 dynamic-slice_select_fusion.1
  42.1 0.1 broadcast_select_fusion.4
  42.2 1.7 %collective-permute-start.4 = (f32[8,16,512]{2,1,0:T(8,128)S(1)}, f32[8,16,512]{2,1,0:T(8,128)S(1)}, u32[]{:S(2)}, u32[]{:S(2)}) collective-permute-start(f32[8,16,512]{2,1,0:T(8,128)S(1)} %broadcast_select_fusion.4), channel_id=1, source_target_pairs={{0,2},{1,3},{2,0},{3,1},{4,6},{5,7},{6,4},{7,5},{8,10},{9,11},{10,... | collective-permute-start | bytes 786440 | tf_op jit(solution)/shard_map/ppermute | solution.py:269
  43.8 0.3 broadcast_select_fusion
  44.2 8.1 %blocks.2 = (f32[2,136,8192]{2,1,0:T(8,128)}, f32[16,8,8192]{2,1,0:T(8,128)}, f32[16,8,8192]{2,1,0:T(8,128)}) custom-call(f32[2,136,8192]{2,1,0:T(8,128)} %get-tuple-element.31.xg, f32[16,8,8192]{2,1,0:T(8,128)} %get-tuple-element.32.blocks_e, f32[16,8,8192]{2,1,0:T(8,128)} %get-tuple-element.33.blocks_a, ...), custom_call_target="tpu_custom_call", output_to_operand_aliasing={{0}: (0, {}), {1}: (1, {}), {2}: (2, {})} | custom-call | flops 62914560 | bytes 36700160 | tf_op jit(solution)/shard_map/blocks/pallas_call | solution.py:419
  52.3 0.1 multiply_add_fusion.1
  52.5 1.4 %collective-permute-start.6 = (f32[8,16,512]{2,1,0:T(8,128)S(1)}, f32[8,16,512]{2,1,0:T(8,128)S(1)}, u32[]{:S(2)}, u32[]{:S(2)}) collective-permute-start(f32[8,16,512]{2,1,0:T(8,128)S(1)} %multiply_add_fusion.1), channel_id=1, source_target_pairs={{2,6},{3,7},{4,0},{5,1},{10,14},{11,15},{12,8},{13,9},{18,22},{19,... | collective-permute-start | bytes 786440 | tf_op jit(solution)/shard_map/ppermute | solution.py:283
  53.9 0.7 collective-permute-start.5
  54.6 11.8 %blocks.3 = (f32[2,136,8192]{2,1,0:T(8,128)}, f32[16,8,8192]{2,1,0:T(8,128)}, f32[16,8,8192]{2,1,0:T(8,128)}) custom-call(f32[2,136,8192]{2,1,0:T(8,128)} %get-tuple-element.39.xg, f32[16,8,8192]{2,1,0:T(8,128)} %get-tuple-element.40.blocks_e, f32[16,8,8192]{2,1,0:T(8,128)} %get-tuple-element.41.blocks_a, ...), custom_call_target="tpu_custom_call", output_to_operand_aliasing={{0}: (0, {}), {1}: (1, {}), {2}: (2, {})} | custom-call | flops 62914560 | bytes 36700160 | tf_op jit(solution)/shard_map/blocks/pallas_call | solution.py:419
  66.4 0.1 select_bitcast_fusion.1
  66.5 0.1 collective-permute-start.7
  66.7 0.1 fusion
  66.7 1.8 %collective-permute-done.7.found = f32[2,8,16,512]{3,2,1,0:T(8,128)S(1)} collective-permute-done((f32[2,8,16,512]{3,2,1,0:T(8,128)S(1)}, f32[2,8,16,512]{3,2,1,0:T(8,128)S(1)}, u32[]{:S(2)}, u32[]{:S(2)}) %collective-permute-start.7) | collective-permute-done | bytes 524320 | tf_op jit(solution)/shard_map/ppermute | solution.py:253
  68.5 33.3 %final.1 = (bf16[128,8192]{1,0:T(8,128)(2,1)}, bf16[3,128,8192]{2,1,0:T(8,128)(2,1)}, f32[32,24,256]{2,1,0:T(8,128)S(1)}) custom-call(s32[1]{0:T(128)} %bitcast.core, bf16[3,128,8192]{2,1,0:T(8,128)(2,1)} %bitcast.84, bf16[2,8,8192]{2,1,0:T(8,128)(2,1)S(1)} %copy-done.5, bf16[2,8,8192]{2,1,0:T(8,128)(2,1)S(1)} %copy-done.3, ...), custom_call_target="tpu_custom_call" | custom-call | tf_op jit(solution)/shard_map/final/pallas_call | solution.py:456
  101.8 0.1 slice_select_fusion.1
  101.8 0.2 collective-permute-start.8
  102.0 0.4 collective-permute-start.16
  102.4 0.9 collective-permute-done.8
  103.3 0.3 collective-permute-done.16
  103.6 0.1 select_add_fusion.1
  103.7 1.6 %collective-permute-start.17 = (f32[4,24,256]{2,1,0:T(8,128)S(1)}, f32[4,24,256]{2,1,0:T(8,128)S(1)}, u32[]{:S(2)}, u32[]{:S(2)}) collective-permute-start(f32[4,24,256]{2,1,0:T(8,128)S(1)} %slice_select_fusion.2), channel_id=1, source_target_pairs={{0,16},{8,24},{16,0},{24,8},{1,17},{9,25},{17,1},{25,9},{2,18},{10... | collective-permute-start | bytes 294920 | tf_op jit(solution)/shard_map/ppermute | solution.py:269
  105.3 1.6 %collective-permute-start.9 = (f32[4,24,256]{2,1,0:T(8,128)S(1)}, f32[4,24,256]{2,1,0:T(8,128)S(1)}, u32[]{:S(2)}, u32[]{:S(2)}) collective-permute-start(f32[4,24,256]{2,1,0:T(8,128)S(1)} %slice_select_fusion.3), channel_id=1, source_target_pairs={{0,8},{8,0},{16,24},{24,16},{1,9},{9,1},{17,25},{25,17},{2,10},{10... | collective-permute-start | bytes 294920 | tf_op jit(solution)/shard_map/ppermute | solution.py:269
  106.9 1.8 %collective-permute-done.17 = f32[4,24,256]{2,1,0:T(8,128)S(1)} collective-permute-done((f32[4,24,256]{2,1,0:T(8,128)S(1)}, f32[4,24,256]{2,1,0:T(8,128)S(1)}, u32[]{:S(2)}, u32[]{:S(2)}) %collective-permute-start.17) | collective-permute-done | bytes 98336 | tf_op jit(solution)/shard_map/ppermute | solution.py:269
  108.8 1.6 %collective-permute-start.18 = (f32[2,24,256]{2,1,0:T(8,128)S(1)}, f32[2,24,256]{2,1,0:T(8,128)S(1)}, u32[]{:S(2)}, u32[]{:S(2)}) collective-permute-start(f32[2,24,256]{2,1,0:T(8,128)S(1)} %slice_select_fusion.4), channel_id=1, source_target_pairs={{0,8},{8,0},{16,24},{24,16},{1,9},{9,1},{17,25},{25,17},{2,10},{10... | collective-permute-start | bytes 147464 | tf_op jit(solution)/shard_map/ppermute | solution.py:269
  110.4 1.6 %collective-permute-start.10 = (f32[2,24,256]{2,1,0:T(8,128)S(1)}, f32[2,24,256]{2,1,0:T(8,128)S(1)}, u32[]{:S(2)}, u32[]{:S(2)}) collective-permute-start(f32[2,24,256]{2,1,0:T(8,128)S(1)} %slice_select_fusion.5), channel_id=1, source_target_pairs={{0,16},{8,24},{16,0},{24,8},{1,17},{9,25},{17,1},{25,9},{2,18},{10... | collective-permute-start | bytes 147464 | tf_op jit(solution)/shard_map/ppermute | solution.py:269
  111.9 1.0 collective-permute-done.18
  112.9 6.4 %collective-permute-start.19 = (f32[2,24,256]{2,1,0:T(8,128)S(1)}, f32[2,24,256]{2,1,0:T(8,128)S(1)}, u32[]{:S(2)}, u32[]{:S(2)}) collective-permute-start(f32[2,24,256]{2,1,0:T(8,128)S(1)} %select_add_fusion.4), channel_id=1, source_target_pairs={{0,4},{1,5},{2,6},{3,7},{4,0},{5,1},{6,2},{7,3},{8,12},{9,13},{10,... | collective-permute-start | bytes 147464 | tf_op jit(solution)/shard_map/ppermute | solution.py:269
  119.4 0.6 collective-permute-start.11
  119.9 1.5 %collective-permute-done.19 = f32[2,24,256]{2,1,0:T(8,128)S(1)} collective-permute-done((f32[2,24,256]{2,1,0:T(8,128)S(1)}, f32[2,24,256]{2,1,0:T(8,128)S(1)}, u32[]{:S(2)}, u32[]{:S(2)}) %collective-permute-start.19) | collective-permute-done | bytes 49184 | tf_op jit(solution)/shard_map/ppermute | solution.py:269
  121.4 2.0 %collective-permute-start.20 = (f32[2,24,256]{2,1,0:T(8,128)S(1)}, f32[2,24,256]{2,1,0:T(8,128)S(1)}, u32[]{:S(2)}, u32[]{:S(2)}) collective-permute-start(f32[2,24,256]{2,1,0:T(8,128)S(1)} %add.62), channel_id=1, source_target_pairs={{0,2},{1,3},{2,0},{3,1},{4,6},{5,7},{6,4},{7,5},{8,10},{9,11},{10,... | collective-permute-start | bytes 147464 | tf_op jit(solution)/shard_map/ppermute | solution.py:269
  123.4 0.1 collective-permute-done.11
  123.5 2.0 %collective-permute-start.12 = (f32[2,24,256]{2,1,0:T(8,128)S(1)}, f32[2,24,256]{2,1,0:T(8,128)S(1)}, u32[]{:S(2)}, u32[]{:S(2)}) collective-permute-start(f32[2,24,256]{2,1,0:T(8,128)S(1)} %add.57), channel_id=1, source_target_pairs={{0,4},{1,5},{2,6},{3,7},{4,0},{5,1},{6,2},{7,3},{8,12},{9,13},{10,... | collective-permute-start | bytes 147464 | tf_op jit(solution)/shard_map/ppermute | solution.py:269
  125.6 0.0 collective-permute-done.20
  125.6 1.6 %collective-permute-start.21 = (f32[2,24,256]{2,1,0:T(8,128)S(1)}, f32[2,24,256]{2,1,0:T(8,128)S(1)}, u32[]{:S(2)}, u32[]{:S(2)}) collective-permute-start(f32[2,24,256]{2,1,0:T(8,128)S(1)} %add.63), channel_id=1, source_target_pairs={{0,8},{8,0},{16,24},{24,16},{1,9},{9,1},{17,25},{25,17},{2,10},{10... | collective-permute-start | bytes 147464 | tf_op jit(solution)/shard_map/ppermute | solution.py:269
  127.2 2.0 %collective-permute-done.12 = f32[2,24,256]{2,1,0:T(8,128)S(1)} collective-permute-done((f32[2,24,256]{2,1,0:T(8,128)S(1)}, f32[2,24,256]{2,1,0:T(8,128)S(1)}, u32[]{:S(2)}, u32[]{:S(2)}) %collective-permute-start.12) | collective-permute-done | bytes 49184 | tf_op jit(solution)/shard_map/ppermute | solution.py:269
  129.1 1.6 %collective-permute-start.13 = (f32[2,24,256]{2,1,0:T(8,128)S(1)}, f32[2,24,256]{2,1,0:T(8,128)S(1)}, u32[]{:S(2)}, u32[]{:S(2)}) collective-permute-start(f32[2,24,256]{2,1,0:T(8,128)S(1)} %add.58), channel_id=1, source_target_pairs={{0,16},{8,24},{16,0},{24,8},{1,17},{9,25},{17,1},{25,9},{2,18},{10... | collective-permute-start | bytes 147464 | tf_op jit(solution)/shard_map/ppermute | solution.py:269
  130.8 0.6 collective-permute-start.22
  131.4 1.9 %collective-permute-done.13 = f32[2,24,256]{2,1,0:T(8,128)S(1)} collective-permute-done((f32[2,24,256]{2,1,0:T(8,128)S(1)}, f32[2,24,256]{2,1,0:T(8,128)S(1)}, u32[]{:S(2)}, u32[]{:S(2)}) %collective-permute-start.13) | collective-permute-done | bytes 49184 | tf_op jit(solution)/shard_map/ppermute | solution.py:269
  133.3 1.0 collective-permute-start.14
  134.4 1.1 collective-permute-done.22
  135.5 0.1 collective-permute-start.23
  135.6 2.4 %collective-permute-done.14 = f32[4,24,256]{2,1,0:T(8,128)S(1)} collective-permute-done((f32[4,24,256]{2,1,0:T(8,128)S(1)}, f32[4,24,256]{2,1,0:T(8,128)S(1)}, u32[]{:S(2)}, u32[]{:S(2)}) %collective-permute-start.14) | collective-permute-done | bytes 98336 | tf_op jit(solution)/shard_map/ppermute | solution.py:269
  138.0 0.1 collective-permute-start.15
  138.2 1.4 collective-permute-done.15
  139.6 0.1 maximum_bitcast_fusion
  139.7 0.6 slice.147
  140.3 0.2 copy.22
  140.5 1.1 reshape.30
  (70 shorter events, 0.6 us)
Async XLA Ops:
  0.6 9.6 %copy-start.12 = (f32[4,8]{1,0:T(4,128)S(1)}, f32[4,8]{1,0:T(4,128)}, u32[]{:S(2)}) copy-start(f32[4,8]{1,0:T(4,128)} %constant.74) | copy-start | bytes 388
  0.6 11.1 %copy-start = (bf16[1,128,8192]{2,1,0:T(8,128)(2,1)S(1)}, bf16[1,128,8192]{2,1,0:T(8,128)(2,1)}, u32[]{:S(2)}) copy-start(bf16[1,128,8192]{2,1,0:T(8,128)(2,1)} %param.16) | copy-start | bytes 6291460
  0.7 9.6 %copy-start.10 = (f32[512,16]{0,1:T(8,128)S(1)}, f32[512,16]{0,1:T(8,128)}, u32[]{:S(2)}) copy-start(f32[512,16]{0,1:T(8,128)} %param.14) | copy-start | bytes 98308
  0.7 11.1 %copy-start.1 = (f32[3,7,8192]{2,1,0:T(8,128)S(1)}, f32[3,7,8192]{2,1,0:T(8,128)}, u32[]{:S(2)}) copy-start(f32[3,7,8192]{2,1,0:T(8,128)} %filt.3) | copy-start | bytes 2064388
  0.7 9.8 %copy-start.11 = (f32[512,16]{0,1:T(8,128)S(1)}, f32[512,16]{0,1:T(8,128)}, u32[]{:S(2)}) copy-start(f32[512,16]{0,1:T(8,128)} %param.14) | copy-start | bytes 98308
  3.2 7.4 %collective-permute-start.1 = (bf16[2,8,8192]{2,1,0:T(8,128)(2,1)S(1)}, bf16[2,8,8192]{2,1,0:T(8,128)(2,1)S(1)}, u32[]{:S(2)}, u32[]{:S(2)}) collective-permute-start(bf16[2,8,8192]{2,1,0:T(8,128)(2,1)S(1)} %get-tuple-element.72), channel_id=1, source_target_pairs={{1,2},{3,4},{5,6},{2,1},{4,3},{6,5},{9,10},{11,12},{13,14},{10,9},... | collective-permute-start | bytes 786440 | tf_op jit(solution)/shard_map/ppermute | solution.py:349
  3.8 6.7 %collective-permute-start = (bf16[2,8,8192]{2,1,0:T(8,128)(2,1)S(1)}, bf16[2,8,8192]{2,1,0:T(8,128)(2,1)S(1)}, u32[]{:S(2)}, u32[]{:S(2)}) collective-permute-start(bf16[2,8,8192]{2,1,0:T(8,128)(2,1)S(1)} %get-tuple-element.73), channel_id=1, source_target_pairs={{1,2},{3,4},{5,6},{2,1},{4,3},{6,5},{9,10},{11,12},{13,14},{10,9},... | collective-permute-start | bytes 786440 | tf_op jit(solution)/shard_map/ppermute | solution.py:349
  4.5 7.2 %collective-permute-start.2 = (bf16[4,8,8192]{2,1,0:T(8,128)(2,1)S(1)}, bf16[4,8,8192]{2,1,0:T(8,128)(2,1)S(1)}, u32[]{:S(2)}, u32[]{:S(2)}) collective-permute-start(bf16[4,8,8192]{2,1,0:T(8,128)(2,1)S(1)} %get-tuple-element.64), channel_id=1, source_target_pairs={{0,1},{1,0},{2,3},{3,2},{4,5},{5,4},{6,7},{7,6},{8,9},{9,8},{10,11... | collective-permute-start | bytes 1572872 | tf_op jit(solution)/shard_map/ppermute | solution.py:253
  10.5 1.3 copy-start.7
  10.6 23.5 %copy-start.2 = (bf16[2,8,8192]{2,1,0:T(8,128)(2,1)}, bf16[2,8,8192]{2,1,0:T(8,128)(2,1)S(1)}, u32[]{:S(2)}) copy-start(bf16[2,8,8192]{2,1,0:T(8,128)(2,1)S(1)} %collective-permute-done.1.hx_high) | copy-start | bytes 786436
  10.6 23.5 %copy-start.4 = (bf16[2,8,8192]{2,1,0:T(8,128)(2,1)}, bf16[2,8,8192]{2,1,0:T(8,128)(2,1)S(1)}, u32[]{:S(2)}) copy-start(bf16[2,8,8192]{2,1,0:T(8,128)(2,1)S(1)} %collective-permute-done.hx_low) | copy-start | bytes 786436
  11.8 26.7 %copy-start.13 = (f32[4]{0:T(128)S(1)}, f32[4]{0:T(128)}, u32[]{:S(2)}) copy-start(f32[4]{0:T(128)} %constant.77) | copy-start | bytes 52
  11.8 27.6 %copy-start.16 = (f32[24]{0:T(128)S(1)}, f32[24]{0:T(128)}, u32[]{:S(2)}) copy-start(f32[24]{0:T(128)} %constant.75) | copy-start | bytes 292
  34.1 9.8 %copy-start.14 = (pred[4,8]{1,0:T(4,128)(4,1)S(1)}, pred[4,8]{1,0:T(4,128)(4,1)}, u32[]{:S(2)}) copy-start(pred[4,8]{1,0:T(4,128)(4,1)} %constant.78) | copy-start | bytes 100
  34.1 9.8 %copy-start.15 = (pred[4,8]{1,0:T(4,128)(4,1)S(1)}, pred[4,8]{1,0:T(4,128)(4,1)}, u32[]{:S(2)}) copy-start(pred[4,8]{1,0:T(4,128)(4,1)} %constant.76) | copy-start | bytes 100
  34.1 10.1 %copy-start.6 = (f32[8192]{0:T(1024)S(1)}, f32[8192]{0:T(1024)}, u32[]{:S(2)}) copy-start(f32[8192]{0:T(1024)} %param.15) | copy-start | bytes 98308
  34.1 6.8 %collective-permute-start.3 = (f32[2,16,16,512]{3,2,1,0:T(8,128)}, f32[2,16,16,512]{3,2,1,0:T(8,128)S(1)}, u32[]{:S(2)}, u32[]{:S(2)}) collective-permute-start(f32[2,16,16,512]{3,2,1,0:T(8,128)} %get-tuple-element.30), channel_id=1, source_target_pairs={{0,1},{1,0},{2,3},{3,2},{4,5},{5,4},{6,7},{7,6},{8,9},{9,8},{10,11... | collective-permute-start | bytes 3145736 | tf_op jit(solution)/shard_map/ppermute | solution.py:253
  42.2 10.1 %collective-permute-start.4 = (f32[8,16,512]{2,1,0:T(8,128)S(1)}, f32[8,16,512]{2,1,0:T(8,128)S(1)}, u32[]{:S(2)}, u32[]{:S(2)}) collective-permute-start(f32[8,16,512]{2,1,0:T(8,128)S(1)} %broadcast_select_fusion.4), channel_id=1, source_target_pairs={{0,2},{1,3},{2,0},{3,1},{4,6},{5,7},{6,4},{7,5},{8,10},{9,11},{10,... | collective-permute-start | bytes 786440 | tf_op jit(solution)/shard_map/ppermute | solution.py:269
  52.4 14.2 %copy-start.8 = (f32[4,16,8,512]{3,2,1,0:T(8,128)S(1)}, f32[4,16,8,512]{3,2,1,0:T(8,128)}, u32[]{:S(2)}) copy-start(f32[4,16,8,512]{3,2,1,0:T(8,128)} %copy-done.7) | copy-start | bytes 3145732
  52.5 14.2 %copy-start.9 = (f32[512,16]{0,1:T(8,128)S(1)}, f32[512,16]{0,1:T(8,128)}, u32[]{:S(2)}) copy-start(f32[512,16]{0,1:T(8,128)} %param.13) | copy-start | bytes 98308
  52.5 16.0 %copy-start.3 = (bf16[2,8,8192]{2,1,0:T(8,128)(2,1)S(1)}, bf16[2,8,8192]{2,1,0:T(8,128)(2,1)}, u32[]{:S(2)}) copy-start(bf16[2,8,8192]{2,1,0:T(8,128)(2,1)} %copy-done.2) | copy-start | bytes 786436
  52.5 16.0 %copy-start.5 = (bf16[2,8,8192]{2,1,0:T(8,128)(2,1)S(1)}, bf16[2,8,8192]{2,1,0:T(8,128)(2,1)}, u32[]{:S(2)}) copy-start(bf16[2,8,8192]{2,1,0:T(8,128)(2,1)} %copy-done.4) | copy-start | bytes 786436
  52.5 13.9 %collective-permute-start.6 = (f32[8,16,512]{2,1,0:T(8,128)S(1)}, f32[8,16,512]{2,1,0:T(8,128)S(1)}, u32[]{:S(2)}, u32[]{:S(2)}) collective-permute-start(f32[8,16,512]{2,1,0:T(8,128)S(1)} %multiply_add_fusion.1), channel_id=1, source_target_pairs={{2,6},{3,7},{4,0},{5,1},{10,14},{11,15},{12,8},{13,9},{18,22},{19,... | collective-permute-start | bytes 786440 | tf_op jit(solution)/shard_map/ppermute | solution.py:283
  53.9 12.5 %collective-permute-start.5 = (f32[8,16,512]{2,1,0:T(8,128)S(1)}, f32[8,16,512]{2,1,0:T(8,128)S(1)}, u32[]{:S(2)}, u32[]{:S(2)}) collective-permute-start(f32[8,16,512]{2,1,0:T(8,128)S(1)} %multiply_add_fusion.1), channel_id=1, source_target_pairs={{2,4},{3,5},{4,2},{5,3},{10,12},{11,13},{12,10},{13,11},{18,20},{1... | collective-permute-start | bytes 786440 | tf_op jit(solution)/shard_map/ppermute | solution.py:282
  66.5 2.0 %collective-permute-start.7 = (f32[2,8,16,512]{3,2,1,0:T(8,128)S(1)}, f32[2,8,16,512]{3,2,1,0:T(8,128)S(1)}, u32[]{:S(2)}, u32[]{:S(2)}) collective-permute-start(f32[2,8,16,512]{3,2,1,0:T(8,128)S(1)} %pad_maximum_fusion.2.both), channel_id=1, source_target_pairs={{0,1},{1,0},{2,3},{3,2},{4,5},{5,4},{6,7},{7,6},{8,9},{9,8},{10,11... | collective-permute-start | bytes 1572872 | tf_op jit(solution)/shard_map/ppermute | solution.py:253
  101.8 1.5 %collective-permute-start.8 = (f32[8,24,256]{2,1,0:T(8,128)S(1)}, f32[8,24,256]{2,1,0:T(8,128)S(1)}, u32[]{:S(2)}, u32[]{:S(2)}) collective-permute-start(f32[8,24,256]{2,1,0:T(8,128)S(1)} %get-tuple-element.70), channel_id=1, source_target_pairs={{0,1},{1,0},{2,3},{3,2},{4,5},{5,4},{6,7},{7,6},{8,9},{9,8},{10,11... | collective-permute-start | bytes 589832 | tf_op jit(solution)/shard_map/ppermute | solution.py:269
  102.0 1.6 %collective-permute-start.16 = (f32[8,24,256]{2,1,0:T(8,128)S(1)}, f32[8,24,256]{2,1,0:T(8,128)S(1)}, u32[]{:S(2)}, u32[]{:S(2)}) collective-permute-start(f32[8,24,256]{2,1,0:T(8,128)S(1)} %get-tuple-element.71), channel_id=1, source_target_pairs={{0,1},{1,0},{2,3},{3,2},{4,5},{5,4},{6,7},{7,6},{8,9},{9,8},{10,11... | collective-permute-start | bytes 589832 | tf_op jit(solution)/shard_map/ppermute | solution.py:269
  103.7 5.0 %collective-permute-start.17 = (f32[4,24,256]{2,1,0:T(8,128)S(1)}, f32[4,24,256]{2,1,0:T(8,128)S(1)}, u32[]{:S(2)}, u32[]{:S(2)}) collective-permute-start(f32[4,24,256]{2,1,0:T(8,128)S(1)} %slice_select_fusion.2), channel_id=1, source_target_pairs={{0,16},{8,24},{16,0},{24,8},{1,17},{9,25},{17,1},{25,9},{2,18},{10... | collective-permute-start | bytes 294920 | tf_op jit(solution)/shard_map/ppermute | solution.py:269
  105.3 5.0 %collective-permute-start.9 = (f32[4,24,256]{2,1,0:T(8,128)S(1)}, f32[4,24,256]{2,1,0:T(8,128)S(1)}, u32[]{:S(2)}, u32[]{:S(2)}) collective-permute-start(f32[4,24,256]{2,1,0:T(8,128)S(1)} %slice_select_fusion.3), channel_id=1, source_target_pairs={{0,8},{8,0},{16,24},{24,16},{1,9},{9,1},{17,25},{25,17},{2,10},{10... | collective-permute-start | bytes 294920 | tf_op jit(solution)/shard_map/ppermute | solution.py:269
  108.8 4.2 %collective-permute-start.18 = (f32[2,24,256]{2,1,0:T(8,128)S(1)}, f32[2,24,256]{2,1,0:T(8,128)S(1)}, u32[]{:S(2)}, u32[]{:S(2)}) collective-permute-start(f32[2,24,256]{2,1,0:T(8,128)S(1)} %slice_select_fusion.4), channel_id=1, source_target_pairs={{0,8},{8,0},{16,24},{24,16},{1,9},{9,1},{17,25},{25,17},{2,10},{10... | collective-permute-start | bytes 147464 | tf_op jit(solution)/shard_map/ppermute | solution.py:269
  110.4 9.0 %collective-permute-start.10 = (f32[2,24,256]{2,1,0:T(8,128)S(1)}, f32[2,24,256]{2,1,0:T(8,128)S(1)}, u32[]{:S(2)}, u32[]{:S(2)}) collective-permute-start(f32[2,24,256]{2,1,0:T(8,128)S(1)} %slice_select_fusion.5), channel_id=1, source_target_pairs={{0,16},{8,24},{16,0},{24,8},{1,17},{9,25},{17,1},{25,9},{2,18},{10... | collective-permute-start | bytes 147464 | tf_op jit(solution)/shard_map/ppermute | solution.py:269
  112.9 8.5 %collective-permute-start.19 = (f32[2,24,256]{2,1,0:T(8,128)S(1)}, f32[2,24,256]{2,1,0:T(8,128)S(1)}, u32[]{:S(2)}, u32[]{:S(2)}) collective-permute-start(f32[2,24,256]{2,1,0:T(8,128)S(1)} %select_add_fusion.4), channel_id=1, source_target_pairs={{0,4},{1,5},{2,6},{3,7},{4,0},{5,1},{6,2},{7,3},{8,12},{9,13},{10,... | collective-permute-start | bytes 147464 | tf_op jit(solution)/shard_map/ppermute | solution.py:269
  119.4 4.2 %collective-permute-start.11 = (f32[2,24,256]{2,1,0:T(8,128)S(1)}, f32[2,24,256]{2,1,0:T(8,128)S(1)}, u32[]{:S(2)}, u32[]{:S(2)}) collective-permute-start(f32[2,24,256]{2,1,0:T(8,128)S(1)} %select_add_fusion.5), channel_id=1, source_target_pairs={{0,2},{1,3},{2,0},{3,1},{4,6},{5,7},{6,4},{7,5},{8,10},{9,11},{10,... | collective-permute-start | bytes 147464 | tf_op jit(solution)/shard_map/ppermute | solution.py:269
  121.4 4.2 %collective-permute-start.20 = (f32[2,24,256]{2,1,0:T(8,128)S(1)}, f32[2,24,256]{2,1,0:T(8,128)S(1)}, u32[]{:S(2)}, u32[]{:S(2)}) collective-permute-start(f32[2,24,256]{2,1,0:T(8,128)S(1)} %add.62), channel_id=1, source_target_pairs={{0,2},{1,3},{2,0},{3,1},{4,6},{5,7},{6,4},{7,5},{8,10},{9,11},{10,... | collective-permute-start | bytes 147464 | tf_op jit(solution)/shard_map/ppermute | solution.py:269
  123.5 5.6 %collective-permute-start.12 = (f32[2,24,256]{2,1,0:T(8,128)S(1)}, f32[2,24,256]{2,1,0:T(8,128)S(1)}, u32[]{:S(2)}, u32[]{:S(2)}) collective-permute-start(f32[2,24,256]{2,1,0:T(8,128)S(1)} %add.57), channel_id=1, source_target_pairs={{0,4},{1,5},{2,6},{3,7},{4,0},{5,1},{6,2},{7,3},{8,12},{9,13},{10,... | collective-permute-start | bytes 147464 | tf_op jit(solution)/shard_map/ppermute | solution.py:269
  125.6 5.1 %collective-permute-start.21 = (f32[2,24,256]{2,1,0:T(8,128)S(1)}, f32[2,24,256]{2,1,0:T(8,128)S(1)}, u32[]{:S(2)}, u32[]{:S(2)}) collective-permute-start(f32[2,24,256]{2,1,0:T(8,128)S(1)} %add.63), channel_id=1, source_target_pairs={{0,8},{8,0},{16,24},{24,16},{1,9},{9,1},{17,25},{25,17},{2,10},{10... | collective-permute-start | bytes 147464 | tf_op jit(solution)/shard_map/ppermute | solution.py:269
  129.1 4.2 %collective-permute-start.13 = (f32[2,24,256]{2,1,0:T(8,128)S(1)}, f32[2,24,256]{2,1,0:T(8,128)S(1)}, u32[]{:S(2)}, u32[]{:S(2)}) collective-permute-start(f32[2,24,256]{2,1,0:T(8,128)S(1)} %add.58), channel_id=1, source_target_pairs={{0,16},{8,24},{16,0},{24,8},{1,17},{9,25},{17,1},{25,9},{2,18},{10... | collective-permute-start | bytes 147464 | tf_op jit(solution)/shard_map/ppermute | solution.py:269
  130.8 4.7 %collective-permute-start.22 = (f32[4,24,256]{2,1,0:T(8,128)S(1)}, f32[4,24,256]{2,1,0:T(8,128)S(1)}, u32[]{:S(2)}, u32[]{:S(2)}) collective-permute-start(f32[4,24,256]{2,1,0:T(8,128)S(1)} %pad_maximum_fusion.7), channel_id=1, source_target_pairs={{0,16},{8,24},{16,0},{24,8},{1,17},{9,25},{17,1},{25,9},{2,18},{10... | collective-permute-start | bytes 294920 | tf_op jit(solution)/shard_map/ppermute | solution.py:269
  133.3 4.7 %collective-permute-start.14 = (f32[4,24,256]{2,1,0:T(8,128)S(1)}, f32[4,24,256]{2,1,0:T(8,128)S(1)}, u32[]{:S(2)}, u32[]{:S(2)}) collective-permute-start(f32[4,24,256]{2,1,0:T(8,128)S(1)} %pad_maximum_fusion.6), channel_id=1, source_target_pairs={{0,8},{8,0},{16,24},{24,16},{1,9},{9,1},{17,25},{25,17},{2,10},{10... | collective-permute-start | bytes 294920 | tf_op jit(solution)/shard_map/ppermute | solution.py:269
  135.5 2.6 %collective-permute-start.23 = (f32[8,24,256]{2,1,0:T(8,128)S(1)}, f32[8,24,256]{2,1,0:T(8,128)S(1)}, u32[]{:S(2)}, u32[]{:S(2)}) collective-permute-start(f32[8,24,256]{2,1,0:T(8,128)S(1)} %pad_maximum_fusion.4), channel_id=1, source_target_pairs={{0,1},{1,0},{2,3},{3,2},{4,5},{5,4},{6,7},{7,6},{8,9},{9,8},{10,11... | collective-permute-start | bytes 589832 | tf_op jit(solution)/shard_map/ppermute | solution.py:269
  138.0 1.5 %collective-permute-start.15 = (f32[8,24,256]{2,1,0:T(8,128)S(1)}, f32[8,24,256]{2,1,0:T(8,128)S(1)}, u32[]{:S(2)}, u32[]{:S(2)}) collective-permute-start(f32[8,24,256]{2,1,0:T(8,128)S(1)} %pad_maximum_fusion.3), channel_id=1, source_target_pairs={{0,1},{1,0},{2,3},{3,2},{4,5},{5,4},{6,7},{7,6},{8,9},{9,8},{10,11... | collective-permute-start | bytes 589832 | tf_op jit(solution)/shard_map/ppermute | solution.py:269

commit v8 on v7

--- a/solution.py
+++ b/solution.py
@@ -81,23 +81,23 @@
         for j in (1, 2, 0):
             for a, total in enumerate(mixed(j)):
                 at = slice(SUB * a, SUB * a + SUB)
-                qkv[j, at, lanes] = total
+                qkv[which, j, at, part] = total
                 if j == 2:
-                    xg[0, at, lanes] = qkv[1, at, lanes] * total
+                    xg[which, 0, at, part] = qkv[which, 1, at, part] * total
                 if j == 0:
-                    xg[1, at, lanes] = xs[3, pl.ds(SUB + a, SUB, stride=run), :] * total
+                    xg[which, 1, at, part] = xs[3, pl.ds(SUB + a, SUB, stride=run), :] * total
         for side, order, weight, blocks in (
             (0, range(run), we, blocks_e),
             (1, range(run - 1, -1, -1), wb, blocks_a),
         ):
             state = None
             for a in order:
-                x = xg[side, SUB * a : SUB * a + SUB, lanes]
+                x = xg[which, side, SUB * a : SUB * a + SUB, part]
                 if a >= own:
                     x = jnp.where(inside, x, 0.0)
                 state = [x] * poles if state is None else [decay[n] * state[n] + x for n in range(poles)]
             for n in range(poles):
-                blocks[n, :, lanes] = state[n]
+                blocks[which, n, :, part] = state[n]
             state = [state[n] * weight[n, :, part] for n in range(poles)]
             for n in range(0, poles, SUB):
                 ends[side, which, n : n + SUB, part] = folded(state[n : n + SUB])
@@ -106,26 +106,33 @@
     lax.fori_loop(0, p.shape[2] // LANES, tile, 0)
 
 
-def blocks_kernel(xg, blocks_e, blocks_a, near, skip, join_e, join_a, conv, from_e, from_a):
-    run = xg.shape[1] // SUB
-    rows = xg.shape[1] - SUB
+def blocks_kernel(
+    xg, blocks_e, blocks_a, near, skip, join_e, join_a, conv, from_e, from_a, skip_sum
+):
+    run = xg.shape[2] // SUB
+    rows = xg.shape[2] - SUB
     taps = near.shape[0] - run
-    poles, groups = blocks_e.shape[0], near.shape[1]
+    poles, groups = blocks_e.shape[1], near.shape[1]
     own = rows - run * (SUB - 1)
     tiles = groups // LANES
 
     def tile(lt, carry):
         lanes = pl.ds(pl.multiple_of(lt * LANES, LANES), LANES)
         part = pl.ds(pl.multiple_of(lax.rem(lt, tiles) * LANES, LANES), LANES)
+        which = lt // tiles
         inside = lax.broadcasted_iota(jnp.int32, (SUB, LANES), 0) < SUB - 1
         gain = spread(skip[0:1, lanes])
         lag = [spread(near[taps + m : taps + m + 1, part]) for m in range(run)]
         lag[0] = lag[0] + gain
-        x = [xg[0, SUB * a : SUB * a + SUB, lanes] for a in range(run)]
+        x = [xg[which, 0, SUB * a : SUB * a + SUB, part] for a in range(run)]
         for a in range(run):
-            conv[0, SUB * a : SUB * a + SUB, lanes] = added([lag[m] * x[a - m] for m in range(a + 1)])
-        x = [xg[1, SUB * a : SUB * a + SUB, lanes] for a in range(run)]
+            conv[which, 0, SUB * a : SUB * a + SUB, part] = added(
+                [lag[m] * x[a - m] for m in range(a + 1)]
+            )
+        gated = x
+        x = [xg[which, 1, SUB * a : SUB * a + SUB, part] for a in range(run)]
         masked = [x[a] if a < own else jnp.where(inside, x[a], 0.0) for a in range(run)]
+        skip_sum[which, :, part] = added([masked[a] * gated[a] for a in range(run)])
         past = [jnp.where(inside, 0.0, gain)] + [
             jnp.where(inside, 0.0, -spread(near[taps - m : taps - m + 1, part]))
             for m in range(1, taps - 1)
@@ -134,23 +141,23 @@
             terms = [lag[m] * masked[a + m] for m in range(run - a)]
             if own <= a < own + taps - 1:
                 terms = terms + [past[m] * x[a - m] for m in range(a - own + 1)]
-            conv[1, SUB * a : SUB * a + SUB, lanes] = added(terms)
+            conv[which, 1, SUB * a : SUB * a + SUB, part] = added(terms)
         for n in range(poles):
-            value = pltpu.roll(blocks_e[n, :, lanes], 1, 0) * join_e[0, n, :, part]
+            value = pltpu.roll(blocks_e[which, n, :, part], 1, 0) * join_e[0, n, :, part]
             for k, step in ((1, 1), (2, 2), (3, 4)):
                 value = value + pltpu.roll(value, step, 0) * join_e[k, n, :, part]
-            from_e[n, :, lanes] = value
-            value = pltpu.roll(blocks_a[n, :, lanes], SUB - 1, 0) * join_a[0, n, :, part]
+            from_e[which, n, :, part] = value
+            value = pltpu.roll(blocks_a[which, n, :, part], SUB - 1, 0) * join_a[0, n, :, part]
             for k, step in ((1, 1), (2, 2), (3, 4)):
                 value = value + pltpu.roll(value, SUB - step, 0) * join_a[k, n, :, part]
-            from_a[n, :, lanes] = value
+            from_a[which, n, :, part] = value
         return carry
 
-    lax.fori_loop(0, xg.shape[2] // LANES, tile, 0)
+    lax.fori_loop(0, xg.shape[0] * tiles, tile, 0)
 
 
 def final_kernel(
-    core, p, hx_low, hx_high, hi, u, qkv, conv, from_e, from_a, both, found, other, filt, f1, f_all, cz, cy,
+    core, p, hx_low, hx_high, hi, u, qkv, conv, from_e, from_a, skip_sum, both, found, other, filt, f1, f_all, cz, cy,
     output, grad_p, sums, ps, us, gs, os, es,
 ):
     rows = p.shape[1]
@@ -187,18 +194,13 @@
         decay = [spread(f1[n : n + 1, part]) for n in range(poles)]
 
         state = [
-            from_e[n, :, lanes] + cz[n, :, part] * spread(es[0, n : n + 1])
+            from_e[which, n, :, part] + cz[n, :, part] * spread(es[0, n : n + 1])
             for n in range(poles)
         ]
-        skip_sum = None
         for a in range(run):
             at = slice(SUB * a, SUB * a + SUB)
-            query, upstream = qkv[0, at, lanes], us[pl.ds(a, SUB, stride=run), :]
-            term = (qkv[1, at, lanes] * qkv[2, at, lanes]) * (query * upstream)
-            if a >= own:
-                term = jnp.where(inside, term, 0.0)
-            skip_sum = term if a == 0 else skip_sum + term
-            filtered = conv[0, at, lanes] + added(list(state))
+            query, upstream = qkv[which, 0, at, part], us[pl.ds(a, SUB, stride=run), :]
+            filtered = conv[which, 0, at, part] + added(list(state))
             os[pl.ds(a, SUB, stride=run), :] = query * filtered
             gs[0, pl.ds(a, SUB, stride=run), :] = upstream * filtered
             if a + 1 < run:
@@ -206,18 +208,17 @@
         output[:, lanes] = os[0:rows].astype(BF16)
 
         state = [
-            from_a[n, :, lanes] + cy[n, :, part] * spread(es[1, n : n + 1])
+            from_a[which, n, :, part] + cy[n, :, part] * spread(es[1, n : n + 1])
             for n in range(poles)
         ]
         for a in range(run - 1, -1, -1):
             at = slice(SUB * a, SUB * a + SUB)
-            grad = conv[1, at, lanes] + added(list(state))
-            gs[1, pl.ds(a, SUB, stride=run), :] = grad * qkv[2, at, lanes]
-            gs[2, pl.ds(a, SUB, stride=run), :] = grad * qkv[1, at, lanes]
+            grad = conv[which, 1, at, part] + added(list(state))
+            gs[1, pl.ds(a, SUB, stride=run), :] = grad * qkv[which, 2, at, part]
+            gs[2, pl.ds(a, SUB, stride=run), :] = grad * qkv[which, 1, at, part]
             if a:
                 state = [state[n] * decay[n] for n in range(poles)]
 
-        rest = []
         for j in range(3):
             tap = [spread(filt[j, i : i + 1, lanes]) for i in range(taps)]
             grads = [gs[j, pl.ds(a, SUB, stride=run), :] for a in range(taps - 1)]
@@ -233,10 +234,9 @@
                     term = grad * views[-1 - i]
                     sums_of[i] = term if a == 0 else sums_of[i] + term
             grad_p[j, :, lanes] = os[0:rows].astype(BF16)
-            rest = rest + sums_of
-        rest = rest + [skip_sum] + [jnp.zeros((SUB, LANES), F32)] * (-(len(rest) + 1) % SUB)
-        for n in range(0, len(rest), SUB):
-            sums[piece, n : n + SUB, spot] = folded(rest[n : n + SUB])
+            extra = [skip_sum[which, :, part]] + [jnp.zeros((SUB, LANES), F32)] * (SUB - taps)
+            extra = extra[: SUB - taps] if j == 0 else extra[1 : SUB - taps + 1]
+            sums[piece, j * SUB : j * SUB + SUB, spot] = folded(sums_of + extra)
         return carry
 
     lax.fori_loop(0, p.shape[2] // LANES, tile, 0)
@@ -385,7 +385,13 @@
     halved = pl.BlockSpec(
         (2, each, poles, groups), lambda w: (0, lax.rem(w, width // each // 2), 0, 0)
     )
-    state_shape = shape_of((poles, SUB, channels), F32)
+    state_shape = shape_of((width, poles, SUB, groups), F32)
+    pair_shape = shape_of((width, 2, held, groups), F32)
+
+    def by_block(*shape, count=each, first=0):
+        return pl.BlockSpec((count,) + shape, lambda w: (w + first,) + (0,) * len(shape))
+
+    state_spec = by_block(poles, SUB, groups)
     qkv, xg, blocks_e, blocks_a, ends = pl.pallas_call(
         states_kernel,
         grid=(width // each,),
@@ -395,11 +401,11 @@
             fixed(f1), fixed(we), fixed(wb),
         ],
         out_specs=[
-            by_w(3, held), by_w(2, held), by_w(poles, SUB), by_w(poles, SUB),
+            by_block(3, held, groups), by_block(2, held, groups), state_spec, state_spec,
             ends_spec,
         ],
         out_shape=[
-            shape_of((3, held, channels), F32), shape_of((2, held, channels), F32),
+            shape_of((width, 3, held, groups), F32), pair_shape,
             state_shape, state_shape, shape_of((2, width, poles, groups), F32),
         ],
         scratch_shapes=[pltpu.VMEM((4, held + SUB, LANES), F32)],
@@ -410,41 +416,46 @@
     many = 2 if width % 2 == 0 else 1
 
     def blocks(first, last):
-        def at_w(*shape):
-            axis = len(shape)
-            return pl.BlockSpec(shape + (many * groups,), lambda w: (0,) * axis + (w + first,))
+        states = by_block(poles, SUB, groups, count=many, first=first)
+        pairs = by_block(2, held, groups, count=many, first=first)
 
         def call(sent, kept):
             close, _ = lax.optimization_barrier((near, sent))
-            return pl.pallas_call(
+            held_before = kept or (xg, blocks_e, blocks_a)
+            out = pl.pallas_call(
                 blocks_kernel,
                 grid=(last - first,),
                 in_specs=[
-                    at_w(2, held), at_w(poles, SUB), at_w(poles, SUB), fixed(near), at_w(1),
+                    pairs, states, states, fixed(near),
+                    pl.BlockSpec((1, many * groups), lambda w: (0, w + first)),
                     fixed(join_e), fixed(join_a),
                 ],
-                out_specs=[at_w(2, held), at_w(poles, SUB), at_w(poles, SUB)],
-                out_shape=[shape_of((2, held, channels), F32), state_shape, state_shape],
+                out_specs=[pairs, states, states, by_block(SUB, groups, count=many)],
+                out_shape=[
+                    pair_shape, state_shape, state_shape,
+                    shape_of(((last - first) * many, SUB, groups), F32),
+                ],
                 input_output_aliases={0: 0, 1: 1, 2: 2},
                 compiler_params=params,
                 cost_estimate=pl.CostEstimate(
                     flops=60 * rows * channels, bytes_accessed=35 * 2**20, transcendentals=0
                 ),
                 name="blocks",
-            )(*(kept or (xg, blocks_e, blocks_a)), close, skip_gain[None], join_e, join_a)
+            )(*held_before[:3], close, skip_gain[None], join_e, join_a)
+            return [*out[:3], jnp.concatenate([*held_before[3:], out[3]], axis=0)]
 
         return call
 
     steps = width // many
     cut = (steps + 1) // 3
     other, chip_e, chip_a = joined(ends, f_all)
-    before, after, (conv, from_e, from_a) = scanned(
+    before, after, (conv, from_e, from_a, skip_sum) = scanned(
         chip_e, chip_a, f_all, (blocks(0, cut), blocks(cut, steps))
     )
     both = jnp.stack([before, after])
     found = swapped(both)
 
-    count = 3 * taps + 3
+    count = 3 * SUB
     split = 2 if groups % (2 * LANES) == 0 else 1
     scratch = [
         pltpu.VMEM((3, held + SUB, LANES), F32),
@@ -458,8 +469,9 @@
         grid=(width // each,),
         in_specs=[
             pl.BlockSpec(memory_space=pltpu.SMEM),
-            by_w(3, rows), by_w(2, SUB), by_w(2, SUB), by_w(4, SUB), by_w(rows), by_w(3, held), by_w(2, held),
-            by_w(poles, SUB), by_w(poles, SUB), halved, halved, ends_spec,
+            by_w(3, rows), by_w(2, SUB), by_w(2, SUB), by_w(4, SUB), by_w(rows),
+            by_block(3, held, groups), by_block(2, held, groups), state_spec, state_spec,
+            by_block(SUB, groups), halved, halved, ends_spec,
             by_w(3, taps), fixed(f1), fixed(f_all), fixed(cz), fixed(cy),
         ],
         out_specs=[
@@ -475,13 +487,12 @@
         compiler_params=params,
         name="final",
     )(
-        core[None], p, *hx, hi, u, qkv, conv, from_e, from_a, both, found, other, short_filter,
+        core[None], p, *hx, hi, u, qkv, conv, from_e, from_a, skip_sum, both, found, other, short_filter,
         f1, f_all, cz, cy,
     )
 
-    total = summed(sums).transpose(1, 0, 2).reshape(count, channels)
-    grad_short = total[: 3 * taps].reshape(3, taps, channels)
-    grad_skip = total[3 * taps]
+    total = summed(sums).transpose(1, 0, 2).reshape(3, SUB, channels)
+    grad_short, grad_skip = total[:, :taps], total[0, taps]
     return output[None], grad_p.transpose(1, 0, 2)[None], grad_short, grad_skip
 
 

time: 143 us -> 141 us (0.986)
  no operation moved by 1% of the time
where the time goes in v8:
time: 141 us; the launch traced here: 140 us
  Pallas kernels  74.9 us (53%)
  starting transfers between devices  38 us (27%)
  waiting for transfers between devices  18 us (13%)
  other arithmetic  4.56 us (3%)
  local copies, waits for them, and re-layouts  3.76 us (3%)
    pallas_call x1, Pallas kernels, local(): pl.pallas_call(final_kernel, grid=(width // each,), in_specs=[pl.BlockSpe...  32.5 us
    ppermute x17, starting transfers between devices, paired(): lax.ppermute(value, axis, [(source, source ^ step) for source in lines or...  24.4 us
    pallas_call x1, Pallas kernels, local(): pl.pallas_call(states_kernel, grid=(width // each,), in_specs=[pl.BlockSp...  22.3 us
    pallas_call x2, Pallas kernels, call(): pl.pallas_call(blocks_kernel, grid=(last - first,), in_specs=[pairs, stat...  20.1 us
    ppermute x17, waiting for transfers between devices, paired(): lax.ppermute(value, axis, [(source, source ^ step) for source in lines or...  14.5 us
    ppermute x3, starting transfers between devices, swapped(): return lax.ppermute(value, 'ctx', [(s, s ^ 1) for s in range(count)])  10.1 us
    ppermute x3, waiting for transfers between devices, swapped(): return lax.ppermute(value, 'ctx', [(s, s ^ 1) for s in range(count)])  3.55 us
  transfers between devices with their start and end apart: 24, of which 14 were waited for; matrix products, arithmetic and copies ran while one was open for 2% of the time, Pallas kernels for 14%

profile of v8, /device:TPU:0, one launch (start us, length us, event | category | flops | bytes accessed | tf_op | source)
XLA Modules:
  0.0 140.4 jit_solution(5817486855481724690)
XLA Ops:
  0.6 0.0 copy-start.13
  0.7 1.1 fusion.9
  1.8 1.2 fusion.8
  3.0 0.1 broadcast_select_fusion.2
  3.2 0.7 collective-permute-start.1
  3.8 0.7 collective-permute-start
  4.5 5.7 %collective-permute-start.2 = (bf16[4,8,8192]{2,1,0:T(8,128)(2,1)S(1)}, bf16[4,8,8192]{2,1,0:T(8,128)(2,1)S(1)}, u32[]{:S(2)}, u32[]{:S(2)}) collective-permute-start(bf16[4,8,8192]{2,1,0:T(8,128)(2,1)S(1)} %get-tuple-element.72), channel_id=1, source_target_pairs={{0,1},{1,0},{2,3},{3,2},{4,5},{5,4},{6,7},{7,6},{8,9},{9,8},{10,11... | collective-permute-start | bytes 1572872 | tf_op jit(solution)/shard_map/ppermute | solution.py:253
  10.2 0.2 multiply_exponential_fusion
  10.6 1.2 collective-permute-done.2.hi
  11.8 22.3 %states.1 = (f32[16,3,136,512]{3,2,1,0:T(8,128)}, f32[16,2,136,512]{3,2,1,0:T(8,128)}, f32[16,16,8,512]{3,2,1,0:T(8,128)}, f32[16,16,8,512]{3,2,1,0:T(8,128)}, f32[2,16,16,512]{3,2,1,0:T(8,128)}) custom-call(s32[1]{0:T(128)} %bitcast.core, bf16[3,128,8192]{2,1,0:T(8,128)(2,1)} %bitcast.83, bf16[2,8,8192]{2,1,0:T(8,128)(2,1)S(1)} %collective-permute-done.hx_low, ...), custom_call_target="tpu_custom_call" | custom-call | tf_op jit(solution)/shard_map/states/pallas_call | solution.py:395
  34.1 4.3 %collective-permute-start.3 = (f32[2,16,16,512]{3,2,1,0:T(8,128)}, f32[2,16,16,512]{3,2,1,0:T(8,128)S(1)}, u32[]{:S(2)}, u32[]{:S(2)}) collective-permute-start(f32[2,16,16,512]{3,2,1,0:T(8,128)} %get-tuple-element.34), channel_id=1, source_target_pairs={{0,1},{1,0},{2,3},{3,2},{4,5},{5,4},{6,7},{7,6},{8,9},{9,8},{10,11... | collective-permute-start | bytes 3145736 | tf_op jit(solution)/shard_map/ppermute | solution.py:253
  38.4 0.1 multiply_exponential_fusion.1
  38.5 0.8 slice_multiply_fusion
  39.3 1.0 multiply_reduce_fusion.near
  40.3 0.6 collective-permute-done.3.other
  40.9 1.2 dynamic-slice_select_fusion.1
  42.1 0.1 broadcast_select_fusion.4
  42.2 1.7 %collective-permute-start.4 = (f32[8,16,512]{2,1,0:T(8,128)S(1)}, f32[8,16,512]{2,1,0:T(8,128)S(1)}, u32[]{:S(2)}, u32[]{:S(2)}) collective-permute-start(f32[8,16,512]{2,1,0:T(8,128)S(1)} %broadcast_select_fusion.4), channel_id=1, source_target_pairs={{0,2},{1,3},{2,0},{3,1},{4,6},{5,7},{6,4},{7,5},{8,10},{9,11},{10,... | collective-permute-start | bytes 786440 | tf_op jit(solution)/shard_map/ppermute | solution.py:269
  43.8 0.3 broadcast_select_fusion
  44.2 8.2 %blocks.2 = (f32[16,2,136,512]{3,2,1,0:T(8,128)}, f32[16,16,8,512]{3,2,1,0:T(8,128)}, f32[16,16,8,512]{3,2,1,0:T(8,128)}, f32[6,8,512]{2,1,0:T(8,128)S(1)}) custom-call(f32[16,2,136,512]{3,2,1,0:T(8,128)} %get-tuple-element.35.xg, f32[16,16,8,512]{3,2,1,0:T(8,128)} %get-tuple-element.36.blocks_e, ...), custom_call_target="tpu_custom_call", output_to_operand_aliasing={{0}: (0, {}), {1}: (1, {}), {2}: (2, {})} | custom-call | flops 62914560 | bytes 36700160 | tf_op jit(solution)/shard_map/blocks/pallas_call | solution.py:425
  52.4 0.1 multiply_add_fusion.1
  52.5 1.4 %collective-permute-start.6 = (f32[8,16,512]{2,1,0:T(8,128)S(1)}, f32[8,16,512]{2,1,0:T(8,128)S(1)}, u32[]{:S(2)}, u32[]{:S(2)}) collective-permute-start(f32[8,16,512]{2,1,0:T(8,128)S(1)} %multiply_add_fusion.1), channel_id=1, source_target_pairs={{2,6},{3,7},{4,0},{5,1},{10,14},{11,15},{12,8},{13,9},{18,22},{19,... | collective-permute-start | bytes 786440 | tf_op jit(solution)/shard_map/ppermute | solution.py:283
  54.0 0.7 collective-permute-start.5
  54.7 11.9 %blocks.3 = (f32[16,2,136,512]{3,2,1,0:T(8,128)}, f32[16,16,8,512]{3,2,1,0:T(8,128)}, f32[16,16,8,512]{3,2,1,0:T(8,128)}, f32[10,8,512]{2,1,0:T(8,128)S(1)}) custom-call(f32[16,2,136,512]{3,2,1,0:T(8,128)} %get-tuple-element.44.xg, f32[16,16,8,512]{3,2,1,0:T(8,128)} %get-tuple-element.45.blocks_e, ...), custom_call_target="tpu_custom_call", output_to_operand_aliasing={{0}: (0, {}), {1}: (1, {}), {2}: (2, {})} | custom-call | flops 62914560 | bytes 36700160 | tf_op jit(solution)/shard_map/blocks/pallas_call | solution.py:425
  66.6 0.1 select_bitcast_fusion.1
  66.8 0.1 collective-permute-start.7
  66.9 0.1 fusion
  67.0 1.8 %collective-permute-done.7.found = f32[2,8,16,512]{3,2,1,0:T(8,128)S(1)} collective-permute-done((f32[2,8,16,512]{3,2,1,0:T(8,128)S(1)}, f32[2,8,16,512]{3,2,1,0:T(8,128)S(1)}, u32[]{:S(2)}, u32[]{:S(2)}) %collective-permute-start.7) | collective-permute-done | bytes 524320 | tf_op jit(solution)/shard_map/ppermute | solution.py:253
  68.7 32.5 %final.1 = (bf16[128,8192]{1,0:T(8,128)(2,1)}, bf16[3,128,8192]{2,1,0:T(8,128)(2,1)}, f32[32,24,256]{2,1,0:T(8,128)S(1)}) custom-call(s32[1]{0:T(128)} %bitcast.core, bf16[3,128,8192]{2,1,0:T(8,128)(2,1)} %bitcast.84, bf16[2,8,8192]{2,1,0:T(8,128)(2,1)S(1)} %copy-done.5, bf16[2,8,8192]{2,1,0:T(8,128)(2,1)S(1)} %copy-done.3, ...), custom_call_target="tpu_custom_call" | custom-call | tf_op jit(solution)/shard_map/final/pallas_call | solution.py:467
  101.2 0.1 slice_select_fusion.1
  101.3 0.2 collective-permute-start.8
  101.5 0.4 collective-permute-start.16
  101.8 0.9 collective-permute-done.8
  102.8 0.3 collective-permute-done.16
  103.1 0.1 select_add_fusion.1
  103.2 1.6 %collective-permute-start.17 = (f32[4,24,256]{2,1,0:T(8,128)S(1)}, f32[4,24,256]{2,1,0:T(8,128)S(1)}, u32[]{:S(2)}, u32[]{:S(2)}) collective-permute-start(f32[4,24,256]{2,1,0:T(8,128)S(1)} %slice_select_fusion.2), channel_id=1, source_target_pairs={{0,16},{8,24},{16,0},{24,8},{1,17},{9,25},{17,1},{25,9},{2,18},{10... | collective-permute-start | bytes 294920 | tf_op jit(solution)/shard_map/ppermute | solution.py:269
  104.8 1.6 %collective-permute-start.9 = (f32[4,24,256]{2,1,0:T(8,128)S(1)}, f32[4,24,256]{2,1,0:T(8,128)S(1)}, u32[]{:S(2)}, u32[]{:S(2)}) collective-permute-start(f32[4,24,256]{2,1,0:T(8,128)S(1)} %slice_select_fusion.3), channel_id=1, source_target_pairs={{0,8},{8,0},{16,24},{24,16},{1,9},{9,1},{17,25},{25,17},{2,10},{10... | collective-permute-start | bytes 294920 | tf_op jit(solution)/shard_map/ppermute | solution.py:269
  106.3 1.8 %collective-permute-done.17 = f32[4,24,256]{2,1,0:T(8,128)S(1)} collective-permute-done((f32[4,24,256]{2,1,0:T(8,128)S(1)}, f32[4,24,256]{2,1,0:T(8,128)S(1)}, u32[]{:S(2)}, u32[]{:S(2)}) %collective-permute-start.17) | collective-permute-done | bytes 98336 | tf_op jit(solution)/shard_map/ppermute | solution.py:269
  108.2 1.6 %collective-permute-start.18 = (f32[2,24,256]{2,1,0:T(8,128)S(1)}, f32[2,24,256]{2,1,0:T(8,128)S(1)}, u32[]{:S(2)}, u32[]{:S(2)}) collective-permute-start(f32[2,24,256]{2,1,0:T(8,128)S(1)} %slice_select_fusion.4), channel_id=1, source_target_pairs={{0,8},{8,0},{16,24},{24,16},{1,9},{9,1},{17,25},{25,17},{2,10},{10... | collective-permute-start | bytes 147464 | tf_op jit(solution)/shard_map/ppermute | solution.py:269
  109.8 1.6 %collective-permute-start.10 = (f32[2,24,256]{2,1,0:T(8,128)S(1)}, f32[2,24,256]{2,1,0:T(8,128)S(1)}, u32[]{:S(2)}, u32[]{:S(2)}) collective-permute-start(f32[2,24,256]{2,1,0:T(8,128)S(1)} %slice_select_fusion.5), channel_id=1, source_target_pairs={{0,16},{8,24},{16,0},{24,8},{1,17},{9,25},{17,1},{25,9},{2,18},{10... | collective-permute-start | bytes 147464 | tf_op jit(solution)/shard_map/ppermute | solution.py:269
  111.4 1.0 collective-permute-done.18
  112.4 6.4 %collective-permute-start.19 = (f32[2,24,256]{2,1,0:T(8,128)S(1)}, f32[2,24,256]{2,1,0:T(8,128)S(1)}, u32[]{:S(2)}, u32[]{:S(2)}) collective-permute-start(f32[2,24,256]{2,1,0:T(8,128)S(1)} %select_add_fusion.4), channel_id=1, source_target_pairs={{0,4},{1,5},{2,6},{3,7},{4,0},{5,1},{6,2},{7,3},{8,12},{9,13},{10,... | collective-permute-start | bytes 147464 | tf_op jit(solution)/shard_map/ppermute | solution.py:269
  118.8 0.6 collective-permute-start.11
  119.4 1.5 %collective-permute-done.19 = f32[2,24,256]{2,1,0:T(8,128)S(1)} collective-permute-done((f32[2,24,256]{2,1,0:T(8,128)S(1)}, f32[2,24,256]{2,1,0:T(8,128)S(1)}, u32[]{:S(2)}, u32[]{:S(2)}) %collective-permute-start.19) | collective-permute-done | bytes 49184 | tf_op jit(solution)/shard_map/ppermute | solution.py:269
  120.9 2.0 %collective-permute-start.20 = (f32[2,24,256]{2,1,0:T(8,128)S(1)}, f32[2,24,256]{2,1,0:T(8,128)S(1)}, u32[]{:S(2)}, u32[]{:S(2)}) collective-permute-start(f32[2,24,256]{2,1,0:T(8,128)S(1)} %add.62), channel_id=1, source_target_pairs={{0,2},{1,3},{2,0},{3,1},{4,6},{5,7},{6,4},{7,5},{8,10},{9,11},{10,... | collective-permute-start | bytes 147464 | tf_op jit(solution)/shard_map/ppermute | solution.py:269
  122.8 0.1 collective-permute-done.11
  123.0 2.0 %collective-permute-start.12 = (f32[2,24,256]{2,1,0:T(8,128)S(1)}, f32[2,24,256]{2,1,0:T(8,128)S(1)}, u32[]{:S(2)}, u32[]{:S(2)}) collective-permute-start(f32[2,24,256]{2,1,0:T(8,128)S(1)} %add.57), channel_id=1, source_target_pairs={{0,4},{1,5},{2,6},{3,7},{4,0},{5,1},{6,2},{7,3},{8,12},{9,13},{10,... | collective-permute-start | bytes 147464 | tf_op jit(solution)/shard_map/ppermute | solution.py:269
  125.0 0.0 collective-permute-done.20
  125.0 1.6 %collective-permute-start.21 = (f32[2,24,256]{2,1,0:T(8,128)S(1)}, f32[2,24,256]{2,1,0:T(8,128)S(1)}, u32[]{:S(2)}, u32[]{:S(2)}) collective-permute-start(f32[2,24,256]{2,1,0:T(8,128)S(1)} %add.63), channel_id=1, source_target_pairs={{0,8},{8,0},{16,24},{24,16},{1,9},{9,1},{17,25},{25,17},{2,10},{10... | collective-permute-start | bytes 147464 | tf_op jit(solution)/shard_map/ppermute | solution.py:269
  126.6 2.0 %collective-permute-done.12 = f32[2,24,256]{2,1,0:T(8,128)S(1)} collective-permute-done((f32[2,24,256]{2,1,0:T(8,128)S(1)}, f32[2,24,256]{2,1,0:T(8,128)S(1)}, u32[]{:S(2)}, u32[]{:S(2)}) %collective-permute-start.12) | collective-permute-done | bytes 49184 | tf_op jit(solution)/shard_map/ppermute | solution.py:269
  128.6 1.6 %collective-permute-start.13 = (f32[2,24,256]{2,1,0:T(8,128)S(1)}, f32[2,24,256]{2,1,0:T(8,128)S(1)}, u32[]{:S(2)}, u32[]{:S(2)}) collective-permute-start(f32[2,24,256]{2,1,0:T(8,128)S(1)} %add.58), channel_id=1, source_target_pairs={{0,16},{8,24},{16,0},{24,8},{1,17},{9,25},{17,1},{25,9},{2,18},{10... | collective-permute-start | bytes 147464 | tf_op jit(solution)/shard_map/ppermute | solution.py:269
  130.2 0.6 collective-permute-start.22
  130.8 1.9 %collective-permute-done.13 = f32[2,24,256]{2,1,0:T(8,128)S(1)} collective-permute-done((f32[2,24,256]{2,1,0:T(8,128)S(1)}, f32[2,24,256]{2,1,0:T(8,128)S(1)}, u32[]{:S(2)}, u32[]{:S(2)}) %collective-permute-start.13) | collective-permute-done | bytes 49184 | tf_op jit(solution)/shard_map/ppermute | solution.py:269
  132.8 1.0 collective-permute-start.14
  133.8 1.1 collective-permute-done.22
  134.9 0.1 collective-permute-start.23
  135.0 2.4 %collective-permute-done.14 = f32[4,24,256]{2,1,0:T(8,128)S(1)} collective-permute-done((f32[4,24,256]{2,1,0:T(8,128)S(1)}, f32[4,24,256]{2,1,0:T(8,128)S(1)}, u32[]{:S(2)}, u32[]{:S(2)}) %collective-permute-start.14) | collective-permute-done | bytes 98336 | tf_op jit(solution)/shard_map/ppermute | solution.py:269
  137.5 0.1 collective-permute-start.15
  137.6 1.4 collective-permute-done.15
  139.0 0.1 maximum_bitcast_fusion
  139.1 0.3 copy.22
  139.3 0.1 reshape.25
  139.5 0.7 slice.145
  140.2 0.2 copy-done.9
  (73 shorter events, 0.6 us)
Async XLA Ops:
  0.6 9.6 %copy-start.13 = (f32[4,8]{1,0:T(4,128)S(1)}, f32[4,8]{1,0:T(4,128)}, u32[]{:S(2)}) copy-start(f32[4,8]{1,0:T(4,128)} %constant.74) | copy-start | bytes 388
  0.6 11.1 %copy-start = (bf16[1,128,8192]{2,1,0:T(8,128)(2,1)S(1)}, bf16[1,128,8192]{2,1,0:T(8,128)(2,1)}, u32[]{:S(2)}) copy-start(bf16[1,128,8192]{2,1,0:T(8,128)(2,1)} %param.16) | copy-start | bytes 6291460
  0.7 9.6 %copy-start.11 = (f32[512,16]{0,1:T(8,128)S(1)}, f32[512,16]{0,1:T(8,128)}, u32[]{:S(2)}) copy-start(f32[512,16]{0,1:T(8,128)} %param.14) | copy-start | bytes 98308
  0.7 11.1 %copy-start.1 = (f32[3,7,8192]{2,1,0:T(8,128)S(1)}, f32[3,7,8192]{2,1,0:T(8,128)}, u32[]{:S(2)}) copy-start(f32[3,7,8192]{2,1,0:T(8,128)} %filt.3) | copy-start | bytes 2064388
  0.7 9.8 %copy-start.12 = (f32[512,16]{0,1:T(8,128)S(1)}, f32[512,16]{0,1:T(8,128)}, u32[]{:S(2)}) copy-start(f32[512,16]{0,1:T(8,128)} %param.14) | copy-start | bytes 98308
  3.2 7.4 %collective-permute-start.1 = (bf16[2,8,8192]{2,1,0:T(8,128)(2,1)S(1)}, bf16[2,8,8192]{2,1,0:T(8,128)(2,1)S(1)}, u32[]{:S(2)}, u32[]{:S(2)}) collective-permute-start(bf16[2,8,8192]{2,1,0:T(8,128)(2,1)S(1)} %get-tuple-element.80), channel_id=1, source_target_pairs={{1,2},{3,4},{5,6},{2,1},{4,3},{6,5},{9,10},{11,12},{13,14},{10,9},... | collective-permute-start | bytes 786440 | tf_op jit(solution)/shard_map/ppermute | solution.py:349
  3.8 6.7 %collective-permute-start = (bf16[2,8,8192]{2,1,0:T(8,128)(2,1)S(1)}, bf16[2,8,8192]{2,1,0:T(8,128)(2,1)S(1)}, u32[]{:S(2)}, u32[]{:S(2)}) collective-permute-start(bf16[2,8,8192]{2,1,0:T(8,128)(2,1)S(1)} %get-tuple-element.81), channel_id=1, source_target_pairs={{1,2},{3,4},{5,6},{2,1},{4,3},{6,5},{9,10},{11,12},{13,14},{10,9},... | collective-permute-start | bytes 786440 | tf_op jit(solution)/shard_map/ppermute | solution.py:349
  4.5 7.2 %collective-permute-start.2 = (bf16[4,8,8192]{2,1,0:T(8,128)(2,1)S(1)}, bf16[4,8,8192]{2,1,0:T(8,128)(2,1)S(1)}, u32[]{:S(2)}, u32[]{:S(2)}) collective-permute-start(bf16[4,8,8192]{2,1,0:T(8,128)(2,1)S(1)} %get-tuple-element.72), channel_id=1, source_target_pairs={{0,1},{1,0},{2,3},{3,2},{4,5},{5,4},{6,7},{7,6},{8,9},{9,8},{10,11... | collective-permute-start | bytes 1572872 | tf_op jit(solution)/shard_map/ppermute | solution.py:253
  10.5 1.3 copy-start.7
  10.6 23.5 %copy-start.2 = (bf16[2,8,8192]{2,1,0:T(8,128)(2,1)}, bf16[2,8,8192]{2,1,0:T(8,128)(2,1)S(1)}, u32[]{:S(2)}) copy-start(bf16[2,8,8192]{2,1,0:T(8,128)(2,1)S(1)} %collective-permute-done.1.hx_high) | copy-start | bytes 786436
  10.6 23.5 %copy-start.4 = (bf16[2,8,8192]{2,1,0:T(8,128)(2,1)}, bf16[2,8,8192]{2,1,0:T(8,128)(2,1)S(1)}, u32[]{:S(2)}) copy-start(bf16[2,8,8192]{2,1,0:T(8,128)(2,1)S(1)} %collective-permute-done.hx_low) | copy-start | bytes 786436
  11.8 26.6 %copy-start.14 = (f32[4]{0:T(128)S(1)}, f32[4]{0:T(128)}, u32[]{:S(2)}) copy-start(f32[4]{0:T(128)} %constant.77) | copy-start | bytes 52
  11.8 27.5 %copy-start.17 = (f32[24]{0:T(128)S(1)}, f32[24]{0:T(128)}, u32[]{:S(2)}) copy-start(f32[24]{0:T(128)} %constant.75) | copy-start | bytes 292
  34.0 9.8 %copy-start.15 = (pred[4,8]{1,0:T(4,128)(4,1)S(1)}, pred[4,8]{1,0:T(4,128)(4,1)}, u32[]{:S(2)}) copy-start(pred[4,8]{1,0:T(4,128)(4,1)} %constant.78) | copy-start | bytes 100
  34.0 9.8 %copy-start.16 = (pred[4,8]{1,0:T(4,128)(4,1)S(1)}, pred[4,8]{1,0:T(4,128)(4,1)}, u32[]{:S(2)}) copy-start(pred[4,8]{1,0:T(4,128)(4,1)} %constant.76) | copy-start | bytes 100
  34.1 10.1 %copy-start.6 = (f32[8192]{0:T(1024)S(1)}, f32[8192]{0:T(1024)}, u32[]{:S(2)}) copy-start(f32[8192]{0:T(1024)} %param.15) | copy-start | bytes 98308
  34.1 6.8 %collective-permute-start.3 = (f32[2,16,16,512]{3,2,1,0:T(8,128)}, f32[2,16,16,512]{3,2,1,0:T(8,128)S(1)}, u32[]{:S(2)}, u32[]{:S(2)}) collective-permute-start(f32[2,16,16,512]{3,2,1,0:T(8,128)} %get-tuple-element.34), channel_id=1, source_target_pairs={{0,1},{1,0},{2,3},{3,2},{4,5},{5,4},{6,7},{7,6},{8,9},{9,8},{10,11... | collective-permute-start | bytes 3145736 | tf_op jit(solution)/shard_map/ppermute | solution.py:253
  42.2 10.2 %collective-permute-start.4 = (f32[8,16,512]{2,1,0:T(8,128)S(1)}, f32[8,16,512]{2,1,0:T(8,128)S(1)}, u32[]{:S(2)}, u32[]{:S(2)}) collective-permute-start(f32[8,16,512]{2,1,0:T(8,128)S(1)} %broadcast_select_fusion.4), channel_id=1, source_target_pairs={{0,2},{1,3},{2,0},{3,1},{4,6},{5,7},{6,4},{7,5},{8,10},{9,11},{10,... | collective-permute-start | bytes 786440 | tf_op jit(solution)/shard_map/ppermute | solution.py:269
  52.5 14.4 %copy-start.8 = (f32[4,16,8,512]{3,2,1,0:T(8,128)S(1)}, f32[4,16,8,512]{3,2,1,0:T(8,128)}, u32[]{:S(2)}) copy-start(f32[4,16,8,512]{3,2,1,0:T(8,128)} %copy-done.7) | copy-start | bytes 3145732
  52.5 14.4 %copy-start.10 = (f32[512,16]{0,1:T(8,128)S(1)}, f32[512,16]{0,1:T(8,128)}, u32[]{:S(2)}) copy-start(f32[512,16]{0,1:T(8,128)} %param.13) | copy-start | bytes 98308
  52.5 14.1 %collective-permute-start.6 = (f32[8,16,512]{2,1,0:T(8,128)S(1)}, f32[8,16,512]{2,1,0:T(8,128)S(1)}, u32[]{:S(2)}, u32[]{:S(2)}) collective-permute-start(f32[8,16,512]{2,1,0:T(8,128)S(1)} %multiply_add_fusion.1), channel_id=1, source_target_pairs={{2,6},{3,7},{4,0},{5,1},{10,14},{11,15},{12,8},{13,9},{18,22},{19,... | collective-permute-start | bytes 786440 | tf_op jit(solution)/shard_map/ppermute | solution.py:283
  54.0 12.6 %collective-permute-start.5 = (f32[8,16,512]{2,1,0:T(8,128)S(1)}, f32[8,16,512]{2,1,0:T(8,128)S(1)}, u32[]{:S(2)}, u32[]{:S(2)}) collective-permute-start(f32[8,16,512]{2,1,0:T(8,128)S(1)} %multiply_add_fusion.1), channel_id=1, source_target_pairs={{2,4},{3,5},{4,2},{5,3},{10,12},{11,13},{12,10},{13,11},{18,20},{1... | collective-permute-start | bytes 786440 | tf_op jit(solution)/shard_map/ppermute | solution.py:282
  66.6 2.2 %copy-start.3 = (bf16[2,8,8192]{2,1,0:T(8,128)(2,1)S(1)}, bf16[2,8,8192]{2,1,0:T(8,128)(2,1)}, u32[]{:S(2)}) copy-start(bf16[2,8,8192]{2,1,0:T(8,128)(2,1)} %copy-done.2) | copy-start | bytes 786436
  66.6 2.2 %copy-start.5 = (bf16[2,8,8192]{2,1,0:T(8,128)(2,1)S(1)}, bf16[2,8,8192]{2,1,0:T(8,128)(2,1)}, u32[]{:S(2)}) copy-start(bf16[2,8,8192]{2,1,0:T(8,128)(2,1)} %copy-done.4) | copy-start | bytes 786436
  66.8 2.0 %collective-permute-start.7 = (f32[2,8,16,512]{3,2,1,0:T(8,128)S(1)}, f32[2,8,16,512]{3,2,1,0:T(8,128)S(1)}, u32[]{:S(2)}, u32[]{:S(2)}) collective-permute-start(f32[2,8,16,512]{3,2,1,0:T(8,128)S(1)} %pad_maximum_fusion.2.both), channel_id=1, source_target_pairs={{0,1},{1,0},{2,3},{3,2},{4,5},{5,4},{6,7},{7,6},{8,9},{9,8},{10,11... | collective-permute-start | bytes 1572872 | tf_op jit(solution)/shard_map/ppermute | solution.py:253
  101.3 1.5 %collective-permute-start.8 = (f32[8,24,256]{2,1,0:T(8,128)S(1)}, f32[8,24,256]{2,1,0:T(8,128)S(1)}, u32[]{:S(2)}, u32[]{:S(2)}) collective-permute-start(f32[8,24,256]{2,1,0:T(8,128)S(1)} %get-tuple-element.78), channel_id=1, source_target_pairs={{0,1},{1,0},{2,3},{3,2},{4,5},{5,4},{6,7},{7,6},{8,9},{9,8},{10,11... | collective-permute-start | bytes 589832 | tf_op jit(solution)/shard_map/ppermute | solution.py:269
  101.5 1.6 %collective-permute-start.16 = (f32[8,24,256]{2,1,0:T(8,128)S(1)}, f32[8,24,256]{2,1,0:T(8,128)S(1)}, u32[]{:S(2)}, u32[]{:S(2)}) collective-permute-start(f32[8,24,256]{2,1,0:T(8,128)S(1)} %get-tuple-element.79), channel_id=1, source_target_pairs={{0,1},{1,0},{2,3},{3,2},{4,5},{5,4},{6,7},{7,6},{8,9},{9,8},{10,11... | collective-permute-start | bytes 589832 | tf_op jit(solution)/shard_map/ppermute | solution.py:269
  103.2 5.0 %collective-permute-start.17 = (f32[4,24,256]{2,1,0:T(8,128)S(1)}, f32[4,24,256]{2,1,0:T(8,128)S(1)}, u32[]{:S(2)}, u32[]{:S(2)}) collective-permute-start(f32[4,24,256]{2,1,0:T(8,128)S(1)} %slice_select_fusion.2), channel_id=1, source_target_pairs={{0,16},{8,24},{16,0},{24,8},{1,17},{9,25},{17,1},{25,9},{2,18},{10... | collective-permute-start | bytes 294920 | tf_op jit(solution)/shard_map/ppermute | solution.py:269
  104.8 5.0 %collective-permute-start.9 = (f32[4,24,256]{2,1,0:T(8,128)S(1)}, f32[4,24,256]{2,1,0:T(8,128)S(1)}, u32[]{:S(2)}, u32[]{:S(2)}) collective-permute-start(f32[4,24,256]{2,1,0:T(8,128)S(1)} %slice_select_fusion.3), channel_id=1, source_target_pairs={{0,8},{8,0},{16,24},{24,16},{1,9},{9,1},{17,25},{25,17},{2,10},{10... | collective-permute-start | bytes 294920 | tf_op jit(solution)/shard_map/ppermute | solution.py:269
  108.2 4.2 %collective-permute-start.18 = (f32[2,24,256]{2,1,0:T(8,128)S(1)}, f32[2,24,256]{2,1,0:T(8,128)S(1)}, u32[]{:S(2)}, u32[]{:S(2)}) collective-permute-start(f32[2,24,256]{2,1,0:T(8,128)S(1)} %slice_select_fusion.4), channel_id=1, source_target_pairs={{0,8},{8,0},{16,24},{24,16},{1,9},{9,1},{17,25},{25,17},{2,10},{10... | collective-permute-start | bytes 147464 | tf_op jit(solution)/shard_map/ppermute | solution.py:269
  109.8 9.0 %collective-permute-start.10 = (f32[2,24,256]{2,1,0:T(8,128)S(1)}, f32[2,24,256]{2,1,0:T(8,128)S(1)}, u32[]{:S(2)}, u32[]{:S(2)}) collective-permute-start(f32[2,24,256]{2,1,0:T(8,128)S(1)} %slice_select_fusion.5), channel_id=1, source_target_pairs={{0,16},{8,24},{16,0},{24,8},{1,17},{9,25},{17,1},{25,9},{2,18},{10... | collective-permute-start | bytes 147464 | tf_op jit(solution)/shard_map/ppermute | solution.py:269
  112.4 8.5 %collective-permute-start.19 = (f32[2,24,256]{2,1,0:T(8,128)S(1)}, f32[2,24,256]{2,1,0:T(8,128)S(1)}, u32[]{:S(2)}, u32[]{:S(2)}) collective-permute-start(f32[2,24,256]{2,1,0:T(8,128)S(1)} %select_add_fusion.4), channel_id=1, source_target_pairs={{0,4},{1,5},{2,6},{3,7},{4,0},{5,1},{6,2},{7,3},{8,12},{9,13},{10,... | collective-permute-start | bytes 147464 | tf_op jit(solution)/shard_map/ppermute | solution.py:269
  118.8 4.2 %collective-permute-start.11 = (f32[2,24,256]{2,1,0:T(8,128)S(1)}, f32[2,24,256]{2,1,0:T(8,128)S(1)}, u32[]{:S(2)}, u32[]{:S(2)}) collective-permute-start(f32[2,24,256]{2,1,0:T(8,128)S(1)} %select_add_fusion.5), channel_id=1, source_target_pairs={{0,2},{1,3},{2,0},{3,1},{4,6},{5,7},{6,4},{7,5},{8,10},{9,11},{10,... | collective-permute-start | bytes 147464 | tf_op jit(solution)/shard_map/ppermute | solution.py:269
  120.9 4.2 %collective-permute-start.20 = (f32[2,24,256]{2,1,0:T(8,128)S(1)}, f32[2,24,256]{2,1,0:T(8,128)S(1)}, u32[]{:S(2)}, u32[]{:S(2)}) collective-permute-start(f32[2,24,256]{2,1,0:T(8,128)S(1)} %add.62), channel_id=1, source_target_pairs={{0,2},{1,3},{2,0},{3,1},{4,6},{5,7},{6,4},{7,5},{8,10},{9,11},{10,... | collective-permute-start | bytes 147464 | tf_op jit(solution)/shard_map/ppermute | solution.py:269
  123.0 5.6 %collective-permute-start.12 = (f32[2,24,256]{2,1,0:T(8,128)S(1)}, f32[2,24,256]{2,1,0:T(8,128)S(1)}, u32[]{:S(2)}, u32[]{:S(2)}) collective-permute-start(f32[2,24,256]{2,1,0:T(8,128)S(1)} %add.57), channel_id=1, source_target_pairs={{0,4},{1,5},{2,6},{3,7},{4,0},{5,1},{6,2},{7,3},{8,12},{9,13},{10,... | collective-permute-start | bytes 147464 | tf_op jit(solution)/shard_map/ppermute | solution.py:269
  125.0 5.1 %collective-permute-start.21 = (f32[2,24,256]{2,1,0:T(8,128)S(1)}, f32[2,24,256]{2,1,0:T(8,128)S(1)}, u32[]{:S(2)}, u32[]{:S(2)}) collective-permute-start(f32[2,24,256]{2,1,0:T(8,128)S(1)} %add.63), channel_id=1, source_target_pairs={{0,8},{8,0},{16,24},{24,16},{1,9},{9,1},{17,25},{25,17},{2,10},{10... | collective-permute-start | bytes 147464 | tf_op jit(solution)/shard_map/ppermute | solution.py:269
  128.6 4.2 %collective-permute-start.13 = (f32[2,24,256]{2,1,0:T(8,128)S(1)}, f32[2,24,256]{2,1,0:T(8,128)S(1)}, u32[]{:S(2)}, u32[]{:S(2)}) collective-permute-start(f32[2,24,256]{2,1,0:T(8,128)S(1)} %add.58), channel_id=1, source_target_pairs={{0,16},{8,24},{16,0},{24,8},{1,17},{9,25},{17,1},{25,9},{2,18},{10... | collective-permute-start | bytes 147464 | tf_op jit(solution)/shard_map/ppermute | solution.py:269
  130.2 4.7 %collective-permute-start.22 = (f32[4,24,256]{2,1,0:T(8,128)S(1)}, f32[4,24,256]{2,1,0:T(8,128)S(1)}, u32[]{:S(2)}, u32[]{:S(2)}) collective-permute-start(f32[4,24,256]{2,1,0:T(8,128)S(1)} %pad_maximum_fusion.8), channel_id=1, source_target_pairs={{0,16},{8,24},{16,0},{24,8},{1,17},{9,25},{17,1},{25,9},{2,18},{10... | collective-permute-start | bytes 294920 | tf_op jit(solution)/shard_map/ppermute | solution.py:269
  132.8 4.7 %collective-permute-start.14 = (f32[4,24,256]{2,1,0:T(8,128)S(1)}, f32[4,24,256]{2,1,0:T(8,128)S(1)}, u32[]{:S(2)}, u32[]{:S(2)}) collective-permute-start(f32[4,24,256]{2,1,0:T(8,128)S(1)} %pad_maximum_fusion.7), channel_id=1, source_target_pairs={{0,8},{8,0},{16,24},{24,16},{1,9},{9,1},{17,25},{25,17},{2,10},{10... | collective-permute-start | bytes 294920 | tf_op jit(solution)/shard_map/ppermute | solution.py:269
  134.9 2.6 %collective-permute-start.23 = (f32[8,24,256]{2,1,0:T(8,128)S(1)}, f32[8,24,256]{2,1,0:T(8,128)S(1)}, u32[]{:S(2)}, u32[]{:S(2)}) collective-permute-start(f32[8,24,256]{2,1,0:T(8,128)S(1)} %pad_maximum_fusion.5), channel_id=1, source_target_pairs={{0,1},{1,0},{2,3},{3,2},{4,5},{5,4},{6,7},{7,6},{8,9},{9,8},{10,11... | collective-permute-start | bytes 589832 | tf_op jit(solution)/shard_map/ppermute | solution.py:269
  137.5 1.5 %collective-permute-start.15 = (f32[8,24,256]{2,1,0:T(8,128)S(1)}, f32[8,24,256]{2,1,0:T(8,128)S(1)}, u32[]{:S(2)}, u32[]{:S(2)}) collective-permute-start(f32[8,24,256]{2,1,0:T(8,128)S(1)} %pad_maximum_fusion.4), channel_id=1, source_target_pairs={{0,1},{1,0},{2,3},{3,2},{4,5},{5,4},{6,7},{7,6},{8,9},{9,8},{10,11... | collective-permute-start | bytes 589832 | tf_op jit(solution)/shard_map/ppermute | solution.py:269
  139.5 0.9 copy-start.9

commit v9 on v8

--- a/solution.py
+++ b/solution.py
@@ -46,7 +46,8 @@
     return values[0]
 
 
-def states_kernel(core, p, hx_low, hx_high, hi, u, filt, f1, we, wb, qkv, xg, blocks_e, blocks_a, ends, xs):
+def states_kernel(core, p, hx, hi, u, filt, f1, we, wb, *rest):
+    qkv, xg, blocks_e, blocks_a, ends, xs = rest[-6:]
     rows = p.shape[1]
     run = (rows + SUB) // SUB
     taps = filt.shape[1]
@@ -61,13 +62,12 @@
         which = lt // tiles
         inside = lax.broadcasted_iota(jnp.int32, (SUB, LANES), 0) < SUB - 1
         for j in range(3):
-            across = (hx_low, hx_high)[j // 2][j % 2, :, lanes].astype(F32)
-            within = hi[j, :, lanes].astype(F32)
+            across, within = hx[j, :, lanes].astype(F32), hi[j, :, lanes].astype(F32)
             xs[j, 0:SUB] = jnp.where(first, across, within)
             xs[j, SUB : SUB + rows] = p[j, :, lanes].astype(F32)
             xs[j, SUB + rows :] = jnp.where(first, within, across)
         xs[3, SUB : SUB + rows] = u[:, lanes].astype(F32)
-        across, within = hx_high[1, :, lanes].astype(F32), hi[3, :, lanes].astype(F32)
+        across, within = hx[3, :, lanes].astype(F32), hi[3, :, lanes].astype(F32)
         xs[3, SUB + rows :] = jnp.where(first, within, across)
 
         def mixed(j):
@@ -106,13 +106,11 @@
     lax.fori_loop(0, p.shape[2] // LANES, tile, 0)
 
 
-def blocks_kernel(
-    xg, blocks_e, blocks_a, near, skip, join_e, join_a, conv, from_e, from_a, skip_sum
-):
+def blocks_kernel(xg, near, skip, conv, skip_sum):
     run = xg.shape[2] // SUB
     rows = xg.shape[2] - SUB
     taps = near.shape[0] - run
-    poles, groups = blocks_e.shape[1], near.shape[1]
+    groups = near.shape[1]
     own = rows - run * (SUB - 1)
     tiles = groups // LANES
 
@@ -142,22 +140,20 @@
             if own <= a < own + taps - 1:
                 terms = terms + [past[m] * x[a - m] for m in range(a - own + 1)]
             conv[which, 1, SUB * a : SUB * a + SUB, part] = added(terms)
-        for n in range(poles):
-            value = pltpu.roll(blocks_e[which, n, :, part], 1, 0) * join_e[0, n, :, part]
-            for k, step in ((1, 1), (2, 2), (3, 4)):
-                value = value + pltpu.roll(value, step, 0) * join_e[k, n, :, part]
-            from_e[which, n, :, part] = value
-            value = pltpu.roll(blocks_a[which, n, :, part], SUB - 1, 0) * join_a[0, n, :, part]
-            for k, step in ((1, 1), (2, 2), (3, 4)):
-                value = value + pltpu.roll(value, SUB - step, 0) * join_a[k, n, :, part]
-            from_a[which, n, :, part] = value
         return carry
 
     lax.fori_loop(0, xg.shape[0] * tiles, tile, 0)
 
 
+def entered(value, join, n, part, turn):
+    value = pltpu.roll(value, turn % SUB, 0) * join[0, n, :, part]
+    for k, step in ((1, 1), (2, 2), (3, 4)):
+        value = value + pltpu.roll(value, (turn * step) % SUB, 0) * join[k, n, :, part]
+    return value
+
+
 def final_kernel(
-    core, p, hx_low, hx_high, hi, u, qkv, conv, from_e, from_a, skip_sum, both, found, other, filt, f1, f_all, cz, cy,
+    core, p, hx_low, hx_high, hi, u, qkv, conv, blocks_e, blocks_a, join_e, join_a, skip_sum, both, found, other, filt, f1, f_all, cz, cy,
     output, grad_p, sums, ps, us, gs, os, es,
 ):
     rows = p.shape[1]
@@ -168,7 +164,8 @@
     tiles = groups // LANES
     first = core[0] == 0
     halves = pl.num_programs(0) // 2
-    kept = (pl.program_id(0) < halves) == first
+    early = pl.program_id(0) < halves
+    kept = early == first
     cut = sums.shape[2] // LANES
 
     def tile(lt, carry):
@@ -183,18 +180,20 @@
             close = other[side, which, :, part] + f_all[:, part] * far
             es[side] = jnp.where(first == (side == 0), far, close)
         for j in range(3):
-            across = (hx_low, hx_high)[j // 2][j % 2, :, lanes].astype(F32)
+            across = jnp.where(early, hx_low[j, :, lanes].astype(F32), hx_high[j, :, lanes].astype(F32))
             within = hi[j, :, lanes].astype(F32)
             ps[j, 0:SUB] = jnp.where(first, across, within)
             ps[j, SUB : SUB + rows] = p[j, :, lanes].astype(F32)
             ps[j, SUB + rows :] = jnp.where(first, within, across)
         us[0:rows] = u[:, lanes].astype(F32)
-        across, within = hx_high[1, :, lanes].astype(F32), hi[3, :, lanes].astype(F32)
+        across = jnp.where(early, hx_low[3, :, lanes].astype(F32), hx_high[3, :, lanes].astype(F32))
+        within = hi[3, :, lanes].astype(F32)
         us[rows:] = jnp.where(first, within, across)
         decay = [spread(f1[n : n + 1, part]) for n in range(poles)]
 
         state = [
-            from_e[which, n, :, part] + cz[n, :, part] * spread(es[0, n : n + 1])
+            entered(blocks_e[which, n, :, part], join_e, n, part, 1)
+            + cz[n, :, part] * spread(es[0, n : n + 1])
             for n in range(poles)
         ]
         for a in range(run):
@@ -208,7 +207,8 @@
         output[:, lanes] = os[0:rows].astype(BF16)
 
         state = [
-            from_a[which, n, :, part] + cy[n, :, part] * spread(es[1, n : n + 1])
+            entered(blocks_a[which, n, :, part], join_a, n, part, -1)
+            + cy[n, :, part] * spread(es[1, n : n + 1])
             for n in range(poles)
         ]
         for a in range(run - 1, -1, -1):
@@ -298,35 +298,33 @@
     return before, after, kept
 
 
-def chain(left, right, turn):
-    index, dp = lax.axis_index("ctx"), lax.axis_index("dp")
-    reaches = []
-    while 2 ** len(reaches) < lax.axis_size("dp"):
-        reaches.append(2 ** len(reaches))
-    chips = []
-    while 2 ** (len(chips) + 1) < lax.axis_size("ctx"):
-        chips.append(2 ** (len(chips) + 1))
-    steps = [("ctx", 1, lax.rem(index, 2) == 0)]
-    steps = steps + [("dp", step, lax.rem(dp // step, 2) == 0) for step in reaches[::turn]]
-    for axis, step, low in steps:
-        value = jnp.where(low, left, right) + paired(jnp.where(low, right, left), axis, step)
-        half = value.shape[0] // 2
-        left, right = value[:half], value[half:]
-    for step in chips[::turn]:
-        value = value + paired(value, "ctx", step)
-    for axis, step, low in reversed(steps):
-        other = paired(value, axis, step)
-        left, right = jnp.where(low, value, other), jnp.where(low, other, value)
-        value = jnp.concatenate([left, right], axis=0)
-    return left, right
+def rotated(value, axis, steps):
+    count = lax.axis_size(axis)
+    return lax.ppermute(value, axis, [(s, (s + steps) % count) for s in range(count)])
 
 
 def summed(value):
-    quarter = value.shape[0] // 4
-    parts = [value[k * quarter : (k + 1) * quarter] for k in range(4)]
-    left, right = chain(parts[0], parts[2], 1)
-    other_left, other_right = chain(parts[1], parts[3], -1)
-    return jnp.concatenate([left, other_left, right, other_right], axis=0)
+    dp, parts = lax.axis_index("dp"), lax.axis_size("dp")
+    low = lax.rem(lax.axis_index("ctx"), 2) == 0
+    half = value.shape[0] // 2
+    left, right = value[:half], value[half:]
+    value = jnp.where(low, left, right) + swapped(jnp.where(low, right, left))
+    size = half // parts
+    piece = lambda k: lax.dynamic_slice_in_dim(value, lax.rem(dp + k, parts) * size, size, 0)
+    total = piece(0)
+    for term in [rotated(piece(k), "dp", k) for k in range(1, parts)]:
+        total = total + term
+    reach = 2
+    while reach < lax.axis_size("ctx"):
+        total = total + paired(total, "ctx", reach)
+        reach = 2 * reach
+    value = jnp.zeros((half,) + value.shape[1:], F32)
+    for k in range(parts):
+        term = rotated(total, "dp", k) if k else total
+        at = lax.rem(dp + parts - k, parts) * size
+        value = lax.dynamic_update_slice_in_dim(value, term, at, 0)
+    other = swapped(value)
+    return jnp.concatenate([jnp.where(low, value, other), jnp.where(low, other, value)], axis=0)
 
 
 def local(projected, short_filter, residues, decay_rates, skip_gain, cotangent):
@@ -346,7 +344,8 @@
     across = [(k, k + 1) for k in range(1, devices - 1, 2)]
     across = across + [(target, source) for source, target in across]
     sent = jnp.where(core == 0, head, tail)
-    hx = [lax.ppermute(sent[2 * k : 2 * k + 2], "ctx", across) for k in range(2)]
+    middle = channels // 2
+    hx = [lax.ppermute(part, "ctx", across) for part in (sent[..., :middle], sent[..., middle:])]
     hi = swapped(jnp.where(core == 0, tail, head))
 
     rate = decay_rates.T
@@ -392,70 +391,78 @@
         return pl.BlockSpec((count,) + shape, lambda w: (w + first,) + (0,) * len(shape))
 
     state_spec = by_block(poles, SUB, groups)
-    qkv, xg, blocks_e, blocks_a, ends = pl.pallas_call(
-        states_kernel,
-        grid=(width // each,),
-        in_specs=[
-            pl.BlockSpec(memory_space=pltpu.SMEM),
-            by_w(3, rows), by_w(2, SUB), by_w(2, SUB), by_w(4, SUB), by_w(rows), by_w(3, taps),
-            fixed(f1), fixed(we), fixed(wb),
-        ],
-        out_specs=[
-            by_block(3, held, groups), by_block(2, held, groups), state_spec, state_spec,
-            ends_spec,
-        ],
-        out_shape=[
-            shape_of((width, 3, held, groups), F32), pair_shape,
-            state_shape, state_shape, shape_of((2, width, poles, groups), F32),
-        ],
-        scratch_shapes=[pltpu.VMEM((4, held + SUB, LANES), F32)],
-        compiler_params=params,
-        name="states",
-    )(core[None], p, *hx, hi, u, short_filter, f1, we, wb)
+    half = width // 2
+
+    def states(k, filled):
+        def at_w(*shape):
+            axis = len(shape)
+            return pl.BlockSpec(shape + (groups,), lambda w: (0,) * axis + (w + k * half,))
+
+        block = functools.partial(by_block, first=k * half)
+        return pl.pallas_call(
+            states_kernel,
+            grid=(half,),
+            in_specs=[
+                pl.BlockSpec(memory_space=pltpu.SMEM),
+                at_w(3, rows), by_w(4, SUB), at_w(4, SUB), at_w(rows), at_w(3, taps),
+                fixed(f1), fixed(we), fixed(wb),
+            ] + [pl.BlockSpec(memory_space=pl.ANY)] * len(filled),
+            out_specs=[
+                block(3, held, groups), block(2, held, groups), block(poles, SUB, groups),
+                block(poles, SUB, groups),
+                pl.BlockSpec((2, each, poles, groups), lambda w: (0, w + k * half, 0, 0)),
+            ],
+            out_shape=[
+                shape_of((width, 3, held, groups), F32), pair_shape,
+                state_shape, state_shape, shape_of((2, width, poles, groups), F32),
+            ],
+            input_output_aliases={9 + side: side for side in range(len(filled))},
+            scratch_shapes=[pltpu.VMEM((4, held + SUB, LANES), F32)],
+            compiler_params=params,
+            name="states",
+        )(core[None], p, hx[k], hi, u, short_filter, f1, we, wb, *filled)
+
+    qkv, xg, blocks_e, blocks_a, ends = states(1, states(0, ()))
 
     many = 2 if width % 2 == 0 else 1
 
     def blocks(first, last):
-        states = by_block(poles, SUB, groups, count=many, first=first)
         pairs = by_block(2, held, groups, count=many, first=first)
 
         def call(sent, kept):
             close, _ = lax.optimization_barrier((near, sent))
-            held_before = kept or (xg, blocks_e, blocks_a)
-            out = pl.pallas_call(
+            pair, *sums = kept or (xg,)
+            pair, skip = pl.pallas_call(
                 blocks_kernel,
                 grid=(last - first,),
                 in_specs=[
-                    pairs, states, states, fixed(near),
-                    pl.BlockSpec((1, many * groups), lambda w: (0, w + first)),
-                    fixed(join_e), fixed(join_a),
+                    pairs, fixed(near), pl.BlockSpec((1, many * groups), lambda w: (0, w + first)),
                 ],
-                out_specs=[pairs, states, states, by_block(SUB, groups, count=many)],
-                out_shape=[
-                    pair_shape, state_shape, state_shape,
-                    shape_of(((last - first) * many, SUB, groups), F32),
-                ],
-                input_output_aliases={0: 0, 1: 1, 2: 2},
+                out_specs=[pairs, by_block(SUB, groups, count=many)],
+                out_shape=[pair_shape, shape_of(((last - first) * many, SUB, groups), F32)],
+                input_output_aliases={0: 0},
                 compiler_params=params,
                 cost_estimate=pl.CostEstimate(
-                    flops=60 * rows * channels, bytes_accessed=35 * 2**20, transcendentals=0
+                    flops=60 * rows * channels, bytes_accessed=18 * 2**20, transcendentals=0
                 ),
                 name="blocks",
-            )(*held_before[:3], close, skip_gain[None], join_e, join_a)
-            return [*out[:3], jnp.concatenate([*held_before[3:], out[3]], axis=0)]
+            )(pair, close, skip_gain[None])
+            return [pair, jnp.concatenate([*sums, skip], axis=0)]
 
         return call
 
     steps = width // many
     cut = (steps + 1) // 3
     other, chip_e, chip_a = joined(ends, f_all)
-    before, after, (conv, from_e, from_a, skip_sum) = scanned(
+    before, after, (conv, skip_sum) = scanned(
         chip_e, chip_a, f_all, (blocks(0, cut), blocks(cut, steps))
     )
     both = jnp.stack([before, after])
     found = swapped(both)
 
     count = 3 * SUB
+    low = pl.BlockSpec((4, SUB, groups), lambda w: (0, 0, jnp.minimum(w, half - 1)))
+    high = pl.BlockSpec((4, SUB, groups), lambda w: (0, 0, jnp.maximum(w - half, 0)))
     split = 2 if groups % (2 * LANES) == 0 else 1
     scratch = [
         pltpu.VMEM((3, held + SUB, LANES), F32),
@@ -469,9 +476,9 @@
         grid=(width // each,),
         in_specs=[
             pl.BlockSpec(memory_space=pltpu.SMEM),
-            by_w(3, rows), by_w(2, SUB), by_w(2, SUB), by_w(4, SUB), by_w(rows),
+            by_w(3, rows), low, high, by_w(4, SUB), by_w(rows),
             by_block(3, held, groups), by_block(2, held, groups), state_spec, state_spec,
-            by_block(SUB, groups), halved, halved, ends_spec,
+            fixed(join_e), fixed(join_a), by_block(SUB, groups), halved, halved, ends_spec,
             by_w(3, taps), fixed(f1), fixed(f_all), fixed(cz), fixed(cy),
         ],
         out_specs=[
@@ -487,7 +494,7 @@
         compiler_params=params,
         name="final",
     )(
-        core[None], p, *hx, hi, u, qkv, conv, from_e, from_a, skip_sum, both, found, other, short_filter,
+        core[None], p, *hx, hi, u, qkv, conv, blocks_e, blocks_a, join_e, join_a, skip_sum, both, found, other, short_filter,
         f1, f_all, cz, cy,
     )
 

time: 141 us -> 141 us (level)
  starting transfers between devices: 38 us -> 21.1 us
  waiting for transfers between devices: 18 us -> 31.1 us
  other arithmetic: 4.56 us -> 6.9 us
    ppermute x17 -> x3, starting transfers between devices: 24.4 us -> 1.8 us  [paired(): lax.ppermute(value, axis, [(source, source ^ step) for source in lines or...]
    ppermute x2 -> x8, starting transfers between devices: 1.35 us -> 9.45 us  [the longest x6 8.11 us: rotated(): lax.ppermute(value, axis, [(s, (s + steps) % count) for s in range(count)])]
    ppermute x2 -> x8, waiting for transfers between devices: 0.01 us -> 7.74 us  [the longest x6 7.73 us: rotated(): lax.ppermute(value, axis, [(s, (s + steps) % count) for s in range(count)])]
    ppermute x1, waiting for transfers between devices: 0.01 us -> 6.04 us  [scanned(): far = lax.ppermute(sent, 'ctx', [(2, 6), (3, 7), (4, 0), (5, 1)])]
    pallas_call x1, Pallas kernels: 32.5 us -> 37.9 us  [local(): pl.pallas_call(final_kernel, grid=(width // each,), in_specs=[pl.BlockSpe...]
    pallas_call x3 -> x4, Pallas kernels: 42.4 us -> 38.1 us  [the longest x2 24.4 us: states(): pl.pallas_call(states_kernel, grid=(half,), in_specs=[pl.BlockSpec(memory...]
    ppermute x17 -> x3, waiting for transfers between devices: 14.5 us -> 11 us  [paired(): lax.ppermute(value, axis, [(source, source ^ step) for source in lines or...]
    ppermute x3 -> x5, waiting for transfers between devices: 3.55 us -> 6.39 us  [swapped(): return lax.ppermute(value, 'ctx', [(s, s ^ 1) for s in range(count)])]
  transfers between devices with their start and end apart: 24 -> 18, of which waited for: 14 -> 14; matrix products, arithmetic and copies ran while one was open for 2% -> 3% of each run, Pallas kernels for 14% -> 18%
where the time goes in v9:
time: 141 us; the launch traced here: 140 us
  Pallas kernels  76 us (54%)
  waiting for transfers between devices  31.1 us (22%)
  starting transfers between devices  21.1 us (15%)
  other arithmetic  6.9 us (5%)
  local copies, waits for them, and re-layouts  4.06 us (3%)
    pallas_call x1, Pallas kernels, local(): pl.pallas_call(final_kernel, grid=(width // each,), in_specs=[pl.BlockSpe...  37.9 us
    pallas_call x2, Pallas kernels, states(): pl.pallas_call(states_kernel, grid=(half,), in_specs=[pl.BlockSpec(memory...  24.4 us
    pallas_call x2, Pallas kernels, call(): pl.pallas_call(blocks_kernel, grid=(last - first,), in_specs=[pairs, fixe...  13.7 us
    ppermute x3, waiting for transfers between devices, paired(): lax.ppermute(value, axis, [(source, source ^ step) for source in lines or...  11 us
    ppermute x6, starting transfers between devices, rotated(): lax.ppermute(value, axis, [(s, (s + steps) % count) for s in range(count)])  8.11 us
    ppermute x5, starting transfers between devices, swapped(): return lax.ppermute(value, 'ctx', [(s, s ^ 1) for s in range(count)])  7.75 us
    ppermute x6, waiting for transfers between devices, rotated(): lax.ppermute(value, axis, [(s, (s + steps) % count) for s in range(count)])  7.73 us
    ppermute x5, waiting for transfers between devices, swapped(): return lax.ppermute(value, 'ctx', [(s, s ^ 1) for s in range(count)])  6.39 us
  transfers between devices with their start and end apart: 18, of which 14 were waited for; matrix products, arithmetic and copies ran while one was open for 3% of the time, Pallas kernels for 18%

profile of v9, /device:TPU:0, one launch (start us, length us, event | category | flops | bytes accessed | tf_op | source)
XLA Modules:
  0.0 140.4 jit_solution(10548326371796569088)
XLA Ops:
  0.7 1.3 fusion.8
  2.0 1.0 fusion.9
  3.0 0.1 broadcast_select_fusion.2
  3.1 0.7 collective-permute-start
  3.8 4.4 %collective-permute-start.2 = (bf16[4,8,8192]{2,1,0:T(8,128)(2,1)S(1)}, bf16[4,8,8192]{2,1,0:T(8,128)(2,1)S(1)}, u32[]{:S(2)}, u32[]{:S(2)}) collective-permute-start(bf16[4,8,8192]{2,1,0:T(8,128)(2,1)S(1)} %get-tuple-element.68), channel_id=1, source_target_pairs={{0,1},{1,0},{2,3},{3,2},{4,5},{5,4},{6,7},{7,6},{8,9},{9,8},{10,11... | collective-permute-start | bytes 1572872 | tf_op jit(solution)/shard_map/ppermute | solution.py:253
  8.3 0.7 collective-permute-start.1
  8.9 0.8 negate_bitcast_fusion
  9.7 0.9 multiply_exponential_fusion
  10.6 0.7 fusion.7
  11.4 0.2 copy-done.7
  11.6 12.2 %states.2 = (f32[16,3,136,512]{3,2,1,0:T(8,128)}, f32[16,2,136,512]{3,2,1,0:T(8,128)}, f32[16,16,8,512]{3,2,1,0:T(8,128)}, f32[16,16,8,512]{3,2,1,0:T(8,128)}, f32[2,16,16,512]{3,2,1,0:T(8,128)}) custom-call(s32[1]{0:T(128)} %bitcast.core, bf16[3,128,8192]{2,1,0:T(8,128)(2,1)} %bitcast.84, bf16[4,8,4096]{2,1,0:T(8,128)(2,1)S(1)} %collective-permute-done.hx.hx_low, ...), custom_call_target="tpu_custom_call" | custom-call | tf_op jit(solution)/shard_map/states/pallas_call | solution.py:402
  23.8 0.0 copy-start.16
  23.8 0.0 copy-start.13
  23.8 12.3 %states.3 = (f32[16,3,136,512]{3,2,1,0:T(8,128)}, f32[16,2,136,512]{3,2,1,0:T(8,128)}, f32[16,16,8,512]{3,2,1,0:T(8,128)}, f32[16,16,8,512]{3,2,1,0:T(8,128)}, f32[2,16,16,512]{3,2,1,0:T(8,128)}) custom-call(s32[1]{0:T(128)} %bitcast.core, ...), custom_call_target="tpu_custom_call", output_to_operand_aliasing={{0}: (9, {}), {1}: (10, {}), {2}: (11, {}), {3}: (12, {}), ... | custom-call | tf_op jit(solution)/shard_map/states/pallas_call | solution.py:402
  36.1 3.0 %collective-permute-start.3 = (f32[2,16,16,512]{3,2,1,0:T(8,128)}, f32[2,16,16,512]{3,2,1,0:T(8,128)}, u32[]{:S(2)}, u32[]{:S(2)}) collective-permute-start(f32[2,16,16,512]{3,2,1,0:T(8,128)} %get-tuple-element.36), channel_id=1, source_target_pairs={{0,1},{1,0},{2,3},{3,2},{4,5},{5,4},{6,7},{7,6},{8,9},{9,8},{10,11... | collective-permute-start | bytes 3145736 | tf_op jit(solution)/shard_map/ppermute | solution.py:253
  39.1 2.6 %collective-permute-done.3.other = f32[2,16,16,512]{3,2,1,0:T(8,128)} collective-permute-done((f32[2,16,16,512]{3,2,1,0:T(8,128)}, f32[2,16,16,512]{3,2,1,0:T(8,128)}, u32[]{:S(2)}, u32[]{:S(2)}) %collective-permute-start.3) | collective-permute-done | bytes 1048608 | tf_op jit(solution)/shard_map/ppermute | solution.py:253
  41.7 1.3 dynamic-slice_select_fusion.1
  43.0 0.1 broadcast_select_fusion.6
  43.1 1.7 %collective-permute-start.4 = (f32[8,16,512]{2,1,0:T(8,128)S(1)}, f32[8,16,512]{2,1,0:T(8,128)S(1)}, u32[]{:S(2)}, u32[]{:S(2)}) collective-permute-start(f32[8,16,512]{2,1,0:T(8,128)S(1)} %broadcast_select_fusion.6), channel_id=1, source_target_pairs={{0,2},{1,3},{2,0},{3,1},{4,6},{5,7},{6,4},{7,5},{8,10},{9,11},{10,... | collective-permute-start | bytes 786440 | tf_op jit(solution)/shard_map/ppermute | solution.py:269
  44.8 1.0 multiply_reduce_fusion.near
  45.8 0.1 multiply_exponential_fusion.1
  45.9 5.5 %blocks.2 = (f32[16,2,136,512]{3,2,1,0:T(8,128)}, f32[6,8,512]{2,1,0:T(8,128)S(1)}) custom-call(f32[16,2,136,512]{3,2,1,0:T(8,128)} %get-tuple-element.37.xg, f32[24,512]{1,0:T(8,128)S(1)} %multiply_reduce_fusion.near, f32[1,8192]{1,0:T(1,128)S(1)} %bitcast.81), custom_call_target="tpu_custom_call", output_to_operand_aliasing={{0}: (0, {})} | custom-call | flops 62914560 | bytes 18874368 | tf_op jit(solution)/shard_map/blocks/pallas_call | solution.py:435
  51.4 0.4 collective-permute-done.4
  51.8 0.1 multiply_add_fusion.1
  51.9 0.8 collective-permute-start.5
  52.8 1.3 collective-permute-start.6
  54.1 0.0 copy-start.14
  54.1 0.0 copy-start.15
  54.2 8.1 %blocks.3 = (f32[16,2,136,512]{3,2,1,0:T(8,128)}, f32[10,8,512]{2,1,0:T(8,128)S(1)}) custom-call(f32[16,2,136,512]{3,2,1,0:T(8,128)} %get-tuple-element.42.xg, f32[24,512]{1,0:T(8,128)S(1)} %multiply_reduce_fusion.near, f32[1,8192]{1,0:T(1,128)S(1)} %bitcast.82), custom_call_target="tpu_custom_call", output_to_operand_aliasing={{0}: (0, {})} | custom-call | flops 62914560 | bytes 18874368 | tf_op jit(solution)/shard_map/blocks/pallas_call | solution.py:435
  62.3 6.0 %collective-permute-done.6 = f32[8,16,512]{2,1,0:T(8,128)S(1)} collective-permute-done((f32[8,16,512]{2,1,0:T(8,128)S(1)}, f32[8,16,512]{2,1,0:T(8,128)S(1)}, u32[]{:S(2)}, u32[]{:S(2)}) %collective-permute-start.6) | collective-permute-done | bytes 262176 | tf_op jit(solution)/shard_map/ppermute | solution.py:283
  68.4 0.1 select_bitcast_fusion.1
  68.5 0.1 collective-permute-start.7
  68.6 0.1 fusion
  68.7 1.3 broadcast_select_fusion
  70.0 0.5 collective-permute-done.7.found
  70.5 37.9 %final.1 = (bf16[128,8192]{1,0:T(8,128)(2,1)}, bf16[3,128,8192]{2,1,0:T(8,128)(2,1)}, f32[32,24,256]{2,1,0:T(8,128)S(1)}) custom-call(s32[1]{0:T(128)} %bitcast.core, bf16[3,128,8192]{2,1,0:T(8,128)(2,1)} %bitcast.86, bf16[4,8,4096]{2,1,0:T(8,128)(2,1)S(1)} %copy-done.5, bf16[4,8,4096]{2,1,0:T(8,128)(2,1)S(1)} %copy-done.3, ...), custom_call_target="tpu_custom_call" | custom-call | tf_op jit(solution)/shard_map/final/pallas_call | solution.py:474
  108.4 0.1 slice_select_fusion
  108.5 0.2 collective-permute-start.8
  108.7 1.6 %collective-permute-done.8 = f32[16,24,256]{2,1,0:T(8,128)S(1)} collective-permute-done((f32[16,24,256]{2,1,0:T(8,128)S(1)}, f32[16,24,256]{2,1,0:T(8,128)S(1)}, u32[]{:S(2)}, u32[]{:S(2)}) %collective-permute-start.8) | collective-permute-done | bytes 393248 | tf_op jit(solution)/shard_map/ppermute | solution.py:253
  110.3 0.1 select_add_fusion
  110.4 1.6 %collective-permute-start.10 = (f32[4,24,256]{2,1,0:T(8,128)S(1)}, f32[4,24,256]{2,1,0:T(8,128)S(1)}, u32[]{:S(2)}, u32[]{:S(2)}) collective-permute-start(f32[4,24,256]{2,1,0:T(8,128)S(1)} %get-tuple-element.78), channel_id=1, source_target_pairs={{0,16},{8,24},{16,0},{24,8},{1,17},{9,25},{17,1},{25,9},{2,18},{10... | collective-permute-start | bytes 294920 | tf_op jit(solution)/shard_map/ppermute | solution.py:303
  112.0 1.4 %collective-permute-start.11 = (f32[4,24,256]{2,1,0:T(8,128)S(1)}, f32[4,24,256]{2,1,0:T(8,128)S(1)}, u32[]{:S(2)}, u32[]{:S(2)}) collective-permute-start(f32[4,24,256]{2,1,0:T(8,128)S(1)} %get-tuple-element.77), channel_id=1, source_target_pairs={{0,24},{8,0},{16,8},{24,16},{1,25},{9,1},{17,9},{25,17},{2,26},{10... | collective-permute-start | bytes 294920 | tf_op jit(solution)/shard_map/ppermute | solution.py:303
  113.4 0.6 collective-permute-start.9
  114.0 1.3 collective-permute-done.10
  115.3 1.4 collective-permute-done.11
  116.6 2.3 %collective-permute-done.9 = f32[4,24,256]{2,1,0:T(8,128)S(1)} collective-permute-done((f32[4,24,256]{2,1,0:T(8,128)S(1)}, f32[4,24,256]{2,1,0:T(8,128)S(1)}, u32[]{:S(2)}, u32[]{:S(2)}) %collective-permute-start.9) | collective-permute-done | bytes 98336 | tf_op jit(solution)/shard_map/ppermute | solution.py:303
  119.0 0.1 collective-permute-start.12
  119.0 4.6 %collective-permute-done.12 = f32[4,24,256]{2,1,0:T(8,128)S(1)} collective-permute-done((f32[4,24,256]{2,1,0:T(8,128)S(1)}, f32[4,24,256]{2,1,0:T(8,128)S(1)}, u32[]{:S(2)}, u32[]{:S(2)}) %collective-permute-start.12) | collective-permute-done | bytes 98336 | tf_op jit(solution)/shard_map/ppermute | solution.py:269
  123.6 0.1 collective-permute-start.13
  123.7 6.0 %collective-permute-done.13 = f32[4,24,256]{2,1,0:T(8,128)S(1)} collective-permute-done((f32[4,24,256]{2,1,0:T(8,128)S(1)}, f32[4,24,256]{2,1,0:T(8,128)S(1)}, u32[]{:S(2)}, u32[]{:S(2)}) %collective-permute-start.13) | collective-permute-done | bytes 98336 | tf_op jit(solution)/shard_map/ppermute | solution.py:269
  129.8 1.2 collective-permute-start.14
  131.0 1.5 %collective-permute-start.15 = (f32[4,24,256]{2,1,0:T(8,128)S(1)}, f32[4,24,256]{2,1,0:T(8,128)S(1)}, u32[]{:S(2)}, u32[]{:S(2)}) collective-permute-start(f32[4,24,256]{2,1,0:T(8,128)S(1)} %get-tuple-element.57), channel_id=1, source_target_pairs={{0,16},{8,24},{16,0},{24,8},{1,17},{9,25},{17,1},{25,9},{2,18},{10... | collective-permute-start | bytes 294920 | tf_op jit(solution)/shard_map/ppermute | solution.py:303
  132.5 1.8 %collective-permute-start.16 = (f32[4,24,256]{2,1,0:T(8,128)S(1)}, f32[4,24,256]{2,1,0:T(8,128)S(1)}, u32[]{:S(2)}, u32[]{:S(2)}) collective-permute-start(f32[4,24,256]{2,1,0:T(8,128)S(1)} %get-tuple-element.57), channel_id=1, source_target_pairs={{0,24},{8,0},{16,8},{24,16},{1,25},{9,1},{17,9},{25,17},{2,26},{10... | collective-permute-start | bytes 294920 | tf_op jit(solution)/shard_map/ppermute | solution.py:303
  134.3 1.2 collective-permute-done.14
  135.4 1.0 collective-permute-done.15
  136.4 0.7 collective-permute-done.16
  137.1 0.1 collective-permute-start.17
  137.2 1.7 %collective-permute-done.17 = f32[16,24,256]{2,1,0:T(8,128)S(1)} collective-permute-done((f32[16,24,256]{2,1,0:T(8,128)S(1)}, f32[16,24,256]{2,1,0:T(8,128)S(1)}, u32[]{:S(2)}, u32[]{:S(2)}) %collective-permute-start.17) | collective-permute-done | bytes 393248 | tf_op jit(solution)/shard_map/ppermute | solution.py:253
  138.9 0.1 broadcast_select_fusion.5
  139.0 0.1 maximum_bitcast_fusion
  139.0 0.3 copy.23
  139.3 0.1 reshape.25
  139.5 0.7 slice.97
  140.2 0.2 copy-done.9
  (47 shorter events, 0.4 us)
Async XLA Ops:
  0.6 11.0 %copy-start = (bf16[1,128,8192]{2,1,0:T(8,128)(2,1)S(1)}, bf16[1,128,8192]{2,1,0:T(8,128)(2,1)}, u32[]{:S(2)}) copy-start(bf16[1,128,8192]{2,1,0:T(8,128)(2,1)} %param.16) | copy-start | bytes 6291460
  0.6 10.0 %copy-start.12 = (f32[512,16]{0,1:T(8,128)S(1)}, f32[512,16]{0,1:T(8,128)}, u32[]{:S(2)}) copy-start(f32[512,16]{0,1:T(8,128)} %param.14) | copy-start | bytes 98308
  0.7 10.9 %copy-start.1 = (f32[3,7,8192]{2,1,0:T(8,128)S(1)}, f32[3,7,8192]{2,1,0:T(8,128)}, u32[]{:S(2)}) copy-start(f32[3,7,8192]{2,1,0:T(8,128)} %filt.5) | copy-start | bytes 2064388
  3.1 8.2 %collective-permute-start = (bf16[4,8,4096]{2,1,0:T(8,128)(2,1)S(1)}, bf16[4,8,4096]{2,1,0:T(8,128)(2,1)S(1)}, u32[]{:S(2)}, u32[]{:S(2)}) collective-permute-start(bf16[4,8,4096]{2,1,0:T(8,128)(2,1)S(1)} %get-tuple-element.75), channel_id=1, source_target_pairs={{1,2},{3,4},{5,6},{2,1},{4,3},{6,5},{9,10},{11,12},{13,14},{10,9},... | collective-permute-start | bytes 786440 | tf_op jit(solution)/shard_map/ppermute | solution.py:348
  3.8 7.5 %collective-permute-start.2 = (bf16[4,8,8192]{2,1,0:T(8,128)(2,1)S(1)}, bf16[4,8,8192]{2,1,0:T(8,128)(2,1)S(1)}, u32[]{:S(2)}, u32[]{:S(2)}) collective-permute-start(bf16[4,8,8192]{2,1,0:T(8,128)(2,1)S(1)} %get-tuple-element.68), channel_id=1, source_target_pairs={{0,1},{1,0},{2,3},{3,2},{4,5},{5,4},{6,7},{7,6},{8,9},{9,8},{10,11... | collective-permute-start | bytes 1572872 | tf_op jit(solution)/shard_map/ppermute | solution.py:253
  8.3 15.5 %collective-permute-start.1 = (bf16[4,8,4096]{2,1,0:T(8,128)(2,1)S(1)}, bf16[4,8,4096]{2,1,0:T(8,128)(2,1)S(1)}, u32[]{:S(2)}, u32[]{:S(2)}) collective-permute-start(bf16[4,8,4096]{2,1,0:T(8,128)(2,1)S(1)} %get-tuple-element.74), channel_id=1, source_target_pairs={{1,2},{3,4},{5,6},{2,1},{4,3},{6,5},{9,10},{11,12},{13,14},{10,9},... | collective-permute-start | bytes 786440 | tf_op jit(solution)/shard_map/ppermute | solution.py:348
  10.6 1.0 copy-start.7
  11.4 12.4 %copy-start.4 = (bf16[4,8,4096]{2,1,0:T(8,128)(2,1)}, bf16[4,8,4096]{2,1,0:T(8,128)(2,1)S(1)}, u32[]{:S(2)}) copy-start(bf16[4,8,4096]{2,1,0:T(8,128)(2,1)S(1)} %collective-permute-done.hx.hx_low) | copy-start | bytes 786436
  23.8 12.3 %copy-start.2 = (bf16[4,8,4096]{2,1,0:T(8,128)(2,1)}, bf16[4,8,4096]{2,1,0:T(8,128)(2,1)S(1)}, u32[]{:S(2)}) copy-start(bf16[4,8,4096]{2,1,0:T(8,128)(2,1)S(1)} %collective-permute-done.1.hx.hx_high) | copy-start | bytes 786436
  23.8 21.0 %copy-start.16 = (f32[24]{0:T(128)S(1)}, f32[24]{0:T(128)}, u32[]{:S(2)}) copy-start(f32[24]{0:T(128)} %constant.80) | copy-start | bytes 292
  23.8 22.0 %copy-start.13 = (f32[4]{0:T(128)S(1)}, f32[4]{0:T(128)}, u32[]{:S(2)}) copy-start(f32[4]{0:T(128)} %constant.82) | copy-start | bytes 52
  23.8 22.1 %copy-start.6 = (f32[8192]{0:T(1024)S(1)}, f32[8192]{0:T(1024)}, u32[]{:S(2)}) copy-start(f32[8192]{0:T(1024)} %param.15) | copy-start | bytes 98308
  36.1 5.6 %collective-permute-start.3 = (f32[2,16,16,512]{3,2,1,0:T(8,128)}, f32[2,16,16,512]{3,2,1,0:T(8,128)}, u32[]{:S(2)}, u32[]{:S(2)}) collective-permute-start(f32[2,16,16,512]{3,2,1,0:T(8,128)} %get-tuple-element.36), channel_id=1, source_target_pairs={{0,1},{1,0},{2,3},{3,2},{4,5},{5,4},{6,7},{7,6},{8,9},{9,8},{10,11... | collective-permute-start | bytes 3145736 | tf_op jit(solution)/shard_map/ppermute | solution.py:253
  39.1 12.7 %copy-start.10 = (f32[16,512]{1,0:T(8,128)S(1)}, f32[16,512]{1,0:T(8,128)}, u32[]{:S(2)}) copy-start(f32[16,512]{1,0:T(8,128)} %get-tuple-element.81) | copy-start | bytes 98308
  43.0 11.0 %copy-start.11 = (f32[512,16]{0,1:T(8,128)S(1)}, f32[512,16]{0,1:T(8,128)}, u32[]{:S(2)}) copy-start(f32[512,16]{0,1:T(8,128)} %param.13) | copy-start | bytes 98308
  43.1 8.7 %collective-permute-start.4 = (f32[8,16,512]{2,1,0:T(8,128)S(1)}, f32[8,16,512]{2,1,0:T(8,128)S(1)}, u32[]{:S(2)}, u32[]{:S(2)}) collective-permute-start(f32[8,16,512]{2,1,0:T(8,128)S(1)} %broadcast_select_fusion.6), channel_id=1, source_target_pairs={{0,2},{1,3},{2,0},{3,1},{4,6},{5,7},{6,4},{7,5},{8,10},{9,11},{10,... | collective-permute-start | bytes 786440 | tf_op jit(solution)/shard_map/ppermute | solution.py:269
  51.9 16.7 %copy-start.8 = (f32[4,16,8,512]{3,2,1,0:T(8,128)S(1)}, f32[4,16,8,512]{3,2,1,0:T(8,128)}, u32[]{:S(2)}) copy-start(f32[4,16,8,512]{3,2,1,0:T(8,128)} %copy-done.7) | copy-start | bytes 3145732
  51.9 10.4 %collective-permute-start.5 = (f32[8,16,512]{2,1,0:T(8,128)S(1)}, f32[8,16,512]{2,1,0:T(8,128)S(1)}, u32[]{:S(2)}, u32[]{:S(2)}) collective-permute-start(f32[8,16,512]{2,1,0:T(8,128)S(1)} %multiply_add_fusion.1), channel_id=1, source_target_pairs={{2,4},{3,5},{4,2},{5,3},{10,12},{11,13},{12,10},{13,11},{18,20},{1... | collective-permute-start | bytes 786440 | tf_op jit(solution)/shard_map/ppermute | solution.py:282
  52.8 15.6 %collective-permute-start.6 = (f32[8,16,512]{2,1,0:T(8,128)S(1)}, f32[8,16,512]{2,1,0:T(8,128)S(1)}, u32[]{:S(2)}, u32[]{:S(2)}) collective-permute-start(f32[8,16,512]{2,1,0:T(8,128)S(1)} %multiply_add_fusion.1), channel_id=1, source_target_pairs={{2,6},{3,7},{4,0},{5,1},{10,14},{11,15},{12,8},{13,9},{18,22},{19,... | collective-permute-start | bytes 786440 | tf_op jit(solution)/shard_map/ppermute | solution.py:283
  54.1 14.5 %copy-start.14 = (pred[4,8]{1,0:T(4,128)(4,1)S(1)}, pred[4,8]{1,0:T(4,128)(4,1)}, u32[]{:S(2)}) copy-start(pred[4,8]{1,0:T(4,128)(4,1)} %constant.81) | copy-start | bytes 100
  54.1 14.5 %copy-start.15 = (pred[4,8]{1,0:T(4,128)(4,1)S(1)}, pred[4,8]{1,0:T(4,128)(4,1)}, u32[]{:S(2)}) copy-start(pred[4,8]{1,0:T(4,128)(4,1)} %constant.83) | copy-start | bytes 100
  54.1 16.3 %copy-start.3 = (bf16[4,8,4096]{2,1,0:T(8,128)(2,1)S(1)}, bf16[4,8,4096]{2,1,0:T(8,128)(2,1)}, u32[]{:S(2)}) copy-start(bf16[4,8,4096]{2,1,0:T(8,128)(2,1)} %copy-done.2) | copy-start | bytes 786436
  54.2 16.3 %copy-start.5 = (bf16[4,8,4096]{2,1,0:T(8,128)(2,1)S(1)}, bf16[4,8,4096]{2,1,0:T(8,128)(2,1)}, u32[]{:S(2)}) copy-start(bf16[4,8,4096]{2,1,0:T(8,128)(2,1)} %copy-done.4) | copy-start | bytes 786436
  68.5 2.0 %collective-permute-start.7 = (f32[2,8,16,512]{3,2,1,0:T(8,128)S(1)}, f32[2,8,16,512]{3,2,1,0:T(8,128)S(1)}, u32[]{:S(2)}, u32[]{:S(2)}) collective-permute-start(f32[2,8,16,512]{3,2,1,0:T(8,128)S(1)} %pad_maximum_fusion.2.both), channel_id=1, source_target_pairs={{0,1},{1,0},{2,3},{3,2},{4,5},{5,4},{6,7},{7,6},{8,9},{9,8},{10,11... | collective-permute-start | bytes 1572872 | tf_op jit(solution)/shard_map/ppermute | solution.py:253
  108.5 1.8 %collective-permute-start.8 = (f32[16,24,256]{2,1,0:T(8,128)S(1)}, f32[16,24,256]{2,1,0:T(8,128)S(1)}, u32[]{:S(2)}, u32[]{:S(2)}) collective-permute-start(f32[16,24,256]{2,1,0:T(8,128)S(1)} %slice_select_fusion), channel_id=1, source_target_pairs={{0,1},{1,0},{2,3},{3,2},{4,5},{5,4},{6,7},{7,6},{8,9},{9,8},{10,11... | collective-permute-start | bytes 1179656 | tf_op jit(solution)/shard_map/ppermute | solution.py:253
  110.4 4.9 %collective-permute-start.10 = (f32[4,24,256]{2,1,0:T(8,128)S(1)}, f32[4,24,256]{2,1,0:T(8,128)S(1)}, u32[]{:S(2)}, u32[]{:S(2)}) collective-permute-start(f32[4,24,256]{2,1,0:T(8,128)S(1)} %get-tuple-element.78), channel_id=1, source_target_pairs={{0,16},{8,24},{16,0},{24,8},{1,17},{9,25},{17,1},{25,9},{2,18},{10... | collective-permute-start | bytes 294920 | tf_op jit(solution)/shard_map/ppermute | solution.py:303
  112.0 4.7 %collective-permute-start.11 = (f32[4,24,256]{2,1,0:T(8,128)S(1)}, f32[4,24,256]{2,1,0:T(8,128)S(1)}, u32[]{:S(2)}, u32[]{:S(2)}) collective-permute-start(f32[4,24,256]{2,1,0:T(8,128)S(1)} %get-tuple-element.77), channel_id=1, source_target_pairs={{0,24},{8,0},{16,8},{24,16},{1,25},{9,1},{17,9},{25,17},{2,26},{10... | collective-permute-start | bytes 294920 | tf_op jit(solution)/shard_map/ppermute | solution.py:303
  113.4 5.5 %collective-permute-start.9 = (f32[4,24,256]{2,1,0:T(8,128)S(1)}, f32[4,24,256]{2,1,0:T(8,128)S(1)}, u32[]{:S(2)}, u32[]{:S(2)}) collective-permute-start(f32[4,24,256]{2,1,0:T(8,128)S(1)} %get-tuple-element.76), channel_id=1, source_target_pairs={{0,8},{8,16},{16,24},{24,0},{1,9},{9,17},{17,25},{25,1},{2,10},{10... | collective-permute-start | bytes 294920 | tf_op jit(solution)/shard_map/ppermute | solution.py:303
  119.0 4.7 %collective-permute-start.12 = (f32[4,24,256]{2,1,0:T(8,128)S(1)}, f32[4,24,256]{2,1,0:T(8,128)S(1)}, u32[]{:S(2)}, u32[]{:S(2)}) collective-permute-start(f32[4,24,256]{2,1,0:T(8,128)S(1)} %add_add_fusion), channel_id=1, source_target_pairs={{0,2},{1,3},{2,0},{3,1},{4,6},{5,7},{6,4},{7,5},{8,10},{9,11},{10,... | collective-permute-start | bytes 294920 | tf_op jit(solution)/shard_map/ppermute | solution.py:269
  123.6 6.1 %collective-permute-start.13 = (f32[4,24,256]{2,1,0:T(8,128)S(1)}, f32[4,24,256]{2,1,0:T(8,128)S(1)}, u32[]{:S(2)}, u32[]{:S(2)}) collective-permute-start(f32[4,24,256]{2,1,0:T(8,128)S(1)} %add.93), channel_id=1, source_target_pairs={{0,4},{1,5},{2,6},{3,7},{4,0},{5,1},{6,2},{7,3},{8,12},{9,13},{10,... | collective-permute-start | bytes 294920 | tf_op jit(solution)/shard_map/ppermute | solution.py:269
  129.8 5.7 %collective-permute-start.14 = (f32[4,24,256]{2,1,0:T(8,128)S(1)}, f32[4,24,256]{2,1,0:T(8,128)S(1)}, u32[]{:S(2)}, u32[]{:S(2)}) collective-permute-start(f32[4,24,256]{2,1,0:T(8,128)S(1)} %get-tuple-element.57), channel_id=1, source_target_pairs={{0,8},{8,16},{16,24},{24,0},{1,9},{9,17},{17,25},{25,1},{2,10},{10... | collective-permute-start | bytes 294920 | tf_op jit(solution)/shard_map/ppermute | solution.py:303
  131.0 5.4 %collective-permute-start.15 = (f32[4,24,256]{2,1,0:T(8,128)S(1)}, f32[4,24,256]{2,1,0:T(8,128)S(1)}, u32[]{:S(2)}, u32[]{:S(2)}) collective-permute-start(f32[4,24,256]{2,1,0:T(8,128)S(1)} %get-tuple-element.57), channel_id=1, source_target_pairs={{0,16},{8,24},{16,0},{24,8},{1,17},{9,25},{17,1},{25,9},{2,18},{10... | collective-permute-start | bytes 294920 | tf_op jit(solution)/shard_map/ppermute | solution.py:303
  132.5 4.6 %collective-permute-start.16 = (f32[4,24,256]{2,1,0:T(8,128)S(1)}, f32[4,24,256]{2,1,0:T(8,128)S(1)}, u32[]{:S(2)}, u32[]{:S(2)}) collective-permute-start(f32[4,24,256]{2,1,0:T(8,128)S(1)} %get-tuple-element.57), channel_id=1, source_target_pairs={{0,24},{8,0},{16,8},{24,16},{1,25},{9,1},{17,9},{25,17},{2,26},{10... | collective-permute-start | bytes 294920 | tf_op jit(solution)/shard_map/ppermute | solution.py:303
  137.1 1.8 %collective-permute-start.17 = (f32[16,24,256]{2,1,0:T(8,128)S(1)}, f32[16,24,256]{2,1,0:T(8,128)S(1)}, u32[]{:S(2)}, u32[]{:S(2)}) collective-permute-start(f32[16,24,256]{2,1,0:T(8,128)S(1)} %constant_dynamic-update-slice_fusion), channel_id=1, source_target_pairs={{0,1},{1,0},{2,3},{3,2},{4,5},{5,4},{6,7},{7,6},{8,9},{9,8},{10,11... | collective-permute-start | bytes 1179656 | tf_op jit(solution)/shard_map/ppermute | solution.py:253
  139.5 0.9 copy-start.9

commit v10 on v8

--- a/solution.py
+++ b/solution.py
@@ -202,7 +202,7 @@
             query, upstream = qkv[which, 0, at, part], us[pl.ds(a, SUB, stride=run), :]
             filtered = conv[which, 0, at, part] + added(list(state))
             os[pl.ds(a, SUB, stride=run), :] = query * filtered
-            gs[0, pl.ds(a, SUB, stride=run), :] = upstream * filtered
+            gs[0, at] = upstream * filtered
             if a + 1 < run:
                 state = [state[n] * decay[n] for n in range(poles)]
         output[:, lanes] = os[0:rows].astype(BF16)
@@ -214,18 +214,21 @@
         for a in range(run - 1, -1, -1):
             at = slice(SUB * a, SUB * a + SUB)
             grad = conv[which, 1, at, part] + added(list(state))
-            gs[1, pl.ds(a, SUB, stride=run), :] = grad * qkv[which, 2, at, part]
-            gs[2, pl.ds(a, SUB, stride=run), :] = grad * qkv[which, 1, at, part]
+            gs[1, at] = grad * qkv[which, 2, at, part]
+            gs[2, at] = grad * qkv[which, 1, at, part]
             if a:
                 state = [state[n] * decay[n] for n in range(poles)]
 
         for j in range(3):
             tap = [spread(filt[j, i : i + 1, lanes]) for i in range(taps)]
-            grads = [gs[j, pl.ds(a, SUB, stride=run), :] for a in range(taps - 1)]
+            grads = [gs[j, SUB * a : SUB * a + SUB] for a in range(taps - 1)]
+            beyond = [pltpu.roll(value, SUB - 1, 0) for value in grads]
             views = [ps[j, pl.ds(SUB + a, SUB, stride=run), :] for a in range(1 - taps, 0)]
             sums_of = [None] * taps
             for a in range(run):
-                grads = grads[-(taps - 1) :] + [gs[j, pl.ds(a + taps - 1, SUB, stride=run), :]]
+                ahead = a + taps - 1
+                ahead = gs[j, SUB * ahead : SUB * ahead + SUB] if ahead < run else beyond[ahead - run]
+                grads = grads[-(taps - 1) :] + [ahead]
                 views = views[-(taps - 1) :] + [ps[j, pl.ds(SUB + a, SUB, stride=run), :]]
                 total = added([tap[i] * grads[i] for i in range(taps)])
                 os[pl.ds(a, SUB, stride=run), :] = total
@@ -280,12 +283,14 @@
         first, kept = lax.optimization_barrier((first, kept))
         sent = jnp.where(odd, chip_e, chip_a) + f_chip * first
         near = lax.ppermute(sent, "ctx", [(2, 4), (3, 5), (4, 2), (5, 3)])
-        far = lax.ppermute(sent, "ctx", [(2, 6), (3, 7), (4, 0), (5, 1)])
         kept = beside[1](sent, kept)
-        near, far, kept = lax.optimization_barrier((near, far, kept))
+        near, kept = lax.optimization_barrier((near, kept))
+        far = lax.ppermute(near, "ctx", [(4, 6), (5, 7), (2, 0), (3, 1)])
+        kept = beside[2](near, kept)
+        far, kept = lax.optimization_barrier((far, kept))
         far = first + f_chip * far
         return jnp.where(odd, far, near), jnp.where(odd, near, far), kept
-    kept = beside[1](chip_e, beside[0](chip_e, None))
+    kept = beside[2](chip_e, beside[1](chip_e, beside[0](chip_e, None)))
     before, after = jnp.zeros_like(chip_e), jnp.zeros_like(chip_a)
     reach = 1
     while reach < chips:
@@ -298,35 +303,33 @@
     return before, after, kept
 
 
-def chain(left, right, turn):
-    index, dp = lax.axis_index("ctx"), lax.axis_index("dp")
-    reaches = []
-    while 2 ** len(reaches) < lax.axis_size("dp"):
-        reaches.append(2 ** len(reaches))
-    chips = []
-    while 2 ** (len(chips) + 1) < lax.axis_size("ctx"):
-        chips.append(2 ** (len(chips) + 1))
-    steps = [("ctx", 1, lax.rem(index, 2) == 0)]
-    steps = steps + [("dp", step, lax.rem(dp // step, 2) == 0) for step in reaches[::turn]]
-    for axis, step, low in steps:
-        value = jnp.where(low, left, right) + paired(jnp.where(low, right, left), axis, step)
-        half = value.shape[0] // 2
-        left, right = value[:half], value[half:]
-    for step in chips[::turn]:
-        value = value + paired(value, "ctx", step)
-    for axis, step, low in reversed(steps):
-        other = paired(value, axis, step)
-        left, right = jnp.where(low, value, other), jnp.where(low, other, value)
-        value = jnp.concatenate([left, right], axis=0)
-    return left, right
+def rotated(value, axis, steps):
+    count = lax.axis_size(axis)
+    return lax.ppermute(value, axis, [(s, (s + steps) % count) for s in range(count)])
 
 
 def summed(value):
-    quarter = value.shape[0] // 4
-    parts = [value[k * quarter : (k + 1) * quarter] for k in range(4)]
-    left, right = chain(parts[0], parts[2], 1)
-    other_left, other_right = chain(parts[1], parts[3], -1)
-    return jnp.concatenate([left, other_left, right, other_right], axis=0)
+    dp, parts = lax.axis_index("dp"), lax.axis_size("dp")
+    low = lax.rem(lax.axis_index("ctx"), 2) == 0
+    half = value.shape[0] // 2
+    left, right = value[:half], value[half:]
+    value = jnp.where(low, left, right) + swapped(jnp.where(low, right, left))
+    size = half // parts
+    piece = lambda k: lax.dynamic_slice_in_dim(value, lax.rem(dp + k, parts) * size, size, 0)
+    total = piece(0)
+    for term in [rotated(piece(k), "dp", k) for k in range(1, parts)]:
+        total = total + term
+    reach = 2
+    while reach < lax.axis_size("ctx"):
+        total = total + paired(total, "ctx", reach)
+        reach = 2 * reach
+    value = jnp.zeros((half,) + value.shape[1:], F32)
+    for k in range(parts):
+        term = rotated(total, "dp", k) if k else total
+        at = lax.rem(dp + parts - k, parts) * size
+        value = lax.dynamic_update_slice_in_dim(value, term, at, 0)
+    other = swapped(value)
+    return jnp.concatenate([jnp.where(low, value, other), jnp.where(low, other, value)], axis=0)
 
 
 def local(projected, short_filter, residues, decay_rates, skip_gain, cotangent):
@@ -447,10 +450,10 @@
         return call
 
     steps = width // many
-    cut = (steps + 1) // 3
+    cuts = (0, steps // 4, (5 * steps) // 8, steps)
     other, chip_e, chip_a = joined(ends, f_all)
     before, after, (conv, from_e, from_a, skip_sum) = scanned(
-        chip_e, chip_a, f_all, (blocks(0, cut), blocks(cut, steps))
+        chip_e, chip_a, f_all, [blocks(cuts[k], cuts[k + 1]) for k in range(3)]
     )
     both = jnp.stack([before, after])
     found = swapped(both)
@@ -460,7 +463,7 @@
     scratch = [
         pltpu.VMEM((3, held + SUB, LANES), F32),
         pltpu.VMEM((held, LANES), F32),
-        pltpu.VMEM((3, held + SUB, LANES), F32),
+        pltpu.VMEM((3, held, LANES), F32),
         pltpu.VMEM((held, LANES), F32),
         pltpu.VMEM((2, poles, LANES), F32),
     ]

time: 141 us -> 139 us (0.986)
  starting transfers between devices: 38 us -> 28.9 us
  waiting for transfers between devices: 18 us -> 22.9 us
  Pallas kernels: 74.9 us -> 76.7 us
    ppermute x17 -> x3, starting transfers between devices: 24.4 us -> 6.1 us  [paired(): lax.ppermute(value, axis, [(source, source ^ step) for source in lines or...]
    ppermute x1 -> x7, waiting for transfers between devices: 0.01 us -> 9.01 us  [the longest x6 7.01 us: rotated(): lax.ppermute(value, axis, [(s, (s + steps) % count) for s in range(count)])]
    ppermute x1 -> x7, starting transfers between devices: 1.42 us -> 10.4 us  [the longest x6 8.99 us: rotated(): lax.ppermute(value, axis, [(s, (s + steps) % count) for s in range(count)])]
    ppermute x17 -> x3, waiting for transfers between devices: 14.5 us -> 7 us  [paired(): lax.ppermute(value, axis, [(source, source ^ step) for source in lines or...]
    ppermute x3 -> x5, waiting for transfers between devices: 3.55 us -> 6.89 us  [swapped(): return lax.ppermute(value, 'ctx', [(s, s ^ 1) for s in range(count)])]
    pallas_call x2 -> x3, Pallas kernels: 20.1 us -> 22 us  [call(): pl.pallas_call(blocks_kernel, grid=(last - first,), in_specs=[pairs, stat...]
    ppermute x3 -> x5, starting transfers between devices: 10.1 us -> 10.3 us  [swapped(): return lax.ppermute(value, 'ctx', [(s, s ^ 1) for s in range(count)])]
  transfers between devices with their start and end apart: 24 -> 18, of which waited for: 14 -> 14; matrix products, arithmetic and copies ran while one was open for 2% -> 2% of each run, Pallas kernels for 14% -> 16%
where the time goes in v10:
time: 139 us; the launch traced here: 138 us
  Pallas kernels  76.7 us (55%)
  starting transfers between devices  28.9 us (21%)
  waiting for transfers between devices  22.9 us (16%)
  other arithmetic  4.39 us (3%)
  local copies, waits for them, and re-layouts  3.85 us (3%)
    pallas_call x1, Pallas kernels, local(): pl.pallas_call(final_kernel, grid=(width // each,), in_specs=[pl.BlockSpe...  32.5 us
    pallas_call x1, Pallas kernels, local(): pl.pallas_call(states_kernel, grid=(width // each,), in_specs=[pl.BlockSp...  22.2 us
    pallas_call x3, Pallas kernels, call(): pl.pallas_call(blocks_kernel, grid=(last - first,), in_specs=[pairs, stat...  22 us
    ppermute x5, starting transfers between devices, swapped(): return lax.ppermute(value, 'ctx', [(s, s ^ 1) for s in range(count)])  10.3 us
    ppermute x6, starting transfers between devices, rotated(): lax.ppermute(value, axis, [(s, (s + steps) % count) for s in range(count)])  8.99 us
    ppermute x6, waiting for transfers between devices, rotated(): lax.ppermute(value, axis, [(s, (s + steps) % count) for s in range(count)])  7.01 us
    ppermute x3, waiting for transfers between devices, paired(): lax.ppermute(value, axis, [(source, source ^ step) for source in lines or...  7 us
    ppermute x5, waiting for transfers between devices, swapped(): return lax.ppermute(value, 'ctx', [(s, s ^ 1) for s in range(count)])  6.89 us
  transfers between devices with their start and end apart: 18, of which 14 were waited for; matrix products, arithmetic and copies ran while one was open for 2% of the time, Pallas kernels for 16%

profile of v10, /device:TPU:0, one launch (start us, length us, event | category | flops | bytes accessed | tf_op | source)
XLA Modules:
  0.0 137.8 jit_solution(3353983011838840716)
XLA Ops:
  0.6 0.0 copy-start.13
  0.7 1.1 fusion.9
  1.8 1.2 fusion.8
  3.0 0.1 broadcast_select_fusion.2
  3.2 0.7 collective-permute-start.1
  3.8 0.7 collective-permute-start
  4.5 5.7 %collective-permute-start.2 = (bf16[4,8,8192]{2,1,0:T(8,128)(2,1)S(1)}, bf16[4,8,8192]{2,1,0:T(8,128)(2,1)S(1)}, u32[]{:S(2)}, u32[]{:S(2)}) collective-permute-start(bf16[4,8,8192]{2,1,0:T(8,128)(2,1)S(1)} %get-tuple-element.92), channel_id=1, source_target_pairs={{0,1},{1,0},{2,3},{3,2},{4,5},{5,4},{6,7},{7,6},{8,9},{9,8},{10,11... | collective-permute-start | bytes 1572872 | tf_op jit(solution)/shard_map/ppermute | solution.py:256
  10.2 0.2 multiply_exponential_fusion
  10.6 1.2 collective-permute-done.2.hi
  11.8 0.0 copy-start.17
  11.8 22.2 %states.1 = (f32[16,3,136,512]{3,2,1,0:T(8,128)}, f32[16,2,136,512]{3,2,1,0:T(8,128)}, f32[16,16,8,512]{3,2,1,0:T(8,128)}, f32[16,16,8,512]{3,2,1,0:T(8,128)}, f32[2,16,16,512]{3,2,1,0:T(8,128)}) custom-call(s32[1]{0:T(128)} %bitcast.core, bf16[3,128,8192]{2,1,0:T(8,128)(2,1)} %bitcast.84, bf16[2,8,8192]{2,1,0:T(8,128)(2,1)S(1)} %collective-permute-done.hx_low, ...), custom_call_target="tpu_custom_call" | custom-call | tf_op jit(solution)/shard_map/states/pallas_call | solution.py:398
  34.0 0.0 copy-start.15
  34.0 0.0 copy-start.16
  34.0 0.0 copy-start.6
  34.0 4.3 %collective-permute-start.3 = (f32[2,16,16,512]{3,2,1,0:T(8,128)}, f32[2,16,16,512]{3,2,1,0:T(8,128)S(1)}, u32[]{:S(2)}, u32[]{:S(2)}) collective-permute-start(f32[2,16,16,512]{3,2,1,0:T(8,128)} %get-tuple-element.43), channel_id=1, source_target_pairs={{0,1},{1,0},{2,3},{3,2},{4,5},{5,4},{6,7},{7,6},{8,9},{9,8},{10,11... | collective-permute-start | bytes 3145736 | tf_op jit(solution)/shard_map/ppermute | solution.py:256
  38.4 0.1 multiply_exponential_fusion.1
  38.5 0.8 slice_multiply_fusion
  39.3 1.0 multiply_reduce_fusion.near
  40.2 0.6 collective-permute-done.3.other
  40.9 1.2 dynamic-slice_select_fusion.1
  42.0 0.1 broadcast_select_fusion.6
  42.1 1.7 %collective-permute-start.4 = (f32[8,16,512]{2,1,0:T(8,128)S(1)}, f32[8,16,512]{2,1,0:T(8,128)S(1)}, u32[]{:S(2)}, u32[]{:S(2)}) collective-permute-start(f32[8,16,512]{2,1,0:T(8,128)S(1)} %broadcast_select_fusion.6), channel_id=1, source_target_pairs={{0,2},{1,3},{2,0},{3,1},{4,6},{5,7},{6,4},{7,5},{8,10},{9,11},{10,... | collective-permute-start | bytes 786440 | tf_op jit(solution)/shard_map/ppermute | solution.py:272
  43.8 0.3 broadcast_select_fusion
  44.1 5.8 %blocks.3 = (f32[16,2,136,512]{3,2,1,0:T(8,128)}, f32[16,16,8,512]{3,2,1,0:T(8,128)}, f32[16,16,8,512]{3,2,1,0:T(8,128)}, f32[4,8,512]{2,1,0:T(8,128)S(1)}) custom-call(f32[16,2,136,512]{3,2,1,0:T(8,128)} %get-tuple-element.44.xg, f32[16,16,8,512]{3,2,1,0:T(8,128)} %get-tuple-element.45.blocks_e, ...), custom_call_target="tpu_custom_call", output_to_operand_aliasing={{0}: (0, {}), {1}: (1, {}), {2}: (2, {})} | custom-call | flops 62914560 | bytes 36700160 | tf_op jit(solution)/shard_map/blocks/pallas_call | solution.py:428
  50.0 0.8 collective-permute-done.4
  50.8 0.1 multiply_add_fusion.1
  50.9 0.7 collective-permute-start.5
  51.6 8.1 %blocks.4 = (f32[16,2,136,512]{3,2,1,0:T(8,128)}, f32[16,16,8,512]{3,2,1,0:T(8,128)}, f32[16,16,8,512]{3,2,1,0:T(8,128)}, f32[6,8,512]{2,1,0:T(8,128)S(1)}) custom-call(f32[16,2,136,512]{3,2,1,0:T(8,128)} %get-tuple-element.53.xg, f32[16,16,8,512]{3,2,1,0:T(8,128)} %get-tuple-element.54.blocks_e, ...), custom_call_target="tpu_custom_call", output_to_operand_aliasing={{0}: (0, {}), {1}: (1, {}), {2}: (2, {})} | custom-call | flops 62914560 | bytes 36700160 | tf_op jit(solution)/shard_map/blocks/pallas_call | solution.py:428
  59.8 1.4 %collective-permute-start.6 = (f32[8,16,512]{2,1,0:T(8,128)S(1)}, f32[8,16,512]{2,1,0:T(8,128)S(1)}, u32[]{:S(2)}, u32[]{:S(2)}) collective-permute-start(f32[8,16,512]{2,1,0:T(8,128)S(1)} %collective-permute-done.5), channel_id=1, source_target_pairs={{4,6},{5,7},{2,0},{3,1},{12,14},{13,15},{10,8},{11,9},{20,22},{21,... | collective-permute-start | bytes 786440 | tf_op jit(solution)/shard_map/ppermute | solution.py:288
  61.2 8.1 %blocks.5 = (f32[16,2,136,512]{3,2,1,0:T(8,128)}, f32[16,16,8,512]{3,2,1,0:T(8,128)}, f32[16,16,8,512]{3,2,1,0:T(8,128)}, f32[6,8,512]{2,1,0:T(8,128)S(1)}) custom-call(f32[16,2,136,512]{3,2,1,0:T(8,128)} %get-tuple-element.63.xg, f32[16,16,8,512]{3,2,1,0:T(8,128)} %get-tuple-element.64.blocks_e, ...), custom_call_target="tpu_custom_call", output_to_operand_aliasing={{0}: (0, {}), {1}: (1, {}), {2}: (2, {})} | custom-call | flops 62914560 | bytes 36700160 | tf_op jit(solution)/shard_map/blocks/pallas_call | solution.py:428
  69.3 2.0 %collective-permute-done.6 = f32[8,16,512]{2,1,0:T(8,128)S(1)} collective-permute-done((f32[8,16,512]{2,1,0:T(8,128)S(1)}, f32[8,16,512]{2,1,0:T(8,128)S(1)}, u32[]{:S(2)}, u32[]{:S(2)}) %collective-permute-start.6) | collective-permute-done | bytes 262176 | tf_op jit(solution)/shard_map/ppermute | solution.py:288
  71.3 0.1 select_bitcast_fusion.1
  71.4 0.1 collective-permute-start.7
  71.5 0.1 fusion
  71.6 1.8 %collective-permute-done.7.found = f32[2,8,16,512]{3,2,1,0:T(8,128)S(1)} collective-permute-done((f32[2,8,16,512]{3,2,1,0:T(8,128)S(1)}, f32[2,8,16,512]{3,2,1,0:T(8,128)S(1)}, u32[]{:S(2)}, u32[]{:S(2)}) %collective-permute-start.7) | collective-permute-done | bytes 524320 | tf_op jit(solution)/shard_map/ppermute | solution.py:256
  73.4 32.5 %final.1 = (bf16[128,8192]{1,0:T(8,128)(2,1)}, bf16[3,128,8192]{2,1,0:T(8,128)(2,1)}, f32[32,24,256]{2,1,0:T(8,128)S(1)}) custom-call(s32[1]{0:T(128)} %bitcast.core, bf16[3,128,8192]{2,1,0:T(8,128)(2,1)} %bitcast.85, bf16[2,8,8192]{2,1,0:T(8,128)(2,1)S(1)} %copy-done.5, bf16[2,8,8192]{2,1,0:T(8,128)(2,1)S(1)} %copy-done.3, ...), custom_call_target="tpu_custom_call" | custom-call | tf_op jit(solution)/shard_map/final/pallas_call | solution.py:470
  105.9 0.1 slice_select_fusion
  105.9 0.2 collective-permute-start.8
  106.1 1.6 %collective-permute-done.8 = f32[16,24,256]{2,1,0:T(8,128)S(1)} collective-permute-done((f32[16,24,256]{2,1,0:T(8,128)S(1)}, f32[16,24,256]{2,1,0:T(8,128)S(1)}, u32[]{:S(2)}, u32[]{:S(2)}) %collective-permute-start.8) | collective-permute-done | bytes 393248 | tf_op jit(solution)/shard_map/ppermute | solution.py:256
  107.7 0.1 select_add_fusion
  107.8 1.5 %collective-permute-start.9 = (f32[4,24,256]{2,1,0:T(8,128)S(1)}, f32[4,24,256]{2,1,0:T(8,128)S(1)}, u32[]{:S(2)}, u32[]{:S(2)}) collective-permute-start(f32[4,24,256]{2,1,0:T(8,128)S(1)} %get-tuple-element.100), channel_id=1, source_target_pairs={{0,8},{8,16},{16,24},{24,0},{1,9},{9,17},{17,25},{25,1},{2,10},{10... | collective-permute-start | bytes 294920 | tf_op jit(solution)/shard_map/ppermute | solution.py:308
  109.4 1.4 %collective-permute-start.11 = (f32[4,24,256]{2,1,0:T(8,128)S(1)}, f32[4,24,256]{2,1,0:T(8,128)S(1)}, u32[]{:S(2)}, u32[]{:S(2)}) collective-permute-start(f32[4,24,256]{2,1,0:T(8,128)S(1)} %get-tuple-element.101), channel_id=1, source_target_pairs={{0,24},{8,0},{16,8},{24,16},{1,25},{9,1},{17,9},{25,17},{2,26},{10... | collective-permute-start | bytes 294920 | tf_op jit(solution)/shard_map/ppermute | solution.py:308
  110.8 1.5 %collective-permute-start.10 = (f32[4,24,256]{2,1,0:T(8,128)S(1)}, f32[4,24,256]{2,1,0:T(8,128)S(1)}, u32[]{:S(2)}, u32[]{:S(2)}) collective-permute-start(f32[4,24,256]{2,1,0:T(8,128)S(1)} %get-tuple-element.102), channel_id=1, source_target_pairs={{0,16},{8,24},{16,0},{24,8},{1,17},{9,25},{17,1},{25,9},{2,18},{10... | collective-permute-start | bytes 294920 | tf_op jit(solution)/shard_map/ppermute | solution.py:308
  112.3 2.1 %collective-permute-done.9 = f32[4,24,256]{2,1,0:T(8,128)S(1)} collective-permute-done((f32[4,24,256]{2,1,0:T(8,128)S(1)}, f32[4,24,256]{2,1,0:T(8,128)S(1)}, u32[]{:S(2)}, u32[]{:S(2)}) %collective-permute-start.9) | collective-permute-done | bytes 98336 | tf_op jit(solution)/shard_map/ppermute | solution.py:308
  114.4 1.4 collective-permute-done.11
  115.8 0.0 collective-permute-done.10
  115.8 2.5 %collective-permute-start.12 = (f32[4,24,256]{2,1,0:T(8,128)S(1)}, f32[4,24,256]{2,1,0:T(8,128)S(1)}, u32[]{:S(2)}, u32[]{:S(2)}) collective-permute-start(f32[4,24,256]{2,1,0:T(8,128)S(1)} %add_add_fusion), channel_id=1, source_target_pairs={{0,2},{1,3},{2,0},{3,1},{4,6},{5,7},{6,4},{7,5},{8,10},{9,11},{10,... | collective-permute-start | bytes 294920 | tf_op jit(solution)/shard_map/ppermute | solution.py:272
  118.3 2.6 %collective-permute-done.12 = f32[4,24,256]{2,1,0:T(8,128)S(1)} collective-permute-done((f32[4,24,256]{2,1,0:T(8,128)S(1)}, f32[4,24,256]{2,1,0:T(8,128)S(1)}, u32[]{:S(2)}, u32[]{:S(2)}) %collective-permute-start.12) | collective-permute-done | bytes 98336 | tf_op jit(solution)/shard_map/ppermute | solution.py:272
  120.9 2.0 %collective-permute-start.13 = (f32[4,24,256]{2,1,0:T(8,128)S(1)}, f32[4,24,256]{2,1,0:T(8,128)S(1)}, u32[]{:S(2)}, u32[]{:S(2)}) collective-permute-start(f32[4,24,256]{2,1,0:T(8,128)S(1)} %add.93), channel_id=1, source_target_pairs={{0,4},{1,5},{2,6},{3,7},{4,0},{5,1},{6,2},{7,3},{8,12},{9,13},{10,... | collective-permute-start | bytes 294920 | tf_op jit(solution)/shard_map/ppermute | solution.py:272
  122.9 3.6 %collective-permute-done.13 = f32[4,24,256]{2,1,0:T(8,128)S(1)} collective-permute-done((f32[4,24,256]{2,1,0:T(8,128)S(1)}, f32[4,24,256]{2,1,0:T(8,128)S(1)}, u32[]{:S(2)}, u32[]{:S(2)}) %collective-permute-start.13) | collective-permute-done | bytes 98336 | tf_op jit(solution)/shard_map/ppermute | solution.py:272
  126.6 2.1 %collective-permute-start.14 = (f32[4,24,256]{2,1,0:T(8,128)S(1)}, f32[4,24,256]{2,1,0:T(8,128)S(1)}, u32[]{:S(2)}, u32[]{:S(2)}) collective-permute-start(f32[4,24,256]{2,1,0:T(8,128)S(1)} %get-tuple-element.81), channel_id=1, source_target_pairs={{0,8},{8,16},{16,24},{24,0},{1,9},{9,17},{17,25},{25,1},{2,10},{10... | collective-permute-start | bytes 294920 | tf_op jit(solution)/shard_map/ppermute | solution.py:308
  128.6 1.4 collective-permute-start.15
  130.0 1.1 collective-permute-start.16
  131.0 1.1 collective-permute-done.14
  132.1 1.1 collective-permute-done.15
  133.3 1.4 collective-permute-done.16
  134.6 0.1 collective-permute-start.17
  134.7 1.7 %collective-permute-done.17 = f32[16,24,256]{2,1,0:T(8,128)S(1)} collective-permute-done((f32[16,24,256]{2,1,0:T(8,128)S(1)}, f32[16,24,256]{2,1,0:T(8,128)S(1)}, u32[]{:S(2)}, u32[]{:S(2)}) %collective-permute-start.17) | collective-permute-done | bytes 393248 | tf_op jit(solution)/shard_map/ppermute | solution.py:256
  136.4 0.1 broadcast_select_fusion.5
  136.5 0.1 maximum_bitcast_fusion
  136.5 0.3 copy.25
  136.8 0.1 reshape.25
  137.0 0.7 slice.97
  137.7 0.2 copy-done.9
  (50 shorter events, 0.4 us)
Async XLA Ops:
  0.6 9.6 %copy-start.13 = (f32[4,8]{1,0:T(4,128)S(1)}, f32[4,8]{1,0:T(4,128)}, u32[]{:S(2)}) copy-start(f32[4,8]{1,0:T(4,128)} %constant.79) | copy-start | bytes 388
  0.6 11.1 %copy-start = (bf16[1,128,8192]{2,1,0:T(8,128)(2,1)S(1)}, bf16[1,128,8192]{2,1,0:T(8,128)(2,1)}, u32[]{:S(2)}) copy-start(bf16[1,128,8192]{2,1,0:T(8,128)(2,1)} %param.16) | copy-start | bytes 6291460
  0.7 9.6 %copy-start.11 = (f32[512,16]{0,1:T(8,128)S(1)}, f32[512,16]{0,1:T(8,128)}, u32[]{:S(2)}) copy-start(f32[512,16]{0,1:T(8,128)} %param.14) | copy-start | bytes 98308
  0.7 11.1 %copy-start.1 = (f32[3,7,8192]{2,1,0:T(8,128)S(1)}, f32[3,7,8192]{2,1,0:T(8,128)}, u32[]{:S(2)}) copy-start(f32[3,7,8192]{2,1,0:T(8,128)} %filt.3) | copy-start | bytes 2064388
  0.7 9.8 %copy-start.12 = (f32[512,16]{0,1:T(8,128)S(1)}, f32[512,16]{0,1:T(8,128)}, u32[]{:S(2)}) copy-start(f32[512,16]{0,1:T(8,128)} %param.14) | copy-start | bytes 98308
  3.2 7.4 %collective-permute-start.1 = (bf16[2,8,8192]{2,1,0:T(8,128)(2,1)S(1)}, bf16[2,8,8192]{2,1,0:T(8,128)(2,1)S(1)}, u32[]{:S(2)}, u32[]{:S(2)}) collective-permute-start(bf16[2,8,8192]{2,1,0:T(8,128)(2,1)S(1)} %get-tuple-element.98), channel_id=1, source_target_pairs={{1,2},{3,4},{5,6},{2,1},{4,3},{6,5},{9,10},{11,12},{13,14},{10,9},... | collective-permute-start | bytes 786440 | tf_op jit(solution)/shard_map/ppermute | solution.py:352
  3.8 6.7 %collective-permute-start = (bf16[2,8,8192]{2,1,0:T(8,128)(2,1)S(1)}, bf16[2,8,8192]{2,1,0:T(8,128)(2,1)S(1)}, u32[]{:S(2)}, u32[]{:S(2)}) collective-permute-start(bf16[2,8,8192]{2,1,0:T(8,128)(2,1)S(1)} %get-tuple-element.99), channel_id=1, source_target_pairs={{1,2},{3,4},{5,6},{2,1},{4,3},{6,5},{9,10},{11,12},{13,14},{10,9},... | collective-permute-start | bytes 786440 | tf_op jit(solution)/shard_map/ppermute | solution.py:352
  4.5 7.2 %collective-permute-start.2 = (bf16[4,8,8192]{2,1,0:T(8,128)(2,1)S(1)}, bf16[4,8,8192]{2,1,0:T(8,128)(2,1)S(1)}, u32[]{:S(2)}, u32[]{:S(2)}) collective-permute-start(bf16[4,8,8192]{2,1,0:T(8,128)(2,1)S(1)} %get-tuple-element.92), channel_id=1, source_target_pairs={{0,1},{1,0},{2,3},{3,2},{4,5},{5,4},{6,7},{7,6},{8,9},{9,8},{10,11... | collective-permute-start | bytes 1572872 | tf_op jit(solution)/shard_map/ppermute | solution.py:256
  10.5 1.3 copy-start.7
  10.6 23.4 %copy-start.2 = (bf16[2,8,8192]{2,1,0:T(8,128)(2,1)}, bf16[2,8,8192]{2,1,0:T(8,128)(2,1)S(1)}, u32[]{:S(2)}) copy-start(bf16[2,8,8192]{2,1,0:T(8,128)(2,1)S(1)} %collective-permute-done.1.hx_high) | copy-start | bytes 786436
  10.6 23.4 %copy-start.4 = (bf16[2,8,8192]{2,1,0:T(8,128)(2,1)}, bf16[2,8,8192]{2,1,0:T(8,128)(2,1)S(1)}, u32[]{:S(2)}) copy-start(bf16[2,8,8192]{2,1,0:T(8,128)(2,1)S(1)} %collective-permute-done.hx_low) | copy-start | bytes 786436
  11.8 26.6 %copy-start.14 = (f32[4]{0:T(128)S(1)}, f32[4]{0:T(128)}, u32[]{:S(2)}) copy-start(f32[4]{0:T(128)} %constant.82) | copy-start | bytes 52
  11.8 27.5 %copy-start.17 = (f32[24]{0:T(128)S(1)}, f32[24]{0:T(128)}, u32[]{:S(2)}) copy-start(f32[24]{0:T(128)} %constant.80) | copy-start | bytes 292
  34.0 9.8 %copy-start.15 = (pred[4,8]{1,0:T(4,128)(4,1)S(1)}, pred[4,8]{1,0:T(4,128)(4,1)}, u32[]{:S(2)}) copy-start(pred[4,8]{1,0:T(4,128)(4,1)} %constant.83) | copy-start | bytes 100
  34.0 9.8 %copy-start.16 = (pred[4,8]{1,0:T(4,128)(4,1)S(1)}, pred[4,8]{1,0:T(4,128)(4,1)}, u32[]{:S(2)}) copy-start(pred[4,8]{1,0:T(4,128)(4,1)} %constant.81) | copy-start | bytes 100
  34.0 10.1 %copy-start.6 = (f32[8192]{0:T(1024)S(1)}, f32[8192]{0:T(1024)}, u32[]{:S(2)}) copy-start(f32[8192]{0:T(1024)} %param.15) | copy-start | bytes 98308
  34.0 6.8 %collective-permute-start.3 = (f32[2,16,16,512]{3,2,1,0:T(8,128)}, f32[2,16,16,512]{3,2,1,0:T(8,128)S(1)}, u32[]{:S(2)}, u32[]{:S(2)}) collective-permute-start(f32[2,16,16,512]{3,2,1,0:T(8,128)} %get-tuple-element.43), channel_id=1, source_target_pairs={{0,1},{1,0},{2,3},{3,2},{4,5},{5,4},{6,7},{7,6},{8,9},{9,8},{10,11... | collective-permute-start | bytes 3145736 | tf_op jit(solution)/shard_map/ppermute | solution.py:256
  42.1 8.7 %collective-permute-start.4 = (f32[8,16,512]{2,1,0:T(8,128)S(1)}, f32[8,16,512]{2,1,0:T(8,128)S(1)}, u32[]{:S(2)}, u32[]{:S(2)}) collective-permute-start(f32[8,16,512]{2,1,0:T(8,128)S(1)} %broadcast_select_fusion.6), channel_id=1, source_target_pairs={{0,2},{1,3},{2,0},{3,1},{4,6},{5,7},{6,4},{7,5},{8,10},{9,11},{10,... | collective-permute-start | bytes 786440 | tf_op jit(solution)/shard_map/ppermute | solution.py:272
  50.9 8.8 %collective-permute-start.5 = (f32[8,16,512]{2,1,0:T(8,128)S(1)}, f32[8,16,512]{2,1,0:T(8,128)S(1)}, u32[]{:S(2)}, u32[]{:S(2)}) collective-permute-start(f32[8,16,512]{2,1,0:T(8,128)S(1)} %multiply_add_fusion.1), channel_id=1, source_target_pairs={{2,4},{3,5},{4,2},{5,3},{10,12},{11,13},{12,10},{13,11},{18,20},{1... | collective-permute-start | bytes 786440 | tf_op jit(solution)/shard_map/ppermute | solution.py:285
  59.7 11.8 %copy-start.8 = (f32[4,16,8,512]{3,2,1,0:T(8,128)S(1)}, f32[4,16,8,512]{3,2,1,0:T(8,128)}, u32[]{:S(2)}) copy-start(f32[4,16,8,512]{3,2,1,0:T(8,128)} %copy-done.7) | copy-start | bytes 3145732
  59.7 11.8 %copy-start.10 = (f32[512,16]{0,1:T(8,128)S(1)}, f32[512,16]{0,1:T(8,128)}, u32[]{:S(2)}) copy-start(f32[512,16]{0,1:T(8,128)} %param.13) | copy-start | bytes 98308
  59.8 11.5 %collective-permute-start.6 = (f32[8,16,512]{2,1,0:T(8,128)S(1)}, f32[8,16,512]{2,1,0:T(8,128)S(1)}, u32[]{:S(2)}, u32[]{:S(2)}) collective-permute-start(f32[8,16,512]{2,1,0:T(8,128)S(1)} %collective-permute-done.5), channel_id=1, source_target_pairs={{4,6},{5,7},{2,0},{3,1},{12,14},{13,15},{10,8},{11,9},{20,22},{21,... | collective-permute-start | bytes 786440 | tf_op jit(solution)/shard_map/ppermute | solution.py:288
  69.3 4.1 %copy-start.3 = (bf16[2,8,8192]{2,1,0:T(8,128)(2,1)S(1)}, bf16[2,8,8192]{2,1,0:T(8,128)(2,1)}, u32[]{:S(2)}) copy-start(bf16[2,8,8192]{2,1,0:T(8,128)(2,1)} %copy-done.2) | copy-start | bytes 786436
  69.3 4.1 %copy-start.5 = (bf16[2,8,8192]{2,1,0:T(8,128)(2,1)S(1)}, bf16[2,8,8192]{2,1,0:T(8,128)(2,1)}, u32[]{:S(2)}) copy-start(bf16[2,8,8192]{2,1,0:T(8,128)(2,1)} %copy-done.4) | copy-start | bytes 786436
  71.4 2.0 %collective-permute-start.7 = (f32[2,8,16,512]{3,2,1,0:T(8,128)S(1)}, f32[2,8,16,512]{3,2,1,0:T(8,128)S(1)}, u32[]{:S(2)}, u32[]{:S(2)}) collective-permute-start(f32[2,8,16,512]{3,2,1,0:T(8,128)S(1)} %pad_maximum_fusion.2.both), channel_id=1, source_target_pairs={{0,1},{1,0},{2,3},{3,2},{4,5},{5,4},{6,7},{7,6},{8,9},{9,8},{10,11... | collective-permute-start | bytes 1572872 | tf_op jit(solution)/shard_map/ppermute | solution.py:256
  105.9 1.8 %collective-permute-start.8 = (f32[16,24,256]{2,1,0:T(8,128)S(1)}, f32[16,24,256]{2,1,0:T(8,128)S(1)}, u32[]{:S(2)}, u32[]{:S(2)}) collective-permute-start(f32[16,24,256]{2,1,0:T(8,128)S(1)} %slice_select_fusion), channel_id=1, source_target_pairs={{0,1},{1,0},{2,3},{3,2},{4,5},{5,4},{6,7},{7,6},{8,9},{9,8},{10,11... | collective-permute-start | bytes 1179656 | tf_op jit(solution)/shard_map/ppermute | solution.py:256
  107.8 6.6 %collective-permute-start.9 = (f32[4,24,256]{2,1,0:T(8,128)S(1)}, f32[4,24,256]{2,1,0:T(8,128)S(1)}, u32[]{:S(2)}, u32[]{:S(2)}) collective-permute-start(f32[4,24,256]{2,1,0:T(8,128)S(1)} %get-tuple-element.100), channel_id=1, source_target_pairs={{0,8},{8,16},{16,24},{24,0},{1,9},{9,17},{17,25},{25,1},{2,10},{10... | collective-permute-start | bytes 294920 | tf_op jit(solution)/shard_map/ppermute | solution.py:308
  109.4 6.4 %collective-permute-start.11 = (f32[4,24,256]{2,1,0:T(8,128)S(1)}, f32[4,24,256]{2,1,0:T(8,128)S(1)}, u32[]{:S(2)}, u32[]{:S(2)}) collective-permute-start(f32[4,24,256]{2,1,0:T(8,128)S(1)} %get-tuple-element.101), channel_id=1, source_target_pairs={{0,24},{8,0},{16,8},{24,16},{1,25},{9,1},{17,9},{25,17},{2,26},{10... | collective-permute-start | bytes 294920 | tf_op jit(solution)/shard_map/ppermute | solution.py:308
  110.8 5.0 %collective-permute-start.10 = (f32[4,24,256]{2,1,0:T(8,128)S(1)}, f32[4,24,256]{2,1,0:T(8,128)S(1)}, u32[]{:S(2)}, u32[]{:S(2)}) collective-permute-start(f32[4,24,256]{2,1,0:T(8,128)S(1)} %get-tuple-element.102), channel_id=1, source_target_pairs={{0,16},{8,24},{16,0},{24,8},{1,17},{9,25},{17,1},{25,9},{2,18},{10... | collective-permute-start | bytes 294920 | tf_op jit(solution)/shard_map/ppermute | solution.py:308
  115.8 5.1 %collective-permute-start.12 = (f32[4,24,256]{2,1,0:T(8,128)S(1)}, f32[4,24,256]{2,1,0:T(8,128)S(1)}, u32[]{:S(2)}, u32[]{:S(2)}) collective-permute-start(f32[4,24,256]{2,1,0:T(8,128)S(1)} %add_add_fusion), channel_id=1, source_target_pairs={{0,2},{1,3},{2,0},{3,1},{4,6},{5,7},{6,4},{7,5},{8,10},{9,11},{10,... | collective-permute-start | bytes 294920 | tf_op jit(solution)/shard_map/ppermute | solution.py:272
  120.9 5.6 %collective-permute-start.13 = (f32[4,24,256]{2,1,0:T(8,128)S(1)}, f32[4,24,256]{2,1,0:T(8,128)S(1)}, u32[]{:S(2)}, u32[]{:S(2)}) collective-permute-start(f32[4,24,256]{2,1,0:T(8,128)S(1)} %add.93), channel_id=1, source_target_pairs={{0,4},{1,5},{2,6},{3,7},{4,0},{5,1},{6,2},{7,3},{8,12},{9,13},{10,... | collective-permute-start | bytes 294920 | tf_op jit(solution)/shard_map/ppermute | solution.py:272
  126.6 5.6 %collective-permute-start.14 = (f32[4,24,256]{2,1,0:T(8,128)S(1)}, f32[4,24,256]{2,1,0:T(8,128)S(1)}, u32[]{:S(2)}, u32[]{:S(2)}) collective-permute-start(f32[4,24,256]{2,1,0:T(8,128)S(1)} %get-tuple-element.81), channel_id=1, source_target_pairs={{0,8},{8,16},{16,24},{24,0},{1,9},{9,17},{17,25},{25,1},{2,10},{10... | collective-permute-start | bytes 294920 | tf_op jit(solution)/shard_map/ppermute | solution.py:308
  128.6 4.6 %collective-permute-start.15 = (f32[4,24,256]{2,1,0:T(8,128)S(1)}, f32[4,24,256]{2,1,0:T(8,128)S(1)}, u32[]{:S(2)}, u32[]{:S(2)}) collective-permute-start(f32[4,24,256]{2,1,0:T(8,128)S(1)} %get-tuple-element.81), channel_id=1, source_target_pairs={{0,16},{8,24},{16,0},{24,8},{1,17},{9,25},{17,1},{25,9},{2,18},{10... | collective-permute-start | bytes 294920 | tf_op jit(solution)/shard_map/ppermute | solution.py:308
  130.0 4.6 %collective-permute-start.16 = (f32[4,24,256]{2,1,0:T(8,128)S(1)}, f32[4,24,256]{2,1,0:T(8,128)S(1)}, u32[]{:S(2)}, u32[]{:S(2)}) collective-permute-start(f32[4,24,256]{2,1,0:T(8,128)S(1)} %get-tuple-element.81), channel_id=1, source_target_pairs={{0,24},{8,0},{16,8},{24,16},{1,25},{9,1},{17,9},{25,17},{2,26},{10... | collective-permute-start | bytes 294920 | tf_op jit(solution)/shard_map/ppermute | solution.py:308
  134.6 1.8 %collective-permute-start.17 = (f32[16,24,256]{2,1,0:T(8,128)S(1)}, f32[16,24,256]{2,1,0:T(8,128)S(1)}, u32[]{:S(2)}, u32[]{:S(2)}) collective-permute-start(f32[16,24,256]{2,1,0:T(8,128)S(1)} %constant_dynamic-update-slice_fusion), channel_id=1, source_target_pairs={{0,1},{1,0},{2,3},{3,2},{4,5},{5,4},{6,7},{7,6},{8,9},{9,8},{10,11... | collective-permute-start | bytes 1179656 | tf_op jit(solution)/shard_map/ppermute | solution.py:256
  136.9 0.9 copy-start.9

commit v11 on v10

--- a/solution.py
+++ b/solution.py
@@ -46,7 +46,7 @@
     return values[0]
 
 
-def states_kernel(core, p, hx_low, hx_high, hi, u, filt, f1, we, wb, qkv, xg, blocks_e, blocks_a, ends, xs):
+def states_kernel(core, p, hx, hi, u, filt, f1, we, wb, qkv, xg, blocks_e, blocks_a, ends, xs):
     rows = p.shape[1]
     run = (rows + SUB) // SUB
     taps = filt.shape[1]
@@ -61,13 +61,12 @@
         which = lt // tiles
         inside = lax.broadcasted_iota(jnp.int32, (SUB, LANES), 0) < SUB - 1
         for j in range(3):
-            across = (hx_low, hx_high)[j // 2][j % 2, :, lanes].astype(F32)
-            within = hi[j, :, lanes].astype(F32)
+            across, within = hx[j, :, lanes].astype(F32), hi[j, :, lanes].astype(F32)
             xs[j, 0:SUB] = jnp.where(first, across, within)
             xs[j, SUB : SUB + rows] = p[j, :, lanes].astype(F32)
             xs[j, SUB + rows :] = jnp.where(first, within, across)
         xs[3, SUB : SUB + rows] = u[:, lanes].astype(F32)
-        across, within = hx_high[1, :, lanes].astype(F32), hi[3, :, lanes].astype(F32)
+        across, within = hx[3, :, lanes].astype(F32), hi[3, :, lanes].astype(F32)
         xs[3, SUB + rows :] = jnp.where(first, within, across)
 
         def mixed(j):
@@ -157,7 +156,7 @@
 
 
 def final_kernel(
-    core, p, hx_low, hx_high, hi, u, qkv, conv, from_e, from_a, skip_sum, both, found, other, filt, f1, f_all, cz, cy,
+    core, p, hx, hi, u, qkv, conv, from_e, from_a, skip_sum, both, found, other, filt, f1, f_all, cz, cy,
     output, grad_p, sums, ps, us, gs, os, es,
 ):
     rows = p.shape[1]
@@ -183,13 +182,12 @@
             close = other[side, which, :, part] + f_all[:, part] * far
             es[side] = jnp.where(first == (side == 0), far, close)
         for j in range(3):
-            across = (hx_low, hx_high)[j // 2][j % 2, :, lanes].astype(F32)
-            within = hi[j, :, lanes].astype(F32)
+            across, within = hx[j, :, lanes].astype(F32), hi[j, :, lanes].astype(F32)
             ps[j, 0:SUB] = jnp.where(first, across, within)
             ps[j, SUB : SUB + rows] = p[j, :, lanes].astype(F32)
             ps[j, SUB + rows :] = jnp.where(first, within, across)
         us[0:rows] = u[:, lanes].astype(F32)
-        across, within = hx_high[1, :, lanes].astype(F32), hi[3, :, lanes].astype(F32)
+        across, within = hx[3, :, lanes].astype(F32), hi[3, :, lanes].astype(F32)
         us[rows:] = jnp.where(first, within, across)
         decay = [spread(f1[n : n + 1, part]) for n in range(poles)]
 
@@ -343,14 +341,17 @@
     p = projected[0].transpose(1, 0, 2)
     u = cotangent[0]
     core = lax.rem(lax.axis_index("ctx"), 2)
-    head = jnp.concatenate([p[:, :SUB], u[None, :SUB]], axis=0)
-    tail = jnp.concatenate([p[:, rows - SUB :], u[None, rows - SUB :]], axis=0)
+
+    def edge(last):
+        start = jnp.where(last, rows - SUB, 0)
+        cut = lambda value, axis: lax.dynamic_slice_in_dim(value, start, SUB, axis)
+        return jnp.concatenate([cut(p, 1), cut(u, 0)[None]], axis=0)
+
     devices = lax.axis_size("ctx")
     across = [(k, k + 1) for k in range(1, devices - 1, 2)]
     across = across + [(target, source) for source, target in across]
-    sent = jnp.where(core == 0, head, tail)
-    hx = [lax.ppermute(sent[2 * k : 2 * k + 2], "ctx", across) for k in range(2)]
-    hi = swapped(jnp.where(core == 0, tail, head))
+    hx = lax.ppermute(edge(core == 1), "ctx", across)
+    hi = swapped(edge(core == 0))
 
     rate = decay_rates.T
     weight = residues.T
@@ -400,7 +401,7 @@
         grid=(width // each,),
         in_specs=[
             pl.BlockSpec(memory_space=pltpu.SMEM),
-            by_w(3, rows), by_w(2, SUB), by_w(2, SUB), by_w(4, SUB), by_w(rows), by_w(3, taps),
+            by_w(3, rows), by_w(4, SUB), by_w(4, SUB), by_w(rows), by_w(3, taps),
             fixed(f1), fixed(we), fixed(wb),
         ],
         out_specs=[
@@ -414,13 +415,13 @@
         scratch_shapes=[pltpu.VMEM((4, held + SUB, LANES), F32)],
         compiler_params=params,
         name="states",
-    )(core[None], p, *hx, hi, u, short_filter, f1, we, wb)
+    )(core[None], p, hx, hi, u, short_filter, f1, we, wb)
 
     many = 2 if width % 2 == 0 else 1
 
     def blocks(first, last):
-        states = by_block(poles, SUB, groups, count=many, first=first)
-        pairs = by_block(2, held, groups, count=many, first=first)
+        place = {"count": many, "first": first}
+        states, pairs = by_block(poles, SUB, groups, **place), by_block(2, held, groups, **place)
 
         def call(sent, kept):
             close, _ = lax.optimization_barrier((near, sent))
@@ -450,7 +451,7 @@
         return call
 
     steps = width // many
-    cuts = (0, steps // 4, (5 * steps) // 8, steps)
+    cuts = (0, (3 * steps) // 8, (5 * steps) // 8, steps)
     other, chip_e, chip_a = joined(ends, f_all)
     before, after, (conv, from_e, from_a, skip_sum) = scanned(
         chip_e, chip_a, f_all, [blocks(cuts[k], cuts[k + 1]) for k in range(3)]
@@ -472,7 +473,7 @@
         grid=(width // each,),
         in_specs=[
             pl.BlockSpec(memory_space=pltpu.SMEM),
-            by_w(3, rows), by_w(2, SUB), by_w(2, SUB), by_w(4, SUB), by_w(rows),
+            by_w(3, rows), by_w(4, SUB), by_w(4, SUB), by_w(rows),
             by_block(3, held, groups), by_block(2, held, groups), state_spec, state_spec,
             by_block(SUB, groups), halved, halved, ends_spec,
             by_w(3, taps), fixed(f1), fixed(f_all), fixed(cz), fixed(cy),
@@ -490,7 +491,7 @@
         compiler_params=params,
         name="final",
     )(
-        core[None], p, *hx, hi, u, qkv, conv, from_e, from_a, skip_sum, both, found, other, short_filter,
+        core[None], p, hx, hi, u, qkv, conv, from_e, from_a, skip_sum, both, found, other, short_filter,
         f1, f_all, cz, cy,
     )
 

time: 139 us -> 138 us (level)
  waiting for transfers between devices: 22.9 us -> 21.5 us
    slice x3 -> x0, local copies, waits for them, and re-layouts: 2.34 us -> none  [the longest x2 2.31 us: local(): head = jnp.concatenate([p[:, :SUB], u[None, :SUB]], axis=0)]
    dynamic_slice x0 -> x2, local copies, waits for them, and re-layouts: none -> 2.31 us  [edge(): cut = lambda value, axis: lax.dynamic_slice_in_dim(value, start, SUB, axis)]
    ppermute x3, waiting for transfers between devices: 7 us -> 5.2 us  [paired(): lax.ppermute(value, axis, [(source, source ^ step) for source in lines or...]
    ppermute x3, starting transfers between devices: 6.1 us -> 7.82 us  [paired(): lax.ppermute(value, axis, [(source, source ^ step) for source in lines or...]
  transfers between devices with their start and end apart: 18 -> 17, of which waited for: 14 -> 13; matrix products, arithmetic and copies ran while one was open for 2% -> 2% of each run, Pallas kernels for 16% -> 16%
where the time goes in v11:
time: 138 us; the launch traced here: 137 us
  Pallas kernels  76.9 us (56%)
  starting transfers between devices  29.6 us (21%)
  waiting for transfers between devices  21.5 us (16%)
  other arithmetic  4.39 us (3%)
  local copies, waits for them, and re-layouts  3.81 us (3%)
    pallas_call x1, Pallas kernels, local(): pl.pallas_call(final_kernel, grid=(width // each,), in_specs=[pl.BlockSpe...  32.4 us
    pallas_call x1, Pallas kernels, local(): pl.pallas_call(states_kernel, grid=(width // each,), in_specs=[pl.BlockSp...  22.4 us
    pallas_call x3, Pallas kernels, call(): pl.pallas_call(blocks_kernel, grid=(last - first,), in_specs=[pairs, stat...  22.2 us
    ppermute x5, starting transfers between devices, swapped(): return lax.ppermute(value, 'ctx', [(s, s ^ 1) for s in range(count)])  10 us
    ppermute x6, starting transfers between devices, rotated(): lax.ppermute(value, axis, [(s, (s + steps) % count) for s in range(count)])  8.99 us
    ppermute x3, starting transfers between devices, paired(): lax.ppermute(value, axis, [(source, source ^ step) for source in lines or...  7.82 us
    ppermute x6, waiting for transfers between devices, rotated(): lax.ppermute(value, axis, [(s, (s + steps) % count) for s in range(count)])  7.01 us
    ppermute x5, waiting for transfers between devices, swapped(): return lax.ppermute(value, 'ctx', [(s, s ^ 1) for s in range(count)])  6.92 us
  transfers between devices with their start and end apart: 17, of which 13 were waited for; matrix products, arithmetic and copies ran while one was open for 2% of the time, Pallas kernels for 16%

profile of v11, /device:TPU:0, one launch (start us, length us, event | category | flops | bytes accessed | tf_op | source)
XLA Modules:
  0.0 137.3 jit_solution(48042010952620996)
XLA Ops:
  0.6 0.0 copy-start.11
  0.6 0.0 copy-start
  0.7 1.1 constant_dynamic-slice_fusion.3
  1.8 1.2 dynamic-slice_bitcast_fusion
  3.1 0.7 collective-permute-start
  3.8 4.4 %collective-permute-start.1 = (bf16[4,8,8192]{2,1,0:T(8,128)(2,1)S(1)}, bf16[4,8,8192]{2,1,0:T(8,128)(2,1)S(1)}, u32[]{:S(2)}, u32[]{:S(2)}) collective-permute-start(bf16[4,8,8192]{2,1,0:T(8,128)(2,1)S(1)} %pad_maximum_fusion.1), channel_id=1, source_target_pairs={{0,1},{1,0},{2,3},{3,2},{4,5},{5,4},{6,7},{7,6},{8,9},{9,8},{10,11... | collective-permute-start | bytes 1572872 | tf_op jit(solution)/shard_map/ppermute | solution.py:254
  8.3 0.2 multiply_exponential_fusion
  8.5 0.0 copy-start.5
  8.6 1.2 collective-permute-done.1.hi
  9.8 0.0 copy-start.12
  9.8 0.0 copy-start.15
  9.8 22.4 %states.1 = (f32[16,3,136,512]{3,2,1,0:T(8,128)}, f32[16,2,136,512]{3,2,1,0:T(8,128)}, f32[16,16,8,512]{3,2,1,0:T(8,128)}, f32[16,16,8,512]{3,2,1,0:T(8,128)}, f32[2,16,16,512]{3,2,1,0:T(8,128)}) custom-call(s32[1]{0:T(128)} %bitcast.core, bf16[3,128,8192]{2,1,0:T(8,128)(2,1)} %bitcast.91, bf16[4,8,8192]{2,1,0:T(8,128)(2,1)S(1)} %collective-permute-done.hx, ...), custom_call_target="tpu_custom_call" | custom-call | tf_op jit(solution)/shard_map/states/pallas_call | solution.py:399
  32.2 0.0 copy-start.14
  32.2 5.3 %collective-permute-start.2 = (f32[2,16,16,512]{3,2,1,0:T(8,128)}, f32[2,16,16,512]{3,2,1,0:T(8,128)S(1)}, u32[]{:S(2)}, u32[]{:S(2)}) collective-permute-start(f32[2,16,16,512]{3,2,1,0:T(8,128)} %get-tuple-element.43), channel_id=1, source_target_pairs={{0,1},{1,0},{2,3},{3,2},{4,5},{5,4},{6,7},{7,6},{8,9},{9,8},{10,11... | collective-permute-start | bytes 3145736 | tf_op jit(solution)/shard_map/ppermute | solution.py:254
  37.5 0.1 multiply_exponential_fusion.1
  37.6 0.8 slice_multiply_fusion
  38.4 1.0 multiply_reduce_fusion.near
  39.4 0.6 collective-permute-done.2.other
  40.0 1.2 dynamic-slice_select_fusion.1
  41.2 0.1 broadcast_select_fusion.4
  41.3 2.1 %collective-permute-start.3 = (f32[8,16,512]{2,1,0:T(8,128)S(1)}, f32[8,16,512]{2,1,0:T(8,128)S(1)}, u32[]{:S(2)}, u32[]{:S(2)}) collective-permute-start(f32[8,16,512]{2,1,0:T(8,128)S(1)} %broadcast_select_fusion.4), channel_id=1, source_target_pairs={{0,2},{1,3},{2,0},{3,1},{4,6},{5,7},{6,4},{7,5},{8,10},{9,11},{10,... | collective-permute-start | bytes 786440 | tf_op jit(solution)/shard_map/ppermute | solution.py:270
  43.3 0.3 broadcast_select_fusion
  43.7 8.2 %blocks.3 = (f32[16,2,136,512]{3,2,1,0:T(8,128)}, f32[16,16,8,512]{3,2,1,0:T(8,128)}, f32[16,16,8,512]{3,2,1,0:T(8,128)}, f32[6,8,512]{2,1,0:T(8,128)S(1)}) custom-call(f32[16,2,136,512]{3,2,1,0:T(8,128)} %get-tuple-element.44.xg, f32[16,16,8,512]{3,2,1,0:T(8,128)} %get-tuple-element.45.blocks_e, ...), custom_call_target="tpu_custom_call", output_to_operand_aliasing={{0}: (0, {}), {1}: (1, {}), {2}: (2, {})} | custom-call | flops 62914560 | bytes 36700160 | tf_op jit(solution)/shard_map/blocks/pallas_call | solution.py:429
  51.9 0.1 multiply_add_fusion.1
  52.0 0.7 collective-permute-start.4
  52.7 5.8 %blocks.4 = (f32[16,2,136,512]{3,2,1,0:T(8,128)}, f32[16,16,8,512]{3,2,1,0:T(8,128)}, f32[16,16,8,512]{3,2,1,0:T(8,128)}, f32[4,8,512]{2,1,0:T(8,128)S(1)}) custom-call(f32[16,2,136,512]{3,2,1,0:T(8,128)} %get-tuple-element.53.xg, f32[16,16,8,512]{3,2,1,0:T(8,128)} %get-tuple-element.54.blocks_e, ...), custom_call_target="tpu_custom_call", output_to_operand_aliasing={{0}: (0, {}), {1}: (1, {}), {2}: (2, {})} | custom-call | flops 62914560 | bytes 36700160 | tf_op jit(solution)/shard_map/blocks/pallas_call | solution.py:429
  58.6 0.0 copy-start.8
  58.6 1.4 %collective-permute-start.5 = (f32[8,16,512]{2,1,0:T(8,128)S(1)}, f32[8,16,512]{2,1,0:T(8,128)S(1)}, u32[]{:S(2)}, u32[]{:S(2)}) collective-permute-start(f32[8,16,512]{2,1,0:T(8,128)S(1)} %collective-permute-done.4), channel_id=1, source_target_pairs={{4,6},{5,7},{2,0},{3,1},{12,14},{13,15},{10,8},{11,9},{20,22},{21,... | collective-permute-start | bytes 786440 | tf_op jit(solution)/shard_map/ppermute | solution.py:286
  60.0 8.1 %blocks.5 = (f32[16,2,136,512]{3,2,1,0:T(8,128)}, f32[16,16,8,512]{3,2,1,0:T(8,128)}, f32[16,16,8,512]{3,2,1,0:T(8,128)}, f32[6,8,512]{2,1,0:T(8,128)S(1)}) custom-call(f32[16,2,136,512]{3,2,1,0:T(8,128)} %get-tuple-element.63.xg, f32[16,16,8,512]{3,2,1,0:T(8,128)} %get-tuple-element.64.blocks_e, ...), custom_call_target="tpu_custom_call", output_to_operand_aliasing={{0}: (0, {}), {1}: (1, {}), {2}: (2, {})} | custom-call | flops 62914560 | bytes 36700160 | tf_op jit(solution)/shard_map/blocks/pallas_call | solution.py:429
  68.2 2.4 %collective-permute-done.5 = f32[8,16,512]{2,1,0:T(8,128)S(1)} collective-permute-done((f32[8,16,512]{2,1,0:T(8,128)S(1)}, f32[8,16,512]{2,1,0:T(8,128)S(1)}, u32[]{:S(2)}, u32[]{:S(2)}) %collective-permute-start.5) | collective-permute-done | bytes 262176 | tf_op jit(solution)/shard_map/ppermute | solution.py:286
  70.6 0.1 select_bitcast_fusion.1
  70.7 0.1 collective-permute-start.6
  70.8 0.1 fusion
  70.9 1.8 %collective-permute-done.6.found = f32[2,8,16,512]{3,2,1,0:T(8,128)S(1)} collective-permute-done((f32[2,8,16,512]{3,2,1,0:T(8,128)S(1)}, f32[2,8,16,512]{3,2,1,0:T(8,128)S(1)}, u32[]{:S(2)}, u32[]{:S(2)}) %collective-permute-start.6) | collective-permute-done | bytes 524320 | tf_op jit(solution)/shard_map/ppermute | solution.py:254
  72.7 32.4 %final.1 = (bf16[128,8192]{1,0:T(8,128)(2,1)}, bf16[3,128,8192]{2,1,0:T(8,128)(2,1)}, f32[32,24,256]{2,1,0:T(8,128)S(1)}) custom-call(s32[1]{0:T(128)} %bitcast.core, bf16[3,128,8192]{2,1,0:T(8,128)(2,1)} %bitcast.92, bf16[4,8,8192]{2,1,0:T(8,128)(2,1)S(1)} %collective-permute-done.hx, bf16[4,8,8192]{2,1,0:T(8,128)(2,1)S(1)} %copy-done.3, ...), custom_call_target="tpu_custom_call" | custom-call | tf_op jit(solution)/shard_map/final/pallas_call | solution.py:471
  105.1 0.1 slice_select_fusion
  105.1 0.2 collective-permute-start.7
  105.3 1.6 %collective-permute-done.7 = f32[16,24,256]{2,1,0:T(8,128)S(1)} collective-permute-done((f32[16,24,256]{2,1,0:T(8,128)S(1)}, f32[16,24,256]{2,1,0:T(8,128)S(1)}, u32[]{:S(2)}, u32[]{:S(2)}) %collective-permute-start.7) | collective-permute-done | bytes 393248 | tf_op jit(solution)/shard_map/ppermute | solution.py:254
  106.9 0.1 select_add_fusion
  107.0 1.5 %collective-permute-start.8 = (f32[4,24,256]{2,1,0:T(8,128)S(1)}, f32[4,24,256]{2,1,0:T(8,128)S(1)}, u32[]{:S(2)}, u32[]{:S(2)}) collective-permute-start(f32[4,24,256]{2,1,0:T(8,128)S(1)} %get-tuple-element.96), channel_id=1, source_target_pairs={{0,8},{8,16},{16,24},{24,0},{1,9},{9,17},{17,25},{25,1},{2,10},{10... | collective-permute-start | bytes 294920 | tf_op jit(solution)/shard_map/ppermute | solution.py:306
  108.6 1.4 %collective-permute-start.10 = (f32[4,24,256]{2,1,0:T(8,128)S(1)}, f32[4,24,256]{2,1,0:T(8,128)S(1)}, u32[]{:S(2)}, u32[]{:S(2)}) collective-permute-start(f32[4,24,256]{2,1,0:T(8,128)S(1)} %get-tuple-element.97), channel_id=1, source_target_pairs={{0,24},{8,0},{16,8},{24,16},{1,25},{9,1},{17,9},{25,17},{2,26},{10... | collective-permute-start | bytes 294920 | tf_op jit(solution)/shard_map/ppermute | solution.py:306
  110.0 1.5 %collective-permute-start.9 = (f32[4,24,256]{2,1,0:T(8,128)S(1)}, f32[4,24,256]{2,1,0:T(8,128)S(1)}, u32[]{:S(2)}, u32[]{:S(2)}) collective-permute-start(f32[4,24,256]{2,1,0:T(8,128)S(1)} %get-tuple-element.98), channel_id=1, source_target_pairs={{0,16},{8,24},{16,0},{24,8},{1,17},{9,25},{17,1},{25,9},{2,18},{10... | collective-permute-start | bytes 294920 | tf_op jit(solution)/shard_map/ppermute | solution.py:306
  111.5 2.1 %collective-permute-done.8 = f32[4,24,256]{2,1,0:T(8,128)S(1)} collective-permute-done((f32[4,24,256]{2,1,0:T(8,128)S(1)}, f32[4,24,256]{2,1,0:T(8,128)S(1)}, u32[]{:S(2)}, u32[]{:S(2)}) %collective-permute-start.8) | collective-permute-done | bytes 98336 | tf_op jit(solution)/shard_map/ppermute | solution.py:306
  113.6 1.4 collective-permute-done.10
  115.0 0.0 collective-permute-done.9
  115.0 2.5 %collective-permute-start.11 = (f32[4,24,256]{2,1,0:T(8,128)S(1)}, f32[4,24,256]{2,1,0:T(8,128)S(1)}, u32[]{:S(2)}, u32[]{:S(2)}) collective-permute-start(f32[4,24,256]{2,1,0:T(8,128)S(1)} %add_add_fusion), channel_id=1, source_target_pairs={{0,2},{1,3},{2,0},{3,1},{4,6},{5,7},{6,4},{7,5},{8,10},{9,11},{10,... | collective-permute-start | bytes 294920 | tf_op jit(solution)/shard_map/ppermute | solution.py:270
  117.5 2.6 %collective-permute-done.11 = f32[4,24,256]{2,1,0:T(8,128)S(1)} collective-permute-done((f32[4,24,256]{2,1,0:T(8,128)S(1)}, f32[4,24,256]{2,1,0:T(8,128)S(1)}, u32[]{:S(2)}, u32[]{:S(2)}) %collective-permute-start.11) | collective-permute-done | bytes 98336 | tf_op jit(solution)/shard_map/ppermute | solution.py:270
  120.1 3.3 %collective-permute-start.12 = (f32[4,24,256]{2,1,0:T(8,128)S(1)}, f32[4,24,256]{2,1,0:T(8,128)S(1)}, u32[]{:S(2)}, u32[]{:S(2)}) collective-permute-start(f32[4,24,256]{2,1,0:T(8,128)S(1)} %add.97), channel_id=1, source_target_pairs={{0,4},{1,5},{2,6},{3,7},{4,0},{5,1},{6,2},{7,3},{8,12},{9,13},{10,... | collective-permute-start | bytes 294920 | tf_op jit(solution)/shard_map/ppermute | solution.py:270
  123.4 2.6 %collective-permute-done.12 = f32[4,24,256]{2,1,0:T(8,128)S(1)} collective-permute-done((f32[4,24,256]{2,1,0:T(8,128)S(1)}, f32[4,24,256]{2,1,0:T(8,128)S(1)}, u32[]{:S(2)}, u32[]{:S(2)}) %collective-permute-start.12) | collective-permute-done | bytes 98336 | tf_op jit(solution)/shard_map/ppermute | solution.py:270
  126.0 2.1 %collective-permute-start.13 = (f32[4,24,256]{2,1,0:T(8,128)S(1)}, f32[4,24,256]{2,1,0:T(8,128)S(1)}, u32[]{:S(2)}, u32[]{:S(2)}) collective-permute-start(f32[4,24,256]{2,1,0:T(8,128)S(1)} %get-tuple-element.81), channel_id=1, source_target_pairs={{0,8},{8,16},{16,24},{24,0},{1,9},{9,17},{17,25},{25,1},{2,10},{10... | collective-permute-start | bytes 294920 | tf_op jit(solution)/shard_map/ppermute | solution.py:306
  128.1 1.4 collective-permute-start.14
  129.5 1.1 collective-permute-start.15
  130.5 1.2 collective-permute-done.13
  131.8 1.0 collective-permute-done.14
  132.8 1.3 collective-permute-done.15
  134.1 0.1 collective-permute-start.16
  134.2 1.7 %collective-permute-done.16 = f32[16,24,256]{2,1,0:T(8,128)S(1)} collective-permute-done((f32[16,24,256]{2,1,0:T(8,128)S(1)}, f32[16,24,256]{2,1,0:T(8,128)S(1)}, u32[]{:S(2)}, u32[]{:S(2)}) %collective-permute-start.16) | collective-permute-done | bytes 393248 | tf_op jit(solution)/shard_map/ppermute | solution.py:254
  135.9 0.1 broadcast_select_fusion.3
  136.0 0.1 maximum_bitcast_fusion
  136.0 0.3 copy.25
  136.3 0.1 reshape.33
  136.4 0.0 copy-start.7
  136.5 0.7 slice.67
  137.2 0.2 copy-done.7
  (44 shorter events, 0.5 us)
Async XLA Ops:
  0.6 7.7 %copy-start.11 = (f32[4,8]{1,0:T(4,128)S(1)}, f32[4,8]{1,0:T(4,128)}, u32[]{:S(2)}) copy-start(f32[4,8]{1,0:T(4,128)} %constant.88) | copy-start | bytes 388
  0.6 9.2 %copy-start = (bf16[1,128,8192]{2,1,0:T(8,128)(2,1)S(1)}, bf16[1,128,8192]{2,1,0:T(8,128)(2,1)}, u32[]{:S(2)}) copy-start(bf16[1,128,8192]{2,1,0:T(8,128)(2,1)} %param.16) | copy-start | bytes 6291460
  0.7 7.6 %copy-start.9 = (f32[512,16]{0,1:T(8,128)S(1)}, f32[512,16]{0,1:T(8,128)}, u32[]{:S(2)}) copy-start(f32[512,16]{0,1:T(8,128)} %param.14) | copy-start | bytes 98308
  0.7 9.1 %copy-start.1 = (f32[3,7,8192]{2,1,0:T(8,128)S(1)}, f32[3,7,8192]{2,1,0:T(8,128)}, u32[]{:S(2)}) copy-start(f32[3,7,8192]{2,1,0:T(8,128)} %filt.3) | copy-start | bytes 2064388
  0.7 7.6 %copy-start.10 = (f32[512,16]{0,1:T(8,128)S(1)}, f32[512,16]{0,1:T(8,128)}, u32[]{:S(2)}) copy-start(f32[512,16]{0,1:T(8,128)} %param.14) | copy-start | bytes 98308
  3.1 5.5 %collective-permute-start = (bf16[4,8,8192]{2,1,0:T(8,128)(2,1)S(1)}, bf16[4,8,8192]{2,1,0:T(8,128)(2,1)S(1)}, u32[]{:S(2)}, u32[]{:S(2)}) collective-permute-start(bf16[4,8,8192]{2,1,0:T(8,128)(2,1)S(1)} %pad_maximum_fusion), channel_id=1, source_target_pairs={{1,2},{3,4},{5,6},{2,1},{4,3},{6,5},{9,10},{11,12},{13,14},{10,9},... | collective-permute-start | bytes 1572872 | tf_op jit(solution)/shard_map/ppermute | solution.py:353
  3.8 6.0 %collective-permute-start.1 = (bf16[4,8,8192]{2,1,0:T(8,128)(2,1)S(1)}, bf16[4,8,8192]{2,1,0:T(8,128)(2,1)S(1)}, u32[]{:S(2)}, u32[]{:S(2)}) collective-permute-start(bf16[4,8,8192]{2,1,0:T(8,128)(2,1)S(1)} %pad_maximum_fusion.1), channel_id=1, source_target_pairs={{0,1},{1,0},{2,3},{3,2},{4,5},{5,4},{6,7},{7,6},{8,9},{9,8},{10,11... | collective-permute-start | bytes 1572872 | tf_op jit(solution)/shard_map/ppermute | solution.py:254
  8.5 1.3 copy-start.5
  9.8 22.4 %copy-start.2 = (bf16[4,8,8192]{2,1,0:T(8,128)(2,1)}, bf16[4,8,8192]{2,1,0:T(8,128)(2,1)S(1)}, u32[]{:S(2)}) copy-start(bf16[4,8,8192]{2,1,0:T(8,128)(2,1)S(1)} %collective-permute-done.1.hi) | copy-start | bytes 1572868
  9.8 27.7 %copy-start.12 = (f32[4]{0:T(128)S(1)}, f32[4]{0:T(128)}, u32[]{:S(2)}) copy-start(f32[4]{0:T(128)} %constant.91) | copy-start | bytes 52
  9.8 28.6 %copy-start.15 = (f32[24]{0:T(128)S(1)}, f32[24]{0:T(128)}, u32[]{:S(2)}) copy-start(f32[24]{0:T(128)} %constant.89) | copy-start | bytes 292
  32.2 11.1 %copy-start.13 = (pred[4,8]{1,0:T(4,128)(4,1)S(1)}, pred[4,8]{1,0:T(4,128)(4,1)}, u32[]{:S(2)}) copy-start(pred[4,8]{1,0:T(4,128)(4,1)} %constant.92) | copy-start | bytes 100
  32.2 11.1 %copy-start.14 = (pred[4,8]{1,0:T(4,128)(4,1)S(1)}, pred[4,8]{1,0:T(4,128)(4,1)}, u32[]{:S(2)}) copy-start(pred[4,8]{1,0:T(4,128)(4,1)} %constant.90) | copy-start | bytes 100
  32.2 11.5 %copy-start.4 = (f32[8192]{0:T(1024)S(1)}, f32[8192]{0:T(1024)}, u32[]{:S(2)}) copy-start(f32[8192]{0:T(1024)} %param.15) | copy-start | bytes 98308
  32.2 7.8 %collective-permute-start.2 = (f32[2,16,16,512]{3,2,1,0:T(8,128)}, f32[2,16,16,512]{3,2,1,0:T(8,128)S(1)}, u32[]{:S(2)}, u32[]{:S(2)}) collective-permute-start(f32[2,16,16,512]{3,2,1,0:T(8,128)} %get-tuple-element.43), channel_id=1, source_target_pairs={{0,1},{1,0},{2,3},{3,2},{4,5},{5,4},{6,7},{7,6},{8,9},{9,8},{10,11... | collective-permute-start | bytes 3145736 | tf_op jit(solution)/shard_map/ppermute | solution.py:254
  41.3 10.6 %collective-permute-start.3 = (f32[8,16,512]{2,1,0:T(8,128)S(1)}, f32[8,16,512]{2,1,0:T(8,128)S(1)}, u32[]{:S(2)}, u32[]{:S(2)}) collective-permute-start(f32[8,16,512]{2,1,0:T(8,128)S(1)} %broadcast_select_fusion.4), channel_id=1, source_target_pairs={{0,2},{1,3},{2,0},{3,1},{4,6},{5,7},{6,4},{7,5},{8,10},{9,11},{10,... | collective-permute-start | bytes 786440 | tf_op jit(solution)/shard_map/ppermute | solution.py:270
  52.0 6.5 %collective-permute-start.4 = (f32[8,16,512]{2,1,0:T(8,128)S(1)}, f32[8,16,512]{2,1,0:T(8,128)S(1)}, u32[]{:S(2)}, u32[]{:S(2)}) collective-permute-start(f32[8,16,512]{2,1,0:T(8,128)S(1)} %multiply_add_fusion.1), channel_id=1, source_target_pairs={{2,4},{3,5},{4,2},{5,3},{10,12},{11,13},{12,10},{13,11},{18,20},{1... | collective-permute-start | bytes 786440 | tf_op jit(solution)/shard_map/ppermute | solution.py:283
  58.5 12.2 %copy-start.6 = (f32[4,16,8,512]{3,2,1,0:T(8,128)S(1)}, f32[4,16,8,512]{3,2,1,0:T(8,128)}, u32[]{:S(2)}) copy-start(f32[4,16,8,512]{3,2,1,0:T(8,128)} %copy-done.5) | copy-start | bytes 3145732
  58.6 12.2 %copy-start.8 = (f32[512,16]{0,1:T(8,128)S(1)}, f32[512,16]{0,1:T(8,128)}, u32[]{:S(2)}) copy-start(f32[512,16]{0,1:T(8,128)} %param.13) | copy-start | bytes 98308
  58.6 12.0 %collective-permute-start.5 = (f32[8,16,512]{2,1,0:T(8,128)S(1)}, f32[8,16,512]{2,1,0:T(8,128)S(1)}, u32[]{:S(2)}, u32[]{:S(2)}) collective-permute-start(f32[8,16,512]{2,1,0:T(8,128)S(1)} %collective-permute-done.4), channel_id=1, source_target_pairs={{4,6},{5,7},{2,0},{3,1},{12,14},{13,15},{10,8},{11,9},{20,22},{21,... | collective-permute-start | bytes 786440 | tf_op jit(solution)/shard_map/ppermute | solution.py:286
  68.2 4.5 %copy-start.3 = (bf16[4,8,8192]{2,1,0:T(8,128)(2,1)S(1)}, bf16[4,8,8192]{2,1,0:T(8,128)(2,1)}, u32[]{:S(2)}) copy-start(bf16[4,8,8192]{2,1,0:T(8,128)(2,1)} %copy-done.2) | copy-start | bytes 1572868
  70.7 2.0 %collective-permute-start.6 = (f32[2,8,16,512]{3,2,1,0:T(8,128)S(1)}, f32[2,8,16,512]{3,2,1,0:T(8,128)S(1)}, u32[]{:S(2)}, u32[]{:S(2)}) collective-permute-start(f32[2,8,16,512]{3,2,1,0:T(8,128)S(1)} %pad_maximum_fusion.2.both), channel_id=1, source_target_pairs={{0,1},{1,0},{2,3},{3,2},{4,5},{5,4},{6,7},{7,6},{8,9},{9,8},{10,11... | collective-permute-start | bytes 1572872 | tf_op jit(solution)/shard_map/ppermute | solution.py:254
  105.1 1.8 %collective-permute-start.7 = (f32[16,24,256]{2,1,0:T(8,128)S(1)}, f32[16,24,256]{2,1,0:T(8,128)S(1)}, u32[]{:S(2)}, u32[]{:S(2)}) collective-permute-start(f32[16,24,256]{2,1,0:T(8,128)S(1)} %slice_select_fusion), channel_id=1, source_target_pairs={{0,1},{1,0},{2,3},{3,2},{4,5},{5,4},{6,7},{7,6},{8,9},{9,8},{10,11... | collective-permute-start | bytes 1179656 | tf_op jit(solution)/shard_map/ppermute | solution.py:254
  107.0 6.6 %collective-permute-start.8 = (f32[4,24,256]{2,1,0:T(8,128)S(1)}, f32[4,24,256]{2,1,0:T(8,128)S(1)}, u32[]{:S(2)}, u32[]{:S(2)}) collective-permute-start(f32[4,24,256]{2,1,0:T(8,128)S(1)} %get-tuple-element.96), channel_id=1, source_target_pairs={{0,8},{8,16},{16,24},{24,0},{1,9},{9,17},{17,25},{25,1},{2,10},{10... | collective-permute-start | bytes 294920 | tf_op jit(solution)/shard_map/ppermute | solution.py:306
  108.6 6.4 %collective-permute-start.10 = (f32[4,24,256]{2,1,0:T(8,128)S(1)}, f32[4,24,256]{2,1,0:T(8,128)S(1)}, u32[]{:S(2)}, u32[]{:S(2)}) collective-permute-start(f32[4,24,256]{2,1,0:T(8,128)S(1)} %get-tuple-element.97), channel_id=1, source_target_pairs={{0,24},{8,0},{16,8},{24,16},{1,25},{9,1},{17,9},{25,17},{2,26},{10... | collective-permute-start | bytes 294920 | tf_op jit(solution)/shard_map/ppermute | solution.py:306
  110.0 5.0 %collective-permute-start.9 = (f32[4,24,256]{2,1,0:T(8,128)S(1)}, f32[4,24,256]{2,1,0:T(8,128)S(1)}, u32[]{:S(2)}, u32[]{:S(2)}) collective-permute-start(f32[4,24,256]{2,1,0:T(8,128)S(1)} %get-tuple-element.98), channel_id=1, source_target_pairs={{0,16},{8,24},{16,0},{24,8},{1,17},{9,25},{17,1},{25,9},{2,18},{10... | collective-permute-start | bytes 294920 | tf_op jit(solution)/shard_map/ppermute | solution.py:306
  115.0 5.1 %collective-permute-start.11 = (f32[4,24,256]{2,1,0:T(8,128)S(1)}, f32[4,24,256]{2,1,0:T(8,128)S(1)}, u32[]{:S(2)}, u32[]{:S(2)}) collective-permute-start(f32[4,24,256]{2,1,0:T(8,128)S(1)} %add_add_fusion), channel_id=1, source_target_pairs={{0,2},{1,3},{2,0},{3,1},{4,6},{5,7},{6,4},{7,5},{8,10},{9,11},{10,... | collective-permute-start | bytes 294920 | tf_op jit(solution)/shard_map/ppermute | solution.py:270
  120.1 5.9 %collective-permute-start.12 = (f32[4,24,256]{2,1,0:T(8,128)S(1)}, f32[4,24,256]{2,1,0:T(8,128)S(1)}, u32[]{:S(2)}, u32[]{:S(2)}) collective-permute-start(f32[4,24,256]{2,1,0:T(8,128)S(1)} %add.97), channel_id=1, source_target_pairs={{0,4},{1,5},{2,6},{3,7},{4,0},{5,1},{6,2},{7,3},{8,12},{9,13},{10,... | collective-permute-start | bytes 294920 | tf_op jit(solution)/shard_map/ppermute | solution.py:270
  126.0 5.7 %collective-permute-start.13 = (f32[4,24,256]{2,1,0:T(8,128)S(1)}, f32[4,24,256]{2,1,0:T(8,128)S(1)}, u32[]{:S(2)}, u32[]{:S(2)}) collective-permute-start(f32[4,24,256]{2,1,0:T(8,128)S(1)} %get-tuple-element.81), channel_id=1, source_target_pairs={{0,8},{8,16},{16,24},{24,0},{1,9},{9,17},{17,25},{25,1},{2,10},{10... | collective-permute-start | bytes 294920 | tf_op jit(solution)/shard_map/ppermute | solution.py:306
  128.1 4.7 %collective-permute-start.14 = (f32[4,24,256]{2,1,0:T(8,128)S(1)}, f32[4,24,256]{2,1,0:T(8,128)S(1)}, u32[]{:S(2)}, u32[]{:S(2)}) collective-permute-start(f32[4,24,256]{2,1,0:T(8,128)S(1)} %get-tuple-element.81), channel_id=1, source_target_pairs={{0,16},{8,24},{16,0},{24,8},{1,17},{9,25},{17,1},{25,9},{2,18},{10... | collective-permute-start | bytes 294920 | tf_op jit(solution)/shard_map/ppermute | solution.py:306
  129.5 4.6 %collective-permute-start.15 = (f32[4,24,256]{2,1,0:T(8,128)S(1)}, f32[4,24,256]{2,1,0:T(8,128)S(1)}, u32[]{:S(2)}, u32[]{:S(2)}) collective-permute-start(f32[4,24,256]{2,1,0:T(8,128)S(1)} %get-tuple-element.81), channel_id=1, source_target_pairs={{0,24},{8,0},{16,8},{24,16},{1,25},{9,1},{17,9},{25,17},{2,26},{10... | collective-permute-start | bytes 294920 | tf_op jit(solution)/shard_map/ppermute | solution.py:306
  134.1 1.8 %collective-permute-start.16 = (f32[16,24,256]{2,1,0:T(8,128)S(1)}, f32[16,24,256]{2,1,0:T(8,128)S(1)}, u32[]{:S(2)}, u32[]{:S(2)}) collective-permute-start(f32[16,24,256]{2,1,0:T(8,128)S(1)} %constant_dynamic-update-slice_fusion), channel_id=1, source_target_pairs={{0,1},{1,0},{2,3},{3,2},{4,5},{5,4},{6,7},{7,6},{8,9},{9,8},{10,11... | collective-permute-start | bytes 1179656 | tf_op jit(solution)/shard_map/ppermute | solution.py:254
  136.4 0.9 copy-start.7

commit v12 on v11

--- a/solution.py
+++ b/solution.py
@@ -66,8 +66,7 @@
             xs[j, SUB : SUB + rows] = p[j, :, lanes].astype(F32)
             xs[j, SUB + rows :] = jnp.where(first, within, across)
         xs[3, SUB : SUB + rows] = u[:, lanes].astype(F32)
-        across, within = hx[3, :, lanes].astype(F32), hi[3, :, lanes].astype(F32)
-        xs[3, SUB + rows :] = jnp.where(first, within, across)
+        xs[3, SUB + rows :] = jnp.ones((SUB, LANES), F32)
 
         def mixed(j):
             tap = [spread(filt[j, i : i + 1, lanes]) for i in range(taps)]
@@ -106,7 +105,7 @@
 
 
 def blocks_kernel(
-    xg, blocks_e, blocks_a, near, skip, join_e, join_a, conv, from_e, from_a, skip_sum
+    xg, blocks_e, blocks_a, hu, near, skip, join_e, join_a, conv, from_e, from_a, skip_sum, es
 ):
     run = xg.shape[2] // SUB
     rows = xg.shape[2] - SUB
@@ -130,6 +129,9 @@
             )
         gated = x
         x = [xg[which, 1, SUB * a : SUB * a + SUB, part] for a in range(run)]
+        es[...] = hu[:, lanes].astype(F32)
+        for a in range(own, run):
+            x[a] = x[a] * jnp.where(inside, 1.0, spread(es[a - own : a - own + 1]))
         masked = [x[a] if a < own else jnp.where(inside, x[a], 0.0) for a in range(run)]
         skip_sum[which, :, part] = added([masked[a] * gated[a] for a in range(run)])
         past = [jnp.where(inside, 0.0, gain)] + [
@@ -156,7 +158,7 @@
 
 
 def final_kernel(
-    core, p, hx, hi, u, qkv, conv, from_e, from_a, skip_sum, both, found, other, filt, f1, f_all, cz, cy,
+    core, p, hx, hi, hu, u, qkv, conv, from_e, from_a, skip_sum, both, found, other, filt, f1, f_all, cz, cy,
     output, grad_p, sums, ps, us, gs, os, es,
 ):
     rows = p.shape[1]
@@ -187,8 +189,7 @@
             ps[j, SUB : SUB + rows] = p[j, :, lanes].astype(F32)
             ps[j, SUB + rows :] = jnp.where(first, within, across)
         us[0:rows] = u[:, lanes].astype(F32)
-        across, within = hx[3, :, lanes].astype(F32), hi[3, :, lanes].astype(F32)
-        us[rows:] = jnp.where(first, within, across)
+        us[rows:] = hu[:, lanes].astype(F32)
         decay = [spread(f1[n : n + 1, part]) for n in range(poles)]
 
         state = [
@@ -343,15 +344,14 @@
     core = lax.rem(lax.axis_index("ctx"), 2)
 
     def edge(last):
-        start = jnp.where(last, rows - SUB, 0)
-        cut = lambda value, axis: lax.dynamic_slice_in_dim(value, start, SUB, axis)
-        return jnp.concatenate([cut(p, 1), cut(u, 0)[None]], axis=0)
+        return lax.dynamic_slice_in_dim(p, jnp.where(last, rows - SUB, 0), SUB, 1)
 
     devices = lax.axis_size("ctx")
     across = [(k, k + 1) for k in range(1, devices - 1, 2)]
     across = across + [(target, source) for source, target in across]
     hx = lax.ppermute(edge(core == 1), "ctx", across)
     hi = swapped(edge(core == 0))
+    hu = shifted(u[:SUB], "ctx", -1)
 
     rate = decay_rates.T
     weight = residues.T
@@ -401,7 +401,7 @@
         grid=(width // each,),
         in_specs=[
             pl.BlockSpec(memory_space=pltpu.SMEM),
-            by_w(3, rows), by_w(4, SUB), by_w(4, SUB), by_w(rows), by_w(3, taps),
+            by_w(3, rows), by_w(3, SUB), by_w(3, SUB), by_w(rows), by_w(3, taps),
             fixed(f1), fixed(we), fixed(wb),
         ],
         out_specs=[
@@ -430,7 +430,8 @@
                 blocks_kernel,
                 grid=(last - first,),
                 in_specs=[
-                    pairs, states, states, fixed(near),
+                    pairs, states, states,
+                    pl.BlockSpec((SUB, many * groups), lambda w: (0, w + first)), fixed(near),
                     pl.BlockSpec((1, many * groups), lambda w: (0, w + first)),
                     fixed(join_e), fixed(join_a),
                 ],
@@ -440,12 +441,13 @@
                     shape_of(((last - first) * many, SUB, groups), F32),
                 ],
                 input_output_aliases={0: 0, 1: 1, 2: 2},
+                scratch_shapes=[pltpu.VMEM((SUB, LANES), F32)],
                 compiler_params=params,
                 cost_estimate=pl.CostEstimate(
                     flops=60 * rows * channels, bytes_accessed=35 * 2**20, transcendentals=0
                 ),
                 name="blocks",
-            )(*held_before[:3], close, skip_gain[None], join_e, join_a)
+            )(*held_before[:3], hu, close, skip_gain[None], join_e, join_a)
             return [*out[:3], jnp.concatenate([*held_before[3:], out[3]], axis=0)]
 
         return call
@@ -473,7 +475,7 @@
         grid=(width // each,),
         in_specs=[
             pl.BlockSpec(memory_space=pltpu.SMEM),
-            by_w(3, rows), by_w(4, SUB), by_w(4, SUB), by_w(rows),
+            by_w(3, rows), by_w(3, SUB), by_w(3, SUB), by_w(SUB), by_w(rows),
             by_block(3, held, groups), by_block(2, held, groups), state_spec, state_spec,
             by_block(SUB, groups), halved, halved, ends_spec,
             by_w(3, taps), fixed(f1), fixed(f_all), fixed(cz), fixed(cy),
@@ -491,7 +493,7 @@
         compiler_params=params,
         name="final",
     )(
-        core[None], p, hx, hi, u, qkv, conv, from_e, from_a, skip_sum, both, found, other, short_filter,
+        core[None], p, hx, hi, hu, u, qkv, conv, from_e, from_a, skip_sum, both, found, other, short_filter,
         f1, f_all, cz, cy,
     )
 

time: 138 us -> 138 us (level)
  other arithmetic: 4.39 us -> 7.28 us
  waiting for transfers between devices: 21.5 us -> 19.4 us
    ppermute x5, starting transfers between devices: 10 us -> 7.14 us  [swapped(): return lax.ppermute(value, 'ctx', [(s, s ^ 1) for s in range(count)])]
    ppermute x5, waiting for transfers between devices: 6.92 us -> 5.12 us  [swapped(): return lax.ppermute(value, 'ctx', [(s, s ^ 1) for s in range(count)])]
    mul x1, other arithmetic: 0.02 us -> 1.42 us  [scanned(): f_chip = f_all * f_all]
  transfers between devices with their start and end apart: 17 -> 18, of which waited for: 13 -> 11; matrix products, arithmetic and copies ran while one was open for 2% -> 5% of each run, Pallas kernels for 16% -> 16%
where the time goes in v12:
time: 138 us; the launch traced here: 137 us
  Pallas kernels  77.2 us (56%)
  starting transfers between devices  29 us (21%)
  waiting for transfers between devices  19.4 us (14%)
  other arithmetic  7.28 us (5%)
  local copies, waits for them, and re-layouts  3.48 us (3%)
    pallas_call x1, Pallas kernels, local(): pl.pallas_call(final_kernel, grid=(width // each,), in_specs=[pl.BlockSpe...  32.5 us
    pallas_call x1, Pallas kernels, local(): pl.pallas_call(states_kernel, grid=(width // each,), in_specs=[pl.BlockSp...  22.4 us
    pallas_call x3, Pallas kernels, call(): pl.pallas_call(blocks_kernel, grid=(last - first,), in_specs=[pairs, stat...  22.3 us
    ppermute x6, starting transfers between devices, rotated(): lax.ppermute(value, axis, [(s, (s + steps) % count) for s in range(count)])  8.99 us
    ppermute x3, starting transfers between devices, paired(): lax.ppermute(value, axis, [(source, source ^ step) for source in lines or...  8.79 us
    ppermute x5, starting transfers between devices, swapped(): return lax.ppermute(value, 'ctx', [(s, s ^ 1) for s in range(count)])  7.14 us
    ppermute x6, waiting for transfers between devices, rotated(): lax.ppermute(value, axis, [(s, (s + steps) % count) for s in range(count)])  7.01 us
    ppermute x3, waiting for transfers between devices, paired(): lax.ppermute(value, axis, [(source, source ^ step) for source in lines or...  5.2 us
  transfers between devices with their start and end apart: 18, of which 11 were waited for; matrix products, arithmetic and copies ran while one was open for 5% of the time, Pallas kernels for 16%

profile of v12, /device:TPU:0, one launch (start us, length us, event | category | flops | bytes accessed | tf_op | source)
XLA Modules:
  0.0 137.4 jit_solution(6467485640561768510)
XLA Ops:
  0.6 0.0 copy-start
  0.7 1.3 dynamic-slice_bitcast_fusion
  2.0 0.5 collective-permute-start.1
  2.5 0.7 collective-permute-start
  3.2 0.8 negate_bitcast_fusion
  4.0 0.9 multiply_exponential_fusion
  4.9 0.0 copy-start.5
  4.9 1.4 %fusion.7 = (f32[16,512]{1,0:T(8,128)}, f32[16,512]{1,0:T(8,128)S(1)}, f32[16,512]{1,0:T(8,128)S(1)}) fusion(f32[512,16]{0,1:T(8,128)} %param.14), kind=kLoop, calls=%fused_computation.50 | loop fusion | flops 24576 | bytes 131072 | tf_op jit(solution)/shard_map/mul | solution.py:276
  6.3 0.0 copy-start.2
  6.4 0.0 copy-start.10
  6.4 22.4 %states.1 = (f32[16,3,136,512]{3,2,1,0:T(8,128)}, f32[16,2,136,512]{3,2,1,0:T(8,128)}, f32[16,16,8,512]{3,2,1,0:T(8,128)}, f32[16,16,8,512]{3,2,1,0:T(8,128)}, f32[2,16,16,512]{3,2,1,0:T(8,128)}) custom-call(s32[1]{0:T(128)} %bitcast.core, bf16[3,128,8192]{2,1,0:T(8,128)(2,1)} %bitcast.93, bf16[3,8,8192]{2,1,0:T(8,128)(2,1)S(1)} %collective-permute-done.hx, ...), custom_call_target="tpu_custom_call" | custom-call | tf_op jit(solution)/shard_map/states/pallas_call | solution.py:399
  28.8 0.0 copy-start.12
  28.8 0.0 copy-start.13
  28.8 0.0 copy-start.4
  28.8 6.3 %collective-permute-start.3 = (f32[2,16,16,512]{3,2,1,0:T(8,128)}, f32[2,16,16,512]{3,2,1,0:T(8,128)}, u32[]{:S(2)}, u32[]{:S(2)}) collective-permute-start(f32[2,16,16,512]{3,2,1,0:T(8,128)} %get-tuple-element.43), channel_id=1, source_target_pairs={{0,1},{1,0},{2,3},{3,2},{4,5},{5,4},{6,7},{7,6},{8,9},{9,8},{10,11... | collective-permute-start | bytes 3145736 | tf_op jit(solution)/shard_map/ppermute | solution.py:255
  35.1 0.7 slice_bitcast_fusion.8
  35.8 1.3 collective-permute-start.2
  37.1 0.1 multiply_exponential_fusion.1
  37.2 0.8 slice_multiply_fusion
  38.0 1.3 dynamic-slice_select_fusion.1
  39.3 0.1 broadcast_select_fusion.4
  39.4 2.8 %collective-permute-start.4 = (f32[8,16,512]{2,1,0:T(8,128)S(1)}, f32[8,16,512]{2,1,0:T(8,128)S(1)}, u32[]{:S(2)}, u32[]{:S(2)}) collective-permute-start(f32[8,16,512]{2,1,0:T(8,128)S(1)} %broadcast_select_fusion.4), channel_id=1, source_target_pairs={{0,2},{1,3},{2,0},{3,1},{4,6},{5,7},{6,4},{7,5},{8,10},{9,11},{10,... | collective-permute-start | bytes 786440 | tf_op jit(solution)/shard_map/ppermute | solution.py:271
  42.2 0.3 broadcast_select_fusion
  42.6 1.0 multiply_reduce_fusion.near
  43.6 8.2 %blocks.3 = (f32[16,2,136,512]{3,2,1,0:T(8,128)}, f32[16,16,8,512]{3,2,1,0:T(8,128)}, f32[16,16,8,512]{3,2,1,0:T(8,128)}, f32[6,8,512]{2,1,0:T(8,128)S(1)}) custom-call(f32[16,2,136,512]{3,2,1,0:T(8,128)} %get-tuple-element.44.xg, f32[16,16,8,512]{3,2,1,0:T(8,128)} %get-tuple-element.45.blocks_e, ...), custom_call_target="tpu_custom_call", output_to_operand_aliasing={{0}: (0, {}), {1}: (1, {}), {2}: (2, {})} | custom-call | flops 62914560 | bytes 36700160 | tf_op jit(solution)/shard_map/blocks/pallas_call | solution.py:429
  51.8 0.1 multiply_add_fusion.1
  52.0 0.7 collective-permute-start.5
  52.6 5.9 %blocks.4 = (f32[16,2,136,512]{3,2,1,0:T(8,128)}, f32[16,16,8,512]{3,2,1,0:T(8,128)}, f32[16,16,8,512]{3,2,1,0:T(8,128)}, f32[4,8,512]{2,1,0:T(8,128)S(1)}) custom-call(f32[16,2,136,512]{3,2,1,0:T(8,128)} %get-tuple-element.53.xg, f32[16,16,8,512]{3,2,1,0:T(8,128)} %get-tuple-element.54.blocks_e, ...), custom_call_target="tpu_custom_call", output_to_operand_aliasing={{0}: (0, {}), {1}: (1, {}), {2}: (2, {})} | custom-call | flops 62914560 | bytes 36700160 | tf_op jit(solution)/shard_map/blocks/pallas_call | solution.py:429
  58.5 1.4 %collective-permute-start.6 = (f32[8,16,512]{2,1,0:T(8,128)S(1)}, f32[8,16,512]{2,1,0:T(8,128)S(1)}, u32[]{:S(2)}, u32[]{:S(2)}) collective-permute-start(f32[8,16,512]{2,1,0:T(8,128)S(1)} %collective-permute-done.5), channel_id=1, source_target_pairs={{4,6},{5,7},{2,0},{3,1},{12,14},{13,15},{10,8},{11,9},{20,22},{21,... | collective-permute-start | bytes 786440 | tf_op jit(solution)/shard_map/ppermute | solution.py:287
  60.0 8.2 %blocks.5 = (f32[16,2,136,512]{3,2,1,0:T(8,128)}, f32[16,16,8,512]{3,2,1,0:T(8,128)}, f32[16,16,8,512]{3,2,1,0:T(8,128)}, f32[6,8,512]{2,1,0:T(8,128)S(1)}) custom-call(f32[16,2,136,512]{3,2,1,0:T(8,128)} %get-tuple-element.63.xg, f32[16,16,8,512]{3,2,1,0:T(8,128)} %get-tuple-element.64.blocks_e, ...), custom_call_target="tpu_custom_call", output_to_operand_aliasing={{0}: (0, {}), {1}: (1, {}), {2}: (2, {})} | custom-call | flops 62914560 | bytes 36700160 | tf_op jit(solution)/shard_map/blocks/pallas_call | solution.py:429
  68.2 2.0 %collective-permute-done.6 = f32[8,16,512]{2,1,0:T(8,128)S(1)} collective-permute-done((f32[8,16,512]{2,1,0:T(8,128)S(1)}, f32[8,16,512]{2,1,0:T(8,128)S(1)}, u32[]{:S(2)}, u32[]{:S(2)}) %collective-permute-start.6) | collective-permute-done | bytes 262176 | tf_op jit(solution)/shard_map/ppermute | solution.py:287
  70.3 0.1 select_bitcast_fusion.1
  70.4 0.1 collective-permute-start.7
  70.5 0.1 fusion
  70.6 1.8 %collective-permute-done.7.found = f32[2,8,16,512]{3,2,1,0:T(8,128)S(1)} collective-permute-done((f32[2,8,16,512]{3,2,1,0:T(8,128)S(1)}, f32[2,8,16,512]{3,2,1,0:T(8,128)S(1)}, u32[]{:S(2)}, u32[]{:S(2)}) %collective-permute-start.7) | collective-permute-done | bytes 524320 | tf_op jit(solution)/shard_map/ppermute | solution.py:255
  72.4 32.5 %final.1 = (bf16[128,8192]{1,0:T(8,128)(2,1)}, bf16[3,128,8192]{2,1,0:T(8,128)(2,1)}, f32[32,24,256]{2,1,0:T(8,128)S(1)}) custom-call(s32[1]{0:T(128)} %bitcast.core, bf16[3,128,8192]{2,1,0:T(8,128)(2,1)} %bitcast.94, bf16[3,8,8192]{2,1,0:T(8,128)(2,1)S(1)} %copy-done.3, bf16[3,8,8192]{2,1,0:T(8,128)(2,1)S(1)} %collective-permute-done.1.hi, ...), custom_call_target="tpu_custom_call" | custom-call | tf_op jit(solution)/shard_map/final/pallas_call | solution.py:473
  104.9 0.1 slice_select_fusion
  104.9 0.2 collective-permute-start.8
  105.1 1.6 %collective-permute-done.8 = f32[16,24,256]{2,1,0:T(8,128)S(1)} collective-permute-done((f32[16,24,256]{2,1,0:T(8,128)S(1)}, f32[16,24,256]{2,1,0:T(8,128)S(1)}, u32[]{:S(2)}, u32[]{:S(2)}) %collective-permute-start.8) | collective-permute-done | bytes 393248 | tf_op jit(solution)/shard_map/ppermute | solution.py:255
  106.7 0.1 select_add_fusion
  106.8 1.5 %collective-permute-start.9 = (f32[4,24,256]{2,1,0:T(8,128)S(1)}, f32[4,24,256]{2,1,0:T(8,128)S(1)}, u32[]{:S(2)}, u32[]{:S(2)}) collective-permute-start(f32[4,24,256]{2,1,0:T(8,128)S(1)} %get-tuple-element.94), channel_id=1, source_target_pairs={{0,8},{8,16},{16,24},{24,0},{1,9},{9,17},{17,25},{25,1},{2,10},{10... | collective-permute-start | bytes 294920 | tf_op jit(solution)/shard_map/ppermute | solution.py:307
  108.4 1.4 %collective-permute-start.11 = (f32[4,24,256]{2,1,0:T(8,128)S(1)}, f32[4,24,256]{2,1,0:T(8,128)S(1)}, u32[]{:S(2)}, u32[]{:S(2)}) collective-permute-start(f32[4,24,256]{2,1,0:T(8,128)S(1)} %get-tuple-element.95), channel_id=1, source_target_pairs={{0,24},{8,0},{16,8},{24,16},{1,25},{9,1},{17,9},{25,17},{2,26},{10... | collective-permute-start | bytes 294920 | tf_op jit(solution)/shard_map/ppermute | solution.py:307
  109.8 1.5 %collective-permute-start.10 = (f32[4,24,256]{2,1,0:T(8,128)S(1)}, f32[4,24,256]{2,1,0:T(8,128)S(1)}, u32[]{:S(2)}, u32[]{:S(2)}) collective-permute-start(f32[4,24,256]{2,1,0:T(8,128)S(1)} %get-tuple-element.96), channel_id=1, source_target_pairs={{0,16},{8,24},{16,0},{24,8},{1,17},{9,25},{17,1},{25,9},{2,18},{10... | collective-permute-start | bytes 294920 | tf_op jit(solution)/shard_map/ppermute | solution.py:307
  111.3 2.1 %collective-permute-done.9 = f32[4,24,256]{2,1,0:T(8,128)S(1)} collective-permute-done((f32[4,24,256]{2,1,0:T(8,128)S(1)}, f32[4,24,256]{2,1,0:T(8,128)S(1)}, u32[]{:S(2)}, u32[]{:S(2)}) %collective-permute-start.9) | collective-permute-done | bytes 98336 | tf_op jit(solution)/shard_map/ppermute | solution.py:307
  113.4 1.4 collective-permute-done.11
  114.8 0.0 collective-permute-done.10
  114.8 2.7 %collective-permute-start.12 = (f32[4,24,256]{2,1,0:T(8,128)S(1)}, f32[4,24,256]{2,1,0:T(8,128)S(1)}, u32[]{:S(2)}, u32[]{:S(2)}) collective-permute-start(f32[4,24,256]{2,1,0:T(8,128)S(1)} %add_add_fusion), channel_id=1, source_target_pairs={{0,2},{1,3},{2,0},{3,1},{4,6},{5,7},{6,4},{7,5},{8,10},{9,11},{10,... | collective-permute-start | bytes 294920 | tf_op jit(solution)/shard_map/ppermute | solution.py:271
  117.6 2.6 %collective-permute-done.12 = f32[4,24,256]{2,1,0:T(8,128)S(1)} collective-permute-done((f32[4,24,256]{2,1,0:T(8,128)S(1)}, f32[4,24,256]{2,1,0:T(8,128)S(1)}, u32[]{:S(2)}, u32[]{:S(2)}) %collective-permute-start.12) | collective-permute-done | bytes 98336 | tf_op jit(solution)/shard_map/ppermute | solution.py:271
  120.2 3.3 %collective-permute-start.13 = (f32[4,24,256]{2,1,0:T(8,128)S(1)}, f32[4,24,256]{2,1,0:T(8,128)S(1)}, u32[]{:S(2)}, u32[]{:S(2)}) collective-permute-start(f32[4,24,256]{2,1,0:T(8,128)S(1)} %add.95), channel_id=1, source_target_pairs={{0,4},{1,5},{2,6},{3,7},{4,0},{5,1},{6,2},{7,3},{8,12},{9,13},{10,... | collective-permute-start | bytes 294920 | tf_op jit(solution)/shard_map/ppermute | solution.py:271
  123.4 2.6 %collective-permute-done.13 = f32[4,24,256]{2,1,0:T(8,128)S(1)} collective-permute-done((f32[4,24,256]{2,1,0:T(8,128)S(1)}, f32[4,24,256]{2,1,0:T(8,128)S(1)}, u32[]{:S(2)}, u32[]{:S(2)}) %collective-permute-start.13) | collective-permute-done | bytes 98336 | tf_op jit(solution)/shard_map/ppermute | solution.py:271
  126.1 2.1 %collective-permute-start.14 = (f32[4,24,256]{2,1,0:T(8,128)S(1)}, f32[4,24,256]{2,1,0:T(8,128)S(1)}, u32[]{:S(2)}, u32[]{:S(2)}) collective-permute-start(f32[4,24,256]{2,1,0:T(8,128)S(1)} %get-tuple-element.81), channel_id=1, source_target_pairs={{0,8},{8,16},{16,24},{24,0},{1,9},{9,17},{17,25},{25,1},{2,10},{10... | collective-permute-start | bytes 294920 | tf_op jit(solution)/shard_map/ppermute | solution.py:307
  128.2 1.4 collective-permute-start.15
  129.5 1.1 collective-permute-start.16
  130.6 1.2 collective-permute-done.14
  131.8 1.0 collective-permute-done.15
  132.9 1.3 collective-permute-done.16
  134.2 0.1 collective-permute-start.17
  134.2 1.7 %collective-permute-done.17 = f32[16,24,256]{2,1,0:T(8,128)S(1)} collective-permute-done((f32[16,24,256]{2,1,0:T(8,128)S(1)}, f32[16,24,256]{2,1,0:T(8,128)S(1)}, u32[]{:S(2)}, u32[]{:S(2)}) %collective-permute-start.17) | collective-permute-done | bytes 393248 | tf_op jit(solution)/shard_map/ppermute | solution.py:255
  136.0 0.1 broadcast_select_fusion.3
  136.0 0.1 maximum_bitcast_fusion
  136.1 0.3 copy.25
  136.3 0.1 reshape.30
  136.5 0.7 slice.75
  137.2 0.2 copy-done.7
  (40 shorter events, 0.3 us)
Async XLA Ops:
  0.6 5.7 %copy-start = (bf16[1,128,8192]{2,1,0:T(8,128)(2,1)S(1)}, bf16[1,128,8192]{2,1,0:T(8,128)(2,1)}, u32[]{:S(2)}) copy-start(bf16[1,128,8192]{2,1,0:T(8,128)(2,1)} %param.16) | copy-start | bytes 6291460
  0.6 5.7 %copy-start.1 = (f32[3,7,8192]{2,1,0:T(8,128)S(1)}, f32[3,7,8192]{2,1,0:T(8,128)}, u32[]{:S(2)}) copy-start(f32[3,7,8192]{2,1,0:T(8,128)} %filt.3) | copy-start | bytes 2064388
  2.0 4.3 %collective-permute-start.1 = (bf16[3,8,8192]{2,1,0:T(8,128)(2,1)S(1)}, bf16[3,8,8192]{2,1,0:T(8,128)(2,1)S(1)}, u32[]{:S(2)}, u32[]{:S(2)}) collective-permute-start(bf16[3,8,8192]{2,1,0:T(8,128)(2,1)S(1)} %get-tuple-element.82), channel_id=1, source_target_pairs={{0,1},{1,0},{2,3},{3,2},{4,5},{5,4},{6,7},{7,6},{8,9},{9,8},{10,11... | collective-permute-start | bytes 1179656 | tf_op jit(solution)/shard_map/ppermute | solution.py:255
  2.5 3.8 %collective-permute-start = (bf16[3,8,8192]{2,1,0:T(8,128)(2,1)S(1)}, bf16[3,8,8192]{2,1,0:T(8,128)(2,1)S(1)}, u32[]{:S(2)}, u32[]{:S(2)}) collective-permute-start(bf16[3,8,8192]{2,1,0:T(8,128)(2,1)S(1)} %get-tuple-element.83), channel_id=1, source_target_pairs={{1,2},{3,4},{5,6},{2,1},{4,3},{6,5},{9,10},{11,12},{13,14},{10,9},... | collective-permute-start | bytes 1179656 | tf_op jit(solution)/shard_map/ppermute | solution.py:352
  4.9 1.5 %copy-start.5 = (f32[4,16,8,512]{3,2,1,0:T(8,128)}, f32[4,16,8,512]{3,2,1,0:T(8,128)S(1)}, u32[]{:S(2)}) copy-start(f32[4,16,8,512]{3,2,1,0:T(8,128)S(1)} %multiply_exponential_fusion) | copy-start | bytes 3145732
  6.3 22.4 %copy-start.2 = (bf16[3,8,8192]{2,1,0:T(8,128)(2,1)}, bf16[3,8,8192]{2,1,0:T(8,128)(2,1)S(1)}, u32[]{:S(2)}) copy-start(bf16[3,8,8192]{2,1,0:T(8,128)(2,1)S(1)} %collective-permute-done.hx) | copy-start | bytes 1179652
  6.4 30.7 %copy-start.10 = (f32[4]{0:T(128)S(1)}, f32[4]{0:T(128)}, u32[]{:S(2)}) copy-start(f32[4]{0:T(128)} %constant.89) | copy-start | bytes 52
  28.8 13.5 %copy-start.11 = (pred[4,8]{1,0:T(4,128)(4,1)S(1)}, pred[4,8]{1,0:T(4,128)(4,1)}, u32[]{:S(2)}) copy-start(pred[4,8]{1,0:T(4,128)(4,1)} %constant.90) | copy-start | bytes 100
  28.8 13.5 %copy-start.12 = (pred[4,8]{1,0:T(4,128)(4,1)S(1)}, pred[4,8]{1,0:T(4,128)(4,1)}, u32[]{:S(2)}) copy-start(pred[4,8]{1,0:T(4,128)(4,1)} %constant.88) | copy-start | bytes 100
  28.8 13.8 %copy-start.13 = (f32[24]{0:T(128)S(1)}, f32[24]{0:T(128)}, u32[]{:S(2)}) copy-start(f32[24]{0:T(128)} %constant.87) | copy-start | bytes 292
  28.8 14.8 %copy-start.4 = (f32[8192]{0:T(1024)S(1)}, f32[8192]{0:T(1024)}, u32[]{:S(2)}) copy-start(f32[8192]{0:T(1024)} %param.15) | copy-start | bytes 98308
  28.8 9.2 %collective-permute-start.3 = (f32[2,16,16,512]{3,2,1,0:T(8,128)}, f32[2,16,16,512]{3,2,1,0:T(8,128)}, u32[]{:S(2)}, u32[]{:S(2)}) collective-permute-start(f32[2,16,16,512]{3,2,1,0:T(8,128)} %get-tuple-element.43), channel_id=1, source_target_pairs={{0,1},{1,0},{2,3},{3,2},{4,5},{5,4},{6,7},{7,6},{8,9},{9,8},{10,11... | collective-permute-start | bytes 3145736 | tf_op jit(solution)/shard_map/ppermute | solution.py:255
  35.8 7.8 %collective-permute-start.2 = (bf16[8,8192]{1,0:T(8,128)(2,1)}, bf16[8,8192]{1,0:T(8,128)(2,1)S(1)}, u32[]{:S(2)}, u32[]{:S(2)}) collective-permute-start(bf16[8,8192]{1,0:T(8,128)(2,1)} %slice_bitcast_fusion.8), channel_id=1, source_target_pairs={{1,0},{2,1},{3,2},{4,3},{5,4},{6,5},{7,6},{9,8},{10,9},{11,10},{12... | collective-permute-start | bytes 393224 | tf_op jit(solution)/shard_map/ppermute | solution.py:250
  39.4 12.4 %collective-permute-start.4 = (f32[8,16,512]{2,1,0:T(8,128)S(1)}, f32[8,16,512]{2,1,0:T(8,128)S(1)}, u32[]{:S(2)}, u32[]{:S(2)}) collective-permute-start(f32[8,16,512]{2,1,0:T(8,128)S(1)} %broadcast_select_fusion.4), channel_id=1, source_target_pairs={{0,2},{1,3},{2,0},{3,1},{4,6},{5,7},{6,4},{7,5},{8,10},{9,11},{10,... | collective-permute-start | bytes 786440 | tf_op jit(solution)/shard_map/ppermute | solution.py:271
  43.6 8.2 %copy-start.8 = (f32[16,512]{1,0:T(8,128)S(1)}, f32[16,512]{1,0:T(8,128)}, u32[]{:S(2)}) copy-start(f32[16,512]{1,0:T(8,128)} %get-tuple-element.99) | copy-start | bytes 98308
  52.0 6.6 %collective-permute-start.5 = (f32[8,16,512]{2,1,0:T(8,128)S(1)}, f32[8,16,512]{2,1,0:T(8,128)S(1)}, u32[]{:S(2)}, u32[]{:S(2)}) collective-permute-start(f32[8,16,512]{2,1,0:T(8,128)S(1)} %multiply_add_fusion.1), channel_id=1, source_target_pairs={{2,4},{3,5},{4,2},{5,3},{10,12},{11,13},{12,10},{13,11},{18,20},{1... | collective-permute-start | bytes 786440 | tf_op jit(solution)/shard_map/ppermute | solution.py:284
  58.5 12.0 %copy-start.6 = (f32[4,16,8,512]{3,2,1,0:T(8,128)S(1)}, f32[4,16,8,512]{3,2,1,0:T(8,128)}, u32[]{:S(2)}) copy-start(f32[4,16,8,512]{3,2,1,0:T(8,128)} %copy-done.5) | copy-start | bytes 3145732
  58.5 12.0 %copy-start.9 = (f32[512,16]{0,1:T(8,128)S(1)}, f32[512,16]{0,1:T(8,128)}, u32[]{:S(2)}) copy-start(f32[512,16]{0,1:T(8,128)} %param.13) | copy-start | bytes 98308
  58.5 11.7 %collective-permute-start.6 = (f32[8,16,512]{2,1,0:T(8,128)S(1)}, f32[8,16,512]{2,1,0:T(8,128)S(1)}, u32[]{:S(2)}, u32[]{:S(2)}) collective-permute-start(f32[8,16,512]{2,1,0:T(8,128)S(1)} %collective-permute-done.5), channel_id=1, source_target_pairs={{4,6},{5,7},{2,0},{3,1},{12,14},{13,15},{10,8},{11,9},{20,22},{21,... | collective-permute-start | bytes 786440 | tf_op jit(solution)/shard_map/ppermute | solution.py:287
  68.2 4.2 %copy-start.3 = (bf16[3,8,8192]{2,1,0:T(8,128)(2,1)S(1)}, bf16[3,8,8192]{2,1,0:T(8,128)(2,1)}, u32[]{:S(2)}) copy-start(bf16[3,8,8192]{2,1,0:T(8,128)(2,1)} %copy-done.2) | copy-start | bytes 1179652
  70.4 2.0 %collective-permute-start.7 = (f32[2,8,16,512]{3,2,1,0:T(8,128)S(1)}, f32[2,8,16,512]{3,2,1,0:T(8,128)S(1)}, u32[]{:S(2)}, u32[]{:S(2)}) collective-permute-start(f32[2,8,16,512]{3,2,1,0:T(8,128)S(1)} %pad_maximum_fusion.both), channel_id=1, source_target_pairs={{0,1},{1,0},{2,3},{3,2},{4,5},{5,4},{6,7},{7,6},{8,9},{9,8},{10,11... | collective-permute-start | bytes 1572872 | tf_op jit(solution)/shard_map/ppermute | solution.py:255
  104.9 1.8 %collective-permute-start.8 = (f32[16,24,256]{2,1,0:T(8,128)S(1)}, f32[16,24,256]{2,1,0:T(8,128)S(1)}, u32[]{:S(2)}, u32[]{:S(2)}) collective-permute-start(f32[16,24,256]{2,1,0:T(8,128)S(1)} %slice_select_fusion), channel_id=1, source_target_pairs={{0,1},{1,0},{2,3},{3,2},{4,5},{5,4},{6,7},{7,6},{8,9},{9,8},{10,11... | collective-permute-start | bytes 1179656 | tf_op jit(solution)/shard_map/ppermute | solution.py:255
  106.8 6.6 %collective-permute-start.9 = (f32[4,24,256]{2,1,0:T(8,128)S(1)}, f32[4,24,256]{2,1,0:T(8,128)S(1)}, u32[]{:S(2)}, u32[]{:S(2)}) collective-permute-start(f32[4,24,256]{2,1,0:T(8,128)S(1)} %get-tuple-element.94), channel_id=1, source_target_pairs={{0,8},{8,16},{16,24},{24,0},{1,9},{9,17},{17,25},{25,1},{2,10},{10... | collective-permute-start | bytes 294920 | tf_op jit(solution)/shard_map/ppermute | solution.py:307
  108.4 6.4 %collective-permute-start.11 = (f32[4,24,256]{2,1,0:T(8,128)S(1)}, f32[4,24,256]{2,1,0:T(8,128)S(1)}, u32[]{:S(2)}, u32[]{:S(2)}) collective-permute-start(f32[4,24,256]{2,1,0:T(8,128)S(1)} %get-tuple-element.95), channel_id=1, source_target_pairs={{0,24},{8,0},{16,8},{24,16},{1,25},{9,1},{17,9},{25,17},{2,26},{10... | collective-permute-start | bytes 294920 | tf_op jit(solution)/shard_map/ppermute | solution.py:307
  109.8 5.0 %collective-permute-start.10 = (f32[4,24,256]{2,1,0:T(8,128)S(1)}, f32[4,24,256]{2,1,0:T(8,128)S(1)}, u32[]{:S(2)}, u32[]{:S(2)}) collective-permute-start(f32[4,24,256]{2,1,0:T(8,128)S(1)} %get-tuple-element.96), channel_id=1, source_target_pairs={{0,16},{8,24},{16,0},{24,8},{1,17},{9,25},{17,1},{25,9},{2,18},{10... | collective-permute-start | bytes 294920 | tf_op jit(solution)/shard_map/ppermute | solution.py:307
  114.8 5.3 %collective-permute-start.12 = (f32[4,24,256]{2,1,0:T(8,128)S(1)}, f32[4,24,256]{2,1,0:T(8,128)S(1)}, u32[]{:S(2)}, u32[]{:S(2)}) collective-permute-start(f32[4,24,256]{2,1,0:T(8,128)S(1)} %add_add_fusion), channel_id=1, source_target_pairs={{0,2},{1,3},{2,0},{3,1},{4,6},{5,7},{6,4},{7,5},{8,10},{9,11},{10,... | collective-permute-start | bytes 294920 | tf_op jit(solution)/shard_map/ppermute | solution.py:271
  120.2 5.9 %collective-permute-start.13 = (f32[4,24,256]{2,1,0:T(8,128)S(1)}, f32[4,24,256]{2,1,0:T(8,128)S(1)}, u32[]{:S(2)}, u32[]{:S(2)}) collective-permute-start(f32[4,24,256]{2,1,0:T(8,128)S(1)} %add.95), channel_id=1, source_target_pairs={{0,4},{1,5},{2,6},{3,7},{4,0},{5,1},{6,2},{7,3},{8,12},{9,13},{10,... | collective-permute-start | bytes 294920 | tf_op jit(solution)/shard_map/ppermute | solution.py:271
  126.1 5.7 %collective-permute-start.14 = (f32[4,24,256]{2,1,0:T(8,128)S(1)}, f32[4,24,256]{2,1,0:T(8,128)S(1)}, u32[]{:S(2)}, u32[]{:S(2)}) collective-permute-start(f32[4,24,256]{2,1,0:T(8,128)S(1)} %get-tuple-element.81), channel_id=1, source_target_pairs={{0,8},{8,16},{16,24},{24,0},{1,9},{9,17},{17,25},{25,1},{2,10},{10... | collective-permute-start | bytes 294920 | tf_op jit(solution)/shard_map/ppermute | solution.py:307
  128.2 4.7 %collective-permute-start.15 = (f32[4,24,256]{2,1,0:T(8,128)S(1)}, f32[4,24,256]{2,1,0:T(8,128)S(1)}, u32[]{:S(2)}, u32[]{:S(2)}) collective-permute-start(f32[4,24,256]{2,1,0:T(8,128)S(1)} %get-tuple-element.81), channel_id=1, source_target_pairs={{0,16},{8,24},{16,0},{24,8},{1,17},{9,25},{17,1},{25,9},{2,18},{10... | collective-permute-start | bytes 294920 | tf_op jit(solution)/shard_map/ppermute | solution.py:307
  129.5 4.6 %collective-permute-start.16 = (f32[4,24,256]{2,1,0:T(8,128)S(1)}, f32[4,24,256]{2,1,0:T(8,128)S(1)}, u32[]{:S(2)}, u32[]{:S(2)}) collective-permute-start(f32[4,24,256]{2,1,0:T(8,128)S(1)} %get-tuple-element.81), channel_id=1, source_target_pairs={{0,24},{8,0},{16,8},{24,16},{1,25},{9,1},{17,9},{25,17},{2,26},{10... | collective-permute-start | bytes 294920 | tf_op jit(solution)/shard_map/ppermute | solution.py:307
  134.2 1.8 %collective-permute-start.17 = (f32[16,24,256]{2,1,0:T(8,128)S(1)}, f32[16,24,256]{2,1,0:T(8,128)S(1)}, u32[]{:S(2)}, u32[]{:S(2)}) collective-permute-start(f32[16,24,256]{2,1,0:T(8,128)S(1)} %constant_dynamic-update-slice_fusion), channel_id=1, source_target_pairs={{0,1},{1,0},{2,3},{3,2},{4,5},{5,4},{6,7},{7,6},{8,9},{9,8},{10,11... | collective-permute-start | bytes 1179656 | tf_op jit(solution)/shard_map/ppermute | solution.py:255
  136.5 0.9 copy-start.7

commit v13 on v12

--- a/solution.py
+++ b/solution.py
@@ -46,6 +46,16 @@
     return values[0]
 
 
+def phases(tap):
+    even, odd = tap[0::2], tap[1::2]
+    both = [even[k] + odd[k] if k < len(odd) else even[k] for k in range(len(even))]
+    return even, odd, both
+
+
+def weighted(tap, values):
+    return added([tap[k] * values[k] for k in range(len(tap))])
+
+
 def states_kernel(core, p, hx, hi, u, filt, f1, we, wb, qkv, xg, blocks_e, blocks_a, ends, xs):
     rows = p.shape[1]
     run = (rows + SUB) // SUB
@@ -69,11 +79,22 @@
         xs[3, SUB + rows :] = jnp.ones((SUB, LANES), F32)
 
         def mixed(j):
-            tap = [spread(filt[j, i : i + 1, lanes]) for i in range(taps)]
-            view = [xs[j, pl.ds(SUB + a, SUB, stride=run), :] for a in range(1 - taps, 0)]
-            for a in range(run):
-                view = view[-(taps - 1) :] + [xs[j, pl.ds(SUB + a, SUB, stride=run), :]]
-                yield added([tap[i] * view[-1 - i] for i in range(taps)])
+            even, odd, both = phases([spread(filt[j, i : i + 1, lanes]) for i in range(taps)])
+            row = lambda a: xs[j, pl.ds(SUB + a, SUB, stride=run), :]
+            reach = len(even)
+            evens = [row(-2 * k) for k in range(1, reach)]
+            odds = [row(1 - 2 * k) for k in range(1, reach)]
+            pairs = [evens[k] + odds[k] for k in range(reach - 1)]
+            before = weighted(odd, odds)
+            for a in range(0, run, 2):
+                evens = [row(a)] + evens[: reach - 1]
+                first = weighted(even, evens)
+                yield first + before
+                if a + 1 < run:
+                    odds = [row(a + 1)] + odds[: reach - 1]
+                    pairs = [evens[0] + odds[0]] + pairs[: reach - 1]
+                    before = weighted(odd, odds)
+                    yield weighted(both, pairs) - first - before
 
         decay = [spread(f1[n : n + 1, part]) for n in range(poles)]
         for j in (1, 2, 0):
@@ -219,22 +240,60 @@
                 state = [state[n] * decay[n] for n in range(poles)]
 
         for j in range(3):
-            tap = [spread(filt[j, i : i + 1, lanes]) for i in range(taps)]
+            even, odd, paired_taps = phases([spread(filt[j, i : i + 1, lanes]) for i in range(taps)])
+            reach = len(even)
             grads = [gs[j, SUB * a : SUB * a + SUB] for a in range(taps - 1)]
             beyond = [pltpu.roll(value, SUB - 1, 0) for value in grads]
-            views = [ps[j, pl.ds(SUB + a, SUB, stride=run), :] for a in range(1 - taps, 0)]
-            sums_of = [None] * taps
-            for a in range(run):
-                ahead = a + taps - 1
-                ahead = gs[j, SUB * ahead : SUB * ahead + SUB] if ahead < run else beyond[ahead - run]
-                grads = grads[-(taps - 1) :] + [ahead]
-                views = views[-(taps - 1) :] + [ps[j, pl.ds(SUB + a, SUB, stride=run), :]]
-                total = added([tap[i] * grads[i] for i in range(taps)])
-                os[pl.ds(a, SUB, stride=run), :] = total
-                grad = grads[0] if a < own else jnp.where(inside, grads[0], 0.0)
-                for i in range(taps):
-                    term = grad * views[-1 - i]
-                    sums_of[i] = term if a == 0 else sums_of[i] + term
+
+            def ahead(a):
+                return gs[j, SUB * a : SUB * a + SUB] if a < run else beyond[a - run]
+
+            def behind(a):
+                return ps[j, pl.ds(SUB + a, SUB, stride=run), :]
+
+            def own_rows(a):
+                return grads[a] if a < own else jnp.where(inside, grads[a], 0.0)
+
+            grads = {a: grads[a] for a in range(taps - 1)}
+            joint = {k: grads[2 * k + 1] + grads[2 * k + 2] for k in range((taps - 3) // 2)}
+            leading = weighted(even, [grads[2 * k] if 2 * k in grads else ahead(2 * k) for k in range(reach)])
+            evens = [behind(-2 * k) for k in range(1, reach)]
+            odds = [behind(1 - 2 * k) for k in range(1, reach)]
+            pairs = [evens[k] + odds[k] for k in range(reach - 1)]
+            sums_of = [[None] * reach for _ in range(3)]
+
+            def collect(kind, grad, values, count):
+                for k in range(count):
+                    term = grad * values[k]
+                    so_far = sums_of[kind][k]
+                    sums_of[kind][k] = term if so_far is None else so_far + term
+
+            previous = None
+            for a in range(0, run, 2):
+                for c in range(a, a + 2 * reach + 1):
+                    if c not in grads and c < run + taps - 1:
+                        grads[c] = ahead(c)
+                here = own_rows(a)
+                collect(1, here if previous is None else here - previous, odds, len(odd))
+                second = weighted(odd, [grads[a + 2 * k + 1] for k in range(len(odd))])
+                os[pl.ds(a, SUB, stride=run), :] = leading + second
+                evens = [behind(a)] + evens[: reach - 1]
+                if a + 1 < run:
+                    previous = own_rows(a + 1)
+                    for k in range(a // 2, a // 2 + reach):
+                        if k not in joint:
+                            joint[k] = grads[2 * k + 1] + grads[2 * k + 2]
+                    following = weighted(even, [grads[a + 2 + 2 * k] for k in range(reach)])
+                    total = weighted(paired_taps, [joint[a // 2 + k] for k in range(reach)])
+                    os[pl.ds(a + 1, SUB, stride=run), :] = total - following - second
+                    leading = following
+                    odds = [behind(a + 1)] + odds[: reach - 1]
+                    pairs = [evens[0] + odds[0]] + pairs[: reach - 1]
+                    collect(0, here - previous, evens, reach)
+                    collect(2, previous, pairs, reach)
+                else:
+                    collect(0, here, evens, reach)
+            sums_of = [sums_of[i % 2][i // 2] + sums_of[2][i // 2] for i in range(taps)]
             grad_p[j, :, lanes] = os[0:rows].astype(BF16)
             extra = [skip_sum[which, :, part]] + [jnp.zeros((SUB, LANES), F32)] * (SUB - taps)
             extra = extra[: SUB - taps] if j == 0 else extra[1 : SUB - taps + 1]
@@ -255,15 +314,15 @@
     return lax.ppermute(value, "ctx", [(s, s ^ 1) for s in range(count)])
 
 
-def joined(ends, f_all):
+def joined(ends, hu, f_all):
     core = lax.rem(lax.axis_index("ctx"), 2)
     half = ends.shape[1] // 2
-    other = swapped(ends)
+    other, hu = lax.optimization_barrier((swapped(ends), hu))
     first = core == 0
     mine = lax.dynamic_slice_in_dim(ends, core * half, half, 1)
     theirs = lax.dynamic_slice_in_dim(other, core * half, half, 1)
     one, two = jnp.where(first, mine, theirs), jnp.where(first, theirs, mine)
-    return other, f_all * one[0] + two[0], one[1] + f_all * two[1]
+    return other, hu, f_all * one[0] + two[0], one[1] + f_all * two[1]
 
 
 def paired(value, axis, step, lines=None):
@@ -351,7 +410,6 @@
     across = across + [(target, source) for source, target in across]
     hx = lax.ppermute(edge(core == 1), "ctx", across)
     hi = swapped(edge(core == 0))
-    hu = shifted(u[:SUB], "ctx", -1)
 
     rate = decay_rates.T
     weight = residues.T
@@ -389,6 +447,9 @@
     halved = pl.BlockSpec(
         (2, each, poles, groups), lambda w: (0, lax.rem(w, width // each // 2), 0, 0)
     )
+    early = (hx, near, join_e, join_a, cz, cy, f_all, u[:SUB])
+    hx, near, join_e, join_a, cz, cy, f_all, u_head = lax.optimization_barrier(early)
+    hu = shifted(u_head, "ctx", -1)
     state_shape = shape_of((width, poles, SUB, groups), F32)
     pair_shape = shape_of((width, 2, held, groups), F32)
 
@@ -454,7 +515,7 @@
 
     steps = width // many
     cuts = (0, (3 * steps) // 8, (5 * steps) // 8, steps)
-    other, chip_e, chip_a = joined(ends, f_all)
+    other, hu, chip_e, chip_a = joined(ends, hu, f_all)
     before, after, (conv, from_e, from_a, skip_sum) = scanned(
         chip_e, chip_a, f_all, [blocks(cuts[k], cuts[k + 1]) for k in range(3)]
     )

time: 138 us -> 141 us (1.022)
  waiting for transfers between devices: 19.4 us -> 25.9 us
  starting transfers between devices: 29 us -> 24.5 us
    ppermute x6, starting transfers between devices: 8.99 us -> 6.56 us  [rotated(): lax.ppermute(value, axis, [(s, (s + steps) % count) for s in range(count)])]
    ppermute x5, starting transfers between devices: 7.14 us -> 4.8 us  [swapped(): return lax.ppermute(value, 'ctx', [(s, s ^ 1) for s in range(count)])]
    ppermute x1, waiting for transfers between devices: 0.01 us -> 2.12 us  [shifted(): lax.ppermute(value, axis, [(source, source + steps) for source in range(f...]
    ppermute x6, waiting for transfers between devices: 7.01 us -> 8.75 us  [rotated(): lax.ppermute(value, axis, [(s, (s + steps) % count) for s in range(count)])]
    ppermute x1, waiting for transfers between devices: 2.03 us -> 3.46 us  [scanned(): far = lax.ppermute(near, 'ctx', [(4, 6), (5, 7), (2, 0), (3, 1)])]
  transfers between devices with their start and end apart: 18 -> 18, of which waited for: 11 -> 12; matrix products, arithmetic and copies ran while one was open for 5% -> 5% of each run, Pallas kernels for 16% -> 16%
where the time goes in v13:
time: 141 us; the launch traced here: 139 us
  Pallas kernels  76 us (54%)
  waiting for transfers between devices  25.9 us (18%)
  starting transfers between devices  24.5 us (17%)
  other arithmetic  7.36 us (5%)
  local copies, waits for them, and re-layouts  4.38 us (3%)
    pallas_call x1, Pallas kernels, local(): pl.pallas_call(final_kernel, grid=(width // each,), in_specs=[pl.BlockSpe...  31.6 us
    pallas_call x3, Pallas kernels, call(): pl.pallas_call(blocks_kernel, grid=(last - first,), in_specs=[pairs, stat...  22.3 us
    pallas_call x1, Pallas kernels, local(): pl.pallas_call(states_kernel, grid=(width // each,), in_specs=[pl.BlockSp...  22.2 us
    ppermute x3, starting transfers between devices, paired(): lax.ppermute(value, axis, [(source, source ^ step) for source in lines or...  9.04 us
    ppermute x6, waiting for transfers between devices, rotated(): lax.ppermute(value, axis, [(s, (s + steps) % count) for s in range(count)])  8.75 us
    ppermute x6, starting transfers between devices, rotated(): lax.ppermute(value, axis, [(s, (s + steps) % count) for s in range(count)])  6.56 us
    ppermute x3, waiting for transfers between devices, paired(): lax.ppermute(value, axis, [(source, source ^ step) for source in lines or...  6.33 us
    ppermute x5, waiting for transfers between devices, swapped(): return lax.ppermute(value, 'ctx', [(s, s ^ 1) for s in range(count)])  5.22 us
  transfers between devices with their start and end apart: 18, of which 12 were waited for; matrix products, arithmetic and copies ran while one was open for 5% of the time, Pallas kernels for 16%

profile of v13, /device:TPU:0, one launch (start us, length us, event | category | flops | bytes accessed | tf_op | source)
XLA Modules:
  0.0 139.2 jit_solution(2351389774318740125)
XLA Ops:
  0.6 0.0 copy-start.11
  0.6 0.0 copy-start.9
  0.7 0.0 copy-start.10
  0.7 0.0 copy-start
  0.7 1.3 dynamic-slice_bitcast_fusion
  2.0 0.7 collective-permute-start
  2.7 4.4 %collective-permute-start.1 = (bf16[3,8,8192]{2,1,0:T(8,128)(2,1)S(1)}, bf16[3,8,8192]{2,1,0:T(8,128)(2,1)S(1)}, u32[]{:S(2)}, u32[]{:S(2)}) collective-permute-start(bf16[3,8,8192]{2,1,0:T(8,128)(2,1)S(1)} %get-tuple-element.102), channel_id=1, source_target_pairs={{0,1},{1,0},{2,3},{3,2},{4,5},{5,4},{6,7},{7,6},{8,9},{9,8},{10,11... | collective-permute-start | bytes 1179656 | tf_op jit(solution)/shard_map/ppermute | solution.py:314
  7.2 0.8 negate_bitcast_fusion
  7.9 0.8 fusion.6
  8.7 0.8 multiply_exponential_fusion.1
  9.5 0.8 slice_multiply_fusion
  10.2 0.9 multiply_exponential_fusion
  11.2 0.8 fusion.4
  12.0 0.2 multiply_reduce_fusion.near
  12.2 1.6 %slice_bitcast_fusion.8 = bf16[8,8192]{1,0:T(8,128)(2,1)} fusion(bf16[1,128,8192]{2,1,0:T(8,128)(2,1)} %param.16), kind=kLoop, calls=%fused_computation.35 | loop fusion | bytes 262144 | tf_op jit(solution)/shard_map/slice | solution.py:450
  13.8 0.3 broadcast_select_fusion
  14.2 0.0 copy-start.2
  14.2 0.0 copy-start.6
  14.3 22.2 %states.1 = (f32[16,3,136,512]{3,2,1,0:T(8,128)}, f32[16,2,136,512]{3,2,1,0:T(8,128)}, f32[16,16,8,512]{3,2,1,0:T(8,128)}, f32[16,16,8,512]{3,2,1,0:T(8,128)}, f32[2,16,16,512]{3,2,1,0:T(8,128)}) custom-call(s32[1]{0:T(128)} %bitcast.core, bf16[3,128,8192]{2,1,0:T(8,128)(2,1)} %bitcast.91, bf16[3,8,8192]{2,1,0:T(8,128)(2,1)S(1)} %collective-permute-done.hx, ...), custom_call_target="tpu_custom_call" | custom-call | tf_op jit(solution)/shard_map/states/pallas_call | solution.py:460
  36.4 0.1 collective-permute-start.2
  36.5 1.3 collective-permute-start.3
  37.8 2.1 %collective-permute-done.3.hu = bf16[8,8192]{1,0:T(8,128)(2,1)S(1)} collective-permute-done((bf16[8,8192]{1,0:T(8,128)(2,1)}, bf16[8,8192]{1,0:T(8,128)(2,1)S(1)}, u32[]{:S(2)}, u32[]{:S(2)}) %collective-permute-start.3) | collective-permute-done | bytes 131104 | tf_op jit(solution)/shard_map/ppermute | solution.py:309
  39.9 1.3 dynamic-slice_select_fusion.1
  41.3 0.1 broadcast_select_fusion.4
  41.4 3.5 %collective-permute-start.4 = (f32[8,16,512]{2,1,0:T(8,128)S(1)}, f32[8,16,512]{2,1,0:T(8,128)S(1)}, u32[]{:S(2)}, u32[]{:S(2)}) collective-permute-start(f32[8,16,512]{2,1,0:T(8,128)S(1)} %broadcast_select_fusion.4), channel_id=1, source_target_pairs={{0,2},{1,3},{2,0},{3,1},{4,6},{5,7},{6,4},{7,5},{8,10},{9,11},{10,... | collective-permute-start | bytes 786440 | tf_op jit(solution)/shard_map/ppermute | solution.py:330
  44.8 8.2 %blocks.3 = (f32[16,2,136,512]{3,2,1,0:T(8,128)}, f32[16,16,8,512]{3,2,1,0:T(8,128)}, f32[16,16,8,512]{3,2,1,0:T(8,128)}, f32[6,8,512]{2,1,0:T(8,128)S(1)}) custom-call(f32[16,2,136,512]{3,2,1,0:T(8,128)} %get-tuple-element.59.xg, f32[16,16,8,512]{3,2,1,0:T(8,128)} %get-tuple-element.60.blocks_e, ...), custom_call_target="tpu_custom_call", output_to_operand_aliasing={{0}: (0, {}), {1}: (1, {}), {2}: (2, {})} | custom-call | flops 62914560 | bytes 36700160 | tf_op jit(solution)/shard_map/blocks/pallas_call | solution.py:490
  53.1 0.1 multiply_add_fusion.1
  53.2 0.7 collective-permute-start.5
  53.9 5.9 %blocks.4 = (f32[16,2,136,512]{3,2,1,0:T(8,128)}, f32[16,16,8,512]{3,2,1,0:T(8,128)}, f32[16,16,8,512]{3,2,1,0:T(8,128)}, f32[4,8,512]{2,1,0:T(8,128)S(1)}) custom-call(f32[16,2,136,512]{3,2,1,0:T(8,128)} %get-tuple-element.71.xg, f32[16,16,8,512]{3,2,1,0:T(8,128)} %get-tuple-element.72.blocks_e, ...), custom_call_target="tpu_custom_call", output_to_operand_aliasing={{0}: (0, {}), {1}: (1, {}), {2}: (2, {})} | custom-call | flops 62914560 | bytes 36700160 | tf_op jit(solution)/shard_map/blocks/pallas_call | solution.py:490
  59.8 0.0 copy-start.3
  59.8 1.4 %collective-permute-start.6 = (f32[8,16,512]{2,1,0:T(8,128)S(1)}, f32[8,16,512]{2,1,0:T(8,128)S(1)}, u32[]{:S(2)}, u32[]{:S(2)}) collective-permute-start(f32[8,16,512]{2,1,0:T(8,128)S(1)} %collective-permute-done.5), channel_id=1, source_target_pairs={{4,6},{5,7},{2,0},{3,1},{12,14},{13,15},{10,8},{11,9},{20,22},{21,... | collective-permute-start | bytes 786440 | tf_op jit(solution)/shard_map/ppermute | solution.py:346
  61.2 8.2 %blocks.5 = (f32[16,2,136,512]{3,2,1,0:T(8,128)}, f32[16,16,8,512]{3,2,1,0:T(8,128)}, f32[16,16,8,512]{3,2,1,0:T(8,128)}, f32[6,8,512]{2,1,0:T(8,128)S(1)}) custom-call(f32[16,2,136,512]{3,2,1,0:T(8,128)} %get-tuple-element.81.xg, f32[16,16,8,512]{3,2,1,0:T(8,128)} %get-tuple-element.82.blocks_e, ...), custom_call_target="tpu_custom_call", output_to_operand_aliasing={{0}: (0, {}), {1}: (1, {}), {2}: (2, {})} | custom-call | flops 62914560 | bytes 36700160 | tf_op jit(solution)/shard_map/blocks/pallas_call | solution.py:490
  69.5 3.5 %collective-permute-done.6 = f32[8,16,512]{2,1,0:T(8,128)S(1)} collective-permute-done((f32[8,16,512]{2,1,0:T(8,128)S(1)}, f32[8,16,512]{2,1,0:T(8,128)S(1)}, u32[]{:S(2)}, u32[]{:S(2)}) %collective-permute-start.6) | collective-permute-done | bytes 262176 | tf_op jit(solution)/shard_map/ppermute | solution.py:346
  72.9 0.1 select_bitcast_fusion.1
  73.1 0.1 collective-permute-start.7
  73.2 1.9 %collective-permute-done.7.found = f32[2,8,16,512]{3,2,1,0:T(8,128)S(1)} collective-permute-done((f32[2,8,16,512]{3,2,1,0:T(8,128)S(1)}, f32[2,8,16,512]{3,2,1,0:T(8,128)S(1)}, u32[]{:S(2)}, u32[]{:S(2)}) %collective-permute-start.7) | collective-permute-done | bytes 524320 | tf_op jit(solution)/shard_map/ppermute | solution.py:314
  75.1 31.6 %final.1 = (bf16[128,8192]{1,0:T(8,128)(2,1)}, bf16[3,128,8192]{2,1,0:T(8,128)(2,1)}, f32[32,24,256]{2,1,0:T(8,128)S(1)}) custom-call(s32[1]{0:T(128)} %bitcast.core, bf16[3,128,8192]{2,1,0:T(8,128)(2,1)} %bitcast.92, bf16[3,8,8192]{2,1,0:T(8,128)(2,1)S(1)} %collective-permute-done.hx, bf16[3,8,8192]{2,1,0:T(8,128)(2,1)S(1)} %copy-done.3, ...), custom_call_target="tpu_custom_call" | custom-call | tf_op jit(solution)/shard_map/final/pallas_call | solution.py:534
  106.6 0.1 slice_select_fusion
  106.7 0.2 collective-permute-start.8
  106.9 1.6 %collective-permute-done.8 = f32[16,24,256]{2,1,0:T(8,128)S(1)} collective-permute-done((f32[16,24,256]{2,1,0:T(8,128)S(1)}, f32[16,24,256]{2,1,0:T(8,128)S(1)}, u32[]{:S(2)}, u32[]{:S(2)}) %collective-permute-start.8) | collective-permute-done | bytes 393248 | tf_op jit(solution)/shard_map/ppermute | solution.py:314
  108.5 0.1 select_add_fusion
  108.6 2.5 %collective-permute-start.11 = (f32[4,24,256]{2,1,0:T(8,128)S(1)}, f32[4,24,256]{2,1,0:T(8,128)S(1)}, u32[]{:S(2)}, u32[]{:S(2)}) collective-permute-start(f32[4,24,256]{2,1,0:T(8,128)S(1)} %get-tuple-element.115), channel_id=1, source_target_pairs={{0,24},{8,0},{16,8},{24,16},{1,25},{9,1},{17,9},{25,17},{2,26},{10... | collective-permute-start | bytes 294920 | tf_op jit(solution)/shard_map/ppermute | solution.py:366
  111.1 0.5 collective-permute-start.10
  111.6 0.6 collective-permute-start.9
  112.2 2.1 %collective-permute-done.11 = f32[4,24,256]{2,1,0:T(8,128)S(1)} collective-permute-done((f32[4,24,256]{2,1,0:T(8,128)S(1)}, f32[4,24,256]{2,1,0:T(8,128)S(1)}, u32[]{:S(2)}, u32[]{:S(2)}) %collective-permute-start.11) | collective-permute-done | bytes 98336 | tf_op jit(solution)/shard_map/ppermute | solution.py:366
  114.3 3.5 %collective-permute-done.10 = f32[4,24,256]{2,1,0:T(8,128)S(1)} collective-permute-done((f32[4,24,256]{2,1,0:T(8,128)S(1)}, f32[4,24,256]{2,1,0:T(8,128)S(1)}, u32[]{:S(2)}, u32[]{:S(2)}) %collective-permute-start.10) | collective-permute-done | bytes 98336 | tf_op jit(solution)/shard_map/ppermute | solution.py:366
  117.9 2.0 %collective-permute-start.12 = (f32[4,24,256]{2,1,0:T(8,128)S(1)}, f32[4,24,256]{2,1,0:T(8,128)S(1)}, u32[]{:S(2)}, u32[]{:S(2)}) collective-permute-start(f32[4,24,256]{2,1,0:T(8,128)S(1)} %add_add_fusion), channel_id=1, source_target_pairs={{0,2},{1,3},{2,0},{3,1},{4,6},{5,7},{6,4},{7,5},{8,10},{9,11},{10,... | collective-permute-start | bytes 294920 | tf_op jit(solution)/shard_map/ppermute | solution.py:330
  119.9 2.7 %collective-permute-done.12 = f32[4,24,256]{2,1,0:T(8,128)S(1)} collective-permute-done((f32[4,24,256]{2,1,0:T(8,128)S(1)}, f32[4,24,256]{2,1,0:T(8,128)S(1)}, u32[]{:S(2)}, u32[]{:S(2)}) %collective-permute-start.12) | collective-permute-done | bytes 98336 | tf_op jit(solution)/shard_map/ppermute | solution.py:330
  122.5 3.6 %collective-permute-start.13 = (f32[4,24,256]{2,1,0:T(8,128)S(1)}, f32[4,24,256]{2,1,0:T(8,128)S(1)}, u32[]{:S(2)}, u32[]{:S(2)}) collective-permute-start(f32[4,24,256]{2,1,0:T(8,128)S(1)} %add.95), channel_id=1, source_target_pairs={{0,4},{1,5},{2,6},{3,7},{4,0},{5,1},{6,2},{7,3},{8,12},{9,13},{10,... | collective-permute-start | bytes 294920 | tf_op jit(solution)/shard_map/ppermute | solution.py:330
  126.1 3.6 %collective-permute-done.13 = f32[4,24,256]{2,1,0:T(8,128)S(1)} collective-permute-done((f32[4,24,256]{2,1,0:T(8,128)S(1)}, f32[4,24,256]{2,1,0:T(8,128)S(1)}, u32[]{:S(2)}, u32[]{:S(2)}) %collective-permute-start.13) | collective-permute-done | bytes 98336 | tf_op jit(solution)/shard_map/ppermute | solution.py:330
  129.8 0.1 collective-permute-start.14
  129.9 0.1 collective-permute-start.15
  130.0 2.8 %collective-permute-start.16 = (f32[4,24,256]{2,1,0:T(8,128)S(1)}, f32[4,24,256]{2,1,0:T(8,128)S(1)}, u32[]{:S(2)}, u32[]{:S(2)}) collective-permute-start(f32[4,24,256]{2,1,0:T(8,128)S(1)} %get-tuple-element.101), channel_id=1, source_target_pairs={{0,24},{8,0},{16,8},{24,16},{1,25},{9,1},{17,9},{25,17},{2,26},{10... | collective-permute-start | bytes 294920 | tf_op jit(solution)/shard_map/ppermute | solution.py:366
  132.8 2.7 %collective-permute-done.14 = f32[4,24,256]{2,1,0:T(8,128)S(1)} collective-permute-done((f32[4,24,256]{2,1,0:T(8,128)S(1)}, f32[4,24,256]{2,1,0:T(8,128)S(1)}, u32[]{:S(2)}, u32[]{:S(2)}) %collective-permute-start.14) | collective-permute-done | bytes 98336 | tf_op jit(solution)/shard_map/ppermute | solution.py:366
  135.5 0.1 collective-permute-done.15
  135.6 0.3 collective-permute-done.16
  136.0 0.1 collective-permute-start.17
  136.1 1.7 %collective-permute-done.17 = f32[16,24,256]{2,1,0:T(8,128)S(1)} collective-permute-done((f32[16,24,256]{2,1,0:T(8,128)S(1)}, f32[16,24,256]{2,1,0:T(8,128)S(1)}, u32[]{:S(2)}, u32[]{:S(2)}) %collective-permute-start.17) | collective-permute-done | bytes 393248 | tf_op jit(solution)/shard_map/ppermute | solution.py:314
  137.8 0.1 broadcast_select_fusion.3
  137.8 0.1 maximum_bitcast_fusion
  137.9 0.3 copy.25
  138.2 0.1 reshape.30
  138.3 0.7 slice.75
  139.0 0.2 copy-done.7
  (37 shorter events, 0.3 us)
Async XLA Ops:
  0.6 11.4 %copy-start.11 = (f32[24]{0:T(128)S(1)}, f32[24]{0:T(128)}, u32[]{:S(2)}) copy-start(f32[24]{0:T(128)} %constant.86) | copy-start | bytes 292
  0.6 13.2 %copy-start.9 = (pred[4,8]{1,0:T(4,128)(4,1)S(1)}, pred[4,8]{1,0:T(4,128)(4,1)}, u32[]{:S(2)}) copy-start(pred[4,8]{1,0:T(4,128)(4,1)} %constant.89) | copy-start | bytes 100
  0.7 13.2 %copy-start.10 = (pred[4,8]{1,0:T(4,128)(4,1)S(1)}, pred[4,8]{1,0:T(4,128)(4,1)}, u32[]{:S(2)}) copy-start(pred[4,8]{1,0:T(4,128)(4,1)} %constant.87) | copy-start | bytes 100
  0.7 10.5 %copy-start.8 = (f32[512,16]{0,1:T(8,128)S(1)}, f32[512,16]{0,1:T(8,128)}, u32[]{:S(2)}) copy-start(f32[512,16]{0,1:T(8,128)} %param.13) | copy-start | bytes 98308
  0.7 13.5 %copy-start = (bf16[1,128,8192]{2,1,0:T(8,128)(2,1)S(1)}, bf16[1,128,8192]{2,1,0:T(8,128)(2,1)}, u32[]{:S(2)}) copy-start(bf16[1,128,8192]{2,1,0:T(8,128)(2,1)} %param.16) | copy-start | bytes 6291460
  0.7 13.5 %copy-start.1 = (f32[3,7,8192]{2,1,0:T(8,128)S(1)}, f32[3,7,8192]{2,1,0:T(8,128)}, u32[]{:S(2)}) copy-start(f32[3,7,8192]{2,1,0:T(8,128)} %filt.3) | copy-start | bytes 2064388
  2.0 12.1 %collective-permute-start = (bf16[3,8,8192]{2,1,0:T(8,128)(2,1)S(1)}, bf16[3,8,8192]{2,1,0:T(8,128)(2,1)S(1)}, u32[]{:S(2)}, u32[]{:S(2)}) collective-permute-start(bf16[3,8,8192]{2,1,0:T(8,128)(2,1)S(1)} %get-tuple-element.103), channel_id=1, source_target_pairs={{1,2},{3,4},{5,6},{2,1},{4,3},{6,5},{9,10},{11,12},{13,14},{10,9},... | collective-permute-start | bytes 1179656 | tf_op jit(solution)/shard_map/ppermute | solution.py:411
  2.7 11.5 %collective-permute-start.1 = (bf16[3,8,8192]{2,1,0:T(8,128)(2,1)S(1)}, bf16[3,8,8192]{2,1,0:T(8,128)(2,1)S(1)}, u32[]{:S(2)}, u32[]{:S(2)}) collective-permute-start(bf16[3,8,8192]{2,1,0:T(8,128)(2,1)S(1)} %get-tuple-element.102), channel_id=1, source_target_pairs={{0,1},{1,0},{2,3},{3,2},{4,5},{5,4},{6,7},{7,6},{8,9},{9,8},{10,11... | collective-permute-start | bytes 1179656 | tf_op jit(solution)/shard_map/ppermute | solution.py:314
  14.2 22.2 %copy-start.2 = (bf16[3,8,8192]{2,1,0:T(8,128)(2,1)}, bf16[3,8,8192]{2,1,0:T(8,128)(2,1)S(1)}, u32[]{:S(2)}) copy-start(bf16[3,8,8192]{2,1,0:T(8,128)(2,1)S(1)} %collective-permute-done.1.hi) | copy-start | bytes 1179652
  14.2 30.6 %copy-start.6 = (f32[8192]{0:T(1024)S(1)}, f32[8192]{0:T(1024)}, u32[]{:S(2)}) copy-start(f32[8192]{0:T(1024)} %param.15) | copy-start | bytes 98308
  36.4 3.5 %collective-permute-start.2 = (f32[2,16,16,512]{3,2,1,0:T(8,128)}, f32[2,16,16,512]{3,2,1,0:T(8,128)}, u32[]{:S(2)}, u32[]{:S(2)}) collective-permute-start(f32[2,16,16,512]{3,2,1,0:T(8,128)} %get-tuple-element.53), channel_id=1, source_target_pairs={{0,1},{1,0},{2,3},{3,2},{4,5},{5,4},{6,7},{7,6},{8,9},{9,8},{10,11... | collective-permute-start | bytes 3145736 | tf_op jit(solution)/shard_map/ppermute | solution.py:314
  36.5 3.5 %collective-permute-start.3 = (bf16[8,8192]{1,0:T(8,128)(2,1)}, bf16[8,8192]{1,0:T(8,128)(2,1)S(1)}, u32[]{:S(2)}, u32[]{:S(2)}) collective-permute-start(bf16[8,8192]{1,0:T(8,128)(2,1)} %slice_bitcast_fusion.8), channel_id=1, source_target_pairs={{1,0},{2,1},{3,2},{4,3},{5,4},{6,5},{7,6},{9,8},{10,9},{11,10},{12... | collective-permute-start | bytes 393224 | tf_op jit(solution)/shard_map/ppermute | solution.py:309
  41.4 11.7 %collective-permute-start.4 = (f32[8,16,512]{2,1,0:T(8,128)S(1)}, f32[8,16,512]{2,1,0:T(8,128)S(1)}, u32[]{:S(2)}, u32[]{:S(2)}) collective-permute-start(f32[8,16,512]{2,1,0:T(8,128)S(1)} %broadcast_select_fusion.4), channel_id=1, source_target_pairs={{0,2},{1,3},{2,0},{3,1},{4,6},{5,7},{6,4},{7,5},{8,10},{9,11},{10,... | collective-permute-start | bytes 786440 | tf_op jit(solution)/shard_map/ppermute | solution.py:330
  53.2 6.6 %collective-permute-start.5 = (f32[8,16,512]{2,1,0:T(8,128)S(1)}, f32[8,16,512]{2,1,0:T(8,128)S(1)}, u32[]{:S(2)}, u32[]{:S(2)}) collective-permute-start(f32[8,16,512]{2,1,0:T(8,128)S(1)} %multiply_add_fusion.1), channel_id=1, source_target_pairs={{2,4},{3,5},{4,2},{5,3},{10,12},{11,13},{12,10},{13,11},{18,20},{1... | collective-permute-start | bytes 786440 | tf_op jit(solution)/shard_map/ppermute | solution.py:343
  59.8 15.3 %copy-start.3 = (bf16[3,8,8192]{2,1,0:T(8,128)(2,1)S(1)}, bf16[3,8,8192]{2,1,0:T(8,128)(2,1)}, u32[]{:S(2)}) copy-start(bf16[3,8,8192]{2,1,0:T(8,128)(2,1)} %copy-done.2) | copy-start | bytes 1179652
  59.8 15.3 %copy-start.4 = (f32[16,8,512]{2,1,0:T(8,128)S(1)}, f32[16,8,512]{2,1,0:T(8,128)}, u32[]{:S(2)}) copy-start(f32[16,8,512]{2,1,0:T(8,128)} %get-tuple-element.96.cy) | copy-start | bytes 786436
  59.8 15.3 %copy-start.5 = (f32[16,8,512]{2,1,0:T(8,128)S(1)}, f32[16,8,512]{2,1,0:T(8,128)}, u32[]{:S(2)}) copy-start(f32[16,8,512]{2,1,0:T(8,128)} %get-tuple-element.95.cz) | copy-start | bytes 786436
  59.8 13.1 %collective-permute-start.6 = (f32[8,16,512]{2,1,0:T(8,128)S(1)}, f32[8,16,512]{2,1,0:T(8,128)S(1)}, u32[]{:S(2)}, u32[]{:S(2)}) collective-permute-start(f32[8,16,512]{2,1,0:T(8,128)S(1)} %collective-permute-done.5), channel_id=1, source_target_pairs={{4,6},{5,7},{2,0},{3,1},{12,14},{13,15},{10,8},{11,9},{20,22},{21,... | collective-permute-start | bytes 786440 | tf_op jit(solution)/shard_map/ppermute | solution.py:346
  73.1 2.0 %collective-permute-start.7 = (f32[2,8,16,512]{3,2,1,0:T(8,128)S(1)}, f32[2,8,16,512]{3,2,1,0:T(8,128)S(1)}, u32[]{:S(2)}, u32[]{:S(2)}) collective-permute-start(f32[2,8,16,512]{3,2,1,0:T(8,128)S(1)} %pad_maximum_fusion.both), channel_id=1, source_target_pairs={{0,1},{1,0},{2,3},{3,2},{4,5},{5,4},{6,7},{7,6},{8,9},{9,8},{10,11... | collective-permute-start | bytes 1572872 | tf_op jit(solution)/shard_map/ppermute | solution.py:314
  106.7 1.8 %collective-permute-start.8 = (f32[16,24,256]{2,1,0:T(8,128)S(1)}, f32[16,24,256]{2,1,0:T(8,128)S(1)}, u32[]{:S(2)}, u32[]{:S(2)}) collective-permute-start(f32[16,24,256]{2,1,0:T(8,128)S(1)} %slice_select_fusion), channel_id=1, source_target_pairs={{0,1},{1,0},{2,3},{3,2},{4,5},{5,4},{6,7},{7,6},{8,9},{9,8},{10,11... | collective-permute-start | bytes 1179656 | tf_op jit(solution)/shard_map/ppermute | solution.py:314
  108.6 5.7 %collective-permute-start.11 = (f32[4,24,256]{2,1,0:T(8,128)S(1)}, f32[4,24,256]{2,1,0:T(8,128)S(1)}, u32[]{:S(2)}, u32[]{:S(2)}) collective-permute-start(f32[4,24,256]{2,1,0:T(8,128)S(1)} %get-tuple-element.115), channel_id=1, source_target_pairs={{0,24},{8,0},{16,8},{24,16},{1,25},{9,1},{17,9},{25,17},{2,26},{10... | collective-permute-start | bytes 294920 | tf_op jit(solution)/shard_map/ppermute | solution.py:366
  111.1 6.7 %collective-permute-start.10 = (f32[4,24,256]{2,1,0:T(8,128)S(1)}, f32[4,24,256]{2,1,0:T(8,128)S(1)}, u32[]{:S(2)}, u32[]{:S(2)}) collective-permute-start(f32[4,24,256]{2,1,0:T(8,128)S(1)} %get-tuple-element.116), channel_id=1, source_target_pairs={{0,16},{8,24},{16,0},{24,8},{1,17},{9,25},{17,1},{25,9},{2,18},{10... | collective-permute-start | bytes 294920 | tf_op jit(solution)/shard_map/ppermute | solution.py:366
  111.6 6.2 %collective-permute-start.9 = (f32[4,24,256]{2,1,0:T(8,128)S(1)}, f32[4,24,256]{2,1,0:T(8,128)S(1)}, u32[]{:S(2)}, u32[]{:S(2)}) collective-permute-start(f32[4,24,256]{2,1,0:T(8,128)S(1)} %get-tuple-element.114), channel_id=1, source_target_pairs={{0,8},{8,16},{16,24},{24,0},{1,9},{9,17},{17,25},{25,1},{2,10},{10... | collective-permute-start | bytes 294920 | tf_op jit(solution)/shard_map/ppermute | solution.py:366
  117.9 4.7 %collective-permute-start.12 = (f32[4,24,256]{2,1,0:T(8,128)S(1)}, f32[4,24,256]{2,1,0:T(8,128)S(1)}, u32[]{:S(2)}, u32[]{:S(2)}) collective-permute-start(f32[4,24,256]{2,1,0:T(8,128)S(1)} %add_add_fusion), channel_id=1, source_target_pairs={{0,2},{1,3},{2,0},{3,1},{4,6},{5,7},{6,4},{7,5},{8,10},{9,11},{10,... | collective-permute-start | bytes 294920 | tf_op jit(solution)/shard_map/ppermute | solution.py:330
  122.5 7.2 %collective-permute-start.13 = (f32[4,24,256]{2,1,0:T(8,128)S(1)}, f32[4,24,256]{2,1,0:T(8,128)S(1)}, u32[]{:S(2)}, u32[]{:S(2)}) collective-permute-start(f32[4,24,256]{2,1,0:T(8,128)S(1)} %add.95), channel_id=1, source_target_pairs={{0,4},{1,5},{2,6},{3,7},{4,0},{5,1},{6,2},{7,3},{8,12},{9,13},{10,... | collective-permute-start | bytes 294920 | tf_op jit(solution)/shard_map/ppermute | solution.py:330
  129.8 5.7 %collective-permute-start.14 = (f32[4,24,256]{2,1,0:T(8,128)S(1)}, f32[4,24,256]{2,1,0:T(8,128)S(1)}, u32[]{:S(2)}, u32[]{:S(2)}) collective-permute-start(f32[4,24,256]{2,1,0:T(8,128)S(1)} %get-tuple-element.101), channel_id=1, source_target_pairs={{0,8},{8,16},{16,24},{24,0},{1,9},{9,17},{17,25},{25,1},{2,10},{10... | collective-permute-start | bytes 294920 | tf_op jit(solution)/shard_map/ppermute | solution.py:366
  129.9 5.7 %collective-permute-start.15 = (f32[4,24,256]{2,1,0:T(8,128)S(1)}, f32[4,24,256]{2,1,0:T(8,128)S(1)}, u32[]{:S(2)}, u32[]{:S(2)}) collective-permute-start(f32[4,24,256]{2,1,0:T(8,128)S(1)} %get-tuple-element.101), channel_id=1, source_target_pairs={{0,16},{8,24},{16,0},{24,8},{1,17},{9,25},{17,1},{25,9},{2,18},{10... | collective-permute-start | bytes 294920 | tf_op jit(solution)/shard_map/ppermute | solution.py:366
  130.0 6.0 %collective-permute-start.16 = (f32[4,24,256]{2,1,0:T(8,128)S(1)}, f32[4,24,256]{2,1,0:T(8,128)S(1)}, u32[]{:S(2)}, u32[]{:S(2)}) collective-permute-start(f32[4,24,256]{2,1,0:T(8,128)S(1)} %get-tuple-element.101), channel_id=1, source_target_pairs={{0,24},{8,0},{16,8},{24,16},{1,25},{9,1},{17,9},{25,17},{2,26},{10... | collective-permute-start | bytes 294920 | tf_op jit(solution)/shard_map/ppermute | solution.py:366
  136.0 1.8 %collective-permute-start.17 = (f32[16,24,256]{2,1,0:T(8,128)S(1)}, f32[16,24,256]{2,1,0:T(8,128)S(1)}, u32[]{:S(2)}, u32[]{:S(2)}) collective-permute-start(f32[16,24,256]{2,1,0:T(8,128)S(1)} %constant_dynamic-update-slice_fusion), channel_id=1, source_target_pairs={{0,1},{1,0},{2,3},{3,2},{4,5},{5,4},{6,7},{7,6},{8,9},{9,8},{10,11... | collective-permute-start | bytes 1179656 | tf_op jit(solution)/shard_map/ppermute | solution.py:314
  138.3 0.9 copy-start.7

commit v14 on v13

--- a/solution.py
+++ b/solution.py
@@ -76,7 +76,8 @@
             xs[j, SUB : SUB + rows] = p[j, :, lanes].astype(F32)
             xs[j, SUB + rows :] = jnp.where(first, within, across)
         xs[3, SUB : SUB + rows] = u[:, lanes].astype(F32)
-        xs[3, SUB + rows :] = jnp.ones((SUB, LANES), F32)
+        across, within = hx[3, :, lanes].astype(F32), hi[3, :, lanes].astype(F32)
+        xs[3, SUB + rows :] = jnp.where(first, within, across)
 
         def mixed(j):
             even, odd, both = phases([spread(filt[j, i : i + 1, lanes]) for i in range(taps)])
@@ -126,7 +127,7 @@
 
 
 def blocks_kernel(
-    xg, blocks_e, blocks_a, hu, near, skip, join_e, join_a, conv, from_e, from_a, skip_sum, es
+    xg, blocks_e, blocks_a, near, skip, join_e, join_a, conv, from_e, from_a, skip_sum
 ):
     run = xg.shape[2] // SUB
     rows = xg.shape[2] - SUB
@@ -150,9 +151,6 @@
             )
         gated = x
         x = [xg[which, 1, SUB * a : SUB * a + SUB, part] for a in range(run)]
-        es[...] = hu[:, lanes].astype(F32)
-        for a in range(own, run):
-            x[a] = x[a] * jnp.where(inside, 1.0, spread(es[a - own : a - own + 1]))
         masked = [x[a] if a < own else jnp.where(inside, x[a], 0.0) for a in range(run)]
         skip_sum[which, :, part] = added([masked[a] * gated[a] for a in range(run)])
         past = [jnp.where(inside, 0.0, gain)] + [
@@ -179,7 +177,7 @@
 
 
 def final_kernel(
-    core, p, hx, hi, hu, u, qkv, conv, from_e, from_a, skip_sum, both, found, other, filt, f1, f_all, cz, cy,
+    core, p, hx, hi, u, qkv, conv, from_e, from_a, skip_sum, both, found, other, filt, f1, f_all, cz, cy,
     output, grad_p, sums, ps, us, gs, os, es,
 ):
     rows = p.shape[1]
@@ -210,7 +208,8 @@
             ps[j, SUB : SUB + rows] = p[j, :, lanes].astype(F32)
             ps[j, SUB + rows :] = jnp.where(first, within, across)
         us[0:rows] = u[:, lanes].astype(F32)
-        us[rows:] = hu[:, lanes].astype(F32)
+        across, within = hx[3, :, lanes].astype(F32), hi[3, :, lanes].astype(F32)
+        us[rows:] = jnp.where(first, within, across)
         decay = [spread(f1[n : n + 1, part]) for n in range(poles)]
 
         state = [
@@ -314,15 +313,15 @@
     return lax.ppermute(value, "ctx", [(s, s ^ 1) for s in range(count)])
 
 
-def joined(ends, hu, f_all):
+def joined(ends, f_all):
     core = lax.rem(lax.axis_index("ctx"), 2)
     half = ends.shape[1] // 2
-    other, hu = lax.optimization_barrier((swapped(ends), hu))
+    other = swapped(ends)
     first = core == 0
     mine = lax.dynamic_slice_in_dim(ends, core * half, half, 1)
     theirs = lax.dynamic_slice_in_dim(other, core * half, half, 1)
     one, two = jnp.where(first, mine, theirs), jnp.where(first, theirs, mine)
-    return other, hu, f_all * one[0] + two[0], one[1] + f_all * two[1]
+    return other, f_all * one[0] + two[0], one[1] + f_all * two[1]
 
 
 def paired(value, axis, step, lines=None):
@@ -403,7 +402,9 @@
     core = lax.rem(lax.axis_index("ctx"), 2)
 
     def edge(last):
-        return lax.dynamic_slice_in_dim(p, jnp.where(last, rows - SUB, 0), SUB, 1)
+        start = jnp.where(last, rows - SUB, 0)
+        cut = lambda value, axis: lax.dynamic_slice_in_dim(value, start, SUB, axis)
+        return jnp.concatenate([cut(p, 1), cut(u, 0)[None]], axis=0)
 
     devices = lax.axis_size("ctx")
     across = [(k, k + 1) for k in range(1, devices - 1, 2)]
@@ -447,9 +448,8 @@
     halved = pl.BlockSpec(
         (2, each, poles, groups), lambda w: (0, lax.rem(w, width // each // 2), 0, 0)
     )
-    early = (hx, near, join_e, join_a, cz, cy, f_all, u[:SUB])
-    hx, near, join_e, join_a, cz, cy, f_all, u_head = lax.optimization_barrier(early)
-    hu = shifted(u_head, "ctx", -1)
+    early = (hx, near, join_e, join_a, cz, cy, f_all)
+    hx, near, join_e, join_a, cz, cy, f_all = lax.optimization_barrier(early)
     state_shape = shape_of((width, poles, SUB, groups), F32)
     pair_shape = shape_of((width, 2, held, groups), F32)
 
@@ -462,7 +462,7 @@
         grid=(width // each,),
         in_specs=[
             pl.BlockSpec(memory_space=pltpu.SMEM),
-            by_w(3, rows), by_w(3, SUB), by_w(3, SUB), by_w(rows), by_w(3, taps),
+            by_w(3, rows), by_w(4, SUB), by_w(4, SUB), by_w(rows), by_w(3, taps),
             fixed(f1), fixed(we), fixed(wb),
         ],
         out_specs=[
@@ -491,8 +491,7 @@
                 blocks_kernel,
                 grid=(last - first,),
                 in_specs=[
-                    pairs, states, states,
-                    pl.BlockSpec((SUB, many * groups), lambda w: (0, w + first)), fixed(near),
+                    pairs, states, states, fixed(near),
                     pl.BlockSpec((1, many * groups), lambda w: (0, w + first)),
                     fixed(join_e), fixed(join_a),
                 ],
@@ -502,20 +501,19 @@
                     shape_of(((last - first) * many, SUB, groups), F32),
                 ],
                 input_output_aliases={0: 0, 1: 1, 2: 2},
-                scratch_shapes=[pltpu.VMEM((SUB, LANES), F32)],
                 compiler_params=params,
                 cost_estimate=pl.CostEstimate(
                     flops=60 * rows * channels, bytes_accessed=35 * 2**20, transcendentals=0
                 ),
                 name="blocks",
-            )(*held_before[:3], hu, close, skip_gain[None], join_e, join_a)
+            )(*held_before[:3], close, skip_gain[None], join_e, join_a)
             return [*out[:3], jnp.concatenate([*held_before[3:], out[3]], axis=0)]
 
         return call
 
     steps = width // many
     cuts = (0, (3 * steps) // 8, (5 * steps) // 8, steps)
-    other, hu, chip_e, chip_a = joined(ends, hu, f_all)
+    other, chip_e, chip_a = joined(ends, f_all)
     before, after, (conv, from_e, from_a, skip_sum) = scanned(
         chip_e, chip_a, f_all, [blocks(cuts[k], cuts[k + 1]) for k in range(3)]
     )
@@ -536,7 +534,7 @@
         grid=(width // each,),
         in_specs=[
             pl.BlockSpec(memory_space=pltpu.SMEM),
-            by_w(3, rows), by_w(3, SUB), by_w(3, SUB), by_w(SUB), by_w(rows),
+            by_w(3, rows), by_w(4, SUB), by_w(4, SUB), by_w(rows),
             by_block(3, held, groups), by_block(2, held, groups), state_spec, state_spec,
             by_block(SUB, groups), halved, halved, ends_spec,
             by_w(3, taps), fixed(f1), fixed(f_all), fixed(cz), fixed(cy),
@@ -554,7 +552,7 @@
         compiler_params=params,
         name="final",
     )(
-        core[None], p, hx, hi, hu, u, qkv, conv, from_e, from_a, skip_sum, both, found, other, short_filter,
+        core[None], p, hx, hi, u, qkv, conv, from_e, from_a, skip_sum, both, found, other, short_filter,
         f1, f_all, cz, cy,
     )
 

time: 141 us -> 139 us (0.986)
  starting transfers between devices: 24.5 us -> 28.2 us
  other arithmetic: 7.36 us -> 3.84 us
    ppermute x5, starting transfers between devices: 4.8 us -> 9.73 us  [swapped(): return lax.ppermute(value, 'ctx', [(s, s ^ 1) for s in range(count)])]
    ppermute x5, waiting for transfers between devices: 5.22 us -> 7.85 us  [swapped(): return lax.ppermute(value, 'ctx', [(s, s ^ 1) for s in range(count)])]
    ppermute x1 -> x0, waiting for transfers between devices: 2.12 us -> none  [shifted(): lax.ppermute(value, axis, [(source, source + steps) for source in range(f...]
    slice x1 -> x0, local copies, waits for them, and re-layouts: 1.57 us -> none  [local(): early = (hx, near, join_e, join_a, cz, cy, f_all, u[:SUB])]
  transfers between devices with their start and end apart: 18 -> 17, of which waited for: 12 -> 12; matrix products, arithmetic and copies ran while one was open for 5% -> 1% of each run, Pallas kernels for 16% -> 16%
where the time goes in v14:
time: 139 us; the launch traced here: 138 us
  Pallas kernels  75.9 us (55%)
  starting transfers between devices  28.2 us (20%)
  waiting for transfers between devices  25 us (18%)
  other arithmetic  3.84 us (3%)
  local copies, waits for them, and re-layouts  3.67 us (3%)
    pallas_call x1, Pallas kernels, local(): pl.pallas_call(final_kernel, grid=(width // each,), in_specs=[pl.BlockSpe...  31.5 us
    pallas_call x1, Pallas kernels, local(): pl.pallas_call(states_kernel, grid=(width // each,), in_specs=[pl.BlockSp...  22.3 us
    pallas_call x3, Pallas kernels, call(): pl.pallas_call(blocks_kernel, grid=(last - first,), in_specs=[pairs, stat...  22.1 us
    ppermute x5, starting transfers between devices, swapped(): return lax.ppermute(value, 'ctx', [(s, s ^ 1) for s in range(count)])  9.73 us
    ppermute x3, starting transfers between devices, paired(): lax.ppermute(value, axis, [(source, source ^ step) for source in lines or...  8.72 us
    ppermute x6, waiting for transfers between devices, rotated(): lax.ppermute(value, axis, [(s, (s + steps) % count) for s in range(count)])  8.53 us
    ppermute x5, waiting for transfers between devices, swapped(): return lax.ppermute(value, 'ctx', [(s, s ^ 1) for s in range(count)])  7.85 us
    ppermute x6, starting transfers between devices, rotated(): lax.ppermute(value, axis, [(s, (s + steps) % count) for s in range(count)])  6.79 us
  transfers between devices with their start and end apart: 17, of which 12 were waited for; matrix products, arithmetic and copies ran while one was open for 1% of the time, Pallas kernels for 16%

profile of v14, /device:TPU:0, one launch (start us, length us, event | category | flops | bytes accessed | tf_op | source)
XLA Modules:
  0.0 137.7 jit_solution(4831788149355681093)
XLA Ops:
  0.6 0.0 copy-start.11
  0.6 0.0 copy-start.10
  0.7 0.0 copy-start.14
  0.7 1.0 constant_dynamic-slice_fusion.3
  1.7 0.0 copy-start.12
  1.7 0.0 copy-start.13
  1.7 1.2 dynamic-slice_bitcast_fusion
  2.9 0.0 copy-start
  2.9 0.0 copy-start.1
  3.0 0.8 collective-permute-start
  3.9 4.5 %collective-permute-start.1 = (bf16[4,8,8192]{2,1,0:T(8,128)(2,1)S(1)}, bf16[4,8,8192]{2,1,0:T(8,128)(2,1)S(1)}, u32[]{:S(2)}, u32[]{:S(2)}) collective-permute-start(bf16[4,8,8192]{2,1,0:T(8,128)(2,1)S(1)} %pad_maximum_fusion.1), channel_id=1, source_target_pairs={{0,1},{1,0},{2,3},{3,2},{4,5},{5,4},{6,7},{7,6},{8,9},{9,8},{10,11... | collective-permute-start | bytes 1572872 | tf_op jit(solution)/shard_map/ppermute | solution.py:313
  8.5 0.1 multiply_exponential_fusion.1
  8.6 0.2 multiply_exponential_fusion
  8.9 0.2 multiply_reduce_fusion.near
  9.1 0.8 fusion.4
  10.0 0.3 broadcast_select_fusion
  10.3 0.0 copy-start.2
  10.4 0.0 copy-start.6
  10.4 22.3 %states.1 = (f32[16,3,136,512]{3,2,1,0:T(8,128)}, f32[16,2,136,512]{3,2,1,0:T(8,128)}, f32[16,16,8,512]{3,2,1,0:T(8,128)}, f32[16,16,8,512]{3,2,1,0:T(8,128)}, f32[2,16,16,512]{3,2,1,0:T(8,128)}) custom-call(s32[1]{0:T(128)} %bitcast.core, bf16[3,128,8192]{2,1,0:T(8,128)(2,1)} %bitcast.89, bf16[4,8,8192]{2,1,0:T(8,128)(2,1)S(1)} %collective-permute-done.hx, ...), custom_call_target="tpu_custom_call" | custom-call | tf_op jit(solution)/shard_map/states/pallas_call | solution.py:460
  32.6 4.9 %collective-permute-start.2 = (f32[2,16,16,512]{3,2,1,0:T(8,128)}, f32[2,16,16,512]{3,2,1,0:T(8,128)}, u32[]{:S(2)}, u32[]{:S(2)}) collective-permute-start(f32[2,16,16,512]{3,2,1,0:T(8,128)} %get-tuple-element.52), channel_id=1, source_target_pairs={{0,1},{1,0},{2,3},{3,2},{4,5},{5,4},{6,7},{7,6},{8,9},{9,8},{10,11... | collective-permute-start | bytes 3145736 | tf_op jit(solution)/shard_map/ppermute | solution.py:313
  37.5 2.6 %collective-permute-done.2.other = f32[2,16,16,512]{3,2,1,0:T(8,128)} collective-permute-done((f32[2,16,16,512]{3,2,1,0:T(8,128)}, f32[2,16,16,512]{3,2,1,0:T(8,128)}, u32[]{:S(2)}, u32[]{:S(2)}) %collective-permute-start.2) | collective-permute-done | bytes 1048608 | tf_op jit(solution)/shard_map/ppermute | solution.py:313
  40.1 1.3 dynamic-slice_select_fusion.1
  41.5 0.1 broadcast_select_fusion.4
  41.6 2.1 %collective-permute-start.3 = (f32[8,16,512]{2,1,0:T(8,128)S(1)}, f32[8,16,512]{2,1,0:T(8,128)S(1)}, u32[]{:S(2)}, u32[]{:S(2)}) collective-permute-start(f32[8,16,512]{2,1,0:T(8,128)S(1)} %broadcast_select_fusion.4), channel_id=1, source_target_pairs={{0,2},{1,3},{2,0},{3,1},{4,6},{5,7},{6,4},{7,5},{8,10},{9,11},{10,... | collective-permute-start | bytes 786440 | tf_op jit(solution)/shard_map/ppermute | solution.py:329
  43.7 8.2 %blocks.3 = (f32[16,2,136,512]{3,2,1,0:T(8,128)}, f32[16,16,8,512]{3,2,1,0:T(8,128)}, f32[16,16,8,512]{3,2,1,0:T(8,128)}, f32[6,8,512]{2,1,0:T(8,128)S(1)}) custom-call(f32[16,2,136,512]{3,2,1,0:T(8,128)} %get-tuple-element.53.xg, f32[16,16,8,512]{3,2,1,0:T(8,128)} %get-tuple-element.54.blocks_e, ...), custom_call_target="tpu_custom_call", output_to_operand_aliasing={{0}: (0, {}), {1}: (1, {}), {2}: (2, {})} | custom-call | flops 62914560 | bytes 36700160 | tf_op jit(solution)/shard_map/blocks/pallas_call | solution.py:490
  51.8 0.1 multiply_add_fusion.1
  52.0 0.7 collective-permute-start.4
  52.7 5.8 %blocks.4 = (f32[16,2,136,512]{3,2,1,0:T(8,128)}, f32[16,16,8,512]{3,2,1,0:T(8,128)}, f32[16,16,8,512]{3,2,1,0:T(8,128)}, f32[4,8,512]{2,1,0:T(8,128)S(1)}) custom-call(f32[16,2,136,512]{3,2,1,0:T(8,128)} %get-tuple-element.65.xg, f32[16,16,8,512]{3,2,1,0:T(8,128)} %get-tuple-element.66.blocks_e, ...), custom_call_target="tpu_custom_call", output_to_operand_aliasing={{0}: (0, {}), {1}: (1, {}), {2}: (2, {})} | custom-call | flops 62914560 | bytes 36700160 | tf_op jit(solution)/shard_map/blocks/pallas_call | solution.py:490
  58.5 0.0 copy-start.3
  58.5 0.0 copy-start.4
  58.6 1.4 %collective-permute-start.5 = (f32[8,16,512]{2,1,0:T(8,128)S(1)}, f32[8,16,512]{2,1,0:T(8,128)S(1)}, u32[]{:S(2)}, u32[]{:S(2)}) collective-permute-start(f32[8,16,512]{2,1,0:T(8,128)S(1)} %collective-permute-done.4), channel_id=1, source_target_pairs={{4,6},{5,7},{2,0},{3,1},{12,14},{13,15},{10,8},{11,9},{20,22},{21,... | collective-permute-start | bytes 786440 | tf_op jit(solution)/shard_map/ppermute | solution.py:345
  60.0 8.1 %blocks.5 = (f32[16,2,136,512]{3,2,1,0:T(8,128)}, f32[16,16,8,512]{3,2,1,0:T(8,128)}, f32[16,16,8,512]{3,2,1,0:T(8,128)}, f32[6,8,512]{2,1,0:T(8,128)S(1)}) custom-call(f32[16,2,136,512]{3,2,1,0:T(8,128)} %get-tuple-element.75.xg, f32[16,16,8,512]{3,2,1,0:T(8,128)} %get-tuple-element.76.blocks_e, ...), custom_call_target="tpu_custom_call", output_to_operand_aliasing={{0}: (0, {}), {1}: (1, {}), {2}: (2, {})} | custom-call | flops 62914560 | bytes 36700160 | tf_op jit(solution)/shard_map/blocks/pallas_call | solution.py:490
  68.1 2.4 %collective-permute-done.5 = f32[8,16,512]{2,1,0:T(8,128)S(1)} collective-permute-done((f32[8,16,512]{2,1,0:T(8,128)S(1)}, f32[8,16,512]{2,1,0:T(8,128)S(1)}, u32[]{:S(2)}, u32[]{:S(2)}) %collective-permute-start.5) | collective-permute-done | bytes 262176 | tf_op jit(solution)/shard_map/ppermute | solution.py:345
  70.6 0.1 select_bitcast_fusion.1
  70.7 0.1 collective-permute-start.6
  70.8 1.9 %collective-permute-done.6.found = f32[2,8,16,512]{3,2,1,0:T(8,128)S(1)} collective-permute-done((f32[2,8,16,512]{3,2,1,0:T(8,128)S(1)}, f32[2,8,16,512]{3,2,1,0:T(8,128)S(1)}, u32[]{:S(2)}, u32[]{:S(2)}) %collective-permute-start.6) | collective-permute-done | bytes 524320 | tf_op jit(solution)/shard_map/ppermute | solution.py:313
  72.7 31.5 %final.1 = (bf16[128,8192]{1,0:T(8,128)(2,1)}, bf16[3,128,8192]{2,1,0:T(8,128)(2,1)}, f32[32,24,256]{2,1,0:T(8,128)S(1)}) custom-call(s32[1]{0:T(128)} %bitcast.core, bf16[3,128,8192]{2,1,0:T(8,128)(2,1)} %bitcast.90, bf16[4,8,8192]{2,1,0:T(8,128)(2,1)S(1)} %collective-permute-done.hx, bf16[4,8,8192]{2,1,0:T(8,128)(2,1)S(1)} %copy-done.3, ...), custom_call_target="tpu_custom_call" | custom-call | tf_op jit(solution)/shard_map/final/pallas_call | solution.py:532
  104.2 0.1 slice_select_fusion
  104.2 0.2 collective-permute-start.7
  104.4 1.6 %collective-permute-done.7 = f32[16,24,256]{2,1,0:T(8,128)S(1)} collective-permute-done((f32[16,24,256]{2,1,0:T(8,128)S(1)}, f32[16,24,256]{2,1,0:T(8,128)S(1)}, u32[]{:S(2)}, u32[]{:S(2)}) %collective-permute-start.7) | collective-permute-done | bytes 393248 | tf_op jit(solution)/shard_map/ppermute | solution.py:313
  106.0 0.1 select_add_fusion
  106.1 2.5 %collective-permute-start.10 = (f32[4,24,256]{2,1,0:T(8,128)S(1)}, f32[4,24,256]{2,1,0:T(8,128)S(1)}, u32[]{:S(2)}, u32[]{:S(2)}) collective-permute-start(f32[4,24,256]{2,1,0:T(8,128)S(1)} %get-tuple-element.111), channel_id=1, source_target_pairs={{0,24},{8,0},{16,8},{24,16},{1,25},{9,1},{17,9},{25,17},{2,26},{10... | collective-permute-start | bytes 294920 | tf_op jit(solution)/shard_map/ppermute | solution.py:365
  108.6 0.5 collective-permute-start.9
  109.1 0.6 collective-permute-start.8
  109.7 2.1 %collective-permute-done.10 = f32[4,24,256]{2,1,0:T(8,128)S(1)} collective-permute-done((f32[4,24,256]{2,1,0:T(8,128)S(1)}, f32[4,24,256]{2,1,0:T(8,128)S(1)}, u32[]{:S(2)}, u32[]{:S(2)}) %collective-permute-start.10) | collective-permute-done | bytes 98336 | tf_op jit(solution)/shard_map/ppermute | solution.py:365
  111.8 3.5 %collective-permute-done.9 = f32[4,24,256]{2,1,0:T(8,128)S(1)} collective-permute-done((f32[4,24,256]{2,1,0:T(8,128)S(1)}, f32[4,24,256]{2,1,0:T(8,128)S(1)}, u32[]{:S(2)}, u32[]{:S(2)}) %collective-permute-start.9) | collective-permute-done | bytes 98336 | tf_op jit(solution)/shard_map/ppermute | solution.py:365
  115.4 2.5 %collective-permute-start.11 = (f32[4,24,256]{2,1,0:T(8,128)S(1)}, f32[4,24,256]{2,1,0:T(8,128)S(1)}, u32[]{:S(2)}, u32[]{:S(2)}) collective-permute-start(f32[4,24,256]{2,1,0:T(8,128)S(1)} %add_add_fusion), channel_id=1, source_target_pairs={{0,2},{1,3},{2,0},{3,1},{4,6},{5,7},{6,4},{7,5},{8,10},{9,11},{10,... | collective-permute-start | bytes 294920 | tf_op jit(solution)/shard_map/ppermute | solution.py:329
  117.9 2.6 %collective-permute-done.11 = f32[4,24,256]{2,1,0:T(8,128)S(1)} collective-permute-done((f32[4,24,256]{2,1,0:T(8,128)S(1)}, f32[4,24,256]{2,1,0:T(8,128)S(1)}, u32[]{:S(2)}, u32[]{:S(2)}) %collective-permute-start.11) | collective-permute-done | bytes 98336 | tf_op jit(solution)/shard_map/ppermute | solution.py:329
  120.5 4.2 %collective-permute-start.12 = (f32[4,24,256]{2,1,0:T(8,128)S(1)}, f32[4,24,256]{2,1,0:T(8,128)S(1)}, u32[]{:S(2)}, u32[]{:S(2)}) collective-permute-start(f32[4,24,256]{2,1,0:T(8,128)S(1)} %add.97), channel_id=1, source_target_pairs={{0,4},{1,5},{2,6},{3,7},{4,0},{5,1},{6,2},{7,3},{8,12},{9,13},{10,... | collective-permute-start | bytes 294920 | tf_op jit(solution)/shard_map/ppermute | solution.py:329
  124.6 3.6 %collective-permute-done.12 = f32[4,24,256]{2,1,0:T(8,128)S(1)} collective-permute-done((f32[4,24,256]{2,1,0:T(8,128)S(1)}, f32[4,24,256]{2,1,0:T(8,128)S(1)}, u32[]{:S(2)}, u32[]{:S(2)}) %collective-permute-start.12) | collective-permute-done | bytes 98336 | tf_op jit(solution)/shard_map/ppermute | solution.py:329
  128.3 0.1 collective-permute-start.13
  128.4 0.3 collective-permute-start.14
  128.7 2.8 %collective-permute-start.15 = (f32[4,24,256]{2,1,0:T(8,128)S(1)}, f32[4,24,256]{2,1,0:T(8,128)S(1)}, u32[]{:S(2)}, u32[]{:S(2)}) collective-permute-start(f32[4,24,256]{2,1,0:T(8,128)S(1)} %get-tuple-element.95), channel_id=1, source_target_pairs={{0,24},{8,0},{16,8},{24,16},{1,25},{9,1},{17,9},{25,17},{2,26},{10... | collective-permute-start | bytes 294920 | tf_op jit(solution)/shard_map/ppermute | solution.py:365
  131.6 2.5 %collective-permute-done.13 = f32[4,24,256]{2,1,0:T(8,128)S(1)} collective-permute-done((f32[4,24,256]{2,1,0:T(8,128)S(1)}, f32[4,24,256]{2,1,0:T(8,128)S(1)}, u32[]{:S(2)}, u32[]{:S(2)}) %collective-permute-start.13) | collective-permute-done | bytes 98336 | tf_op jit(solution)/shard_map/ppermute | solution.py:365
  134.0 0.1 collective-permute-done.14
  134.2 0.3 collective-permute-done.15
  134.5 0.1 collective-permute-start.16
  134.6 1.7 %collective-permute-done.16 = f32[16,24,256]{2,1,0:T(8,128)S(1)} collective-permute-done((f32[16,24,256]{2,1,0:T(8,128)S(1)}, f32[16,24,256]{2,1,0:T(8,128)S(1)}, u32[]{:S(2)}, u32[]{:S(2)}) %collective-permute-start.16) | collective-permute-done | bytes 393248 | tf_op jit(solution)/shard_map/ppermute | solution.py:313
  136.3 0.1 broadcast_select_fusion.3
  136.3 0.1 maximum_bitcast_fusion
  136.4 0.3 copy.25
  136.7 0.1 reshape.33
  136.8 0.7 slice.67
  137.6 0.2 copy-done.7
  (43 shorter events, 0.5 us)
Async XLA Ops:
  0.6 7.8 %copy-start.11 = (f32[4]{0:T(128)S(1)}, f32[4]{0:T(128)}, u32[]{:S(2)}) copy-start(f32[4]{0:T(128)} %constant.90) | copy-start | bytes 52
  0.6 8.0 %copy-start.10 = (f32[4,8]{1,0:T(4,128)S(1)}, f32[4,8]{1,0:T(4,128)}, u32[]{:S(2)}) copy-start(f32[4,8]{1,0:T(4,128)} %constant.92) | copy-start | bytes 388
  0.7 8.2 %copy-start.14 = (f32[24]{0:T(128)S(1)}, f32[24]{0:T(128)}, u32[]{:S(2)}) copy-start(f32[24]{0:T(128)} %constant.88) | copy-start | bytes 292
  0.7 7.8 %copy-start.9 = (f32[512,16]{0,1:T(8,128)S(1)}, f32[512,16]{0,1:T(8,128)}, u32[]{:S(2)}) copy-start(f32[512,16]{0,1:T(8,128)} %param.14) | copy-start | bytes 98308
  0.7 7.9 %copy-start.8 = (f32[512,16]{0,1:T(8,128)S(1)}, f32[512,16]{0,1:T(8,128)}, u32[]{:S(2)}) copy-start(f32[512,16]{0,1:T(8,128)} %param.13) | copy-start | bytes 98308
  1.7 8.3 %copy-start.12 = (pred[4,8]{1,0:T(4,128)(4,1)S(1)}, pred[4,8]{1,0:T(4,128)(4,1)}, u32[]{:S(2)}) copy-start(pred[4,8]{1,0:T(4,128)(4,1)} %constant.91) | copy-start | bytes 100
  1.7 8.3 %copy-start.13 = (pred[4,8]{1,0:T(4,128)(4,1)S(1)}, pred[4,8]{1,0:T(4,128)(4,1)}, u32[]{:S(2)}) copy-start(pred[4,8]{1,0:T(4,128)(4,1)} %constant.89) | copy-start | bytes 100
  2.9 7.4 %copy-start = (bf16[1,128,8192]{2,1,0:T(8,128)(2,1)S(1)}, bf16[1,128,8192]{2,1,0:T(8,128)(2,1)}, u32[]{:S(2)}) copy-start(bf16[1,128,8192]{2,1,0:T(8,128)(2,1)} %param.16) | copy-start | bytes 6291460
  2.9 7.4 %copy-start.1 = (f32[3,7,8192]{2,1,0:T(8,128)S(1)}, f32[3,7,8192]{2,1,0:T(8,128)}, u32[]{:S(2)}) copy-start(f32[3,7,8192]{2,1,0:T(8,128)} %filt.3) | copy-start | bytes 2064388
  3.0 7.3 %collective-permute-start = (bf16[4,8,8192]{2,1,0:T(8,128)(2,1)S(1)}, bf16[4,8,8192]{2,1,0:T(8,128)(2,1)S(1)}, u32[]{:S(2)}, u32[]{:S(2)}) collective-permute-start(bf16[4,8,8192]{2,1,0:T(8,128)(2,1)S(1)} %pad_maximum_fusion), channel_id=1, source_target_pairs={{1,2},{3,4},{5,6},{2,1},{4,3},{6,5},{9,10},{11,12},{13,14},{10,9},... | collective-permute-start | bytes 1572872 | tf_op jit(solution)/shard_map/ppermute | solution.py:412
  3.9 6.5 %collective-permute-start.1 = (bf16[4,8,8192]{2,1,0:T(8,128)(2,1)S(1)}, bf16[4,8,8192]{2,1,0:T(8,128)(2,1)S(1)}, u32[]{:S(2)}, u32[]{:S(2)}) collective-permute-start(bf16[4,8,8192]{2,1,0:T(8,128)(2,1)S(1)} %pad_maximum_fusion.1), channel_id=1, source_target_pairs={{0,1},{1,0},{2,3},{3,2},{4,5},{5,4},{6,7},{7,6},{8,9},{9,8},{10,11... | collective-permute-start | bytes 1572872 | tf_op jit(solution)/shard_map/ppermute | solution.py:313
  10.3 22.3 %copy-start.2 = (bf16[4,8,8192]{2,1,0:T(8,128)(2,1)}, bf16[4,8,8192]{2,1,0:T(8,128)(2,1)S(1)}, u32[]{:S(2)}) copy-start(bf16[4,8,8192]{2,1,0:T(8,128)(2,1)S(1)} %collective-permute-done.1.hi) | copy-start | bytes 1572868
  10.4 33.3 %copy-start.6 = (f32[8192]{0:T(1024)S(1)}, f32[8192]{0:T(1024)}, u32[]{:S(2)}) copy-start(f32[8192]{0:T(1024)} %param.15) | copy-start | bytes 98308
  32.6 7.5 %collective-permute-start.2 = (f32[2,16,16,512]{3,2,1,0:T(8,128)}, f32[2,16,16,512]{3,2,1,0:T(8,128)}, u32[]{:S(2)}, u32[]{:S(2)}) collective-permute-start(f32[2,16,16,512]{3,2,1,0:T(8,128)} %get-tuple-element.52), channel_id=1, source_target_pairs={{0,1},{1,0},{2,3},{3,2},{4,5},{5,4},{6,7},{7,6},{8,9},{9,8},{10,11... | collective-permute-start | bytes 3145736 | tf_op jit(solution)/shard_map/ppermute | solution.py:313
  41.6 10.3 %collective-permute-start.3 = (f32[8,16,512]{2,1,0:T(8,128)S(1)}, f32[8,16,512]{2,1,0:T(8,128)S(1)}, u32[]{:S(2)}, u32[]{:S(2)}) collective-permute-start(f32[8,16,512]{2,1,0:T(8,128)S(1)} %broadcast_select_fusion.4), channel_id=1, source_target_pairs={{0,2},{1,3},{2,0},{3,1},{4,6},{5,7},{6,4},{7,5},{8,10},{9,11},{10,... | collective-permute-start | bytes 786440 | tf_op jit(solution)/shard_map/ppermute | solution.py:329
  52.0 6.5 %collective-permute-start.4 = (f32[8,16,512]{2,1,0:T(8,128)S(1)}, f32[8,16,512]{2,1,0:T(8,128)S(1)}, u32[]{:S(2)}, u32[]{:S(2)}) collective-permute-start(f32[8,16,512]{2,1,0:T(8,128)S(1)} %multiply_add_fusion.1), channel_id=1, source_target_pairs={{2,4},{3,5},{4,2},{5,3},{10,12},{11,13},{12,10},{13,11},{18,20},{1... | collective-permute-start | bytes 786440 | tf_op jit(solution)/shard_map/ppermute | solution.py:342
  58.5 14.1 %copy-start.3 = (bf16[4,8,8192]{2,1,0:T(8,128)(2,1)S(1)}, bf16[4,8,8192]{2,1,0:T(8,128)(2,1)}, u32[]{:S(2)}) copy-start(bf16[4,8,8192]{2,1,0:T(8,128)(2,1)} %copy-done.2) | copy-start | bytes 1572868
  58.5 14.1 %copy-start.4 = (f32[16,8,512]{2,1,0:T(8,128)S(1)}, f32[16,8,512]{2,1,0:T(8,128)}, u32[]{:S(2)}) copy-start(f32[16,8,512]{2,1,0:T(8,128)} %get-tuple-element.90.cy) | copy-start | bytes 786436
  58.5 14.1 %copy-start.5 = (f32[16,8,512]{2,1,0:T(8,128)S(1)}, f32[16,8,512]{2,1,0:T(8,128)}, u32[]{:S(2)}) copy-start(f32[16,8,512]{2,1,0:T(8,128)} %get-tuple-element.89.cz) | copy-start | bytes 786436
  58.6 12.0 %collective-permute-start.5 = (f32[8,16,512]{2,1,0:T(8,128)S(1)}, f32[8,16,512]{2,1,0:T(8,128)S(1)}, u32[]{:S(2)}, u32[]{:S(2)}) collective-permute-start(f32[8,16,512]{2,1,0:T(8,128)S(1)} %collective-permute-done.4), channel_id=1, source_target_pairs={{4,6},{5,7},{2,0},{3,1},{12,14},{13,15},{10,8},{11,9},{20,22},{21,... | collective-permute-start | bytes 786440 | tf_op jit(solution)/shard_map/ppermute | solution.py:345
  70.7 2.0 %collective-permute-start.6 = (f32[2,8,16,512]{3,2,1,0:T(8,128)S(1)}, f32[2,8,16,512]{3,2,1,0:T(8,128)S(1)}, u32[]{:S(2)}, u32[]{:S(2)}) collective-permute-start(f32[2,8,16,512]{3,2,1,0:T(8,128)S(1)} %pad_maximum_fusion.2.both), channel_id=1, source_target_pairs={{0,1},{1,0},{2,3},{3,2},{4,5},{5,4},{6,7},{7,6},{8,9},{9,8},{10,11... | collective-permute-start | bytes 1572872 | tf_op jit(solution)/shard_map/ppermute | solution.py:313
  104.2 1.8 %collective-permute-start.7 = (f32[16,24,256]{2,1,0:T(8,128)S(1)}, f32[16,24,256]{2,1,0:T(8,128)S(1)}, u32[]{:S(2)}, u32[]{:S(2)}) collective-permute-start(f32[16,24,256]{2,1,0:T(8,128)S(1)} %slice_select_fusion), channel_id=1, source_target_pairs={{0,1},{1,0},{2,3},{3,2},{4,5},{5,4},{6,7},{7,6},{8,9},{9,8},{10,11... | collective-permute-start | bytes 1179656 | tf_op jit(solution)/shard_map/ppermute | solution.py:313
  106.1 5.7 %collective-permute-start.10 = (f32[4,24,256]{2,1,0:T(8,128)S(1)}, f32[4,24,256]{2,1,0:T(8,128)S(1)}, u32[]{:S(2)}, u32[]{:S(2)}) collective-permute-start(f32[4,24,256]{2,1,0:T(8,128)S(1)} %get-tuple-element.111), channel_id=1, source_target_pairs={{0,24},{8,0},{16,8},{24,16},{1,25},{9,1},{17,9},{25,17},{2,26},{10... | collective-permute-start | bytes 294920 | tf_op jit(solution)/shard_map/ppermute | solution.py:365
  108.6 6.7 %collective-permute-start.9 = (f32[4,24,256]{2,1,0:T(8,128)S(1)}, f32[4,24,256]{2,1,0:T(8,128)S(1)}, u32[]{:S(2)}, u32[]{:S(2)}) collective-permute-start(f32[4,24,256]{2,1,0:T(8,128)S(1)} %get-tuple-element.112), channel_id=1, source_target_pairs={{0,16},{8,24},{16,0},{24,8},{1,17},{9,25},{17,1},{25,9},{2,18},{10... | collective-permute-start | bytes 294920 | tf_op jit(solution)/shard_map/ppermute | solution.py:365
  109.1 6.2 %collective-permute-start.8 = (f32[4,24,256]{2,1,0:T(8,128)S(1)}, f32[4,24,256]{2,1,0:T(8,128)S(1)}, u32[]{:S(2)}, u32[]{:S(2)}) collective-permute-start(f32[4,24,256]{2,1,0:T(8,128)S(1)} %get-tuple-element.110), channel_id=1, source_target_pairs={{0,8},{8,16},{16,24},{24,0},{1,9},{9,17},{17,25},{25,1},{2,10},{10... | collective-permute-start | bytes 294920 | tf_op jit(solution)/shard_map/ppermute | solution.py:365
  115.4 5.1 %collective-permute-start.11 = (f32[4,24,256]{2,1,0:T(8,128)S(1)}, f32[4,24,256]{2,1,0:T(8,128)S(1)}, u32[]{:S(2)}, u32[]{:S(2)}) collective-permute-start(f32[4,24,256]{2,1,0:T(8,128)S(1)} %add_add_fusion), channel_id=1, source_target_pairs={{0,2},{1,3},{2,0},{3,1},{4,6},{5,7},{6,4},{7,5},{8,10},{9,11},{10,... | collective-permute-start | bytes 294920 | tf_op jit(solution)/shard_map/ppermute | solution.py:329
  120.5 7.8 %collective-permute-start.12 = (f32[4,24,256]{2,1,0:T(8,128)S(1)}, f32[4,24,256]{2,1,0:T(8,128)S(1)}, u32[]{:S(2)}, u32[]{:S(2)}) collective-permute-start(f32[4,24,256]{2,1,0:T(8,128)S(1)} %add.97), channel_id=1, source_target_pairs={{0,4},{1,5},{2,6},{3,7},{4,0},{5,1},{6,2},{7,3},{8,12},{9,13},{10,... | collective-permute-start | bytes 294920 | tf_op jit(solution)/shard_map/ppermute | solution.py:329
  128.3 5.7 %collective-permute-start.13 = (f32[4,24,256]{2,1,0:T(8,128)S(1)}, f32[4,24,256]{2,1,0:T(8,128)S(1)}, u32[]{:S(2)}, u32[]{:S(2)}) collective-permute-start(f32[4,24,256]{2,1,0:T(8,128)S(1)} %get-tuple-element.95), channel_id=1, source_target_pairs={{0,8},{8,16},{16,24},{24,0},{1,9},{9,17},{17,25},{25,1},{2,10},{10... | collective-permute-start | bytes 294920 | tf_op jit(solution)/shard_map/ppermute | solution.py:365
  128.4 5.7 %collective-permute-start.14 = (f32[4,24,256]{2,1,0:T(8,128)S(1)}, f32[4,24,256]{2,1,0:T(8,128)S(1)}, u32[]{:S(2)}, u32[]{:S(2)}) collective-permute-start(f32[4,24,256]{2,1,0:T(8,128)S(1)} %get-tuple-element.95), channel_id=1, source_target_pairs={{0,16},{8,24},{16,0},{24,8},{1,17},{9,25},{17,1},{25,9},{2,18},{10... | collective-permute-start | bytes 294920 | tf_op jit(solution)/shard_map/ppermute | solution.py:365
  128.7 5.8 %collective-permute-start.15 = (f32[4,24,256]{2,1,0:T(8,128)S(1)}, f32[4,24,256]{2,1,0:T(8,128)S(1)}, u32[]{:S(2)}, u32[]{:S(2)}) collective-permute-start(f32[4,24,256]{2,1,0:T(8,128)S(1)} %get-tuple-element.95), channel_id=1, source_target_pairs={{0,24},{8,0},{16,8},{24,16},{1,25},{9,1},{17,9},{25,17},{2,26},{10... | collective-permute-start | bytes 294920 | tf_op jit(solution)/shard_map/ppermute | solution.py:365
  134.5 1.8 %collective-permute-start.16 = (f32[16,24,256]{2,1,0:T(8,128)S(1)}, f32[16,24,256]{2,1,0:T(8,128)S(1)}, u32[]{:S(2)}, u32[]{:S(2)}) collective-permute-start(f32[16,24,256]{2,1,0:T(8,128)S(1)} %constant_dynamic-update-slice_fusion), channel_id=1, source_target_pairs={{0,1},{1,0},{2,3},{3,2},{4,5},{5,4},{6,7},{7,6},{8,9},{9,8},{10,11... | collective-permute-start | bytes 1179656 | tf_op jit(solution)/shard_map/ppermute | solution.py:313
  136.8 0.9 copy-start.7

commit v15 on v14

--- a/solution.py
+++ b/solution.py
@@ -360,11 +360,6 @@
     return before, after, kept
 
 
-def rotated(value, axis, steps):
-    count = lax.axis_size(axis)
-    return lax.ppermute(value, axis, [(s, (s + steps) % count) for s in range(count)])
-
-
 def summed(value):
     dp, parts = lax.axis_index("dp"), lax.axis_size("dp")
     low = lax.rem(lax.axis_index("ctx"), 2) == 0
@@ -372,19 +367,19 @@
     left, right = value[:half], value[half:]
     value = jnp.where(low, left, right) + swapped(jnp.where(low, right, left))
     size = half // parts
-    piece = lambda k: lax.dynamic_slice_in_dim(value, lax.rem(dp + k, parts) * size, size, 0)
+    piece = lambda k: lax.dynamic_slice_in_dim(value, jnp.bitwise_xor(dp, k) * size, size, 0)
     total = piece(0)
-    for term in [rotated(piece(k), "dp", k) for k in range(1, parts)]:
+    for term in [paired(piece(k), "dp", k) for k in range(1, parts)]:
         total = total + term
-    reach = 2
-    while reach < lax.axis_size("ctx"):
-        total = total + paired(total, "ctx", reach)
-        reach = 2 * reach
+    count = lax.axis_size("ctx")
+    reaches = [2 << k for k in range((count // 2).bit_length() - 1)]
+    for near, far in zip(reaches, reversed(reaches)):
+        pairs = [(s, s ^ (far if s % 2 else near)) for s in range(count)]
+        total = total + lax.ppermute(total, "ctx", pairs)
     value = jnp.zeros((half,) + value.shape[1:], F32)
     for k in range(parts):
-        term = rotated(total, "dp", k) if k else total
-        at = lax.rem(dp + parts - k, parts) * size
-        value = lax.dynamic_update_slice_in_dim(value, term, at, 0)
+        term = paired(total, "dp", k) if k else total
+        value = lax.dynamic_update_slice_in_dim(value, term, jnp.bitwise_xor(dp, k) * size, 0)
     other = swapped(value)
     return jnp.concatenate([jnp.where(low, value, other), jnp.where(low, other, value)], axis=0)
 

time: 139 us -> 137 us (0.986)
  starting transfers between devices: 28.2 us -> 26.6 us
    ppermute x6 -> x2, starting transfers between devices: 6.79 us -> 4.74 us  [summed(): total = total + lax.ppermute(total, 'ctx', pairs)]
    ppermute x3 -> x7, waiting for transfers between devices: 6.25 us -> 8.19 us  [paired(): lax.ppermute(value, axis, [(source, source ^ step) for source in lines or...]
    ppermute x6 -> x2, waiting for transfers between devices: 8.53 us -> 6.94 us  [summed(): total = total + lax.ppermute(total, 'ctx', pairs)]
    ppermute x3 -> x7, starting transfers between devices: 8.72 us -> 9.16 us  [paired(): lax.ppermute(value, axis, [(source, source ^ step) for source in lines or...]
  transfers between devices with their start and end apart: 17 -> 17, of which waited for: 12 -> 13; matrix products, arithmetic and copies ran while one was open for 1% -> 1% of each run, Pallas kernels for 16% -> 16%
where the time goes in v15:
time: 137 us; the launch traced here: 136 us
  Pallas kernels  75.9 us (55%)
  starting transfers between devices  26.6 us (19%)
  waiting for transfers between devices  25.4 us (19%)
  other arithmetic  3.86 us (3%)
  local copies, waits for them, and re-layouts  3.67 us (3%)
    pallas_call x1, Pallas kernels, local(): pl.pallas_call(final_kernel, grid=(width // each,), in_specs=[pl.BlockSpe...  31.5 us
    pallas_call x1, Pallas kernels, local(): pl.pallas_call(states_kernel, grid=(width // each,), in_specs=[pl.BlockSp...  22.3 us
    pallas_call x3, Pallas kernels, call(): pl.pallas_call(blocks_kernel, grid=(last - first,), in_specs=[pairs, stat...  22.1 us
    ppermute x5, starting transfers between devices, swapped(): return lax.ppermute(value, 'ctx', [(s, s ^ 1) for s in range(count)])  9.73 us
    ppermute x7, starting transfers between devices, paired(): lax.ppermute(value, axis, [(source, source ^ step) for source in lines or...  9.16 us
    ppermute x7, waiting for transfers between devices, paired(): lax.ppermute(value, axis, [(source, source ^ step) for source in lines or...  8.19 us
    ppermute x5, waiting for transfers between devices, swapped(): return lax.ppermute(value, 'ctx', [(s, s ^ 1) for s in range(count)])  7.85 us
    ppermute x2, waiting for transfers between devices, summed(): total = total + lax.ppermute(total, 'ctx', pairs)  6.94 us
  transfers between devices with their start and end apart: 17, of which 13 were waited for; matrix products, arithmetic and copies ran while one was open for 1% of the time, Pallas kernels for 16%

profile of v15, /device:TPU:0, one launch (start us, length us, event | category | flops | bytes accessed | tf_op | source)
XLA Modules:
  0.0 136.5 jit_solution(8492256441301782525)
XLA Ops:
  0.6 0.0 copy-start.11
  0.6 0.0 copy-start.10
  0.7 0.0 copy-start.14
  0.7 1.0 constant_dynamic-slice_fusion.3
  1.7 0.0 copy-start.12
  1.7 0.0 copy-start.13
  1.7 1.2 dynamic-slice_bitcast_fusion
  2.9 0.0 copy-start
  2.9 0.0 copy-start.1
  3.0 0.8 collective-permute-start
  3.9 4.5 %collective-permute-start.1 = (bf16[4,8,8192]{2,1,0:T(8,128)(2,1)S(1)}, bf16[4,8,8192]{2,1,0:T(8,128)(2,1)S(1)}, u32[]{:S(2)}, u32[]{:S(2)}) collective-permute-start(bf16[4,8,8192]{2,1,0:T(8,128)(2,1)S(1)} %pad_maximum_fusion.1), channel_id=1, source_target_pairs={{0,1},{1,0},{2,3},{3,2},{4,5},{5,4},{6,7},{7,6},{8,9},{9,8},{10,11... | collective-permute-start | bytes 1572872 | tf_op jit(solution)/shard_map/ppermute | solution.py:313
  8.5 0.1 multiply_exponential_fusion.1
  8.6 0.2 multiply_exponential_fusion
  8.9 0.2 multiply_reduce_fusion.near
  9.1 0.8 fusion.4
  10.0 0.3 broadcast_select_fusion
  10.3 0.0 copy-start.2
  10.4 0.0 copy-start.6
  10.4 22.3 %states.1 = (f32[16,3,136,512]{3,2,1,0:T(8,128)}, f32[16,2,136,512]{3,2,1,0:T(8,128)}, f32[16,16,8,512]{3,2,1,0:T(8,128)}, f32[16,16,8,512]{3,2,1,0:T(8,128)}, f32[2,16,16,512]{3,2,1,0:T(8,128)}) custom-call(s32[1]{0:T(128)} %bitcast.core, bf16[3,128,8192]{2,1,0:T(8,128)(2,1)} %bitcast.89, bf16[4,8,8192]{2,1,0:T(8,128)(2,1)S(1)} %collective-permute-done.hx, ...), custom_call_target="tpu_custom_call" | custom-call | tf_op jit(solution)/shard_map/states/pallas_call | solution.py:455
  32.6 4.9 %collective-permute-start.2 = (f32[2,16,16,512]{3,2,1,0:T(8,128)}, f32[2,16,16,512]{3,2,1,0:T(8,128)}, u32[]{:S(2)}, u32[]{:S(2)}) collective-permute-start(f32[2,16,16,512]{3,2,1,0:T(8,128)} %get-tuple-element.52), channel_id=1, source_target_pairs={{0,1},{1,0},{2,3},{3,2},{4,5},{5,4},{6,7},{7,6},{8,9},{9,8},{10,11... | collective-permute-start | bytes 3145736 | tf_op jit(solution)/shard_map/ppermute | solution.py:313
  37.5 2.6 %collective-permute-done.2.other = f32[2,16,16,512]{3,2,1,0:T(8,128)} collective-permute-done((f32[2,16,16,512]{3,2,1,0:T(8,128)}, f32[2,16,16,512]{3,2,1,0:T(8,128)}, u32[]{:S(2)}, u32[]{:S(2)}) %collective-permute-start.2) | collective-permute-done | bytes 1048608 | tf_op jit(solution)/shard_map/ppermute | solution.py:313
  40.1 1.3 dynamic-slice_select_fusion.1
  41.5 0.1 broadcast_select_fusion.4
  41.6 2.1 %collective-permute-start.3 = (f32[8,16,512]{2,1,0:T(8,128)S(1)}, f32[8,16,512]{2,1,0:T(8,128)S(1)}, u32[]{:S(2)}, u32[]{:S(2)}) collective-permute-start(f32[8,16,512]{2,1,0:T(8,128)S(1)} %broadcast_select_fusion.4), channel_id=1, source_target_pairs={{0,2},{1,3},{2,0},{3,1},{4,6},{5,7},{6,4},{7,5},{8,10},{9,11},{10,... | collective-permute-start | bytes 786440 | tf_op jit(solution)/shard_map/ppermute | solution.py:329
  43.7 8.2 %blocks.3 = (f32[16,2,136,512]{3,2,1,0:T(8,128)}, f32[16,16,8,512]{3,2,1,0:T(8,128)}, f32[16,16,8,512]{3,2,1,0:T(8,128)}, f32[6,8,512]{2,1,0:T(8,128)S(1)}) custom-call(f32[16,2,136,512]{3,2,1,0:T(8,128)} %get-tuple-element.53.xg, f32[16,16,8,512]{3,2,1,0:T(8,128)} %get-tuple-element.54.blocks_e, ...), custom_call_target="tpu_custom_call", output_to_operand_aliasing={{0}: (0, {}), {1}: (1, {}), {2}: (2, {})} | custom-call | flops 62914560 | bytes 36700160 | tf_op jit(solution)/shard_map/blocks/pallas_call | solution.py:485
  51.8 0.1 multiply_add_fusion.1
  52.0 0.7 collective-permute-start.4
  52.7 5.8 %blocks.4 = (f32[16,2,136,512]{3,2,1,0:T(8,128)}, f32[16,16,8,512]{3,2,1,0:T(8,128)}, f32[16,16,8,512]{3,2,1,0:T(8,128)}, f32[4,8,512]{2,1,0:T(8,128)S(1)}) custom-call(f32[16,2,136,512]{3,2,1,0:T(8,128)} %get-tuple-element.65.xg, f32[16,16,8,512]{3,2,1,0:T(8,128)} %get-tuple-element.66.blocks_e, ...), custom_call_target="tpu_custom_call", output_to_operand_aliasing={{0}: (0, {}), {1}: (1, {}), {2}: (2, {})} | custom-call | flops 62914560 | bytes 36700160 | tf_op jit(solution)/shard_map/blocks/pallas_call | solution.py:485
  58.5 0.0 copy-start.3
  58.6 1.4 %collective-permute-start.5 = (f32[8,16,512]{2,1,0:T(8,128)S(1)}, f32[8,16,512]{2,1,0:T(8,128)S(1)}, u32[]{:S(2)}, u32[]{:S(2)}) collective-permute-start(f32[8,16,512]{2,1,0:T(8,128)S(1)} %collective-permute-done.4), channel_id=1, source_target_pairs={{4,6},{5,7},{2,0},{3,1},{12,14},{13,15},{10,8},{11,9},{20,22},{21,... | collective-permute-start | bytes 786440 | tf_op jit(solution)/shard_map/ppermute | solution.py:345
  60.0 8.1 %blocks.5 = (f32[16,2,136,512]{3,2,1,0:T(8,128)}, f32[16,16,8,512]{3,2,1,0:T(8,128)}, f32[16,16,8,512]{3,2,1,0:T(8,128)}, f32[6,8,512]{2,1,0:T(8,128)S(1)}) custom-call(f32[16,2,136,512]{3,2,1,0:T(8,128)} %get-tuple-element.75.xg, f32[16,16,8,512]{3,2,1,0:T(8,128)} %get-tuple-element.76.blocks_e, ...), custom_call_target="tpu_custom_call", output_to_operand_aliasing={{0}: (0, {}), {1}: (1, {}), {2}: (2, {})} | custom-call | flops 62914560 | bytes 36700160 | tf_op jit(solution)/shard_map/blocks/pallas_call | solution.py:485
  68.1 2.4 %collective-permute-done.5 = f32[8,16,512]{2,1,0:T(8,128)S(1)} collective-permute-done((f32[8,16,512]{2,1,0:T(8,128)S(1)}, f32[8,16,512]{2,1,0:T(8,128)S(1)}, u32[]{:S(2)}, u32[]{:S(2)}) %collective-permute-start.5) | collective-permute-done | bytes 262176 | tf_op jit(solution)/shard_map/ppermute | solution.py:345
  70.6 0.1 select_bitcast_fusion.1
  70.7 0.1 collective-permute-start.6
  70.8 1.9 %collective-permute-done.6.found = f32[2,8,16,512]{3,2,1,0:T(8,128)S(1)} collective-permute-done((f32[2,8,16,512]{3,2,1,0:T(8,128)S(1)}, f32[2,8,16,512]{3,2,1,0:T(8,128)S(1)}, u32[]{:S(2)}, u32[]{:S(2)}) %collective-permute-start.6) | collective-permute-done | bytes 524320 | tf_op jit(solution)/shard_map/ppermute | solution.py:313
  72.7 31.5 %final.1 = (bf16[128,8192]{1,0:T(8,128)(2,1)}, bf16[3,128,8192]{2,1,0:T(8,128)(2,1)}, f32[32,24,256]{2,1,0:T(8,128)S(1)}) custom-call(s32[1]{0:T(128)} %bitcast.core, bf16[3,128,8192]{2,1,0:T(8,128)(2,1)} %bitcast.90, bf16[4,8,8192]{2,1,0:T(8,128)(2,1)S(1)} %collective-permute-done.hx, bf16[4,8,8192]{2,1,0:T(8,128)(2,1)S(1)} %copy-done.3, ...), custom_call_target="tpu_custom_call" | custom-call | tf_op jit(solution)/shard_map/final/pallas_call | solution.py:527
  104.2 0.1 slice_select_fusion
  104.2 0.2 collective-permute-start.7
  104.4 1.6 %collective-permute-done.7 = f32[16,24,256]{2,1,0:T(8,128)S(1)} collective-permute-done((f32[16,24,256]{2,1,0:T(8,128)S(1)}, f32[16,24,256]{2,1,0:T(8,128)S(1)}, u32[]{:S(2)}, u32[]{:S(2)}) %collective-permute-start.7) | collective-permute-done | bytes 393248 | tf_op jit(solution)/shard_map/ppermute | solution.py:313
  106.0 0.1 select_add_fusion
  106.1 2.5 %collective-permute-start.10 = (f32[4,24,256]{2,1,0:T(8,128)S(1)}, f32[4,24,256]{2,1,0:T(8,128)S(1)}, u32[]{:S(2)}, u32[]{:S(2)}) collective-permute-start(f32[4,24,256]{2,1,0:T(8,128)S(1)} %get-tuple-element.111), channel_id=1, source_target_pairs={{0,24},{8,16},{16,8},{24,0},{1,25},{9,17},{17,9},{25,1},{2,26},{10... | collective-permute-start | bytes 294920 | tf_op jit(solution)/shard_map/ppermute | solution.py:329
  108.6 0.5 collective-permute-start.9
  109.1 0.5 collective-permute-start.8
  109.7 2.3 %collective-permute-done.10 = f32[4,24,256]{2,1,0:T(8,128)S(1)} collective-permute-done((f32[4,24,256]{2,1,0:T(8,128)S(1)}, f32[4,24,256]{2,1,0:T(8,128)S(1)}, u32[]{:S(2)}, u32[]{:S(2)}) %collective-permute-start.10) | collective-permute-done | bytes 98336 | tf_op jit(solution)/shard_map/ppermute | solution.py:329
  112.0 2.0 %collective-permute-done.9 = f32[4,24,256]{2,1,0:T(8,128)S(1)} collective-permute-done((f32[4,24,256]{2,1,0:T(8,128)S(1)}, f32[4,24,256]{2,1,0:T(8,128)S(1)}, u32[]{:S(2)}, u32[]{:S(2)}) %collective-permute-start.9) | collective-permute-done | bytes 98336 | tf_op jit(solution)/shard_map/ppermute | solution.py:329
  114.0 0.1 collective-permute-done.8
  114.1 2.5 %collective-permute-start.11 = (f32[4,24,256]{2,1,0:T(8,128)S(1)}, f32[4,24,256]{2,1,0:T(8,128)S(1)}, u32[]{:S(2)}, u32[]{:S(2)}) collective-permute-start(f32[4,24,256]{2,1,0:T(8,128)S(1)} %add_add_fusion), channel_id=1, source_target_pairs={{0,2},{1,5},{2,0},{3,7},{4,6},{5,1},{6,4},{7,3},{8,10},{9,13},{10,... | collective-permute-start | bytes 294920 | tf_op jit(solution)/shard_map/ppermute | solution.py:378
  116.6 3.6 %collective-permute-done.11 = f32[4,24,256]{2,1,0:T(8,128)S(1)} collective-permute-done((f32[4,24,256]{2,1,0:T(8,128)S(1)}, f32[4,24,256]{2,1,0:T(8,128)S(1)}, u32[]{:S(2)}, u32[]{:S(2)}) %collective-permute-start.11) | collective-permute-done | bytes 98336 | tf_op jit(solution)/shard_map/ppermute | solution.py:378
  120.2 2.2 %collective-permute-start.12 = (f32[4,24,256]{2,1,0:T(8,128)S(1)}, f32[4,24,256]{2,1,0:T(8,128)S(1)}, u32[]{:S(2)}, u32[]{:S(2)}) collective-permute-start(f32[4,24,256]{2,1,0:T(8,128)S(1)} %add.68), channel_id=1, source_target_pairs={{0,4},{1,3},{2,6},{3,1},{4,0},{5,7},{6,2},{7,5},{8,12},{9,11},{10,... | collective-permute-start | bytes 294920 | tf_op jit(solution)/shard_map/ppermute | solution.py:378
  122.5 3.3 %collective-permute-done.12 = f32[4,24,256]{2,1,0:T(8,128)S(1)} collective-permute-done((f32[4,24,256]{2,1,0:T(8,128)S(1)}, f32[4,24,256]{2,1,0:T(8,128)S(1)}, u32[]{:S(2)}, u32[]{:S(2)}) %collective-permute-start.12) | collective-permute-done | bytes 98336 | tf_op jit(solution)/shard_map/ppermute | solution.py:378
  125.9 1.6 %collective-permute-start.13 = (f32[4,24,256]{2,1,0:T(8,128)S(1)}, f32[4,24,256]{2,1,0:T(8,128)S(1)}, u32[]{:S(2)}, u32[]{:S(2)}) collective-permute-start(f32[4,24,256]{2,1,0:T(8,128)S(1)} %get-tuple-element.95), channel_id=1, source_target_pairs={{0,8},{8,0},{16,24},{24,16},{1,9},{9,1},{17,25},{25,17},{2,10},{10... | collective-permute-start | bytes 294920 | tf_op jit(solution)/shard_map/ppermute | solution.py:329
  127.5 0.2 collective-permute-start.14
  127.7 1.7 %collective-permute-start.15 = (f32[4,24,256]{2,1,0:T(8,128)S(1)}, f32[4,24,256]{2,1,0:T(8,128)S(1)}, u32[]{:S(2)}, u32[]{:S(2)}) collective-permute-start(f32[4,24,256]{2,1,0:T(8,128)S(1)} %get-tuple-element.95), channel_id=1, source_target_pairs={{0,24},{8,16},{16,8},{24,0},{1,25},{9,17},{17,9},{25,1},{2,26},{10... | collective-permute-start | bytes 294920 | tf_op jit(solution)/shard_map/ppermute | solution.py:329
  129.4 1.9 %collective-permute-done.13 = f32[4,24,256]{2,1,0:T(8,128)S(1)} collective-permute-done((f32[4,24,256]{2,1,0:T(8,128)S(1)}, f32[4,24,256]{2,1,0:T(8,128)S(1)}, u32[]{:S(2)}, u32[]{:S(2)}) %collective-permute-start.13) | collective-permute-done | bytes 98336 | tf_op jit(solution)/shard_map/ppermute | solution.py:329
  131.3 0.8 collective-permute-done.14
  132.1 1.1 collective-permute-done.15
  133.2 0.1 collective-permute-start.16
  133.3 1.7 %collective-permute-done.16 = f32[16,24,256]{2,1,0:T(8,128)S(1)} collective-permute-done((f32[16,24,256]{2,1,0:T(8,128)S(1)}, f32[16,24,256]{2,1,0:T(8,128)S(1)}, u32[]{:S(2)}, u32[]{:S(2)}) %collective-permute-start.16) | collective-permute-done | bytes 393248 | tf_op jit(solution)/shard_map/ppermute | solution.py:313
  135.0 0.1 broadcast_select_fusion.3
  135.1 0.1 maximum_bitcast_fusion
  135.2 0.3 copy.25
  135.4 0.1 reshape.33
  135.6 0.7 slice.67
  136.3 0.2 copy-done.7
  (43 shorter events, 0.5 us)
Async XLA Ops:
  0.6 7.8 %copy-start.11 = (f32[4]{0:T(128)S(1)}, f32[4]{0:T(128)}, u32[]{:S(2)}) copy-start(f32[4]{0:T(128)} %constant.68) | copy-start | bytes 52
  0.6 8.0 %copy-start.10 = (f32[4,8]{1,0:T(4,128)S(1)}, f32[4,8]{1,0:T(4,128)}, u32[]{:S(2)}) copy-start(f32[4,8]{1,0:T(4,128)} %constant.70) | copy-start | bytes 388
  0.7 8.2 %copy-start.14 = (f32[24]{0:T(128)S(1)}, f32[24]{0:T(128)}, u32[]{:S(2)}) copy-start(f32[24]{0:T(128)} %constant.66) | copy-start | bytes 292
  0.7 7.8 %copy-start.9 = (f32[512,16]{0,1:T(8,128)S(1)}, f32[512,16]{0,1:T(8,128)}, u32[]{:S(2)}) copy-start(f32[512,16]{0,1:T(8,128)} %param.14) | copy-start | bytes 98308
  0.7 7.9 %copy-start.8 = (f32[512,16]{0,1:T(8,128)S(1)}, f32[512,16]{0,1:T(8,128)}, u32[]{:S(2)}) copy-start(f32[512,16]{0,1:T(8,128)} %param.13) | copy-start | bytes 98308
  1.7 8.3 %copy-start.12 = (pred[4,8]{1,0:T(4,128)(4,1)S(1)}, pred[4,8]{1,0:T(4,128)(4,1)}, u32[]{:S(2)}) copy-start(pred[4,8]{1,0:T(4,128)(4,1)} %constant.69) | copy-start | bytes 100
  1.7 8.3 %copy-start.13 = (pred[4,8]{1,0:T(4,128)(4,1)S(1)}, pred[4,8]{1,0:T(4,128)(4,1)}, u32[]{:S(2)}) copy-start(pred[4,8]{1,0:T(4,128)(4,1)} %constant.67) | copy-start | bytes 100
  2.9 7.4 %copy-start = (bf16[1,128,8192]{2,1,0:T(8,128)(2,1)S(1)}, bf16[1,128,8192]{2,1,0:T(8,128)(2,1)}, u32[]{:S(2)}) copy-start(bf16[1,128,8192]{2,1,0:T(8,128)(2,1)} %param.16) | copy-start | bytes 6291460
  2.9 7.4 %copy-start.1 = (f32[3,7,8192]{2,1,0:T(8,128)S(1)}, f32[3,7,8192]{2,1,0:T(8,128)}, u32[]{:S(2)}) copy-start(f32[3,7,8192]{2,1,0:T(8,128)} %filt.3) | copy-start | bytes 2064388
  3.0 7.3 %collective-permute-start = (bf16[4,8,8192]{2,1,0:T(8,128)(2,1)S(1)}, bf16[4,8,8192]{2,1,0:T(8,128)(2,1)S(1)}, u32[]{:S(2)}, u32[]{:S(2)}) collective-permute-start(bf16[4,8,8192]{2,1,0:T(8,128)(2,1)S(1)} %pad_maximum_fusion), channel_id=1, source_target_pairs={{1,2},{3,4},{5,6},{2,1},{4,3},{6,5},{9,10},{11,12},{13,14},{10,9},... | collective-permute-start | bytes 1572872 | tf_op jit(solution)/shard_map/ppermute | solution.py:407
  3.9 6.5 %collective-permute-start.1 = (bf16[4,8,8192]{2,1,0:T(8,128)(2,1)S(1)}, bf16[4,8,8192]{2,1,0:T(8,128)(2,1)S(1)}, u32[]{:S(2)}, u32[]{:S(2)}) collective-permute-start(bf16[4,8,8192]{2,1,0:T(8,128)(2,1)S(1)} %pad_maximum_fusion.1), channel_id=1, source_target_pairs={{0,1},{1,0},{2,3},{3,2},{4,5},{5,4},{6,7},{7,6},{8,9},{9,8},{10,11... | collective-permute-start | bytes 1572872 | tf_op jit(solution)/shard_map/ppermute | solution.py:313
  10.3 22.3 %copy-start.2 = (bf16[4,8,8192]{2,1,0:T(8,128)(2,1)}, bf16[4,8,8192]{2,1,0:T(8,128)(2,1)S(1)}, u32[]{:S(2)}) copy-start(bf16[4,8,8192]{2,1,0:T(8,128)(2,1)S(1)} %collective-permute-done.1.hi) | copy-start | bytes 1572868
  10.4 33.3 %copy-start.6 = (f32[8192]{0:T(1024)S(1)}, f32[8192]{0:T(1024)}, u32[]{:S(2)}) copy-start(f32[8192]{0:T(1024)} %param.15) | copy-start | bytes 98308
  32.6 7.5 %collective-permute-start.2 = (f32[2,16,16,512]{3,2,1,0:T(8,128)}, f32[2,16,16,512]{3,2,1,0:T(8,128)}, u32[]{:S(2)}, u32[]{:S(2)}) collective-permute-start(f32[2,16,16,512]{3,2,1,0:T(8,128)} %get-tuple-element.52), channel_id=1, source_target_pairs={{0,1},{1,0},{2,3},{3,2},{4,5},{5,4},{6,7},{7,6},{8,9},{9,8},{10,11... | collective-permute-start | bytes 3145736 | tf_op jit(solution)/shard_map/ppermute | solution.py:313
  41.6 10.3 %collective-permute-start.3 = (f32[8,16,512]{2,1,0:T(8,128)S(1)}, f32[8,16,512]{2,1,0:T(8,128)S(1)}, u32[]{:S(2)}, u32[]{:S(2)}) collective-permute-start(f32[8,16,512]{2,1,0:T(8,128)S(1)} %broadcast_select_fusion.4), channel_id=1, source_target_pairs={{0,2},{1,3},{2,0},{3,1},{4,6},{5,7},{6,4},{7,5},{8,10},{9,11},{10,... | collective-permute-start | bytes 786440 | tf_op jit(solution)/shard_map/ppermute | solution.py:329
  52.0 6.5 %collective-permute-start.4 = (f32[8,16,512]{2,1,0:T(8,128)S(1)}, f32[8,16,512]{2,1,0:T(8,128)S(1)}, u32[]{:S(2)}, u32[]{:S(2)}) collective-permute-start(f32[8,16,512]{2,1,0:T(8,128)S(1)} %multiply_add_fusion.1), channel_id=1, source_target_pairs={{2,4},{3,5},{4,2},{5,3},{10,12},{11,13},{12,10},{13,11},{18,20},{1... | collective-permute-start | bytes 786440 | tf_op jit(solution)/shard_map/ppermute | solution.py:342
  58.5 14.1 %copy-start.3 = (bf16[4,8,8192]{2,1,0:T(8,128)(2,1)S(1)}, bf16[4,8,8192]{2,1,0:T(8,128)(2,1)}, u32[]{:S(2)}) copy-start(bf16[4,8,8192]{2,1,0:T(8,128)(2,1)} %copy-done.2) | copy-start | bytes 1572868
  58.5 14.1 %copy-start.4 = (f32[16,8,512]{2,1,0:T(8,128)S(1)}, f32[16,8,512]{2,1,0:T(8,128)}, u32[]{:S(2)}) copy-start(f32[16,8,512]{2,1,0:T(8,128)} %get-tuple-element.90.cy) | copy-start | bytes 786436
  58.5 14.1 %copy-start.5 = (f32[16,8,512]{2,1,0:T(8,128)S(1)}, f32[16,8,512]{2,1,0:T(8,128)}, u32[]{:S(2)}) copy-start(f32[16,8,512]{2,1,0:T(8,128)} %get-tuple-element.89.cz) | copy-start | bytes 786436
  58.6 12.0 %collective-permute-start.5 = (f32[8,16,512]{2,1,0:T(8,128)S(1)}, f32[8,16,512]{2,1,0:T(8,128)S(1)}, u32[]{:S(2)}, u32[]{:S(2)}) collective-permute-start(f32[8,16,512]{2,1,0:T(8,128)S(1)} %collective-permute-done.4), channel_id=1, source_target_pairs={{4,6},{5,7},{2,0},{3,1},{12,14},{13,15},{10,8},{11,9},{20,22},{21,... | collective-permute-start | bytes 786440 | tf_op jit(solution)/shard_map/ppermute | solution.py:345
  70.7 2.0 %collective-permute-start.6 = (f32[2,8,16,512]{3,2,1,0:T(8,128)S(1)}, f32[2,8,16,512]{3,2,1,0:T(8,128)S(1)}, u32[]{:S(2)}, u32[]{:S(2)}) collective-permute-start(f32[2,8,16,512]{3,2,1,0:T(8,128)S(1)} %pad_maximum_fusion.2.both), channel_id=1, source_target_pairs={{0,1},{1,0},{2,3},{3,2},{4,5},{5,4},{6,7},{7,6},{8,9},{9,8},{10,11... | collective-permute-start | bytes 1572872 | tf_op jit(solution)/shard_map/ppermute | solution.py:313
  104.2 1.8 %collective-permute-start.7 = (f32[16,24,256]{2,1,0:T(8,128)S(1)}, f32[16,24,256]{2,1,0:T(8,128)S(1)}, u32[]{:S(2)}, u32[]{:S(2)}) collective-permute-start(f32[16,24,256]{2,1,0:T(8,128)S(1)} %slice_select_fusion), channel_id=1, source_target_pairs={{0,1},{1,0},{2,3},{3,2},{4,5},{5,4},{6,7},{7,6},{8,9},{9,8},{10,11... | collective-permute-start | bytes 1179656 | tf_op jit(solution)/shard_map/ppermute | solution.py:313
  106.1 5.9 %collective-permute-start.10 = (f32[4,24,256]{2,1,0:T(8,128)S(1)}, f32[4,24,256]{2,1,0:T(8,128)S(1)}, u32[]{:S(2)}, u32[]{:S(2)}) collective-permute-start(f32[4,24,256]{2,1,0:T(8,128)S(1)} %get-tuple-element.111), channel_id=1, source_target_pairs={{0,24},{8,16},{16,8},{24,0},{1,25},{9,17},{17,9},{25,1},{2,26},{10... | collective-permute-start | bytes 294920 | tf_op jit(solution)/shard_map/ppermute | solution.py:329
  108.6 5.4 %collective-permute-start.9 = (f32[4,24,256]{2,1,0:T(8,128)S(1)}, f32[4,24,256]{2,1,0:T(8,128)S(1)}, u32[]{:S(2)}, u32[]{:S(2)}) collective-permute-start(f32[4,24,256]{2,1,0:T(8,128)S(1)} %get-tuple-element.112), channel_id=1, source_target_pairs={{0,16},{8,24},{16,0},{24,8},{1,17},{9,25},{17,1},{25,9},{2,18},{10... | collective-permute-start | bytes 294920 | tf_op jit(solution)/shard_map/ppermute | solution.py:329
  109.1 4.9 %collective-permute-start.8 = (f32[4,24,256]{2,1,0:T(8,128)S(1)}, f32[4,24,256]{2,1,0:T(8,128)S(1)}, u32[]{:S(2)}, u32[]{:S(2)}) collective-permute-start(f32[4,24,256]{2,1,0:T(8,128)S(1)} %get-tuple-element.110), channel_id=1, source_target_pairs={{0,8},{8,0},{16,24},{24,16},{1,9},{9,1},{17,25},{25,17},{2,10},{10... | collective-permute-start | bytes 294920 | tf_op jit(solution)/shard_map/ppermute | solution.py:329
  114.1 6.1 %collective-permute-start.11 = (f32[4,24,256]{2,1,0:T(8,128)S(1)}, f32[4,24,256]{2,1,0:T(8,128)S(1)}, u32[]{:S(2)}, u32[]{:S(2)}) collective-permute-start(f32[4,24,256]{2,1,0:T(8,128)S(1)} %add_add_fusion), channel_id=1, source_target_pairs={{0,2},{1,5},{2,0},{3,7},{4,6},{5,1},{6,4},{7,3},{8,10},{9,13},{10,... | collective-permute-start | bytes 294920 | tf_op jit(solution)/shard_map/ppermute | solution.py:378
  120.2 5.6 %collective-permute-start.12 = (f32[4,24,256]{2,1,0:T(8,128)S(1)}, f32[4,24,256]{2,1,0:T(8,128)S(1)}, u32[]{:S(2)}, u32[]{:S(2)}) collective-permute-start(f32[4,24,256]{2,1,0:T(8,128)S(1)} %add.68), channel_id=1, source_target_pairs={{0,4},{1,3},{2,6},{3,1},{4,0},{5,7},{6,2},{7,5},{8,12},{9,11},{10,... | collective-permute-start | bytes 294920 | tf_op jit(solution)/shard_map/ppermute | solution.py:378
  125.9 5.4 %collective-permute-start.13 = (f32[4,24,256]{2,1,0:T(8,128)S(1)}, f32[4,24,256]{2,1,0:T(8,128)S(1)}, u32[]{:S(2)}, u32[]{:S(2)}) collective-permute-start(f32[4,24,256]{2,1,0:T(8,128)S(1)} %get-tuple-element.95), channel_id=1, source_target_pairs={{0,8},{8,0},{16,24},{24,16},{1,9},{9,1},{17,25},{25,17},{2,10},{10... | collective-permute-start | bytes 294920 | tf_op jit(solution)/shard_map/ppermute | solution.py:329
  127.5 4.6 %collective-permute-start.14 = (f32[4,24,256]{2,1,0:T(8,128)S(1)}, f32[4,24,256]{2,1,0:T(8,128)S(1)}, u32[]{:S(2)}, u32[]{:S(2)}) collective-permute-start(f32[4,24,256]{2,1,0:T(8,128)S(1)} %get-tuple-element.95), channel_id=1, source_target_pairs={{0,16},{8,24},{16,0},{24,8},{1,17},{9,25},{17,1},{25,9},{2,18},{10... | collective-permute-start | bytes 294920 | tf_op jit(solution)/shard_map/ppermute | solution.py:329
  127.7 5.5 %collective-permute-start.15 = (f32[4,24,256]{2,1,0:T(8,128)S(1)}, f32[4,24,256]{2,1,0:T(8,128)S(1)}, u32[]{:S(2)}, u32[]{:S(2)}) collective-permute-start(f32[4,24,256]{2,1,0:T(8,128)S(1)} %get-tuple-element.95), channel_id=1, source_target_pairs={{0,24},{8,16},{16,8},{24,0},{1,25},{9,17},{17,9},{25,1},{2,26},{10... | collective-permute-start | bytes 294920 | tf_op jit(solution)/shard_map/ppermute | solution.py:329
  133.2 1.8 %collective-permute-start.16 = (f32[16,24,256]{2,1,0:T(8,128)S(1)}, f32[16,24,256]{2,1,0:T(8,128)S(1)}, u32[]{:S(2)}, u32[]{:S(2)}) collective-permute-start(f32[16,24,256]{2,1,0:T(8,128)S(1)} %constant_dynamic-update-slice_fusion), channel_id=1, source_target_pairs={{0,1},{1,0},{2,3},{3,2},{4,5},{5,4},{6,7},{7,6},{8,9},{9,8},{10,11... | collective-permute-start | bytes 1179656 | tf_op jit(solution)/shard_map/ppermute | solution.py:313
  135.6 0.9 copy-start.7

commit v16 on v15

--- a/solution.py
+++ b/solution.py
@@ -56,7 +56,31 @@
     return added([tap[k] * values[k] for k in range(len(tap))])
 
 
-def states_kernel(core, p, hx, hi, u, filt, f1, we, wb, qkv, xg, blocks_e, blocks_a, ends, xs):
+def edges_kernel(core, p_head, p_tail, u_head, u_tail, across, within, heads, tails):
+    first = core[0] == 0
+    reach = across.shape[0] // 4
+    for j in range(4):
+        head = (p_head[j] if j < 3 else u_head[...]).astype(F32)
+        tail = (p_tail[j] if j < 3 else u_tail[...]).astype(F32)
+        heads[reach * j : reach * j + reach] = head[:reach]
+        tails[reach * j : reach * j + reach] = tail[tail.shape[0] - reach :]
+    head, tail = heads[...], tails[...]
+    across[...] = jnp.where(first, head, tail).astype(BF16)
+    within[...] = jnp.where(first, tail, head).astype(BF16)
+
+
+def place_edges(first, hx, hi, lanes, edges, streams, rows):
+    across, within = hx[:, lanes].astype(F32), hi[:, lanes].astype(F32)
+    edges[0], edges[1] = jnp.where(first, across, within), jnp.where(first, within, across)
+    reach = across.shape[0] // 4
+    for j in range(len(streams)):
+        if j < 3:
+            streams[j][SUB - reach : SUB] = edges[0, reach * j : reach * j + reach]
+        streams[j][SUB + rows :] = jnp.zeros((SUB, LANES), F32)
+        streams[j][SUB + rows : SUB + rows + reach] = edges[1, reach * j : reach * j + reach]
+
+
+def states_kernel(core, p, hx, hi, u, filt, f1, we, wb, qkv, xg, blocks_e, blocks_a, ends, xs, edges):
     rows = p.shape[1]
     run = (rows + SUB) // SUB
     taps = filt.shape[1]
@@ -71,13 +95,9 @@
         which = lt // tiles
         inside = lax.broadcasted_iota(jnp.int32, (SUB, LANES), 0) < SUB - 1
         for j in range(3):
-            across, within = hx[j, :, lanes].astype(F32), hi[j, :, lanes].astype(F32)
-            xs[j, 0:SUB] = jnp.where(first, across, within)
             xs[j, SUB : SUB + rows] = p[j, :, lanes].astype(F32)
-            xs[j, SUB + rows :] = jnp.where(first, within, across)
         xs[3, SUB : SUB + rows] = u[:, lanes].astype(F32)
-        across, within = hx[3, :, lanes].astype(F32), hi[3, :, lanes].astype(F32)
-        xs[3, SUB + rows :] = jnp.where(first, within, across)
+        place_edges(first, hx, hi, lanes, edges, [xs.at[j] for j in range(4)], rows)
 
         def mixed(j):
             even, odd, both = phases([spread(filt[j, i : i + 1, lanes]) for i in range(taps)])
@@ -178,7 +198,7 @@
 
 def final_kernel(
     core, p, hx, hi, u, qkv, conv, from_e, from_a, skip_sum, both, found, other, filt, f1, f_all, cz, cy,
-    output, grad_p, sums, ps, us, gs, os, es,
+    output, grad_p, sums, ps, gs, os, es, edges,
 ):
     rows = p.shape[1]
     run = (rows + SUB) // SUB
@@ -203,13 +223,9 @@
             close = other[side, which, :, part] + f_all[:, part] * far
             es[side] = jnp.where(first == (side == 0), far, close)
         for j in range(3):
-            across, within = hx[j, :, lanes].astype(F32), hi[j, :, lanes].astype(F32)
-            ps[j, 0:SUB] = jnp.where(first, across, within)
             ps[j, SUB : SUB + rows] = p[j, :, lanes].astype(F32)
-            ps[j, SUB + rows :] = jnp.where(first, within, across)
-        us[0:rows] = u[:, lanes].astype(F32)
-        across, within = hx[3, :, lanes].astype(F32), hi[3, :, lanes].astype(F32)
-        us[rows:] = jnp.where(first, within, across)
+        ps[3, SUB : SUB + rows] = u[:, lanes].astype(F32)
+        place_edges(first, hx, hi, lanes, edges, [ps.at[j] for j in range(4)], rows)
         decay = [spread(f1[n : n + 1, part]) for n in range(poles)]
 
         state = [
@@ -218,7 +234,7 @@
         ]
         for a in range(run):
             at = slice(SUB * a, SUB * a + SUB)
-            query, upstream = qkv[which, 0, at, part], us[pl.ds(a, SUB, stride=run), :]
+            query, upstream = qkv[which, 0, at, part], ps[3, pl.ds(SUB + a, SUB, stride=run), :]
             filtered = conv[which, 0, at, part] + added(list(state))
             os[pl.ds(a, SUB, stride=run), :] = query * filtered
             gs[0, at] = upstream * filtered
@@ -371,11 +387,10 @@
     total = piece(0)
     for term in [paired(piece(k), "dp", k) for k in range(1, parts)]:
         total = total + term
-    count = lax.axis_size("ctx")
-    reaches = [2 << k for k in range((count // 2).bit_length() - 1)]
-    for near, far in zip(reaches, reversed(reaches)):
-        pairs = [(s, s ^ (far if s % 2 else near)) for s in range(count)]
-        total = total + lax.ppermute(total, "ctx", pairs)
+    reach = 2
+    while reach < lax.axis_size("ctx"):
+        total = total + paired(total, "ctx", reach)
+        reach = 2 * reach
     value = jnp.zeros((half,) + value.shape[1:], F32)
     for k in range(parts):
         term = paired(total, "dp", k) if k else total
@@ -395,17 +410,31 @@
     p = projected[0].transpose(1, 0, 2)
     u = cotangent[0]
     core = lax.rem(lax.axis_index("ctx"), 2)
-
-    def edge(last):
-        start = jnp.where(last, rows - SUB, 0)
-        cut = lambda value, axis: lax.dynamic_slice_in_dim(value, start, SUB, axis)
-        return jnp.concatenate([cut(p, 1), cut(u, 0)[None]], axis=0)
-
+    params = pltpu.CompilerParams(vmem_limit_bytes=48 * 1024 * 1024)
+    shape_of = jax.ShapeDtypeStruct
+    span, tail, chunk = taps - 1, 2 * SUB, channels // 4
+    packed = pl.BlockSpec((4 * span, chunk), lambda w: (0, w))
+    to_across, to_within = pl.pallas_call(
+        edges_kernel,
+        grid=(4,),
+        in_specs=[
+            pl.BlockSpec(memory_space=pltpu.SMEM),
+            pl.BlockSpec((3, tail, chunk), lambda w: (0, 0, w)),
+            pl.BlockSpec((3, tail, chunk), lambda w: (0, rows // tail - 1, w)),
+            pl.BlockSpec((tail, chunk), lambda w: (0, w)),
+            pl.BlockSpec((tail, chunk), lambda w: (rows // tail - 1, w)),
+        ],
+        out_specs=[packed, packed],
+        out_shape=[shape_of((4 * span, channels), BF16)] * 2,
+        scratch_shapes=[pltpu.VMEM((4 * span, chunk), F32)] * 2,
+        compiler_params=params,
+        name="edges",
+    )(core[None], p, p, u, u)
     devices = lax.axis_size("ctx")
     across = [(k, k + 1) for k in range(1, devices - 1, 2)]
     across = across + [(target, source) for source, target in across]
-    hx = lax.ppermute(edge(core == 1), "ctx", across)
-    hi = swapped(edge(core == 0))
+    hx = lax.ppermute(to_across, "ctx", across)
+    hi = swapped(to_within)
 
     rate = decay_rates.T
     weight = residues.T
@@ -437,8 +466,6 @@
             value.shape, lambda w: (0,) * value.ndim, pipeline_mode=pl.Buffered(1)
         )
 
-    params = pltpu.CompilerParams(vmem_limit_bytes=48 * 1024 * 1024)
-    shape_of = jax.ShapeDtypeStruct
     ends_spec = pl.BlockSpec((2, each, poles, groups), lambda w: (0, w, 0, 0))
     halved = pl.BlockSpec(
         (2, each, poles, groups), lambda w: (0, lax.rem(w, width // each // 2), 0, 0)
@@ -457,7 +484,7 @@
         grid=(width // each,),
         in_specs=[
             pl.BlockSpec(memory_space=pltpu.SMEM),
-            by_w(3, rows), by_w(4, SUB), by_w(4, SUB), by_w(rows), by_w(3, taps),
+            by_w(3, rows), by_w(4 * span), by_w(4 * span), by_w(rows), by_w(3, taps),
             fixed(f1), fixed(we), fixed(wb),
         ],
         out_specs=[
@@ -468,7 +495,9 @@
             shape_of((width, 3, held, groups), F32), pair_shape,
             state_shape, state_shape, shape_of((2, width, poles, groups), F32),
         ],
-        scratch_shapes=[pltpu.VMEM((4, held + SUB, LANES), F32)],
+        scratch_shapes=[
+            pltpu.VMEM((4, held + SUB, LANES), F32), pltpu.VMEM((2, 4 * span, LANES), F32),
+        ],
         compiler_params=params,
         name="states",
     )(core[None], p, hx, hi, u, short_filter, f1, we, wb)
@@ -518,18 +547,18 @@
     count = 3 * SUB
     split = 2 if groups % (2 * LANES) == 0 else 1
     scratch = [
-        pltpu.VMEM((3, held + SUB, LANES), F32),
-        pltpu.VMEM((held, LANES), F32),
+        pltpu.VMEM((4, held + SUB, LANES), F32),
         pltpu.VMEM((3, held, LANES), F32),
         pltpu.VMEM((held, LANES), F32),
         pltpu.VMEM((2, poles, LANES), F32),
+        pltpu.VMEM((2, 4 * span, LANES), F32),
     ]
     output, grad_p, sums = pl.pallas_call(
         final_kernel,
         grid=(width // each,),
         in_specs=[
             pl.BlockSpec(memory_space=pltpu.SMEM),
-            by_w(3, rows), by_w(4, SUB), by_w(4, SUB), by_w(rows),
+            by_w(3, rows), by_w(4 * span), by_w(4 * span), by_w(rows),
             by_block(3, held, groups), by_block(2, held, groups), state_spec, state_spec,
             by_block(SUB, groups), halved, halved, ends_spec,
             by_w(3, taps), fixed(f1), fixed(f_all), fixed(cz), fixed(cy),

time: 137 us -> 139 us (1.015)
  Pallas kernels: 75.9 us -> 78.4 us
    ppermute x3 -> x1, waiting for transfers between devices: 6.94 us -> 0.01 us  [local(): hx = lax.ppermute(to_across, 'ctx', across)]
    ppermute x7 -> x9, starting transfers between devices: 9.16 us -> 15.8 us  [paired(): lax.ppermute(value, axis, [(source, source ^ step) for source in lines or...]
    ppermute x7 -> x9, waiting for transfers between devices: 8.19 us -> 14.1 us  [paired(): lax.ppermute(value, axis, [(source, source ^ step) for source in lines or...]
    ppermute x3 -> x1, starting transfers between devices: 5.56 us -> 0.82 us  [local(): hx = lax.ppermute(to_across, 'ctx', across)]
    pallas_call x0 -> x1, Pallas kernels: none -> 2.57 us  [local(): pl.pallas_call(edges_kernel, grid=(4,), in_specs=[pl.BlockSpec(memory_spa...]
    dynamic_slice x2 -> x0, local copies, waits for them, and re-layouts: 2.17 us -> none  [edge(): cut = lambda value, axis: lax.dynamic_slice_in_dim(value, start, SUB, axis)]
    unnamed x30, local copies, waits for them, and re-layouts: 0.25 us -> 1.82 us
    ppermute x5, starting transfers between devices: 9.73 us -> 8.24 us  [swapped(): return lax.ppermute(value, 'ctx', [(s, s ^ 1) for s in range(count)])]
where the time goes in v16:
time: 139 us; the launch traced here: 138 us
  Pallas kernels  78.4 us (56%)
  starting transfers between devices  26.9 us (19%)
  waiting for transfers between devices  24.4 us (18%)
  other arithmetic  3.76 us (3%)
  local copies, waits for them, and re-layouts  3.08 us (2%)
    pallas_call x1, Pallas kernels, local(): pl.pallas_call(final_kernel, grid=(width // each,), in_specs=[pl.BlockSpe...  31.4 us
    pallas_call x1, Pallas kernels, local(): pl.pallas_call(states_kernel, grid=(width // each,), in_specs=[pl.BlockSp...  22.4 us
    pallas_call x3, Pallas kernels, call(): pl.pallas_call(blocks_kernel, grid=(last - first,), in_specs=[pairs, stat...  22.1 us
    ppermute x9, starting transfers between devices, paired(): lax.ppermute(value, axis, [(source, source ^ step) for source in lines or...  15.8 us
    ppermute x9, waiting for transfers between devices, paired(): lax.ppermute(value, axis, [(source, source ^ step) for source in lines or...  14.1 us
    ppermute x5, starting transfers between devices, swapped(): return lax.ppermute(value, 'ctx', [(s, s ^ 1) for s in range(count)])  8.24 us
    ppermute x5, waiting for transfers between devices, swapped(): return lax.ppermute(value, 'ctx', [(s, s ^ 1) for s in range(count)])  7.85 us
  transfers between devices with their start and end apart: 17, of which 13 were waited for; matrix products, arithmetic and copies ran while one was open for 1% of the time, Pallas kernels for 16%

profile of v16, /device:TPU:0, one launch (start us, length us, event | category | flops | bytes accessed | tf_op | source)
XLA Modules:
  0.0 137.6 jit_solution(15782364195543070706)
XLA Ops:
  0.6 0.0 copy-start
  0.6 1.6 %copy-done = bf16[1,128,8192]{2,1,0:T(8,128)(2,1)S(1)} copy-done((bf16[1,128,8192]{2,1,0:T(8,128)(2,1)S(1)}, bf16[1,128,8192]{2,1,0:T(8,128)(2,1)}, u32[]{:S(2)}) %copy-start) | copy-done | bytes 2097176
  2.2 0.0 copy-start.14
  2.3 2.6 %edges.1 = (bf16[24,8192]{1,0:T(8,128)(2,1)S(1)}, bf16[24,8192]{1,0:T(8,128)(2,1)S(1)}) custom-call(s32[1]{0:T(128)} %bitcast.core, bf16[3,128,8192]{2,1,0:T(8,128)(2,1)} %bitcast.83, bf16[3,128,8192]{2,1,0:T(8,128)(2,1)} %bitcast.84, bf16[128,8192]{1,0:T(8,128)(2,1)S(1)} %bitcast.77, bf16[128,8192]{1,0:T(8,128)(2,1)S(1)} %bitcast.78), custom_call_target="tpu_custom_call" | custom-call | tf_op jit(solution)/shard_map/edges/pallas_call | solution.py:417
  4.8 0.0 copy-start.12
  4.8 0.0 copy-start.13
  4.9 0.0 copy-start.1
  4.9 0.8 collective-permute-start
  5.7 4.4 %collective-permute-start.1 = (bf16[24,8192]{1,0:T(8,128)(2,1)S(1)}, bf16[24,8192]{1,0:T(8,128)(2,1)S(1)}, u32[]{:S(2)}, u32[]{:S(2)}) collective-permute-start(bf16[24,8192]{1,0:T(8,128)(2,1)S(1)} %get-tuple-element.53), channel_id=1, source_target_pairs={{0,1},{1,0},{2,3},{3,2},{4,5},{5,4},{6,7},{7,6},{8,9},{9,8},{10,11... | collective-permute-start | bytes 1179656 | tf_op jit(solution)/shard_map/ppermute | solution.py:329
  10.2 0.1 multiply_exponential_fusion.1
  10.3 0.2 multiply_exponential_fusion
  10.6 0.9 fusion.4
  11.4 0.2 multiply_reduce_fusion.near
  11.7 0.3 broadcast_select_fusion
  12.0 0.0 copy-start.2
  12.1 0.0 copy-start.6
  12.1 22.4 %states.1 = (f32[16,3,136,512]{3,2,1,0:T(8,128)}, f32[16,2,136,512]{3,2,1,0:T(8,128)}, f32[16,16,8,512]{3,2,1,0:T(8,128)}, f32[16,16,8,512]{3,2,1,0:T(8,128)}, f32[2,16,16,512]{3,2,1,0:T(8,128)}) custom-call(s32[1]{0:T(128)} %bitcast.core, bf16[3,128,8192]{2,1,0:T(8,128)(2,1)} %bitcast.85, bf16[24,8192]{1,0:T(8,128)(2,1)S(1)} %collective-permute-done.hx, ...), custom_call_target="tpu_custom_call" | custom-call | tf_op jit(solution)/shard_map/states/pallas_call | solution.py:482
  34.4 3.5 %collective-permute-start.2 = (f32[2,16,16,512]{3,2,1,0:T(8,128)}, f32[2,16,16,512]{3,2,1,0:T(8,128)}, u32[]{:S(2)}, u32[]{:S(2)}) collective-permute-start(f32[2,16,16,512]{3,2,1,0:T(8,128)} %get-tuple-element.56), channel_id=1, source_target_pairs={{0,1},{1,0},{2,3},{3,2},{4,5},{5,4},{6,7},{7,6},{8,9},{9,8},{10,11... | collective-permute-start | bytes 3145736 | tf_op jit(solution)/shard_map/ppermute | solution.py:329
  37.9 2.6 %collective-permute-done.2.other = f32[2,16,16,512]{3,2,1,0:T(8,128)} collective-permute-done((f32[2,16,16,512]{3,2,1,0:T(8,128)}, f32[2,16,16,512]{3,2,1,0:T(8,128)}, u32[]{:S(2)}, u32[]{:S(2)}) %collective-permute-start.2) | collective-permute-done | bytes 1048608 | tf_op jit(solution)/shard_map/ppermute | solution.py:329
  40.6 1.3 dynamic-slice_select_fusion.1
  41.9 0.1 broadcast_select_fusion.4
  42.0 2.1 %collective-permute-start.3 = (f32[8,16,512]{2,1,0:T(8,128)S(1)}, f32[8,16,512]{2,1,0:T(8,128)S(1)}, u32[]{:S(2)}, u32[]{:S(2)}) collective-permute-start(f32[8,16,512]{2,1,0:T(8,128)S(1)} %broadcast_select_fusion.4), channel_id=1, source_target_pairs={{0,2},{1,3},{2,0},{3,1},{4,6},{5,7},{6,4},{7,5},{8,10},{9,11},{10,... | collective-permute-start | bytes 786440 | tf_op jit(solution)/shard_map/ppermute | solution.py:345
  44.1 8.2 %blocks.3 = (f32[16,2,136,512]{3,2,1,0:T(8,128)}, f32[16,16,8,512]{3,2,1,0:T(8,128)}, f32[16,16,8,512]{3,2,1,0:T(8,128)}, f32[6,8,512]{2,1,0:T(8,128)S(1)}) custom-call(f32[16,2,136,512]{3,2,1,0:T(8,128)} %get-tuple-element.57.xg, f32[16,16,8,512]{3,2,1,0:T(8,128)} %get-tuple-element.58.blocks_e, ...), custom_call_target="tpu_custom_call", output_to_operand_aliasing={{0}: (0, {}), {1}: (1, {}), {2}: (2, {})} | custom-call | flops 62914560 | bytes 36700160 | tf_op jit(solution)/shard_map/blocks/pallas_call | solution.py:514
  52.3 0.1 multiply_add_fusion.1
  52.5 0.7 collective-permute-start.4
  53.1 5.8 %blocks.4 = (f32[16,2,136,512]{3,2,1,0:T(8,128)}, f32[16,16,8,512]{3,2,1,0:T(8,128)}, f32[16,16,8,512]{3,2,1,0:T(8,128)}, f32[4,8,512]{2,1,0:T(8,128)S(1)}) custom-call(f32[16,2,136,512]{3,2,1,0:T(8,128)} %get-tuple-element.69.xg, f32[16,16,8,512]{3,2,1,0:T(8,128)} %get-tuple-element.70.blocks_e, ...), custom_call_target="tpu_custom_call", output_to_operand_aliasing={{0}: (0, {}), {1}: (1, {}), {2}: (2, {})} | custom-call | flops 62914560 | bytes 36700160 | tf_op jit(solution)/shard_map/blocks/pallas_call | solution.py:514
  59.0 0.0 copy-start.3
  59.0 0.0 copy-start.4
  59.0 1.4 %collective-permute-start.5 = (f32[8,16,512]{2,1,0:T(8,128)S(1)}, f32[8,16,512]{2,1,0:T(8,128)S(1)}, u32[]{:S(2)}, u32[]{:S(2)}) collective-permute-start(f32[8,16,512]{2,1,0:T(8,128)S(1)} %collective-permute-done.4), channel_id=1, source_target_pairs={{4,6},{5,7},{2,0},{3,1},{12,14},{13,15},{10,8},{11,9},{20,22},{21,... | collective-permute-start | bytes 786440 | tf_op jit(solution)/shard_map/ppermute | solution.py:361
  60.4 8.1 %blocks.5 = (f32[16,2,136,512]{3,2,1,0:T(8,128)}, f32[16,16,8,512]{3,2,1,0:T(8,128)}, f32[16,16,8,512]{3,2,1,0:T(8,128)}, f32[6,8,512]{2,1,0:T(8,128)S(1)}) custom-call(f32[16,2,136,512]{3,2,1,0:T(8,128)} %get-tuple-element.79.xg, f32[16,16,8,512]{3,2,1,0:T(8,128)} %get-tuple-element.80.blocks_e, ...), custom_call_target="tpu_custom_call", output_to_operand_aliasing={{0}: (0, {}), {1}: (1, {}), {2}: (2, {})} | custom-call | flops 62914560 | bytes 36700160 | tf_op jit(solution)/shard_map/blocks/pallas_call | solution.py:514
  68.6 2.4 %collective-permute-done.5 = f32[8,16,512]{2,1,0:T(8,128)S(1)} collective-permute-done((f32[8,16,512]{2,1,0:T(8,128)S(1)}, f32[8,16,512]{2,1,0:T(8,128)S(1)}, u32[]{:S(2)}, u32[]{:S(2)}) %collective-permute-start.5) | collective-permute-done | bytes 262176 | tf_op jit(solution)/shard_map/ppermute | solution.py:361
  71.0 0.1 select_bitcast_fusion.1
  71.1 0.1 collective-permute-start.6
  71.2 1.9 %collective-permute-done.6.found = f32[2,8,16,512]{3,2,1,0:T(8,128)S(1)} collective-permute-done((f32[2,8,16,512]{3,2,1,0:T(8,128)S(1)}, f32[2,8,16,512]{3,2,1,0:T(8,128)S(1)}, u32[]{:S(2)}, u32[]{:S(2)}) %collective-permute-start.6) | collective-permute-done | bytes 524320 | tf_op jit(solution)/shard_map/ppermute | solution.py:329
  73.1 31.4 %final.1 = (bf16[128,8192]{1,0:T(8,128)(2,1)}, bf16[3,128,8192]{2,1,0:T(8,128)(2,1)}, f32[32,24,256]{2,1,0:T(8,128)S(1)}) custom-call(s32[1]{0:T(128)} %bitcast.core, bf16[3,128,8192]{2,1,0:T(8,128)(2,1)} %bitcast.86, bf16[24,8192]{1,0:T(8,128)(2,1)S(1)} %collective-permute-done.hx, bf16[24,8192]{1,0:T(8,128)(2,1)S(1)} %copy-done.3, ...), custom_call_target="tpu_custom_call" | custom-call | tf_op jit(solution)/shard_map/final/pallas_call | solution.py:556
  104.5 0.1 slice_select_fusion
  104.5 0.2 collective-permute-start.7
  104.7 1.6 %collective-permute-done.7 = f32[16,24,256]{2,1,0:T(8,128)S(1)} collective-permute-done((f32[16,24,256]{2,1,0:T(8,128)S(1)}, f32[16,24,256]{2,1,0:T(8,128)S(1)}, u32[]{:S(2)}, u32[]{:S(2)}) %collective-permute-start.7) | collective-permute-done | bytes 393248 | tf_op jit(solution)/shard_map/ppermute | solution.py:329
  106.3 0.1 select_add_fusion
  106.4 2.5 %collective-permute-start.10 = (f32[4,24,256]{2,1,0:T(8,128)S(1)}, f32[4,24,256]{2,1,0:T(8,128)S(1)}, u32[]{:S(2)}, u32[]{:S(2)}) collective-permute-start(f32[4,24,256]{2,1,0:T(8,128)S(1)} %get-tuple-element.111), channel_id=1, source_target_pairs={{0,24},{8,16},{16,8},{24,0},{1,25},{9,17},{17,9},{25,1},{2,26},{10... | collective-permute-start | bytes 294920 | tf_op jit(solution)/shard_map/ppermute | solution.py:345
  108.9 0.5 collective-permute-start.9
  109.5 0.5 collective-permute-start.8
  110.0 2.3 %collective-permute-done.10 = f32[4,24,256]{2,1,0:T(8,128)S(1)} collective-permute-done((f32[4,24,256]{2,1,0:T(8,128)S(1)}, f32[4,24,256]{2,1,0:T(8,128)S(1)}, u32[]{:S(2)}, u32[]{:S(2)}) %collective-permute-start.10) | collective-permute-done | bytes 98336 | tf_op jit(solution)/shard_map/ppermute | solution.py:345
  112.3 2.0 %collective-permute-done.9 = f32[4,24,256]{2,1,0:T(8,128)S(1)} collective-permute-done((f32[4,24,256]{2,1,0:T(8,128)S(1)}, f32[4,24,256]{2,1,0:T(8,128)S(1)}, u32[]{:S(2)}, u32[]{:S(2)}) %collective-permute-start.9) | collective-permute-done | bytes 98336 | tf_op jit(solution)/shard_map/ppermute | solution.py:345
  114.3 0.1 collective-permute-done.8
  114.4 2.5 %collective-permute-start.11 = (f32[4,24,256]{2,1,0:T(8,128)S(1)}, f32[4,24,256]{2,1,0:T(8,128)S(1)}, u32[]{:S(2)}, u32[]{:S(2)}) collective-permute-start(f32[4,24,256]{2,1,0:T(8,128)S(1)} %add_add_fusion), channel_id=1, source_target_pairs={{0,2},{1,3},{2,0},{3,1},{4,6},{5,7},{6,4},{7,5},{8,10},{9,11},{10,... | collective-permute-start | bytes 294920 | tf_op jit(solution)/shard_map/ppermute | solution.py:345
  116.9 2.7 %collective-permute-done.11 = f32[4,24,256]{2,1,0:T(8,128)S(1)} collective-permute-done((f32[4,24,256]{2,1,0:T(8,128)S(1)}, f32[4,24,256]{2,1,0:T(8,128)S(1)}, u32[]{:S(2)}, u32[]{:S(2)}) %collective-permute-start.11) | collective-permute-done | bytes 98336 | tf_op jit(solution)/shard_map/ppermute | solution.py:345
  119.7 3.1 %collective-permute-start.12 = (f32[4,24,256]{2,1,0:T(8,128)S(1)}, f32[4,24,256]{2,1,0:T(8,128)S(1)}, u32[]{:S(2)}, u32[]{:S(2)}) collective-permute-start(f32[4,24,256]{2,1,0:T(8,128)S(1)} %add.64), channel_id=1, source_target_pairs={{0,4},{1,5},{2,6},{3,7},{4,0},{5,1},{6,2},{7,3},{8,12},{9,13},{10,... | collective-permute-start | bytes 294920 | tf_op jit(solution)/shard_map/ppermute | solution.py:345
  122.8 2.8 %collective-permute-done.12 = f32[4,24,256]{2,1,0:T(8,128)S(1)} collective-permute-done((f32[4,24,256]{2,1,0:T(8,128)S(1)}, f32[4,24,256]{2,1,0:T(8,128)S(1)}, u32[]{:S(2)}, u32[]{:S(2)}) %collective-permute-start.12) | collective-permute-done | bytes 98336 | tf_op jit(solution)/shard_map/ppermute | solution.py:345
  125.7 2.9 %collective-permute-start.13 = (f32[4,24,256]{2,1,0:T(8,128)S(1)}, f32[4,24,256]{2,1,0:T(8,128)S(1)}, u32[]{:S(2)}, u32[]{:S(2)}) collective-permute-start(f32[4,24,256]{2,1,0:T(8,128)S(1)} %get-tuple-element.99), channel_id=1, source_target_pairs={{0,8},{8,0},{16,24},{24,16},{1,9},{9,1},{17,25},{25,17},{2,10},{10... | collective-permute-start | bytes 294920 | tf_op jit(solution)/shard_map/ppermute | solution.py:345
  128.6 0.2 collective-permute-start.14
  128.8 1.4 %collective-permute-start.15 = (f32[4,24,256]{2,1,0:T(8,128)S(1)}, f32[4,24,256]{2,1,0:T(8,128)S(1)}, u32[]{:S(2)}, u32[]{:S(2)}) collective-permute-start(f32[4,24,256]{2,1,0:T(8,128)S(1)} %get-tuple-element.99), channel_id=1, source_target_pairs={{0,24},{8,16},{16,8},{24,0},{1,25},{9,17},{17,9},{25,1},{2,26},{10... | collective-permute-start | bytes 294920 | tf_op jit(solution)/shard_map/ppermute | solution.py:345
  130.2 1.8 %collective-permute-done.13 = f32[4,24,256]{2,1,0:T(8,128)S(1)} collective-permute-done((f32[4,24,256]{2,1,0:T(8,128)S(1)}, f32[4,24,256]{2,1,0:T(8,128)S(1)}, u32[]{:S(2)}, u32[]{:S(2)}) %collective-permute-start.13) | collective-permute-done | bytes 98336 | tf_op jit(solution)/shard_map/ppermute | solution.py:345
  132.0 1.2 collective-permute-done.14
  133.3 1.1 collective-permute-done.15
  134.4 0.1 collective-permute-start.16
  134.5 1.7 %collective-permute-done.16 = f32[16,24,256]{2,1,0:T(8,128)S(1)} collective-permute-done((f32[16,24,256]{2,1,0:T(8,128)S(1)}, f32[16,24,256]{2,1,0:T(8,128)S(1)}, u32[]{:S(2)}, u32[]{:S(2)}) %collective-permute-start.16) | collective-permute-done | bytes 393248 | tf_op jit(solution)/shard_map/ppermute | solution.py:329
  136.2 0.1 broadcast_select_fusion.3
  136.2 0.1 maximum_bitcast_fusion
  136.3 0.3 copy.25
  136.6 0.1 reshape.21
  136.7 0.0 copy-start.7
  136.7 0.7 slice.67
  137.4 0.2 copy-done.7
  (40 shorter events, 0.4 us)
Async XLA Ops:
  0.6 1.6 %copy-start = (bf16[1,128,8192]{2,1,0:T(8,128)(2,1)S(1)}, bf16[1,128,8192]{2,1,0:T(8,128)(2,1)}, u32[]{:S(2)}) copy-start(bf16[1,128,8192]{2,1,0:T(8,128)(2,1)} %param.16) | copy-start | bytes 6291460
  2.2 7.9 %copy-start.9 = (f32[512,16]{0,1:T(8,128)S(1)}, f32[512,16]{0,1:T(8,128)}, u32[]{:S(2)}) copy-start(f32[512,16]{0,1:T(8,128)} %param.14) | copy-start | bytes 98308
  2.2 7.9 %copy-start.11 = (f32[4]{0:T(128)S(1)}, f32[4]{0:T(128)}, u32[]{:S(2)}) copy-start(f32[4]{0:T(128)} %constant.59) | copy-start | bytes 52
  2.2 8.0 %copy-start.8 = (f32[512,16]{0,1:T(8,128)S(1)}, f32[512,16]{0,1:T(8,128)}, u32[]{:S(2)}) copy-start(f32[512,16]{0,1:T(8,128)} %param.13) | copy-start | bytes 98308
  2.2 8.1 %copy-start.10 = (f32[4,8]{1,0:T(4,128)S(1)}, f32[4,8]{1,0:T(4,128)}, u32[]{:S(2)}) copy-start(f32[4,8]{1,0:T(4,128)} %constant.61) | copy-start | bytes 388
  2.2 9.2 %copy-start.14 = (f32[24]{0:T(128)S(1)}, f32[24]{0:T(128)}, u32[]{:S(2)}) copy-start(f32[24]{0:T(128)} %constant.57) | copy-start | bytes 292
  4.8 6.8 %copy-start.12 = (pred[4,8]{1,0:T(4,128)(4,1)S(1)}, pred[4,8]{1,0:T(4,128)(4,1)}, u32[]{:S(2)}) copy-start(pred[4,8]{1,0:T(4,128)(4,1)} %constant.60) | copy-start | bytes 100
  4.8 6.8 %copy-start.13 = (pred[4,8]{1,0:T(4,128)(4,1)S(1)}, pred[4,8]{1,0:T(4,128)(4,1)}, u32[]{:S(2)}) copy-start(pred[4,8]{1,0:T(4,128)(4,1)} %constant.58) | copy-start | bytes 100
  4.9 7.2 %copy-start.1 = (f32[3,7,8192]{2,1,0:T(8,128)S(1)}, f32[3,7,8192]{2,1,0:T(8,128)}, u32[]{:S(2)}) copy-start(f32[3,7,8192]{2,1,0:T(8,128)} %filt.3) | copy-start | bytes 2064388
  4.9 7.2 %collective-permute-start = (bf16[24,8192]{1,0:T(8,128)(2,1)S(1)}, bf16[24,8192]{1,0:T(8,128)(2,1)S(1)}, u32[]{:S(2)}, u32[]{:S(2)}) collective-permute-start(bf16[24,8192]{1,0:T(8,128)(2,1)S(1)} %get-tuple-element.51), channel_id=1, source_target_pairs={{1,2},{3,4},{5,6},{2,1},{4,3},{6,5},{9,10},{11,12},{13,14},{10,9},... | collective-permute-start | bytes 1179656 | tf_op jit(solution)/shard_map/ppermute | solution.py:436
  5.7 6.3 %collective-permute-start.1 = (bf16[24,8192]{1,0:T(8,128)(2,1)S(1)}, bf16[24,8192]{1,0:T(8,128)(2,1)S(1)}, u32[]{:S(2)}, u32[]{:S(2)}) collective-permute-start(bf16[24,8192]{1,0:T(8,128)(2,1)S(1)} %get-tuple-element.53), channel_id=1, source_target_pairs={{0,1},{1,0},{2,3},{3,2},{4,5},{5,4},{6,7},{7,6},{8,9},{9,8},{10,11... | collective-permute-start | bytes 1179656 | tf_op jit(solution)/shard_map/ppermute | solution.py:329
  12.0 22.4 %copy-start.2 = (bf16[24,8192]{1,0:T(8,128)(2,1)}, bf16[24,8192]{1,0:T(8,128)(2,1)S(1)}, u32[]{:S(2)}) copy-start(bf16[24,8192]{1,0:T(8,128)(2,1)S(1)} %collective-permute-done.1.hi) | copy-start | bytes 1179652
  12.1 32.0 %copy-start.6 = (f32[8192]{0:T(1024)S(1)}, f32[8192]{0:T(1024)}, u32[]{:S(2)}) copy-start(f32[8192]{0:T(1024)} %param.15) | copy-start | bytes 98308
  34.4 6.1 %collective-permute-start.2 = (f32[2,16,16,512]{3,2,1,0:T(8,128)}, f32[2,16,16,512]{3,2,1,0:T(8,128)}, u32[]{:S(2)}, u32[]{:S(2)}) collective-permute-start(f32[2,16,16,512]{3,2,1,0:T(8,128)} %get-tuple-element.56), channel_id=1, source_target_pairs={{0,1},{1,0},{2,3},{3,2},{4,5},{5,4},{6,7},{7,6},{8,9},{9,8},{10,11... | collective-permute-start | bytes 3145736 | tf_op jit(solution)/shard_map/ppermute | solution.py:329
  42.0 10.3 %collective-permute-start.3 = (f32[8,16,512]{2,1,0:T(8,128)S(1)}, f32[8,16,512]{2,1,0:T(8,128)S(1)}, u32[]{:S(2)}, u32[]{:S(2)}) collective-permute-start(f32[8,16,512]{2,1,0:T(8,128)S(1)} %broadcast_select_fusion.4), channel_id=1, source_target_pairs={{0,2},{1,3},{2,0},{3,1},{4,6},{5,7},{6,4},{7,5},{8,10},{9,11},{10,... | collective-permute-start | bytes 786440 | tf_op jit(solution)/shard_map/ppermute | solution.py:345
  52.5 6.5 %collective-permute-start.4 = (f32[8,16,512]{2,1,0:T(8,128)S(1)}, f32[8,16,512]{2,1,0:T(8,128)S(1)}, u32[]{:S(2)}, u32[]{:S(2)}) collective-permute-start(f32[8,16,512]{2,1,0:T(8,128)S(1)} %multiply_add_fusion.1), channel_id=1, source_target_pairs={{2,4},{3,5},{4,2},{5,3},{10,12},{11,13},{12,10},{13,11},{18,20},{1... | collective-permute-start | bytes 786440 | tf_op jit(solution)/shard_map/ppermute | solution.py:358
  59.0 14.1 %copy-start.3 = (bf16[24,8192]{1,0:T(8,128)(2,1)S(1)}, bf16[24,8192]{1,0:T(8,128)(2,1)}, u32[]{:S(2)}) copy-start(bf16[24,8192]{1,0:T(8,128)(2,1)} %copy-done.2) | copy-start | bytes 1179652
  59.0 14.1 %copy-start.4 = (f32[16,8,512]{2,1,0:T(8,128)S(1)}, f32[16,8,512]{2,1,0:T(8,128)}, u32[]{:S(2)}) copy-start(f32[16,8,512]{2,1,0:T(8,128)} %get-tuple-element.94.cy) | copy-start | bytes 786436
  59.0 14.1 %copy-start.5 = (f32[16,8,512]{2,1,0:T(8,128)S(1)}, f32[16,8,512]{2,1,0:T(8,128)}, u32[]{:S(2)}) copy-start(f32[16,8,512]{2,1,0:T(8,128)} %get-tuple-element.93.cz) | copy-start | bytes 786436
  59.0 12.0 %collective-permute-start.5 = (f32[8,16,512]{2,1,0:T(8,128)S(1)}, f32[8,16,512]{2,1,0:T(8,128)S(1)}, u32[]{:S(2)}, u32[]{:S(2)}) collective-permute-start(f32[8,16,512]{2,1,0:T(8,128)S(1)} %collective-permute-done.4), channel_id=1, source_target_pairs={{4,6},{5,7},{2,0},{3,1},{12,14},{13,15},{10,8},{11,9},{20,22},{21,... | collective-permute-start | bytes 786440 | tf_op jit(solution)/shard_map/ppermute | solution.py:361
  71.1 2.0 %collective-permute-start.6 = (f32[2,8,16,512]{3,2,1,0:T(8,128)S(1)}, f32[2,8,16,512]{3,2,1,0:T(8,128)S(1)}, u32[]{:S(2)}, u32[]{:S(2)}) collective-permute-start(f32[2,8,16,512]{3,2,1,0:T(8,128)S(1)} %pad_maximum_fusion.both), channel_id=1, source_target_pairs={{0,1},{1,0},{2,3},{3,2},{4,5},{5,4},{6,7},{7,6},{8,9},{9,8},{10,11... | collective-permute-start | bytes 1572872 | tf_op jit(solution)/shard_map/ppermute | solution.py:329
  104.5 1.8 %collective-permute-start.7 = (f32[16,24,256]{2,1,0:T(8,128)S(1)}, f32[16,24,256]{2,1,0:T(8,128)S(1)}, u32[]{:S(2)}, u32[]{:S(2)}) collective-permute-start(f32[16,24,256]{2,1,0:T(8,128)S(1)} %slice_select_fusion), channel_id=1, source_target_pairs={{0,1},{1,0},{2,3},{3,2},{4,5},{5,4},{6,7},{7,6},{8,9},{9,8},{10,11... | collective-permute-start | bytes 1179656 | tf_op jit(solution)/shard_map/ppermute | solution.py:329
  106.4 5.9 %collective-permute-start.10 = (f32[4,24,256]{2,1,0:T(8,128)S(1)}, f32[4,24,256]{2,1,0:T(8,128)S(1)}, u32[]{:S(2)}, u32[]{:S(2)}) collective-permute-start(f32[4,24,256]{2,1,0:T(8,128)S(1)} %get-tuple-element.111), channel_id=1, source_target_pairs={{0,24},{8,16},{16,8},{24,0},{1,25},{9,17},{17,9},{25,1},{2,26},{10... | collective-permute-start | bytes 294920 | tf_op jit(solution)/shard_map/ppermute | solution.py:345
  108.9 5.4 %collective-permute-start.9 = (f32[4,24,256]{2,1,0:T(8,128)S(1)}, f32[4,24,256]{2,1,0:T(8,128)S(1)}, u32[]{:S(2)}, u32[]{:S(2)}) collective-permute-start(f32[4,24,256]{2,1,0:T(8,128)S(1)} %get-tuple-element.112), channel_id=1, source_target_pairs={{0,16},{8,24},{16,0},{24,8},{1,17},{9,25},{17,1},{25,9},{2,18},{10... | collective-permute-start | bytes 294920 | tf_op jit(solution)/shard_map/ppermute | solution.py:345
  109.5 4.9 %collective-permute-start.8 = (f32[4,24,256]{2,1,0:T(8,128)S(1)}, f32[4,24,256]{2,1,0:T(8,128)S(1)}, u32[]{:S(2)}, u32[]{:S(2)}) collective-permute-start(f32[4,24,256]{2,1,0:T(8,128)S(1)} %get-tuple-element.110), channel_id=1, source_target_pairs={{0,8},{8,0},{16,24},{24,16},{1,9},{9,1},{17,25},{25,17},{2,10},{10... | collective-permute-start | bytes 294920 | tf_op jit(solution)/shard_map/ppermute | solution.py:345
  114.4 5.2 %collective-permute-start.11 = (f32[4,24,256]{2,1,0:T(8,128)S(1)}, f32[4,24,256]{2,1,0:T(8,128)S(1)}, u32[]{:S(2)}, u32[]{:S(2)}) collective-permute-start(f32[4,24,256]{2,1,0:T(8,128)S(1)} %add_add_fusion), channel_id=1, source_target_pairs={{0,2},{1,3},{2,0},{3,1},{4,6},{5,7},{6,4},{7,5},{8,10},{9,11},{10,... | collective-permute-start | bytes 294920 | tf_op jit(solution)/shard_map/ppermute | solution.py:345
  119.7 5.9 %collective-permute-start.12 = (f32[4,24,256]{2,1,0:T(8,128)S(1)}, f32[4,24,256]{2,1,0:T(8,128)S(1)}, u32[]{:S(2)}, u32[]{:S(2)}) collective-permute-start(f32[4,24,256]{2,1,0:T(8,128)S(1)} %add.64), channel_id=1, source_target_pairs={{0,4},{1,5},{2,6},{3,7},{4,0},{5,1},{6,2},{7,3},{8,12},{9,13},{10,... | collective-permute-start | bytes 294920 | tf_op jit(solution)/shard_map/ppermute | solution.py:345
  125.7 6.3 %collective-permute-start.13 = (f32[4,24,256]{2,1,0:T(8,128)S(1)}, f32[4,24,256]{2,1,0:T(8,128)S(1)}, u32[]{:S(2)}, u32[]{:S(2)}) collective-permute-start(f32[4,24,256]{2,1,0:T(8,128)S(1)} %get-tuple-element.99), channel_id=1, source_target_pairs={{0,8},{8,0},{16,24},{24,16},{1,9},{9,1},{17,25},{25,17},{2,10},{10... | collective-permute-start | bytes 294920 | tf_op jit(solution)/shard_map/ppermute | solution.py:345
  128.6 4.6 %collective-permute-start.14 = (f32[4,24,256]{2,1,0:T(8,128)S(1)}, f32[4,24,256]{2,1,0:T(8,128)S(1)}, u32[]{:S(2)}, u32[]{:S(2)}) collective-permute-start(f32[4,24,256]{2,1,0:T(8,128)S(1)} %get-tuple-element.99), channel_id=1, source_target_pairs={{0,16},{8,24},{16,0},{24,8},{1,17},{9,25},{17,1},{25,9},{2,18},{10... | collective-permute-start | bytes 294920 | tf_op jit(solution)/shard_map/ppermute | solution.py:345
  128.8 5.5 %collective-permute-start.15 = (f32[4,24,256]{2,1,0:T(8,128)S(1)}, f32[4,24,256]{2,1,0:T(8,128)S(1)}, u32[]{:S(2)}, u32[]{:S(2)}) collective-permute-start(f32[4,24,256]{2,1,0:T(8,128)S(1)} %get-tuple-element.99), channel_id=1, source_target_pairs={{0,24},{8,16},{16,8},{24,0},{1,25},{9,17},{17,9},{25,1},{2,26},{10... | collective-permute-start | bytes 294920 | tf_op jit(solution)/shard_map/ppermute | solution.py:345
  134.4 1.8 %collective-permute-start.16 = (f32[16,24,256]{2,1,0:T(8,128)S(1)}, f32[16,24,256]{2,1,0:T(8,128)S(1)}, u32[]{:S(2)}, u32[]{:S(2)}) collective-permute-start(f32[16,24,256]{2,1,0:T(8,128)S(1)} %constant_dynamic-update-slice_fusion), channel_id=1, source_target_pairs={{0,1},{1,0},{2,3},{3,2},{4,5},{5,4},{6,7},{7,6},{8,9},{9,8},{10,11... | collective-permute-start | bytes 1179656 | tf_op jit(solution)/shard_map/ppermute | solution.py:329
  136.7 0.9 copy-start.7

commit v17 on v15

--- a/solution.py
+++ b/solution.py
@@ -176,9 +176,50 @@
     lax.fori_loop(0, xg.shape[0] * tiles, tile, 0)
 
 
+def back_conv(row, tap, run, os):
+    even, odd, both = phases(tap)
+    reach = len(even)
+    known, joint = {}, {}
+
+    def get(a):
+        if a not in known:
+            known[a] = row(a) if a < run else pltpu.roll(row(a - run), SUB - 1, 0)
+        return known[a]
+
+    def pair(k):
+        if k not in joint:
+            joint[k] = get(2 * k + 1) + get(2 * k + 2)
+        return joint[k]
+
+    leading = weighted(even, [get(2 * k) for k in range(reach)])
+    for a in range(0, run, 2):
+        second = weighted(odd, [get(a + 2 * k + 1) for k in range(len(odd))])
+        os[pl.ds(a, SUB, stride=run), :] = leading + second
+        if a + 1 < run:
+            following = weighted(even, [get(a + 2 + 2 * k) for k in range(reach)])
+            total = weighted(both, [pair(a // 2 + k) for k in range(reach)])
+            os[pl.ds(a + 1, SUB, stride=run), :] = total - following - second
+            leading = following
+
+
+def later_kernel(later, filt, filled, grad_p, os):
+    rows = grad_p.shape[1]
+    run = (rows + SUB) // SUB
+
+    def tile(lt, carry):
+        lanes = pl.ds(pl.multiple_of(lt * LANES, LANES), LANES)
+        for j in range(3):
+            tap = [spread(filt[j, i : i + 1, lanes]) for i in range(filt.shape[1])]
+            back_conv(lambda a: later[0, j, SUB * a : SUB * a + SUB, lanes], tap, run, os)
+            grad_p[j, :, lanes] = os[0:rows].astype(BF16)
+        return carry
+
+    lax.fori_loop(0, grad_p.shape[2] // LANES, tile, 0)
+
+
 def final_kernel(
-    core, p, hx, hi, u, qkv, conv, from_e, from_a, skip_sum, both, found, other, filt, f1, f_all, cz, cy,
-    output, grad_p, sums, ps, us, gs, os, es,
+    here, core, p, hx, hi, u, qkv, conv, from_e, from_a, skip_sum, both, found, other, filt, f1, f_all, cz, cy,
+    output, grad_p, sums, later, ps, us, gs, os, es,
 ):
     rows = p.shape[1]
     run = (rows + SUB) // SUB
@@ -239,23 +280,16 @@
                 state = [state[n] * decay[n] for n in range(poles)]
 
         for j in range(3):
-            even, odd, paired_taps = phases([spread(filt[j, i : i + 1, lanes]) for i in range(taps)])
-            reach = len(even)
-            grads = [gs[j, SUB * a : SUB * a + SUB] for a in range(taps - 1)]
-            beyond = [pltpu.roll(value, SUB - 1, 0) for value in grads]
-
-            def ahead(a):
-                return gs[j, SUB * a : SUB * a + SUB] if a < run else beyond[a - run]
+            reach = (taps + 1) // 2
+            odd_count = taps // 2
 
             def behind(a):
                 return ps[j, pl.ds(SUB + a, SUB, stride=run), :]
 
             def own_rows(a):
-                return grads[a] if a < own else jnp.where(inside, grads[a], 0.0)
-
-            grads = {a: grads[a] for a in range(taps - 1)}
-            joint = {k: grads[2 * k + 1] + grads[2 * k + 2] for k in range((taps - 3) // 2)}
-            leading = weighted(even, [grads[2 * k] if 2 * k in grads else ahead(2 * k) for k in range(reach)])
+                value = gs[j, SUB * a : SUB * a + SUB]
+                return value if a < own else jnp.where(inside, value, 0.0)
+
             evens = [behind(-2 * k) for k in range(1, reach)]
             odds = [behind(1 - 2 * k) for k in range(1, reach)]
             pairs = [evens[k] + odds[k] for k in range(reach - 1)]
@@ -269,34 +303,34 @@
 
             previous = None
             for a in range(0, run, 2):
-                for c in range(a, a + 2 * reach + 1):
-                    if c not in grads and c < run + taps - 1:
-                        grads[c] = ahead(c)
-                here = own_rows(a)
-                collect(1, here if previous is None else here - previous, odds, len(odd))
-                second = weighted(odd, [grads[a + 2 * k + 1] for k in range(len(odd))])
-                os[pl.ds(a, SUB, stride=run), :] = leading + second
+                current = own_rows(a)
+                collect(1, current if previous is None else current - previous, odds, odd_count)
                 evens = [behind(a)] + evens[: reach - 1]
                 if a + 1 < run:
                     previous = own_rows(a + 1)
-                    for k in range(a // 2, a // 2 + reach):
-                        if k not in joint:
-                            joint[k] = grads[2 * k + 1] + grads[2 * k + 2]
-                    following = weighted(even, [grads[a + 2 + 2 * k] for k in range(reach)])
-                    total = weighted(paired_taps, [joint[a // 2 + k] for k in range(reach)])
-                    os[pl.ds(a + 1, SUB, stride=run), :] = total - following - second
-                    leading = following
                     odds = [behind(a + 1)] + odds[: reach - 1]
                     pairs = [evens[0] + odds[0]] + pairs[: reach - 1]
-                    collect(0, here - previous, evens, reach)
+                    collect(0, current - previous, evens, reach)
                     collect(2, previous, pairs, reach)
                 else:
-                    collect(0, here, evens, reach)
+                    collect(0, current, evens, reach)
             sums_of = [sums_of[i % 2][i // 2] + sums_of[2][i // 2] for i in range(taps)]
-            grad_p[j, :, lanes] = os[0:rows].astype(BF16)
             extra = [skip_sum[which, :, part]] + [jnp.zeros((SUB, LANES), F32)] * (SUB - taps)
             extra = extra[: SUB - taps] if j == 0 else extra[1 : SUB - taps + 1]
             sums[piece, j * SUB : j * SUB + SUB, spot] = folded(sums_of + extra)
+
+        @pl.when(pl.program_id(0) < here)
+        def _():
+            for j in range(3):
+                tap = [spread(filt[j, i : i + 1, lanes]) for i in range(taps)]
+                back_conv(lambda a: gs[j, SUB * a : SUB * a + SUB], tap, run, os)
+                grad_p[j, :, lanes] = os[0:rows].astype(BF16)
+
+        @pl.when(pl.program_id(0) >= here)
+        def _():
+            for j in range(3):
+                later[which, j, :, part] = gs[j]
+
         return carry
 
     lax.fori_loop(0, p.shape[2] // LANES, tile, 0)
@@ -360,7 +394,7 @@
     return before, after, kept
 
 
-def summed(value):
+def summed(value, beside, kept):
     dp, parts = lax.axis_index("dp"), lax.axis_size("dp")
     low = lax.rem(lax.axis_index("ctx"), 2) == 0
     half = value.shape[0] // 2
@@ -371,17 +405,24 @@
     total = piece(0)
     for term in [paired(piece(k), "dp", k) for k in range(1, parts)]:
         total = total + term
-    count = lax.axis_size("ctx")
-    reaches = [2 << k for k in range((count // 2).bit_length() - 1)]
-    for near, far in zip(reaches, reversed(reaches)):
-        pairs = [(s, s ^ (far if s % 2 else near)) for s in range(count)]
-        total = total + lax.ppermute(total, "ctx", pairs)
+    reach = 2
+    beside = list(beside)
+    while reach < lax.axis_size("ctx"):
+        found = paired(total, "ctx", reach)
+        if beside:
+            kept = beside.pop(0)(total, kept)
+            found, kept = lax.optimization_barrier((found, kept))
+        total = total + found
+        reach = 2 * reach
+    for rest in beside:
+        kept = rest(total, kept)
     value = jnp.zeros((half,) + value.shape[1:], F32)
     for k in range(parts):
         term = paired(total, "dp", k) if k else total
         value = lax.dynamic_update_slice_in_dim(value, term, jnp.bitwise_xor(dp, k) * size, 0)
     other = swapped(value)
-    return jnp.concatenate([jnp.where(low, value, other), jnp.where(low, other, value)], axis=0)
+    value = jnp.concatenate([jnp.where(low, value, other), jnp.where(low, other, value)], axis=0)
+    return value, kept
 
 
 def local(projected, short_filter, residues, decay_rates, skip_gain, cotangent):
@@ -524,8 +565,9 @@
         pltpu.VMEM((held, LANES), F32),
         pltpu.VMEM((2, poles, LANES), F32),
     ]
-    output, grad_p, sums = pl.pallas_call(
-        final_kernel,
+    here = width // 2
+    output, grad_p, sums, later = pl.pallas_call(
+        functools.partial(final_kernel, here),
         grid=(width // each,),
         in_specs=[
             pl.BlockSpec(memory_space=pltpu.SMEM),
@@ -535,13 +577,16 @@
             by_w(3, taps), fixed(f1), fixed(f_all), fixed(cz), fixed(cy),
         ],
         out_specs=[
-            by_w(rows), by_w(3, rows),
+            by_w(rows),
+            pl.BlockSpec((3, rows, groups), lambda w: (0, 0, jnp.minimum(w, here - 1))),
             pl.BlockSpec((each * split, count, groups // split), lambda w: (w, 0, 0)),
+            pl.BlockSpec((1, 3, held, groups), lambda w: (jnp.maximum(w - here, 0), 0, 0, 0)),
         ],
         out_shape=[
             shape_of((rows, channels), BF16),
             shape_of((3, rows, channels), BF16),
             shape_of((width * split, count, groups // split), F32),
+            shape_of((width - here, 3, held, groups), F32),
         ],
         scratch_shapes=scratch,
         compiler_params=params,
@@ -551,7 +596,33 @@
         f1, f_all, cz, cy,
     )
 
-    total = summed(sums).transpose(1, 0, 2).reshape(3, SUB, channels)
+    def rest(first, last):
+        def call(sent, filled):
+            tap, _ = lax.optimization_barrier((short_filter, sent))
+            return pl.pallas_call(
+                later_kernel,
+                grid=(last - first,),
+                in_specs=[
+                    pl.BlockSpec((1, 3, held, groups), lambda w: (w + first, 0, 0, 0)),
+                    pl.BlockSpec((3, taps, groups), lambda w: (0, 0, w + first + here)),
+                    pl.BlockSpec(memory_space=pl.ANY),
+                ],
+                out_specs=pl.BlockSpec((3, rows, groups), lambda w: (0, 0, w + first + here)),
+                out_shape=shape_of((3, rows, channels), BF16),
+                input_output_aliases={2: 0},
+                scratch_shapes=[pltpu.VMEM((held, LANES), F32)],
+                compiler_params=params,
+                cost_estimate=pl.CostEstimate(
+                    flops=40 * rows * channels // 4, bytes_accessed=5 * 2**20, transcendentals=0
+                ),
+                name="later",
+            )(later, tap, filled)
+
+        return call
+
+    middle = (width - here) // 2
+    total, grad_p = summed(sums, (rest(0, middle), rest(middle, width - here)), grad_p)
+    total = total.transpose(1, 0, 2).reshape(3, SUB, channels)
     grad_short, grad_skip = total[:, :taps], total[0, taps]
     return output[None], grad_p.transpose(1, 0, 2)[None], grad_short, grad_skip
 

time: 137 us -> 142 us (1.036)
  Pallas kernels: 75.9 us -> 85.8 us
  starting transfers between devices: 26.6 us -> 21 us
  waiting for transfers between devices: 25.4 us -> 20.6 us
  other arithmetic: 3.86 us -> 8.23 us
    pallas_call x1 -> x3, Pallas kernels: 31.5 us -> 41.2 us  [the longest x1 31.6 us: local(): pl.pallas_call(functools.partial(final_kernel, here), grid=(width // each...]
    ppermute x2 -> x0, waiting for transfers between devices: 6.94 us -> none  [summed(): total = total + lax.ppermute(total, 'ctx', pairs)]
    ppermute x2 -> x0, starting transfers between devices: 4.74 us -> none  [summed(): total = total + lax.ppermute(total, 'ctx', pairs)]
    ppermute x5, starting transfers between devices: 9.73 us -> 5.25 us  [swapped(): return lax.ppermute(value, 'ctx', [(s, s ^ 1) for s in range(count)])]
    ppermute x7 -> x9, starting transfers between devices: 9.16 us -> 12.9 us  [paired(): lax.ppermute(value, axis, [(source, source ^ step) for source in lines or...]
    ppermute x7 -> x9, waiting for transfers between devices: 8.19 us -> 10.4 us  [paired(): lax.ppermute(value, axis, [(source, source ^ step) for source in lines or...]
  transfers between devices with their start and end apart: 17 -> 17, of which waited for: 13 -> 11; matrix products, arithmetic and copies ran while one was open for 1% -> 4% of each run, Pallas kernels for 16% -> 23%
where the time goes in v17:
time: 142 us; the launch traced here: 140 us
  Pallas kernels  85.8 us (60%)
  starting transfers between devices  21 us (15%)
  waiting for transfers between devices  20.6 us (15%)
  other arithmetic  8.23 us (6%)
  local copies, waits for them, and re-layouts  3.79 us (3%)
    pallas_call x1, Pallas kernels, local(): pl.pallas_call(functools.partial(final_kernel, here), grid=(width // each...  31.6 us
    pallas_call x1, Pallas kernels, local(): pl.pallas_call(states_kernel, grid=(width // each,), in_specs=[pl.BlockSp...  22.4 us
    pallas_call x3, Pallas kernels, call(): pl.pallas_call(blocks_kernel, grid=(last - first,), in_specs=[pairs, stat...  22.2 us
    ppermute x9, starting transfers between devices, paired(): lax.ppermute(value, axis, [(source, source ^ step) for source in lines or...  12.9 us
    ppermute x9, waiting for transfers between devices, paired(): lax.ppermute(value, axis, [(source, source ^ step) for source in lines or...  10.4 us
    pallas_call x2, Pallas kernels, call(): pl.pallas_call(later_kernel, grid=(last - first,), in_specs=[pl.BlockSpec...  9.61 us
    ppermute x5, waiting for transfers between devices, swapped(): return lax.ppermute(value, 'ctx', [(s, s ^ 1) for s in range(count)])  7.85 us
    ppermute x5, starting transfers between devices, swapped(): return lax.ppermute(value, 'ctx', [(s, s ^ 1) for s in range(count)])  5.25 us
  transfers between devices with their start and end apart: 17, of which 11 were waited for; matrix products, arithmetic and copies ran while one was open for 4% of the time, Pallas kernels for 23%

profile of v17, /device:TPU:0, one launch (start us, length us, event | category | flops | bytes accessed | tf_op | source)
XLA Modules:
  0.0 140.5 jit_solution(18232088756111849493)
XLA Ops:
  0.6 0.0 copy-start.9
  0.6 0.0 copy-start.10
  0.7 0.0 copy-start.8
  0.7 0.0 copy-start.1
  0.7 1.1 constant_dynamic-slice_fusion.3
  1.8 1.2 dynamic-slice_bitcast_fusion
  3.1 0.7 collective-permute-start
  3.8 4.4 %collective-permute-start.1 = (bf16[4,8,8192]{2,1,0:T(8,128)(2,1)S(1)}, bf16[4,8,8192]{2,1,0:T(8,128)(2,1)S(1)}, u32[]{:S(2)}, u32[]{:S(2)}) collective-permute-start(bf16[4,8,8192]{2,1,0:T(8,128)(2,1)S(1)} %pad_maximum_fusion.1), channel_id=1, source_target_pairs={{0,1},{1,0},{2,3},{3,2},{4,5},{5,4},{6,7},{7,6},{8,9},{9,8},{10,11... | collective-permute-start | bytes 1572872 | tf_op jit(solution)/shard_map/ppermute | solution.py:347
  8.3 0.8 negate_bitcast_fusion
  9.0 0.8 fusion.6
  9.8 0.8 multiply_exponential_fusion.1
  10.6 0.8 slice_multiply_fusion
  11.3 0.9 multiply_exponential_fusion
  12.2 1.0 multiply_reduce_fusion.near
  13.2 0.8 fusion.4
  14.2 0.3 broadcast_select_fusion
  14.5 0.0 copy-start.2
  14.5 0.0 copy-start.6
  14.6 22.4 %states.1 = (f32[16,3,136,512]{3,2,1,0:T(8,128)}, f32[16,2,136,512]{3,2,1,0:T(8,128)}, f32[16,16,8,512]{3,2,1,0:T(8,128)}, f32[16,16,8,512]{3,2,1,0:T(8,128)}, f32[2,16,16,512]{3,2,1,0:T(8,128)}) custom-call(s32[1]{0:T(128)} %bitcast.core, bf16[3,128,8192]{2,1,0:T(8,128)(2,1)} %bitcast.89, bf16[4,8,8192]{2,1,0:T(8,128)(2,1)S(1)} %collective-permute-done.hx, ...), custom_call_target="tpu_custom_call" | custom-call | tf_op jit(solution)/shard_map/states/pallas_call | solution.py:496
  36.9 0.5 collective-permute-start.2
  37.4 2.6 %collective-permute-done.2.other = f32[2,16,16,512]{3,2,1,0:T(8,128)} collective-permute-done((f32[2,16,16,512]{3,2,1,0:T(8,128)}, f32[2,16,16,512]{3,2,1,0:T(8,128)}, u32[]{:S(2)}, u32[]{:S(2)}) %collective-permute-start.2) | collective-permute-done | bytes 1048608 | tf_op jit(solution)/shard_map/ppermute | solution.py:347
  40.1 1.3 dynamic-slice_select_fusion.1
  41.4 0.1 broadcast_select_fusion.4
  41.5 2.1 %collective-permute-start.3 = (f32[8,16,512]{2,1,0:T(8,128)S(1)}, f32[8,16,512]{2,1,0:T(8,128)S(1)}, u32[]{:S(2)}, u32[]{:S(2)}) collective-permute-start(f32[8,16,512]{2,1,0:T(8,128)S(1)} %broadcast_select_fusion.4), channel_id=1, source_target_pairs={{0,2},{1,3},{2,0},{3,1},{4,6},{5,7},{6,4},{7,5},{8,10},{9,11},{10,... | collective-permute-start | bytes 786440 | tf_op jit(solution)/shard_map/ppermute | solution.py:363
  43.6 8.2 %blocks.3 = (f32[16,2,136,512]{3,2,1,0:T(8,128)}, f32[16,16,8,512]{3,2,1,0:T(8,128)}, f32[16,16,8,512]{3,2,1,0:T(8,128)}, f32[6,8,512]{2,1,0:T(8,128)S(1)}) custom-call(f32[16,2,136,512]{3,2,1,0:T(8,128)} %get-tuple-element.60.xg, f32[16,16,8,512]{3,2,1,0:T(8,128)} %get-tuple-element.61.blocks_e, ...), custom_call_target="tpu_custom_call", output_to_operand_aliasing={{0}: (0, {}), {1}: (1, {}), {2}: (2, {})} | custom-call | flops 62914560 | bytes 36700160 | tf_op jit(solution)/shard_map/blocks/pallas_call | solution.py:526
  51.8 0.1 multiply_add_fusion.1
  52.0 0.7 collective-permute-start.4
  52.7 5.8 %blocks.4 = (f32[16,2,136,512]{3,2,1,0:T(8,128)}, f32[16,16,8,512]{3,2,1,0:T(8,128)}, f32[16,16,8,512]{3,2,1,0:T(8,128)}, f32[4,8,512]{2,1,0:T(8,128)S(1)}) custom-call(f32[16,2,136,512]{3,2,1,0:T(8,128)} %get-tuple-element.72.xg, f32[16,16,8,512]{3,2,1,0:T(8,128)} %get-tuple-element.73.blocks_e, ...), custom_call_target="tpu_custom_call", output_to_operand_aliasing={{0}: (0, {}), {1}: (1, {}), {2}: (2, {})} | custom-call | flops 62914560 | bytes 36700160 | tf_op jit(solution)/shard_map/blocks/pallas_call | solution.py:526
  58.6 1.4 %collective-permute-start.5 = (f32[8,16,512]{2,1,0:T(8,128)S(1)}, f32[8,16,512]{2,1,0:T(8,128)S(1)}, u32[]{:S(2)}, u32[]{:S(2)}) collective-permute-start(f32[8,16,512]{2,1,0:T(8,128)S(1)} %collective-permute-done.4), channel_id=1, source_target_pairs={{4,6},{5,7},{2,0},{3,1},{12,14},{13,15},{10,8},{11,9},{20,22},{21,... | collective-permute-start | bytes 786440 | tf_op jit(solution)/shard_map/ppermute | solution.py:379
  60.0 8.1 %blocks.5 = (f32[16,2,136,512]{3,2,1,0:T(8,128)}, f32[16,16,8,512]{3,2,1,0:T(8,128)}, f32[16,16,8,512]{3,2,1,0:T(8,128)}, f32[6,8,512]{2,1,0:T(8,128)S(1)}) custom-call(f32[16,2,136,512]{3,2,1,0:T(8,128)} %get-tuple-element.82.xg, f32[16,16,8,512]{3,2,1,0:T(8,128)} %get-tuple-element.83.blocks_e, ...), custom_call_target="tpu_custom_call", output_to_operand_aliasing={{0}: (0, {}), {1}: (1, {}), {2}: (2, {})} | custom-call | flops 62914560 | bytes 36700160 | tf_op jit(solution)/shard_map/blocks/pallas_call | solution.py:526
  68.1 2.4 %collective-permute-done.5 = f32[8,16,512]{2,1,0:T(8,128)S(1)} collective-permute-done((f32[8,16,512]{2,1,0:T(8,128)S(1)}, f32[8,16,512]{2,1,0:T(8,128)S(1)}, u32[]{:S(2)}, u32[]{:S(2)}) %collective-permute-start.5) | collective-permute-done | bytes 262176 | tf_op jit(solution)/shard_map/ppermute | solution.py:379
  70.5 0.1 select_bitcast_fusion.1
  70.7 0.1 collective-permute-start.6
  70.7 1.9 %collective-permute-done.6.found = f32[2,8,16,512]{3,2,1,0:T(8,128)S(1)} collective-permute-done((f32[2,8,16,512]{3,2,1,0:T(8,128)S(1)}, f32[2,8,16,512]{3,2,1,0:T(8,128)S(1)}, u32[]{:S(2)}, u32[]{:S(2)}) %collective-permute-start.6) | collective-permute-done | bytes 524320 | tf_op jit(solution)/shard_map/ppermute | solution.py:347
  72.6 31.6 %final.1 = (bf16[128,8192]{1,0:T(8,128)(2,1)}, bf16[3,128,8192]{2,1,0:T(8,128)(2,1)}, f32[32,24,256]{2,1,0:T(8,128)S(1)}, f32[8,3,136,512]{3,2,1,0:T(8,128)}) custom-call(s32[1]{0:T(128)} %bitcast.core, bf16[3,128,8192]{2,1,0:T(8,128)(2,1)} %bitcast.90, bf16[4,8,8192]{2,1,0:T(8,128)(2,1)S(1)} %collective-permute-done.hx, bf16[4,8,8192]{2,1,0:T(8,128)(2,1)S(1)} %copy-done.3, ...), custom_call_target="tpu_custom_call" | custom-call | tf_op jit(solution)/shard_map/final/pallas_call | solution.py:569
  104.2 0.1 slice_select_fusion
  104.3 0.2 collective-permute-start.7
  104.5 1.6 %collective-permute-done.7 = f32[16,24,256]{2,1,0:T(8,128)S(1)} collective-permute-done((f32[16,24,256]{2,1,0:T(8,128)S(1)}, f32[16,24,256]{2,1,0:T(8,128)S(1)}, u32[]{:S(2)}, u32[]{:S(2)}) %collective-permute-start.7) | collective-permute-done | bytes 393248 | tf_op jit(solution)/shard_map/ppermute | solution.py:347
  106.1 0.1 select_add_fusion
  106.2 2.5 %collective-permute-start.10 = (f32[4,24,256]{2,1,0:T(8,128)S(1)}, f32[4,24,256]{2,1,0:T(8,128)S(1)}, u32[]{:S(2)}, u32[]{:S(2)}) collective-permute-start(f32[4,24,256]{2,1,0:T(8,128)S(1)} %get-tuple-element.125), channel_id=1, source_target_pairs={{0,24},{8,16},{16,8},{24,0},{1,25},{9,17},{17,9},{25,1},{2,26},{10... | collective-permute-start | bytes 294920 | tf_op jit(solution)/shard_map/ppermute | solution.py:363
  108.7 0.5 collective-permute-start.9
  109.2 0.5 collective-permute-start.8
  109.8 2.3 %collective-permute-done.10 = f32[4,24,256]{2,1,0:T(8,128)S(1)} collective-permute-done((f32[4,24,256]{2,1,0:T(8,128)S(1)}, f32[4,24,256]{2,1,0:T(8,128)S(1)}, u32[]{:S(2)}, u32[]{:S(2)}) %collective-permute-start.10) | collective-permute-done | bytes 98336 | tf_op jit(solution)/shard_map/ppermute | solution.py:363
  112.1 2.0 %collective-permute-done.9 = f32[4,24,256]{2,1,0:T(8,128)S(1)} collective-permute-done((f32[4,24,256]{2,1,0:T(8,128)S(1)}, f32[4,24,256]{2,1,0:T(8,128)S(1)}, u32[]{:S(2)}, u32[]{:S(2)}) %collective-permute-start.9) | collective-permute-done | bytes 98336 | tf_op jit(solution)/shard_map/ppermute | solution.py:363
  114.1 0.1 collective-permute-done.8
  114.2 2.5 %collective-permute-start.11 = (f32[4,24,256]{2,1,0:T(8,128)S(1)}, f32[4,24,256]{2,1,0:T(8,128)S(1)}, u32[]{:S(2)}, u32[]{:S(2)}) collective-permute-start(f32[4,24,256]{2,1,0:T(8,128)S(1)} %add_add_fusion), channel_id=1, source_target_pairs={{0,2},{1,3},{2,0},{3,1},{4,6},{5,7},{6,4},{7,5},{8,10},{9,11},{10,... | collective-permute-start | bytes 294920 | tf_op jit(solution)/shard_map/ppermute | solution.py:363
  116.7 4.8 %later.2.filled = bf16[3,128,8192]{2,1,0:T(8,128)(2,1)} custom-call(f32[8,3,136,512]{3,2,1,0:T(8,128)} %get-tuple-element.100.later, f32[3,7,8192]{2,1,0:T(8,128)S(1)} %copy-done, bf16[3,128,8192]{2,1,0:T(8,128)(2,1)} %get-tuple-element.102.filled), custom_call_target="tpu_custom_call", output_to_operand_aliasing={{}: (2, {})} | custom-call | flops 10485760 | bytes 5242880 | tf_op jit(solution)/shard_map/later/pallas_call | solution.py:602
  121.5 1.3 collective-permute-start.12
  122.8 4.8 %later.3 = bf16[3,128,8192]{2,1,0:T(8,128)(2,1)} custom-call(f32[8,3,136,512]{3,2,1,0:T(8,128)} %get-tuple-element.100.later, f32[3,7,8192]{2,1,0:T(8,128)S(1)} %copy-done, bf16[3,128,8192]{2,1,0:T(8,128)(2,1)} %later.2.filled), custom_call_target="tpu_custom_call", output_to_operand_aliasing={{}: (2, {})} | custom-call | flops 10485760 | bytes 5242880 | tf_op jit(solution)/shard_map/later/pallas_call | solution.py:602
  127.6 1.2 collective-permute-done.12
  128.8 1.7 %collective-permute-start.13 = (f32[4,24,256]{2,1,0:T(8,128)S(1)}, f32[4,24,256]{2,1,0:T(8,128)S(1)}, u32[]{:S(2)}, u32[]{:S(2)}) collective-permute-start(f32[4,24,256]{2,1,0:T(8,128)S(1)} %get-tuple-element.109), channel_id=1, source_target_pairs={{0,8},{8,0},{16,24},{24,16},{1,9},{9,1},{17,25},{25,17},{2,10},{10... | collective-permute-start | bytes 294920 | tf_op jit(solution)/shard_map/ppermute | solution.py:363
  130.6 0.1 collective-permute-start.14
  130.7 1.7 %collective-permute-start.15 = (f32[4,24,256]{2,1,0:T(8,128)S(1)}, f32[4,24,256]{2,1,0:T(8,128)S(1)}, u32[]{:S(2)}, u32[]{:S(2)}) collective-permute-start(f32[4,24,256]{2,1,0:T(8,128)S(1)} %get-tuple-element.109), channel_id=1, source_target_pairs={{0,24},{8,16},{16,8},{24,0},{1,25},{9,17},{17,9},{25,1},{2,26},{10... | collective-permute-start | bytes 294920 | tf_op jit(solution)/shard_map/ppermute | solution.py:363
  132.4 1.3 collective-permute-done.13
  133.7 3.5 %collective-permute-done.14 = f32[4,24,256]{2,1,0:T(8,128)S(1)} collective-permute-done((f32[4,24,256]{2,1,0:T(8,128)S(1)}, f32[4,24,256]{2,1,0:T(8,128)S(1)}, u32[]{:S(2)}, u32[]{:S(2)}) %collective-permute-start.14) | collective-permute-done | bytes 98336 | tf_op jit(solution)/shard_map/ppermute | solution.py:363
  137.2 0.1 collective-permute-start.16
  137.3 1.7 %collective-permute-done.16 = f32[16,24,256]{2,1,0:T(8,128)S(1)} collective-permute-done((f32[16,24,256]{2,1,0:T(8,128)S(1)}, f32[16,24,256]{2,1,0:T(8,128)S(1)}, u32[]{:S(2)}, u32[]{:S(2)}) %collective-permute-start.16) | collective-permute-done | bytes 393248 | tf_op jit(solution)/shard_map/ppermute | solution.py:347
  139.0 0.1 broadcast_select_fusion.3
  139.1 0.1 maximum_bitcast_fusion
  139.1 0.3 copy.27
  139.4 0.1 reshape.33
  139.6 0.0 copy-start.7
  139.6 0.7 slice.67
  140.3 0.2 copy-done.7
  (37 shorter events, 0.4 us)
Async XLA Ops:
  0.6 13.5 %copy-start.9 = (pred[4,8]{1,0:T(4,128)(4,1)S(1)}, pred[4,8]{1,0:T(4,128)(4,1)}, u32[]{:S(2)}) copy-start(pred[4,8]{1,0:T(4,128)(4,1)} %constant.69) | copy-start | bytes 100
  0.6 13.5 %copy-start.10 = (pred[4,8]{1,0:T(4,128)(4,1)S(1)}, pred[4,8]{1,0:T(4,128)(4,1)}, u32[]{:S(2)}) copy-start(pred[4,8]{1,0:T(4,128)(4,1)} %constant.67) | copy-start | bytes 100
  0.7 12.6 %copy-start.8 = (f32[512,16]{0,1:T(8,128)S(1)}, f32[512,16]{0,1:T(8,128)}, u32[]{:S(2)}) copy-start(f32[512,16]{0,1:T(8,128)} %param.13) | copy-start | bytes 98308
  0.7 13.9 %copy-start = (f32[3,7,8192]{2,1,0:T(8,128)S(1)}, f32[3,7,8192]{2,1,0:T(8,128)}, u32[]{:S(2)}) copy-start(f32[3,7,8192]{2,1,0:T(8,128)} %filt.5) | copy-start | bytes 2064388
  0.7 13.8 %copy-start.1 = (bf16[1,128,8192]{2,1,0:T(8,128)(2,1)S(1)}, bf16[1,128,8192]{2,1,0:T(8,128)(2,1)}, u32[]{:S(2)}) copy-start(bf16[1,128,8192]{2,1,0:T(8,128)(2,1)} %param.16) | copy-start | bytes 6291460
  3.1 11.4 %collective-permute-start = (bf16[4,8,8192]{2,1,0:T(8,128)(2,1)S(1)}, bf16[4,8,8192]{2,1,0:T(8,128)(2,1)S(1)}, u32[]{:S(2)}, u32[]{:S(2)}) collective-permute-start(bf16[4,8,8192]{2,1,0:T(8,128)(2,1)S(1)} %pad_maximum_fusion), channel_id=1, source_target_pairs={{1,2},{3,4},{5,6},{2,1},{4,3},{6,5},{9,10},{11,12},{13,14},{10,9},... | collective-permute-start | bytes 1572872 | tf_op jit(solution)/shard_map/ppermute | solution.py:448
  3.8 10.7 %collective-permute-start.1 = (bf16[4,8,8192]{2,1,0:T(8,128)(2,1)S(1)}, bf16[4,8,8192]{2,1,0:T(8,128)(2,1)S(1)}, u32[]{:S(2)}, u32[]{:S(2)}) collective-permute-start(bf16[4,8,8192]{2,1,0:T(8,128)(2,1)S(1)} %pad_maximum_fusion.1), channel_id=1, source_target_pairs={{0,1},{1,0},{2,3},{3,2},{4,5},{5,4},{6,7},{7,6},{8,9},{9,8},{10,11... | collective-permute-start | bytes 1572872 | tf_op jit(solution)/shard_map/ppermute | solution.py:347
  14.5 22.4 %copy-start.2 = (bf16[4,8,8192]{2,1,0:T(8,128)(2,1)}, bf16[4,8,8192]{2,1,0:T(8,128)(2,1)S(1)}, u32[]{:S(2)}) copy-start(bf16[4,8,8192]{2,1,0:T(8,128)(2,1)S(1)} %collective-permute-done.1.hi) | copy-start | bytes 1572868
  14.5 29.0 %copy-start.6 = (f32[8192]{0:T(1024)S(1)}, f32[8192]{0:T(1024)}, u32[]{:S(2)}) copy-start(f32[8192]{0:T(1024)} %param.15) | copy-start | bytes 98308
  36.9 3.1 %collective-permute-start.2 = (f32[2,16,16,512]{3,2,1,0:T(8,128)}, f32[2,16,16,512]{3,2,1,0:T(8,128)}, u32[]{:S(2)}, u32[]{:S(2)}) collective-permute-start(f32[2,16,16,512]{3,2,1,0:T(8,128)} %get-tuple-element.59), channel_id=1, source_target_pairs={{0,1},{1,0},{2,3},{3,2},{4,5},{5,4},{6,7},{7,6},{8,9},{9,8},{10,11... | collective-permute-start | bytes 3145736 | tf_op jit(solution)/shard_map/ppermute | solution.py:347
  41.5 10.3 %collective-permute-start.3 = (f32[8,16,512]{2,1,0:T(8,128)S(1)}, f32[8,16,512]{2,1,0:T(8,128)S(1)}, u32[]{:S(2)}, u32[]{:S(2)}) collective-permute-start(f32[8,16,512]{2,1,0:T(8,128)S(1)} %broadcast_select_fusion.4), channel_id=1, source_target_pairs={{0,2},{1,3},{2,0},{3,1},{4,6},{5,7},{6,4},{7,5},{8,10},{9,11},{10,... | collective-permute-start | bytes 786440 | tf_op jit(solution)/shard_map/ppermute | solution.py:363
  52.0 6.5 %collective-permute-start.4 = (f32[8,16,512]{2,1,0:T(8,128)S(1)}, f32[8,16,512]{2,1,0:T(8,128)S(1)}, u32[]{:S(2)}, u32[]{:S(2)}) collective-permute-start(f32[8,16,512]{2,1,0:T(8,128)S(1)} %multiply_add_fusion.1), channel_id=1, source_target_pairs={{2,4},{3,5},{4,2},{5,3},{10,12},{11,13},{12,10},{13,11},{18,20},{1... | collective-permute-start | bytes 786440 | tf_op jit(solution)/shard_map/ppermute | solution.py:376
  58.5 14.1 %copy-start.3 = (bf16[4,8,8192]{2,1,0:T(8,128)(2,1)S(1)}, bf16[4,8,8192]{2,1,0:T(8,128)(2,1)}, u32[]{:S(2)}) copy-start(bf16[4,8,8192]{2,1,0:T(8,128)(2,1)} %copy-done.2) | copy-start | bytes 1572868
  58.5 14.1 %copy-start.4 = (f32[16,8,512]{2,1,0:T(8,128)S(1)}, f32[16,8,512]{2,1,0:T(8,128)}, u32[]{:S(2)}) copy-start(f32[16,8,512]{2,1,0:T(8,128)} %get-tuple-element.97.cy) | copy-start | bytes 786436
  58.5 14.1 %copy-start.5 = (f32[16,8,512]{2,1,0:T(8,128)S(1)}, f32[16,8,512]{2,1,0:T(8,128)}, u32[]{:S(2)}) copy-start(f32[16,8,512]{2,1,0:T(8,128)} %get-tuple-element.96.cz) | copy-start | bytes 786436
  58.6 12.0 %collective-permute-start.5 = (f32[8,16,512]{2,1,0:T(8,128)S(1)}, f32[8,16,512]{2,1,0:T(8,128)S(1)}, u32[]{:S(2)}, u32[]{:S(2)}) collective-permute-start(f32[8,16,512]{2,1,0:T(8,128)S(1)} %collective-permute-done.4), channel_id=1, source_target_pairs={{4,6},{5,7},{2,0},{3,1},{12,14},{13,15},{10,8},{11,9},{20,22},{21,... | collective-permute-start | bytes 786440 | tf_op jit(solution)/shard_map/ppermute | solution.py:379
  70.7 2.0 %collective-permute-start.6 = (f32[2,8,16,512]{3,2,1,0:T(8,128)S(1)}, f32[2,8,16,512]{3,2,1,0:T(8,128)S(1)}, u32[]{:S(2)}, u32[]{:S(2)}) collective-permute-start(f32[2,8,16,512]{3,2,1,0:T(8,128)S(1)} %pad_maximum_fusion.2.both), channel_id=1, source_target_pairs={{0,1},{1,0},{2,3},{3,2},{4,5},{5,4},{6,7},{7,6},{8,9},{9,8},{10,11... | collective-permute-start | bytes 1572872 | tf_op jit(solution)/shard_map/ppermute | solution.py:347
  104.3 1.8 %collective-permute-start.7 = (f32[16,24,256]{2,1,0:T(8,128)S(1)}, f32[16,24,256]{2,1,0:T(8,128)S(1)}, u32[]{:S(2)}, u32[]{:S(2)}) collective-permute-start(f32[16,24,256]{2,1,0:T(8,128)S(1)} %slice_select_fusion), channel_id=1, source_target_pairs={{0,1},{1,0},{2,3},{3,2},{4,5},{5,4},{6,7},{7,6},{8,9},{9,8},{10,11... | collective-permute-start | bytes 1179656 | tf_op jit(solution)/shard_map/ppermute | solution.py:347
  106.2 5.9 %collective-permute-start.10 = (f32[4,24,256]{2,1,0:T(8,128)S(1)}, f32[4,24,256]{2,1,0:T(8,128)S(1)}, u32[]{:S(2)}, u32[]{:S(2)}) collective-permute-start(f32[4,24,256]{2,1,0:T(8,128)S(1)} %get-tuple-element.125), channel_id=1, source_target_pairs={{0,24},{8,16},{16,8},{24,0},{1,25},{9,17},{17,9},{25,1},{2,26},{10... | collective-permute-start | bytes 294920 | tf_op jit(solution)/shard_map/ppermute | solution.py:363
  108.7 5.4 %collective-permute-start.9 = (f32[4,24,256]{2,1,0:T(8,128)S(1)}, f32[4,24,256]{2,1,0:T(8,128)S(1)}, u32[]{:S(2)}, u32[]{:S(2)}) collective-permute-start(f32[4,24,256]{2,1,0:T(8,128)S(1)} %get-tuple-element.126), channel_id=1, source_target_pairs={{0,16},{8,24},{16,0},{24,8},{1,17},{9,25},{17,1},{25,9},{2,18},{10... | collective-permute-start | bytes 294920 | tf_op jit(solution)/shard_map/ppermute | solution.py:363
  109.2 4.9 %collective-permute-start.8 = (f32[4,24,256]{2,1,0:T(8,128)S(1)}, f32[4,24,256]{2,1,0:T(8,128)S(1)}, u32[]{:S(2)}, u32[]{:S(2)}) collective-permute-start(f32[4,24,256]{2,1,0:T(8,128)S(1)} %get-tuple-element.124), channel_id=1, source_target_pairs={{0,8},{8,0},{16,24},{24,16},{1,9},{9,1},{17,25},{25,17},{2,10},{10... | collective-permute-start | bytes 294920 | tf_op jit(solution)/shard_map/ppermute | solution.py:363
  114.2 7.3 %collective-permute-start.11 = (f32[4,24,256]{2,1,0:T(8,128)S(1)}, f32[4,24,256]{2,1,0:T(8,128)S(1)}, u32[]{:S(2)}, u32[]{:S(2)}) collective-permute-start(f32[4,24,256]{2,1,0:T(8,128)S(1)} %add_add_fusion), channel_id=1, source_target_pairs={{0,2},{1,3},{2,0},{3,1},{4,6},{5,7},{6,4},{7,5},{8,10},{9,11},{10,... | collective-permute-start | bytes 294920 | tf_op jit(solution)/shard_map/ppermute | solution.py:363
  121.5 7.3 %collective-permute-start.12 = (f32[4,24,256]{2,1,0:T(8,128)S(1)}, f32[4,24,256]{2,1,0:T(8,128)S(1)}, u32[]{:S(2)}, u32[]{:S(2)}) collective-permute-start(f32[4,24,256]{2,1,0:T(8,128)S(1)} %add.68), channel_id=1, source_target_pairs={{0,4},{1,5},{2,6},{3,7},{4,0},{5,1},{6,2},{7,3},{8,12},{9,13},{10,... | collective-permute-start | bytes 294920 | tf_op jit(solution)/shard_map/ppermute | solution.py:363
  128.8 4.8 %collective-permute-start.13 = (f32[4,24,256]{2,1,0:T(8,128)S(1)}, f32[4,24,256]{2,1,0:T(8,128)S(1)}, u32[]{:S(2)}, u32[]{:S(2)}) collective-permute-start(f32[4,24,256]{2,1,0:T(8,128)S(1)} %get-tuple-element.109), channel_id=1, source_target_pairs={{0,8},{8,0},{16,24},{24,16},{1,9},{9,1},{17,25},{25,17},{2,10},{10... | collective-permute-start | bytes 294920 | tf_op jit(solution)/shard_map/ppermute | solution.py:363
  130.6 6.6 %collective-permute-start.14 = (f32[4,24,256]{2,1,0:T(8,128)S(1)}, f32[4,24,256]{2,1,0:T(8,128)S(1)}, u32[]{:S(2)}, u32[]{:S(2)}) collective-permute-start(f32[4,24,256]{2,1,0:T(8,128)S(1)} %get-tuple-element.109), channel_id=1, source_target_pairs={{0,16},{8,24},{16,0},{24,8},{1,17},{9,25},{17,1},{25,9},{2,18},{10... | collective-permute-start | bytes 294920 | tf_op jit(solution)/shard_map/ppermute | solution.py:363
  130.7 6.5 %collective-permute-start.15 = (f32[4,24,256]{2,1,0:T(8,128)S(1)}, f32[4,24,256]{2,1,0:T(8,128)S(1)}, u32[]{:S(2)}, u32[]{:S(2)}) collective-permute-start(f32[4,24,256]{2,1,0:T(8,128)S(1)} %get-tuple-element.109), channel_id=1, source_target_pairs={{0,24},{8,16},{16,8},{24,0},{1,25},{9,17},{17,9},{25,1},{2,26},{10... | collective-permute-start | bytes 294920 | tf_op jit(solution)/shard_map/ppermute | solution.py:363
  137.2 1.8 %collective-permute-start.16 = (f32[16,24,256]{2,1,0:T(8,128)S(1)}, f32[16,24,256]{2,1,0:T(8,128)S(1)}, u32[]{:S(2)}, u32[]{:S(2)}) collective-permute-start(f32[16,24,256]{2,1,0:T(8,128)S(1)} %constant_dynamic-update-slice_fusion), channel_id=1, source_target_pairs={{0,1},{1,0},{2,3},{3,2},{4,5},{5,4},{6,7},{7,6},{8,9},{9,8},{10,11... | collective-permute-start | bytes 1179656 | tf_op jit(solution)/shard_map/ppermute | solution.py:347
  139.6 0.9 copy-start.7

commit v18 on v15

--- a/solution.py
+++ b/solution.py
@@ -56,7 +56,25 @@
     return added([tap[k] * values[k] for k in range(len(tap))])
 
 
-def states_kernel(core, p, hx, hi, u, filt, f1, we, wb, qkv, xg, blocks_e, blocks_a, ends, xs):
+def tap_sums(row, tap, run):
+    even, odd, both = phases(tap)
+    reach = len(even)
+    evens = [row(-2 * k) for k in range(1, reach)]
+    odds = [row(1 - 2 * k) for k in range(1, reach)]
+    pairs = [evens[k] + odds[k] for k in range(reach - 1)]
+    before = weighted(odd, odds)
+    for a in range(0, run, 2):
+        evens = [row(a)] + evens[: reach - 1]
+        first = weighted(even, evens)
+        yield first + before
+        if a + 1 < run:
+            odds = [row(a + 1)] + odds[: reach - 1]
+            pairs = [evens[0] + odds[0]] + pairs[: reach - 1]
+            before = weighted(odd, odds)
+            yield weighted(both, pairs) - first - before
+
+
+def states_kernel(core, p, hx, hi, u, filt, f1, we, wb, kv, xg, blocks_e, blocks_a, ends, xs):
     rows = p.shape[1]
     run = (rows + SUB) // SUB
     taps = filt.shape[1]
@@ -80,30 +98,17 @@
         xs[3, SUB + rows :] = jnp.where(first, within, across)
 
         def mixed(j):
-            even, odd, both = phases([spread(filt[j, i : i + 1, lanes]) for i in range(taps)])
-            row = lambda a: xs[j, pl.ds(SUB + a, SUB, stride=run), :]
-            reach = len(even)
-            evens = [row(-2 * k) for k in range(1, reach)]
-            odds = [row(1 - 2 * k) for k in range(1, reach)]
-            pairs = [evens[k] + odds[k] for k in range(reach - 1)]
-            before = weighted(odd, odds)
-            for a in range(0, run, 2):
-                evens = [row(a)] + evens[: reach - 1]
-                first = weighted(even, evens)
-                yield first + before
-                if a + 1 < run:
-                    odds = [row(a + 1)] + odds[: reach - 1]
-                    pairs = [evens[0] + odds[0]] + pairs[: reach - 1]
-                    before = weighted(odd, odds)
-                    yield weighted(both, pairs) - first - before
+            tap = [spread(filt[j, i : i + 1, lanes]) for i in range(taps)]
+            return tap_sums(lambda a: xs[j, pl.ds(SUB + a, SUB, stride=run), :], tap, run)
 
         decay = [spread(f1[n : n + 1, part]) for n in range(poles)]
         for j in (1, 2, 0):
             for a, total in enumerate(mixed(j)):
                 at = slice(SUB * a, SUB * a + SUB)
-                qkv[which, j, at, part] = total
+                if j > 0:
+                    kv[which, j - 1, at, part] = total
                 if j == 2:
-                    xg[which, 0, at, part] = qkv[which, 1, at, part] * total
+                    xg[which, 0, at, part] = kv[which, 0, at, part] * total
                 if j == 0:
                     xg[which, 1, at, part] = xs[3, pl.ds(SUB + a, SUB, stride=run), :] * total
         for side, order, weight, blocks in (
@@ -177,7 +182,7 @@
 
 
 def final_kernel(
-    core, p, hx, hi, u, qkv, conv, from_e, from_a, skip_sum, both, found, other, filt, f1, f_all, cz, cy,
+    core, p, hx, hi, u, kv, conv, from_e, from_a, skip_sum, both, found, other, filt, f1, f_all, cz, cy,
     output, grad_p, sums, ps, us, gs, os, es,
 ):
     rows = p.shape[1]
@@ -216,9 +221,11 @@
             from_e[which, n, :, part] + cz[n, :, part] * spread(es[0, n : n + 1])
             for n in range(poles)
         ]
+        tap = [spread(filt[0, i : i + 1, lanes]) for i in range(taps)]
+        queries = tap_sums(lambda a: ps[0, pl.ds(SUB + a, SUB, stride=run), :], tap, run)
         for a in range(run):
             at = slice(SUB * a, SUB * a + SUB)
-            query, upstream = qkv[which, 0, at, part], us[pl.ds(a, SUB, stride=run), :]
+            query, upstream = next(queries), us[pl.ds(a, SUB, stride=run), :]
             filtered = conv[which, 0, at, part] + added(list(state))
             os[pl.ds(a, SUB, stride=run), :] = query * filtered
             gs[0, at] = upstream * filtered
@@ -233,8 +240,8 @@
         for a in range(run - 1, -1, -1):
             at = slice(SUB * a, SUB * a + SUB)
             grad = conv[which, 1, at, part] + added(list(state))
-            gs[1, at] = grad * qkv[which, 2, at, part]
-            gs[2, at] = grad * qkv[which, 1, at, part]
+            gs[1, at] = grad * kv[which, 1, at, part]
+            gs[2, at] = grad * kv[which, 0, at, part]
             if a:
                 state = [state[n] * decay[n] for n in range(poles)]
 
@@ -371,11 +378,10 @@
     total = piece(0)
     for term in [paired(piece(k), "dp", k) for k in range(1, parts)]:
         total = total + term
-    count = lax.axis_size("ctx")
-    reaches = [2 << k for k in range((count // 2).bit_length() - 1)]
-    for near, far in zip(reaches, reversed(reaches)):
-        pairs = [(s, s ^ (far if s % 2 else near)) for s in range(count)]
-        total = total + lax.ppermute(total, "ctx", pairs)
+    reach = 2
+    while reach < lax.axis_size("ctx"):
+        total = total + paired(total, "ctx", reach)
+        reach = 2 * reach
     value = jnp.zeros((half,) + value.shape[1:], F32)
     for k in range(parts):
         term = paired(total, "dp", k) if k else total
@@ -452,7 +458,7 @@
         return pl.BlockSpec((count,) + shape, lambda w: (w + first,) + (0,) * len(shape))
 
     state_spec = by_block(poles, SUB, groups)
-    qkv, xg, blocks_e, blocks_a, ends = pl.pallas_call(
+    kv, xg, blocks_e, blocks_a, ends = pl.pallas_call(
         states_kernel,
         grid=(width // each,),
         in_specs=[
@@ -461,11 +467,11 @@
             fixed(f1), fixed(we), fixed(wb),
         ],
         out_specs=[
-            by_block(3, held, groups), by_block(2, held, groups), state_spec, state_spec,
+            by_block(2, held, groups), by_block(2, held, groups), state_spec, state_spec,
             ends_spec,
         ],
         out_shape=[
-            shape_of((width, 3, held, groups), F32), pair_shape,
+            pair_shape, pair_shape,
             state_shape, state_shape, shape_of((2, width, poles, groups), F32),
         ],
         scratch_shapes=[pltpu.VMEM((4, held + SUB, LANES), F32)],
@@ -530,7 +536,7 @@
         in_specs=[
             pl.BlockSpec(memory_space=pltpu.SMEM),
             by_w(3, rows), by_w(4, SUB), by_w(4, SUB), by_w(rows),
-            by_block(3, held, groups), by_block(2, held, groups), state_spec, state_spec,
+            by_block(2, held, groups), by_block(2, held, groups), state_spec, state_spec,
             by_block(SUB, groups), halved, halved, ends_spec,
             by_w(3, taps), fixed(f1), fixed(f_all), fixed(cz), fixed(cy),
         ],
@@ -547,7 +553,7 @@
         compiler_params=params,
         name="final",
     )(
-        core[None], p, hx, hi, u, qkv, conv, from_e, from_a, skip_sum, both, found, other, short_filter,
+        core[None], p, hx, hi, u, kv, conv, from_e, from_a, skip_sum, both, found, other, short_filter,
         f1, f_all, cz, cy,
     )
 

time: 137 us -> 140 us (1.022)
  Pallas kernels: 75.9 us -> 77.8 us
  starting transfers between devices: 26.6 us -> 28.4 us
    ppermute x2 -> x0, waiting for transfers between devices: 6.94 us -> none  [summed(): total = total + lax.ppermute(total, 'ctx', pairs)]
    ppermute x7 -> x9, starting transfers between devices: 9.16 us -> 15.7 us  [paired(): lax.ppermute(value, axis, [(source, source ^ step) for source in lines or...]
    ppermute x7 -> x9, waiting for transfers between devices: 8.19 us -> 14.1 us  [paired(): lax.ppermute(value, axis, [(source, source ^ step) for source in lines or...]
    ppermute x2 -> x0, starting transfers between devices: 4.74 us -> none  [summed(): total = total + lax.ppermute(total, 'ctx', pairs)]
    pallas_call x1, Pallas kernels: 31.5 us -> 33.5 us  [local(): pl.pallas_call(final_kernel, grid=(width // each,), in_specs=[pl.BlockSpe...]
where the time goes in v18:
time: 140 us; the launch traced here: 139 us
  Pallas kernels  77.8 us (56%)
  starting transfers between devices  28.4 us (20%)
  waiting for transfers between devices  24.4 us (17%)
  other arithmetic  3.86 us (3%)
  local copies, waits for them, and re-layouts  3.67 us (3%)
    pallas_call x1, Pallas kernels, local(): pl.pallas_call(final_kernel, grid=(width // each,), in_specs=[pl.BlockSpe...  33.5 us
    pallas_call x3, Pallas kernels, call(): pl.pallas_call(blocks_kernel, grid=(last - first,), in_specs=[pairs, stat...  22.1 us
    pallas_call x1, Pallas kernels, local(): pl.pallas_call(states_kernel, grid=(width // each,), in_specs=[pl.BlockSp...  22.1 us
    ppermute x9, starting transfers between devices, paired(): lax.ppermute(value, axis, [(source, source ^ step) for source in lines or...  15.7 us
    ppermute x9, waiting for transfers between devices, paired(): lax.ppermute(value, axis, [(source, source ^ step) for source in lines or...  14.1 us
    ppermute x5, starting transfers between devices, swapped(): return lax.ppermute(value, 'ctx', [(s, s ^ 1) for s in range(count)])  9.73 us
    ppermute x5, waiting for transfers between devices, swapped(): return lax.ppermute(value, 'ctx', [(s, s ^ 1) for s in range(count)])  7.85 us
  transfers between devices with their start and end apart: 17, of which 13 were waited for; matrix products, arithmetic and copies ran while one was open for 1% of the time, Pallas kernels for 16%

profile of v18, /device:TPU:0, one launch (start us, length us, event | category | flops | bytes accessed | tf_op | source)
XLA Modules:
  0.0 139.2 jit_solution(7564655222678650611)
XLA Ops:
  0.6 0.0 copy-start.11
  0.6 0.0 copy-start.10
  0.7 0.0 copy-start.14
  0.7 1.0 constant_dynamic-slice_fusion.3
  1.7 0.0 copy-start.12
  1.7 0.0 copy-start.13
  1.7 1.2 dynamic-slice_bitcast_fusion
  2.9 0.0 copy-start
  2.9 0.0 copy-start.1
  3.0 0.8 collective-permute-start
  3.9 4.5 %collective-permute-start.1 = (bf16[4,8,8192]{2,1,0:T(8,128)(2,1)S(1)}, bf16[4,8,8192]{2,1,0:T(8,128)(2,1)S(1)}, u32[]{:S(2)}, u32[]{:S(2)}) collective-permute-start(bf16[4,8,8192]{2,1,0:T(8,128)(2,1)S(1)} %pad_maximum_fusion.1), channel_id=1, source_target_pairs={{0,1},{1,0},{2,3},{3,2},{4,5},{5,4},{6,7},{7,6},{8,9},{9,8},{10,11... | collective-permute-start | bytes 1572872 | tf_op jit(solution)/shard_map/ppermute | solution.py:320
  8.5 0.1 multiply_exponential_fusion.1
  8.6 0.2 multiply_exponential_fusion
  8.9 0.2 multiply_reduce_fusion.near
  9.1 0.8 fusion.4
  10.0 0.3 broadcast_select_fusion
  10.3 0.0 copy-start.2
  10.4 22.1 %states.1 = (f32[16,2,136,512]{3,2,1,0:T(8,128)}, f32[16,2,136,512]{3,2,1,0:T(8,128)}, f32[16,16,8,512]{3,2,1,0:T(8,128)}, f32[16,16,8,512]{3,2,1,0:T(8,128)}, f32[2,16,16,512]{3,2,1,0:T(8,128)}) custom-call(s32[1]{0:T(128)} %bitcast.core, bf16[3,128,8192]{2,1,0:T(8,128)(2,1)} %bitcast.89, bf16[4,8,8192]{2,1,0:T(8,128)(2,1)S(1)} %collective-permute-done.hx, ...), custom_call_target="tpu_custom_call" | custom-call | tf_op jit(solution)/shard_map/states/pallas_call | solution.py:461
  32.5 4.9 %collective-permute-start.2 = (f32[2,16,16,512]{3,2,1,0:T(8,128)}, f32[2,16,16,512]{3,2,1,0:T(8,128)}, u32[]{:S(2)}, u32[]{:S(2)}) collective-permute-start(f32[2,16,16,512]{3,2,1,0:T(8,128)} %get-tuple-element.52), channel_id=1, source_target_pairs={{0,1},{1,0},{2,3},{3,2},{4,5},{5,4},{6,7},{7,6},{8,9},{9,8},{10,11... | collective-permute-start | bytes 3145736 | tf_op jit(solution)/shard_map/ppermute | solution.py:320
  37.4 2.6 %collective-permute-done.2.other = f32[2,16,16,512]{3,2,1,0:T(8,128)} collective-permute-done((f32[2,16,16,512]{3,2,1,0:T(8,128)}, f32[2,16,16,512]{3,2,1,0:T(8,128)}, u32[]{:S(2)}, u32[]{:S(2)}) %collective-permute-start.2) | collective-permute-done | bytes 1048608 | tf_op jit(solution)/shard_map/ppermute | solution.py:320
  40.0 1.3 dynamic-slice_select_fusion.1
  41.3 0.1 broadcast_select_fusion.4
  41.4 2.1 %collective-permute-start.3 = (f32[8,16,512]{2,1,0:T(8,128)S(1)}, f32[8,16,512]{2,1,0:T(8,128)S(1)}, u32[]{:S(2)}, u32[]{:S(2)}) collective-permute-start(f32[8,16,512]{2,1,0:T(8,128)S(1)} %broadcast_select_fusion.4), channel_id=1, source_target_pairs={{0,2},{1,3},{2,0},{3,1},{4,6},{5,7},{6,4},{7,5},{8,10},{9,11},{10,... | collective-permute-start | bytes 786440 | tf_op jit(solution)/shard_map/ppermute | solution.py:336
  43.5 8.2 %blocks.3 = (f32[16,2,136,512]{3,2,1,0:T(8,128)}, f32[16,16,8,512]{3,2,1,0:T(8,128)}, f32[16,16,8,512]{3,2,1,0:T(8,128)}, f32[6,8,512]{2,1,0:T(8,128)S(1)}) custom-call(f32[16,2,136,512]{3,2,1,0:T(8,128)} %get-tuple-element.53.xg, f32[16,16,8,512]{3,2,1,0:T(8,128)} %get-tuple-element.54.blocks_e, ...), custom_call_target="tpu_custom_call", output_to_operand_aliasing={{0}: (0, {}), {1}: (1, {}), {2}: (2, {})} | custom-call | flops 62914560 | bytes 36700160 | tf_op jit(solution)/shard_map/blocks/pallas_call | solution.py:491
  51.7 0.1 multiply_add_fusion.1
  51.9 0.7 collective-permute-start.4
  52.6 5.8 %blocks.4 = (f32[16,2,136,512]{3,2,1,0:T(8,128)}, f32[16,16,8,512]{3,2,1,0:T(8,128)}, f32[16,16,8,512]{3,2,1,0:T(8,128)}, f32[4,8,512]{2,1,0:T(8,128)S(1)}) custom-call(f32[16,2,136,512]{3,2,1,0:T(8,128)} %get-tuple-element.65.xg, f32[16,16,8,512]{3,2,1,0:T(8,128)} %get-tuple-element.66.blocks_e, ...), custom_call_target="tpu_custom_call", output_to_operand_aliasing={{0}: (0, {}), {1}: (1, {}), {2}: (2, {})} | custom-call | flops 62914560 | bytes 36700160 | tf_op jit(solution)/shard_map/blocks/pallas_call | solution.py:491
  58.4 0.0 copy-start.3
  58.5 1.4 %collective-permute-start.5 = (f32[8,16,512]{2,1,0:T(8,128)S(1)}, f32[8,16,512]{2,1,0:T(8,128)S(1)}, u32[]{:S(2)}, u32[]{:S(2)}) collective-permute-start(f32[8,16,512]{2,1,0:T(8,128)S(1)} %collective-permute-done.4), channel_id=1, source_target_pairs={{4,6},{5,7},{2,0},{3,1},{12,14},{13,15},{10,8},{11,9},{20,22},{21,... | collective-permute-start | bytes 786440 | tf_op jit(solution)/shard_map/ppermute | solution.py:352
  59.9 8.1 %blocks.5 = (f32[16,2,136,512]{3,2,1,0:T(8,128)}, f32[16,16,8,512]{3,2,1,0:T(8,128)}, f32[16,16,8,512]{3,2,1,0:T(8,128)}, f32[6,8,512]{2,1,0:T(8,128)S(1)}) custom-call(f32[16,2,136,512]{3,2,1,0:T(8,128)} %get-tuple-element.75.xg, f32[16,16,8,512]{3,2,1,0:T(8,128)} %get-tuple-element.76.blocks_e, ...), custom_call_target="tpu_custom_call", output_to_operand_aliasing={{0}: (0, {}), {1}: (1, {}), {2}: (2, {})} | custom-call | flops 62914560 | bytes 36700160 | tf_op jit(solution)/shard_map/blocks/pallas_call | solution.py:491
  68.0 2.4 %collective-permute-done.5 = f32[8,16,512]{2,1,0:T(8,128)S(1)} collective-permute-done((f32[8,16,512]{2,1,0:T(8,128)S(1)}, f32[8,16,512]{2,1,0:T(8,128)S(1)}, u32[]{:S(2)}, u32[]{:S(2)}) %collective-permute-start.5) | collective-permute-done | bytes 262176 | tf_op jit(solution)/shard_map/ppermute | solution.py:352
  70.4 0.1 select_bitcast_fusion.1
  70.6 0.1 collective-permute-start.6
  70.7 1.9 %collective-permute-done.6.found = f32[2,8,16,512]{3,2,1,0:T(8,128)S(1)} collective-permute-done((f32[2,8,16,512]{3,2,1,0:T(8,128)S(1)}, f32[2,8,16,512]{3,2,1,0:T(8,128)S(1)}, u32[]{:S(2)}, u32[]{:S(2)}) %collective-permute-start.6) | collective-permute-done | bytes 524320 | tf_op jit(solution)/shard_map/ppermute | solution.py:320
  72.6 33.5 %final.1 = (bf16[128,8192]{1,0:T(8,128)(2,1)}, bf16[3,128,8192]{2,1,0:T(8,128)(2,1)}, f32[32,24,256]{2,1,0:T(8,128)S(1)}) custom-call(s32[1]{0:T(128)} %bitcast.core, bf16[3,128,8192]{2,1,0:T(8,128)(2,1)} %bitcast.90, bf16[4,8,8192]{2,1,0:T(8,128)(2,1)S(1)} %collective-permute-done.hx, bf16[4,8,8192]{2,1,0:T(8,128)(2,1)S(1)} %copy-done.3, ...), custom_call_target="tpu_custom_call" | custom-call | tf_op jit(solution)/shard_map/final/pallas_call | solution.py:533
  106.1 0.1 slice_select_fusion
  106.1 0.2 collective-permute-start.7
  106.3 1.6 %collective-permute-done.7 = f32[16,24,256]{2,1,0:T(8,128)S(1)} collective-permute-done((f32[16,24,256]{2,1,0:T(8,128)S(1)}, f32[16,24,256]{2,1,0:T(8,128)S(1)}, u32[]{:S(2)}, u32[]{:S(2)}) %collective-permute-start.7) | collective-permute-done | bytes 393248 | tf_op jit(solution)/shard_map/ppermute | solution.py:320
  107.9 0.1 select_add_fusion
  108.0 2.5 %collective-permute-start.10 = (f32[4,24,256]{2,1,0:T(8,128)S(1)}, f32[4,24,256]{2,1,0:T(8,128)S(1)}, u32[]{:S(2)}, u32[]{:S(2)}) collective-permute-start(f32[4,24,256]{2,1,0:T(8,128)S(1)} %get-tuple-element.111), channel_id=1, source_target_pairs={{0,24},{8,16},{16,8},{24,0},{1,25},{9,17},{17,9},{25,1},{2,26},{10... | collective-permute-start | bytes 294920 | tf_op jit(solution)/shard_map/ppermute | solution.py:336
  110.6 0.5 collective-permute-start.9
  111.1 0.5 collective-permute-start.8
  111.6 2.3 %collective-permute-done.10 = f32[4,24,256]{2,1,0:T(8,128)S(1)} collective-permute-done((f32[4,24,256]{2,1,0:T(8,128)S(1)}, f32[4,24,256]{2,1,0:T(8,128)S(1)}, u32[]{:S(2)}, u32[]{:S(2)}) %collective-permute-start.10) | collective-permute-done | bytes 98336 | tf_op jit(solution)/shard_map/ppermute | solution.py:336
  113.9 2.0 %collective-permute-done.9 = f32[4,24,256]{2,1,0:T(8,128)S(1)} collective-permute-done((f32[4,24,256]{2,1,0:T(8,128)S(1)}, f32[4,24,256]{2,1,0:T(8,128)S(1)}, u32[]{:S(2)}, u32[]{:S(2)}) %collective-permute-start.9) | collective-permute-done | bytes 98336 | tf_op jit(solution)/shard_map/ppermute | solution.py:336
  116.0 0.1 collective-permute-done.8
  116.0 2.5 %collective-permute-start.11 = (f32[4,24,256]{2,1,0:T(8,128)S(1)}, f32[4,24,256]{2,1,0:T(8,128)S(1)}, u32[]{:S(2)}, u32[]{:S(2)}) collective-permute-start(f32[4,24,256]{2,1,0:T(8,128)S(1)} %add_add_fusion), channel_id=1, source_target_pairs={{0,2},{1,3},{2,0},{3,1},{4,6},{5,7},{6,4},{7,5},{8,10},{9,11},{10,... | collective-permute-start | bytes 294920 | tf_op jit(solution)/shard_map/ppermute | solution.py:336
  118.5 2.7 %collective-permute-done.11 = f32[4,24,256]{2,1,0:T(8,128)S(1)} collective-permute-done((f32[4,24,256]{2,1,0:T(8,128)S(1)}, f32[4,24,256]{2,1,0:T(8,128)S(1)}, u32[]{:S(2)}, u32[]{:S(2)}) %collective-permute-start.11) | collective-permute-done | bytes 98336 | tf_op jit(solution)/shard_map/ppermute | solution.py:336
  121.3 3.1 %collective-permute-start.12 = (f32[4,24,256]{2,1,0:T(8,128)S(1)}, f32[4,24,256]{2,1,0:T(8,128)S(1)}, u32[]{:S(2)}, u32[]{:S(2)}) collective-permute-start(f32[4,24,256]{2,1,0:T(8,128)S(1)} %add.68), channel_id=1, source_target_pairs={{0,4},{1,5},{2,6},{3,7},{4,0},{5,1},{6,2},{7,3},{8,12},{9,13},{10,... | collective-permute-start | bytes 294920 | tf_op jit(solution)/shard_map/ppermute | solution.py:336
  124.4 2.8 %collective-permute-done.12 = f32[4,24,256]{2,1,0:T(8,128)S(1)} collective-permute-done((f32[4,24,256]{2,1,0:T(8,128)S(1)}, f32[4,24,256]{2,1,0:T(8,128)S(1)}, u32[]{:S(2)}, u32[]{:S(2)}) %collective-permute-start.12) | collective-permute-done | bytes 98336 | tf_op jit(solution)/shard_map/ppermute | solution.py:336
  127.3 2.9 %collective-permute-start.13 = (f32[4,24,256]{2,1,0:T(8,128)S(1)}, f32[4,24,256]{2,1,0:T(8,128)S(1)}, u32[]{:S(2)}, u32[]{:S(2)}) collective-permute-start(f32[4,24,256]{2,1,0:T(8,128)S(1)} %get-tuple-element.95), channel_id=1, source_target_pairs={{0,8},{8,0},{16,24},{24,16},{1,9},{9,1},{17,25},{25,17},{2,10},{10... | collective-permute-start | bytes 294920 | tf_op jit(solution)/shard_map/ppermute | solution.py:336
  130.2 0.2 collective-permute-start.14
  130.4 1.4 collective-permute-start.15
  131.8 1.8 %collective-permute-done.13 = f32[4,24,256]{2,1,0:T(8,128)S(1)} collective-permute-done((f32[4,24,256]{2,1,0:T(8,128)S(1)}, f32[4,24,256]{2,1,0:T(8,128)S(1)}, u32[]{:S(2)}, u32[]{:S(2)}) %collective-permute-start.13) | collective-permute-done | bytes 98336 | tf_op jit(solution)/shard_map/ppermute | solution.py:336
  133.6 1.2 collective-permute-done.14
  134.8 1.1 collective-permute-done.15
  135.9 0.1 collective-permute-start.16
  136.0 1.7 %collective-permute-done.16 = f32[16,24,256]{2,1,0:T(8,128)S(1)} collective-permute-done((f32[16,24,256]{2,1,0:T(8,128)S(1)}, f32[16,24,256]{2,1,0:T(8,128)S(1)}, u32[]{:S(2)}, u32[]{:S(2)}) %collective-permute-start.16) | collective-permute-done | bytes 393248 | tf_op jit(solution)/shard_map/ppermute | solution.py:320
  137.7 0.1 broadcast_select_fusion.3
  137.8 0.1 maximum_bitcast_fusion
  137.9 0.3 copy.25
  138.1 0.1 reshape.33
  138.3 0.0 copy-start.7
  138.3 0.7 slice.67
  139.0 0.2 copy-done.7
  (43 shorter events, 0.5 us)
Async XLA Ops:
  0.6 7.8 %copy-start.11 = (f32[4]{0:T(128)S(1)}, f32[4]{0:T(128)}, u32[]{:S(2)}) copy-start(f32[4]{0:T(128)} %constant.68) | copy-start | bytes 52
  0.6 8.0 %copy-start.10 = (f32[4,8]{1,0:T(4,128)S(1)}, f32[4,8]{1,0:T(4,128)}, u32[]{:S(2)}) copy-start(f32[4,8]{1,0:T(4,128)} %constant.70) | copy-start | bytes 388
  0.7 8.2 %copy-start.14 = (f32[24]{0:T(128)S(1)}, f32[24]{0:T(128)}, u32[]{:S(2)}) copy-start(f32[24]{0:T(128)} %constant.66) | copy-start | bytes 292
  0.7 7.8 %copy-start.9 = (f32[512,16]{0,1:T(8,128)S(1)}, f32[512,16]{0,1:T(8,128)}, u32[]{:S(2)}) copy-start(f32[512,16]{0,1:T(8,128)} %param.14) | copy-start | bytes 98308
  0.7 7.9 %copy-start.8 = (f32[512,16]{0,1:T(8,128)S(1)}, f32[512,16]{0,1:T(8,128)}, u32[]{:S(2)}) copy-start(f32[512,16]{0,1:T(8,128)} %param.13) | copy-start | bytes 98308
  1.7 8.3 %copy-start.12 = (pred[4,8]{1,0:T(4,128)(4,1)S(1)}, pred[4,8]{1,0:T(4,128)(4,1)}, u32[]{:S(2)}) copy-start(pred[4,8]{1,0:T(4,128)(4,1)} %constant.69) | copy-start | bytes 100
  1.7 8.3 %copy-start.13 = (pred[4,8]{1,0:T(4,128)(4,1)S(1)}, pred[4,8]{1,0:T(4,128)(4,1)}, u32[]{:S(2)}) copy-start(pred[4,8]{1,0:T(4,128)(4,1)} %constant.67) | copy-start | bytes 100
  2.9 7.4 %copy-start = (bf16[1,128,8192]{2,1,0:T(8,128)(2,1)S(1)}, bf16[1,128,8192]{2,1,0:T(8,128)(2,1)}, u32[]{:S(2)}) copy-start(bf16[1,128,8192]{2,1,0:T(8,128)(2,1)} %param.16) | copy-start | bytes 6291460
  2.9 7.4 %copy-start.1 = (f32[3,7,8192]{2,1,0:T(8,128)S(1)}, f32[3,7,8192]{2,1,0:T(8,128)}, u32[]{:S(2)}) copy-start(f32[3,7,8192]{2,1,0:T(8,128)} %filt.3) | copy-start | bytes 2064388
  3.0 7.3 %collective-permute-start = (bf16[4,8,8192]{2,1,0:T(8,128)(2,1)S(1)}, bf16[4,8,8192]{2,1,0:T(8,128)(2,1)S(1)}, u32[]{:S(2)}, u32[]{:S(2)}) collective-permute-start(bf16[4,8,8192]{2,1,0:T(8,128)(2,1)S(1)} %pad_maximum_fusion), channel_id=1, source_target_pairs={{1,2},{3,4},{5,6},{2,1},{4,3},{6,5},{9,10},{11,12},{13,14},{10,9},... | collective-permute-start | bytes 1572872 | tf_op jit(solution)/shard_map/ppermute | solution.py:413
  3.9 6.5 %collective-permute-start.1 = (bf16[4,8,8192]{2,1,0:T(8,128)(2,1)S(1)}, bf16[4,8,8192]{2,1,0:T(8,128)(2,1)S(1)}, u32[]{:S(2)}, u32[]{:S(2)}) collective-permute-start(bf16[4,8,8192]{2,1,0:T(8,128)(2,1)S(1)} %pad_maximum_fusion.1), channel_id=1, source_target_pairs={{0,1},{1,0},{2,3},{3,2},{4,5},{5,4},{6,7},{7,6},{8,9},{9,8},{10,11... | collective-permute-start | bytes 1572872 | tf_op jit(solution)/shard_map/ppermute | solution.py:320
  10.3 22.2 %copy-start.2 = (bf16[4,8,8192]{2,1,0:T(8,128)(2,1)}, bf16[4,8,8192]{2,1,0:T(8,128)(2,1)S(1)}, u32[]{:S(2)}) copy-start(bf16[4,8,8192]{2,1,0:T(8,128)(2,1)S(1)} %collective-permute-done.1.hi) | copy-start | bytes 1572868
  10.4 33.1 %copy-start.6 = (f32[8192]{0:T(1024)S(1)}, f32[8192]{0:T(1024)}, u32[]{:S(2)}) copy-start(f32[8192]{0:T(1024)} %param.15) | copy-start | bytes 98308
  32.5 7.5 %collective-permute-start.2 = (f32[2,16,16,512]{3,2,1,0:T(8,128)}, f32[2,16,16,512]{3,2,1,0:T(8,128)}, u32[]{:S(2)}, u32[]{:S(2)}) collective-permute-start(f32[2,16,16,512]{3,2,1,0:T(8,128)} %get-tuple-element.52), channel_id=1, source_target_pairs={{0,1},{1,0},{2,3},{3,2},{4,5},{5,4},{6,7},{7,6},{8,9},{9,8},{10,11... | collective-permute-start | bytes 3145736 | tf_op jit(solution)/shard_map/ppermute | solution.py:320
  41.4 10.3 %collective-permute-start.3 = (f32[8,16,512]{2,1,0:T(8,128)S(1)}, f32[8,16,512]{2,1,0:T(8,128)S(1)}, u32[]{:S(2)}, u32[]{:S(2)}) collective-permute-start(f32[8,16,512]{2,1,0:T(8,128)S(1)} %broadcast_select_fusion.4), channel_id=1, source_target_pairs={{0,2},{1,3},{2,0},{3,1},{4,6},{5,7},{6,4},{7,5},{8,10},{9,11},{10,... | collective-permute-start | bytes 786440 | tf_op jit(solution)/shard_map/ppermute | solution.py:336
  51.9 6.5 %collective-permute-start.4 = (f32[8,16,512]{2,1,0:T(8,128)S(1)}, f32[8,16,512]{2,1,0:T(8,128)S(1)}, u32[]{:S(2)}, u32[]{:S(2)}) collective-permute-start(f32[8,16,512]{2,1,0:T(8,128)S(1)} %multiply_add_fusion.1), channel_id=1, source_target_pairs={{2,4},{3,5},{4,2},{5,3},{10,12},{11,13},{12,10},{13,11},{18,20},{1... | collective-permute-start | bytes 786440 | tf_op jit(solution)/shard_map/ppermute | solution.py:349
  58.4 14.1 %copy-start.3 = (bf16[4,8,8192]{2,1,0:T(8,128)(2,1)S(1)}, bf16[4,8,8192]{2,1,0:T(8,128)(2,1)}, u32[]{:S(2)}) copy-start(bf16[4,8,8192]{2,1,0:T(8,128)(2,1)} %copy-done.2) | copy-start | bytes 1572868
  58.4 14.1 %copy-start.4 = (f32[16,8,512]{2,1,0:T(8,128)S(1)}, f32[16,8,512]{2,1,0:T(8,128)}, u32[]{:S(2)}) copy-start(f32[16,8,512]{2,1,0:T(8,128)} %get-tuple-element.90.cy) | copy-start | bytes 786436
  58.5 14.1 %copy-start.5 = (f32[16,8,512]{2,1,0:T(8,128)S(1)}, f32[16,8,512]{2,1,0:T(8,128)}, u32[]{:S(2)}) copy-start(f32[16,8,512]{2,1,0:T(8,128)} %get-tuple-element.89.cz) | copy-start | bytes 786436
  58.5 12.0 %collective-permute-start.5 = (f32[8,16,512]{2,1,0:T(8,128)S(1)}, f32[8,16,512]{2,1,0:T(8,128)S(1)}, u32[]{:S(2)}, u32[]{:S(2)}) collective-permute-start(f32[8,16,512]{2,1,0:T(8,128)S(1)} %collective-permute-done.4), channel_id=1, source_target_pairs={{4,6},{5,7},{2,0},{3,1},{12,14},{13,15},{10,8},{11,9},{20,22},{21,... | collective-permute-start | bytes 786440 | tf_op jit(solution)/shard_map/ppermute | solution.py:352
  70.6 2.0 %collective-permute-start.6 = (f32[2,8,16,512]{3,2,1,0:T(8,128)S(1)}, f32[2,8,16,512]{3,2,1,0:T(8,128)S(1)}, u32[]{:S(2)}, u32[]{:S(2)}) collective-permute-start(f32[2,8,16,512]{3,2,1,0:T(8,128)S(1)} %pad_maximum_fusion.2.both), channel_id=1, source_target_pairs={{0,1},{1,0},{2,3},{3,2},{4,5},{5,4},{6,7},{7,6},{8,9},{9,8},{10,11... | collective-permute-start | bytes 1572872 | tf_op jit(solution)/shard_map/ppermute | solution.py:320
  106.1 1.8 %collective-permute-start.7 = (f32[16,24,256]{2,1,0:T(8,128)S(1)}, f32[16,24,256]{2,1,0:T(8,128)S(1)}, u32[]{:S(2)}, u32[]{:S(2)}) collective-permute-start(f32[16,24,256]{2,1,0:T(8,128)S(1)} %slice_select_fusion), channel_id=1, source_target_pairs={{0,1},{1,0},{2,3},{3,2},{4,5},{5,4},{6,7},{7,6},{8,9},{9,8},{10,11... | collective-permute-start | bytes 1179656 | tf_op jit(solution)/shard_map/ppermute | solution.py:320
  108.0 5.9 %collective-permute-start.10 = (f32[4,24,256]{2,1,0:T(8,128)S(1)}, f32[4,24,256]{2,1,0:T(8,128)S(1)}, u32[]{:S(2)}, u32[]{:S(2)}) collective-permute-start(f32[4,24,256]{2,1,0:T(8,128)S(1)} %get-tuple-element.111), channel_id=1, source_target_pairs={{0,24},{8,16},{16,8},{24,0},{1,25},{9,17},{17,9},{25,1},{2,26},{10... | collective-permute-start | bytes 294920 | tf_op jit(solution)/shard_map/ppermute | solution.py:336
  110.6 5.4 %collective-permute-start.9 = (f32[4,24,256]{2,1,0:T(8,128)S(1)}, f32[4,24,256]{2,1,0:T(8,128)S(1)}, u32[]{:S(2)}, u32[]{:S(2)}) collective-permute-start(f32[4,24,256]{2,1,0:T(8,128)S(1)} %get-tuple-element.112), channel_id=1, source_target_pairs={{0,16},{8,24},{16,0},{24,8},{1,17},{9,25},{17,1},{25,9},{2,18},{10... | collective-permute-start | bytes 294920 | tf_op jit(solution)/shard_map/ppermute | solution.py:336
  111.1 4.9 %collective-permute-start.8 = (f32[4,24,256]{2,1,0:T(8,128)S(1)}, f32[4,24,256]{2,1,0:T(8,128)S(1)}, u32[]{:S(2)}, u32[]{:S(2)}) collective-permute-start(f32[4,24,256]{2,1,0:T(8,128)S(1)} %get-tuple-element.110), channel_id=1, source_target_pairs={{0,8},{8,0},{16,24},{24,16},{1,9},{9,1},{17,25},{25,17},{2,10},{10... | collective-permute-start | bytes 294920 | tf_op jit(solution)/shard_map/ppermute | solution.py:336
  116.0 5.2 %collective-permute-start.11 = (f32[4,24,256]{2,1,0:T(8,128)S(1)}, f32[4,24,256]{2,1,0:T(8,128)S(1)}, u32[]{:S(2)}, u32[]{:S(2)}) collective-permute-start(f32[4,24,256]{2,1,0:T(8,128)S(1)} %add_add_fusion), channel_id=1, source_target_pairs={{0,2},{1,3},{2,0},{3,1},{4,6},{5,7},{6,4},{7,5},{8,10},{9,11},{10,... | collective-permute-start | bytes 294920 | tf_op jit(solution)/shard_map/ppermute | solution.py:336
  121.3 5.9 %collective-permute-start.12 = (f32[4,24,256]{2,1,0:T(8,128)S(1)}, f32[4,24,256]{2,1,0:T(8,128)S(1)}, u32[]{:S(2)}, u32[]{:S(2)}) collective-permute-start(f32[4,24,256]{2,1,0:T(8,128)S(1)} %add.68), channel_id=1, source_target_pairs={{0,4},{1,5},{2,6},{3,7},{4,0},{5,1},{6,2},{7,3},{8,12},{9,13},{10,... | collective-permute-start | bytes 294920 | tf_op jit(solution)/shard_map/ppermute | solution.py:336
  127.3 6.3 %collective-permute-start.13 = (f32[4,24,256]{2,1,0:T(8,128)S(1)}, f32[4,24,256]{2,1,0:T(8,128)S(1)}, u32[]{:S(2)}, u32[]{:S(2)}) collective-permute-start(f32[4,24,256]{2,1,0:T(8,128)S(1)} %get-tuple-element.95), channel_id=1, source_target_pairs={{0,8},{8,0},{16,24},{24,16},{1,9},{9,1},{17,25},{25,17},{2,10},{10... | collective-permute-start | bytes 294920 | tf_op jit(solution)/shard_map/ppermute | solution.py:336
  130.2 4.6 %collective-permute-start.14 = (f32[4,24,256]{2,1,0:T(8,128)S(1)}, f32[4,24,256]{2,1,0:T(8,128)S(1)}, u32[]{:S(2)}, u32[]{:S(2)}) collective-permute-start(f32[4,24,256]{2,1,0:T(8,128)S(1)} %get-tuple-element.95), channel_id=1, source_target_pairs={{0,16},{8,24},{16,0},{24,8},{1,17},{9,25},{17,1},{25,9},{2,18},{10... | collective-permute-start | bytes 294920 | tf_op jit(solution)/shard_map/ppermute | solution.py:336
  130.4 5.5 %collective-permute-start.15 = (f32[4,24,256]{2,1,0:T(8,128)S(1)}, f32[4,24,256]{2,1,0:T(8,128)S(1)}, u32[]{:S(2)}, u32[]{:S(2)}) collective-permute-start(f32[4,24,256]{2,1,0:T(8,128)S(1)} %get-tuple-element.95), channel_id=1, source_target_pairs={{0,24},{8,16},{16,8},{24,0},{1,25},{9,17},{17,9},{25,1},{2,26},{10... | collective-permute-start | bytes 294920 | tf_op jit(solution)/shard_map/ppermute | solution.py:336
  135.9 1.8 %collective-permute-start.16 = (f32[16,24,256]{2,1,0:T(8,128)S(1)}, f32[16,24,256]{2,1,0:T(8,128)S(1)}, u32[]{:S(2)}, u32[]{:S(2)}) collective-permute-start(f32[16,24,256]{2,1,0:T(8,128)S(1)} %constant_dynamic-update-slice_fusion), channel_id=1, source_target_pairs={{0,1},{1,0},{2,3},{3,2},{4,5},{5,4},{6,7},{7,6},{8,9},{9,8},{10,11... | collective-permute-start | bytes 1179656 | tf_op jit(solution)/shard_map/ppermute | solution.py:320
  138.3 0.9 copy-start.7

commit v19 on v15

--- a/solution.py
+++ b/solution.py
@@ -106,16 +106,18 @@
                     xg[which, 0, at, part] = qkv[which, 1, at, part] * total
                 if j == 0:
                     xg[which, 1, at, part] = xs[3, pl.ds(SUB + a, SUB, stride=run), :] * total
-        for side, order, weight, blocks in (
-            (0, range(run), we, blocks_e),
-            (1, range(run - 1, -1, -1), wb, blocks_a),
-        ):
-            state = None
-            for a in order:
+        states = [None, None]
+        for step in range(run):
+            for side, a in ((0, step), (1, run - 1 - step)):
                 x = xg[which, side, SUB * a : SUB * a + SUB, part]
                 if a >= own:
                     x = jnp.where(inside, x, 0.0)
-                state = [x] * poles if state is None else [decay[n] * state[n] + x for n in range(poles)]
+                if step == 0:
+                    states[side] = [x] * poles
+                else:
+                    states[side] = [decay[n] * states[side][n] + x for n in range(poles)]
+        for side, weight, blocks in ((0, we, blocks_e), (1, wb, blocks_a)):
+            state = states[side]
             for n in range(poles):
                 blocks[which, n, :, part] = state[n]
             state = [state[n] * weight[n, :, part] for n in range(poles)]
@@ -371,11 +373,10 @@
     total = piece(0)
     for term in [paired(piece(k), "dp", k) for k in range(1, parts)]:
         total = total + term
-    count = lax.axis_size("ctx")
-    reaches = [2 << k for k in range((count // 2).bit_length() - 1)]
-    for near, far in zip(reaches, reversed(reaches)):
-        pairs = [(s, s ^ (far if s % 2 else near)) for s in range(count)]
-        total = total + lax.ppermute(total, "ctx", pairs)
+    reach = 2
+    while reach < lax.axis_size("ctx"):
+        total = total + paired(total, "ctx", reach)
+        reach = 2 * reach
     value = jnp.zeros((half,) + value.shape[1:], F32)
     for k in range(parts):
         term = paired(total, "dp", k) if k else total

time: 137 us -> 138 us (level)
  starting transfers between devices: 26.6 us -> 28.4 us
    ppermute x2 -> x0, waiting for transfers between devices: 6.94 us -> none  [summed(): total = total + lax.ppermute(total, 'ctx', pairs)]
    ppermute x7 -> x9, starting transfers between devices: 9.16 us -> 15.8 us  [paired(): lax.ppermute(value, axis, [(source, source ^ step) for source in lines or...]
    ppermute x7 -> x9, waiting for transfers between devices: 8.19 us -> 14.1 us  [paired(): lax.ppermute(value, axis, [(source, source ^ step) for source in lines or...]
    ppermute x2 -> x0, starting transfers between devices: 4.74 us -> none  [summed(): total = total + lax.ppermute(total, 'ctx', pairs)]
where the time goes in v19:
time: 138 us; the launch traced here: 137 us
  Pallas kernels  76 us (55%)
  starting transfers between devices  28.4 us (21%)
  waiting for transfers between devices  24.4 us (18%)
  other arithmetic  3.86 us (3%)
  local copies, waits for them, and re-layouts  3.67 us (3%)
    pallas_call x1, Pallas kernels, local(): pl.pallas_call(final_kernel, grid=(width // each,), in_specs=[pl.BlockSpe...  31.5 us
    pallas_call x1, Pallas kernels, local(): pl.pallas_call(states_kernel, grid=(width // each,), in_specs=[pl.BlockSp...  22.4 us
    pallas_call x3, Pallas kernels, call(): pl.pallas_call(blocks_kernel, grid=(last - first,), in_specs=[pairs, stat...  22.1 us
    ppermute x9, starting transfers between devices, paired(): lax.ppermute(value, axis, [(source, source ^ step) for source in lines or...  15.8 us
    ppermute x9, waiting for transfers between devices, paired(): lax.ppermute(value, axis, [(source, source ^ step) for source in lines or...  14.1 us
    ppermute x5, starting transfers between devices, swapped(): return lax.ppermute(value, 'ctx', [(s, s ^ 1) for s in range(count)])  9.73 us
    ppermute x5, waiting for transfers between devices, swapped(): return lax.ppermute(value, 'ctx', [(s, s ^ 1) for s in range(count)])  7.85 us
  transfers between devices with their start and end apart: 17, of which 13 were waited for; matrix products, arithmetic and copies ran while one was open for 1% of the time, Pallas kernels for 16%

profile of v19, /device:TPU:0, one launch (start us, length us, event | category | flops | bytes accessed | tf_op | source)
XLA Modules:
  0.0 137.4 jit_solution(5637514655775355630)
XLA Ops:
  0.6 0.0 copy-start.11
  0.6 0.0 copy-start.10
  0.7 0.0 copy-start.14
  0.7 1.0 constant_dynamic-slice_fusion.3
  1.7 0.0 copy-start.12
  1.7 0.0 copy-start.13
  1.7 1.2 dynamic-slice_bitcast_fusion
  2.9 0.0 copy-start.1
  3.0 0.8 collective-permute-start
  3.9 4.5 %collective-permute-start.1 = (bf16[4,8,8192]{2,1,0:T(8,128)(2,1)S(1)}, bf16[4,8,8192]{2,1,0:T(8,128)(2,1)S(1)}, u32[]{:S(2)}, u32[]{:S(2)}) collective-permute-start(bf16[4,8,8192]{2,1,0:T(8,128)(2,1)S(1)} %pad_maximum_fusion.1), channel_id=1, source_target_pairs={{0,1},{1,0},{2,3},{3,2},{4,5},{5,4},{6,7},{7,6},{8,9},{9,8},{10,11... | collective-permute-start | bytes 1572872 | tf_op jit(solution)/shard_map/ppermute | solution.py:315
  8.5 0.1 multiply_exponential_fusion.1
  8.6 0.2 multiply_exponential_fusion
  8.9 0.2 multiply_reduce_fusion.near
  9.1 0.8 fusion.4
  10.0 0.3 broadcast_select_fusion
  10.3 0.0 copy-start.2
  10.4 0.0 copy-start.6
  10.4 22.4 %states.1 = (f32[16,3,136,512]{3,2,1,0:T(8,128)}, f32[16,2,136,512]{3,2,1,0:T(8,128)}, f32[16,16,8,512]{3,2,1,0:T(8,128)}, f32[16,16,8,512]{3,2,1,0:T(8,128)}, f32[2,16,16,512]{3,2,1,0:T(8,128)}) custom-call(s32[1]{0:T(128)} %bitcast.core, bf16[3,128,8192]{2,1,0:T(8,128)(2,1)} %bitcast.89, bf16[4,8,8192]{2,1,0:T(8,128)(2,1)S(1)} %collective-permute-done.hx, ...), custom_call_target="tpu_custom_call" | custom-call | tf_op jit(solution)/shard_map/states/pallas_call | solution.py:456
  32.8 4.9 %collective-permute-start.2 = (f32[2,16,16,512]{3,2,1,0:T(8,128)}, f32[2,16,16,512]{3,2,1,0:T(8,128)}, u32[]{:S(2)}, u32[]{:S(2)}) collective-permute-start(f32[2,16,16,512]{3,2,1,0:T(8,128)} %get-tuple-element.52), channel_id=1, source_target_pairs={{0,1},{1,0},{2,3},{3,2},{4,5},{5,4},{6,7},{7,6},{8,9},{9,8},{10,11... | collective-permute-start | bytes 3145736 | tf_op jit(solution)/shard_map/ppermute | solution.py:315
  37.6 2.6 %collective-permute-done.2.other = f32[2,16,16,512]{3,2,1,0:T(8,128)} collective-permute-done((f32[2,16,16,512]{3,2,1,0:T(8,128)}, f32[2,16,16,512]{3,2,1,0:T(8,128)}, u32[]{:S(2)}, u32[]{:S(2)}) %collective-permute-start.2) | collective-permute-done | bytes 1048608 | tf_op jit(solution)/shard_map/ppermute | solution.py:315
  40.2 1.3 dynamic-slice_select_fusion.1
  41.6 0.1 broadcast_select_fusion.4
  41.7 2.1 %collective-permute-start.3 = (f32[8,16,512]{2,1,0:T(8,128)S(1)}, f32[8,16,512]{2,1,0:T(8,128)S(1)}, u32[]{:S(2)}, u32[]{:S(2)}) collective-permute-start(f32[8,16,512]{2,1,0:T(8,128)S(1)} %broadcast_select_fusion.4), channel_id=1, source_target_pairs={{0,2},{1,3},{2,0},{3,1},{4,6},{5,7},{6,4},{7,5},{8,10},{9,11},{10,... | collective-permute-start | bytes 786440 | tf_op jit(solution)/shard_map/ppermute | solution.py:331
  43.8 8.2 %blocks.3 = (f32[16,2,136,512]{3,2,1,0:T(8,128)}, f32[16,16,8,512]{3,2,1,0:T(8,128)}, f32[16,16,8,512]{3,2,1,0:T(8,128)}, f32[6,8,512]{2,1,0:T(8,128)S(1)}) custom-call(f32[16,2,136,512]{3,2,1,0:T(8,128)} %get-tuple-element.53.xg, f32[16,16,8,512]{3,2,1,0:T(8,128)} %get-tuple-element.54.blocks_e, ...), custom_call_target="tpu_custom_call", output_to_operand_aliasing={{0}: (0, {}), {1}: (1, {}), {2}: (2, {})} | custom-call | flops 62914560 | bytes 36700160 | tf_op jit(solution)/shard_map/blocks/pallas_call | solution.py:486
  52.0 0.1 multiply_add_fusion.1
  52.1 0.7 collective-permute-start.4
  52.8 5.8 %blocks.4 = (f32[16,2,136,512]{3,2,1,0:T(8,128)}, f32[16,16,8,512]{3,2,1,0:T(8,128)}, f32[16,16,8,512]{3,2,1,0:T(8,128)}, f32[4,8,512]{2,1,0:T(8,128)S(1)}) custom-call(f32[16,2,136,512]{3,2,1,0:T(8,128)} %get-tuple-element.65.xg, f32[16,16,8,512]{3,2,1,0:T(8,128)} %get-tuple-element.66.blocks_e, ...), custom_call_target="tpu_custom_call", output_to_operand_aliasing={{0}: (0, {}), {1}: (1, {}), {2}: (2, {})} | custom-call | flops 62914560 | bytes 36700160 | tf_op jit(solution)/shard_map/blocks/pallas_call | solution.py:486
  58.6 0.0 copy-start.4
  58.7 1.4 %collective-permute-start.5 = (f32[8,16,512]{2,1,0:T(8,128)S(1)}, f32[8,16,512]{2,1,0:T(8,128)S(1)}, u32[]{:S(2)}, u32[]{:S(2)}) collective-permute-start(f32[8,16,512]{2,1,0:T(8,128)S(1)} %collective-permute-done.4), channel_id=1, source_target_pairs={{4,6},{5,7},{2,0},{3,1},{12,14},{13,15},{10,8},{11,9},{20,22},{21,... | collective-permute-start | bytes 786440 | tf_op jit(solution)/shard_map/ppermute | solution.py:347
  60.1 8.1 %blocks.5 = (f32[16,2,136,512]{3,2,1,0:T(8,128)}, f32[16,16,8,512]{3,2,1,0:T(8,128)}, f32[16,16,8,512]{3,2,1,0:T(8,128)}, f32[6,8,512]{2,1,0:T(8,128)S(1)}) custom-call(f32[16,2,136,512]{3,2,1,0:T(8,128)} %get-tuple-element.75.xg, f32[16,16,8,512]{3,2,1,0:T(8,128)} %get-tuple-element.76.blocks_e, ...), custom_call_target="tpu_custom_call", output_to_operand_aliasing={{0}: (0, {}), {1}: (1, {}), {2}: (2, {})} | custom-call | flops 62914560 | bytes 36700160 | tf_op jit(solution)/shard_map/blocks/pallas_call | solution.py:486
  68.2 2.4 %collective-permute-done.5 = f32[8,16,512]{2,1,0:T(8,128)S(1)} collective-permute-done((f32[8,16,512]{2,1,0:T(8,128)S(1)}, f32[8,16,512]{2,1,0:T(8,128)S(1)}, u32[]{:S(2)}, u32[]{:S(2)}) %collective-permute-start.5) | collective-permute-done | bytes 262176 | tf_op jit(solution)/shard_map/ppermute | solution.py:347
  70.7 0.1 select_bitcast_fusion.1
  70.8 0.1 collective-permute-start.6
  70.9 1.9 %collective-permute-done.6.found = f32[2,8,16,512]{3,2,1,0:T(8,128)S(1)} collective-permute-done((f32[2,8,16,512]{3,2,1,0:T(8,128)S(1)}, f32[2,8,16,512]{3,2,1,0:T(8,128)S(1)}, u32[]{:S(2)}, u32[]{:S(2)}) %collective-permute-start.6) | collective-permute-done | bytes 524320 | tf_op jit(solution)/shard_map/ppermute | solution.py:315
  72.8 31.5 %final.1 = (bf16[128,8192]{1,0:T(8,128)(2,1)}, bf16[3,128,8192]{2,1,0:T(8,128)(2,1)}, f32[32,24,256]{2,1,0:T(8,128)S(1)}) custom-call(s32[1]{0:T(128)} %bitcast.core, bf16[3,128,8192]{2,1,0:T(8,128)(2,1)} %bitcast.90, bf16[4,8,8192]{2,1,0:T(8,128)(2,1)S(1)} %collective-permute-done.hx, bf16[4,8,8192]{2,1,0:T(8,128)(2,1)S(1)} %copy-done.3, ...), custom_call_target="tpu_custom_call" | custom-call | tf_op jit(solution)/shard_map/final/pallas_call | solution.py:528
  104.3 0.1 slice_select_fusion
  104.3 0.2 collective-permute-start.7
  104.5 1.6 %collective-permute-done.7 = f32[16,24,256]{2,1,0:T(8,128)S(1)} collective-permute-done((f32[16,24,256]{2,1,0:T(8,128)S(1)}, f32[16,24,256]{2,1,0:T(8,128)S(1)}, u32[]{:S(2)}, u32[]{:S(2)}) %collective-permute-start.7) | collective-permute-done | bytes 393248 | tf_op jit(solution)/shard_map/ppermute | solution.py:315
  106.1 0.1 select_add_fusion
  106.2 2.5 %collective-permute-start.10 = (f32[4,24,256]{2,1,0:T(8,128)S(1)}, f32[4,24,256]{2,1,0:T(8,128)S(1)}, u32[]{:S(2)}, u32[]{:S(2)}) collective-permute-start(f32[4,24,256]{2,1,0:T(8,128)S(1)} %get-tuple-element.111), channel_id=1, source_target_pairs={{0,24},{8,16},{16,8},{24,0},{1,25},{9,17},{17,9},{25,1},{2,26},{10... | collective-permute-start | bytes 294920 | tf_op jit(solution)/shard_map/ppermute | solution.py:331
  108.7 0.5 collective-permute-start.9
  109.2 0.5 collective-permute-start.8
  109.8 2.3 %collective-permute-done.10 = f32[4,24,256]{2,1,0:T(8,128)S(1)} collective-permute-done((f32[4,24,256]{2,1,0:T(8,128)S(1)}, f32[4,24,256]{2,1,0:T(8,128)S(1)}, u32[]{:S(2)}, u32[]{:S(2)}) %collective-permute-start.10) | collective-permute-done | bytes 98336 | tf_op jit(solution)/shard_map/ppermute | solution.py:331
  112.1 2.0 %collective-permute-done.9 = f32[4,24,256]{2,1,0:T(8,128)S(1)} collective-permute-done((f32[4,24,256]{2,1,0:T(8,128)S(1)}, f32[4,24,256]{2,1,0:T(8,128)S(1)}, u32[]{:S(2)}, u32[]{:S(2)}) %collective-permute-start.9) | collective-permute-done | bytes 98336 | tf_op jit(solution)/shard_map/ppermute | solution.py:331
  114.1 0.1 collective-permute-done.8
  114.2 2.5 %collective-permute-start.11 = (f32[4,24,256]{2,1,0:T(8,128)S(1)}, f32[4,24,256]{2,1,0:T(8,128)S(1)}, u32[]{:S(2)}, u32[]{:S(2)}) collective-permute-start(f32[4,24,256]{2,1,0:T(8,128)S(1)} %add_add_fusion), channel_id=1, source_target_pairs={{0,2},{1,3},{2,0},{3,1},{4,6},{5,7},{6,4},{7,5},{8,10},{9,11},{10,... | collective-permute-start | bytes 294920 | tf_op jit(solution)/shard_map/ppermute | solution.py:331
  116.7 2.7 %collective-permute-done.11 = f32[4,24,256]{2,1,0:T(8,128)S(1)} collective-permute-done((f32[4,24,256]{2,1,0:T(8,128)S(1)}, f32[4,24,256]{2,1,0:T(8,128)S(1)}, u32[]{:S(2)}, u32[]{:S(2)}) %collective-permute-start.11) | collective-permute-done | bytes 98336 | tf_op jit(solution)/shard_map/ppermute | solution.py:331
  119.5 3.1 %collective-permute-start.12 = (f32[4,24,256]{2,1,0:T(8,128)S(1)}, f32[4,24,256]{2,1,0:T(8,128)S(1)}, u32[]{:S(2)}, u32[]{:S(2)}) collective-permute-start(f32[4,24,256]{2,1,0:T(8,128)S(1)} %add.68), channel_id=1, source_target_pairs={{0,4},{1,5},{2,6},{3,7},{4,0},{5,1},{6,2},{7,3},{8,12},{9,13},{10,... | collective-permute-start | bytes 294920 | tf_op jit(solution)/shard_map/ppermute | solution.py:331
  122.6 2.8 %collective-permute-done.12 = f32[4,24,256]{2,1,0:T(8,128)S(1)} collective-permute-done((f32[4,24,256]{2,1,0:T(8,128)S(1)}, f32[4,24,256]{2,1,0:T(8,128)S(1)}, u32[]{:S(2)}, u32[]{:S(2)}) %collective-permute-start.12) | collective-permute-done | bytes 98336 | tf_op jit(solution)/shard_map/ppermute | solution.py:331
  125.5 2.9 %collective-permute-start.13 = (f32[4,24,256]{2,1,0:T(8,128)S(1)}, f32[4,24,256]{2,1,0:T(8,128)S(1)}, u32[]{:S(2)}, u32[]{:S(2)}) collective-permute-start(f32[4,24,256]{2,1,0:T(8,128)S(1)} %get-tuple-element.95), channel_id=1, source_target_pairs={{0,8},{8,0},{16,24},{24,16},{1,9},{9,1},{17,25},{25,17},{2,10},{10... | collective-permute-start | bytes 294920 | tf_op jit(solution)/shard_map/ppermute | solution.py:331
  128.4 0.2 collective-permute-start.14
  128.6 1.4 %collective-permute-start.15 = (f32[4,24,256]{2,1,0:T(8,128)S(1)}, f32[4,24,256]{2,1,0:T(8,128)S(1)}, u32[]{:S(2)}, u32[]{:S(2)}) collective-permute-start(f32[4,24,256]{2,1,0:T(8,128)S(1)} %get-tuple-element.95), channel_id=1, source_target_pairs={{0,24},{8,16},{16,8},{24,0},{1,25},{9,17},{17,9},{25,1},{2,26},{10... | collective-permute-start | bytes 294920 | tf_op jit(solution)/shard_map/ppermute | solution.py:331
  130.0 1.8 %collective-permute-done.13 = f32[4,24,256]{2,1,0:T(8,128)S(1)} collective-permute-done((f32[4,24,256]{2,1,0:T(8,128)S(1)}, f32[4,24,256]{2,1,0:T(8,128)S(1)}, u32[]{:S(2)}, u32[]{:S(2)}) %collective-permute-start.13) | collective-permute-done | bytes 98336 | tf_op jit(solution)/shard_map/ppermute | solution.py:331
  131.8 1.2 collective-permute-done.14
  133.0 1.1 collective-permute-done.15
  134.2 0.1 collective-permute-start.16
  134.2 1.7 %collective-permute-done.16 = f32[16,24,256]{2,1,0:T(8,128)S(1)} collective-permute-done((f32[16,24,256]{2,1,0:T(8,128)S(1)}, f32[16,24,256]{2,1,0:T(8,128)S(1)}, u32[]{:S(2)}, u32[]{:S(2)}) %collective-permute-start.16) | collective-permute-done | bytes 393248 | tf_op jit(solution)/shard_map/ppermute | solution.py:315
  136.0 0.1 broadcast_select_fusion.3
  136.0 0.1 maximum_bitcast_fusion
  136.1 0.3 copy.25
  136.3 0.1 reshape.33
  136.5 0.0 copy-start.7
  136.5 0.7 slice.67
  137.2 0.2 copy-done.7
  (43 shorter events, 0.5 us)
Async XLA Ops:
  0.6 7.8 %copy-start.11 = (f32[4]{0:T(128)S(1)}, f32[4]{0:T(128)}, u32[]{:S(2)}) copy-start(f32[4]{0:T(128)} %constant.68) | copy-start | bytes 52
  0.6 8.0 %copy-start.10 = (f32[4,8]{1,0:T(4,128)S(1)}, f32[4,8]{1,0:T(4,128)}, u32[]{:S(2)}) copy-start(f32[4,8]{1,0:T(4,128)} %constant.70) | copy-start | bytes 388
  0.7 8.2 %copy-start.14 = (f32[24]{0:T(128)S(1)}, f32[24]{0:T(128)}, u32[]{:S(2)}) copy-start(f32[24]{0:T(128)} %constant.66) | copy-start | bytes 292
  0.7 7.8 %copy-start.9 = (f32[512,16]{0,1:T(8,128)S(1)}, f32[512,16]{0,1:T(8,128)}, u32[]{:S(2)}) copy-start(f32[512,16]{0,1:T(8,128)} %param.14) | copy-start | bytes 98308
  0.7 7.9 %copy-start.8 = (f32[512,16]{0,1:T(8,128)S(1)}, f32[512,16]{0,1:T(8,128)}, u32[]{:S(2)}) copy-start(f32[512,16]{0,1:T(8,128)} %param.13) | copy-start | bytes 98308
  1.7 8.3 %copy-start.12 = (pred[4,8]{1,0:T(4,128)(4,1)S(1)}, pred[4,8]{1,0:T(4,128)(4,1)}, u32[]{:S(2)}) copy-start(pred[4,8]{1,0:T(4,128)(4,1)} %constant.69) | copy-start | bytes 100
  1.7 8.3 %copy-start.13 = (pred[4,8]{1,0:T(4,128)(4,1)S(1)}, pred[4,8]{1,0:T(4,128)(4,1)}, u32[]{:S(2)}) copy-start(pred[4,8]{1,0:T(4,128)(4,1)} %constant.67) | copy-start | bytes 100
  2.9 7.4 %copy-start = (bf16[1,128,8192]{2,1,0:T(8,128)(2,1)S(1)}, bf16[1,128,8192]{2,1,0:T(8,128)(2,1)}, u32[]{:S(2)}) copy-start(bf16[1,128,8192]{2,1,0:T(8,128)(2,1)} %param.16) | copy-start | bytes 6291460
  2.9 7.4 %copy-start.1 = (f32[3,7,8192]{2,1,0:T(8,128)S(1)}, f32[3,7,8192]{2,1,0:T(8,128)}, u32[]{:S(2)}) copy-start(f32[3,7,8192]{2,1,0:T(8,128)} %filt.3) | copy-start | bytes 2064388
  3.0 7.3 %collective-permute-start = (bf16[4,8,8192]{2,1,0:T(8,128)(2,1)S(1)}, bf16[4,8,8192]{2,1,0:T(8,128)(2,1)S(1)}, u32[]{:S(2)}, u32[]{:S(2)}) collective-permute-start(bf16[4,8,8192]{2,1,0:T(8,128)(2,1)S(1)} %pad_maximum_fusion), channel_id=1, source_target_pairs={{1,2},{3,4},{5,6},{2,1},{4,3},{6,5},{9,10},{11,12},{13,14},{10,9},... | collective-permute-start | bytes 1572872 | tf_op jit(solution)/shard_map/ppermute | solution.py:408
  3.9 6.5 %collective-permute-start.1 = (bf16[4,8,8192]{2,1,0:T(8,128)(2,1)S(1)}, bf16[4,8,8192]{2,1,0:T(8,128)(2,1)S(1)}, u32[]{:S(2)}, u32[]{:S(2)}) collective-permute-start(bf16[4,8,8192]{2,1,0:T(8,128)(2,1)S(1)} %pad_maximum_fusion.1), channel_id=1, source_target_pairs={{0,1},{1,0},{2,3},{3,2},{4,5},{5,4},{6,7},{7,6},{8,9},{9,8},{10,11... | collective-permute-start | bytes 1572872 | tf_op jit(solution)/shard_map/ppermute | solution.py:315
  10.3 22.4 %copy-start.2 = (bf16[4,8,8192]{2,1,0:T(8,128)(2,1)}, bf16[4,8,8192]{2,1,0:T(8,128)(2,1)S(1)}, u32[]{:S(2)}) copy-start(bf16[4,8,8192]{2,1,0:T(8,128)(2,1)S(1)} %collective-permute-done.1.hi) | copy-start | bytes 1572868
  10.4 33.4 %copy-start.6 = (f32[8192]{0:T(1024)S(1)}, f32[8192]{0:T(1024)}, u32[]{:S(2)}) copy-start(f32[8192]{0:T(1024)} %param.15) | copy-start | bytes 98308
  32.8 7.5 %collective-permute-start.2 = (f32[2,16,16,512]{3,2,1,0:T(8,128)}, f32[2,16,16,512]{3,2,1,0:T(8,128)}, u32[]{:S(2)}, u32[]{:S(2)}) collective-permute-start(f32[2,16,16,512]{3,2,1,0:T(8,128)} %get-tuple-element.52), channel_id=1, source_target_pairs={{0,1},{1,0},{2,3},{3,2},{4,5},{5,4},{6,7},{7,6},{8,9},{9,8},{10,11... | collective-permute-start | bytes 3145736 | tf_op jit(solution)/shard_map/ppermute | solution.py:315
  41.7 10.3 %collective-permute-start.3 = (f32[8,16,512]{2,1,0:T(8,128)S(1)}, f32[8,16,512]{2,1,0:T(8,128)S(1)}, u32[]{:S(2)}, u32[]{:S(2)}) collective-permute-start(f32[8,16,512]{2,1,0:T(8,128)S(1)} %broadcast_select_fusion.4), channel_id=1, source_target_pairs={{0,2},{1,3},{2,0},{3,1},{4,6},{5,7},{6,4},{7,5},{8,10},{9,11},{10,... | collective-permute-start | bytes 786440 | tf_op jit(solution)/shard_map/ppermute | solution.py:331
  52.1 6.5 %collective-permute-start.4 = (f32[8,16,512]{2,1,0:T(8,128)S(1)}, f32[8,16,512]{2,1,0:T(8,128)S(1)}, u32[]{:S(2)}, u32[]{:S(2)}) collective-permute-start(f32[8,16,512]{2,1,0:T(8,128)S(1)} %multiply_add_fusion.1), channel_id=1, source_target_pairs={{2,4},{3,5},{4,2},{5,3},{10,12},{11,13},{12,10},{13,11},{18,20},{1... | collective-permute-start | bytes 786440 | tf_op jit(solution)/shard_map/ppermute | solution.py:344
  58.6 14.1 %copy-start.3 = (bf16[4,8,8192]{2,1,0:T(8,128)(2,1)S(1)}, bf16[4,8,8192]{2,1,0:T(8,128)(2,1)}, u32[]{:S(2)}) copy-start(bf16[4,8,8192]{2,1,0:T(8,128)(2,1)} %copy-done.2) | copy-start | bytes 1572868
  58.6 14.1 %copy-start.4 = (f32[16,8,512]{2,1,0:T(8,128)S(1)}, f32[16,8,512]{2,1,0:T(8,128)}, u32[]{:S(2)}) copy-start(f32[16,8,512]{2,1,0:T(8,128)} %get-tuple-element.90.cy) | copy-start | bytes 786436
  58.7 14.1 %copy-start.5 = (f32[16,8,512]{2,1,0:T(8,128)S(1)}, f32[16,8,512]{2,1,0:T(8,128)}, u32[]{:S(2)}) copy-start(f32[16,8,512]{2,1,0:T(8,128)} %get-tuple-element.89.cz) | copy-start | bytes 786436
  58.7 12.0 %collective-permute-start.5 = (f32[8,16,512]{2,1,0:T(8,128)S(1)}, f32[8,16,512]{2,1,0:T(8,128)S(1)}, u32[]{:S(2)}, u32[]{:S(2)}) collective-permute-start(f32[8,16,512]{2,1,0:T(8,128)S(1)} %collective-permute-done.4), channel_id=1, source_target_pairs={{4,6},{5,7},{2,0},{3,1},{12,14},{13,15},{10,8},{11,9},{20,22},{21,... | collective-permute-start | bytes 786440 | tf_op jit(solution)/shard_map/ppermute | solution.py:347
  70.8 2.0 %collective-permute-start.6 = (f32[2,8,16,512]{3,2,1,0:T(8,128)S(1)}, f32[2,8,16,512]{3,2,1,0:T(8,128)S(1)}, u32[]{:S(2)}, u32[]{:S(2)}) collective-permute-start(f32[2,8,16,512]{3,2,1,0:T(8,128)S(1)} %pad_maximum_fusion.2.both), channel_id=1, source_target_pairs={{0,1},{1,0},{2,3},{3,2},{4,5},{5,4},{6,7},{7,6},{8,9},{9,8},{10,11... | collective-permute-start | bytes 1572872 | tf_op jit(solution)/shard_map/ppermute | solution.py:315
  104.3 1.8 %collective-permute-start.7 = (f32[16,24,256]{2,1,0:T(8,128)S(1)}, f32[16,24,256]{2,1,0:T(8,128)S(1)}, u32[]{:S(2)}, u32[]{:S(2)}) collective-permute-start(f32[16,24,256]{2,1,0:T(8,128)S(1)} %slice_select_fusion), channel_id=1, source_target_pairs={{0,1},{1,0},{2,3},{3,2},{4,5},{5,4},{6,7},{7,6},{8,9},{9,8},{10,11... | collective-permute-start | bytes 1179656 | tf_op jit(solution)/shard_map/ppermute | solution.py:315
  106.2 5.9 %collective-permute-start.10 = (f32[4,24,256]{2,1,0:T(8,128)S(1)}, f32[4,24,256]{2,1,0:T(8,128)S(1)}, u32[]{:S(2)}, u32[]{:S(2)}) collective-permute-start(f32[4,24,256]{2,1,0:T(8,128)S(1)} %get-tuple-element.111), channel_id=1, source_target_pairs={{0,24},{8,16},{16,8},{24,0},{1,25},{9,17},{17,9},{25,1},{2,26},{10... | collective-permute-start | bytes 294920 | tf_op jit(solution)/shard_map/ppermute | solution.py:331
  108.7 5.4 %collective-permute-start.9 = (f32[4,24,256]{2,1,0:T(8,128)S(1)}, f32[4,24,256]{2,1,0:T(8,128)S(1)}, u32[]{:S(2)}, u32[]{:S(2)}) collective-permute-start(f32[4,24,256]{2,1,0:T(8,128)S(1)} %get-tuple-element.112), channel_id=1, source_target_pairs={{0,16},{8,24},{16,0},{24,8},{1,17},{9,25},{17,1},{25,9},{2,18},{10... | collective-permute-start | bytes 294920 | tf_op jit(solution)/shard_map/ppermute | solution.py:331
  109.2 4.9 %collective-permute-start.8 = (f32[4,24,256]{2,1,0:T(8,128)S(1)}, f32[4,24,256]{2,1,0:T(8,128)S(1)}, u32[]{:S(2)}, u32[]{:S(2)}) collective-permute-start(f32[4,24,256]{2,1,0:T(8,128)S(1)} %get-tuple-element.110), channel_id=1, source_target_pairs={{0,8},{8,0},{16,24},{24,16},{1,9},{9,1},{17,25},{25,17},{2,10},{10... | collective-permute-start | bytes 294920 | tf_op jit(solution)/shard_map/ppermute | solution.py:331
  114.2 5.2 %collective-permute-start.11 = (f32[4,24,256]{2,1,0:T(8,128)S(1)}, f32[4,24,256]{2,1,0:T(8,128)S(1)}, u32[]{:S(2)}, u32[]{:S(2)}) collective-permute-start(f32[4,24,256]{2,1,0:T(8,128)S(1)} %add_add_fusion), channel_id=1, source_target_pairs={{0,2},{1,3},{2,0},{3,1},{4,6},{5,7},{6,4},{7,5},{8,10},{9,11},{10,... | collective-permute-start | bytes 294920 | tf_op jit(solution)/shard_map/ppermute | solution.py:331
  119.5 5.9 %collective-permute-start.12 = (f32[4,24,256]{2,1,0:T(8,128)S(1)}, f32[4,24,256]{2,1,0:T(8,128)S(1)}, u32[]{:S(2)}, u32[]{:S(2)}) collective-permute-start(f32[4,24,256]{2,1,0:T(8,128)S(1)} %add.68), channel_id=1, source_target_pairs={{0,4},{1,5},{2,6},{3,7},{4,0},{5,1},{6,2},{7,3},{8,12},{9,13},{10,... | collective-permute-start | bytes 294920 | tf_op jit(solution)/shard_map/ppermute | solution.py:331
  125.5 6.3 %collective-permute-start.13 = (f32[4,24,256]{2,1,0:T(8,128)S(1)}, f32[4,24,256]{2,1,0:T(8,128)S(1)}, u32[]{:S(2)}, u32[]{:S(2)}) collective-permute-start(f32[4,24,256]{2,1,0:T(8,128)S(1)} %get-tuple-element.95), channel_id=1, source_target_pairs={{0,8},{8,0},{16,24},{24,16},{1,9},{9,1},{17,25},{25,17},{2,10},{10... | collective-permute-start | bytes 294920 | tf_op jit(solution)/shard_map/ppermute | solution.py:331
  128.4 4.6 %collective-permute-start.14 = (f32[4,24,256]{2,1,0:T(8,128)S(1)}, f32[4,24,256]{2,1,0:T(8,128)S(1)}, u32[]{:S(2)}, u32[]{:S(2)}) collective-permute-start(f32[4,24,256]{2,1,0:T(8,128)S(1)} %get-tuple-element.95), channel_id=1, source_target_pairs={{0,16},{8,24},{16,0},{24,8},{1,17},{9,25},{17,1},{25,9},{2,18},{10... | collective-permute-start | bytes 294920 | tf_op jit(solution)/shard_map/ppermute | solution.py:331
  128.6 5.5 %collective-permute-start.15 = (f32[4,24,256]{2,1,0:T(8,128)S(1)}, f32[4,24,256]{2,1,0:T(8,128)S(1)}, u32[]{:S(2)}, u32[]{:S(2)}) collective-permute-start(f32[4,24,256]{2,1,0:T(8,128)S(1)} %get-tuple-element.95), channel_id=1, source_target_pairs={{0,24},{8,16},{16,8},{24,0},{1,25},{9,17},{17,9},{25,1},{2,26},{10... | collective-permute-start | bytes 294920 | tf_op jit(solution)/shard_map/ppermute | solution.py:331
  134.2 1.8 %collective-permute-start.16 = (f32[16,24,256]{2,1,0:T(8,128)S(1)}, f32[16,24,256]{2,1,0:T(8,128)S(1)}, u32[]{:S(2)}, u32[]{:S(2)}) collective-permute-start(f32[16,24,256]{2,1,0:T(8,128)S(1)} %constant_dynamic-update-slice_fusion), channel_id=1, source_target_pairs={{0,1},{1,0},{2,3},{3,2},{4,5},{5,4},{6,7},{7,6},{8,9},{9,8},{10,11... | collective-permute-start | bytes 1179656 | tf_op jit(solution)/shard_map/ppermute | solution.py:315
  136.5 0.9 copy-start.7

commit v20 on v15

--- a/solution.py
+++ b/solution.py
@@ -371,11 +371,10 @@
     total = piece(0)
     for term in [paired(piece(k), "dp", k) for k in range(1, parts)]:
         total = total + term
-    count = lax.axis_size("ctx")
-    reaches = [2 << k for k in range((count // 2).bit_length() - 1)]
-    for near, far in zip(reaches, reversed(reaches)):
-        pairs = [(s, s ^ (far if s % 2 else near)) for s in range(count)]
-        total = total + lax.ppermute(total, "ctx", pairs)
+    reach = 2
+    while reach < lax.axis_size("ctx"):
+        total = total + paired(total, "ctx", reach)
+        reach = 2 * reach
     value = jnp.zeros((half,) + value.shape[1:], F32)
     for k in range(parts):
         term = paired(total, "dp", k) if k else total

time: 137 us -> 138 us (level)
  starting transfers between devices: 26.6 us -> 28.4 us
    ppermute x2 -> x0, waiting for transfers between devices: 6.94 us -> none  [summed(): total = total + lax.ppermute(total, 'ctx', pairs)]
    ppermute x7 -> x9, starting transfers between devices: 9.16 us -> 15.8 us  [paired(): lax.ppermute(value, axis, [(source, source ^ step) for source in lines or...]
    ppermute x7 -> x9, waiting for transfers between devices: 8.19 us -> 14.1 us  [paired(): lax.ppermute(value, axis, [(source, source ^ step) for source in lines or...]
    ppermute x2 -> x0, starting transfers between devices: 4.74 us -> none  [summed(): total = total + lax.ppermute(total, 'ctx', pairs)]
where the time goes in v20:
time: 138 us; the launch traced here: 137 us
  Pallas kernels  75.9 us (55%)
  starting transfers between devices  28.4 us (21%)
  waiting for transfers between devices  24.4 us (18%)
  other arithmetic  3.86 us (3%)
  local copies, waits for them, and re-layouts  3.67 us (3%)
    pallas_call x1, Pallas kernels, local(): pl.pallas_call(final_kernel, grid=(width // each,), in_specs=[pl.BlockSpe...  31.5 us
    pallas_call x1, Pallas kernels, local(): pl.pallas_call(states_kernel, grid=(width // each,), in_specs=[pl.BlockSp...  22.3 us
    pallas_call x3, Pallas kernels, call(): pl.pallas_call(blocks_kernel, grid=(last - first,), in_specs=[pairs, stat...  22.1 us
    ppermute x9, starting transfers between devices, paired(): lax.ppermute(value, axis, [(source, source ^ step) for source in lines or...  15.8 us
    ppermute x9, waiting for transfers between devices, paired(): lax.ppermute(value, axis, [(source, source ^ step) for source in lines or...  14.1 us
    ppermute x5, starting transfers between devices, swapped(): return lax.ppermute(value, 'ctx', [(s, s ^ 1) for s in range(count)])  9.73 us
    ppermute x5, waiting for transfers between devices, swapped(): return lax.ppermute(value, 'ctx', [(s, s ^ 1) for s in range(count)])  7.85 us
  transfers between devices with their start and end apart: 17, of which 13 were waited for; matrix products, arithmetic and copies ran while one was open for 1% of the time, Pallas kernels for 16%

profile of v20, /device:TPU:0, one launch (start us, length us, event | category | flops | bytes accessed | tf_op | source)
XLA Modules:
  0.0 137.3 jit_solution(2994702079699089949)
XLA Ops:
  0.6 0.0 copy-start.11
  0.6 0.0 copy-start.10
  0.7 0.0 copy-start.14
  0.7 1.0 constant_dynamic-slice_fusion.3
  1.7 0.0 copy-start.12
  1.7 0.0 copy-start.13
  1.7 1.2 dynamic-slice_bitcast_fusion
  2.9 0.0 copy-start.1
  3.0 0.8 collective-permute-start
  3.9 4.5 %collective-permute-start.1 = (bf16[4,8,8192]{2,1,0:T(8,128)(2,1)S(1)}, bf16[4,8,8192]{2,1,0:T(8,128)(2,1)S(1)}, u32[]{:S(2)}, u32[]{:S(2)}) collective-permute-start(bf16[4,8,8192]{2,1,0:T(8,128)(2,1)S(1)} %pad_maximum_fusion.1), channel_id=1, source_target_pairs={{0,1},{1,0},{2,3},{3,2},{4,5},{5,4},{6,7},{7,6},{8,9},{9,8},{10,11... | collective-permute-start | bytes 1572872 | tf_op jit(solution)/shard_map/ppermute | solution.py:313
  8.5 0.1 multiply_exponential_fusion.1
  8.6 0.2 multiply_exponential_fusion
  8.9 0.2 multiply_reduce_fusion.near
  9.1 0.8 fusion.4
  10.0 0.3 broadcast_select_fusion
  10.3 0.0 copy-start.2
  10.4 0.0 copy-start.6
  10.4 22.3 %states.1 = (f32[16,3,136,512]{3,2,1,0:T(8,128)}, f32[16,2,136,512]{3,2,1,0:T(8,128)}, f32[16,16,8,512]{3,2,1,0:T(8,128)}, f32[16,16,8,512]{3,2,1,0:T(8,128)}, f32[2,16,16,512]{3,2,1,0:T(8,128)}) custom-call(s32[1]{0:T(128)} %bitcast.core, bf16[3,128,8192]{2,1,0:T(8,128)(2,1)} %bitcast.89, bf16[4,8,8192]{2,1,0:T(8,128)(2,1)S(1)} %collective-permute-done.hx, ...), custom_call_target="tpu_custom_call" | custom-call | tf_op jit(solution)/shard_map/states/pallas_call | solution.py:454
  32.6 4.9 %collective-permute-start.2 = (f32[2,16,16,512]{3,2,1,0:T(8,128)}, f32[2,16,16,512]{3,2,1,0:T(8,128)}, u32[]{:S(2)}, u32[]{:S(2)}) collective-permute-start(f32[2,16,16,512]{3,2,1,0:T(8,128)} %get-tuple-element.52), channel_id=1, source_target_pairs={{0,1},{1,0},{2,3},{3,2},{4,5},{5,4},{6,7},{7,6},{8,9},{9,8},{10,11... | collective-permute-start | bytes 3145736 | tf_op jit(solution)/shard_map/ppermute | solution.py:313
  37.5 2.6 %collective-permute-done.2.other = f32[2,16,16,512]{3,2,1,0:T(8,128)} collective-permute-done((f32[2,16,16,512]{3,2,1,0:T(8,128)}, f32[2,16,16,512]{3,2,1,0:T(8,128)}, u32[]{:S(2)}, u32[]{:S(2)}) %collective-permute-start.2) | collective-permute-done | bytes 1048608 | tf_op jit(solution)/shard_map/ppermute | solution.py:313
  40.1 1.3 dynamic-slice_select_fusion.1
  41.5 0.1 broadcast_select_fusion.4
  41.6 2.1 %collective-permute-start.3 = (f32[8,16,512]{2,1,0:T(8,128)S(1)}, f32[8,16,512]{2,1,0:T(8,128)S(1)}, u32[]{:S(2)}, u32[]{:S(2)}) collective-permute-start(f32[8,16,512]{2,1,0:T(8,128)S(1)} %broadcast_select_fusion.4), channel_id=1, source_target_pairs={{0,2},{1,3},{2,0},{3,1},{4,6},{5,7},{6,4},{7,5},{8,10},{9,11},{10,... | collective-permute-start | bytes 786440 | tf_op jit(solution)/shard_map/ppermute | solution.py:329
  43.7 8.2 %blocks.3 = (f32[16,2,136,512]{3,2,1,0:T(8,128)}, f32[16,16,8,512]{3,2,1,0:T(8,128)}, f32[16,16,8,512]{3,2,1,0:T(8,128)}, f32[6,8,512]{2,1,0:T(8,128)S(1)}) custom-call(f32[16,2,136,512]{3,2,1,0:T(8,128)} %get-tuple-element.53.xg, f32[16,16,8,512]{3,2,1,0:T(8,128)} %get-tuple-element.54.blocks_e, ...), custom_call_target="tpu_custom_call", output_to_operand_aliasing={{0}: (0, {}), {1}: (1, {}), {2}: (2, {})} | custom-call | flops 62914560 | bytes 36700160 | tf_op jit(solution)/shard_map/blocks/pallas_call | solution.py:484
  51.8 0.1 multiply_add_fusion.1
  52.0 0.7 collective-permute-start.4
  52.7 5.8 %blocks.4 = (f32[16,2,136,512]{3,2,1,0:T(8,128)}, f32[16,16,8,512]{3,2,1,0:T(8,128)}, f32[16,16,8,512]{3,2,1,0:T(8,128)}, f32[4,8,512]{2,1,0:T(8,128)S(1)}) custom-call(f32[16,2,136,512]{3,2,1,0:T(8,128)} %get-tuple-element.65.xg, f32[16,16,8,512]{3,2,1,0:T(8,128)} %get-tuple-element.66.blocks_e, ...), custom_call_target="tpu_custom_call", output_to_operand_aliasing={{0}: (0, {}), {1}: (1, {}), {2}: (2, {})} | custom-call | flops 62914560 | bytes 36700160 | tf_op jit(solution)/shard_map/blocks/pallas_call | solution.py:484
  58.5 0.0 copy-start.3
  58.5 0.0 copy-start.4
  58.6 1.4 %collective-permute-start.5 = (f32[8,16,512]{2,1,0:T(8,128)S(1)}, f32[8,16,512]{2,1,0:T(8,128)S(1)}, u32[]{:S(2)}, u32[]{:S(2)}) collective-permute-start(f32[8,16,512]{2,1,0:T(8,128)S(1)} %collective-permute-done.4), channel_id=1, source_target_pairs={{4,6},{5,7},{2,0},{3,1},{12,14},{13,15},{10,8},{11,9},{20,22},{21,... | collective-permute-start | bytes 786440 | tf_op jit(solution)/shard_map/ppermute | solution.py:345
  60.0 8.1 %blocks.5 = (f32[16,2,136,512]{3,2,1,0:T(8,128)}, f32[16,16,8,512]{3,2,1,0:T(8,128)}, f32[16,16,8,512]{3,2,1,0:T(8,128)}, f32[6,8,512]{2,1,0:T(8,128)S(1)}) custom-call(f32[16,2,136,512]{3,2,1,0:T(8,128)} %get-tuple-element.75.xg, f32[16,16,8,512]{3,2,1,0:T(8,128)} %get-tuple-element.76.blocks_e, ...), custom_call_target="tpu_custom_call", output_to_operand_aliasing={{0}: (0, {}), {1}: (1, {}), {2}: (2, {})} | custom-call | flops 62914560 | bytes 36700160 | tf_op jit(solution)/shard_map/blocks/pallas_call | solution.py:484
  68.1 2.4 %collective-permute-done.5 = f32[8,16,512]{2,1,0:T(8,128)S(1)} collective-permute-done((f32[8,16,512]{2,1,0:T(8,128)S(1)}, f32[8,16,512]{2,1,0:T(8,128)S(1)}, u32[]{:S(2)}, u32[]{:S(2)}) %collective-permute-start.5) | collective-permute-done | bytes 262176 | tf_op jit(solution)/shard_map/ppermute | solution.py:345
  70.6 0.1 select_bitcast_fusion.1
  70.7 0.1 collective-permute-start.6
  70.8 1.9 %collective-permute-done.6.found = f32[2,8,16,512]{3,2,1,0:T(8,128)S(1)} collective-permute-done((f32[2,8,16,512]{3,2,1,0:T(8,128)S(1)}, f32[2,8,16,512]{3,2,1,0:T(8,128)S(1)}, u32[]{:S(2)}, u32[]{:S(2)}) %collective-permute-start.6) | collective-permute-done | bytes 524320 | tf_op jit(solution)/shard_map/ppermute | solution.py:313
  72.7 31.5 %final.1 = (bf16[128,8192]{1,0:T(8,128)(2,1)}, bf16[3,128,8192]{2,1,0:T(8,128)(2,1)}, f32[32,24,256]{2,1,0:T(8,128)S(1)}) custom-call(s32[1]{0:T(128)} %bitcast.core, bf16[3,128,8192]{2,1,0:T(8,128)(2,1)} %bitcast.90, bf16[4,8,8192]{2,1,0:T(8,128)(2,1)S(1)} %collective-permute-done.hx, bf16[4,8,8192]{2,1,0:T(8,128)(2,1)S(1)} %copy-done.3, ...), custom_call_target="tpu_custom_call" | custom-call | tf_op jit(solution)/shard_map/final/pallas_call | solution.py:526
  104.2 0.1 slice_select_fusion
  104.2 0.2 collective-permute-start.7
  104.4 1.6 %collective-permute-done.7 = f32[16,24,256]{2,1,0:T(8,128)S(1)} collective-permute-done((f32[16,24,256]{2,1,0:T(8,128)S(1)}, f32[16,24,256]{2,1,0:T(8,128)S(1)}, u32[]{:S(2)}, u32[]{:S(2)}) %collective-permute-start.7) | collective-permute-done | bytes 393248 | tf_op jit(solution)/shard_map/ppermute | solution.py:313
  106.0 0.1 select_add_fusion
  106.1 2.5 %collective-permute-start.10 = (f32[4,24,256]{2,1,0:T(8,128)S(1)}, f32[4,24,256]{2,1,0:T(8,128)S(1)}, u32[]{:S(2)}, u32[]{:S(2)}) collective-permute-start(f32[4,24,256]{2,1,0:T(8,128)S(1)} %get-tuple-element.111), channel_id=1, source_target_pairs={{0,24},{8,16},{16,8},{24,0},{1,25},{9,17},{17,9},{25,1},{2,26},{10... | collective-permute-start | bytes 294920 | tf_op jit(solution)/shard_map/ppermute | solution.py:329
  108.6 0.5 collective-permute-start.9
  109.1 0.5 collective-permute-start.8
  109.7 2.3 %collective-permute-done.10 = f32[4,24,256]{2,1,0:T(8,128)S(1)} collective-permute-done((f32[4,24,256]{2,1,0:T(8,128)S(1)}, f32[4,24,256]{2,1,0:T(8,128)S(1)}, u32[]{:S(2)}, u32[]{:S(2)}) %collective-permute-start.10) | collective-permute-done | bytes 98336 | tf_op jit(solution)/shard_map/ppermute | solution.py:329
  112.0 2.0 %collective-permute-done.9 = f32[4,24,256]{2,1,0:T(8,128)S(1)} collective-permute-done((f32[4,24,256]{2,1,0:T(8,128)S(1)}, f32[4,24,256]{2,1,0:T(8,128)S(1)}, u32[]{:S(2)}, u32[]{:S(2)}) %collective-permute-start.9) | collective-permute-done | bytes 98336 | tf_op jit(solution)/shard_map/ppermute | solution.py:329
  114.0 0.1 collective-permute-done.8
  114.1 2.5 %collective-permute-start.11 = (f32[4,24,256]{2,1,0:T(8,128)S(1)}, f32[4,24,256]{2,1,0:T(8,128)S(1)}, u32[]{:S(2)}, u32[]{:S(2)}) collective-permute-start(f32[4,24,256]{2,1,0:T(8,128)S(1)} %add_add_fusion), channel_id=1, source_target_pairs={{0,2},{1,3},{2,0},{3,1},{4,6},{5,7},{6,4},{7,5},{8,10},{9,11},{10,... | collective-permute-start | bytes 294920 | tf_op jit(solution)/shard_map/ppermute | solution.py:329
  116.6 2.7 %collective-permute-done.11 = f32[4,24,256]{2,1,0:T(8,128)S(1)} collective-permute-done((f32[4,24,256]{2,1,0:T(8,128)S(1)}, f32[4,24,256]{2,1,0:T(8,128)S(1)}, u32[]{:S(2)}, u32[]{:S(2)}) %collective-permute-start.11) | collective-permute-done | bytes 98336 | tf_op jit(solution)/shard_map/ppermute | solution.py:329
  119.4 3.1 %collective-permute-start.12 = (f32[4,24,256]{2,1,0:T(8,128)S(1)}, f32[4,24,256]{2,1,0:T(8,128)S(1)}, u32[]{:S(2)}, u32[]{:S(2)}) collective-permute-start(f32[4,24,256]{2,1,0:T(8,128)S(1)} %add.68), channel_id=1, source_target_pairs={{0,4},{1,5},{2,6},{3,7},{4,0},{5,1},{6,2},{7,3},{8,12},{9,13},{10,... | collective-permute-start | bytes 294920 | tf_op jit(solution)/shard_map/ppermute | solution.py:329
  122.5 2.8 %collective-permute-done.12 = f32[4,24,256]{2,1,0:T(8,128)S(1)} collective-permute-done((f32[4,24,256]{2,1,0:T(8,128)S(1)}, f32[4,24,256]{2,1,0:T(8,128)S(1)}, u32[]{:S(2)}, u32[]{:S(2)}) %collective-permute-start.12) | collective-permute-done | bytes 98336 | tf_op jit(solution)/shard_map/ppermute | solution.py:329
  125.4 2.9 %collective-permute-start.13 = (f32[4,24,256]{2,1,0:T(8,128)S(1)}, f32[4,24,256]{2,1,0:T(8,128)S(1)}, u32[]{:S(2)}, u32[]{:S(2)}) collective-permute-start(f32[4,24,256]{2,1,0:T(8,128)S(1)} %get-tuple-element.95), channel_id=1, source_target_pairs={{0,8},{8,0},{16,24},{24,16},{1,9},{9,1},{17,25},{25,17},{2,10},{10... | collective-permute-start | bytes 294920 | tf_op jit(solution)/shard_map/ppermute | solution.py:329
  128.3 0.2 collective-permute-start.14
  128.5 1.4 %collective-permute-start.15 = (f32[4,24,256]{2,1,0:T(8,128)S(1)}, f32[4,24,256]{2,1,0:T(8,128)S(1)}, u32[]{:S(2)}, u32[]{:S(2)}) collective-permute-start(f32[4,24,256]{2,1,0:T(8,128)S(1)} %get-tuple-element.95), channel_id=1, source_target_pairs={{0,24},{8,16},{16,8},{24,0},{1,25},{9,17},{17,9},{25,1},{2,26},{10... | collective-permute-start | bytes 294920 | tf_op jit(solution)/shard_map/ppermute | solution.py:329
  129.9 1.8 %collective-permute-done.13 = f32[4,24,256]{2,1,0:T(8,128)S(1)} collective-permute-done((f32[4,24,256]{2,1,0:T(8,128)S(1)}, f32[4,24,256]{2,1,0:T(8,128)S(1)}, u32[]{:S(2)}, u32[]{:S(2)}) %collective-permute-start.13) | collective-permute-done | bytes 98336 | tf_op jit(solution)/shard_map/ppermute | solution.py:329
  131.7 1.2 collective-permute-done.14
  132.9 1.1 collective-permute-done.15
  134.1 0.1 collective-permute-start.16
  134.1 1.7 %collective-permute-done.16 = f32[16,24,256]{2,1,0:T(8,128)S(1)} collective-permute-done((f32[16,24,256]{2,1,0:T(8,128)S(1)}, f32[16,24,256]{2,1,0:T(8,128)S(1)}, u32[]{:S(2)}, u32[]{:S(2)}) %collective-permute-start.16) | collective-permute-done | bytes 393248 | tf_op jit(solution)/shard_map/ppermute | solution.py:313
  135.8 0.1 broadcast_select_fusion.3
  135.9 0.1 maximum_bitcast_fusion
  136.0 0.3 copy.25
  136.2 0.1 reshape.33
  136.4 0.7 slice.67
  137.1 0.2 copy-done.7
  (43 shorter events, 0.5 us)
Async XLA Ops:
  0.6 7.8 %copy-start.11 = (f32[4]{0:T(128)S(1)}, f32[4]{0:T(128)}, u32[]{:S(2)}) copy-start(f32[4]{0:T(128)} %constant.68) | copy-start | bytes 52
  0.6 8.0 %copy-start.10 = (f32[4,8]{1,0:T(4,128)S(1)}, f32[4,8]{1,0:T(4,128)}, u32[]{:S(2)}) copy-start(f32[4,8]{1,0:T(4,128)} %constant.70) | copy-start | bytes 388
  0.7 8.2 %copy-start.14 = (f32[24]{0:T(128)S(1)}, f32[24]{0:T(128)}, u32[]{:S(2)}) copy-start(f32[24]{0:T(128)} %constant.66) | copy-start | bytes 292
  0.7 7.8 %copy-start.9 = (f32[512,16]{0,1:T(8,128)S(1)}, f32[512,16]{0,1:T(8,128)}, u32[]{:S(2)}) copy-start(f32[512,16]{0,1:T(8,128)} %param.14) | copy-start | bytes 98308
  0.7 7.9 %copy-start.8 = (f32[512,16]{0,1:T(8,128)S(1)}, f32[512,16]{0,1:T(8,128)}, u32[]{:S(2)}) copy-start(f32[512,16]{0,1:T(8,128)} %param.13) | copy-start | bytes 98308
  1.7 8.3 %copy-start.12 = (pred[4,8]{1,0:T(4,128)(4,1)S(1)}, pred[4,8]{1,0:T(4,128)(4,1)}, u32[]{:S(2)}) copy-start(pred[4,8]{1,0:T(4,128)(4,1)} %constant.69) | copy-start | bytes 100
  1.7 8.3 %copy-start.13 = (pred[4,8]{1,0:T(4,128)(4,1)S(1)}, pred[4,8]{1,0:T(4,128)(4,1)}, u32[]{:S(2)}) copy-start(pred[4,8]{1,0:T(4,128)(4,1)} %constant.67) | copy-start | bytes 100
  2.9 7.4 %copy-start = (bf16[1,128,8192]{2,1,0:T(8,128)(2,1)S(1)}, bf16[1,128,8192]{2,1,0:T(8,128)(2,1)}, u32[]{:S(2)}) copy-start(bf16[1,128,8192]{2,1,0:T(8,128)(2,1)} %param.16) | copy-start | bytes 6291460
  2.9 7.4 %copy-start.1 = (f32[3,7,8192]{2,1,0:T(8,128)S(1)}, f32[3,7,8192]{2,1,0:T(8,128)}, u32[]{:S(2)}) copy-start(f32[3,7,8192]{2,1,0:T(8,128)} %filt.3) | copy-start | bytes 2064388
  3.0 7.3 %collective-permute-start = (bf16[4,8,8192]{2,1,0:T(8,128)(2,1)S(1)}, bf16[4,8,8192]{2,1,0:T(8,128)(2,1)S(1)}, u32[]{:S(2)}, u32[]{:S(2)}) collective-permute-start(bf16[4,8,8192]{2,1,0:T(8,128)(2,1)S(1)} %pad_maximum_fusion), channel_id=1, source_target_pairs={{1,2},{3,4},{5,6},{2,1},{4,3},{6,5},{9,10},{11,12},{13,14},{10,9},... | collective-permute-start | bytes 1572872 | tf_op jit(solution)/shard_map/ppermute | solution.py:406
  3.9 6.5 %collective-permute-start.1 = (bf16[4,8,8192]{2,1,0:T(8,128)(2,1)S(1)}, bf16[4,8,8192]{2,1,0:T(8,128)(2,1)S(1)}, u32[]{:S(2)}, u32[]{:S(2)}) collective-permute-start(bf16[4,8,8192]{2,1,0:T(8,128)(2,1)S(1)} %pad_maximum_fusion.1), channel_id=1, source_target_pairs={{0,1},{1,0},{2,3},{3,2},{4,5},{5,4},{6,7},{7,6},{8,9},{9,8},{10,11... | collective-permute-start | bytes 1572872 | tf_op jit(solution)/shard_map/ppermute | solution.py:313
  10.3 22.3 %copy-start.2 = (bf16[4,8,8192]{2,1,0:T(8,128)(2,1)}, bf16[4,8,8192]{2,1,0:T(8,128)(2,1)S(1)}, u32[]{:S(2)}) copy-start(bf16[4,8,8192]{2,1,0:T(8,128)(2,1)S(1)} %collective-permute-done.1.hi) | copy-start | bytes 1572868
  10.4 33.3 %copy-start.6 = (f32[8192]{0:T(1024)S(1)}, f32[8192]{0:T(1024)}, u32[]{:S(2)}) copy-start(f32[8192]{0:T(1024)} %param.15) | copy-start | bytes 98308
  32.6 7.5 %collective-permute-start.2 = (f32[2,16,16,512]{3,2,1,0:T(8,128)}, f32[2,16,16,512]{3,2,1,0:T(8,128)}, u32[]{:S(2)}, u32[]{:S(2)}) collective-permute-start(f32[2,16,16,512]{3,2,1,0:T(8,128)} %get-tuple-element.52), channel_id=1, source_target_pairs={{0,1},{1,0},{2,3},{3,2},{4,5},{5,4},{6,7},{7,6},{8,9},{9,8},{10,11... | collective-permute-start | bytes 3145736 | tf_op jit(solution)/shard_map/ppermute | solution.py:313
  41.6 10.3 %collective-permute-start.3 = (f32[8,16,512]{2,1,0:T(8,128)S(1)}, f32[8,16,512]{2,1,0:T(8,128)S(1)}, u32[]{:S(2)}, u32[]{:S(2)}) collective-permute-start(f32[8,16,512]{2,1,0:T(8,128)S(1)} %broadcast_select_fusion.4), channel_id=1, source_target_pairs={{0,2},{1,3},{2,0},{3,1},{4,6},{5,7},{6,4},{7,5},{8,10},{9,11},{10,... | collective-permute-start | bytes 786440 | tf_op jit(solution)/shard_map/ppermute | solution.py:329
  52.0 6.5 %collective-permute-start.4 = (f32[8,16,512]{2,1,0:T(8,128)S(1)}, f32[8,16,512]{2,1,0:T(8,128)S(1)}, u32[]{:S(2)}, u32[]{:S(2)}) collective-permute-start(f32[8,16,512]{2,1,0:T(8,128)S(1)} %multiply_add_fusion.1), channel_id=1, source_target_pairs={{2,4},{3,5},{4,2},{5,3},{10,12},{11,13},{12,10},{13,11},{18,20},{1... | collective-permute-start | bytes 786440 | tf_op jit(solution)/shard_map/ppermute | solution.py:342
  58.5 14.1 %copy-start.3 = (bf16[4,8,8192]{2,1,0:T(8,128)(2,1)S(1)}, bf16[4,8,8192]{2,1,0:T(8,128)(2,1)}, u32[]{:S(2)}) copy-start(bf16[4,8,8192]{2,1,0:T(8,128)(2,1)} %copy-done.2) | copy-start | bytes 1572868
  58.5 14.1 %copy-start.4 = (f32[16,8,512]{2,1,0:T(8,128)S(1)}, f32[16,8,512]{2,1,0:T(8,128)}, u32[]{:S(2)}) copy-start(f32[16,8,512]{2,1,0:T(8,128)} %get-tuple-element.90.cy) | copy-start | bytes 786436
  58.5 14.1 %copy-start.5 = (f32[16,8,512]{2,1,0:T(8,128)S(1)}, f32[16,8,512]{2,1,0:T(8,128)}, u32[]{:S(2)}) copy-start(f32[16,8,512]{2,1,0:T(8,128)} %get-tuple-element.89.cz) | copy-start | bytes 786436
  58.6 12.0 %collective-permute-start.5 = (f32[8,16,512]{2,1,0:T(8,128)S(1)}, f32[8,16,512]{2,1,0:T(8,128)S(1)}, u32[]{:S(2)}, u32[]{:S(2)}) collective-permute-start(f32[8,16,512]{2,1,0:T(8,128)S(1)} %collective-permute-done.4), channel_id=1, source_target_pairs={{4,6},{5,7},{2,0},{3,1},{12,14},{13,15},{10,8},{11,9},{20,22},{21,... | collective-permute-start | bytes 786440 | tf_op jit(solution)/shard_map/ppermute | solution.py:345
  70.7 2.0 %collective-permute-start.6 = (f32[2,8,16,512]{3,2,1,0:T(8,128)S(1)}, f32[2,8,16,512]{3,2,1,0:T(8,128)S(1)}, u32[]{:S(2)}, u32[]{:S(2)}) collective-permute-start(f32[2,8,16,512]{3,2,1,0:T(8,128)S(1)} %pad_maximum_fusion.2.both), channel_id=1, source_target_pairs={{0,1},{1,0},{2,3},{3,2},{4,5},{5,4},{6,7},{7,6},{8,9},{9,8},{10,11... | collective-permute-start | bytes 1572872 | tf_op jit(solution)/shard_map/ppermute | solution.py:313
  104.2 1.8 %collective-permute-start.7 = (f32[16,24,256]{2,1,0:T(8,128)S(1)}, f32[16,24,256]{2,1,0:T(8,128)S(1)}, u32[]{:S(2)}, u32[]{:S(2)}) collective-permute-start(f32[16,24,256]{2,1,0:T(8,128)S(1)} %slice_select_fusion), channel_id=1, source_target_pairs={{0,1},{1,0},{2,3},{3,2},{4,5},{5,4},{6,7},{7,6},{8,9},{9,8},{10,11... | collective-permute-start | bytes 1179656 | tf_op jit(solution)/shard_map/ppermute | solution.py:313
  106.1 5.9 %collective-permute-start.10 = (f32[4,24,256]{2,1,0:T(8,128)S(1)}, f32[4,24,256]{2,1,0:T(8,128)S(1)}, u32[]{:S(2)}, u32[]{:S(2)}) collective-permute-start(f32[4,24,256]{2,1,0:T(8,128)S(1)} %get-tuple-element.111), channel_id=1, source_target_pairs={{0,24},{8,16},{16,8},{24,0},{1,25},{9,17},{17,9},{25,1},{2,26},{10... | collective-permute-start | bytes 294920 | tf_op jit(solution)/shard_map/ppermute | solution.py:329
  108.6 5.4 %collective-permute-start.9 = (f32[4,24,256]{2,1,0:T(8,128)S(1)}, f32[4,24,256]{2,1,0:T(8,128)S(1)}, u32[]{:S(2)}, u32[]{:S(2)}) collective-permute-start(f32[4,24,256]{2,1,0:T(8,128)S(1)} %get-tuple-element.112), channel_id=1, source_target_pairs={{0,16},{8,24},{16,0},{24,8},{1,17},{9,25},{17,1},{25,9},{2,18},{10... | collective-permute-start | bytes 294920 | tf_op jit(solution)/shard_map/ppermute | solution.py:329
  109.1 4.9 %collective-permute-start.8 = (f32[4,24,256]{2,1,0:T(8,128)S(1)}, f32[4,24,256]{2,1,0:T(8,128)S(1)}, u32[]{:S(2)}, u32[]{:S(2)}) collective-permute-start(f32[4,24,256]{2,1,0:T(8,128)S(1)} %get-tuple-element.110), channel_id=1, source_target_pairs={{0,8},{8,0},{16,24},{24,16},{1,9},{9,1},{17,25},{25,17},{2,10},{10... | collective-permute-start | bytes 294920 | tf_op jit(solution)/shard_map/ppermute | solution.py:329
  114.1 5.2 %collective-permute-start.11 = (f32[4,24,256]{2,1,0:T(8,128)S(1)}, f32[4,24,256]{2,1,0:T(8,128)S(1)}, u32[]{:S(2)}, u32[]{:S(2)}) collective-permute-start(f32[4,24,256]{2,1,0:T(8,128)S(1)} %add_add_fusion), channel_id=1, source_target_pairs={{0,2},{1,3},{2,0},{3,1},{4,6},{5,7},{6,4},{7,5},{8,10},{9,11},{10,... | collective-permute-start | bytes 294920 | tf_op jit(solution)/shard_map/ppermute | solution.py:329
  119.4 5.9 %collective-permute-start.12 = (f32[4,24,256]{2,1,0:T(8,128)S(1)}, f32[4,24,256]{2,1,0:T(8,128)S(1)}, u32[]{:S(2)}, u32[]{:S(2)}) collective-permute-start(f32[4,24,256]{2,1,0:T(8,128)S(1)} %add.68), channel_id=1, source_target_pairs={{0,4},{1,5},{2,6},{3,7},{4,0},{5,1},{6,2},{7,3},{8,12},{9,13},{10,... | collective-permute-start | bytes 294920 | tf_op jit(solution)/shard_map/ppermute | solution.py:329
  125.4 6.3 %collective-permute-start.13 = (f32[4,24,256]{2,1,0:T(8,128)S(1)}, f32[4,24,256]{2,1,0:T(8,128)S(1)}, u32[]{:S(2)}, u32[]{:S(2)}) collective-permute-start(f32[4,24,256]{2,1,0:T(8,128)S(1)} %get-tuple-element.95), channel_id=1, source_target_pairs={{0,8},{8,0},{16,24},{24,16},{1,9},{9,1},{17,25},{25,17},{2,10},{10... | collective-permute-start | bytes 294920 | tf_op jit(solution)/shard_map/ppermute | solution.py:329
  128.3 4.6 %collective-permute-start.14 = (f32[4,24,256]{2,1,0:T(8,128)S(1)}, f32[4,24,256]{2,1,0:T(8,128)S(1)}, u32[]{:S(2)}, u32[]{:S(2)}) collective-permute-start(f32[4,24,256]{2,1,0:T(8,128)S(1)} %get-tuple-element.95), channel_id=1, source_target_pairs={{0,16},{8,24},{16,0},{24,8},{1,17},{9,25},{17,1},{25,9},{2,18},{10... | collective-permute-start | bytes 294920 | tf_op jit(solution)/shard_map/ppermute | solution.py:329
  128.5 5.5 %collective-permute-start.15 = (f32[4,24,256]{2,1,0:T(8,128)S(1)}, f32[4,24,256]{2,1,0:T(8,128)S(1)}, u32[]{:S(2)}, u32[]{:S(2)}) collective-permute-start(f32[4,24,256]{2,1,0:T(8,128)S(1)} %get-tuple-element.95), channel_id=1, source_target_pairs={{0,24},{8,16},{16,8},{24,0},{1,25},{9,17},{17,9},{25,1},{2,26},{10... | collective-permute-start | bytes 294920 | tf_op jit(solution)/shard_map/ppermute | solution.py:329
  134.1 1.8 %collective-permute-start.16 = (f32[16,24,256]{2,1,0:T(8,128)S(1)}, f32[16,24,256]{2,1,0:T(8,128)S(1)}, u32[]{:S(2)}, u32[]{:S(2)}) collective-permute-start(f32[16,24,256]{2,1,0:T(8,128)S(1)} %constant_dynamic-update-slice_fusion), channel_id=1, source_target_pairs={{0,1},{1,0},{2,3},{3,2},{4,5},{5,4},{6,7},{7,6},{8,9},{9,8},{10,11... | collective-permute-start | bytes 1179656 | tf_op jit(solution)/shard_map/ppermute | solution.py:313
  136.4 0.9 copy-start.7

commit v21 on v15

--- a/solution.py
+++ b/solution.py
@@ -74,10 +74,10 @@
             across, within = hx[j, :, lanes].astype(F32), hi[j, :, lanes].astype(F32)
             xs[j, 0:SUB] = jnp.where(first, across, within)
             xs[j, SUB : SUB + rows] = p[j, :, lanes].astype(F32)
-            xs[j, SUB + rows :] = jnp.where(first, within, across)
+            xs[j, SUB + rows : 2 * SUB + rows] = jnp.where(first, within, across)
         xs[3, SUB : SUB + rows] = u[:, lanes].astype(F32)
         across, within = hx[3, :, lanes].astype(F32), hi[3, :, lanes].astype(F32)
-        xs[3, SUB + rows :] = jnp.where(first, within, across)
+        xs[3, SUB + rows : 2 * SUB + rows] = jnp.where(first, within, across)
 
         def mixed(j):
             even, odd, both = phases([spread(filt[j, i : i + 1, lanes]) for i in range(taps)])
@@ -206,10 +206,10 @@
             across, within = hx[j, :, lanes].astype(F32), hi[j, :, lanes].astype(F32)
             ps[j, 0:SUB] = jnp.where(first, across, within)
             ps[j, SUB : SUB + rows] = p[j, :, lanes].astype(F32)
-            ps[j, SUB + rows :] = jnp.where(first, within, across)
+            ps[j, SUB + rows : 2 * SUB + rows] = jnp.where(first, within, across)
         us[0:rows] = u[:, lanes].astype(F32)
         across, within = hx[3, :, lanes].astype(F32), hi[3, :, lanes].astype(F32)
-        us[rows:] = jnp.where(first, within, across)
+        us[rows : SUB + rows] = jnp.where(first, within, across)
         decay = [spread(f1[n : n + 1, part]) for n in range(poles)]
 
         state = [
@@ -468,7 +468,7 @@
             shape_of((width, 3, held, groups), F32), pair_shape,
             state_shape, state_shape, shape_of((2, width, poles, groups), F32),
         ],
-        scratch_shapes=[pltpu.VMEM((4, held + SUB, LANES), F32)],
+        scratch_shapes=[pltpu.VMEM((4, held + 4 * SUB, LANES), F32)],
         compiler_params=params,
         name="states",
     )(core[None], p, hx, hi, u, short_filter, f1, we, wb)
@@ -518,10 +518,10 @@
     count = 3 * SUB
     split = 2 if groups % (2 * LANES) == 0 else 1
     scratch = [
-        pltpu.VMEM((3, held + SUB, LANES), F32),
-        pltpu.VMEM((held, LANES), F32),
+        pltpu.VMEM((3, held + 4 * SUB, LANES), F32),
+        pltpu.VMEM((held + 4 * SUB, LANES), F32),
         pltpu.VMEM((3, held, LANES), F32),
-        pltpu.VMEM((held, LANES), F32),
+        pltpu.VMEM((held + 4 * SUB, LANES), F32),
         pltpu.VMEM((2, poles, LANES), F32),
     ]
     output, grad_p, sums = pl.pallas_call(

time: 137 us -> 137 us (level)
  no operation moved by 1% of the time
where the time goes in v21:
time: 137 us; the launch traced here: 136 us
  Pallas kernels  75.7 us (55%)
  starting transfers between devices  26.6 us (19%)
  waiting for transfers between devices  25.4 us (19%)
  other arithmetic  3.86 us (3%)
  local copies, waits for them, and re-layouts  3.67 us (3%)
    pallas_call x1, Pallas kernels, local(): pl.pallas_call(final_kernel, grid=(width // each,), in_specs=[pl.BlockSpe...  31.4 us
    pallas_call x3, Pallas kernels, call(): pl.pallas_call(blocks_kernel, grid=(last - first,), in_specs=[pairs, stat...  22.1 us
    pallas_call x1, Pallas kernels, local(): pl.pallas_call(states_kernel, grid=(width // each,), in_specs=[pl.BlockSp...  22.1 us
    ppermute x5, starting transfers between devices, swapped(): return lax.ppermute(value, 'ctx', [(s, s ^ 1) for s in range(count)])  9.72 us
    ppermute x7, starting transfers between devices, paired(): lax.ppermute(value, axis, [(source, source ^ step) for source in lines or...  9.16 us
    ppermute x7, waiting for transfers between devices, paired(): lax.ppermute(value, axis, [(source, source ^ step) for source in lines or...  8.19 us
    ppermute x5, waiting for transfers between devices, swapped(): return lax.ppermute(value, 'ctx', [(s, s ^ 1) for s in range(count)])  7.85 us
    ppermute x2, waiting for transfers between devices, summed(): total = total + lax.ppermute(total, 'ctx', pairs)  6.94 us
  transfers between devices with their start and end apart: 17, of which 13 were waited for; matrix products, arithmetic and copies ran while one was open for 1% of the time, Pallas kernels for 16%

profile of v21, /device:TPU:0, one launch (start us, length us, event | category | flops | bytes accessed | tf_op | source)
XLA Modules:
  0.0 136.3 jit_solution(11927785250203957751)
XLA Ops:
  0.6 0.0 copy-start.11
  0.6 0.0 copy-start.10
  0.7 0.0 copy-start.14
  0.7 1.0 constant_dynamic-slice_fusion.3
  1.7 0.0 copy-start.12
  1.7 0.0 copy-start.13
  1.7 1.2 dynamic-slice_bitcast_fusion
  2.9 0.0 copy-start
  2.9 0.0 copy-start.1
  3.0 0.8 collective-permute-start
  3.9 4.5 %collective-permute-start.1 = (bf16[4,8,8192]{2,1,0:T(8,128)(2,1)S(1)}, bf16[4,8,8192]{2,1,0:T(8,128)(2,1)S(1)}, u32[]{:S(2)}, u32[]{:S(2)}) collective-permute-start(bf16[4,8,8192]{2,1,0:T(8,128)(2,1)S(1)} %pad_maximum_fusion.1), channel_id=1, source_target_pairs={{0,1},{1,0},{2,3},{3,2},{4,5},{5,4},{6,7},{7,6},{8,9},{9,8},{10,11... | collective-permute-start | bytes 1572872 | tf_op jit(solution)/shard_map/ppermute | solution.py:313
  8.5 0.1 multiply_exponential_fusion.1
  8.6 0.2 multiply_exponential_fusion
  8.9 0.2 multiply_reduce_fusion.near
  9.1 0.8 fusion.4
  10.0 0.3 broadcast_select_fusion
  10.3 0.0 copy-start.2
  10.4 0.0 copy-start.6
  10.4 22.1 %states.1 = (f32[16,3,136,512]{3,2,1,0:T(8,128)}, f32[16,2,136,512]{3,2,1,0:T(8,128)}, f32[16,16,8,512]{3,2,1,0:T(8,128)}, f32[16,16,8,512]{3,2,1,0:T(8,128)}, f32[2,16,16,512]{3,2,1,0:T(8,128)}) custom-call(s32[1]{0:T(128)} %bitcast.core, bf16[3,128,8192]{2,1,0:T(8,128)(2,1)} %bitcast.89, bf16[4,8,8192]{2,1,0:T(8,128)(2,1)S(1)} %collective-permute-done.hx, ...), custom_call_target="tpu_custom_call" | custom-call | tf_op jit(solution)/shard_map/states/pallas_call | solution.py:455
  32.5 4.9 %collective-permute-start.2 = (f32[2,16,16,512]{3,2,1,0:T(8,128)}, f32[2,16,16,512]{3,2,1,0:T(8,128)}, u32[]{:S(2)}, u32[]{:S(2)}) collective-permute-start(f32[2,16,16,512]{3,2,1,0:T(8,128)} %get-tuple-element.52), channel_id=1, source_target_pairs={{0,1},{1,0},{2,3},{3,2},{4,5},{5,4},{6,7},{7,6},{8,9},{9,8},{10,11... | collective-permute-start | bytes 3145736 | tf_op jit(solution)/shard_map/ppermute | solution.py:313
  37.3 2.6 %collective-permute-done.2.other = f32[2,16,16,512]{3,2,1,0:T(8,128)} collective-permute-done((f32[2,16,16,512]{3,2,1,0:T(8,128)}, f32[2,16,16,512]{3,2,1,0:T(8,128)}, u32[]{:S(2)}, u32[]{:S(2)}) %collective-permute-start.2) | collective-permute-done | bytes 1048608 | tf_op jit(solution)/shard_map/ppermute | solution.py:313
  40.0 1.3 dynamic-slice_select_fusion.1
  41.3 0.1 broadcast_select_fusion.4
  41.4 2.1 %collective-permute-start.3 = (f32[8,16,512]{2,1,0:T(8,128)S(1)}, f32[8,16,512]{2,1,0:T(8,128)S(1)}, u32[]{:S(2)}, u32[]{:S(2)}) collective-permute-start(f32[8,16,512]{2,1,0:T(8,128)S(1)} %broadcast_select_fusion.4), channel_id=1, source_target_pairs={{0,2},{1,3},{2,0},{3,1},{4,6},{5,7},{6,4},{7,5},{8,10},{9,11},{10,... | collective-permute-start | bytes 786440 | tf_op jit(solution)/shard_map/ppermute | solution.py:329
  43.5 8.2 %blocks.3 = (f32[16,2,136,512]{3,2,1,0:T(8,128)}, f32[16,16,8,512]{3,2,1,0:T(8,128)}, f32[16,16,8,512]{3,2,1,0:T(8,128)}, f32[6,8,512]{2,1,0:T(8,128)S(1)}) custom-call(f32[16,2,136,512]{3,2,1,0:T(8,128)} %get-tuple-element.53.xg, f32[16,16,8,512]{3,2,1,0:T(8,128)} %get-tuple-element.54.blocks_e, ...), custom_call_target="tpu_custom_call", output_to_operand_aliasing={{0}: (0, {}), {1}: (1, {}), {2}: (2, {})} | custom-call | flops 62914560 | bytes 36700160 | tf_op jit(solution)/shard_map/blocks/pallas_call | solution.py:485
  51.7 0.1 multiply_add_fusion.1
  51.8 0.7 collective-permute-start.4
  52.5 5.8 %blocks.4 = (f32[16,2,136,512]{3,2,1,0:T(8,128)}, f32[16,16,8,512]{3,2,1,0:T(8,128)}, f32[16,16,8,512]{3,2,1,0:T(8,128)}, f32[4,8,512]{2,1,0:T(8,128)S(1)}) custom-call(f32[16,2,136,512]{3,2,1,0:T(8,128)} %get-tuple-element.65.xg, f32[16,16,8,512]{3,2,1,0:T(8,128)} %get-tuple-element.66.blocks_e, ...), custom_call_target="tpu_custom_call", output_to_operand_aliasing={{0}: (0, {}), {1}: (1, {}), {2}: (2, {})} | custom-call | flops 62914560 | bytes 36700160 | tf_op jit(solution)/shard_map/blocks/pallas_call | solution.py:485
  58.4 0.0 copy-start.4
  58.4 1.4 %collective-permute-start.5 = (f32[8,16,512]{2,1,0:T(8,128)S(1)}, f32[8,16,512]{2,1,0:T(8,128)S(1)}, u32[]{:S(2)}, u32[]{:S(2)}) collective-permute-start(f32[8,16,512]{2,1,0:T(8,128)S(1)} %collective-permute-done.4), channel_id=1, source_target_pairs={{4,6},{5,7},{2,0},{3,1},{12,14},{13,15},{10,8},{11,9},{20,22},{21,... | collective-permute-start | bytes 786440 | tf_op jit(solution)/shard_map/ppermute | solution.py:345
  59.8 8.1 %blocks.5 = (f32[16,2,136,512]{3,2,1,0:T(8,128)}, f32[16,16,8,512]{3,2,1,0:T(8,128)}, f32[16,16,8,512]{3,2,1,0:T(8,128)}, f32[6,8,512]{2,1,0:T(8,128)S(1)}) custom-call(f32[16,2,136,512]{3,2,1,0:T(8,128)} %get-tuple-element.75.xg, f32[16,16,8,512]{3,2,1,0:T(8,128)} %get-tuple-element.76.blocks_e, ...), custom_call_target="tpu_custom_call", output_to_operand_aliasing={{0}: (0, {}), {1}: (1, {}), {2}: (2, {})} | custom-call | flops 62914560 | bytes 36700160 | tf_op jit(solution)/shard_map/blocks/pallas_call | solution.py:485
  68.0 2.4 %collective-permute-done.5 = f32[8,16,512]{2,1,0:T(8,128)S(1)} collective-permute-done((f32[8,16,512]{2,1,0:T(8,128)S(1)}, f32[8,16,512]{2,1,0:T(8,128)S(1)}, u32[]{:S(2)}, u32[]{:S(2)}) %collective-permute-start.5) | collective-permute-done | bytes 262176 | tf_op jit(solution)/shard_map/ppermute | solution.py:345
  70.4 0.1 select_bitcast_fusion.1
  70.5 0.1 collective-permute-start.6
  70.6 1.9 %collective-permute-done.6.found = f32[2,8,16,512]{3,2,1,0:T(8,128)S(1)} collective-permute-done((f32[2,8,16,512]{3,2,1,0:T(8,128)S(1)}, f32[2,8,16,512]{3,2,1,0:T(8,128)S(1)}, u32[]{:S(2)}, u32[]{:S(2)}) %collective-permute-start.6) | collective-permute-done | bytes 524320 | tf_op jit(solution)/shard_map/ppermute | solution.py:313
  72.5 31.4 %final.1 = (bf16[128,8192]{1,0:T(8,128)(2,1)}, bf16[3,128,8192]{2,1,0:T(8,128)(2,1)}, f32[32,24,256]{2,1,0:T(8,128)S(1)}) custom-call(s32[1]{0:T(128)} %bitcast.core, bf16[3,128,8192]{2,1,0:T(8,128)(2,1)} %bitcast.90, bf16[4,8,8192]{2,1,0:T(8,128)(2,1)S(1)} %collective-permute-done.hx, bf16[4,8,8192]{2,1,0:T(8,128)(2,1)S(1)} %copy-done.3, ...), custom_call_target="tpu_custom_call" | custom-call | tf_op jit(solution)/shard_map/final/pallas_call | solution.py:527
  103.9 0.1 slice_select_fusion
  104.0 0.2 collective-permute-start.7
  104.2 1.6 %collective-permute-done.7 = f32[16,24,256]{2,1,0:T(8,128)S(1)} collective-permute-done((f32[16,24,256]{2,1,0:T(8,128)S(1)}, f32[16,24,256]{2,1,0:T(8,128)S(1)}, u32[]{:S(2)}, u32[]{:S(2)}) %collective-permute-start.7) | collective-permute-done | bytes 393248 | tf_op jit(solution)/shard_map/ppermute | solution.py:313
  105.8 0.1 select_add_fusion
  105.9 2.5 %collective-permute-start.10 = (f32[4,24,256]{2,1,0:T(8,128)S(1)}, f32[4,24,256]{2,1,0:T(8,128)S(1)}, u32[]{:S(2)}, u32[]{:S(2)}) collective-permute-start(f32[4,24,256]{2,1,0:T(8,128)S(1)} %get-tuple-element.111), channel_id=1, source_target_pairs={{0,24},{8,16},{16,8},{24,0},{1,25},{9,17},{17,9},{25,1},{2,26},{10... | collective-permute-start | bytes 294920 | tf_op jit(solution)/shard_map/ppermute | solution.py:329
  108.4 0.5 collective-permute-start.9
  108.9 0.5 collective-permute-start.8
  109.5 2.3 %collective-permute-done.10 = f32[4,24,256]{2,1,0:T(8,128)S(1)} collective-permute-done((f32[4,24,256]{2,1,0:T(8,128)S(1)}, f32[4,24,256]{2,1,0:T(8,128)S(1)}, u32[]{:S(2)}, u32[]{:S(2)}) %collective-permute-start.10) | collective-permute-done | bytes 98336 | tf_op jit(solution)/shard_map/ppermute | solution.py:329
  111.8 2.0 %collective-permute-done.9 = f32[4,24,256]{2,1,0:T(8,128)S(1)} collective-permute-done((f32[4,24,256]{2,1,0:T(8,128)S(1)}, f32[4,24,256]{2,1,0:T(8,128)S(1)}, u32[]{:S(2)}, u32[]{:S(2)}) %collective-permute-start.9) | collective-permute-done | bytes 98336 | tf_op jit(solution)/shard_map/ppermute | solution.py:329
  113.8 0.1 collective-permute-done.8
  113.9 2.5 %collective-permute-start.11 = (f32[4,24,256]{2,1,0:T(8,128)S(1)}, f32[4,24,256]{2,1,0:T(8,128)S(1)}, u32[]{:S(2)}, u32[]{:S(2)}) collective-permute-start(f32[4,24,256]{2,1,0:T(8,128)S(1)} %add_add_fusion), channel_id=1, source_target_pairs={{0,2},{1,5},{2,0},{3,7},{4,6},{5,1},{6,4},{7,3},{8,10},{9,13},{10,... | collective-permute-start | bytes 294920 | tf_op jit(solution)/shard_map/ppermute | solution.py:378
  116.4 3.6 %collective-permute-done.11 = f32[4,24,256]{2,1,0:T(8,128)S(1)} collective-permute-done((f32[4,24,256]{2,1,0:T(8,128)S(1)}, f32[4,24,256]{2,1,0:T(8,128)S(1)}, u32[]{:S(2)}, u32[]{:S(2)}) %collective-permute-start.11) | collective-permute-done | bytes 98336 | tf_op jit(solution)/shard_map/ppermute | solution.py:378
  120.0 2.2 %collective-permute-start.12 = (f32[4,24,256]{2,1,0:T(8,128)S(1)}, f32[4,24,256]{2,1,0:T(8,128)S(1)}, u32[]{:S(2)}, u32[]{:S(2)}) collective-permute-start(f32[4,24,256]{2,1,0:T(8,128)S(1)} %add.68), channel_id=1, source_target_pairs={{0,4},{1,3},{2,6},{3,1},{4,0},{5,7},{6,2},{7,5},{8,12},{9,11},{10,... | collective-permute-start | bytes 294920 | tf_op jit(solution)/shard_map/ppermute | solution.py:378
  122.3 3.3 %collective-permute-done.12 = f32[4,24,256]{2,1,0:T(8,128)S(1)} collective-permute-done((f32[4,24,256]{2,1,0:T(8,128)S(1)}, f32[4,24,256]{2,1,0:T(8,128)S(1)}, u32[]{:S(2)}, u32[]{:S(2)}) %collective-permute-start.12) | collective-permute-done | bytes 98336 | tf_op jit(solution)/shard_map/ppermute | solution.py:378
  125.7 1.6 %collective-permute-start.13 = (f32[4,24,256]{2,1,0:T(8,128)S(1)}, f32[4,24,256]{2,1,0:T(8,128)S(1)}, u32[]{:S(2)}, u32[]{:S(2)}) collective-permute-start(f32[4,24,256]{2,1,0:T(8,128)S(1)} %get-tuple-element.95), channel_id=1, source_target_pairs={{0,8},{8,0},{16,24},{24,16},{1,9},{9,1},{17,25},{25,17},{2,10},{10... | collective-permute-start | bytes 294920 | tf_op jit(solution)/shard_map/ppermute | solution.py:329
  127.3 0.2 collective-permute-start.14
  127.5 1.7 %collective-permute-start.15 = (f32[4,24,256]{2,1,0:T(8,128)S(1)}, f32[4,24,256]{2,1,0:T(8,128)S(1)}, u32[]{:S(2)}, u32[]{:S(2)}) collective-permute-start(f32[4,24,256]{2,1,0:T(8,128)S(1)} %get-tuple-element.95), channel_id=1, source_target_pairs={{0,24},{8,16},{16,8},{24,0},{1,25},{9,17},{17,9},{25,1},{2,26},{10... | collective-permute-start | bytes 294920 | tf_op jit(solution)/shard_map/ppermute | solution.py:329
  129.2 1.9 %collective-permute-done.13 = f32[4,24,256]{2,1,0:T(8,128)S(1)} collective-permute-done((f32[4,24,256]{2,1,0:T(8,128)S(1)}, f32[4,24,256]{2,1,0:T(8,128)S(1)}, u32[]{:S(2)}, u32[]{:S(2)}) %collective-permute-start.13) | collective-permute-done | bytes 98336 | tf_op jit(solution)/shard_map/ppermute | solution.py:329
  131.1 0.8 collective-permute-done.14
  131.9 1.1 collective-permute-done.15
  133.0 0.1 collective-permute-start.16
  133.1 1.7 %collective-permute-done.16 = f32[16,24,256]{2,1,0:T(8,128)S(1)} collective-permute-done((f32[16,24,256]{2,1,0:T(8,128)S(1)}, f32[16,24,256]{2,1,0:T(8,128)S(1)}, u32[]{:S(2)}, u32[]{:S(2)}) %collective-permute-start.16) | collective-permute-done | bytes 393248 | tf_op jit(solution)/shard_map/ppermute | solution.py:313
  134.8 0.1 broadcast_select_fusion.3
  134.9 0.1 maximum_bitcast_fusion
  134.9 0.3 copy.25
  135.2 0.1 reshape.33
  135.4 0.7 slice.67
  136.1 0.2 copy-done.7
  (43 shorter events, 0.5 us)
Async XLA Ops:
  0.6 7.8 %copy-start.11 = (f32[4]{0:T(128)S(1)}, f32[4]{0:T(128)}, u32[]{:S(2)}) copy-start(f32[4]{0:T(128)} %constant.68) | copy-start | bytes 52
  0.6 8.0 %copy-start.10 = (f32[4,8]{1,0:T(4,128)S(1)}, f32[4,8]{1,0:T(4,128)}, u32[]{:S(2)}) copy-start(f32[4,8]{1,0:T(4,128)} %constant.70) | copy-start | bytes 388
  0.7 8.2 %copy-start.14 = (f32[24]{0:T(128)S(1)}, f32[24]{0:T(128)}, u32[]{:S(2)}) copy-start(f32[24]{0:T(128)} %constant.66) | copy-start | bytes 292
  0.7 7.8 %copy-start.9 = (f32[512,16]{0,1:T(8,128)S(1)}, f32[512,16]{0,1:T(8,128)}, u32[]{:S(2)}) copy-start(f32[512,16]{0,1:T(8,128)} %param.14) | copy-start | bytes 98308
  0.7 7.9 %copy-start.8 = (f32[512,16]{0,1:T(8,128)S(1)}, f32[512,16]{0,1:T(8,128)}, u32[]{:S(2)}) copy-start(f32[512,16]{0,1:T(8,128)} %param.13) | copy-start | bytes 98308
  1.7 8.3 %copy-start.12 = (pred[4,8]{1,0:T(4,128)(4,1)S(1)}, pred[4,8]{1,0:T(4,128)(4,1)}, u32[]{:S(2)}) copy-start(pred[4,8]{1,0:T(4,128)(4,1)} %constant.69) | copy-start | bytes 100
  1.7 8.3 %copy-start.13 = (pred[4,8]{1,0:T(4,128)(4,1)S(1)}, pred[4,8]{1,0:T(4,128)(4,1)}, u32[]{:S(2)}) copy-start(pred[4,8]{1,0:T(4,128)(4,1)} %constant.67) | copy-start | bytes 100
  2.9 7.4 %copy-start = (bf16[1,128,8192]{2,1,0:T(8,128)(2,1)S(1)}, bf16[1,128,8192]{2,1,0:T(8,128)(2,1)}, u32[]{:S(2)}) copy-start(bf16[1,128,8192]{2,1,0:T(8,128)(2,1)} %param.16) | copy-start | bytes 6291460
  2.9 7.4 %copy-start.1 = (f32[3,7,8192]{2,1,0:T(8,128)S(1)}, f32[3,7,8192]{2,1,0:T(8,128)}, u32[]{:S(2)}) copy-start(f32[3,7,8192]{2,1,0:T(8,128)} %filt.3) | copy-start | bytes 2064388
  3.0 7.3 %collective-permute-start = (bf16[4,8,8192]{2,1,0:T(8,128)(2,1)S(1)}, bf16[4,8,8192]{2,1,0:T(8,128)(2,1)S(1)}, u32[]{:S(2)}, u32[]{:S(2)}) collective-permute-start(bf16[4,8,8192]{2,1,0:T(8,128)(2,1)S(1)} %pad_maximum_fusion), channel_id=1, source_target_pairs={{1,2},{3,4},{5,6},{2,1},{4,3},{6,5},{9,10},{11,12},{13,14},{10,9},... | collective-permute-start | bytes 1572872 | tf_op jit(solution)/shard_map/ppermute | solution.py:407
  3.9 6.5 %collective-permute-start.1 = (bf16[4,8,8192]{2,1,0:T(8,128)(2,1)S(1)}, bf16[4,8,8192]{2,1,0:T(8,128)(2,1)S(1)}, u32[]{:S(2)}, u32[]{:S(2)}) collective-permute-start(bf16[4,8,8192]{2,1,0:T(8,128)(2,1)S(1)} %pad_maximum_fusion.1), channel_id=1, source_target_pairs={{0,1},{1,0},{2,3},{3,2},{4,5},{5,4},{6,7},{7,6},{8,9},{9,8},{10,11... | collective-permute-start | bytes 1572872 | tf_op jit(solution)/shard_map/ppermute | solution.py:313
  10.3 22.1 %copy-start.2 = (bf16[4,8,8192]{2,1,0:T(8,128)(2,1)}, bf16[4,8,8192]{2,1,0:T(8,128)(2,1)S(1)}, u32[]{:S(2)}) copy-start(bf16[4,8,8192]{2,1,0:T(8,128)(2,1)S(1)} %collective-permute-done.1.hi) | copy-start | bytes 1572868
  10.4 33.1 %copy-start.6 = (f32[8192]{0:T(1024)S(1)}, f32[8192]{0:T(1024)}, u32[]{:S(2)}) copy-start(f32[8192]{0:T(1024)} %param.15) | copy-start | bytes 98308
  32.5 7.5 %collective-permute-start.2 = (f32[2,16,16,512]{3,2,1,0:T(8,128)}, f32[2,16,16,512]{3,2,1,0:T(8,128)}, u32[]{:S(2)}, u32[]{:S(2)}) collective-permute-start(f32[2,16,16,512]{3,2,1,0:T(8,128)} %get-tuple-element.52), channel_id=1, source_target_pairs={{0,1},{1,0},{2,3},{3,2},{4,5},{5,4},{6,7},{7,6},{8,9},{9,8},{10,11... | collective-permute-start | bytes 3145736 | tf_op jit(solution)/shard_map/ppermute | solution.py:313
  41.4 10.3 %collective-permute-start.3 = (f32[8,16,512]{2,1,0:T(8,128)S(1)}, f32[8,16,512]{2,1,0:T(8,128)S(1)}, u32[]{:S(2)}, u32[]{:S(2)}) collective-permute-start(f32[8,16,512]{2,1,0:T(8,128)S(1)} %broadcast_select_fusion.4), channel_id=1, source_target_pairs={{0,2},{1,3},{2,0},{3,1},{4,6},{5,7},{6,4},{7,5},{8,10},{9,11},{10,... | collective-permute-start | bytes 786440 | tf_op jit(solution)/shard_map/ppermute | solution.py:329
  51.8 6.5 %collective-permute-start.4 = (f32[8,16,512]{2,1,0:T(8,128)S(1)}, f32[8,16,512]{2,1,0:T(8,128)S(1)}, u32[]{:S(2)}, u32[]{:S(2)}) collective-permute-start(f32[8,16,512]{2,1,0:T(8,128)S(1)} %multiply_add_fusion.1), channel_id=1, source_target_pairs={{2,4},{3,5},{4,2},{5,3},{10,12},{11,13},{12,10},{13,11},{18,20},{1... | collective-permute-start | bytes 786440 | tf_op jit(solution)/shard_map/ppermute | solution.py:342
  58.3 14.1 %copy-start.3 = (bf16[4,8,8192]{2,1,0:T(8,128)(2,1)S(1)}, bf16[4,8,8192]{2,1,0:T(8,128)(2,1)}, u32[]{:S(2)}) copy-start(bf16[4,8,8192]{2,1,0:T(8,128)(2,1)} %copy-done.2) | copy-start | bytes 1572868
  58.4 14.1 %copy-start.4 = (f32[16,8,512]{2,1,0:T(8,128)S(1)}, f32[16,8,512]{2,1,0:T(8,128)}, u32[]{:S(2)}) copy-start(f32[16,8,512]{2,1,0:T(8,128)} %get-tuple-element.90.cy) | copy-start | bytes 786436
  58.4 14.1 %copy-start.5 = (f32[16,8,512]{2,1,0:T(8,128)S(1)}, f32[16,8,512]{2,1,0:T(8,128)}, u32[]{:S(2)}) copy-start(f32[16,8,512]{2,1,0:T(8,128)} %get-tuple-element.89.cz) | copy-start | bytes 786436
  58.4 12.0 %collective-permute-start.5 = (f32[8,16,512]{2,1,0:T(8,128)S(1)}, f32[8,16,512]{2,1,0:T(8,128)S(1)}, u32[]{:S(2)}, u32[]{:S(2)}) collective-permute-start(f32[8,16,512]{2,1,0:T(8,128)S(1)} %collective-permute-done.4), channel_id=1, source_target_pairs={{4,6},{5,7},{2,0},{3,1},{12,14},{13,15},{10,8},{11,9},{20,22},{21,... | collective-permute-start | bytes 786440 | tf_op jit(solution)/shard_map/ppermute | solution.py:345
  70.5 2.0 %collective-permute-start.6 = (f32[2,8,16,512]{3,2,1,0:T(8,128)S(1)}, f32[2,8,16,512]{3,2,1,0:T(8,128)S(1)}, u32[]{:S(2)}, u32[]{:S(2)}) collective-permute-start(f32[2,8,16,512]{3,2,1,0:T(8,128)S(1)} %pad_maximum_fusion.2.both), channel_id=1, source_target_pairs={{0,1},{1,0},{2,3},{3,2},{4,5},{5,4},{6,7},{7,6},{8,9},{9,8},{10,11... | collective-permute-start | bytes 1572872 | tf_op jit(solution)/shard_map/ppermute | solution.py:313
  104.0 1.8 %collective-permute-start.7 = (f32[16,24,256]{2,1,0:T(8,128)S(1)}, f32[16,24,256]{2,1,0:T(8,128)S(1)}, u32[]{:S(2)}, u32[]{:S(2)}) collective-permute-start(f32[16,24,256]{2,1,0:T(8,128)S(1)} %slice_select_fusion), channel_id=1, source_target_pairs={{0,1},{1,0},{2,3},{3,2},{4,5},{5,4},{6,7},{7,6},{8,9},{9,8},{10,11... | collective-permute-start | bytes 1179656 | tf_op jit(solution)/shard_map/ppermute | solution.py:313
  105.9 5.9 %collective-permute-start.10 = (f32[4,24,256]{2,1,0:T(8,128)S(1)}, f32[4,24,256]{2,1,0:T(8,128)S(1)}, u32[]{:S(2)}, u32[]{:S(2)}) collective-permute-start(f32[4,24,256]{2,1,0:T(8,128)S(1)} %get-tuple-element.111), channel_id=1, source_target_pairs={{0,24},{8,16},{16,8},{24,0},{1,25},{9,17},{17,9},{25,1},{2,26},{10... | collective-permute-start | bytes 294920 | tf_op jit(solution)/shard_map/ppermute | solution.py:329
  108.4 5.4 %collective-permute-start.9 = (f32[4,24,256]{2,1,0:T(8,128)S(1)}, f32[4,24,256]{2,1,0:T(8,128)S(1)}, u32[]{:S(2)}, u32[]{:S(2)}) collective-permute-start(f32[4,24,256]{2,1,0:T(8,128)S(1)} %get-tuple-element.112), channel_id=1, source_target_pairs={{0,16},{8,24},{16,0},{24,8},{1,17},{9,25},{17,1},{25,9},{2,18},{10... | collective-permute-start | bytes 294920 | tf_op jit(solution)/shard_map/ppermute | solution.py:329
  108.9 4.9 %collective-permute-start.8 = (f32[4,24,256]{2,1,0:T(8,128)S(1)}, f32[4,24,256]{2,1,0:T(8,128)S(1)}, u32[]{:S(2)}, u32[]{:S(2)}) collective-permute-start(f32[4,24,256]{2,1,0:T(8,128)S(1)} %get-tuple-element.110), channel_id=1, source_target_pairs={{0,8},{8,0},{16,24},{24,16},{1,9},{9,1},{17,25},{25,17},{2,10},{10... | collective-permute-start | bytes 294920 | tf_op jit(solution)/shard_map/ppermute | solution.py:329
  113.9 6.1 %collective-permute-start.11 = (f32[4,24,256]{2,1,0:T(8,128)S(1)}, f32[4,24,256]{2,1,0:T(8,128)S(1)}, u32[]{:S(2)}, u32[]{:S(2)}) collective-permute-start(f32[4,24,256]{2,1,0:T(8,128)S(1)} %add_add_fusion), channel_id=1, source_target_pairs={{0,2},{1,5},{2,0},{3,7},{4,6},{5,1},{6,4},{7,3},{8,10},{9,13},{10,... | collective-permute-start | bytes 294920 | tf_op jit(solution)/shard_map/ppermute | solution.py:378
  120.0 5.6 %collective-permute-start.12 = (f32[4,24,256]{2,1,0:T(8,128)S(1)}, f32[4,24,256]{2,1,0:T(8,128)S(1)}, u32[]{:S(2)}, u32[]{:S(2)}) collective-permute-start(f32[4,24,256]{2,1,0:T(8,128)S(1)} %add.68), channel_id=1, source_target_pairs={{0,4},{1,3},{2,6},{3,1},{4,0},{5,7},{6,2},{7,5},{8,12},{9,11},{10,... | collective-permute-start | bytes 294920 | tf_op jit(solution)/shard_map/ppermute | solution.py:378
  125.7 5.4 %collective-permute-start.13 = (f32[4,24,256]{2,1,0:T(8,128)S(1)}, f32[4,24,256]{2,1,0:T(8,128)S(1)}, u32[]{:S(2)}, u32[]{:S(2)}) collective-permute-start(f32[4,24,256]{2,1,0:T(8,128)S(1)} %get-tuple-element.95), channel_id=1, source_target_pairs={{0,8},{8,0},{16,24},{24,16},{1,9},{9,1},{17,25},{25,17},{2,10},{10... | collective-permute-start | bytes 294920 | tf_op jit(solution)/shard_map/ppermute | solution.py:329
  127.3 4.6 %collective-permute-start.14 = (f32[4,24,256]{2,1,0:T(8,128)S(1)}, f32[4,24,256]{2,1,0:T(8,128)S(1)}, u32[]{:S(2)}, u32[]{:S(2)}) collective-permute-start(f32[4,24,256]{2,1,0:T(8,128)S(1)} %get-tuple-element.95), channel_id=1, source_target_pairs={{0,16},{8,24},{16,0},{24,8},{1,17},{9,25},{17,1},{25,9},{2,18},{10... | collective-permute-start | bytes 294920 | tf_op jit(solution)/shard_map/ppermute | solution.py:329
  127.5 5.5 %collective-permute-start.15 = (f32[4,24,256]{2,1,0:T(8,128)S(1)}, f32[4,24,256]{2,1,0:T(8,128)S(1)}, u32[]{:S(2)}, u32[]{:S(2)}) collective-permute-start(f32[4,24,256]{2,1,0:T(8,128)S(1)} %get-tuple-element.95), channel_id=1, source_target_pairs={{0,24},{8,16},{16,8},{24,0},{1,25},{9,17},{17,9},{25,1},{2,26},{10... | collective-permute-start | bytes 294920 | tf_op jit(solution)/shard_map/ppermute | solution.py:329
  133.0 1.8 %collective-permute-start.16 = (f32[16,24,256]{2,1,0:T(8,128)S(1)}, f32[16,24,256]{2,1,0:T(8,128)S(1)}, u32[]{:S(2)}, u32[]{:S(2)}) collective-permute-start(f32[16,24,256]{2,1,0:T(8,128)S(1)} %constant_dynamic-update-slice_fusion), channel_id=1, source_target_pairs={{0,1},{1,0},{2,3},{3,2},{4,5},{5,4},{6,7},{7,6},{8,9},{9,8},{10,11... | collective-permute-start | bytes 1179656 | tf_op jit(solution)/shard_map/ppermute | solution.py:313
  135.4 0.9 copy-start.7
